TPU v7x, 32 devices: a whole 2x2x4 slice. The times are simulated.
32 devices in a mesh: grp: 2 (over x), chan: 16 (over z, y, core).
Axes of the slice: x: 2, y: 2, z: 4, core: 2. Of those that a mesh axis runs over, the one named last changes fastest.
Arguments:
- spectra: bfloat16 [1024, 2, 4, 4096], P(None, None, None, ('grp', 'chan')), parts along dimension 3, may hold values from -6 to 6
- quality: int32 [32, 4], P(('grp', 'chan')), parts along dimension 0, may hold values 0 or 1
Outputs:
- near_corr: bfloat16 [32, 9, 128, 128], P(('grp', 'chan')), parts along dimension 0
- far_corr: bfloat16 [32, 9, 128, 128], P(('grp', 'chan')), parts along dimension 0
There are 2 independent parts, one for each index of `grp`. A program takes and returns all parts, laid end to end along the dimension named above; each array names one. Nothing has to cross between parts.
All inputs are finite; a program needn't handle non-finite values. No bound on the sum of `quality` on one device may be relied on, other than what follows from the above.
Results may differ from a plain program's by a relative error of at most 0.012.
Values may be sent and summed in bfloat16 or wider, within the bound.
No kernel may reach another device: no remote copies, remote signals or barrier semaphores. Data moves between devices by JAX's collectives and lax.ppermute only.
A program may use at most 64 MiB of HBM per device.

v0:
```python
import math

import jax
import jax.numpy as jnp
from jax import lax
from jax.sharding import PartitionSpec as P

HL = 4


def passed_along(value, axis, steps):
    count = lax.axis_size(axis)
    pairs = [(source, (source + steps) % count) for source in range(count)]
    return lax.ppermute(value, axis, pairs)


def lag_table(freq_count, window_count):
    lag_values = jnp.arange(2 * HL + 1, dtype=jnp.float32) - HL
    freq_values = jnp.arange(freq_count, dtype=jnp.float32)
    phases = jnp.pi / freq_count * lag_values[:, None] * freq_values[None, :]
    factor = 1.0 / math.sqrt(window_count * freq_count)
    return jnp.stack([jnp.cos(phases) * factor, -jnp.sin(phases) * factor], axis=1).astype(
        jnp.bfloat16
    )


def pair_weights(own_flags, partner_flags):
    return (own_flags[0] * partner_flags[0]).astype(jnp.bfloat16)


def cross_lag(first_spec, second_spec, weights, lag_coeffs):
    freq_count = first_spec.shape[0]
    channel_count = first_spec.shape[3]
    block_len = min(128, freq_count)
    masked = second_spec * weights[None, None, :, None]

    def add_block(step, accum):
        offset = (step * block_len).astype(jnp.int32)
        first_blk = lax.dynamic_slice_in_dim(first_spec, offset, block_len, 0).astype(jnp.float32)
        second_blk = lax.dynamic_slice_in_dim(masked, offset, block_len, 0)
        coeff_blk = lax.dynamic_slice_in_dim(lag_coeffs, offset, block_len, 2).astype(jnp.float32)
        cos_part = coeff_blk[:, 0][:, :, None, None]
        sin_part = coeff_blk[:, 1][:, :, None, None]
        real_in = first_blk[None, :, 0]
        imag_in = first_blk[None, :, 1]
        left_real = cos_part * real_in + sin_part * imag_in
        left_imag = cos_part * imag_in - sin_part * real_in
        left = jnp.stack([left_real, left_imag], axis=2).astype(jnp.bfloat16)
        return accum + jnp.einsum(
            "lfcwi,fcwj->lij", left, second_blk, preferred_element_type=jnp.float32
        )

    start = jnp.zeros((lag_coeffs.shape[0], channel_count, channel_count), jnp.float32)
    return lax.fori_loop(jnp.int32(0), jnp.int32(freq_count // block_len), add_block, start)


def local(spectra, quality):
    devices = lax.axis_size("chan")
    freq_count = spectra.shape[0]
    coeffs = lag_table(freq_count, spectra.shape[2])
    neighbour, neighbour_flags = passed_along((spectra, quality), "chan", -1)
    near_sum = cross_lag(spectra, neighbour, pair_weights(quality, neighbour_flags), coeffs)
    opposite, opposite_flags = passed_along((spectra, quality), "chan", devices // 2)
    far_sum = cross_lag(spectra, opposite, pair_weights(quality, opposite_flags), coeffs)
    return (near_sum.astype(jnp.bfloat16)[None], far_sum.astype(jnp.bfloat16)[None])


def solution(mesh):
    return jax.shard_map(
        local,
        mesh=mesh,
        in_specs=(P(None, None, None, ("grp", "chan")), P(("grp", "chan"), None)),
        out_specs=(P(("grp", "chan"), None, None, None), P(("grp", "chan"), None, None, None)),
        check_vma=False,
    )
```

profile of v0, /device:TPU:0, one launch (start us, length us, event | category | flops | bytes accessed | tf_op | source)
XLA Modules:
  0.0 173.7 jit_solution(12029398885218769035)
XLA Ops:
  0.6 3.3 %copy.4 = bf16[1024,2,4,128]{3,0,2,1:T(8,128)(2,1)} copy(bf16[1024,2,4,128]{3,2,1,0:T(4,128)(2,1)} %param.6) | data formatting | bytes 4194304 | tf_op args[0]
  4.0 5.4 %collective-permute-start = (bf16[1024,2,4,128]{3,0,2,1:T(8,128)(2,1)}, bf16[1024,2,4,128]{3,0,2,1:T(8,128)(2,1)}, u32[]{:S(2)}, u32[]{:S(2)}) collective-permute-start(bf16[1024,2,4,128]{3,0,2,1:T(8,128)(2,1)} %copy.4), channel_id=1, source_target_pairs={{0,15},{1,0},{2,1},{3,2},{4,3},{5,4},{6,5},{7,6},{8,7},{9,8},{10,9... | collective-permute-start | bytes 6291464 | tf_op jit(solution)/shard_map/ppermute | solution.py:14
  10.1 2.9 %collective-permute-start.2 = (bf16[1024,2,4,128]{3,0,2,1:T(8,128)(2,1)}, bf16[1024,2,4,128]{3,0,2,1:T(8,128)(2,1)}, u32[]{:S(2)}, u32[]{:S(2)}) collective-permute-start(bf16[1024,2,4,128]{3,0,2,1:T(8,128)(2,1)} %copy.4), channel_id=1, source_target_pairs={{0,8},{1,9},{2,10},{3,11},{4,12},{5,13},{6,14},{7,15},{8,0},{9,1},... | collective-permute-start | bytes 6291464 | tf_op jit(solution)/shard_map/ppermute | solution.py:14
  13.0 3.1 %copy.5 = bf16[1024,2,4,128]{0,3,2,1:T(8,128)(2,1)} copy(bf16[1024,2,4,128]{3,2,1,0:T(4,128)(2,1)S(1)} %copy-done) | data formatting | bytes 4194304
  17.2 36.5 %collective-permute-done.1 = s32[1,4]{1,0:T(1,128)S(1)} collective-permute-done((s32[1,4]{1,0:T(1,128)S(1)}, s32[1,4]{1,0:T(1,128)S(1)}, u32[]{:S(2)}, u32[]{:S(2)}) %collective-permute-start.1) | collective-permute-done | bytes 48 | tf_op jit(solution)/shard_map/ppermute | solution.py:14
  53.6 43.8 %collective-permute-done.3 = s32[1,4]{1,0:T(1,128)S(1)} collective-permute-done((s32[1,4]{1,0:T(1,128)S(1)}, s32[1,4]{1,0:T(1,128)S(1)}, u32[]{:S(2)}, u32[]{:S(2)}) %collective-permute-start.3) | collective-permute-done | bytes 48 | tf_op jit(solution)/shard_map/ppermute | solution.py:14
  97.4 3.2 %broadcast_multiply_fusion.1 = bf16[1024,2,4,128]{3,0,2,1:T(8,128)(2,1)} fusion(bf16[1024,2,4,128]{3,0,2,1:T(8,128)(2,1)} %collective-permute-done, bf16[4]{0:T(256)(128)(2,1)S(1)} %get-tuple-element.137), kind=kLoop, calls=%fused_computation.37 | loop fusion | flops 1048576 | bytes 4194312 | tf_op jit(solution)/shard_map/mul | solution.py:35
  100.6 34.5 %while.22 = (s32[]{:T(128)}, f32[9,128,128]{2,1,0:T(8,128)S(1)}, bf16[9,2,1024]{2,0,1:T(8,128)(2,1)}, bf16[1024,2,4,128]{0,3,2,1:T(8,128)(2,1)}, bf16[1024,2,4,1...) while((s32[]{:T(128)}, f32[9,128,128]{2,1,0:T(8,128)S(1)}, ...), condition=%wide.region_1.0_spmd.clone, body=%wide.region_0.0_spmd.clone.sunk | while | flops 308316416 | bytes 8561313 | solution.py:54
  107.2 1.9 %fusion.36 = f32[9,128,128]{2,1,0:T(8,128)S(1)} fusion(bf16[9,128,1,4,128]{1,4,3,2,0:T(8,128)(2,1)S(1)} %get-tuple-element.215, bf16[9,128,1,4,128]{1,4,3,2,0:T(8,128)(2,1)S(1)} %get-tuple-element.216, f32[9,128,128]{2,1,0:T(8,128)S(1)} %get-tuple-element.265, pred[]{:T(512)S(6)} %compare.6, bf16[1024,2,4,128]{3,0,2,1:T(8,128)(2,1)} %get-tuple-element.277, ...), kind=kOutput, calls=%fused_computation.7.clone.1 | convolution fusion | flops 303464448 | bytes 3801093 | tf_op jit(solution)/shard_map/while/body/lfcwi,fcwj->lij/dot_general | solution.py:49
  111.6 1.9 %fusion.36 = f32[9,128,128]{2,1,0:T(8,128)S(1)} fusion(bf16[9,128,1,4,128]{1,4,3,2,0:T(8,128)(2,1)S(1)} %get-tuple-element.215, bf16[9,128,1,4,128]{1,4,3,2,0:T(8,128)(2,1)S(1)} %get-tuple-element.216, f32[9,128,128]{2,1,0:T(8,128)S(1)} %get-tuple-element.265, pred[]{:T(512)S(6)} %compare.6, bf16[1024,2,4,128]{3,0,2,1:T(8,128)(2,1)} %get-tuple-element.277, ...), kind=kOutput, calls=%fused_computation.7.clone.1 | convolution fusion | flops 303464448 | bytes 3801093 | tf_op jit(solution)/shard_map/while/body/lfcwi,fcwj->lij/dot_general | solution.py:49
  115.9 1.9 %fusion.36 = f32[9,128,128]{2,1,0:T(8,128)S(1)} fusion(bf16[9,128,1,4,128]{1,4,3,2,0:T(8,128)(2,1)S(1)} %get-tuple-element.215, bf16[9,128,1,4,128]{1,4,3,2,0:T(8,128)(2,1)S(1)} %get-tuple-element.216, f32[9,128,128]{2,1,0:T(8,128)S(1)} %get-tuple-element.265, pred[]{:T(512)S(6)} %compare.6, bf16[1024,2,4,128]{3,0,2,1:T(8,128)(2,1)} %get-tuple-element.277, ...), kind=kOutput, calls=%fused_computation.7.clone.1 | convolution fusion | flops 303464448 | bytes 3801093 | tf_op jit(solution)/shard_map/while/body/lfcwi,fcwj->lij/dot_general | solution.py:49
  120.2 1.9 %fusion.36 = f32[9,128,128]{2,1,0:T(8,128)S(1)} fusion(bf16[9,128,1,4,128]{1,4,3,2,0:T(8,128)(2,1)S(1)} %get-tuple-element.215, bf16[9,128,1,4,128]{1,4,3,2,0:T(8,128)(2,1)S(1)} %get-tuple-element.216, f32[9,128,128]{2,1,0:T(8,128)S(1)} %get-tuple-element.265, pred[]{:T(512)S(6)} %compare.6, bf16[1024,2,4,128]{3,0,2,1:T(8,128)(2,1)} %get-tuple-element.277, ...), kind=kOutput, calls=%fused_computation.7.clone.1 | convolution fusion | flops 303464448 | bytes 3801093 | tf_op jit(solution)/shard_map/while/body/lfcwi,fcwj->lij/dot_general | solution.py:49
  124.5 1.9 %fusion.36 = f32[9,128,128]{2,1,0:T(8,128)S(1)} fusion(bf16[9,128,1,4,128]{1,4,3,2,0:T(8,128)(2,1)S(1)} %get-tuple-element.215, bf16[9,128,1,4,128]{1,4,3,2,0:T(8,128)(2,1)S(1)} %get-tuple-element.216, f32[9,128,128]{2,1,0:T(8,128)S(1)} %get-tuple-element.265, pred[]{:T(512)S(6)} %compare.6, bf16[1024,2,4,128]{3,0,2,1:T(8,128)(2,1)} %get-tuple-element.277, ...), kind=kOutput, calls=%fused_computation.7.clone.1 | convolution fusion | flops 303464448 | bytes 3801093 | tf_op jit(solution)/shard_map/while/body/lfcwi,fcwj->lij/dot_general | solution.py:49
  128.8 1.9 %fusion.36 = f32[9,128,128]{2,1,0:T(8,128)S(1)} fusion(bf16[9,128,1,4,128]{1,4,3,2,0:T(8,128)(2,1)S(1)} %get-tuple-element.215, bf16[9,128,1,4,128]{1,4,3,2,0:T(8,128)(2,1)S(1)} %get-tuple-element.216, f32[9,128,128]{2,1,0:T(8,128)S(1)} %get-tuple-element.265, pred[]{:T(512)S(6)} %compare.6, bf16[1024,2,4,128]{3,0,2,1:T(8,128)(2,1)} %get-tuple-element.277, ...), kind=kOutput, calls=%fused_computation.7.clone.1 | convolution fusion | flops 303464448 | bytes 3801093 | tf_op jit(solution)/shard_map/while/body/lfcwi,fcwj->lij/dot_general | solution.py:49
  133.2 1.9 %fusion.36 = f32[9,128,128]{2,1,0:T(8,128)S(1)} fusion(bf16[9,128,1,4,128]{1,4,3,2,0:T(8,128)(2,1)S(1)} %get-tuple-element.215, bf16[9,128,1,4,128]{1,4,3,2,0:T(8,128)(2,1)S(1)} %get-tuple-element.216, f32[9,128,128]{2,1,0:T(8,128)S(1)} %get-tuple-element.265, pred[]{:T(512)S(6)} %compare.6, bf16[1024,2,4,128]{3,0,2,1:T(8,128)(2,1)} %get-tuple-element.277, ...), kind=kOutput, calls=%fused_computation.7.clone.1 | convolution fusion | flops 303464448 | bytes 3801093 | tf_op jit(solution)/shard_map/while/body/lfcwi,fcwj->lij/dot_general | solution.py:49
  135.1 3.1 %broadcast_multiply_fusion = bf16[1024,2,4,128]{3,0,2,1:T(8,128)(2,1)} fusion(bf16[1024,2,4,128]{3,0,2,1:T(8,128)(2,1)} %collective-permute-done.2, bf16[4]{0:T(256)(128)(2,1)S(1)} %get-tuple-element.136), kind=kLoop, calls=%fused_computation.36 | loop fusion | flops 1048576 | bytes 4194312 | tf_op jit(solution)/shard_map/mul | solution.py:35
  138.2 34.5 %while.23 = (s32[]{:T(128)}, f32[9,128,128]{2,1,0:T(8,128)S(1)}, bf16[9,2,1024]{2,0,1:T(8,128)(2,1)}, bf16[1024,2,4,128]{0,3,2,1:T(8,128)(2,1)}, bf16[1024,2,4,1...) while((s32[]{:T(128)}, f32[9,128,128]{2,1,0:T(8,128)S(1)}, ...), condition=%wide.region_3.0_spmd.clone, body=%wide.region_2.0_spmd.clone.sunk | while | flops 308316416 | bytes 8561313 | solution.py:54
  140.6 1.9 %fusion.39 = f32[9,128,128]{2,1,0:T(8,128)S(1)} fusion(bf16[9,128,1,4,128]{1,4,3,2,0:T(8,128)(2,1)S(1)} %get-tuple-element.226, bf16[9,128,1,4,128]{1,4,3,2,0:T(8,128)(2,1)S(1)} %get-tuple-element.227, f32[9,128,128]{2,1,0:T(8,128)S(1)} %get-tuple-element.238, pred[]{:T(512)S(6)} %compare.7, bf16[1024,2,4,128]{3,0,2,1:T(8,128)(2,1)} %get-tuple-element.250, ...), kind=kOutput, calls=%fused_computation.25.clone.1 | convolution fusion | flops 303464448 | bytes 3801093 | tf_op jit(solution)/shard_map/while/body/lfcwi,fcwj->lij/dot_general | solution.py:49
  149.2 1.9 %fusion.39 = f32[9,128,128]{2,1,0:T(8,128)S(1)} fusion(bf16[9,128,1,4,128]{1,4,3,2,0:T(8,128)(2,1)S(1)} %get-tuple-element.226, bf16[9,128,1,4,128]{1,4,3,2,0:T(8,128)(2,1)S(1)} %get-tuple-element.227, f32[9,128,128]{2,1,0:T(8,128)S(1)} %get-tuple-element.238, pred[]{:T(512)S(6)} %compare.7, bf16[1024,2,4,128]{3,0,2,1:T(8,128)(2,1)} %get-tuple-element.250, ...), kind=kOutput, calls=%fused_computation.25.clone.1 | convolution fusion | flops 303464448 | bytes 3801093 | tf_op jit(solution)/shard_map/while/body/lfcwi,fcwj->lij/dot_general | solution.py:49
  153.6 1.9 %fusion.39 = f32[9,128,128]{2,1,0:T(8,128)S(1)} fusion(bf16[9,128,1,4,128]{1,4,3,2,0:T(8,128)(2,1)S(1)} %get-tuple-element.226, bf16[9,128,1,4,128]{1,4,3,2,0:T(8,128)(2,1)S(1)} %get-tuple-element.227, f32[9,128,128]{2,1,0:T(8,128)S(1)} %get-tuple-element.238, pred[]{:T(512)S(6)} %compare.7, bf16[1024,2,4,128]{3,0,2,1:T(8,128)(2,1)} %get-tuple-element.250, ...), kind=kOutput, calls=%fused_computation.25.clone.1 | convolution fusion | flops 303464448 | bytes 3801093 | tf_op jit(solution)/shard_map/while/body/lfcwi,fcwj->lij/dot_general | solution.py:49
  157.9 1.9 %fusion.39 = f32[9,128,128]{2,1,0:T(8,128)S(1)} fusion(bf16[9,128,1,4,128]{1,4,3,2,0:T(8,128)(2,1)S(1)} %get-tuple-element.226, bf16[9,128,1,4,128]{1,4,3,2,0:T(8,128)(2,1)S(1)} %get-tuple-element.227, f32[9,128,128]{2,1,0:T(8,128)S(1)} %get-tuple-element.238, pred[]{:T(512)S(6)} %compare.7, bf16[1024,2,4,128]{3,0,2,1:T(8,128)(2,1)} %get-tuple-element.250, ...), kind=kOutput, calls=%fused_computation.25.clone.1 | convolution fusion | flops 303464448 | bytes 3801093 | tf_op jit(solution)/shard_map/while/body/lfcwi,fcwj->lij/dot_general | solution.py:49
  162.2 1.9 %fusion.39 = f32[9,128,128]{2,1,0:T(8,128)S(1)} fusion(bf16[9,128,1,4,128]{1,4,3,2,0:T(8,128)(2,1)S(1)} %get-tuple-element.226, bf16[9,128,1,4,128]{1,4,3,2,0:T(8,128)(2,1)S(1)} %get-tuple-element.227, f32[9,128,128]{2,1,0:T(8,128)S(1)} %get-tuple-element.238, pred[]{:T(512)S(6)} %compare.7, bf16[1024,2,4,128]{3,0,2,1:T(8,128)(2,1)} %get-tuple-element.250, ...), kind=kOutput, calls=%fused_computation.25.clone.1 | convolution fusion | flops 303464448 | bytes 3801093 | tf_op jit(solution)/shard_map/while/body/lfcwi,fcwj->lij/dot_general | solution.py:49
  166.5 1.9 %fusion.39 = f32[9,128,128]{2,1,0:T(8,128)S(1)} fusion(bf16[9,128,1,4,128]{1,4,3,2,0:T(8,128)(2,1)S(1)} %get-tuple-element.226, bf16[9,128,1,4,128]{1,4,3,2,0:T(8,128)(2,1)S(1)} %get-tuple-element.227, f32[9,128,128]{2,1,0:T(8,128)S(1)} %get-tuple-element.238, pred[]{:T(512)S(6)} %compare.7, bf16[1024,2,4,128]{3,0,2,1:T(8,128)(2,1)} %get-tuple-element.250, ...), kind=kOutput, calls=%fused_computation.25.clone.1 | convolution fusion | flops 303464448 | bytes 3801093 | tf_op jit(solution)/shard_map/while/body/lfcwi,fcwj->lij/dot_general | solution.py:49
  170.8 1.9 %fusion.39 = f32[9,128,128]{2,1,0:T(8,128)S(1)} fusion(bf16[9,128,1,4,128]{1,4,3,2,0:T(8,128)(2,1)S(1)} %get-tuple-element.226, bf16[9,128,1,4,128]{1,4,3,2,0:T(8,128)(2,1)S(1)} %get-tuple-element.227, f32[9,128,128]{2,1,0:T(8,128)S(1)} %get-tuple-element.238, pred[]{:T(512)S(6)} %compare.7, bf16[1024,2,4,128]{3,0,2,1:T(8,128)(2,1)} %get-tuple-element.250, ...), kind=kOutput, calls=%fused_computation.25.clone.1 | convolution fusion | flops 303464448 | bytes 3801093 | tf_op jit(solution)/shard_map/while/body/lfcwi,fcwj->lij/dot_general | solution.py:49
  (97 shorter events, 44.1 us)
Async XLA Ops:
  0.6 12.4 %copy-start = (bf16[1024,2,4,128]{3,2,1,0:T(4,128)(2,1)S(1)}, bf16[1024,2,4,128]{3,2,1,0:T(4,128)(2,1)}, u32[]{:S(2)}) copy-start(bf16[1024,2,4,128]{3,2,1,0:T(4,128)(2,1)} %param.6) | copy-start | bytes 6291460
  0.6 8.8 %copy-start.1 = (s32[1,4]{1,0:T(1,128)S(1)}, s32[1,4]{1,0:T(1,128)}, u32[]{:S(2)}) copy-start(s32[1,4]{1,0:T(1,128)} %param.7) | copy-start | bytes 52
  4.0 93.4 %collective-permute-start = (bf16[1024,2,4,128]{3,0,2,1:T(8,128)(2,1)}, bf16[1024,2,4,128]{3,0,2,1:T(8,128)(2,1)}, u32[]{:S(2)}, u32[]{:S(2)}) collective-permute-start(bf16[1024,2,4,128]{3,0,2,1:T(8,128)(2,1)} %copy.4), channel_id=1, source_target_pairs={{0,15},{1,0},{2,1},{3,2},{4,3},{5,4},{6,5},{7,6},{8,7},{9,8},{10,9... | collective-permute-start | bytes 6291464 | tf_op jit(solution)/shard_map/ppermute | solution.py:14
  9.4 44.2 %collective-permute-start.1 = (s32[1,4]{1,0:T(1,128)S(1)}, s32[1,4]{1,0:T(1,128)S(1)}, u32[]{:S(2)}, u32[]{:S(2)}) collective-permute-start(s32[1,4]{1,0:T(1,128)S(1)} %copy-done.1), channel_id=1, source_target_pairs={{0,15},{1,0},{2,1},{3,2},{4,3},{5,4},{6,5},{7,6},{8,7},{9,8},{10,9... | collective-permute-start | bytes 56 | tf_op jit(solution)/shard_map/ppermute | solution.py:14
  10.1 87.3 %collective-permute-start.3 = (s32[1,4]{1,0:T(1,128)S(1)}, s32[1,4]{1,0:T(1,128)S(1)}, u32[]{:S(2)}, u32[]{:S(2)}) collective-permute-start(s32[1,4]{1,0:T(1,128)S(1)} %copy-done.1), channel_id=1, source_target_pairs={{0,8},{1,9},{2,10},{3,11},{4,12},{5,13},{6,14},{7,15},{8,0},{9,1},... | collective-permute-start | bytes 56 | tf_op jit(solution)/shard_map/ppermute | solution.py:14
  10.1 125.0 %collective-permute-start.2 = (bf16[1024,2,4,128]{3,0,2,1:T(8,128)(2,1)}, bf16[1024,2,4,128]{3,0,2,1:T(8,128)(2,1)}, u32[]{:S(2)}, u32[]{:S(2)}) collective-permute-start(bf16[1024,2,4,128]{3,0,2,1:T(8,128)(2,1)} %copy.4), channel_id=1, source_target_pairs={{0,8},{1,9},{2,10},{3,11},{4,12},{5,13},{6,14},{7,15},{8,0},{9,1},... | collective-permute-start | bytes 6291464 | tf_op jit(solution)/shard_map/ppermute | solution.py:14
where the time goes:
time: 176 us; the launch traced here: 174 us
  waiting for transfers between devices  80.2 us (46%)
  other arithmetic  45.2 us (26%)
  matrix products  30.7 us (17%)
  starting transfers between devices  9.04 us (5%)
  local copies, waits for them, and re-layouts  7.15 us (4%)
    ppermute x4, waiting for transfers between devices, passed_along(): return lax.ppermute(value, axis, pairs)  80.2 us
    dot_general x16, matrix products, add_block(): jnp.einsum('lfcwi,fcwj->lij', left, second_blk, preferred_element_type=jn...  30.7 us
    convert_element_type x16, other arithmetic, add_block(): lax.dynamic_slice_in_dim(first_spec, offset, block_len, 0)  15.8 us
    convert_element_type x16, other arithmetic, add_block(): lax.dynamic_slice_in_dim(lag_coeffs, offset, block_len, 2)  11.3 us
    another operation x17, other arithmetic  10.1 us
    ppermute x4, starting transfers between devices, passed_along(): return lax.ppermute(value, axis, pairs)  9.04 us
    unnamed x6, local copies, waits for them, and re-layouts  6.48 us
    mul x2, other arithmetic, cross_lag(): masked = second_spec * weights[None, None, :, None]  6.28 us
  transfers between devices with their start and end apart: 4, of which 2 were waited for; matrix products, arithmetic and copies ran while one was open for 24% of the time, Pallas kernels for 0%

commit v1 on v0

v1 whole, which is shorter than its diff:
```python
import functools
import math

import jax
import jax.numpy as jnp
from jax import lax
from jax.experimental import pallas as pl
from jax.experimental.pallas import tpu as pltpu
from jax.sharding import PartitionSpec as P

HL = 4
LAGS = 2 * HL + 1
STEP = 1024
PARTS = 4


def goes_down(pair, half):
    return pair == 0 or pair == half - 1 or (pair % 2 == 1 and pair != 1)


def lag_rows(freq_count, window_count):
    per_bin = 2 * window_count
    row = jnp.arange(freq_count * per_bin, dtype=jnp.int32)
    freq_values = (row // per_bin).astype(jnp.float32)
    sign = jnp.where(row % per_bin < window_count, 1.0, -1.0)
    lag_values = jnp.arange(HL + 1, dtype=jnp.float32)
    phases = jnp.pi / freq_count * lag_values[:, None] * freq_values[None, :]
    factor = 1.0 / math.sqrt(window_count * freq_count)
    cos_part = jnp.cos(phases) * factor
    sin_part = -jnp.sin(phases[1:]) * factor * sign[None, :]
    return jnp.concatenate([cos_part, sin_part], axis=0).astype(jnp.bfloat16)


def turn_kernel(x_ref, plain_ref, swapped_ref):
    x = x_ref[...].astype(jnp.float32)
    rows, cols = x.shape
    swapped = pltpu.roll(x.reshape(rows // 8, 8, cols), 4, 1).reshape(rows, cols)
    plain_ref[...] = x.T.astype(jnp.bfloat16)
    swapped_ref[...] = swapped.T.astype(jnp.bfloat16)


def turn(x):
    rows, cols = x.shape
    out = jax.ShapeDtypeStruct((cols, rows), jnp.bfloat16)
    return pl.pallas_call(
        turn_kernel,
        grid=(rows // STEP,),
        in_specs=[pl.BlockSpec((STEP, cols), lambda s: (s, 0))],
        out_specs=[pl.BlockSpec((cols, STEP), lambda s: (0, s))] * 2,
        out_shape=[out, out],
        compiler_params=pltpu.CompilerParams(vmem_limit_bytes=32 * 1024 * 1024),
        cost_estimate=pl.CostEstimate(flops=0, bytes_accessed=6 * rows * cols, transcendentals=0),
        name="turn",
    )(x)


def corr_kernel(first, last, mirrored, flag_ref, plain_ref, swapped_ref, coeff_ref, partner_ref, weight_ref, *rest):
    acc_in = None if first else rest[0]
    outs = rest if first else rest[1:]
    scratch = outs[-1]
    outs = outs[:-1]
    if last:
        acc = outs[-1]
        outs = outs[:-1]
    else:
        acc = outs[0]
    step = pl.program_id(0)
    cols = partner_ref.shape[1]

    @pl.when(step == 0)
    def _():
        if first:
            acc[...] = jnp.zeros_like(acc)
        else:
            acc[...] = acc_in[...]

    for k in range(HL + 1):
        scratch[k * cols:(k + 1) * cols, :] = plain_ref[...] * coeff_ref[k:k + 1, :]
    for k in range(HL + 1, LAGS):
        scratch[k * cols:(k + 1) * cols, :] = swapped_ref[...] * coeff_ref[k:k + 1, :]
    rows = partner_ref.shape[0]
    weights = jnp.broadcast_to(weight_ref[...][None], (rows // 16, 16, cols)).reshape(rows, cols)
    acc[...] += jnp.dot(scratch[...], partner_ref[...] * weights, preferred_element_type=jnp.float32)

    if last:
        @pl.when(step == pl.num_programs(0) - 1)
        def _():
            def result(lag):
                k = abs(lag - HL)
                even = acc[k * cols:(k + 1) * cols, :]
                if k == 0:
                    return even
                odd = acc[(HL + k) * cols:(HL + k + 1) * cols, :]
                return even + odd if lag > HL else even - odd

            if mirrored == "both":
                for lag in range(LAGS):
                    value = result(lag)
                    outs[0][lag] = value.astype(jnp.bfloat16)
                    outs[1][LAGS - 1 - lag] = value.T.astype(jnp.bfloat16)
            elif mirrored == "no":
                for lag in range(LAGS):
                    outs[0][lag] = result(lag).astype(jnp.bfloat16)
            else:
                @pl.when(flag_ref[0] == 0)
                def _():
                    for lag in range(LAGS):
                        outs[0][lag] = result(lag).astype(jnp.bfloat16)

                @pl.when(flag_ref[0] != 0)
                def _():
                    for lag in range(LAGS):
                        outs[0][LAGS - 1 - lag] = result(lag).T.astype(jnp.bfloat16)


def corr(turned, coeffs, partner, start, weights, flag, acc, last, mirrored, name):
    plain, swapped = turned
    cols = plain.shape[0]
    rows = partner.shape[0]
    first = acc is None
    skip = start // STEP
    acc_shape = jax.ShapeDtypeStruct((LAGS * cols, cols), jnp.float32)
    acc_spec = pl.BlockSpec((LAGS * cols, cols), lambda s: (0, 0))
    res_shape = jax.ShapeDtypeStruct((LAGS, cols, cols), jnp.bfloat16)
    res_spec = pl.BlockSpec((LAGS, cols, cols), lambda s: (0, 0, 0))
    in_specs = [
        pl.BlockSpec(memory_space=pltpu.SMEM),
        pl.BlockSpec((cols, STEP), lambda s: (0, s + skip)),
        pl.BlockSpec((cols, STEP), lambda s: (0, s + skip)),
        pl.BlockSpec((LAGS, STEP), lambda s: (0, s + skip)),
        pl.BlockSpec((STEP, cols), lambda s: (s, 0)),
        pl.BlockSpec((16, cols), lambda s: (0, 0)),
    ]
    args = [flag, plain, swapped, coeffs, partner, weights]
    if not first:
        in_specs.append(acc_spec)
        args.append(acc)
    scratch = [pltpu.VMEM((LAGS * cols, STEP), jnp.bfloat16)]
    if last:
        count = 2 if mirrored == "both" else 1
        out_shape, out_specs = [res_shape] * count, [res_spec] * count
        scratch = [pltpu.VMEM((LAGS * cols, cols), jnp.float32)] + scratch
    else:
        out_shape, out_specs = [acc_shape], [acc_spec]
    return pl.pallas_call(
        functools.partial(corr_kernel, first, last, mirrored),
        grid=(rows // STEP,),
        in_specs=in_specs,
        out_specs=out_specs,
        out_shape=out_shape,
        scratch_shapes=scratch,
        compiler_params=pltpu.CompilerParams(vmem_limit_bytes=32 * 1024 * 1024),
        cost_estimate=pl.CostEstimate(
            flops=2 * LAGS * cols * cols * rows, bytes_accessed=6 * rows * cols, transcendentals=0
        ),
        name=name,
    )(*args)


def row_weights(own_flags, partner_flags, cols):
    both = (own_flags * partner_flags).astype(jnp.bfloat16)
    return jnp.broadcast_to(jnp.tile(both, 16 // both.shape[0])[:, None], (16, cols))


def local(spectra, quality):
    count = lax.axis_size("chan")
    half = count // 2
    me = lax.axis_index("chan")
    freq_count, _, window_count, cols = spectra.shape
    block = spectra.reshape(-1, cols)
    rows = block.shape[0]

    down = [goes_down(p, half) for p in range(half)]
    far_pairs = [(p + half, p) if d else (p, p + half) for p, d in enumerate(down)]
    back_pairs = [(p, p + half) if d else (p + half, p) for p, d in enumerate(down)]
    near_pairs = [(d + 1, d) for d in range(count - 1) if d != half - 1]
    swap_pairs = [(0, half - 1), (half - 1, 0)]
    side_pairs = [(0, half - 1), (half - 1, count - 1)]

    piece = rows // PARTS
    far_in = [lax.ppermute(block[s * piece:(s + 1) * piece], "chan", far_pairs) for s in range(PARTS)]
    near_in = lax.ppermute(block, "chan", near_pairs)
    swap_in = lax.ppermute(block, "chan", swap_pairs)

    flags = lax.all_gather(quality[0], "chan")
    near_at = lax.rem(me + 1, count)
    far_at = lax.rem(me + half, count)
    swap_at = jnp.where(me == 0, half - 1, 0)

    def flags_of(at):
        return lax.dynamic_index_in_dim(flags, at, 0, keepdims=False)

    near_w = row_weights(quality[0], flags_of(near_at), cols)
    far_w = row_weights(quality[0], flags_of(far_at), cols)
    side_w = row_weights(flags_of(swap_at), flags_of(far_at), cols)

    coeffs = lag_rows(freq_count, window_count)
    turned = turn(block)
    swap_turned = turn(swap_in)
    flag = (me == half - 1).astype(jnp.int32).reshape(1)

    near_own, = corr(turned, coeffs, near_in, 0, near_w, flag, None, True, "no", "near_corr")
    far_acc = side_acc = None
    for s in range(PARTS - 1):
        far_acc, = corr(turned, coeffs, far_in[s], s * piece, far_w, flag, far_acc, False, "no", "far_part")
        side_acc, = corr(swap_turned, coeffs, far_in[s], s * piece, side_w, flag, side_acc, False, "no", "side_part")
    at = (PARTS - 1) * piece
    far_own, far_mirror = corr(turned, coeffs, far_in[-1], at, far_w, flag, far_acc, True, "both", "far_last")
    side_own, = corr(swap_turned, coeffs, far_in[-1], at, side_w, flag, side_acc, True, "flag", "side_last")

    far_back = lax.ppermute(far_mirror, "chan", back_pairs)
    side_back = lax.ppermute(side_own, "chan", side_pairs)

    is_down = jnp.asarray(down)[lax.rem(me, half)]
    hosts = is_down == (me < half)
    far = jnp.where(hosts, far_own, far_back)
    near = jnp.where((me == half - 1) | (me == count - 1), side_back, near_own)
    return near[None], far[None]


def solution(mesh):
    return jax.shard_map(
        local,
        mesh=mesh,
        in_specs=(P(None, None, None, ("grp", "chan")), P(("grp", "chan"), None)),
        out_specs=(P(("grp", "chan"), None, None, None), P(("grp", "chan"), None, None, None)),
        check_vma=False,
    )
```

time: 176 us -> 125 us (0.71)
  the two profiles are of different devices: /device:TPU:0 before, /device:TPU:1 now
where the time goes in v1:
time: 125 us; the launch traced here: 123 us
  Pallas kernels  33.8 us (27%)
  waiting for transfers between devices  27.4 us (22%)
  blocking collectives  26 us (21%)
  starting transfers between devices  20.7 us (17%)
  local copies, waits for them, and re-layouts  9.57 us (8%)
  other arithmetic  4.42 us (4%)
  between operations  1.48 us (1%)
    ppermute x4, waiting for transfers between devices, local(): lax.ppermute(block[s * piece:(s + 1) * piece], 'chan', far_pairs)  27.3 us
    pallas_call x9, Pallas kernels, corr(): pl.pallas_call(functools.partial(corr_kernel, first, last, mirrored), gri...  26.7 us
    all_gather x1, blocking collectives, local(): flags = lax.all_gather(quality[0], 'chan')  26 us
    ppermute x4, starting transfers between devices, local(): lax.ppermute(block[s * piece:(s + 1) * piece], 'chan', far_pairs)  11.4 us
    pallas_call x2, Pallas kernels, turn(): pl.pallas_call(turn_kernel, grid=(rows // STEP,), in_specs=[pl.BlockSpec(...  7.04 us
    ppermute x1, starting transfers between devices, local(): near_in = lax.ppermute(block, 'chan', near_pairs)  5.33 us
    unnamed x16, local copies, waits for them, and re-layouts  5.26 us
    slice x1, local copies, waits for them, and re-layouts, local(): block[s * piece:(s + 1) * piece]  3.27 us
  transfers between devices with their start and end apart: 8, of which 1 were waited for; matrix products, arithmetic and copies ran while one was open for 6% of the time, Pallas kernels for 27%

profile of v1, /device:TPU:1, one launch (start us, length us, event | category | flops | bytes accessed | tf_op | source)
XLA Modules:
  0.0 123.2 jit_solution(12823636505557595619)
XLA Ops:
  0.6 2.0 %collective-permute-start = (bf16[8192,128]{1,0:T(8,128)(2,1)}, bf16[8192,128]{1,0:T(8,128)(2,1)}, u32[]{:S(2)}, u32[]{:S(2)}) collective-permute-start(bf16[8192,128]{1,0:T(8,128)(2,1)} %bitcast.40), channel_id=1, source_target_pairs={{0,7},{7,0},{16,23},{23,16}} | collective-permute-start | bytes 6291464 | tf_op jit(solution)/shard_map/ppermute | solution.py:183
  2.6 5.3 %collective-permute-start.6 = (bf16[8192,128]{1,0:T(8,128)(2,1)}, bf16[8192,128]{1,0:T(8,128)(2,1)}, u32[]{:S(2)}, u32[]{:S(2)}) collective-permute-start(bf16[8192,128]{1,0:T(8,128)(2,1)} %bitcast.41), channel_id=1, source_target_pairs={{1,0},{2,1},{3,2},{4,3},{5,4},{6,5},{7,6},{9,8},{10,9},{11,10},{12... | collective-permute-start | bytes 6291464 | tf_op jit(solution)/shard_map/ppermute | solution.py:182
  7.9 3.3 %fusion.21 = (bf16[256,2,4,128]{3,2,1,0:T(4,128)(2,1)S(1)}, bf16[256,2,4,128]{3,2,1,0:T(4,128)(2,1)}, bf16[256,2,4,128]{3,2,1,0:T(4,128)(2,1)}, bf16[256,2,4,128]{3,2,1,0:T(4,128)(2,1)}) fusion(bf16[1024,2,4,128]{3,2,1,0:T(4,128)(2,1)} %param.3), kind=kLoop, calls=%fused_computation.37 | loop fusion | bytes 4194304 | tf_op jit(solution)/shard_map/slice | solution.py:181
  11.2 2.4 %collective-permute-start.1 = (bf16[2048,128]{1,0:T(8,128)(2,1)}, bf16[2048,128]{1,0:T(8,128)(2,1)S(1)}, u32[]{:S(2)}, u32[]{:S(2)}) collective-permute-start(bf16[2048,128]{1,0:T(8,128)(2,1)} %bitcast.2), channel_id=1, source_target_pairs={{8,0},{1,9},{2,10},{11,3},{4,12},{13,5},{6,14},{15,7},{24,16},{17,... | collective-permute-start | bytes 1572872 | tf_op jit(solution)/shard_map/ppermute | solution.py:181
  13.7 2.1 %collective-permute-start.2 = (bf16[2048,128]{1,0:T(8,128)(2,1)}, bf16[2048,128]{1,0:T(8,128)(2,1)}, u32[]{:S(2)}, u32[]{:S(2)}) collective-permute-start(bf16[2048,128]{1,0:T(8,128)(2,1)} %bitcast.7), channel_id=1, source_target_pairs={{8,0},{1,9},{2,10},{11,3},{4,12},{13,5},{6,14},{15,7},{24,16},{17,... | collective-permute-start | bytes 1572872 | tf_op jit(solution)/shard_map/ppermute | solution.py:181
  15.8 1.3 %collective-permute-start.4 = (bf16[2048,128]{1,0:T(8,128)(2,1)S(1)}, bf16[2048,128]{1,0:T(8,128)(2,1)S(1)}, u32[]{:S(2)}, u32[]{:S(2)}) collective-permute-start(bf16[2048,128]{1,0:T(8,128)(2,1)S(1)} %bitcast.43), channel_id=1, source_target_pairs={{8,0},{1,9},{2,10},{11,3},{4,12},{13,5},{6,14},{15,7},{24,16},{17,... | collective-permute-start | bytes 1572872 | tf_op jit(solution)/shard_map/ppermute | solution.py:181
  18.9 27.3 %collective-permute-done.4.partner_ref = bf16[2048,128]{1,0:T(8,128)(2,1)S(1)} collective-permute-done((bf16[2048,128]{1,0:T(8,128)(2,1)S(1)}, bf16[2048,128]{1,0:T(8,128)(2,1)S(1)}, u32[]{:S(2)}, u32[]{:S(2)}) %collective-permute-start.4) | collective-permute-done | bytes 524320 | tf_op jit(solution)/shard_map/ppermute | solution.py:181
  46.3 5.6 %collective-permute-start.3 = (bf16[2048,128]{1,0:T(8,128)(2,1)}, bf16[2048,128]{1,0:T(8,128)(2,1)}, u32[]{:S(2)}, u32[]{:S(2)}) collective-permute-start(bf16[2048,128]{1,0:T(8,128)(2,1)} %bitcast.8), channel_id=1, source_target_pairs={{8,0},{1,9},{2,10},{11,3},{4,12},{13,5},{6,14},{15,7},{24,16},{17,... | collective-permute-start | bytes 1572872 | tf_op jit(solution)/shard_map/ppermute | solution.py:181
  52.0 1.6 %copy-done.3 = bf16[1024,2,4,128]{3,2,1,0:T(4,128)(2,1)S(1)} copy-done((bf16[1024,2,4,128]{3,2,1,0:T(4,128)(2,1)S(1)}, bf16[1024,2,4,128]{3,2,1,0:T(4,128)(2,1)}, u32[]{:S(2)}) %copy-start.3) | copy-done | bytes 2097176
  53.5 1.9 %turn.3 = (bf16[128,8192]{1,0:T(8,128)(2,1)S(1)}, bf16[128,8192]{1,0:T(8,128)(2,1)S(1)}) custom-call(bf16[8192,128]{1,0:T(8,128)(2,1)S(1)} %bitcast.42), custom_call_target="tpu_custom_call" | custom-call | bytes 6291456 | tf_op jit(solution)/shard_map/turn/pallas_call | solution.py:45
  55.5 1.3 %copy-done = bf16[128,8192]{1,0:T(8,128)(2,1)} copy-done((bf16[128,8192]{1,0:T(8,128)(2,1)}, bf16[128,8192]{1,0:T(8,128)(2,1)S(1)}, u32[]{:S(2)}) %copy-start) | copy-done | bytes 2097176
  56.8 26.0 %all-gather = s32[16,1,4]{2,1,0:T(1,128)S(1)} all-gather(s32[1,1,4]{2,1,0:T(1,128)S(1)} %bitcast.44), channel_id=1, replica_groups=mesh['grp'=2,'chan'=16] {'chan'}, dimensions={0}, use_global_device_ids=true | all-gather | bytes 272 | tf_op jit(solution)/shard_map/all_gather | solution.py:185
  83.0 1.6 %copy-done.1 = bf16[128,8192]{1,0:T(8,128)(2,1)S(1)} copy-done((bf16[128,8192]{1,0:T(8,128)(2,1)S(1)}, bf16[128,8192]{1,0:T(8,128)(2,1)}, u32[]{:S(2)}) %copy-start.1) | copy-done | bytes 2097176
  84.6 1.7 %far_part.3.rest_0_ = f32[1152,128]{1,0:T(8,128)S(1)} custom-call(s32[1]{0:T(128)} %bitcast.flag_ref, bf16[128,8192]{1,0:T(8,128)(2,1)S(1)} %get-tuple-element.10.plain_ref, bf16[128,8192]{1,0:T(8,128)(2,1)S(1)} %copy-done.1, bf16[9,8192]{1,0:T(8,128)(2,1)S(1)} %pad_maximum_fusion.coeff_ref, bf16[2048,128]{1,0:T(8,128)(2,1)S(1)} %collective-permute-done.4.partner_ref, ...), custom_call_target="tpu_custom_call" | custom-call | flops 603979776 | bytes 1572864 | tf_op jit(solution)/shard_map/far_part/pallas_call | solution.py:145
  86.4 2.7 %far_part.4.rest_0_ = f32[1152,128]{1,0:T(8,128)S(1)} custom-call(s32[1]{0:T(128)} %bitcast.flag_ref, bf16[128,8192]{1,0:T(8,128)(2,1)S(1)} %get-tuple-element.10.plain_ref, bf16[128,8192]{1,0:T(8,128)(2,1)S(1)} %copy-done.1, bf16[9,8192]{1,0:T(8,128)(2,1)S(1)} %pad_maximum_fusion.coeff_ref, bf16[2048,128]{1,0:T(8,128)(2,1)} %collective-permute-done.3.partner_ref, ...), custom_call_target="tpu_custom_call" | custom-call | flops 603979776 | bytes 1572864 | tf_op jit(solution)/shard_map/far_part/pallas_call | solution.py:145
  89.1 2.7 %far_part.5.rest_0_ = f32[1152,128]{1,0:T(8,128)S(1)} custom-call(s32[1]{0:T(128)} %bitcast.flag_ref, bf16[128,8192]{1,0:T(8,128)(2,1)S(1)} %get-tuple-element.10.plain_ref, bf16[128,8192]{1,0:T(8,128)(2,1)S(1)} %copy-done.1, bf16[9,8192]{1,0:T(8,128)(2,1)S(1)} %pad_maximum_fusion.coeff_ref, bf16[2048,128]{1,0:T(8,128)(2,1)} %collective-permute-done.2.partner_ref, ...), custom_call_target="tpu_custom_call" | custom-call | flops 603979776 | bytes 1572864 | tf_op jit(solution)/shard_map/far_part/pallas_call | solution.py:145
  91.8 2.6 %far_last.1 = (bf16[9,128,128]{2,1,0:T(8,128)(2,1)S(1)}, bf16[9,128,128]{2,1,0:T(8,128)(2,1)}) custom-call(s32[1]{0:T(128)} %bitcast.flag_ref, bf16[128,8192]{1,0:T(8,128)(2,1)S(1)} %get-tuple-element.10.plain_ref, bf16[128,8192]{1,0:T(8,128)(2,1)S(1)} %copy-done.1, bf16[9,8192]{1,0:T(8,128)(2,1)S(1)} %pad_maximum_fusion.coeff_ref, ...), custom_call_target="tpu_custom_call" | custom-call | flops 603979776 | bytes 1572864 | tf_op jit(solution)/shard_map/far_last/pallas_call | solution.py:145
  97.7 5.1 %turn.2 = (bf16[128,8192]{1,0:T(8,128)(2,1)S(1)}, bf16[128,8192]{1,0:T(8,128)(2,1)S(1)}) custom-call(bf16[8192,128]{1,0:T(8,128)(2,1)} %collective-permute-done.x_ref), custom_call_target="tpu_custom_call" | custom-call | bytes 6291456 | tf_op jit(solution)/shard_map/turn/pallas_call | solution.py:45
  102.9 1.7 %side_part.3.rest_0_ = f32[1152,128]{1,0:T(8,128)S(1)} custom-call(s32[1]{0:T(128)} %bitcast.flag_ref, bf16[128,8192]{1,0:T(8,128)(2,1)S(1)} %get-tuple-element.8.plain_ref, bf16[128,8192]{1,0:T(8,128)(2,1)S(1)} %get-tuple-element.9.swapped_ref, bf16[9,8192]{1,0:T(8,128)(2,1)S(1)} %pad_maximum_fusion.coeff_ref, ...), custom_call_target="tpu_custom_call" | custom-call | flops 603979776 | bytes 1572864 | tf_op jit(solution)/shard_map/side_part/pallas_call | solution.py:145
  104.7 2.7 %side_part.4.rest_0_ = f32[1152,128]{1,0:T(8,128)S(1)} custom-call(s32[1]{0:T(128)} %bitcast.flag_ref, bf16[128,8192]{1,0:T(8,128)(2,1)S(1)} %get-tuple-element.8.plain_ref, bf16[128,8192]{1,0:T(8,128)(2,1)S(1)} %get-tuple-element.9.swapped_ref, bf16[9,8192]{1,0:T(8,128)(2,1)S(1)} %pad_maximum_fusion.coeff_ref, ...), custom_call_target="tpu_custom_call" | custom-call | flops 603979776 | bytes 1572864 | tf_op jit(solution)/shard_map/side_part/pallas_call | solution.py:145
  107.3 2.7 %side_part.5.rest_0_ = f32[1152,128]{1,0:T(8,128)S(1)} custom-call(s32[1]{0:T(128)} %bitcast.flag_ref, bf16[128,8192]{1,0:T(8,128)(2,1)S(1)} %get-tuple-element.8.plain_ref, bf16[128,8192]{1,0:T(8,128)(2,1)S(1)} %get-tuple-element.9.swapped_ref, bf16[9,8192]{1,0:T(8,128)(2,1)S(1)} %pad_maximum_fusion.coeff_ref, ...), custom_call_target="tpu_custom_call" | custom-call | flops 603979776 | bytes 1572864 | tf_op jit(solution)/shard_map/side_part/pallas_call | solution.py:145
  110.0 1.8 %side_last.1 = bf16[9,128,128]{2,1,0:T(8,128)(2,1)S(1)} custom-call(s32[1]{0:T(128)} %bitcast.flag_ref, bf16[128,8192]{1,0:T(8,128)(2,1)S(1)} %get-tuple-element.8.plain_ref, bf16[128,8192]{1,0:T(8,128)(2,1)S(1)} %get-tuple-element.9.swapped_ref, bf16[9,8192]{1,0:T(8,128)(2,1)S(1)} %pad_maximum_fusion.coeff_ref, ...), custom_call_target="tpu_custom_call" | custom-call | flops 603979776 | bytes 1572864 | tf_op jit(solution)/shard_map/side_last/pallas_call | solution.py:145
  112.5 1.7 %select_bitcast_fusion = bf16[1,9,128,128]{3,2,1,0:T(8,128)(2,1)} fusion(bf16[9,128,128]{2,1,0:T(8,128)(2,1)S(1)} %copy-done.5, bf16[9,128,128]{2,1,0:T(8,128)(2,1)} %collective-permute-done.7, pred[]{:T(512)S(6)} %eq.18), kind=kLoop, calls=%fused_computation | loop fusion | flops 147456 | bytes 884737 | tf_op jit(solution)/shard_map/broadcast_in_dim | solution.py:218
  114.3 8.1 %near_corr.1 = bf16[9,128,128]{2,1,0:T(8,128)(2,1)S(1)} custom-call(s32[1]{0:T(128)} %bitcast.flag_ref, bf16[128,8192]{1,0:T(8,128)(2,1)S(1)} %get-tuple-element.10.plain_ref, bf16[128,8192]{1,0:T(8,128)(2,1)S(1)} %copy-done.2, bf16[9,8192]{1,0:T(8,128)(2,1)S(1)} %pad_maximum_fusion.coeff_ref, bf16[8192,128]{1,0:T(8,128)(2,1)} %collective-permute-done.6.partner_ref, ...), custom_call_target="tpu_custom_call" | custom-call | flops 2415919104 | bytes 6291456 | tf_op jit(solution)/shard_map/near_corr/pallas_call | solution.py:145
  (40 shorter events, 6.5 us)
Async XLA Ops:
  0.6 97.1 %collective-permute-start = (bf16[8192,128]{1,0:T(8,128)(2,1)}, bf16[8192,128]{1,0:T(8,128)(2,1)}, u32[]{:S(2)}, u32[]{:S(2)}) collective-permute-start(bf16[8192,128]{1,0:T(8,128)(2,1)} %bitcast.40), channel_id=1, source_target_pairs={{0,7},{7,0},{16,23},{23,16}} | collective-permute-start | bytes 6291464 | tf_op jit(solution)/shard_map/ppermute | solution.py:183
  2.6 111.7 %collective-permute-start.6 = (bf16[8192,128]{1,0:T(8,128)(2,1)}, bf16[8192,128]{1,0:T(8,128)(2,1)}, u32[]{:S(2)}, u32[]{:S(2)}) collective-permute-start(bf16[8192,128]{1,0:T(8,128)(2,1)} %bitcast.41), channel_id=1, source_target_pairs={{1,0},{2,1},{3,2},{4,3},{5,4},{6,5},{7,6},{9,8},{10,9},{11,10},{12... | collective-permute-start | bytes 6291464 | tf_op jit(solution)/shard_map/ppermute | solution.py:182
  11.2 45.6 %copy-start.6 = (s32[1,4]{1,0:T(1,128)S(1)}, s32[1,4]{1,0:T(1,128)}, u32[]{:S(2)}) copy-start(s32[1,4]{1,0:T(1,128)} %param.4) | copy-start | bytes 52
  11.2 80.5 %collective-permute-start.1 = (bf16[2048,128]{1,0:T(8,128)(2,1)}, bf16[2048,128]{1,0:T(8,128)(2,1)S(1)}, u32[]{:S(2)}, u32[]{:S(2)}) collective-permute-start(bf16[2048,128]{1,0:T(8,128)(2,1)} %bitcast.2), channel_id=1, source_target_pairs={{8,0},{1,9},{2,10},{11,3},{4,12},{13,5},{6,14},{15,7},{24,16},{17,... | collective-permute-start | bytes 1572872 | tf_op jit(solution)/shard_map/ppermute | solution.py:181
  13.7 75.4 %collective-permute-start.2 = (bf16[2048,128]{1,0:T(8,128)(2,1)}, bf16[2048,128]{1,0:T(8,128)(2,1)}, u32[]{:S(2)}, u32[]{:S(2)}) collective-permute-start(bf16[2048,128]{1,0:T(8,128)(2,1)} %bitcast.7), channel_id=1, source_target_pairs={{8,0},{1,9},{2,10},{11,3},{4,12},{13,5},{6,14},{15,7},{24,16},{17,... | collective-permute-start | bytes 1572872 | tf_op jit(solution)/shard_map/ppermute | solution.py:181
  15.8 30.5 %collective-permute-start.4 = (bf16[2048,128]{1,0:T(8,128)(2,1)S(1)}, bf16[2048,128]{1,0:T(8,128)(2,1)S(1)}, u32[]{:S(2)}, u32[]{:S(2)}) collective-permute-start(bf16[2048,128]{1,0:T(8,128)(2,1)S(1)} %bitcast.43), channel_id=1, source_target_pairs={{8,0},{1,9},{2,10},{11,3},{4,12},{13,5},{6,14},{15,7},{24,16},{17,... | collective-permute-start | bytes 1572872 | tf_op jit(solution)/shard_map/ppermute | solution.py:181
  46.3 40.1 %collective-permute-start.3 = (bf16[2048,128]{1,0:T(8,128)(2,1)}, bf16[2048,128]{1,0:T(8,128)(2,1)}, u32[]{:S(2)}, u32[]{:S(2)}) collective-permute-start(bf16[2048,128]{1,0:T(8,128)(2,1)} %bitcast.8), channel_id=1, source_target_pairs={{8,0},{1,9},{2,10},{11,3},{4,12},{13,5},{6,14},{15,7},{24,16},{17,... | collective-permute-start | bytes 1572872 | tf_op jit(solution)/shard_map/ppermute | solution.py:181
  51.9 1.6 %copy-start.3 = (bf16[1024,2,4,128]{3,2,1,0:T(4,128)(2,1)S(1)}, bf16[1024,2,4,128]{3,2,1,0:T(4,128)(2,1)}, u32[]{:S(2)}) copy-start(bf16[1024,2,4,128]{3,2,1,0:T(4,128)(2,1)} %param.3) | copy-start | bytes 6291460
  55.5 1.3 %copy-start = (bf16[128,8192]{1,0:T(8,128)(2,1)}, bf16[128,8192]{1,0:T(8,128)(2,1)S(1)}, u32[]{:S(2)}) copy-start(bf16[128,8192]{1,0:T(8,128)(2,1)S(1)} %get-tuple-element.11.swapped_ref) | copy-start | bytes 6291460
  83.0 1.6 %copy-start.1 = (bf16[128,8192]{1,0:T(8,128)(2,1)S(1)}, bf16[128,8192]{1,0:T(8,128)(2,1)}, u32[]{:S(2)}) copy-start(bf16[128,8192]{1,0:T(8,128)(2,1)} %copy-done) | copy-start | bytes 6291460
  91.7 4.9 %copy-start.7 = (pred[8]{0:T(512)(128)(4,1)S(1)}, pred[8]{0:T(512)(128)(4,1)}, u32[]{:S(2)}) copy-start(pred[8]{0:T(512)(128)(4,1)} %constant.74.clone) | copy-start | bytes 28
  94.4 0.7 copy-start.4
  95.1 17.4 %collective-permute-start.7 = (bf16[9,128,128]{2,1,0:T(8,128)(2,1)}, bf16[9,128,128]{2,1,0:T(8,128)(2,1)}, u32[]{:S(2)}, u32[]{:S(2)}) collective-permute-start(bf16[9,128,128]{2,1,0:T(8,128)(2,1)} %get-tuple-element.13), channel_id=1, source_target_pairs={{0,8},{9,1},{10,2},{3,11},{12,4},{5,13},{14,6},{7,15},{16,24},{25,... | collective-permute-start | bytes 884744 | tf_op jit(solution)/shard_map/ppermute | solution.py:211
  110.0 2.5 %copy-start.5 = (bf16[9,128,128]{2,1,0:T(8,128)(2,1)S(1)}, bf16[9,128,128]{2,1,0:T(8,128)(2,1)}, u32[]{:S(2)}) copy-start(bf16[9,128,128]{2,1,0:T(8,128)(2,1)} %copy-done.4) | copy-start | bytes 884740
  110.0 4.3 %copy-start.2 = (bf16[128,8192]{1,0:T(8,128)(2,1)S(1)}, bf16[128,8192]{1,0:T(8,128)(2,1)}, u32[]{:S(2)}) copy-start(bf16[128,8192]{1,0:T(8,128)(2,1)} %copy-done) | copy-start | bytes 6291460
  111.8 10.6 %collective-permute-start.5 = (bf16[9,128,128]{2,1,0:T(8,128)(2,1)S(1)}, bf16[9,128,128]{2,1,0:T(8,128)(2,1)S(1)}, u32[]{:S(2)}, u32[]{:S(2)}) collective-permute-start(bf16[9,128,128]{2,1,0:T(8,128)(2,1)S(1)} %side_last.1), channel_id=1, source_target_pairs={{0,7},{7,15},{16,23},{23,31}} | collective-permute-start | bytes 884744 | tf_op jit(solution)/shard_map/ppermute | solution.py:212

commit v2 on v1

--- a/solution.py
+++ b/solution.py
@@ -11,7 +11,7 @@
 HL = 4
 LAGS = 2 * HL + 1
 STEP = 1024
-PARTS = 4
+PIECES = (2, 6, 8)
 
 
 def goes_down(pair, half):
@@ -31,6 +31,30 @@
     return jnp.concatenate([cos_part, sin_part], axis=0).astype(jnp.bfloat16)
 
 
+def mask_kernel(x_ref, weight_ref, masked_ref):
+    rows, cols = x_ref.shape
+    weights = jnp.broadcast_to(weight_ref[...][None], (rows // 16, 16, cols)).reshape(rows, cols)
+    masked_ref[...] = x_ref[...] * weights
+
+
+def mask(x, weights, start, rows, name):
+    cols = x.shape[1]
+    skip = start // STEP
+    return pl.pallas_call(
+        mask_kernel,
+        grid=(rows // STEP,),
+        in_specs=[
+            pl.BlockSpec((STEP, cols), lambda s: (s + skip, 0)),
+            pl.BlockSpec((16, cols), lambda s: (0, 0)),
+        ],
+        out_specs=pl.BlockSpec((STEP, cols), lambda s: (s, 0)),
+        out_shape=jax.ShapeDtypeStruct((rows, cols), jnp.bfloat16),
+        compiler_params=pltpu.CompilerParams(vmem_limit_bytes=32 * 1024 * 1024),
+        cost_estimate=pl.CostEstimate(flops=rows * cols, bytes_accessed=4 * rows * cols, transcendentals=0),
+        name=name,
+    )(x, weights)
+
+
 def turn_kernel(x_ref, plain_ref, swapped_ref):
     x = x_ref[...].astype(jnp.float32)
     rows, cols = x.shape
@@ -39,7 +63,7 @@
     swapped_ref[...] = swapped.T.astype(jnp.bfloat16)
 
 
-def turn(x):
+def turn(x, name):
     rows, cols = x.shape
     out = jax.ShapeDtypeStruct((cols, rows), jnp.bfloat16)
     return pl.pallas_call(
@@ -50,11 +74,11 @@
         out_shape=[out, out],
         compiler_params=pltpu.CompilerParams(vmem_limit_bytes=32 * 1024 * 1024),
         cost_estimate=pl.CostEstimate(flops=0, bytes_accessed=6 * rows * cols, transcendentals=0),
-        name="turn",
+        name=name,
     )(x)
 
 
-def corr_kernel(first, last, mirrored, flag_ref, plain_ref, swapped_ref, coeff_ref, partner_ref, weight_ref, *rest):
+def corr_kernel(first, last, mirrored, flag_ref, plain_ref, swapped_ref, coeff_ref, partner_ref, *rest):
     acc_in = None if first else rest[0]
     outs = rest if first else rest[1:]
     scratch = outs[-1]
@@ -78,9 +102,7 @@
         scratch[k * cols:(k + 1) * cols, :] = plain_ref[...] * coeff_ref[k:k + 1, :]
     for k in range(HL + 1, LAGS):
         scratch[k * cols:(k + 1) * cols, :] = swapped_ref[...] * coeff_ref[k:k + 1, :]
-    rows = partner_ref.shape[0]
-    weights = jnp.broadcast_to(weight_ref[...][None], (rows // 16, 16, cols)).reshape(rows, cols)
-    acc[...] += jnp.dot(scratch[...], partner_ref[...] * weights, preferred_element_type=jnp.float32)
+    acc[...] += jnp.dot(scratch[...], partner_ref[...], preferred_element_type=jnp.float32)
 
     if last:
         @pl.when(step == pl.num_programs(0) - 1)
@@ -113,7 +135,7 @@
                         outs[0][LAGS - 1 - lag] = result(lag).T.astype(jnp.bfloat16)
 
 
-def corr(turned, coeffs, partner, start, weights, flag, acc, last, mirrored, name):
+def corr(turned, coeffs, partner, start, flag, acc, last, mirrored, name):
     plain, swapped = turned
     cols = plain.shape[0]
     rows = partner.shape[0]
@@ -129,9 +151,8 @@
         pl.BlockSpec((cols, STEP), lambda s: (0, s + skip)),
         pl.BlockSpec((LAGS, STEP), lambda s: (0, s + skip)),
         pl.BlockSpec((STEP, cols), lambda s: (s, 0)),
-        pl.BlockSpec((16, cols), lambda s: (0, 0)),
     ]
-    args = [flag, plain, swapped, coeffs, partner, weights]
+    args = [flag, plain, swapped, coeffs, partner]
     if not first:
         in_specs.append(acc_spec)
         args.append(acc)
@@ -157,11 +178,6 @@
     )(*args)
 
 
-def row_weights(own_flags, partner_flags, cols):
-    both = (own_flags * partner_flags).astype(jnp.bfloat16)
-    return jnp.broadcast_to(jnp.tile(both, 16 // both.shape[0])[:, None], (16, cols))
-
-
 def local(spectra, quality):
     count = lax.axis_size("chan")
     half = count // 2
@@ -169,52 +185,46 @@
     freq_count, _, window_count, cols = spectra.shape
     block = spectra.reshape(-1, cols)
     rows = block.shape[0]
+    weights = jnp.tile(quality[0].astype(jnp.bfloat16), 16 // window_count)
+    weights = jnp.broadcast_to(weights[:, None], (16, cols))
 
     down = [goes_down(p, half) for p in range(half)]
     far_pairs = [(p + half, p) if d else (p, p + half) for p, d in enumerate(down)]
+    far_pairs += [(0, 1), (half - 1, half - 2)]
+    near_pairs = [(d + 1, d) for d in range(1, count - 1) if d not in (half - 2, half - 1)]
+    near_pairs += [(0, half - 1), (half - 1, 0)]
     back_pairs = [(p, p + half) if d else (p + half, p) for p, d in enumerate(down)]
-    near_pairs = [(d + 1, d) for d in range(count - 1) if d != half - 1]
-    swap_pairs = [(0, half - 1), (half - 1, 0)]
+    back_pairs += [(1, 0)]
     side_pairs = [(0, half - 1), (half - 1, count - 1)]
 
-    piece = rows // PARTS
-    far_in = [lax.ppermute(block[s * piece:(s + 1) * piece], "chan", far_pairs) for s in range(PARTS)]
-    near_in = lax.ppermute(block, "chan", near_pairs)
-    swap_in = lax.ppermute(block, "chan", swap_pairs)
-
-    flags = lax.all_gather(quality[0], "chan")
-    near_at = lax.rem(me + 1, count)
-    far_at = lax.rem(me + half, count)
-    swap_at = jnp.where(me == 0, half - 1, 0)
-
-    def flags_of(at):
-        return lax.dynamic_index_in_dim(flags, at, 0, keepdims=False)
-
-    near_w = row_weights(quality[0], flags_of(near_at), cols)
-    far_w = row_weights(quality[0], flags_of(far_at), cols)
-    side_w = row_weights(flags_of(swap_at), flags_of(far_at), cols)
+    ends = [rows * e // 8 for e in PIECES]
+    starts = [0] + ends[:-1]
+    pieces = [mask(block, weights, a, b - a, f"mask_{s}") for s, (a, b) in enumerate(zip(starts, ends))]
+    far_in = [lax.ppermute(piece, "chan", far_pairs) for piece in pieces]
+    block, weights, _ = lax.optimization_barrier((block, weights, pieces))
+    masked = mask(block, weights, 0, rows, "mask_all")
+    near_in = lax.ppermute(masked, "chan", near_pairs)
 
     coeffs = lag_rows(freq_count, window_count)
-    turned = turn(block)
-    swap_turned = turn(swap_in)
+    turned = turn(masked, "turn_own")
     flag = (me == half - 1).astype(jnp.int32).reshape(1)
-
-    near_own, = corr(turned, coeffs, near_in, 0, near_w, flag, None, True, "no", "near_corr")
+    near_own, = corr(turned, coeffs, near_in, 0, flag, None, True, "no", "near_corr")
+    side_turned = turn(near_in, "turn_near")
+
     far_acc = side_acc = None
-    for s in range(PARTS - 1):
-        far_acc, = corr(turned, coeffs, far_in[s], s * piece, far_w, flag, far_acc, False, "no", "far_part")
-        side_acc, = corr(swap_turned, coeffs, far_in[s], s * piece, side_w, flag, side_acc, False, "no", "side_part")
-    at = (PARTS - 1) * piece
-    far_own, far_mirror = corr(turned, coeffs, far_in[-1], at, far_w, flag, far_acc, True, "both", "far_last")
-    side_own, = corr(swap_turned, coeffs, far_in[-1], at, side_w, flag, side_acc, True, "flag", "side_last")
-
+    for s in range(len(pieces) - 1):
+        far_acc, = corr(turned, coeffs, far_in[s], starts[s], flag, far_acc, False, "no", f"far_{s}")
+        side_acc, = corr(side_turned, coeffs, far_in[s], starts[s], flag, side_acc, False, "no", f"side_{s}")
+    far_acc, side_acc, near_own, last_in = lax.optimization_barrier((far_acc, side_acc, near_own, far_in[-1]))
+    far_own, far_mirror = corr(turned, coeffs, last_in, starts[-1], flag, far_acc, True, "both", "far_last")
     far_back = lax.ppermute(far_mirror, "chan", back_pairs)
+    side_own, = corr(side_turned, coeffs, last_in, starts[-1], flag, side_acc, True, "flag", "side_last")
     side_back = lax.ppermute(side_own, "chan", side_pairs)
 
-    is_down = jnp.asarray(down)[lax.rem(me, half)]
-    hosts = is_down == (me < half)
+    hosts = jnp.asarray(down)[lax.rem(me, half)] == (me < half)
     far = jnp.where(hosts, far_own, far_back)
     near = jnp.where((me == half - 1) | (me == count - 1), side_back, near_own)
+    near = jnp.where(me == 0, far_back, jnp.where(me == half - 2, far_own, near))
     return near[None], far[None]
 
 

time: 125 us -> 108 us (0.86)
  blocking collectives: 26 us -> 0 us
  waiting for transfers between devices: 27.4 us -> 40.3 us
  Pallas kernels: 33.8 us -> 42.3 us
  starting transfers between devices: 20.7 us -> 14.2 us
  local copies, waits for them, and re-layouts: 9.57 us -> 5.28 us
    all_gather x1 -> x0, blocking collectives: 26 us -> none  [local(): flags = lax.all_gather(quality[0], 'chan')]
    ppermute x6 -> x4, starting transfers between devices: 18.7 us -> 10.1 us  [the longest x3 8.85 us: local(): far_in = [lax.ppermute(piece, 'chan', far_pairs) for piece in pieces]]
    ppermute x1, waiting for transfers between devices: 0.01 us -> 6.79 us  [local(): far_back = lax.ppermute(far_mirror, 'chan', back_pairs)]
    pallas_call x0 -> x4, Pallas kernels: none -> 6.42 us  [mask(): pl.pallas_call(mask_kernel, grid=(rows // STEP,), in_specs=[pl.BlockSpec(...]
    ppermute x6 -> x4, waiting for transfers between devices: 27.3 us -> 33.5 us  [the longest x1 33.5 us: local(): near_in = lax.ppermute(masked, 'chan', near_pairs)]
    slice x1 -> x0, local copies, waits for them, and re-layouts: 3.27 us -> none  [local(): block[s * piece:(s + 1) * piece]]
    pallas_call x2, Pallas kernels: 7.04 us -> 10.2 us  [turn(): pl.pallas_call(turn_kernel, grid=(rows // STEP,), in_specs=[pl.BlockSpec(...]
    broadcast_in_dim x2 -> x1, other arithmetic: 2.49 us -> 0.87 us  [local(): return (near[None], far[None])]
  transfers between devices with their start and end apart: 8 -> 6, of which waited for: 1 -> 2; matrix products, arithmetic and copies ran while one was open for 6% -> 2% of each run, Pallas kernels for 27% -> 36%
where the time goes in v2:
time: 108 us; the launch traced here: 107 us
  Pallas kernels  42.3 us (39%)
  waiting for transfers between devices  40.3 us (37%)
  starting transfers between devices  14.2 us (13%)
  local copies, waits for them, and re-layouts  5.28 us (5%)
  other arithmetic  3.46 us (3%)
  between operations  1.53 us (1%)
    ppermute x1, waiting for transfers between devices, local(): near_in = lax.ppermute(masked, 'chan', near_pairs)  33.5 us
    pallas_call x7, Pallas kernels, corr(): pl.pallas_call(functools.partial(corr_kernel, first, last, mirrored), gri...  25.7 us
    pallas_call x2, Pallas kernels, turn(): pl.pallas_call(turn_kernel, grid=(rows // STEP,), in_specs=[pl.BlockSpec(...  10.2 us
    ppermute x3, starting transfers between devices, local(): far_in = [lax.ppermute(piece, 'chan', far_pairs) for piece in pieces]  8.85 us
    ppermute x1, waiting for transfers between devices, local(): far_back = lax.ppermute(far_mirror, 'chan', back_pairs)  6.79 us
    pallas_call x4, Pallas kernels, mask(): pl.pallas_call(mask_kernel, grid=(rows // STEP,), in_specs=[pl.BlockSpec(...  6.42 us
    unnamed x10, local copies, waits for them, and re-layouts  4.52 us
    ppermute x1, starting transfers between devices, local(): far_back = lax.ppermute(far_mirror, 'chan', back_pairs)  2.7 us
  transfers between devices with their start and end apart: 6, of which 2 were waited for; matrix products, arithmetic and copies ran while one was open for 2% of the time, Pallas kernels for 36%

profile of v2, /device:TPU:1, one launch (start us, length us, event | category | flops | bytes accessed | tf_op | source)
XLA Modules:
  0.0 107.1 jit_solution(2827000300655416989)
XLA Ops:
  1.5 1.6 %copy-done = bf16[1024,2,4,128]{3,2,1,0:T(4,128)(2,1)S(1)} copy-done((bf16[1024,2,4,128]{3,2,1,0:T(4,128)(2,1)S(1)}, bf16[1024,2,4,128]{3,2,1,0:T(4,128)(2,1)}, u32[]{:S(2)}) %copy-start) | copy-done | bytes 2097176
  3.9 5.0 %collective-permute-start.1 = (bf16[2048,128]{1,0:T(8,128)(2,1)}, bf16[2048,128]{1,0:T(8,128)(2,1)}, u32[]{:S(2)}, u32[]{:S(2)}) collective-permute-start(bf16[2048,128]{1,0:T(8,128)(2,1)} %mask_0.1), channel_id=1, source_target_pairs={{8,0},{1,9},{2,10},{11,3},{4,12},{13,5},{6,14},{15,7},{0,1},{7,6},... | collective-permute-start | bytes 1572872 | tf_op jit(solution)/shard_map/ppermute | solution.py:203
  8.9 1.6 %mask_1.1 = bf16[4096,128]{1,0:T(8,128)(2,1)} custom-call(bf16[8192,128]{1,0:T(8,128)(2,1)S(1)} %bitcast.10, bf16[16,128]{1,0:T(8,128)(2,1)S(1)} %broadcast_in_dim.25.weight_ref), custom_call_target="tpu_custom_call" | custom-call | flops 524288 | bytes 2097152 | tf_op jit(solution)/shard_map/mask_1/pallas_call | solution.py:43
  10.5 1.9 %collective-permute-start = (bf16[4096,128]{1,0:T(8,128)(2,1)}, bf16[4096,128]{1,0:T(8,128)(2,1)S(1)}, u32[]{:S(2)}, u32[]{:S(2)}) collective-permute-start(bf16[4096,128]{1,0:T(8,128)(2,1)} %mask_1.1), channel_id=1, source_target_pairs={{8,0},{1,9},{2,10},{11,3},{4,12},{13,5},{6,14},{15,7},{0,1},{7,6},... | collective-permute-start | bytes 3145736 | tf_op jit(solution)/shard_map/ppermute | solution.py:203
  12.5 0.9 mask_2.1
  13.4 1.9 %collective-permute-start.3 = (bf16[2048,128]{1,0:T(8,128)(2,1)}, bf16[2048,128]{1,0:T(8,128)(2,1)}, u32[]{:S(2)}, u32[]{:S(2)}) collective-permute-start(bf16[2048,128]{1,0:T(8,128)(2,1)} %mask_2.1), channel_id=1, source_target_pairs={{8,0},{1,9},{2,10},{11,3},{4,12},{13,5},{6,14},{15,7},{0,1},{7,6},... | collective-permute-start | bytes 1572872 | tf_op jit(solution)/shard_map/ppermute | solution.py:203
  15.3 3.1 %mask_all.1.x_ref = bf16[8192,128]{1,0:T(8,128)(2,1)} custom-call(bf16[8192,128]{1,0:T(8,128)(2,1)S(1)} %bitcast.12, bf16[16,128]{1,0:T(8,128)(2,1)S(1)} %broadcast_in_dim.25.weight_ref), custom_call_target="tpu_custom_call" | custom-call | flops 1048576 | bytes 4194304 | tf_op jit(solution)/shard_map/mask_all/pallas_call | solution.py:43
  18.4 1.3 %collective-permute-start.2 = (bf16[8192,128]{1,0:T(8,128)(2,1)}, bf16[8192,128]{1,0:T(8,128)(2,1)}, u32[]{:S(2)}, u32[]{:S(2)}) collective-permute-start(bf16[8192,128]{1,0:T(8,128)(2,1)} %mask_all.1.x_ref), channel_id=1, source_target_pairs={{2,1},{3,2},{4,3},{5,4},{6,5},{9,8},{10,9},{11,10},{12,11},{13,12}... | collective-permute-start | bytes 6291464 | tf_op jit(solution)/shard_map/ppermute | solution.py:206
  19.7 0.9 multiply_convert_fusion
  21.5 5.1 %turn_own.1 = (bf16[128,8192]{1,0:T(8,128)(2,1)S(1)}, bf16[128,8192]{1,0:T(8,128)(2,1)S(1)}) custom-call(bf16[8192,128]{1,0:T(8,128)(2,1)} %mask_all.1.x_ref), custom_call_target="tpu_custom_call" | custom-call | bytes 6291456 | tf_op jit(solution)/shard_map/turn_own/pallas_call | solution.py:69
  26.6 1.3 %copy-done.1 = bf16[128,8192]{1,0:T(8,128)(2,1)} copy-done((bf16[128,8192]{1,0:T(8,128)(2,1)}, bf16[128,8192]{1,0:T(8,128)(2,1)S(1)}, u32[]{:S(2)}) %copy-start.1) | copy-done | bytes 2097176
  28.1 1.6 %copy-done.2 = bf16[128,8192]{1,0:T(8,128)(2,1)S(1)} copy-done((bf16[128,8192]{1,0:T(8,128)(2,1)S(1)}, bf16[128,8192]{1,0:T(8,128)(2,1)}, u32[]{:S(2)}) %copy-start.2) | copy-done | bytes 2097176
  29.6 2.6 %far_0.1.rest_0_ = f32[1152,128]{1,0:T(8,128)S(1)} custom-call(s32[1]{0:T(128)} %bitcast.flag_ref, bf16[128,8192]{1,0:T(8,128)(2,1)S(1)} %get-tuple-element.16.plain_ref, bf16[128,8192]{1,0:T(8,128)(2,1)S(1)} %copy-done.2, bf16[9,8192]{1,0:T(8,128)(2,1)S(1)} %pad_maximum_fusion.coeff_ref, bf16[2048,128]{1,0:T(8,128)(2,1)} %collective-permute-done.1.partner_ref), custom_call_target="tpu_custom_call" | custom-call | flops 603979776 | bytes 1572864 | tf_op jit(solution)/shard_map/far_0/pallas_call | solution.py:166
  32.3 3.4 %far_1.1.rest_0_ = f32[1152,128]{1,0:T(8,128)S(1)} custom-call(s32[1]{0:T(128)} %bitcast.flag_ref, bf16[128,8192]{1,0:T(8,128)(2,1)S(1)} %get-tuple-element.16.plain_ref, bf16[128,8192]{1,0:T(8,128)(2,1)S(1)} %copy-done.2, bf16[9,8192]{1,0:T(8,128)(2,1)S(1)} %pad_maximum_fusion.coeff_ref, bf16[4096,128]{1,0:T(8,128)(2,1)S(1)} %collective-permute-done.partner_ref, ...), custom_call_target="tpu_custom_call" | custom-call | flops 1207959552 | bytes 3145728 | tf_op jit(solution)/shard_map/far_1/pallas_call | solution.py:166
  35.7 33.5 %collective-permute-done.2.x_ref.partner_ref = bf16[8192,128]{1,0:T(8,128)(2,1)} collective-permute-done((bf16[8192,128]{1,0:T(8,128)(2,1)}, bf16[8192,128]{1,0:T(8,128)(2,1)}, u32[]{:S(2)}, u32[]{:S(2)}) %collective-permute-start.2) | collective-permute-done | bytes 2097184 | tf_op jit(solution)/shard_map/ppermute | solution.py:206
  69.2 5.1 %turn_near.1 = (bf16[128,8192]{1,0:T(8,128)(2,1)S(1)}, bf16[128,8192]{1,0:T(8,128)(2,1)S(1)}) custom-call(bf16[8192,128]{1,0:T(8,128)(2,1)} %collective-permute-done.2.x_ref.partner_ref), custom_call_target="tpu_custom_call" | custom-call | bytes 6291456 | tf_op jit(solution)/shard_map/turn_near/pallas_call | solution.py:69
  74.3 2.6 %side_0.1.rest_0_ = f32[1152,128]{1,0:T(8,128)S(1)} custom-call(s32[1]{0:T(128)} %bitcast.flag_ref, bf16[128,8192]{1,0:T(8,128)(2,1)S(1)} %get-tuple-element.18.plain_ref, bf16[128,8192]{1,0:T(8,128)(2,1)S(1)} %get-tuple-element.19.swapped_ref, bf16[9,8192]{1,0:T(8,128)(2,1)S(1)} %pad_maximum_fusion.coeff_ref, ...), custom_call_target="tpu_custom_call" | custom-call | flops 603979776 | bytes 1572864 | tf_op jit(solution)/shard_map/side_0/pallas_call | solution.py:166
  77.0 3.4 %side_1.1.rest_0_ = f32[1152,128]{1,0:T(8,128)S(1)} custom-call(s32[1]{0:T(128)} %bitcast.flag_ref, bf16[128,8192]{1,0:T(8,128)(2,1)S(1)} %get-tuple-element.18.plain_ref, bf16[128,8192]{1,0:T(8,128)(2,1)S(1)} %get-tuple-element.19.swapped_ref, bf16[9,8192]{1,0:T(8,128)(2,1)S(1)} %pad_maximum_fusion.coeff_ref, ...), custom_call_target="tpu_custom_call" | custom-call | flops 1207959552 | bytes 3145728 | tf_op jit(solution)/shard_map/side_1/pallas_call | solution.py:166
  80.4 8.1 %near_corr.1 = bf16[9,128,128]{2,1,0:T(8,128)(2,1)S(1)} custom-call(s32[1]{0:T(128)} %bitcast.flag_ref, bf16[128,8192]{1,0:T(8,128)(2,1)S(1)} %get-tuple-element.16.plain_ref, bf16[128,8192]{1,0:T(8,128)(2,1)S(1)} %copy-done.3, bf16[9,8192]{1,0:T(8,128)(2,1)S(1)} %pad_maximum_fusion.coeff_ref, bf16[8192,128]{1,0:T(8,128)(2,1)} %collective-permute-done.2.x_ref.partner_ref), custom_call_target="tpu_custom_call" | custom-call | flops 2415919104 | bytes 6291456 | tf_op jit(solution)/shard_map/near_corr/pallas_call | solution.py:166
  88.5 2.7 %side_last.1 = bf16[9,128,128]{2,1,0:T(8,128)(2,1)S(1)} custom-call(s32[1]{0:T(128)} %bitcast.flag_ref, bf16[128,8192]{1,0:T(8,128)(2,1)S(1)} %get-tuple-element.18.plain_ref, bf16[128,8192]{1,0:T(8,128)(2,1)S(1)} %get-tuple-element.19.swapped_ref, bf16[9,8192]{1,0:T(8,128)(2,1)S(1)} %pad_maximum_fusion.coeff_ref, ...), custom_call_target="tpu_custom_call" | custom-call | flops 603979776 | bytes 1572864 | tf_op jit(solution)/shard_map/side_last/pallas_call | solution.py:166
  91.3 1.4 %collective-permute-start.5 = (bf16[9,128,128]{2,1,0:T(8,128)(2,1)S(1)}, bf16[9,128,128]{2,1,0:T(8,128)(2,1)}, u32[]{:S(2)}, u32[]{:S(2)}) collective-permute-start(bf16[9,128,128]{2,1,0:T(8,128)(2,1)S(1)} %side_last.1), channel_id=1, source_target_pairs={{0,7},{7,15},{16,23},{23,31}} | collective-permute-start | bytes 884744 | tf_op jit(solution)/shard_map/ppermute | solution.py:222
  92.6 2.8 %far_last.1 = (bf16[9,128,128]{2,1,0:T(8,128)(2,1)S(1)}, bf16[9,128,128]{2,1,0:T(8,128)(2,1)S(1)}) custom-call(s32[1]{0:T(128)} %bitcast.flag_ref, bf16[128,8192]{1,0:T(8,128)(2,1)S(1)} %get-tuple-element.16.plain_ref, bf16[128,8192]{1,0:T(8,128)(2,1)S(1)} %copy-done.3, bf16[9,8192]{1,0:T(8,128)(2,1)S(1)} %pad_maximum_fusion.coeff_ref, ...), custom_call_target="tpu_custom_call" | custom-call | flops 603979776 | bytes 1572864 | tf_op jit(solution)/shard_map/far_last/pallas_call | solution.py:166
  95.4 2.7 %collective-permute-start.4 = (bf16[9,128,128]{2,1,0:T(8,128)(2,1)S(1)}, bf16[9,128,128]{2,1,0:T(8,128)(2,1)S(1)}, u32[]{:S(2)}, u32[]{:S(2)}) collective-permute-start(bf16[9,128,128]{2,1,0:T(8,128)(2,1)S(1)} %get-tuple-element.22), channel_id=1, source_target_pairs={{0,8},{9,1},{10,2},{3,11},{12,4},{5,13},{14,6},{7,15},{1,0},{16,24... | collective-permute-start | bytes 884744 | tf_op jit(solution)/shard_map/ppermute | solution.py:220
  99.4 6.8 %collective-permute-done.4 = bf16[9,128,128]{2,1,0:T(8,128)(2,1)S(1)} collective-permute-done((bf16[9,128,128]{2,1,0:T(8,128)(2,1)S(1)}, bf16[9,128,128]{2,1,0:T(8,128)(2,1)S(1)}, u32[]{:S(2)}, u32[]{:S(2)}) %collective-permute-start.4) | collective-permute-done | bytes 294944 | tf_op jit(solution)/shard_map/ppermute | solution.py:220
  (23 shorter events, 4.2 us)
Async XLA Ops:
  1.5 1.6 %copy-start = (bf16[1024,2,4,128]{3,2,1,0:T(4,128)(2,1)S(1)}, bf16[1024,2,4,128]{3,2,1,0:T(4,128)(2,1)}, u32[]{:S(2)}) copy-start(bf16[1024,2,4,128]{3,2,1,0:T(4,128)(2,1)} %param.3) | copy-start | bytes 6291460
  3.9 24.1 %collective-permute-start.1 = (bf16[2048,128]{1,0:T(8,128)(2,1)}, bf16[2048,128]{1,0:T(8,128)(2,1)}, u32[]{:S(2)}, u32[]{:S(2)}) collective-permute-start(bf16[2048,128]{1,0:T(8,128)(2,1)} %mask_0.1), channel_id=1, source_target_pairs={{8,0},{1,9},{2,10},{11,3},{4,12},{13,5},{6,14},{15,7},{0,1},{7,6},... | collective-permute-start | bytes 1572872 | tf_op jit(solution)/shard_map/ppermute | solution.py:203
  10.5 21.7 %collective-permute-start = (bf16[4096,128]{1,0:T(8,128)(2,1)}, bf16[4096,128]{1,0:T(8,128)(2,1)S(1)}, u32[]{:S(2)}, u32[]{:S(2)}) collective-permute-start(bf16[4096,128]{1,0:T(8,128)(2,1)} %mask_1.1), channel_id=1, source_target_pairs={{8,0},{1,9},{2,10},{11,3},{4,12},{13,5},{6,14},{15,7},{0,1},{7,6},... | collective-permute-start | bytes 3145736 | tf_op jit(solution)/shard_map/ppermute | solution.py:203
  13.4 75.2 %collective-permute-start.3 = (bf16[2048,128]{1,0:T(8,128)(2,1)}, bf16[2048,128]{1,0:T(8,128)(2,1)}, u32[]{:S(2)}, u32[]{:S(2)}) collective-permute-start(bf16[2048,128]{1,0:T(8,128)(2,1)} %mask_2.1), channel_id=1, source_target_pairs={{8,0},{1,9},{2,10},{11,3},{4,12},{13,5},{6,14},{15,7},{0,1},{7,6},... | collective-permute-start | bytes 1572872 | tf_op jit(solution)/shard_map/ppermute | solution.py:203
  18.4 50.9 %collective-permute-start.2 = (bf16[8192,128]{1,0:T(8,128)(2,1)}, bf16[8192,128]{1,0:T(8,128)(2,1)}, u32[]{:S(2)}, u32[]{:S(2)}) collective-permute-start(bf16[8192,128]{1,0:T(8,128)(2,1)} %mask_all.1.x_ref), channel_id=1, source_target_pairs={{2,1},{3,2},{4,3},{5,4},{6,5},{9,8},{10,9},{11,10},{12,11},{13,12}... | collective-permute-start | bytes 6291464 | tf_op jit(solution)/shard_map/ppermute | solution.py:206
  26.6 1.3 %copy-start.1 = (bf16[128,8192]{1,0:T(8,128)(2,1)}, bf16[128,8192]{1,0:T(8,128)(2,1)S(1)}, u32[]{:S(2)}) copy-start(bf16[128,8192]{1,0:T(8,128)(2,1)S(1)} %get-tuple-element.17.swapped_ref) | copy-start | bytes 6291460
  28.0 1.6 %copy-start.2 = (bf16[128,8192]{1,0:T(8,128)(2,1)S(1)}, bf16[128,8192]{1,0:T(8,128)(2,1)}, u32[]{:S(2)}) copy-start(bf16[128,8192]{1,0:T(8,128)(2,1)} %copy-done.1) | copy-start | bytes 6291460
  77.0 3.5 %copy-start.3 = (bf16[128,8192]{1,0:T(8,128)(2,1)S(1)}, bf16[128,8192]{1,0:T(8,128)(2,1)}, u32[]{:S(2)}) copy-start(bf16[128,8192]{1,0:T(8,128)(2,1)} %copy-done.1) | copy-start | bytes 6291460
  91.2 6.9 %copy-start.4 = (pred[8]{0:T(512)(128)(4,1)S(1)}, pred[8]{0:T(512)(128)(4,1)}, u32[]{:S(2)}) copy-start(pred[8]{0:T(512)(128)(4,1)} %constant.56.clone) | copy-start | bytes 28
  91.3 8.2 %collective-permute-start.5 = (bf16[9,128,128]{2,1,0:T(8,128)(2,1)S(1)}, bf16[9,128,128]{2,1,0:T(8,128)(2,1)}, u32[]{:S(2)}, u32[]{:S(2)}) collective-permute-start(bf16[9,128,128]{2,1,0:T(8,128)(2,1)S(1)} %side_last.1), channel_id=1, source_target_pairs={{0,7},{7,15},{16,23},{23,31}} | collective-permute-start | bytes 884744 | tf_op jit(solution)/shard_map/ppermute | solution.py:222
  95.4 10.8 %collective-permute-start.4 = (bf16[9,128,128]{2,1,0:T(8,128)(2,1)S(1)}, bf16[9,128,128]{2,1,0:T(8,128)(2,1)S(1)}, u32[]{:S(2)}, u32[]{:S(2)}) collective-permute-start(bf16[9,128,128]{2,1,0:T(8,128)(2,1)S(1)} %get-tuple-element.22), channel_id=1, source_target_pairs={{0,8},{9,1},{10,2},{3,11},{12,4},{5,13},{14,6},{7,15},{1,0},{16,24... | collective-permute-start | bytes 884744 | tf_op jit(solution)/shard_map/ppermute | solution.py:220

commit v3 on v0

v3 whole, which is shorter than its diff:
```python
import functools
import math

import jax
import jax.numpy as jnp
from jax import lax
from jax.experimental import pallas as pl
from jax.experimental.pallas import tpu as pltpu
from jax.sharding import PartitionSpec as P

HL = 4
LAGS = 2 * HL + 1
STEP = 1024
TILE = 256
ENDS = (5, 8)
PARAMS = pltpu.CompilerParams(vmem_limit_bytes=32 * 1024 * 1024)


def goes_down(pair, half):
    return pair in (0, half - 1) or pair % 2 == 1 and pair != 1


def lag_rows(freq_count, window_count):
    per_bin = 2 * window_count
    row = jnp.arange(freq_count * per_bin, dtype=jnp.int32)
    freq_values = (row // per_bin).astype(jnp.float32)
    sign = jnp.where(row % per_bin < window_count, 1.0, -1.0)
    lag_values = jnp.arange(HL + 1, dtype=jnp.float32)
    phases = jnp.pi / freq_count * lag_values[:, None] * freq_values[None, :]
    factor = 1.0 / math.sqrt(window_count * freq_count)
    cos_part = jnp.cos(phases) * factor
    sin_part = -jnp.sin(phases[1:]) * factor * sign[None, :]
    return jnp.concatenate([cos_part, sin_part], axis=0).astype(jnp.bfloat16)


def mask_kernel(ends, flags_ref, x_ref, *piece_refs):
    rows, cols = x_ref.shape
    windows = flags_ref.shape[1]
    step = pl.program_id(0)
    window = lax.broadcasted_iota(jnp.int32, (16, cols), 0) % windows
    weights = jnp.zeros((16, cols), jnp.float32)
    for w in range(windows):
        weights = jnp.where(window == w, flags_ref[0, w].astype(jnp.float32), weights)
    weights = jnp.broadcast_to(weights.astype(jnp.bfloat16)[None], (rows // 16, 16, cols))
    masked = x_ref[...] * weights.reshape(rows, cols)
    begin = 0
    for end, piece_ref in zip(ends, piece_refs):
        @pl.when((step >= begin) & (step < end))
        def _():
            piece_ref[...] = masked
        begin = end


def mask(x, flags):
    rows, cols = x.shape
    steps = rows // STEP
    ends = [steps * e // 8 for e in ENDS]
    begins = [0] + ends[:-1]
    sizes = [e - b for b, e in zip(begins, ends)]

    def place(begin, size):
        return lambda s: (jnp.clip(s - begin, 0, size - 1), 0)

    return pl.pallas_call(
        functools.partial(mask_kernel, ends),
        grid=(steps,),
        in_specs=[pl.BlockSpec(memory_space=pltpu.SMEM), pl.BlockSpec((STEP, cols), lambda s: (s, 0))],
        out_specs=[pl.BlockSpec((STEP, cols), place(b, n)) for b, n in zip(begins, sizes)],
        out_shape=[jax.ShapeDtypeStruct((n * STEP, cols), jnp.bfloat16) for n in sizes],
        compiler_params=PARAMS,
        cost_estimate=pl.CostEstimate(flops=rows * cols, bytes_accessed=4 * rows * cols, transcendentals=0),
        name="mask",
    )(flags, x)


def turn_kernel(active_ref, x_ref, plain_ref, swapped_ref):
    @pl.when(active_ref[0] != 0)
    def _():
        rows, cols = x_ref.shape
        same = lax.broadcasted_iota(jnp.int32, (cols, cols), 0) == lax.broadcasted_iota(jnp.int32, (cols, cols), 1)
        eye = jnp.where(same, 1.0, 0.0).astype(jnp.bfloat16)
        source = lax.broadcasted_iota(jnp.int32, (TILE, TILE), 0)
        target = lax.broadcasted_iota(jnp.int32, (TILE, TILE), 1)
        exchange = jnp.where((source ^ 4) == target, 1.0, 0.0).astype(jnp.bfloat16)
        plain = lax.dot_general(eye, x_ref[...], (((1,), (1,)), ((), ())), preferred_element_type=jnp.float32)
        plain = plain.astype(jnp.bfloat16)
        plain_ref[...] = plain
        for t in range(0, rows, TILE):
            swapped = jnp.dot(plain[:, t:t + TILE], exchange, preferred_element_type=jnp.float32)
            swapped_ref[:, t:t + TILE] = swapped.astype(jnp.bfloat16)


def turn(x, active, name):
    rows, cols = x.shape
    out = jax.ShapeDtypeStruct((cols, rows), jnp.bfloat16)
    return pl.pallas_call(
        turn_kernel,
        grid_spec=pltpu.PrefetchScalarGridSpec(
            num_scalar_prefetch=1,
            grid=(rows // STEP,),
            in_specs=[pl.BlockSpec((STEP, cols), lambda s, on: (s * on[0], 0))],
            out_specs=[pl.BlockSpec((cols, STEP), lambda s, on: (0, s * on[0]))] * 2,
        ),
        out_shape=[out, out],
        compiler_params=PARAMS,
        cost_estimate=pl.CostEstimate(flops=0, bytes_accessed=6 * rows * cols, transcendentals=0),
        name=name,
    )(active, x)


def lag_result(acc, cols, lag):
    k = abs(lag - HL)
    even = acc[k * cols:(k + 1) * cols, :]
    if k == 0:
        return even.astype(jnp.bfloat16)
    odd = acc[(HL + k) * cols:(HL + k + 1) * cols, :]
    return (even + odd if lag > HL else even - odd).astype(jnp.bfloat16)


def corr_kernel(first, kind, active_ref, plain_ref, swapped_ref, coeff_ref, partner_ref, *rest):
    acc_in = None if first else rest[0]
    refs = list(rest if first else rest[1:])
    buffers = [refs.pop(), refs.pop()]
    acc = refs.pop()
    step = pl.program_id(0)
    cols = partner_ref.shape[1]

    @pl.when(active_ref[0] != 0)
    def _():
        @pl.when(step == 0)
        def _():
            if first:
                acc[...] = jnp.zeros_like(acc)
            else:
                acc[...] = acc_in[...]

        def build(t):
            at = slice(t * TILE, (t + 1) * TILE)
            for k in range(LAGS):
                part = plain_ref if k <= HL else swapped_ref
                buffers[t % 2][k * cols:(k + 1) * cols, :] = part[:, at] * coeff_ref[k:k + 1, at]

        build(0)
        for t in range(STEP // TILE):
            if (t + 1) * TILE < STEP:
                build(t + 1)
            acc[...] += jnp.dot(
                buffers[t % 2][...], partner_ref[t * TILE:(t + 1) * TILE, :], preferred_element_type=jnp.float32
            )

        if kind != "part":
            @pl.when(step == pl.num_programs(0) - 1)
            def _():
                def write(out, mirrored):
                    for lag in range(LAGS):
                        value = lag_result(acc, cols, lag)
                        if mirrored:
                            out[LAGS - 1 - lag] = value.T
                        else:
                            out[lag] = value

                if kind == "plain":
                    write(refs[0], False)
                elif kind == "both":
                    write(refs[1], True)
                    write(refs[0], False)
                else:
                    pl.when(active_ref[1] == 0)(lambda: write(refs[0], False))
                    pl.when(active_ref[1] != 0)(lambda: write(refs[0], True))


def corr(active, turned, coeffs, start, partner, acc, kind, name):
    plain, swapped = turned
    cols = plain.shape[0]
    rows = partner.shape[0]
    first = acc is None
    skip = start // STEP
    acc_shape = jax.ShapeDtypeStruct((LAGS * cols, cols), jnp.float32)
    acc_spec = pl.BlockSpec((LAGS * cols, cols), lambda s, on: (0, 0))
    res_shape = jax.ShapeDtypeStruct((LAGS, cols, cols), jnp.bfloat16)
    res_spec = pl.BlockSpec((LAGS, cols, cols), lambda s, on: (0, 0, 0))
    in_specs = [
        pl.BlockSpec((cols, STEP), lambda s, on: (0, s * on[0])),
        pl.BlockSpec((cols, STEP), lambda s, on: (0, s * on[0])),
        pl.BlockSpec((LAGS, STEP), lambda s, on: (0, s * on[0] + skip)),
        pl.BlockSpec((STEP, cols), lambda s, on: (s * on[0], 0)),
    ]
    args = [plain, swapped, coeffs, partner]
    if not first:
        in_specs.append(acc_spec)
        args.append(acc)
    scratch = [pltpu.VMEM((LAGS * cols, TILE), jnp.bfloat16)] * 2
    if kind == "part":
        out_shape, out_specs = [acc_shape], [acc_spec]
    else:
        results = 2 if kind == "both" else 1
        out_shape, out_specs = [res_shape] * results, [res_spec] * results
        scratch = [pltpu.VMEM((LAGS * cols, cols), jnp.float32)] + scratch
    return pl.pallas_call(
        functools.partial(corr_kernel, first, kind),
        grid_spec=pltpu.PrefetchScalarGridSpec(
            num_scalar_prefetch=1,
            grid=(rows // STEP,),
            in_specs=in_specs,
            out_specs=out_specs,
            scratch_shapes=scratch,
        ),
        out_shape=out_shape,
        compiler_params=PARAMS,
        cost_estimate=pl.CostEstimate(
            flops=2 * LAGS * cols * cols * rows, bytes_accessed=6 * rows * cols, transcendentals=0
        ),
        name=name,
    )(active, *args)


def local(spectra, quality):
    count = lax.axis_size("chan")
    half = count // 2
    me = lax.axis_index("chan")
    freq_count, _, window_count, cols = spectra.shape
    block = spectra.reshape(-1, cols)

    down = [goes_down(p, half) for p in range(half)]
    far_pairs = [(p + half, p) if d else (p, p + half) for p, d in enumerate(down)]
    far_pairs += [(0, 1), (half - 1, half - 2)]
    near_pairs = [(d + 1, d) for d in range(1, count - 1) if d not in (half - 2, half - 1)]
    near_pairs += [(0, half - 1), (half - 1, 0)]
    back_pairs = [(p, p + half) if d else (p + half, p) for p, d in enumerate(down)]
    back_pairs += [(1, 0)]
    side_pairs = [(0, half - 1), (half - 1, count - 1)]

    def among(devices):
        return functools.reduce(jnp.logical_or, [me == d for d in devices])

    def switch(on, other=False):
        return jnp.stack([jnp.asarray(on), jnp.asarray(other)]).astype(jnp.int32)

    hosts = among([p if d else p + half for p, d in enumerate(down)])
    far_on = switch(hosts | (me == 1) | (me == half - 2))
    near_on = switch(~among([0, half - 2, half - 1, count - 1]))
    side_on = switch((me == 0) | (me == half - 1), me == half - 1)
    always = switch(True)

    pieces = mask(block, quality)
    starts = [0] + [piece.shape[0] for piece in pieces[:-1]]
    far_in, near_in = [], []
    for piece in pieces:
        far_in.append(lax.ppermute(piece, "chan", far_pairs))
        near_in.append(lax.ppermute(piece, "chan", near_pairs))

    coeffs = lag_rows(freq_count, window_count)
    own = [turn(piece, always, f"turn_own_{s}") for s, piece in enumerate(pieces)]
    side = [turn(near_in[0], side_on, "turn_side_0")]

    near_acc, = corr(near_on, own[0], coeffs, 0, near_in[0], None, "part", "near_first")
    side_acc, = corr(side_on, side[0], coeffs, 0, far_in[0], None, "part", "side_first")
    far_acc, = corr(far_on, own[0], coeffs, 0, far_in[0], None, "part", "far_first")

    near_acc, side_acc, far_acc, far_last_in, near_last_in = lax.optimization_barrier(
        (near_acc, side_acc, far_acc, far_in[1], near_in[1])
    )
    far_own, far_mirror = corr(far_on, own[1], coeffs, starts[1], far_last_in, far_acc, "both", "far_last")
    far_back = lax.ppermute(far_mirror, "chan", back_pairs)
    far_own, near_last_in = lax.optimization_barrier((far_own, near_last_in))
    side.append(turn(near_last_in, side_on, "turn_side_1"))
    side_own, = corr(side_on, side[1], coeffs, starts[1], far_last_in, side_acc, "flag", "side_last")
    side_back = lax.ppermute(side_own, "chan", side_pairs)
    side_own, near_acc = lax.optimization_barrier((side_own, near_acc))
    near_own, = corr(near_on, own[1], coeffs, starts[1], near_last_in, near_acc, "plain", "near_last")

    far = jnp.where(hosts, far_own, far_back)
    near = jnp.where((me == half - 1) | (me == count - 1), side_back, near_own)
    near = jnp.where(me == 0, far_back, jnp.where(me == half - 2, far_own, near))
    return near[None], far[None]


def solution(mesh):
    return jax.shard_map(
        local,
        mesh=mesh,
        in_specs=(P(None, None, None, ("grp", "chan")), P(("grp", "chan"), None)),
        out_specs=(P(("grp", "chan"), None, None, None), P(("grp", "chan"), None, None, None)),
        check_vma=False,
    )
```

time: 176 us -> 98.7 us (0.56)
  waiting for transfers between devices: 80.2 us -> 27 us
  other arithmetic: 45.2 us -> 3.91 us
  Pallas kernels: 0 us -> 35.9 us
  matrix products: 30.7 us -> 0 us
  starting transfers between devices: 9.04 us -> 21.9 us
    ppermute x4 -> x6, waiting for transfers between devices: 80.2 us -> 27 us  [the longest x2 24.2 us: local(): near_in.append(lax.ppermute(piece, 'chan', near_pairs))]
    pallas_call x0 -> x11, Pallas kernels: none -> 35.9 us  [the longest x6 23.6 us: corr(): pl.pallas_call(functools.partial(corr_kernel, first, kind), grid_spec=plt...]
    dot_general x16 -> x0, matrix products: 30.7 us -> none  [add_block(): jnp.einsum('lfcwi,fcwj->lij', left, second_blk, preferred_element_type=jn...]
    convert_element_type x33 -> x3, other arithmetic: 27.2 us -> 0.16 us  [the longest x2 0.15 us: switch(): return jnp.stack([jnp.asarray(on), jnp.asarray(other)]).astype(jnp.int32)]
    ppermute x4 -> x6, starting transfers between devices: 9.04 us -> 21.9 us  [the longest x2 9.67 us: local(): near_in.append(lax.ppermute(piece, 'chan', near_pairs))]
    another operation x18 -> x2, other arithmetic: 10.8 us -> 1.81 us
    mul x3 -> x2, other arithmetic: 6.29 us -> 0.02 us  [the longest x1 0.01 us: lag_rows(): sin_part = -jnp.sin(phases[1:]) * factor * sign[None, :]]
    unnamed x6 -> x32, local copies, waits for them, and re-layouts: 6.48 us -> 8.35 us
  transfers between devices with their start and end apart: 4 -> 6, of which waited for: 2 -> 2; matrix products, arithmetic and copies ran while one was open for 24% -> 2% of each run, Pallas kernels for 0% -> 30%
where the time goes in v3:
time: 98.7 us; the launch traced here: 98 us
  Pallas kernels  35.9 us (36%)
  waiting for transfers between devices  27 us (27%)
  starting transfers between devices  21.9 us (22%)
  local copies, waits for them, and re-layouts  8.35 us (8%)
  other arithmetic  3.91 us (4%)
    ppermute x2, waiting for transfers between devices, local(): near_in.append(lax.ppermute(piece, 'chan', near_pairs))  24.2 us
    pallas_call x6, Pallas kernels, corr(): pl.pallas_call(functools.partial(corr_kernel, first, kind), grid_spec=plt...  23.6 us
    pallas_call x4, Pallas kernels, turn(): pl.pallas_call(turn_kernel, grid_spec=pltpu.PrefetchScalarGridSpec(num_sc...  11 us
    ppermute x2, starting transfers between devices, local(): near_in.append(lax.ppermute(piece, 'chan', near_pairs))  9.67 us
    unnamed x32, local copies, waits for them, and re-layouts  8.35 us
    ppermute x1, starting transfers between devices, local(): side_back = lax.ppermute(side_own, 'chan', side_pairs)  5.71 us
    ppermute x2, starting transfers between devices, local(): far_in.append(lax.ppermute(piece, 'chan', far_pairs))  4.67 us
    ppermute x1, waiting for transfers between devices, local(): side_back = lax.ppermute(side_own, 'chan', side_pairs)  2.75 us
  transfers between devices with their start and end apart: 6, of which 2 were waited for; matrix products, arithmetic and copies ran while one was open for 2% of the time, Pallas kernels for 30%

profile of v3, /device:TPU:0, one launch (start us, length us, event | category | flops | bytes accessed | tf_op | source)
XLA Modules:
  0.0 98.0 jit_solution(12406814329960510551)
XLA Ops:
  0.6 1.6 %copy-done = bf16[1024,2,4,128]{3,2,1,0:T(4,128)(2,1)S(1)} copy-done((bf16[1024,2,4,128]{3,2,1,0:T(4,128)(2,1)S(1)}, bf16[1024,2,4,128]{3,2,1,0:T(4,128)(2,1)}, u32[]{:S(2)}) %copy-start) | copy-done | bytes 2097176
  2.9 1.2 %mask.1 = (bf16[5120,128]{1,0:T(8,128)(2,1)S(1)}, bf16[3072,128]{1,0:T(8,128)(2,1)S(1)}) custom-call(s32[1,4]{1,0:T(1,128)S(1)} %copy-done.11, bf16[8192,128]{1,0:T(8,128)(2,1)S(1)} %bitcast.9), custom_call_target="tpu_custom_call" | custom-call | flops 1048576 | bytes 4194304 | tf_op jit(solution)/shard_map/mask/pallas_call | solution.py:64
  4.1 5.3 %collective-permute-start.3 = (bf16[3072,128]{1,0:T(8,128)(2,1)S(1)}, bf16[3072,128]{1,0:T(8,128)(2,1)S(1)}, u32[]{:S(2)}, u32[]{:S(2)}) collective-permute-start(bf16[3072,128]{1,0:T(8,128)(2,1)S(1)} %get-tuple-element.22.x_ref), channel_id=1, source_target_pairs={{2,1},{3,2},{4,3},{5,4},{6,5},{9,8},{10,9},{11,10},{12,11},{13,12}... | collective-permute-start | bytes 2359304 | tf_op jit(solution)/shard_map/ppermute | solution.py:250
  9.4 1.9 %collective-permute-start.2 = (bf16[3072,128]{1,0:T(8,128)(2,1)S(1)}, bf16[3072,128]{1,0:T(8,128)(2,1)}, u32[]{:S(2)}, u32[]{:S(2)}) collective-permute-start(bf16[3072,128]{1,0:T(8,128)(2,1)S(1)} %get-tuple-element.22.x_ref), channel_id=1, source_target_pairs={{8,0},{1,9},{2,10},{11,3},{4,12},{13,5},{6,14},{15,7},{0,1},{7,6},... | collective-permute-start | bytes 2359304 | tf_op jit(solution)/shard_map/ppermute | solution.py:249
  11.4 2.7 %collective-permute-start.1 = (bf16[5120,128]{1,0:T(8,128)(2,1)S(1)}, bf16[5120,128]{1,0:T(8,128)(2,1)}, u32[]{:S(2)}, u32[]{:S(2)}) collective-permute-start(bf16[5120,128]{1,0:T(8,128)(2,1)S(1)} %get-tuple-element.25.x_ref), channel_id=1, source_target_pairs={{8,0},{1,9},{2,10},{11,3},{4,12},{13,5},{6,14},{15,7},{0,1},{7,6},... | collective-permute-start | bytes 3932168 | tf_op jit(solution)/shard_map/ppermute | solution.py:249
  14.1 4.3 %collective-permute-start = (bf16[5120,128]{1,0:T(8,128)(2,1)S(1)}, bf16[5120,128]{1,0:T(8,128)(2,1)}, u32[]{:S(2)}, u32[]{:S(2)}) collective-permute-start(bf16[5120,128]{1,0:T(8,128)(2,1)S(1)} %get-tuple-element.25.x_ref), channel_id=1, source_target_pairs={{2,1},{3,2},{4,3},{5,4},{6,5},{9,8},{10,9},{11,10},{12,11},{13,12}... | collective-permute-start | bytes 3932168 | tf_op jit(solution)/shard_map/ppermute | solution.py:250
  18.5 0.9 multiply_convert_fusion
  20.4 1.8 %turn_own_1.1 = (bf16[128,3072]{1,0:T(8,128)(2,1)S(1)}, bf16[128,3072]{1,0:T(8,128)(2,1)S(1)}) custom-call(s32[2]{0:T(128)S(1)} %copy-done.10, bf16[3072,128]{1,0:T(8,128)(2,1)S(1)} %get-tuple-element.22.x_ref), custom_call_target="tpu_custom_call" | custom-call | bytes 2359296 | tf_op jit(solution)/shard_map/turn_own_1/pallas_call | solution.py:96
  24.1 2.7 %turn_own_0.1 = (bf16[128,5120]{1,0:T(8,128)(2,1)S(1)}, bf16[128,5120]{1,0:T(8,128)(2,1)S(1)}) custom-call(s32[2]{0:T(128)S(1)} %copy-done.10, bf16[5120,128]{1,0:T(8,128)(2,1)S(1)} %get-tuple-element.25.x_ref), custom_call_target="tpu_custom_call" | custom-call | bytes 3932160 | tf_op jit(solution)/shard_map/turn_own_0/pallas_call | solution.py:96
  26.8 1.1 %copy-done.12 = bf16[128,5120]{1,0:T(8,128)(2,1)} copy-done((bf16[128,5120]{1,0:T(8,128)(2,1)}, bf16[128,5120]{1,0:T(8,128)(2,1)S(1)}, u32[]{:S(2)}) %copy-start.12) | copy-done | bytes 1310744
  27.8 1.1 %copy-done.14 = bf16[128,5120]{1,0:T(8,128)(2,1)} copy-done((bf16[128,5120]{1,0:T(8,128)(2,1)}, bf16[128,5120]{1,0:T(8,128)(2,1)S(1)}, u32[]{:S(2)}) %copy-start.14) | copy-done | bytes 1310744
  29.1 24.2 %collective-permute-done.partner_ref.x_ref = bf16[5120,128]{1,0:T(8,128)(2,1)} collective-permute-done((bf16[5120,128]{1,0:T(8,128)(2,1)S(1)}, bf16[5120,128]{1,0:T(8,128)(2,1)}, u32[]{:S(2)}, u32[]{:S(2)}) %collective-permute-start) | collective-permute-done | bytes 1310752 | tf_op jit(solution)/shard_map/ppermute | solution.py:250
  53.3 4.7 %turn_side_0.1 = (bf16[128,5120]{1,0:T(8,128)(2,1)S(1)}, bf16[128,5120]{1,0:T(8,128)(2,1)S(1)}) custom-call(s32[2]{0:T(128)S(1)} %add_convert_fusion.active_ref, bf16[5120,128]{1,0:T(8,128)(2,1)} %collective-permute-done.partner_ref.x_ref), custom_call_target="tpu_custom_call" | custom-call | bytes 3932160 | tf_op jit(solution)/shard_map/turn_side_0/pallas_call | solution.py:96
  58.0 1.3 %copy-done.15 = bf16[128,5120]{1,0:T(8,128)(2,1)S(1)} copy-done((bf16[128,5120]{1,0:T(8,128)(2,1)S(1)}, bf16[128,5120]{1,0:T(8,128)(2,1)}, u32[]{:S(2)}) %copy-start.15) | copy-done | bytes 1310744
  59.3 1.6 %near_first.1.rest_0_ = f32[1152,128]{1,0:T(8,128)S(1)} custom-call(s32[2]{0:T(128)S(1)} %get-tuple-element.47.active_ref, bf16[128,5120]{1,0:T(8,128)(2,1)S(1)} %copy-done.13, bf16[128,5120]{1,0:T(8,128)(2,1)S(1)} %copy-done.15, bf16[9,8192]{1,0:T(8,128)(2,1)S(1)} %pad_maximum_fusion.coeff_ref, bf16[5120,128]{1,0:T(8,128)(2,1)} %collective-permute-done.partner_ref.x_ref), custom_call_target="tpu_custom_call" | custom-call | flops 1509949440 | bytes 3932160 | tf_op jit(solution)/shard_map/near_first/pallas_call | solution.py:199
  61.7 6.0 %far_first.1.rest_0_ = f32[1152,128]{1,0:T(8,128)S(1)} custom-call(s32[2]{0:T(128)S(1)} %get-tuple-element.46.active_ref, bf16[128,5120]{1,0:T(8,128)(2,1)S(1)} %copy-done.13, bf16[128,5120]{1,0:T(8,128)(2,1)S(1)} %copy-done.15, bf16[9,8192]{1,0:T(8,128)(2,1)S(1)} %pad_maximum_fusion.coeff_ref, bf16[5120,128]{1,0:T(8,128)(2,1)} %collective-permute-done.1.partner_ref), custom_call_target="tpu_custom_call" | custom-call | flops 1509949440 | bytes 3932160 | tf_op jit(solution)/shard_map/far_first/pallas_call | solution.py:199
  67.8 6.0 %side_first.1.rest_0_ = f32[1152,128]{1,0:T(8,128)S(1)} custom-call(s32[2]{0:T(128)S(1)} %add_convert_fusion.active_ref, bf16[128,5120]{1,0:T(8,128)(2,1)S(1)} %get-tuple-element.28.plain_ref, bf16[128,5120]{1,0:T(8,128)(2,1)S(1)} %get-tuple-element.29.swapped_ref, bf16[9,8192]{1,0:T(8,128)(2,1)S(1)} %pad_maximum_fusion.coeff_ref, ...), custom_call_target="tpu_custom_call" | custom-call | flops 1509949440 | bytes 3932160 | tf_op jit(solution)/shard_map/side_first/pallas_call | solution.py:199
  73.8 5.0 %far_last.1 = (bf16[9,128,128]{2,1,0:T(8,128)(2,1)S(1)}, bf16[9,128,128]{2,1,0:T(8,128)(2,1)}) custom-call(s32[2]{0:T(128)S(1)} %get-tuple-element.46.active_ref, bf16[128,3072]{1,0:T(8,128)(2,1)S(1)} %copy-done.2, bf16[128,3072]{1,0:T(8,128)(2,1)S(1)} %copy-done.4, bf16[9,8192]{1,0:T(8,128)(2,1)S(1)} %pad_maximum_fusion.coeff_ref, ...), custom_call_target="tpu_custom_call" | custom-call | flops 905969664 | bytes 2359296 | tf_op jit(solution)/shard_map/far_last/pallas_call | solution.py:199
  78.9 1.9 %collective-permute-start.4 = (bf16[9,128,128]{2,1,0:T(8,128)(2,1)}, bf16[9,128,128]{2,1,0:T(8,128)(2,1)}, u32[]{:S(2)}, u32[]{:S(2)}) collective-permute-start(bf16[9,128,128]{2,1,0:T(8,128)(2,1)} %get-tuple-element.32), channel_id=1, source_target_pairs={{0,8},{9,1},{10,2},{3,11},{12,4},{5,13},{14,6},{7,15},{1,0},{16,24... | collective-permute-start | bytes 884744 | tf_op jit(solution)/shard_map/ppermute | solution.py:264
  80.8 1.8 %turn_side_1.1 = (bf16[128,3072]{1,0:T(8,128)(2,1)S(1)}, bf16[128,3072]{1,0:T(8,128)(2,1)S(1)}) custom-call(s32[2]{0:T(128)S(1)} %add_convert_fusion.active_ref, bf16[3072,128]{1,0:T(8,128)(2,1)S(1)} %collective-permute-done.3.x_ref.partner_ref), custom_call_target="tpu_custom_call" | custom-call | bytes 2359296 | tf_op jit(solution)/shard_map/turn_side_1/pallas_call | solution.py:96
  82.7 4.2 %side_last.1 = bf16[9,128,128]{2,1,0:T(8,128)(2,1)S(1)} custom-call(s32[2]{0:T(128)S(1)} %add_convert_fusion.active_ref, bf16[128,3072]{1,0:T(8,128)(2,1)S(1)} %get-tuple-element.37.plain_ref, bf16[128,3072]{1,0:T(8,128)(2,1)S(1)} %get-tuple-element.38.swapped_ref, bf16[9,8192]{1,0:T(8,128)(2,1)S(1)} %pad_maximum_fusion.coeff_ref, ...), custom_call_target="tpu_custom_call" | custom-call | flops 905969664 | bytes 2359296 | tf_op jit(solution)/shard_map/side_last/pallas_call | solution.py:199
  86.9 5.7 %collective-permute-start.5 = (bf16[9,128,128]{2,1,0:T(8,128)(2,1)S(1)}, bf16[9,128,128]{2,1,0:T(8,128)(2,1)}, u32[]{:S(2)}, u32[]{:S(2)}) collective-permute-start(bf16[9,128,128]{2,1,0:T(8,128)(2,1)S(1)} %side_last.1), channel_id=1, source_target_pairs={{0,7},{7,15},{16,23},{23,31}} | collective-permute-start | bytes 884744 | tf_op jit(solution)/shard_map/ppermute | solution.py:268
  93.4 2.8 %collective-permute-done.5 = bf16[9,128,128]{2,1,0:T(8,128)(2,1)} collective-permute-done((bf16[9,128,128]{2,1,0:T(8,128)(2,1)S(1)}, bf16[9,128,128]{2,1,0:T(8,128)(2,1)}, u32[]{:S(2)}, u32[]{:S(2)}) %collective-permute-start.5) | collective-permute-done | bytes 294944 | tf_op jit(solution)/shard_map/ppermute | solution.py:268
  96.1 1.8 %select_bitcast_fusion = (bf16[1,9,128,128]{3,2,1,0:T(8,128)(2,1)}, bf16[1,9,128,128]{3,2,1,0:T(8,128)(2,1)}) fusion(bf16[9,128,128]{2,1,0:T(8,128)(2,1)S(1)} %copy-done.9, bf16[9,128,128]{2,1,0:T(8,128)(2,1)} %collective-permute-done.4, pred[]{:T(512)S(6)} %or.48, bf16[9,128,128]{2,1,0:T(8,128)(2,1)} %collective-permute-done.5, ...), kind=kLoop, calls=%fused_computation | loop fusion | flops 589824 | bytes 1769476 | tf_op jit(solution)/shard_map/broadcast_in_dim | solution.py:275
  (40 shorter events, 5.2 us)
Async XLA Ops:
  0.6 1.6 %copy-start = (bf16[1024,2,4,128]{3,2,1,0:T(4,128)(2,1)S(1)}, bf16[1024,2,4,128]{3,2,1,0:T(4,128)(2,1)}, u32[]{:S(2)}) copy-start(bf16[1024,2,4,128]{3,2,1,0:T(4,128)(2,1)} %param.2) | copy-start | bytes 6291460
  2.2 0.7 copy-start.11
  2.9 17.6 %copy-start.10 = (s32[2]{0:T(128)S(1)}, s32[2]{0:T(128)}, u32[]{:S(2)}) copy-start(s32[2]{0:T(128)} %constant.59.clone.1.active_ref) | copy-start | bytes 28
  4.1 69.7 %collective-permute-start.3 = (bf16[3072,128]{1,0:T(8,128)(2,1)S(1)}, bf16[3072,128]{1,0:T(8,128)(2,1)S(1)}, u32[]{:S(2)}, u32[]{:S(2)}) collective-permute-start(bf16[3072,128]{1,0:T(8,128)(2,1)S(1)} %get-tuple-element.22.x_ref), channel_id=1, source_target_pairs={{2,1},{3,2},{4,3},{5,4},{6,5},{9,8},{10,9},{11,10},{12,11},{13,12}... | collective-permute-start | bytes 2359304 | tf_op jit(solution)/shard_map/ppermute | solution.py:250
  9.4 64.4 %collective-permute-start.2 = (bf16[3072,128]{1,0:T(8,128)(2,1)S(1)}, bf16[3072,128]{1,0:T(8,128)(2,1)}, u32[]{:S(2)}, u32[]{:S(2)}) collective-permute-start(bf16[3072,128]{1,0:T(8,128)(2,1)S(1)} %get-tuple-element.22.x_ref), channel_id=1, source_target_pairs={{8,0},{1,9},{2,10},{11,3},{4,12},{13,5},{6,14},{15,7},{0,1},{7,6},... | collective-permute-start | bytes 2359304 | tf_op jit(solution)/shard_map/ppermute | solution.py:249
  11.4 50.3 %collective-permute-start.1 = (bf16[5120,128]{1,0:T(8,128)(2,1)S(1)}, bf16[5120,128]{1,0:T(8,128)(2,1)}, u32[]{:S(2)}, u32[]{:S(2)}) collective-permute-start(bf16[5120,128]{1,0:T(8,128)(2,1)S(1)} %get-tuple-element.25.x_ref), channel_id=1, source_target_pairs={{8,0},{1,9},{2,10},{11,3},{4,12},{13,5},{6,14},{15,7},{0,1},{7,6},... | collective-permute-start | bytes 3932168 | tf_op jit(solution)/shard_map/ppermute | solution.py:249
  14.1 39.2 %collective-permute-start = (bf16[5120,128]{1,0:T(8,128)(2,1)S(1)}, bf16[5120,128]{1,0:T(8,128)(2,1)}, u32[]{:S(2)}, u32[]{:S(2)}) collective-permute-start(bf16[5120,128]{1,0:T(8,128)(2,1)S(1)} %get-tuple-element.25.x_ref), channel_id=1, source_target_pairs={{2,1},{3,2},{4,3},{5,4},{6,5},{9,8},{10,9},{11,10},{12,11},{13,12}... | collective-permute-start | bytes 3932168 | tf_op jit(solution)/shard_map/ppermute | solution.py:250
  22.3 0.9 copy-start.1
  23.2 0.9 copy-start.3
  26.8 1.1 %copy-start.12 = (bf16[128,5120]{1,0:T(8,128)(2,1)}, bf16[128,5120]{1,0:T(8,128)(2,1)S(1)}, u32[]{:S(2)}) copy-start(bf16[128,5120]{1,0:T(8,128)(2,1)S(1)} %get-tuple-element.26.plain_ref) | copy-start | bytes 3932164
  27.8 1.1 %copy-start.14 = (bf16[128,5120]{1,0:T(8,128)(2,1)}, bf16[128,5120]{1,0:T(8,128)(2,1)S(1)}, u32[]{:S(2)}) copy-start(bf16[128,5120]{1,0:T(8,128)(2,1)S(1)} %get-tuple-element.27.swapped_ref) | copy-start | bytes 3932164
  28.9 29.1 %copy-start.13 = (bf16[128,5120]{1,0:T(8,128)(2,1)S(1)}, bf16[128,5120]{1,0:T(8,128)(2,1)}, u32[]{:S(2)}) copy-start(bf16[128,5120]{1,0:T(8,128)(2,1)} %copy-done.12) | copy-start | bytes 3932164
  58.0 1.3 %copy-start.15 = (bf16[128,5120]{1,0:T(8,128)(2,1)S(1)}, bf16[128,5120]{1,0:T(8,128)(2,1)}, u32[]{:S(2)}) copy-start(bf16[128,5120]{1,0:T(8,128)(2,1)} %copy-done.14) | copy-start | bytes 3932164
  60.9 0.8 copy-start.6
  67.7 6.1 %copy-start.2 = (bf16[128,3072]{1,0:T(8,128)(2,1)S(1)}, bf16[128,3072]{1,0:T(8,128)(2,1)}, u32[]{:S(2)}) copy-start(bf16[128,3072]{1,0:T(8,128)(2,1)} %copy-done.1) | copy-start | bytes 2359300
  67.7 6.1 %copy-start.4 = (bf16[128,3072]{1,0:T(8,128)(2,1)S(1)}, bf16[128,3072]{1,0:T(8,128)(2,1)}, u32[]{:S(2)}) copy-start(bf16[128,3072]{1,0:T(8,128)(2,1)} %copy-done.3) | copy-start | bytes 2359300
  78.9 8.0 %copy-start.8 = (bf16[9,128,128]{2,1,0:T(8,128)(2,1)}, bf16[9,128,128]{2,1,0:T(8,128)(2,1)S(1)}, u32[]{:S(2)}) copy-start(bf16[9,128,128]{2,1,0:T(8,128)(2,1)S(1)} %get-tuple-element.35) | copy-start | bytes 884740
  78.9 14.5 %collective-permute-start.4 = (bf16[9,128,128]{2,1,0:T(8,128)(2,1)}, bf16[9,128,128]{2,1,0:T(8,128)(2,1)}, u32[]{:S(2)}, u32[]{:S(2)}) collective-permute-start(bf16[9,128,128]{2,1,0:T(8,128)(2,1)} %get-tuple-element.32), channel_id=1, source_target_pairs={{0,8},{9,1},{10,2},{3,11},{12,4},{5,13},{14,6},{7,15},{1,0},{16,24... | collective-permute-start | bytes 884744 | tf_op jit(solution)/shard_map/ppermute | solution.py:264
  82.6 10.0 %copy-start.5 = (bf16[128,3072]{1,0:T(8,128)(2,1)S(1)}, bf16[128,3072]{1,0:T(8,128)(2,1)}, u32[]{:S(2)}) copy-start(bf16[128,3072]{1,0:T(8,128)(2,1)} %copy-done.3) | copy-start | bytes 2359300
  82.7 10.0 %copy-start.7 = (f32[1152,128]{1,0:T(8,128)S(1)}, f32[1152,128]{1,0:T(8,128)}, u32[]{:S(2)}) copy-start(f32[1152,128]{1,0:T(8,128)} %copy-done.6) | copy-start | bytes 1769476
  86.9 9.2 %collective-permute-start.5 = (bf16[9,128,128]{2,1,0:T(8,128)(2,1)S(1)}, bf16[9,128,128]{2,1,0:T(8,128)(2,1)}, u32[]{:S(2)}, u32[]{:S(2)}) collective-permute-start(bf16[9,128,128]{2,1,0:T(8,128)(2,1)S(1)} %side_last.1), channel_id=1, source_target_pairs={{0,7},{7,15},{16,23},{23,31}} | collective-permute-start | bytes 884744 | tf_op jit(solution)/shard_map/ppermute | solution.py:268
  92.6 3.5 %copy-start.9 = (bf16[9,128,128]{2,1,0:T(8,128)(2,1)S(1)}, bf16[9,128,128]{2,1,0:T(8,128)(2,1)}, u32[]{:S(2)}) copy-start(bf16[9,128,128]{2,1,0:T(8,128)(2,1)} %copy-done.8) | copy-start | bytes 884740

commit v4 on v3

v4 whole, which is shorter than its diff:
```python
import functools
import math

import jax
import jax.numpy as jnp
from jax import lax
from jax.experimental import pallas as pl
from jax.experimental.pallas import tpu as pltpu
from jax.sharding import PartitionSpec as P

HL = 4
LAGS = 2 * HL + 1
STEP = 2048
TILE = 1024
PARAMS = pltpu.CompilerParams(vmem_limit_bytes=48 * 1024 * 1024)


def lag_rows(freq_count, window_count):
    per_bin = 2 * window_count
    row = jnp.arange(freq_count * per_bin, dtype=jnp.int32)
    freq_values = (row // per_bin).astype(jnp.float32)
    sign = jnp.where(row % per_bin < window_count, 1.0, -1.0)
    lag_values = jnp.arange(HL + 1, dtype=jnp.float32)
    phases = jnp.pi / freq_count * lag_values[:, None] * freq_values[None, :]
    factor = 1.0 / math.sqrt(window_count * freq_count)
    cos_part = jnp.cos(phases) * factor
    sin_part = -jnp.sin(phases[1:]) * factor * sign[None, :]
    return jnp.concatenate([cos_part, sin_part], axis=0).astype(jnp.bfloat16)


def mask_kernel(flags_ref, x_ref, masked_ref):
    rows, cols = x_ref.shape
    windows = flags_ref.shape[1]
    window = lax.broadcasted_iota(jnp.int32, (16, cols), 0) % windows
    weights = jnp.zeros((16, cols), jnp.float32)
    for w in range(windows):
        weights = jnp.where(window == w, flags_ref[0, w].astype(jnp.float32), weights)
    weights = jnp.broadcast_to(weights.astype(jnp.bfloat16)[None], (rows // 16, 16, cols))
    masked_ref[...] = x_ref[...] * weights.reshape(rows, cols)


def mask(x, flags):
    rows, cols = x.shape
    return pl.pallas_call(
        mask_kernel,
        grid=(rows // TILE,),
        in_specs=[pl.BlockSpec(memory_space=pltpu.SMEM), pl.BlockSpec((TILE, cols), lambda s: (s, 0))],
        out_specs=pl.BlockSpec((TILE, cols), lambda s: (s, 0)),
        out_shape=jax.ShapeDtypeStruct((rows, cols), jnp.bfloat16),
        compiler_params=PARAMS,
        cost_estimate=pl.CostEstimate(flops=rows * cols, bytes_accessed=4 * rows * cols, transcendentals=0),
        name="mask",
    )(flags, x)


def turn_kernel(active_ref, x_ref, plain_ref, swapped_ref):
    @pl.when(active_ref[0] != 0)
    def _():
        rows, cols = x_ref.shape
        same = lax.broadcasted_iota(jnp.int32, (cols, cols), 0) == lax.broadcasted_iota(jnp.int32, (cols, cols), 1)
        eye = jnp.where(same, 1.0, 0.0).astype(jnp.bfloat16)
        source = lax.broadcasted_iota(jnp.int32, (2 * cols, 2 * cols), 0)
        target = lax.broadcasted_iota(jnp.int32, (2 * cols, 2 * cols), 1)
        exchange = jnp.where((source ^ 4) == target, 1.0, 0.0).astype(jnp.bfloat16)
        plain = lax.dot_general(eye, x_ref[...], (((1,), (1,)), ((), ())), preferred_element_type=jnp.float32)
        plain = plain.astype(jnp.bfloat16)
        plain_ref[...] = plain
        for t in range(0, rows, 2 * cols):
            swapped = jnp.dot(plain[:, t:t + 2 * cols], exchange, preferred_element_type=jnp.float32)
            swapped_ref[:, t:t + 2 * cols] = swapped.astype(jnp.bfloat16)


def turn(x, active, name):
    rows, cols = x.shape
    out = jax.ShapeDtypeStruct((cols, rows), jnp.bfloat16)
    return pl.pallas_call(
        turn_kernel,
        grid_spec=pltpu.PrefetchScalarGridSpec(
            num_scalar_prefetch=1,
            grid=(rows // STEP,),
            in_specs=[pl.BlockSpec((STEP, cols), lambda s, on: (s * on[0], 0))],
            out_specs=[pl.BlockSpec((cols, STEP), lambda s, on: (0, s * on[0]))] * 2,
        ),
        out_shape=[out, out],
        compiler_params=PARAMS,
        cost_estimate=pl.CostEstimate(flops=0, bytes_accessed=6 * rows * cols, transcendentals=0),
        name=name,
    )(active, x)


def lag_result(acc, at, cols, lag):
    k = abs(lag - HL)
    even = acc[k * cols:(k + 1) * cols, at]
    if k == 0:
        return even.astype(jnp.bfloat16)
    odd = acc[(HL + k) * cols:(HL + k + 1) * cols, at]
    return (even + odd if lag > HL else even - odd).astype(jnp.bfloat16)


def corr_kernel(kinds, switch_ref, plain_ref, swapped_ref, coeff_ref, *rest):
    count = len(kinds)
    partner_refs = rest[:count]
    outs = list(rest[count:-3])
    acc, *buffers = rest[-3:]
    step = pl.program_id(0)
    cols = plain_ref.shape[0]

    @pl.when(switch_ref[0] != 0)
    def _():
        @pl.when(step == 0)
        def _():
            acc[...] = jnp.zeros_like(acc)

        def build(t):
            at = slice(t * TILE, (t + 1) * TILE)
            for k in range(LAGS):
                part = plain_ref if k <= HL else swapped_ref
                buffers[t % 2][k * cols:(k + 1) * cols, :] = part[:, at] * coeff_ref[k:k + 1, at]

        build(0)
        for t in range(STEP // TILE):
            if (t + 1) * TILE < STEP:
                build(t + 1)
            partner = [ref[t * TILE:(t + 1) * TILE, :] for ref in partner_refs]
            partner = partner[0] if count == 1 else jnp.concatenate(partner, axis=1)
            acc[...] += jnp.dot(buffers[t % 2][...], partner, preferred_element_type=jnp.float32)

        @pl.when(step == pl.num_programs(0) - 1)
        def _():
            def write(out, index, mirrored):
                for lag in range(LAGS):
                    value = lag_result(acc, slice(index * cols, (index + 1) * cols), cols, lag)
                    if mirrored:
                        out[LAGS - 1 - lag] = value.T
                    else:
                        out[lag] = value

            for index, kind in enumerate(kinds):
                out = outs.pop(0)
                if kind == "either":
                    pl.when(switch_ref[1] == 0)(functools.partial(write, out, index, False))
                    pl.when(switch_ref[1] != 0)(functools.partial(write, out, index, True))
                else:
                    write(out, index, False)
                if kind == "both":
                    write(outs.pop(0), index, True)


def corr(switch, turned, coeffs, partners, kinds, name):
    plain, swapped = turned
    cols, rows = plain.shape
    count = len(partners)
    res_shape = jax.ShapeDtypeStruct((LAGS, cols, cols), jnp.bfloat16)
    res_spec = pl.BlockSpec((LAGS, cols, cols), lambda s, on: (0, 0, 0))
    results = count + kinds.count("both")
    return pl.pallas_call(
        functools.partial(corr_kernel, kinds),
        grid_spec=pltpu.PrefetchScalarGridSpec(
            num_scalar_prefetch=1,
            grid=(rows // STEP,),
            in_specs=[
                pl.BlockSpec((cols, STEP), lambda s, on: (0, s * on[0])),
                pl.BlockSpec((cols, STEP), lambda s, on: (0, s * on[0])),
                pl.BlockSpec((LAGS, STEP), lambda s, on: (0, s * on[0])),
            ] + [pl.BlockSpec((STEP, cols), lambda s, on: (s * on[0], 0))] * count,
            out_specs=[res_spec] * results,
            scratch_shapes=[pltpu.VMEM((LAGS * cols, count * cols), jnp.float32)]
            + [pltpu.VMEM((LAGS * cols, TILE), jnp.bfloat16)] * 2,
        ),
        out_shape=[res_shape] * results,
        compiler_params=PARAMS,
        cost_estimate=pl.CostEstimate(
            flops=2 * count * LAGS * cols * cols * rows,
            bytes_accessed=2 * (2 + count) * rows * cols,
            transcendentals=0,
        ),
        name=name,
    )(switch, plain, swapped, coeffs, *partners)


def local(spectra, quality):
    count = lax.axis_size("chan")
    half = count // 2
    me = lax.axis_index("chan")
    freq_count, _, window_count, cols = spectra.shape
    block = spectra.reshape(-1, cols)

    first_far, second_far = [], []
    for p in range(half):
        if p in (0, half - 1):
            first_far.append((p + half, p))
        elif p % 2 == 0 and p >= half // 2:
            first_far.append((p, p + half))
        elif p in (1, 3):
            second_far.append((p, p + half))
        else:
            second_far.append((p + half, p))
    late_near = [(2, 1), (4, 3)]
    first_pairs = first_far + [(0, 1), (half - 1, half - 2)]
    second_pairs = second_far + late_near
    near_pairs = [(d + 1, d) for d in range(1, count - 1) if d not in (1, 3, half - 2, half - 1)]
    near_pairs += [(0, half - 1), (half - 1, 0)]
    first_back = [(t, s) for s, t in first_far] + [(1, 0)]
    second_back = [(t, s) for s, t in second_far]
    side_pairs = [(0, half - 1), (half - 1, count - 1)]

    def among(devices):
        return functools.reduce(jnp.logical_or, [me == d for d in devices])

    def switch(on, other=False):
        return jnp.stack([jnp.asarray(on), jnp.asarray(other)]).astype(jnp.int32)

    always = switch(True)
    second_on = switch(among([t for _, t in second_pairs]))
    side_on = switch(among([0, half - 1]), me == half - 1)

    masked = mask(block, quality)
    first_in = lax.ppermute(masked, "chan", first_pairs)
    near_in = lax.ppermute(masked, "chan", near_pairs)
    coeffs = lag_rows(freq_count, window_count)
    own = turn(masked, always, "turn_own")
    late, first_in, near_in, own, coeffs = lax.optimization_barrier((masked, first_in, near_in, own, coeffs))
    second_in = lax.ppermute(late, "chan", second_pairs)

    near, first, first_mirror = corr(always, own, coeffs, [near_in, first_in], ["plain", "both"], "near_first")
    first_returned = lax.ppermute(first_mirror, "chan", first_back)
    near, near_in = lax.optimization_barrier((near, near_in))
    side_turned = turn(near_in, side_on, "turn_side")
    side, = corr(side_on, side_turned, coeffs, [first_in], ["either"], "side")
    side_returned = lax.ppermute(side, "chan", side_pairs)

    side, second_in = lax.optimization_barrier((side, second_in))
    second, second_mirror = corr(second_on, own, coeffs, [second_in], ["both"], "second")
    second_returned = lax.ppermute(second_mirror, "chan", second_back)

    far = jnp.where(among([t for _, t in first_far]), first, second)
    far = jnp.where(among([s for s, _ in first_far]), first_returned, far)
    far = jnp.where(among([s for s, _ in second_far]), second_returned, far)
    near = jnp.where(among([t for _, t in late_near]), second, near)
    near = jnp.where(among([half - 1, count - 1]), side_returned, near)
    near = jnp.where(me == 0, first_returned, jnp.where(me == half - 2, first, near))
    return near[None], far[None]


def solution(mesh):
    return jax.shard_map(
        local,
        mesh=mesh,
        in_specs=(P(None, None, None, ("grp", "chan")), P(("grp", "chan"), None)),
        out_specs=(P(("grp", "chan"), None, None, None), P(("grp", "chan"), None, None, None)),
        check_vma=False,
    )
```

time: 98.7 us -> 86.8 us (0.88)
  the two profiles are of different devices: /device:TPU:0 before, /device:TPU:1 now
where the time goes in v4:
time: 86.8 us; the launch traced here: 86.2 us
  starting transfers between devices  40.5 us (47%)
  Pallas kernels  24.8 us (29%)
  local copies, waits for them, and re-layouts  10 us (12%)
  waiting for transfers between devices  7.01 us (8%)
  other arithmetic  3.01 us (3%)
  between operations  0.96 us (1%)
    ppermute x1, starting transfers between devices, local(): second_in = lax.ppermute(late, 'chan', second_pairs)  21.6 us
    pallas_call x3, Pallas kernels, corr(): pl.pallas_call(functools.partial(corr_kernel, kinds), grid_spec=pltpu.Pre...  17.8 us
    ppermute x1, starting transfers between devices, local(): first_returned = lax.ppermute(first_mirror, 'chan', first_back)  14.8 us
    unnamed x24, local copies, waits for them, and re-layouts  10 us
    ppermute x1, waiting for transfers between devices, local(): second_returned = lax.ppermute(second_mirror, 'chan', second_back)  7 us
    pallas_call x2, Pallas kernels, turn(): pl.pallas_call(turn_kernel, grid_spec=pltpu.PrefetchScalarGridSpec(num_sc...  5.99 us
    another operation x2, other arithmetic  1.81 us
  transfers between devices with their start and end apart: 6, of which 1 were waited for; matrix products, arithmetic and copies ran while one was open for 2% of the time, Pallas kernels for 28%

profile of v4, /device:TPU:1, one launch (start us, length us, event | category | flops | bytes accessed | tf_op | source)
XLA Modules:
  0.0 86.2 jit_solution(10720631136738439033)
XLA Ops:
  0.6 1.6 %copy-done.1 = bf16[1024,2,4,128]{3,2,1,0:T(4,128)(2,1)S(1)} copy-done((bf16[1024,2,4,128]{3,2,1,0:T(4,128)(2,1)S(1)}, bf16[1024,2,4,128]{3,2,1,0:T(4,128)(2,1)}, u32[]{:S(2)}) %copy-start.1) | copy-done | bytes 2097176
  2.2 0.7 copy-done.2
  2.9 1.0 %mask.1.x_ref = bf16[8192,128]{1,0:T(8,128)(2,1)S(1)} custom-call(s32[1,4]{1,0:T(1,128)S(1)} %copy-done.2, bf16[8192,128]{1,0:T(8,128)(2,1)S(1)} %bitcast.8), custom_call_target="tpu_custom_call" | custom-call | flops 1048576 | bytes 4194304 | tf_op jit(solution)/shard_map/mask/pallas_call | solution.py:44
  3.9 1.3 %collective-permute-start = (bf16[8192,128]{1,0:T(8,128)(2,1)S(1)}, bf16[8192,128]{1,0:T(8,128)(2,1)S(1)}, u32[]{:S(2)}, u32[]{:S(2)}) collective-permute-start(bf16[8192,128]{1,0:T(8,128)(2,1)S(1)} %mask.1.x_ref), channel_id=1, source_target_pairs={{8,0},{4,12},{6,14},{15,7},{0,1},{7,6},{24,16},{20,28},{22,30},{31... | collective-permute-start | bytes 6291464 | tf_op jit(solution)/shard_map/ppermute | solution.py:218
  5.2 0.8 collective-permute-start.1
  6.1 4.3 %turn_own.1 = (bf16[128,8192]{1,0:T(8,128)(2,1)S(1)}, bf16[128,8192]{1,0:T(8,128)(2,1)S(1)}) custom-call(s32[2]{0:T(128)S(1)} %copy-done.3, bf16[8192,128]{1,0:T(8,128)(2,1)} %copy-done), custom_call_target="tpu_custom_call" | custom-call | bytes 6291456 | tf_op jit(solution)/shard_map/turn_own/pallas_call | solution.py:76
  10.4 1.3 %copy-done.4 = bf16[128,8192]{1,0:T(8,128)(2,1)} copy-done((bf16[128,8192]{1,0:T(8,128)(2,1)}, bf16[128,8192]{1,0:T(8,128)(2,1)S(1)}, u32[]{:S(2)}) %copy-start.4) | copy-done | bytes 2097176
  11.7 1.3 %copy-done.7 = bf16[128,8192]{1,0:T(8,128)(2,1)} copy-done((bf16[128,8192]{1,0:T(8,128)(2,1)}, bf16[128,8192]{1,0:T(8,128)(2,1)S(1)}, u32[]{:S(2)}) %copy-start.7) | copy-done | bytes 2097176
  13.0 0.9 %multiply_convert_fusion = (bf16[5,8192]{1,0:T(8,128)(2,1)S(1)}, f32[5,8192]{1,0:T(8,128)S(1)}) fusion(f32[8192]{0:T(1024)S(1)} %fusion.9, f32[5]{0:T(128)S(1)} %iota_multiply_fusion), kind=kLoop, calls=%fused_computation.3 | loop fusion | flops 122880 | bytes 278548 | tf_op jit(solution)/shard_map/convert
  13.9 0.9 %fusion.2 = bf16[4,8192]{1,0:T(4,128)(2,1)S(1)} fusion(f32[5,8192]{1,0:T(8,128)S(1)} %get-tuple-element.41, f32[8192]{0:T(1024)S(1)} %select_multiply_fusion), kind=kLoop, calls=%fused_computation.7 | loop fusion | flops 98304 | bytes 229376 | tf_op jit(solution)/shard_map/convert.1
  14.9 1.4 %copy-done.10 = bf16[8192,128]{1,0:T(8,128)(2,1)} copy-done((bf16[8192,128]{1,0:T(8,128)(2,1)}, bf16[8192,128]{1,0:T(8,128)(2,1)S(1)}, u32[]{:S(2)}) %copy-start.10) | copy-done | bytes 2097176
  16.3 0.6 copy-done.11
  16.9 21.6 %collective-permute-start.4 = (bf16[8192,128]{1,0:T(8,128)(2,1)}, bf16[8192,128]{1,0:T(8,128)(2,1)}, u32[]{:S(2)}, u32[]{:S(2)}) collective-permute-start(bf16[8192,128]{1,0:T(8,128)(2,1)} %copy-done), channel_id=1, source_target_pairs={{1,9},{10,2},{3,11},{13,5},{2,1},{4,3},{17,25},{26,18},{19,27},{29... | collective-permute-start | bytes 6291464 | tf_op jit(solution)/shard_map/ppermute | solution.py:223
  38.7 1.6 %copy-done.5 = bf16[128,8192]{1,0:T(8,128)(2,1)S(1)} copy-done((bf16[128,8192]{1,0:T(8,128)(2,1)S(1)}, bf16[128,8192]{1,0:T(8,128)(2,1)}, u32[]{:S(2)}) %copy-start.5) | copy-done | bytes 2097176
  40.3 1.6 %copy-done.8 = bf16[128,8192]{1,0:T(8,128)(2,1)S(1)} copy-done((bf16[128,8192]{1,0:T(8,128)(2,1)S(1)}, bf16[128,8192]{1,0:T(8,128)(2,1)}, u32[]{:S(2)}) %copy-start.8) | copy-done | bytes 2097176
  41.9 8.0 %near_first.1 = (bf16[9,128,128]{2,1,0:T(8,128)(2,1)S(1)}, bf16[9,128,128]{2,1,0:T(8,128)(2,1)S(1)}, bf16[9,128,128]{2,1,0:T(8,128)(2,1)S(1)}) custom-call(s32[2]{0:T(128)S(1)} %copy-done.3, bf16[128,8192]{1,0:T(8,128)(2,1)S(1)} %copy-done.5, bf16[128,8192]{1,0:T(8,128)(2,1)S(1)} %copy-done.8, bf16[9,8192]{1,0:T(8,128)(2,1)S(1)} %pad_maximum_fusion.coeff_ref, ...), custom_call_target="tpu_custom_call" | custom-call | flops 4831838208 | bytes 8388608 | tf_op jit(solution)/shard_map/near_first/pallas_call | solution.py:156
  49.9 1.7 %turn_side.1 = (bf16[128,8192]{1,0:T(8,128)(2,1)S(1)}, bf16[128,8192]{1,0:T(8,128)(2,1)S(1)}) custom-call(s32[2]{0:T(128)S(1)} %add_convert_fusion.active_ref.switch_ref, bf16[8192,128]{1,0:T(8,128)(2,1)} %copy-done.10), custom_call_target="tpu_custom_call" | custom-call | bytes 6291456 | tf_op jit(solution)/shard_map/turn_side/pallas_call | solution.py:76
  51.6 2.0 %side.1 = bf16[9,128,128]{2,1,0:T(8,128)(2,1)S(1)} custom-call(s32[2]{0:T(128)S(1)} %add_convert_fusion.active_ref.switch_ref, bf16[128,8192]{1,0:T(8,128)(2,1)S(1)} %get-tuple-element.31.plain_ref, bf16[128,8192]{1,0:T(8,128)(2,1)S(1)} %get-tuple-element.32.swapped_ref, bf16[9,8192]{1,0:T(8,128)(2,1)S(1)} %pad_maximum_fusion.coeff_ref, ...), custom_call_target="tpu_custom_call" | custom-call | flops 2415919104 | bytes 6291456 | tf_op jit(solution)/shard_map/side/pallas_call | solution.py:156
  53.7 0.7 collective-permute-start.3
  54.3 14.8 %collective-permute-start.2 = (bf16[9,128,128]{2,1,0:T(8,128)(2,1)S(1)}, bf16[9,128,128]{2,1,0:T(8,128)(2,1)S(1)}, u32[]{:S(2)}, u32[]{:S(2)}) collective-permute-start(bf16[9,128,128]{2,1,0:T(8,128)(2,1)S(1)} %get-tuple-element.27), channel_id=1, source_target_pairs={{0,8},{12,4},{14,6},{7,15},{1,0},{16,24},{28,20},{30,22},{23,31},{... | collective-permute-start | bytes 884744 | tf_op jit(solution)/shard_map/ppermute | solution.py:226
  69.2 7.7 %second.1 = (bf16[9,128,128]{2,1,0:T(8,128)(2,1)S(1)}, bf16[9,128,128]{2,1,0:T(8,128)(2,1)S(1)}) custom-call(s32[2]{0:T(128)S(1)} %add_convert_fusion.1.switch_ref, bf16[128,8192]{1,0:T(8,128)(2,1)S(1)} %copy-done.6, bf16[128,8192]{1,0:T(8,128)(2,1)S(1)} %copy-done.9, bf16[9,8192]{1,0:T(8,128)(2,1)S(1)} %pad_maximum_fusion.coeff_ref, ...), custom_call_target="tpu_custom_call" | custom-call | flops 2415919104 | bytes 6291456 | tf_op jit(solution)/shard_map/second/pallas_call | solution.py:156
  76.9 1.3 %collective-permute-start.5 = (bf16[9,128,128]{2,1,0:T(8,128)(2,1)S(1)}, bf16[9,128,128]{2,1,0:T(8,128)(2,1)S(1)}, u32[]{:S(2)}, u32[]{:S(2)}) collective-permute-start(bf16[9,128,128]{2,1,0:T(8,128)(2,1)S(1)} %get-tuple-element.37), channel_id=1, source_target_pairs={{9,1},{2,10},{11,3},{5,13},{25,17},{18,26},{27,19},{21,29}} | collective-permute-start | bytes 884744 | tf_op jit(solution)/shard_map/ppermute | solution.py:234
  78.3 7.0 %collective-permute-done.5 = bf16[9,128,128]{2,1,0:T(8,128)(2,1)S(1)} collective-permute-done((bf16[9,128,128]{2,1,0:T(8,128)(2,1)S(1)}, bf16[9,128,128]{2,1,0:T(8,128)(2,1)S(1)}, u32[]{:S(2)}, u32[]{:S(2)}) %collective-permute-start.5) | collective-permute-done | bytes 294944 | tf_op jit(solution)/shard_map/ppermute | solution.py:234
  85.3 0.9 %select_bitcast_fusion = (bf16[1,9,128,128]{3,2,1,0:T(8,128)(2,1)}, bf16[1,9,128,128]{3,2,1,0:T(8,128)(2,1)}) fusion(bf16[9,128,128]{2,1,0:T(8,128)(2,1)S(1)} %collective-permute-done.5, bf16[9,128,128]{2,1,0:T(8,128)(2,1)S(1)} %collective-permute-done.2, bf16[9,128,128]{2,1,0:T(8,128)(2,1)S(1)} %get-tuple-element.28, ...), kind=kLoop, calls=%fused_computation | loop fusion | flops 1032192 | bytes 2359303 | tf_op jit(solution)/shard_map/broadcast_in_dim | solution.py:242
  (27 shorter events, 0.3 us)
Async XLA Ops:
  0.6 1.6 %copy-start.1 = (bf16[1024,2,4,128]{3,2,1,0:T(4,128)(2,1)S(1)}, bf16[1024,2,4,128]{3,2,1,0:T(4,128)(2,1)}, u32[]{:S(2)}) copy-start(bf16[1024,2,4,128]{3,2,1,0:T(4,128)(2,1)} %param.2) | copy-start | bytes 6291460
  2.2 0.7 copy-start.2
  2.9 3.2 %copy-start.3 = (s32[2]{0:T(128)S(1)}, s32[2]{0:T(128)}, u32[]{:S(2)}) copy-start(s32[2]{0:T(128)} %constant.26.clone.1.active_ref.switch_ref) | copy-start | bytes 28
  3.9 2.2 %copy-start = (bf16[8192,128]{1,0:T(8,128)(2,1)}, bf16[8192,128]{1,0:T(8,128)(2,1)S(1)}, u32[]{:S(2)}) copy-start(bf16[8192,128]{1,0:T(8,128)(2,1)S(1)} %mask.1.x_ref) | copy-start | bytes 6291460
  3.9 11.0 %collective-permute-start = (bf16[8192,128]{1,0:T(8,128)(2,1)S(1)}, bf16[8192,128]{1,0:T(8,128)(2,1)S(1)}, u32[]{:S(2)}, u32[]{:S(2)}) collective-permute-start(bf16[8192,128]{1,0:T(8,128)(2,1)S(1)} %mask.1.x_ref), channel_id=1, source_target_pairs={{8,0},{4,12},{6,14},{15,7},{0,1},{7,6},{24,16},{20,28},{22,30},{31... | collective-permute-start | bytes 6291464 | tf_op jit(solution)/shard_map/ppermute | solution.py:218
  5.2 9.7 %collective-permute-start.1 = (bf16[8192,128]{1,0:T(8,128)(2,1)S(1)}, bf16[8192,128]{1,0:T(8,128)(2,1)S(1)}, u32[]{:S(2)}, u32[]{:S(2)}) collective-permute-start(bf16[8192,128]{1,0:T(8,128)(2,1)S(1)} %mask.1.x_ref), channel_id=1, source_target_pairs={{3,2},{5,4},{6,5},{9,8},{10,9},{11,10},{12,11},{13,12},{14,13},{15... | collective-permute-start | bytes 6291464 | tf_op jit(solution)/shard_map/ppermute | solution.py:219
  10.4 1.3 %copy-start.4 = (bf16[128,8192]{1,0:T(8,128)(2,1)}, bf16[128,8192]{1,0:T(8,128)(2,1)S(1)}, u32[]{:S(2)}) copy-start(bf16[128,8192]{1,0:T(8,128)(2,1)S(1)} %get-tuple-element.22.plain_ref) | copy-start | bytes 6291460
  11.7 1.3 %copy-start.7 = (bf16[128,8192]{1,0:T(8,128)(2,1)}, bf16[128,8192]{1,0:T(8,128)(2,1)S(1)}, u32[]{:S(2)}) copy-start(bf16[128,8192]{1,0:T(8,128)(2,1)S(1)} %get-tuple-element.23.swapped_ref) | copy-start | bytes 6291460
  14.9 2.0 %copy-start.11 = (bf16[8192,128]{1,0:T(8,128)(2,1)}, bf16[8192,128]{1,0:T(8,128)(2,1)S(1)}, u32[]{:S(2)}) copy-start(bf16[8192,128]{1,0:T(8,128)(2,1)S(1)} %collective-permute-done.rest_1_.rest_0_) | copy-start | bytes 6291460
  14.9 1.4 %copy-start.10 = (bf16[8192,128]{1,0:T(8,128)(2,1)}, bf16[8192,128]{1,0:T(8,128)(2,1)S(1)}, u32[]{:S(2)}) copy-start(bf16[8192,128]{1,0:T(8,128)(2,1)S(1)} %collective-permute-done.1.rest_0_.x_ref) | copy-start | bytes 6291460
  16.9 52.3 %collective-permute-start.4 = (bf16[8192,128]{1,0:T(8,128)(2,1)}, bf16[8192,128]{1,0:T(8,128)(2,1)}, u32[]{:S(2)}, u32[]{:S(2)}) collective-permute-start(bf16[8192,128]{1,0:T(8,128)(2,1)} %copy-done), channel_id=1, source_target_pairs={{1,9},{10,2},{3,11},{13,5},{2,1},{4,3},{17,25},{26,18},{19,27},{29... | collective-permute-start | bytes 6291464 | tf_op jit(solution)/shard_map/ppermute | solution.py:223
  38.7 1.6 %copy-start.5 = (bf16[128,8192]{1,0:T(8,128)(2,1)S(1)}, bf16[128,8192]{1,0:T(8,128)(2,1)}, u32[]{:S(2)}) copy-start(bf16[128,8192]{1,0:T(8,128)(2,1)} %copy-done.4) | copy-start | bytes 6291460
  40.3 1.6 %copy-start.8 = (bf16[128,8192]{1,0:T(8,128)(2,1)S(1)}, bf16[128,8192]{1,0:T(8,128)(2,1)}, u32[]{:S(2)}) copy-start(bf16[128,8192]{1,0:T(8,128)(2,1)} %copy-done.7) | copy-start | bytes 6291460
  51.6 17.6 %copy-start.6 = (bf16[128,8192]{1,0:T(8,128)(2,1)S(1)}, bf16[128,8192]{1,0:T(8,128)(2,1)}, u32[]{:S(2)}) copy-start(bf16[128,8192]{1,0:T(8,128)(2,1)} %copy-done.4) | copy-start | bytes 6291460
  51.6 17.6 %copy-start.9 = (bf16[128,8192]{1,0:T(8,128)(2,1)S(1)}, bf16[128,8192]{1,0:T(8,128)(2,1)}, u32[]{:S(2)}) copy-start(bf16[128,8192]{1,0:T(8,128)(2,1)} %copy-done.7) | copy-start | bytes 6291460
  53.7 24.6 %collective-permute-start.3 = (bf16[9,128,128]{2,1,0:T(8,128)(2,1)S(1)}, bf16[9,128,128]{2,1,0:T(8,128)(2,1)S(1)}, u32[]{:S(2)}, u32[]{:S(2)}) collective-permute-start(bf16[9,128,128]{2,1,0:T(8,128)(2,1)S(1)} %side.1), channel_id=1, source_target_pairs={{0,7},{7,15},{16,23},{23,31}} | collective-permute-start | bytes 884744 | tf_op jit(solution)/shard_map/ppermute | solution.py:230
  54.3 24.0 %collective-permute-start.2 = (bf16[9,128,128]{2,1,0:T(8,128)(2,1)S(1)}, bf16[9,128,128]{2,1,0:T(8,128)(2,1)S(1)}, u32[]{:S(2)}, u32[]{:S(2)}) collective-permute-start(bf16[9,128,128]{2,1,0:T(8,128)(2,1)S(1)} %get-tuple-element.27), channel_id=1, source_target_pairs={{0,8},{12,4},{14,6},{7,15},{1,0},{16,24},{28,20},{30,22},{23,31},{... | collective-permute-start | bytes 884744 | tf_op jit(solution)/shard_map/ppermute | solution.py:226
  76.9 8.4 %collective-permute-start.5 = (bf16[9,128,128]{2,1,0:T(8,128)(2,1)S(1)}, bf16[9,128,128]{2,1,0:T(8,128)(2,1)S(1)}, u32[]{:S(2)}, u32[]{:S(2)}) collective-permute-start(bf16[9,128,128]{2,1,0:T(8,128)(2,1)S(1)} %get-tuple-element.37), channel_id=1, source_target_pairs={{9,1},{2,10},{11,3},{5,13},{25,17},{18,26},{27,19},{21,29}} | collective-permute-start | bytes 884744 | tf_op jit(solution)/shard_map/ppermute | solution.py:234

commit v5 on v4

v5 whole, which is shorter than its diff:
```python
import functools
import math

import jax
import jax.numpy as jnp
from jax import lax
from jax.experimental import pallas as pl
from jax.experimental.pallas import tpu as pltpu
from jax.sharding import PartitionSpec as P

HL = 4
LAGS = 2 * HL + 1
STEP = 1024
ENDS = (5, 8)
PARAMS = pltpu.CompilerParams(vmem_limit_bytes=63 * 1024 * 1024)


def lag_rows(freq_count, window_count):
    per_bin = 2 * window_count
    row = jnp.arange(freq_count * per_bin, dtype=jnp.int32)
    freq_values = (row // per_bin).astype(jnp.float32)
    sign = jnp.where(row % per_bin < window_count, 1.0, -1.0)
    lag_values = jnp.arange(HL + 1, dtype=jnp.float32)
    phases = jnp.pi / freq_count * lag_values[:, None] * freq_values[None, :]
    factor = 1.0 / math.sqrt(window_count * freq_count)
    cos_part = jnp.cos(phases) * factor
    sin_part = -jnp.sin(phases[1:]) * factor * sign[None, :]
    return jnp.concatenate([cos_part, sin_part], axis=0).astype(jnp.bfloat16)


def piece_specs(pieces, active):
    specs, begin = [], 0
    for piece in pieces:
        rows, cols = piece.shape
        count = rows // STEP

        def place(step, *switch, begin=begin, count=count):
            at = jnp.clip(step - begin, 0, count - 1)
            return (at * switch[0][0] if active else at, 0)

        specs.append(pl.BlockSpec((STEP, cols), place))
        begin += count
    return specs


def pick(refs, ends, step):
    value = refs[-1][...]
    for ref, end in reversed(list(zip(refs[:-1], ends))):
        value = jnp.where(step < end, ref[...], value)
    return value


def piece_ends(pieces):
    ends, end = [], 0
    for piece in pieces:
        end += piece.shape[0] // STEP
        ends.append(end)
    return ends


def mask_kernel(ends, flags_ref, x_ref, *piece_refs):
    rows, cols = x_ref.shape
    windows = flags_ref.shape[1]
    step = pl.program_id(0)
    window = lax.broadcasted_iota(jnp.int32, (16, cols), 0) % windows
    weights = jnp.zeros((16, cols), jnp.float32)
    for w in range(windows):
        weights = jnp.where(window == w, flags_ref[0, w].astype(jnp.float32), weights)
    weights = jnp.broadcast_to(weights.astype(jnp.bfloat16)[None], (rows // 16, 16, cols))
    masked = x_ref[...] * weights.reshape(rows, cols)
    begin = 0
    for end, piece_ref in zip(ends, piece_refs):
        @pl.when((step >= begin) & (step < end))
        def _():
            piece_ref[...] = masked
        begin = end


def mask(x, flags):
    rows, cols = x.shape
    ends = [rows * e // 8 for e in ENDS]
    shapes = [jax.ShapeDtypeStruct((e - b, cols), jnp.bfloat16) for b, e in zip([0] + ends, ends)]
    return pl.pallas_call(
        functools.partial(mask_kernel, piece_ends(shapes)),
        grid=(rows // STEP,),
        in_specs=[pl.BlockSpec(memory_space=pltpu.SMEM), pl.BlockSpec((STEP, cols), lambda s: (s, 0))],
        out_specs=piece_specs(shapes, False),
        out_shape=shapes,
        compiler_params=PARAMS,
        cost_estimate=pl.CostEstimate(flops=rows * cols, bytes_accessed=4 * rows * cols, transcendentals=0),
        name="mask",
    )(flags, x)


def turn_kernel(ends, switch_ref, *refs):
    plain_ref, swapped_ref = refs[-2:]

    @pl.when(switch_ref[0] != 0)
    def _():
        x = pick(refs[:-2], ends, pl.program_id(0))
        rows, cols = x.shape
        same = lax.broadcasted_iota(jnp.int32, (cols, cols), 0) == lax.broadcasted_iota(jnp.int32, (cols, cols), 1)
        eye = jnp.where(same, 1.0, 0.0).astype(jnp.bfloat16)
        source = lax.broadcasted_iota(jnp.int32, (2 * cols, 2 * cols), 0)
        target = lax.broadcasted_iota(jnp.int32, (2 * cols, 2 * cols), 1)
        exchange = jnp.where((source ^ 4) == target, 1.0, 0.0).astype(jnp.bfloat16)
        plain = lax.dot_general(eye, x, (((1,), (1,)), ((), ())), preferred_element_type=jnp.float32)
        plain = plain.astype(jnp.bfloat16)
        plain_ref[...] = plain
        for t in range(0, rows, 2 * cols):
            swapped = jnp.dot(plain[:, t:t + 2 * cols], exchange, preferred_element_type=jnp.float32)
            swapped_ref[:, t:t + 2 * cols] = swapped.astype(jnp.bfloat16)


def turn(pieces, switch, name, common=True):
    cols = pieces[0].shape[1]
    rows = sum(piece.shape[0] for piece in pieces)
    out = jax.ShapeDtypeStruct((cols, rows), jnp.bfloat16)
    return pl.pallas_call(
        functools.partial(turn_kernel, piece_ends(pieces)),
        grid_spec=pltpu.PrefetchScalarGridSpec(
            num_scalar_prefetch=1,
            grid=(rows // STEP,),
            in_specs=piece_specs(pieces, True),
            out_specs=[pl.BlockSpec((cols, STEP), lambda s, on: (0, s * on[0]))] * 2,
        ),
        out_shape=[out, out],
        compiler_params=PARAMS,
        cost_estimate=pl.CostEstimate(flops=0, bytes_accessed=6 * rows * cols if common else 0, transcendentals=0),
        name=name,
    )(switch, *pieces)


def lag_result(acc, at, cols, lag):
    k = abs(lag - HL)
    even = acc[k * cols:(k + 1) * cols, at]
    if k == 0:
        return even.astype(jnp.bfloat16)
    odd = acc[(HL + k) * cols:(HL + k + 1) * cols, at]
    return (even + odd if lag > HL else even - odd).astype(jnp.bfloat16)


def corr_kernel(ends, first, kinds, switch_ref, plain_ref, swapped_ref, coeff_ref, *rest):
    rest = list(rest)
    partner_refs = [[rest.pop(0) for _ in group] for group in ends]
    acc_in = None if first else rest.pop(0)
    scaled = rest.pop()
    acc = rest.pop()
    step = pl.program_id(0)
    cols = plain_ref.shape[0]

    @pl.when(switch_ref[0] != 0)
    def _():
        @pl.when(step == 0)
        def _():
            acc[...] = jnp.zeros_like(acc) if first else acc_in[...]

        for k in range(LAGS):
            part = plain_ref if k <= HL else swapped_ref
            scaled[k * cols:(k + 1) * cols, :] = part[...] * coeff_ref[k:k + 1, :]
        partner = [pick(refs, group, step) for refs, group in zip(partner_refs, ends)]
        partner = partner[0] if len(partner) == 1 else jnp.concatenate(partner, axis=1)
        acc[...] += jnp.dot(scaled[...], partner, preferred_element_type=jnp.float32)

        @pl.when(step == pl.num_programs(0) - 1)
        def _():
            def write(out, index, mirrored):
                for lag in range(LAGS):
                    value = lag_result(acc, slice(index * cols, (index + 1) * cols), cols, lag)
                    if mirrored:
                        out[LAGS - 1 - lag] = value.T
                    else:
                        out[lag] = value

            for index, kind in enumerate(kinds):
                out = rest.pop(0)
                if kind == "either":
                    pl.when(switch_ref[1] == 0)(functools.partial(write, out, index, False))
                    pl.when(switch_ref[1] != 0)(functools.partial(write, out, index, True))
                else:
                    write(out, index, False)
                if kind == "both":
                    write(rest.pop(0), index, True)


def corr(switch, turned, coeffs, partners, kinds, name, start=0, acc=None, common=True):
    plain, swapped = turned
    cols = plain.shape[0]
    rows = sum(piece.shape[0] for piece in partners[0])
    skip = start // STEP
    count = len(partners)
    total_shape = jax.ShapeDtypeStruct((LAGS * cols, count * cols), jnp.float32)
    total_spec = pl.BlockSpec(total_shape.shape, lambda s, on: (0, 0))
    in_specs = [
        pl.BlockSpec((cols, STEP), lambda s, on: (0, s * on[0] + skip)),
        pl.BlockSpec((cols, STEP), lambda s, on: (0, s * on[0] + skip)),
        pl.BlockSpec((LAGS, STEP), lambda s, on: (0, s * on[0] + skip)),
    ]
    args = [plain, swapped, coeffs]
    for pieces in partners:
        in_specs += piece_specs(pieces, True)
        args += pieces
    if acc is not None:
        in_specs.append(total_spec)
        args.append(acc)
    scratch = [pltpu.VMEM((LAGS * cols, STEP), jnp.bfloat16)]
    if kinds:
        results = count + kinds.count("both")
        out_shape = [jax.ShapeDtypeStruct((LAGS, cols, cols), jnp.bfloat16)] * results
        out_specs = [pl.BlockSpec((LAGS, cols, cols), lambda s, on: (0, 0, 0))] * results
        scratch = [pltpu.VMEM(total_shape.shape, jnp.float32)] + scratch
    else:
        out_shape, out_specs = [total_shape], [total_spec]
    return pl.pallas_call(
        functools.partial(corr_kernel, [piece_ends(pieces) for pieces in partners], acc is None, kinds or ()),
        grid_spec=pltpu.PrefetchScalarGridSpec(
            num_scalar_prefetch=1,
            grid=(rows // STEP,),
            in_specs=in_specs,
            out_specs=out_specs,
            scratch_shapes=scratch,
        ),
        out_shape=out_shape,
        compiler_params=PARAMS,
        cost_estimate=pl.CostEstimate(
            flops=2 * count * LAGS * cols * cols * rows if common else 0,
            bytes_accessed=2 * (2 + count) * rows * cols if common else 0,
            transcendentals=0,
        ),
        name=name,
    )(switch, *args)


def local(spectra, quality):
    count = lax.axis_size("chan")
    half = count // 2
    me = lax.axis_index("chan")
    freq_count, _, window_count, cols = spectra.shape
    block = spectra.reshape(-1, cols)

    first_far, second_far = [], []
    for p in range(half):
        if p in (0, half - 1):
            first_far.append((p + half, p))
        elif p % 2 == 0 and p >= half // 2:
            first_far.append((p, p + half))
        elif p in (1, 3):
            second_far.append((p, p + half))
        else:
            second_far.append((p + half, p))
    late_near = [(2, 1), (4, 3)]
    first_pairs = first_far + [(0, 1), (half - 1, half - 2)]
    second_pairs = second_far + late_near
    near_pairs = [(d + 1, d) for d in range(1, count - 1) if d not in (1, 3, half - 2, half - 1)]
    near_pairs += [(0, half - 1), (half - 1, 0)]
    first_back = [(t, s) for s, t in first_far] + [(1, 0)]
    second_back = [(t, s) for s, t in second_far]
    side_pairs = [(0, half - 1), (half - 1, count - 1)]

    def among(devices):
        return functools.reduce(jnp.logical_or, [me == d for d in devices])

    def switch(on, other=False):
        return jnp.stack([jnp.asarray(on), jnp.asarray(other)]).astype(jnp.int32)

    always = switch(True)
    second_on = switch(among([t for _, t in second_pairs]))
    side_on = switch(among([0, half - 1]), me == half - 1)

    large, small = mask(block, quality)
    first_large = lax.ppermute(large, "chan", first_pairs)
    near_small = lax.ppermute(small, "chan", near_pairs)
    near_large = lax.ppermute(large, "chan", near_pairs)
    first_small = lax.ppermute(small, "chan", first_pairs)
    coeffs = lag_rows(freq_count, window_count)
    own = turn([large, small], always, "turn_own")

    late_large, own, near_small = lax.optimization_barrier((large, own, near_small))
    second_large = lax.ppermute(late_large, "chan", second_pairs)
    first_in, near_in = [first_large, first_small], [near_large, near_small]
    near, first, first_mirror = corr(always, own, coeffs, [near_in, first_in], ["plain", "both"], "near_first")
    late_small, near = lax.optimization_barrier((small, near))
    second_small = lax.ppermute(late_small, "chan", second_pairs)
    first_returned = lax.ppermute(first_mirror, "chan", first_back)

    side_switch, near = lax.optimization_barrier((side_on, near))
    side_turned = turn(near_in, side_switch, "turn_side", common=False)
    side, = corr(side_switch, side_turned, coeffs, [first_in], ["either"], "side", common=False)
    side_returned = lax.ppermute(side, "chan", side_pairs)

    second_switch, side = lax.optimization_barrier((second_on, side))
    total, = corr(second_switch, own, coeffs, [[second_large]], None, "second_large")
    second, second_mirror = corr(
        second_switch, own, coeffs, [[second_small]], ["both"], "second_small", large.shape[0], total
    )
    second_returned = lax.ppermute(second_mirror, "chan", second_back)

    far = jnp.where(among([t for _, t in first_far]), first, second)
    far = jnp.where(among([s for s, _ in first_far]), first_returned, far)
    far = jnp.where(among([s for s, _ in second_far]), second_returned, far)
    near = jnp.where(among([t for _, t in late_near]), second, near)
    near = jnp.where(among([half - 1, count - 1]), side_returned, near)
    near = jnp.where(me == 0, first_returned, jnp.where(me == half - 2, first, near))
    return near[None], far[None]


def solution(mesh):
    return jax.shard_map(
        local,
        mesh=mesh,
        in_specs=(P(None, None, None, ("grp", "chan")), P(("grp", "chan"), None)),
        out_specs=(P(("grp", "chan"), None, None, None), P(("grp", "chan"), None, None, None)),
        check_vma=False,
    )
```

time: 86.8 us -> 104 us (1.20)
  Pallas kernels: 24.8 us -> 43.6 us
  local copies, waits for them, and re-layouts: 10 us -> 0.89 us
  starting transfers between devices: 40.5 us -> 44.1 us
  other arithmetic: 3.01 us -> 5.87 us
    pallas_call x6 -> x7, Pallas kernels: 24.8 us -> 43.6 us  [the longest x4 26.8 us: corr(): pl.pallas_call(functools.partial(corr_kernel, [piece_ends(pieces) for pie...]
    unnamed x24 -> x4, local copies, waits for them, and re-layouts: 10 us -> 0.89 us
    ppermute x1, starting transfers between devices: 14.8 us -> 17 us  [local(): first_returned = lax.ppermute(first_mirror, 'chan', first_back)]
    broadcast_in_dim x1, other arithmetic: 0.93 us -> 2.04 us  [local(): return (near[None], far[None])]
    convert_element_type x2, other arithmetic: 0.15 us -> 1.2 us  [switch(): return jnp.stack([jnp.asarray(on), jnp.asarray(other)]).astype(jnp.int32)]
    ppermute x3 -> x6, starting transfers between devices: 23.7 us -> 24.5 us  [the longest x1 17.5 us: local(): second_large = lax.ppermute(late_large, 'chan', second_pairs)]
  transfers between devices with their start and end apart: 6 -> 9, of which waited for: 1 -> 1; matrix products, arithmetic and copies ran while one was open for 2% -> 4% of each run, Pallas kernels for 28% -> 37%
where the time goes in v5:
time: 104 us; the launch traced here: 102 us
  starting transfers between devices  44.1 us (42%)
  Pallas kernels  43.6 us (42%)
  waiting for transfers between devices  7.23 us (7%)
  other arithmetic  5.87 us (6%)
    pallas_call x4, Pallas kernels, corr(): pl.pallas_call(functools.partial(corr_kernel, [piece_ends(pieces) for pie...  26.8 us
    ppermute x1, starting transfers between devices, local(): second_large = lax.ppermute(late_large, 'chan', second_pairs)  17.5 us
    ppermute x1, starting transfers between devices, local(): first_returned = lax.ppermute(first_mirror, 'chan', first_back)  17 us
    pallas_call x2, Pallas kernels, turn(): pl.pallas_call(functools.partial(turn_kernel, piece_ends(pieces)), grid_s...  10.7 us
    ppermute x1, waiting for transfers between devices, local(): second_returned = lax.ppermute(second_mirror, 'chan', second_back)  7.21 us
    pallas_call x1, Pallas kernels, mask(): pl.pallas_call(functools.partial(mask_kernel, piece_ends(shapes)), grid=(...  5.99 us
  transfers between devices with their start and end apart: 9, of which 1 were waited for; matrix products, arithmetic and copies ran while one was open for 4% of the time, Pallas kernels for 37%

profile of v5, /device:TPU:1, one launch (start us, length us, event | category | flops | bytes accessed | tf_op | source)
XLA Modules:
  0.0 102.5 jit_solution(17755054199138766637)
XLA Ops:
  0.6 6.0 %mask.1 = (bf16[5120,128]{1,0:T(8,128)(2,1)}, bf16[3072,128]{1,0:T(8,128)(2,1)}) custom-call(s32[1,4]{1,0:T(1,128)} %flags_ref.1, bf16[8192,128]{1,0:T(8,128)(2,1)} %bitcast.8), custom_call_target="tpu_custom_call" | custom-call | flops 1048576 | bytes 4194304 | tf_op jit(solution)/shard_map/mask/pallas_call | solution.py:83
  6.6 1.8 %collective-permute-start.1 = (bf16[5120,128]{1,0:T(8,128)(2,1)}, bf16[5120,128]{1,0:T(8,128)(2,1)}, u32[]{:S(2)}, u32[]{:S(2)}) collective-permute-start(bf16[5120,128]{1,0:T(8,128)(2,1)} %get-tuple-element.38.refs_0_), channel_id=1, source_target_pairs={{3,2},{5,4},{6,5},{9,8},{10,9},{11,10},{12,11},{13,12},{14,13},{15... | collective-permute-start | bytes 3932168 | tf_op jit(solution)/shard_map/ppermute | solution.py:273
  8.4 1.3 %collective-permute-start.2 = (bf16[5120,128]{1,0:T(8,128)(2,1)}, bf16[5120,128]{1,0:T(8,128)(2,1)}, u32[]{:S(2)}, u32[]{:S(2)}) collective-permute-start(bf16[5120,128]{1,0:T(8,128)(2,1)} %get-tuple-element.38.refs_0_), channel_id=1, source_target_pairs={{8,0},{4,12},{6,14},{15,7},{0,1},{7,6},{24,16},{20,28},{22,30},{31... | collective-permute-start | bytes 3932168 | tf_op jit(solution)/shard_map/ppermute | solution.py:271
  9.7 0.7 collective-permute-start
  10.4 1.3 %collective-permute-start.3 = (bf16[3072,128]{1,0:T(8,128)(2,1)}, bf16[3072,128]{1,0:T(8,128)(2,1)}, u32[]{:S(2)}, u32[]{:S(2)}) collective-permute-start(bf16[3072,128]{1,0:T(8,128)(2,1)} %get-tuple-element.37.refs_1_), channel_id=1, source_target_pairs={{8,0},{4,12},{6,14},{15,7},{0,1},{7,6},{24,16},{20,28},{22,30},{31... | collective-permute-start | bytes 2359304 | tf_op jit(solution)/shard_map/ppermute | solution.py:274
  11.8 0.9 multiply_convert_fusion
  12.7 0.9 fusion.2
  13.6 8.2 %turn_own.1 = (bf16[128,8192]{1,0:T(8,128)(2,1)}, bf16[128,8192]{1,0:T(8,128)(2,1)}) custom-call(s32[2]{0:T(128)} %constant.26.clone.1.switch_ref, bf16[5120,128]{1,0:T(8,128)(2,1)} %get-tuple-element.38.refs_0_, bf16[3072,128]{1,0:T(8,128)(2,1)} %get-tuple-element.37.refs_1_), custom_call_target="tpu_custom_call" | custom-call | bytes 6291456 | tf_op jit(solution)/shard_map/turn_own/pallas_call | solution.py:119
  21.8 17.5 %collective-permute-start.7 = (bf16[5120,128]{1,0:T(8,128)(2,1)}, bf16[5120,128]{1,0:T(8,128)(2,1)}, u32[]{:S(2)}, u32[]{:S(2)}) collective-permute-start(bf16[5120,128]{1,0:T(8,128)(2,1)} %get-tuple-element.38.refs_0_), channel_id=1, source_target_pairs={{1,9},{10,2},{3,11},{13,5},{2,1},{4,3},{17,25},{26,18},{19,27},{29... | collective-permute-start | bytes 3932168 | tf_op jit(solution)/shard_map/ppermute | solution.py:279
  39.3 0.8 pad_maximum_fusion.coeff_ref
  40.1 11.1 %near_first.1 = (bf16[9,128,128]{2,1,0:T(8,128)(2,1)}, bf16[9,128,128]{2,1,0:T(8,128)(2,1)}, bf16[9,128,128]{2,1,0:T(8,128)(2,1)}) custom-call(s32[2]{0:T(128)} %constant.26.clone.1.switch_ref, bf16[128,8192]{1,0:T(8,128)(2,1)} %get-tuple-element.26.plain_ref, bf16[128,8192]{1,0:T(8,128)(2,1)} %get-tuple-element.27.swapped_ref, ...), custom_call_target="tpu_custom_call" | custom-call | flops 4831838208 | bytes 8388608 | tf_op jit(solution)/shard_map/near_first/pallas_call | solution.py:214
  51.2 1.9 %collective-permute-start.6 = (bf16[3072,128]{1,0:T(8,128)(2,1)}, bf16[3072,128]{1,0:T(8,128)(2,1)S(1)}, u32[]{:S(2)}, u32[]{:S(2)}) collective-permute-start(bf16[3072,128]{1,0:T(8,128)(2,1)} %get-tuple-element.37.refs_1_), channel_id=1, source_target_pairs={{1,9},{10,2},{3,11},{13,5},{2,1},{4,3},{17,25},{26,18},{19,27},{29... | collective-permute-start | bytes 2359304 | tf_op jit(solution)/shard_map/ppermute | solution.py:283
  53.2 0.6 add_convert_fusion.switch_ref
  53.8 0.6 add_convert_fusion.1.switch_ref
  54.4 2.5 %turn_side.1 = (bf16[128,8192]{1,0:T(8,128)(2,1)}, bf16[128,8192]{1,0:T(8,128)(2,1)}) custom-call(s32[2]{0:T(128)} %add_convert_fusion.switch_ref, bf16[5120,128]{1,0:T(8,128)(2,1)} %collective-permute-done.1.rest_0_.refs_0_, bf16[3072,128]{1,0:T(8,128)(2,1)} %copy-done.1), custom_call_target="tpu_custom_call" | custom-call | tf_op jit(solution)/shard_map/turn_side/pallas_call | solution.py:119
  56.9 2.6 %side.1 = bf16[9,128,128]{2,1,0:T(8,128)(2,1)} custom-call(s32[2]{0:T(128)} %add_convert_fusion.switch_ref, bf16[128,8192]{1,0:T(8,128)(2,1)} %get-tuple-element.34.plain_ref, bf16[128,8192]{1,0:T(8,128)(2,1)} %get-tuple-element.35.swapped_ref, bf16[9,8192]{1,0:T(8,128)(2,1)} %pad_maximum_fusion.coeff_ref, ...), custom_call_target="tpu_custom_call" | custom-call | tf_op jit(solution)/shard_map/side/pallas_call | solution.py:214
  59.5 1.4 %collective-permute-start.5 = (bf16[9,128,128]{2,1,0:T(8,128)(2,1)}, bf16[9,128,128]{2,1,0:T(8,128)(2,1)}, u32[]{:S(2)}, u32[]{:S(2)}) collective-permute-start(bf16[9,128,128]{2,1,0:T(8,128)(2,1)} %side.1), channel_id=1, source_target_pairs={{0,7},{7,15},{16,23},{23,31}} | collective-permute-start | bytes 884744 | tf_op jit(solution)/shard_map/ppermute | solution.py:289
  60.9 17.0 %collective-permute-start.4 = (bf16[9,128,128]{2,1,0:T(8,128)(2,1)}, bf16[9,128,128]{2,1,0:T(8,128)(2,1)}, u32[]{:S(2)}, u32[]{:S(2)}) collective-permute-start(bf16[9,128,128]{2,1,0:T(8,128)(2,1)} %get-tuple-element.29), channel_id=1, source_target_pairs={{0,8},{12,4},{14,6},{7,15},{1,0},{16,24},{28,20},{30,22},{23,31},{... | collective-permute-start | bytes 884744 | tf_op jit(solution)/shard_map/ppermute | solution.py:284
  77.9 7.3 %second_large.1.rest_1_ = f32[1152,128]{1,0:T(8,128)} custom-call(s32[2]{0:T(128)} %add_convert_fusion.1.switch_ref, bf16[128,8192]{1,0:T(8,128)(2,1)} %get-tuple-element.26.plain_ref, bf16[128,8192]{1,0:T(8,128)(2,1)} %get-tuple-element.27.swapped_ref, bf16[9,8192]{1,0:T(8,128)(2,1)} %pad_maximum_fusion.coeff_ref, ...), custom_call_target="tpu_custom_call" | custom-call | flops 1509949440 | bytes 3932160 | tf_op jit(solution)/shard_map/second_large/pallas_call | solution.py:214
  85.2 0.9 copy-done
  86.1 5.8 %second_small.1 = (bf16[9,128,128]{2,1,0:T(8,128)(2,1)}, bf16[9,128,128]{2,1,0:T(8,128)(2,1)}) custom-call(s32[2]{0:T(128)} %add_convert_fusion.1.switch_ref, bf16[128,8192]{1,0:T(8,128)(2,1)} %get-tuple-element.26.plain_ref, bf16[128,8192]{1,0:T(8,128)(2,1)} %get-tuple-element.27.swapped_ref, bf16[9,8192]{1,0:T(8,128)(2,1)} %pad_maximum_fusion.coeff_ref, ...), custom_call_target="tpu_custom_call" | custom-call | flops 905969664 | bytes 2359296 | tf_op jit(solution)/shard_map/second_small/pallas_call | solution.py:214
  91.9 1.3 %collective-permute-start.8 = (bf16[9,128,128]{2,1,0:T(8,128)(2,1)}, bf16[9,128,128]{2,1,0:T(8,128)(2,1)S(1)}, u32[]{:S(2)}, u32[]{:S(2)}) collective-permute-start(bf16[9,128,128]{2,1,0:T(8,128)(2,1)} %get-tuple-element.41), channel_id=1, source_target_pairs={{9,1},{2,10},{11,3},{5,13},{25,17},{18,26},{27,19},{21,29}} | collective-permute-start | bytes 884744 | tf_op jit(solution)/shard_map/ppermute | solution.py:296
  93.2 7.2 %collective-permute-done.8 = bf16[9,128,128]{2,1,0:T(8,128)(2,1)S(1)} collective-permute-done((bf16[9,128,128]{2,1,0:T(8,128)(2,1)}, bf16[9,128,128]{2,1,0:T(8,128)(2,1)S(1)}, u32[]{:S(2)}, u32[]{:S(2)}) %collective-permute-start.8) | collective-permute-done | bytes 294944 | tf_op jit(solution)/shard_map/ppermute | solution.py:296
  100.5 2.0 %select_bitcast_fusion = (bf16[1,9,128,128]{3,2,1,0:T(8,128)(2,1)}, bf16[1,9,128,128]{3,2,1,0:T(8,128)(2,1)}) fusion(bf16[9,128,128]{2,1,0:T(8,128)(2,1)S(1)} %collective-permute-done.8, bf16[9,128,128]{2,1,0:T(8,128)(2,1)} %collective-permute-done.4, bf16[9,128,128]{2,1,0:T(8,128)(2,1)} %get-tuple-element.30, bf16[9,128,128]{2,1,0:T(8,128)(2,1)} %get-tuple-element.39, ...), kind=kLoop, calls=%fused_computation | loop fusion | flops 1032192 | bytes 2359303 | tf_op jit(solution)/shard_map/broadcast_in_dim | solution.py:304
  (14 shorter events, 0.1 us)
Async XLA Ops:
  6.6 33.5 %collective-permute-start.1 = (bf16[5120,128]{1,0:T(8,128)(2,1)}, bf16[5120,128]{1,0:T(8,128)(2,1)}, u32[]{:S(2)}, u32[]{:S(2)}) collective-permute-start(bf16[5120,128]{1,0:T(8,128)(2,1)} %get-tuple-element.38.refs_0_), channel_id=1, source_target_pairs={{3,2},{5,4},{6,5},{9,8},{10,9},{11,10},{12,11},{13,12},{14,13},{15... | collective-permute-start | bytes 3932168 | tf_op jit(solution)/shard_map/ppermute | solution.py:273
  8.4 31.7 %collective-permute-start.2 = (bf16[5120,128]{1,0:T(8,128)(2,1)}, bf16[5120,128]{1,0:T(8,128)(2,1)}, u32[]{:S(2)}, u32[]{:S(2)}) collective-permute-start(bf16[5120,128]{1,0:T(8,128)(2,1)} %get-tuple-element.38.refs_0_), channel_id=1, source_target_pairs={{8,0},{4,12},{6,14},{15,7},{0,1},{7,6},{24,16},{20,28},{22,30},{31... | collective-permute-start | bytes 3932168 | tf_op jit(solution)/shard_map/ppermute | solution.py:271
  9.7 12.1 %collective-permute-start = (bf16[3072,128]{1,0:T(8,128)(2,1)}, bf16[3072,128]{1,0:T(8,128)(2,1)S(1)}, u32[]{:S(2)}, u32[]{:S(2)}) collective-permute-start(bf16[3072,128]{1,0:T(8,128)(2,1)} %get-tuple-element.37.refs_1_), channel_id=1, source_target_pairs={{3,2},{5,4},{6,5},{9,8},{10,9},{11,10},{12,11},{13,12},{14,13},{15... | collective-permute-start | bytes 2359304 | tf_op jit(solution)/shard_map/ppermute | solution.py:272
  10.4 29.7 %collective-permute-start.3 = (bf16[3072,128]{1,0:T(8,128)(2,1)}, bf16[3072,128]{1,0:T(8,128)(2,1)}, u32[]{:S(2)}, u32[]{:S(2)}) collective-permute-start(bf16[3072,128]{1,0:T(8,128)(2,1)} %get-tuple-element.37.refs_1_), channel_id=1, source_target_pairs={{8,0},{4,12},{6,14},{15,7},{0,1},{7,6},{24,16},{20,28},{22,30},{31... | collective-permute-start | bytes 2359304 | tf_op jit(solution)/shard_map/ppermute | solution.py:274
  21.8 18.3 %copy-start.1 = (bf16[3072,128]{1,0:T(8,128)(2,1)}, bf16[3072,128]{1,0:T(8,128)(2,1)S(1)}, u32[]{:S(2)}) copy-start(bf16[3072,128]{1,0:T(8,128)(2,1)S(1)} %collective-permute-done.rest_1_.refs_1_) | copy-start | bytes 2359300
  21.8 56.1 %collective-permute-start.7 = (bf16[5120,128]{1,0:T(8,128)(2,1)}, bf16[5120,128]{1,0:T(8,128)(2,1)}, u32[]{:S(2)}, u32[]{:S(2)}) collective-permute-start(bf16[5120,128]{1,0:T(8,128)(2,1)} %get-tuple-element.38.refs_0_), channel_id=1, source_target_pairs={{1,9},{10,2},{3,11},{13,5},{2,1},{4,3},{17,25},{26,18},{19,27},{29... | collective-permute-start | bytes 3932168 | tf_op jit(solution)/shard_map/ppermute | solution.py:279
  51.2 34.0 %collective-permute-start.6 = (bf16[3072,128]{1,0:T(8,128)(2,1)}, bf16[3072,128]{1,0:T(8,128)(2,1)S(1)}, u32[]{:S(2)}, u32[]{:S(2)}) collective-permute-start(bf16[3072,128]{1,0:T(8,128)(2,1)} %get-tuple-element.37.refs_1_), channel_id=1, source_target_pairs={{1,9},{10,2},{3,11},{13,5},{2,1},{4,3},{17,25},{26,18},{19,27},{29... | collective-permute-start | bytes 2359304 | tf_op jit(solution)/shard_map/ppermute | solution.py:283
  59.5 33.7 %collective-permute-start.5 = (bf16[9,128,128]{2,1,0:T(8,128)(2,1)}, bf16[9,128,128]{2,1,0:T(8,128)(2,1)}, u32[]{:S(2)}, u32[]{:S(2)}) collective-permute-start(bf16[9,128,128]{2,1,0:T(8,128)(2,1)} %side.1), channel_id=1, source_target_pairs={{0,7},{7,15},{16,23},{23,31}} | collective-permute-start | bytes 884744 | tf_op jit(solution)/shard_map/ppermute | solution.py:289
  60.9 32.3 %collective-permute-start.4 = (bf16[9,128,128]{2,1,0:T(8,128)(2,1)}, bf16[9,128,128]{2,1,0:T(8,128)(2,1)}, u32[]{:S(2)}, u32[]{:S(2)}) collective-permute-start(bf16[9,128,128]{2,1,0:T(8,128)(2,1)} %get-tuple-element.29), channel_id=1, source_target_pairs={{0,8},{12,4},{14,6},{7,15},{1,0},{16,24},{28,20},{30,22},{23,31},{... | collective-permute-start | bytes 884744 | tf_op jit(solution)/shard_map/ppermute | solution.py:284
  85.2 0.9 copy-start
  91.9 8.6 %collective-permute-start.8 = (bf16[9,128,128]{2,1,0:T(8,128)(2,1)}, bf16[9,128,128]{2,1,0:T(8,128)(2,1)S(1)}, u32[]{:S(2)}, u32[]{:S(2)}) collective-permute-start(bf16[9,128,128]{2,1,0:T(8,128)(2,1)} %get-tuple-element.41), channel_id=1, source_target_pairs={{9,1},{2,10},{11,3},{5,13},{25,17},{18,26},{27,19},{21,29}} | collective-permute-start | bytes 884744 | tf_op jit(solution)/shard_map/ppermute | solution.py:296

commit v6 on v5

--- a/solution.py
+++ b/solution.py
@@ -11,8 +11,8 @@
 HL = 4
 LAGS = 2 * HL + 1
 STEP = 1024
-ENDS = (5, 8)
-PARAMS = pltpu.CompilerParams(vmem_limit_bytes=63 * 1024 * 1024)
+ENDS = (6, 8)
+PARAMS = pltpu.CompilerParams(vmem_limit_bytes=16 * 1024 * 1024)
 
 
 def lag_rows(freq_count, window_count):
@@ -58,7 +58,7 @@
     return ends
 
 
-def mask_kernel(ends, flags_ref, x_ref, *piece_refs):
+def mask_kernel(ends, flags_ref, x_ref, whole_ref, *piece_refs):
     rows, cols = x_ref.shape
     windows = flags_ref.shape[1]
     step = pl.program_id(0)
@@ -68,6 +68,7 @@
         weights = jnp.where(window == w, flags_ref[0, w].astype(jnp.float32), weights)
     weights = jnp.broadcast_to(weights.astype(jnp.bfloat16)[None], (rows // 16, 16, cols))
     masked = x_ref[...] * weights.reshape(rows, cols)
+    whole_ref[...] = masked
     begin = 0
     for end, piece_ref in zip(ends, piece_refs):
         @pl.when((step >= begin) & (step < end))
@@ -78,14 +79,15 @@
 
 def mask(x, flags):
     rows, cols = x.shape
+    block_spec = pl.BlockSpec((STEP, cols), lambda s: (s, 0))
     ends = [rows * e // 8 for e in ENDS]
     shapes = [jax.ShapeDtypeStruct((e - b, cols), jnp.bfloat16) for b, e in zip([0] + ends, ends)]
     return pl.pallas_call(
         functools.partial(mask_kernel, piece_ends(shapes)),
         grid=(rows // STEP,),
-        in_specs=[pl.BlockSpec(memory_space=pltpu.SMEM), pl.BlockSpec((STEP, cols), lambda s: (s, 0))],
-        out_specs=piece_specs(shapes, False),
-        out_shape=shapes,
+        in_specs=[pl.BlockSpec(memory_space=pltpu.SMEM), block_spec],
+        out_specs=[block_spec] + piece_specs(shapes, False),
+        out_shape=[jax.ShapeDtypeStruct((rows, cols), jnp.bfloat16)] + shapes,
         compiler_params=PARAMS,
         cost_estimate=pl.CostEstimate(flops=rows * cols, bytes_accessed=4 * rows * cols, transcendentals=0),
         name="mask",
@@ -267,28 +269,27 @@
     second_on = switch(among([t for _, t in second_pairs]))
     side_on = switch(among([0, half - 1]), me == half - 1)
 
-    large, small = mask(block, quality)
-    first_large = lax.ppermute(large, "chan", first_pairs)
+    whole, large, small = mask(block, quality)
+    first_in = lax.ppermute(whole, "chan", first_pairs)
+    near_large = lax.ppermute(large, "chan", near_pairs)
     near_small = lax.ppermute(small, "chan", near_pairs)
-    near_large = lax.ppermute(large, "chan", near_pairs)
-    first_small = lax.ppermute(small, "chan", first_pairs)
     coeffs = lag_rows(freq_count, window_count)
-    own = turn([large, small], always, "turn_own")
+    own = turn([whole], always, "turn_own")
 
     late_large, own, near_small = lax.optimization_barrier((large, own, near_small))
     second_large = lax.ppermute(late_large, "chan", second_pairs)
-    first_in, near_in = [first_large, first_small], [near_large, near_small]
-    near, first, first_mirror = corr(always, own, coeffs, [near_in, first_in], ["plain", "both"], "near_first")
+    near_in = [near_large, near_small]
+    near, first, first_mirror = corr(always, own, coeffs, [near_in, [first_in]], ["plain", "both"], "near_first")
     late_small, near = lax.optimization_barrier((small, near))
     second_small = lax.ppermute(late_small, "chan", second_pairs)
     first_returned = lax.ppermute(first_mirror, "chan", first_back)
 
     side_switch, near = lax.optimization_barrier((side_on, near))
     side_turned = turn(near_in, side_switch, "turn_side", common=False)
-    side, = corr(side_switch, side_turned, coeffs, [first_in], ["either"], "side", common=False)
+    side, = corr(side_switch, side_turned, coeffs, [[first_in]], ["either"], "side", common=False)
     side_returned = lax.ppermute(side, "chan", side_pairs)
 
-    second_switch, side = lax.optimization_barrier((second_on, side))
+    second_switch, side, first_returned = lax.optimization_barrier((second_on, side, first_returned))
     total, = corr(second_switch, own, coeffs, [[second_large]], None, "second_large")
     second, second_mirror = corr(
         second_switch, own, coeffs, [[second_small]], ["both"], "second_small", large.shape[0], total

time: 104 us -> 103 us (level); the launches traced: 102 us -> 103 us
  Pallas kernels: 43.6 us -> 28.2 us
  starting transfers between devices: 44.1 us -> 56.7 us
  local copies, waits for them, and re-layouts: 0.89 us -> 5.96 us
  other arithmetic: 5.87 us -> 4.12 us
    ppermute x1, starting transfers between devices: 1.91 us -> 12.8 us  [local(): second_small = lax.ppermute(late_small, 'chan', second_pairs)]
    ppermute x1, starting transfers between devices: 17 us -> 27.4 us  [local(): first_returned = lax.ppermute(first_mirror, 'chan', first_back)]
    pallas_call x4, Pallas kernels: 26.8 us -> 19.5 us  [corr(): pl.pallas_call(functools.partial(corr_kernel, [piece_ends(pieces) for pie...]
    ppermute x1, starting transfers between devices: 17.5 us -> 11.1 us  [local(): second_large = lax.ppermute(late_large, 'chan', second_pairs)]
    pallas_call x2, Pallas kernels: 10.7 us -> 4.79 us  [turn(): pl.pallas_call(functools.partial(turn_kernel, piece_ends(pieces)), grid_s...]
    unnamed x4 -> x24, local copies, waits for them, and re-layouts: 0.89 us -> 5.96 us
    pallas_call x1, Pallas kernels: 5.99 us -> 3.84 us  [mask(): pl.pallas_call(functools.partial(mask_kernel, piece_ends(shapes)), grid=(...]
    ppermute x2 -> x1, starting transfers between devices: 2.57 us -> 1.29 us  [local(): first_in = lax.ppermute(whole, 'chan', first_pairs)]
  transfers between devices with their start and end apart: 9 -> 8, of which waited for: 1 -> 1; matrix products, arithmetic and copies ran while one was open for 4% -> 2% of each run, Pallas kernels for 37% -> 24%
where the time goes in v6:
time: 103 us
  starting transfers between devices  56.7 us (55%)
  Pallas kernels  28.2 us (27%)
  waiting for transfers between devices  7.24 us (7%)
  local copies, waits for them, and re-layouts  5.96 us (6%)
  other arithmetic  4.12 us (4%)
    ppermute x1, starting transfers between devices, local(): first_returned = lax.ppermute(first_mirror, 'chan', first_back)  27.4 us
    pallas_call x4, Pallas kernels, corr(): pl.pallas_call(functools.partial(corr_kernel, [piece_ends(pieces) for pie...  19.5 us
    ppermute x1, starting transfers between devices, local(): second_small = lax.ppermute(late_small, 'chan', second_pairs)  12.8 us
    ppermute x1, starting transfers between devices, local(): second_large = lax.ppermute(late_large, 'chan', second_pairs)  11.1 us
    ppermute x1, waiting for transfers between devices, local(): second_returned = lax.ppermute(second_mirror, 'chan', second_back)  7.22 us
    unnamed x24, local copies, waits for them, and re-layouts  5.96 us
    pallas_call x2, Pallas kernels, turn(): pl.pallas_call(functools.partial(turn_kernel, piece_ends(pieces)), grid_s...  4.79 us
    pallas_call x1, Pallas kernels, mask(): pl.pallas_call(functools.partial(mask_kernel, piece_ends(shapes)), grid=(...  3.84 us
  transfers between devices with their start and end apart: 8, of which 1 were waited for; matrix products, arithmetic and copies ran while one was open for 2% of the time, Pallas kernels for 24%

profile of v6, /device:TPU:1, one launch (start us, length us, event | category | flops | bytes accessed | tf_op | source)
XLA Modules:
  0.0 103.1 jit_solution(7524106150743927452)
XLA Ops:
  0.7 1.6 %copy-done = bf16[1024,2,4,128]{3,2,1,0:T(4,128)(2,1)S(1)} copy-done((bf16[1024,2,4,128]{3,2,1,0:T(4,128)(2,1)S(1)}, bf16[1024,2,4,128]{3,2,1,0:T(4,128)(2,1)}, u32[]{:S(2)}) %copy-start) | copy-done | bytes 2097176
  2.9 3.8 %mask.1 = (bf16[8192,128]{1,0:T(8,128)(2,1)S(1)}, bf16[6144,128]{1,0:T(8,128)(2,1)}, bf16[2048,128]{1,0:T(8,128)(2,1)}) custom-call(s32[1,4]{1,0:T(1,128)S(1)} %copy-done.10, bf16[8192,128]{1,0:T(8,128)(2,1)S(1)} %bitcast.8), custom_call_target="tpu_custom_call" | custom-call | flops 1048576 | bytes 4194304 | tf_op jit(solution)/shard_map/mask/pallas_call | solution.py:85
  6.7 0.7 collective-permute-start
  7.4 1.3 %collective-permute-start.2 = (bf16[8192,128]{1,0:T(8,128)(2,1)S(1)}, bf16[8192,128]{1,0:T(8,128)(2,1)S(1)}, u32[]{:S(2)}, u32[]{:S(2)}) collective-permute-start(bf16[8192,128]{1,0:T(8,128)(2,1)S(1)} %get-tuple-element.26.refs_0_), channel_id=1, source_target_pairs={{8,0},{4,12},{6,14},{15,7},{0,1},{7,6},{24,16},{20,28},{22,30},{31... | collective-permute-start | bytes 6291464 | tf_op jit(solution)/shard_map/ppermute | solution.py:273
  8.7 0.8 collective-permute-start.1
  9.5 0.9 multiply_convert_fusion
  10.5 0.9 fusion.2
  11.4 4.0 %turn_own.1 = (bf16[128,8192]{1,0:T(8,128)(2,1)S(1)}, bf16[128,8192]{1,0:T(8,128)(2,1)S(1)}) custom-call(s32[2]{0:T(128)S(1)} %copy-done.11, bf16[8192,128]{1,0:T(8,128)(2,1)S(1)} %get-tuple-element.26.refs_0_), custom_call_target="tpu_custom_call" | custom-call | bytes 6291456 | tf_op jit(solution)/shard_map/turn_own/pallas_call | solution.py:121
  15.3 11.1 %collective-permute-start.6 = (bf16[6144,128]{1,0:T(8,128)(2,1)}, bf16[6144,128]{1,0:T(8,128)(2,1)}, u32[]{:S(2)}, u32[]{:S(2)}) collective-permute-start(bf16[6144,128]{1,0:T(8,128)(2,1)} %get-tuple-element.42), channel_id=1, source_target_pairs={{1,9},{10,2},{3,11},{13,5},{2,1},{4,3},{17,25},{26,18},{19,27},{29... | collective-permute-start | bytes 4718600 | tf_op jit(solution)/shard_map/ppermute | solution.py:280
  26.6 8.5 %near_first.1 = (bf16[9,128,128]{2,1,0:T(8,128)(2,1)S(1)}, bf16[9,128,128]{2,1,0:T(8,128)(2,1)S(1)}, bf16[9,128,128]{2,1,0:T(8,128)(2,1)}) custom-call(s32[2]{0:T(128)S(1)} %copy-done.11, bf16[128,8192]{1,0:T(8,128)(2,1)S(1)} %get-tuple-element.29.plain_ref, bf16[128,8192]{1,0:T(8,128)(2,1)S(1)} %get-tuple-element.30.swapped_ref, ...), custom_call_target="tpu_custom_call" | custom-call | flops 4831838208 | bytes 8388608 | tf_op jit(solution)/shard_map/near_first/pallas_call | solution.py:216
  35.1 0.7 copy-done.7
  35.9 0.7 copy-done.8
  36.6 12.8 %collective-permute-start.5 = (bf16[2048,128]{1,0:T(8,128)(2,1)}, bf16[2048,128]{1,0:T(8,128)(2,1)S(1)}, u32[]{:S(2)}, u32[]{:S(2)}) collective-permute-start(bf16[2048,128]{1,0:T(8,128)(2,1)} %get-tuple-element.41), channel_id=1, source_target_pairs={{1,9},{10,2},{3,11},{13,5},{2,1},{4,3},{17,25},{26,18},{19,27},{29... | collective-permute-start | bytes 1572872 | tf_op jit(solution)/shard_map/ppermute | solution.py:284
  49.4 27.4 %collective-permute-start.3 = (bf16[9,128,128]{2,1,0:T(8,128)(2,1)}, bf16[9,128,128]{2,1,0:T(8,128)(2,1)}, u32[]{:S(2)}, u32[]{:S(2)}) collective-permute-start(bf16[9,128,128]{2,1,0:T(8,128)(2,1)} %get-tuple-element.37), channel_id=1, source_target_pairs={{0,8},{12,4},{14,6},{7,15},{1,0},{16,24},{28,20},{30,22},{23,31},{... | collective-permute-start | bytes 884744 | tf_op jit(solution)/shard_map/ppermute | solution.py:285
  76.9 1.5 %copy-done.6 = bf16[6144,128]{1,0:T(8,128)(2,1)S(1)} copy-done((bf16[6144,128]{1,0:T(8,128)(2,1)S(1)}, bf16[6144,128]{1,0:T(8,128)(2,1)}, u32[]{:S(2)}) %copy-start.6) | copy-done | bytes 1572888
  78.4 0.8 turn_side.1
  79.3 0.9 side.1
  80.2 1.4 %collective-permute-start.4 = (bf16[9,128,128]{2,1,0:T(8,128)(2,1)S(1)}, bf16[9,128,128]{2,1,0:T(8,128)(2,1)}, u32[]{:S(2)}, u32[]{:S(2)}) collective-permute-start(bf16[9,128,128]{2,1,0:T(8,128)(2,1)S(1)} %side.1), channel_id=1, source_target_pairs={{0,7},{7,15},{16,23},{23,31}} | collective-permute-start | bytes 884744 | tf_op jit(solution)/shard_map/ppermute | solution.py:290
  81.6 6.9 %second_large.1.rest_1_ = f32[1152,128]{1,0:T(8,128)S(1)} custom-call(s32[2]{0:T(128)S(1)} %add_convert_fusion.switch_ref, bf16[128,8192]{1,0:T(8,128)(2,1)S(1)} %get-tuple-element.29.plain_ref, bf16[128,8192]{1,0:T(8,128)(2,1)S(1)} %copy-done.2, bf16[9,8192]{1,0:T(8,128)(2,1)S(1)} %pad_maximum_fusion.coeff_ref, bf16[6144,128]{1,0:T(8,128)(2,1)} %collective-permute-done.6.rest_0_), custom_call_target="tpu_custom_call" | custom-call | flops 1811939328 | bytes 4718592 | tf_op jit(solution)/shard_map/second_large/pallas_call | solution.py:216
  88.5 3.2 %second_small.1 = (bf16[9,128,128]{2,1,0:T(8,128)(2,1)S(1)}, bf16[9,128,128]{2,1,0:T(8,128)(2,1)}) custom-call(s32[2]{0:T(128)S(1)} %add_convert_fusion.switch_ref, bf16[128,8192]{1,0:T(8,128)(2,1)S(1)} %get-tuple-element.29.plain_ref, bf16[128,8192]{1,0:T(8,128)(2,1)S(1)} %copy-done.2, bf16[9,8192]{1,0:T(8,128)(2,1)S(1)} %pad_maximum_fusion.coeff_ref, ...), custom_call_target="tpu_custom_call" | custom-call | flops 603979776 | bytes 1572864 | tf_op jit(solution)/shard_map/second_small/pallas_call | solution.py:216
  91.7 0.7 copy-done.9
  92.5 1.3 %collective-permute-start.7 = (bf16[9,128,128]{2,1,0:T(8,128)(2,1)}, bf16[9,128,128]{2,1,0:T(8,128)(2,1)S(1)}, u32[]{:S(2)}, u32[]{:S(2)}) collective-permute-start(bf16[9,128,128]{2,1,0:T(8,128)(2,1)} %get-tuple-element.45), channel_id=1, source_target_pairs={{9,1},{2,10},{11,3},{5,13},{25,17},{18,26},{27,19},{21,29}} | collective-permute-start | bytes 884744 | tf_op jit(solution)/shard_map/ppermute | solution.py:297
  93.8 7.2 %collective-permute-done.7 = bf16[9,128,128]{2,1,0:T(8,128)(2,1)S(1)} collective-permute-done((bf16[9,128,128]{2,1,0:T(8,128)(2,1)}, bf16[9,128,128]{2,1,0:T(8,128)(2,1)S(1)}, u32[]{:S(2)}, u32[]{:S(2)}) %collective-permute-start.7) | collective-permute-done | bytes 294944 | tf_op jit(solution)/shard_map/ppermute | solution.py:297
  101.0 2.0 %select_bitcast_fusion = (bf16[1,9,128,128]{3,2,1,0:T(8,128)(2,1)}, bf16[1,9,128,128]{3,2,1,0:T(8,128)(2,1)}) fusion(bf16[9,128,128]{2,1,0:T(8,128)(2,1)S(1)} %collective-permute-done.7, bf16[9,128,128]{2,1,0:T(8,128)(2,1)} %collective-permute-done.3, bf16[9,128,128]{2,1,0:T(8,128)(2,1)} %copy-done.8, bf16[9,128,128]{2,1,0:T(8,128)(2,1)} %copy-done.9, ...), kind=kLoop, calls=%fused_computation | loop fusion | flops 1032192 | bytes 2359303 | tf_op jit(solution)/shard_map/broadcast_in_dim | solution.py:305
  (32 shorter events, 1.0 us)
Async XLA Ops:
  0.6 10.7 %copy-start.11 = (s32[2]{0:T(128)S(1)}, s32[2]{0:T(128)}, u32[]{:S(2)}) copy-start(s32[2]{0:T(128)} %constant.23.clone.1.switch_ref) | copy-start | bytes 28
  0.6 1.6 %copy-start = (bf16[1024,2,4,128]{3,2,1,0:T(4,128)(2,1)S(1)}, bf16[1024,2,4,128]{3,2,1,0:T(4,128)(2,1)}, u32[]{:S(2)}) copy-start(bf16[1024,2,4,128]{3,2,1,0:T(4,128)(2,1)} %param.2) | copy-start | bytes 6291460
  2.2 0.7 copy-start.10
  6.7 8.6 %collective-permute-start = (bf16[2048,128]{1,0:T(8,128)(2,1)}, bf16[2048,128]{1,0:T(8,128)(2,1)S(1)}, u32[]{:S(2)}, u32[]{:S(2)}) collective-permute-start(bf16[2048,128]{1,0:T(8,128)(2,1)} %get-tuple-element.41), channel_id=1, source_target_pairs={{3,2},{5,4},{6,5},{9,8},{10,9},{11,10},{12,11},{13,12},{14,13},{15... | collective-permute-start | bytes 1572872 | tf_op jit(solution)/shard_map/ppermute | solution.py:275
  7.4 19.2 %collective-permute-start.2 = (bf16[8192,128]{1,0:T(8,128)(2,1)S(1)}, bf16[8192,128]{1,0:T(8,128)(2,1)S(1)}, u32[]{:S(2)}, u32[]{:S(2)}) collective-permute-start(bf16[8192,128]{1,0:T(8,128)(2,1)S(1)} %get-tuple-element.26.refs_0_), channel_id=1, source_target_pairs={{8,0},{4,12},{6,14},{15,7},{0,1},{7,6},{24,16},{20,28},{22,30},{31... | collective-permute-start | bytes 6291464 | tf_op jit(solution)/shard_map/ppermute | solution.py:273
  8.7 17.9 %collective-permute-start.1 = (bf16[6144,128]{1,0:T(8,128)(2,1)}, bf16[6144,128]{1,0:T(8,128)(2,1)S(1)}, u32[]{:S(2)}, u32[]{:S(2)}) collective-permute-start(bf16[6144,128]{1,0:T(8,128)(2,1)} %get-tuple-element.42), channel_id=1, source_target_pairs={{3,2},{5,4},{6,5},{9,8},{10,9},{11,10},{12,11},{13,12},{14,13},{15... | collective-permute-start | bytes 4718600 | tf_op jit(solution)/shard_map/ppermute | solution.py:274
  15.3 19.8 %copy-start.1 = (bf16[128,8192]{1,0:T(8,128)(2,1)}, bf16[128,8192]{1,0:T(8,128)(2,1)S(1)}, u32[]{:S(2)}) copy-start(bf16[128,8192]{1,0:T(8,128)(2,1)S(1)} %get-tuple-element.30.swapped_ref) | copy-start | bytes 6291460
  15.3 66.2 %collective-permute-start.6 = (bf16[6144,128]{1,0:T(8,128)(2,1)}, bf16[6144,128]{1,0:T(8,128)(2,1)}, u32[]{:S(2)}, u32[]{:S(2)}) collective-permute-start(bf16[6144,128]{1,0:T(8,128)(2,1)} %get-tuple-element.42), channel_id=1, source_target_pairs={{1,9},{10,2},{3,11},{13,5},{2,1},{4,3},{17,25},{26,18},{19,27},{29... | collective-permute-start | bytes 4718600 | tf_op jit(solution)/shard_map/ppermute | solution.py:280
  26.6 8.5 %copy-start.5 = (bf16[6144,128]{1,0:T(8,128)(2,1)}, bf16[6144,128]{1,0:T(8,128)(2,1)S(1)}, u32[]{:S(2)}) copy-start(bf16[6144,128]{1,0:T(8,128)(2,1)S(1)} %collective-permute-done.1.rest_0_.refs_0_) | copy-start | bytes 4718596
  26.6 8.5 %copy-start.3 = (bf16[8192,128]{1,0:T(8,128)(2,1)}, bf16[8192,128]{1,0:T(8,128)(2,1)S(1)}, u32[]{:S(2)}) copy-start(bf16[8192,128]{1,0:T(8,128)(2,1)S(1)} %collective-permute-done.2.rest_2_.rest_0_) | copy-start | bytes 6291460
  35.1 0.7 copy-start.7
  35.9 0.7 copy-start.8
  36.6 52.0 %collective-permute-start.5 = (bf16[2048,128]{1,0:T(8,128)(2,1)}, bf16[2048,128]{1,0:T(8,128)(2,1)S(1)}, u32[]{:S(2)}, u32[]{:S(2)}) collective-permute-start(bf16[2048,128]{1,0:T(8,128)(2,1)} %get-tuple-element.41), channel_id=1, source_target_pairs={{1,9},{10,2},{3,11},{13,5},{2,1},{4,3},{17,25},{26,18},{19,27},{29... | collective-permute-start | bytes 1572872 | tf_op jit(solution)/shard_map/ppermute | solution.py:284
  49.4 32.2 %collective-permute-start.3 = (bf16[9,128,128]{2,1,0:T(8,128)(2,1)}, bf16[9,128,128]{2,1,0:T(8,128)(2,1)}, u32[]{:S(2)}, u32[]{:S(2)}) collective-permute-start(bf16[9,128,128]{2,1,0:T(8,128)(2,1)} %get-tuple-element.37), channel_id=1, source_target_pairs={{0,8},{12,4},{14,6},{7,15},{1,0},{16,24},{28,20},{30,22},{23,31},{... | collective-permute-start | bytes 884744 | tf_op jit(solution)/shard_map/ppermute | solution.py:285
  76.7 2.5 %copy-start.4 = (bf16[8192,128]{1,0:T(8,128)(2,1)S(1)}, bf16[8192,128]{1,0:T(8,128)(2,1)}, u32[]{:S(2)}) copy-start(bf16[8192,128]{1,0:T(8,128)(2,1)} %copy-done.3) | copy-start | bytes 6291460
  76.9 1.5 %copy-start.6 = (bf16[6144,128]{1,0:T(8,128)(2,1)S(1)}, bf16[6144,128]{1,0:T(8,128)(2,1)}, u32[]{:S(2)}) copy-start(bf16[6144,128]{1,0:T(8,128)(2,1)} %copy-done.5) | copy-start | bytes 4718596
  79.3 2.3 %copy-start.2 = (bf16[128,8192]{1,0:T(8,128)(2,1)S(1)}, bf16[128,8192]{1,0:T(8,128)(2,1)}, u32[]{:S(2)}) copy-start(bf16[128,8192]{1,0:T(8,128)(2,1)} %copy-done.1) | copy-start | bytes 6291460
  80.2 13.6 %collective-permute-start.4 = (bf16[9,128,128]{2,1,0:T(8,128)(2,1)S(1)}, bf16[9,128,128]{2,1,0:T(8,128)(2,1)}, u32[]{:S(2)}, u32[]{:S(2)}) collective-permute-start(bf16[9,128,128]{2,1,0:T(8,128)(2,1)S(1)} %side.1), channel_id=1, source_target_pairs={{0,7},{7,15},{16,23},{23,31}} | collective-permute-start | bytes 884744 | tf_op jit(solution)/shard_map/ppermute | solution.py:290
  91.7 0.7 copy-start.9
  92.5 8.6 %collective-permute-start.7 = (bf16[9,128,128]{2,1,0:T(8,128)(2,1)}, bf16[9,128,128]{2,1,0:T(8,128)(2,1)S(1)}, u32[]{:S(2)}, u32[]{:S(2)}) collective-permute-start(bf16[9,128,128]{2,1,0:T(8,128)(2,1)} %get-tuple-element.45), channel_id=1, source_target_pairs={{9,1},{2,10},{11,3},{5,13},{25,17},{18,26},{27,19},{21,29}} | collective-permute-start | bytes 884744 | tf_op jit(solution)/shard_map/ppermute | solution.py:297

commit v7 on v5

v7 whole, which is shorter than its diff:
```python
import functools
import math

import jax
import jax.numpy as jnp
from jax import lax
from jax.experimental import pallas as pl
from jax.experimental.pallas import tpu as pltpu
from jax.sharding import PartitionSpec as P

HL = 4
LAGS = 2 * HL + 1
STEP = 1024
PARAMS = pltpu.CompilerParams(vmem_limit_bytes=16 * 1024 * 1024)


def lag_rows(freq_count, window_count):
    per_bin = 2 * window_count
    row = jnp.arange(freq_count * per_bin, dtype=jnp.int32)
    freq_values = (row // per_bin).astype(jnp.float32)
    sign = jnp.where(row % per_bin < window_count, 1.0, -1.0)
    lag_values = jnp.arange(HL + 1, dtype=jnp.float32)
    phases = jnp.pi / freq_count * lag_values[:, None] * freq_values[None, :]
    factor = 1.0 / math.sqrt(window_count * freq_count)
    cos_part = jnp.cos(phases) * factor
    sin_part = -jnp.sin(phases[1:]) * factor * sign[None, :]
    return jnp.concatenate([cos_part, sin_part], axis=0).astype(jnp.bfloat16)


def split_kernel(x_ref, *half_refs):
    middle = pl.num_programs(0) // 2
    step = pl.program_id(0)

    @pl.when(step < middle)
    def _():
        half_refs[0][...] = x_ref[...]

    @pl.when(step >= middle)
    def _():
        half_refs[1][...] = x_ref[...]


def split(x):
    rows, cols = x.shape
    steps = rows // STEP
    half = jax.ShapeDtypeStruct((rows // 2, cols), x.dtype)
    return pl.pallas_call(
        split_kernel,
        grid=(steps,),
        in_specs=[pl.BlockSpec((STEP, cols), lambda s: (s, 0))],
        out_specs=[
            pl.BlockSpec((STEP, cols), lambda s: (jnp.minimum(s, steps // 2 - 1), 0)),
            pl.BlockSpec((STEP, cols), lambda s: (jnp.maximum(s - steps // 2, 0), 0)),
        ],
        out_shape=[half, half],
        compiler_params=PARAMS,
        cost_estimate=pl.CostEstimate(flops=0, bytes_accessed=4 * rows * cols, transcendentals=0),
        name="split",
    )(x)


def turn_kernel(active_ref, x_ref, plain_ref, swapped_ref):
    @pl.when(active_ref[0] != 0)
    def _():
        rows, cols = x_ref.shape
        same = lax.broadcasted_iota(jnp.int32, (cols, cols), 0) == lax.broadcasted_iota(jnp.int32, (cols, cols), 1)
        eye = jnp.where(same, 1.0, 0.0).astype(jnp.bfloat16)
        source = lax.broadcasted_iota(jnp.int32, (2 * cols, 2 * cols), 0)
        target = lax.broadcasted_iota(jnp.int32, (2 * cols, 2 * cols), 1)
        exchange = jnp.where((source ^ 4) == target, 1.0, 0.0).astype(jnp.bfloat16)
        plain = lax.dot_general(eye, x_ref[...], (((1,), (1,)), ((), ())), preferred_element_type=jnp.float32)
        plain = plain.astype(jnp.bfloat16)
        plain_ref[...] = plain
        for t in range(0, rows, 2 * cols):
            swapped = jnp.dot(plain[:, t:t + 2 * cols], exchange, preferred_element_type=jnp.float32)
            swapped_ref[:, t:t + 2 * cols] = swapped.astype(jnp.bfloat16)


def turn(x, switch, name, common=True):
    rows, cols = x.shape
    out = jax.ShapeDtypeStruct((cols, rows), jnp.bfloat16)
    return pl.pallas_call(
        turn_kernel,
        grid_spec=pltpu.PrefetchScalarGridSpec(
            num_scalar_prefetch=1,
            grid=(rows // STEP,),
            in_specs=[pl.BlockSpec((STEP, cols), lambda s, on: (s * on[0], 0))],
            out_specs=[pl.BlockSpec((cols, STEP), lambda s, on: (0, s * on[0]))] * 2,
        ),
        out_shape=[out, out],
        compiler_params=PARAMS,
        cost_estimate=pl.CostEstimate(flops=0, bytes_accessed=6 * rows * cols if common else 0, transcendentals=0),
        name=name,
    )(switch, x)


def lag_result(acc, at, cols, lag):
    k = abs(lag - HL)
    even = acc[k * cols:(k + 1) * cols, at]
    if k == 0:
        return even.astype(jnp.bfloat16)
    odd = acc[(HL + k) * cols:(HL + k + 1) * cols, at]
    return (even + odd if lag > HL else even - odd).astype(jnp.bfloat16)


def corr_kernel(windows, count, first, kinds, switch_ref, plain_ref, swapped_ref, coeff_ref, *rest):
    rest = list(rest)
    partner_refs = [rest.pop(0) for _ in range(count)]
    acc_in = None if first else rest.pop(0)
    scaled = rest.pop()
    acc = rest.pop()
    step = pl.program_id(0)
    cols, rows = plain_ref.shape

    @pl.when(switch_ref[0] != 0)
    def _():
        @pl.when(step == 0)
        def _():
            acc[...] = jnp.zeros_like(acc) if first else acc_in[...]

        for k in range(LAGS):
            part = plain_ref if k <= HL else swapped_ref
            scaled[k * cols:(k + 1) * cols, :] = part[...] * coeff_ref[k:k + 1, :]

        window = lax.broadcasted_iota(jnp.int32, (16, cols), 0) % windows
        partner = []
        for index, ref in enumerate(partner_refs):
            weights = jnp.zeros((16, cols), jnp.float32)
            for w in range(windows):
                weight = switch_ref[2 + index * windows + w].astype(jnp.float32)
                weights = jnp.where(window == w, weight, weights)
            weights = jnp.broadcast_to(weights.astype(jnp.bfloat16)[None], (rows // 16, 16, cols))
            partner.append(ref[...] * weights.reshape(rows, cols))
        partner = partner[0] if count == 1 else jnp.concatenate(partner, axis=1)
        acc[...] += jnp.dot(scaled[...], partner, preferred_element_type=jnp.float32)

        @pl.when(step == pl.num_programs(0) - 1)
        def _():
            def write(out, index, mirrored):
                for lag in range(LAGS):
                    value = lag_result(acc, slice(index * cols, (index + 1) * cols), cols, lag)
                    if mirrored:
                        out[LAGS - 1 - lag] = value.T
                    else:
                        out[lag] = value

            for index, kind in enumerate(kinds):
                out = rest.pop(0)
                if kind == "either":
                    pl.when(switch_ref[1] == 0)(functools.partial(write, out, index, False))
                    pl.when(switch_ref[1] != 0)(functools.partial(write, out, index, True))
                else:
                    write(out, index, False)
                if kind == "both":
                    write(rest.pop(0), index, True)


def corr(switch, turned, coeffs, partners, kinds, name, start=0, acc=None, common=True):
    plain, swapped = turned
    cols = plain.shape[0]
    rows = partners[0].shape[0]
    skip = start // STEP
    count = len(partners)
    windows = (switch.shape[0] - 2) // count
    total_shape = jax.ShapeDtypeStruct((LAGS * cols, count * cols), jnp.float32)
    total_spec = pl.BlockSpec(total_shape.shape, lambda s, on: (0, 0))
    in_specs = [
        pl.BlockSpec((cols, STEP), lambda s, on: (0, s * on[0] + skip)),
        pl.BlockSpec((cols, STEP), lambda s, on: (0, s * on[0] + skip)),
        pl.BlockSpec((LAGS, STEP), lambda s, on: (0, s * on[0] + skip)),
    ] + [pl.BlockSpec((STEP, cols), lambda s, on: (s * on[0], 0))] * count
    args = [plain, swapped, coeffs, *partners]
    if acc is not None:
        in_specs.append(total_spec)
        args.append(acc)
    scratch = [pltpu.VMEM((LAGS * cols, STEP), jnp.bfloat16)]
    if kinds:
        results = count + kinds.count("both")
        out_shape = [jax.ShapeDtypeStruct((LAGS, cols, cols), jnp.bfloat16)] * results
        out_specs = [pl.BlockSpec((LAGS, cols, cols), lambda s, on: (0, 0, 0))] * results
        scratch = [pltpu.VMEM(total_shape.shape, jnp.float32)] + scratch
    else:
        out_shape, out_specs = [total_shape], [total_spec]
    return pl.pallas_call(
        functools.partial(corr_kernel, windows, count, acc is None, kinds),
        grid_spec=pltpu.PrefetchScalarGridSpec(
            num_scalar_prefetch=1,
            grid=(rows // STEP,),
            in_specs=in_specs,
            out_specs=out_specs,
            scratch_shapes=scratch,
        ),
        out_shape=out_shape,
        compiler_params=PARAMS,
        cost_estimate=pl.CostEstimate(
            flops=2 * count * LAGS * cols * cols * rows if common else 0,
            bytes_accessed=2 * (2 + count) * rows * cols if common else 0,
            transcendentals=0,
        ),
        name=name,
    )(switch, *args)


def local(spectra, quality):
    count = lax.axis_size("chan")
    half = count // 2
    me = lax.axis_index("chan")
    freq_count, _, window_count, cols = spectra.shape
    block = spectra.reshape(-1, cols)

    first_far, second_far = [], []
    for p in range(half):
        if p in (0, half - 1):
            first_far.append((p + half, p))
        elif p % 2 == 0 and p >= half // 2:
            first_far.append((p, p + half))
        elif p in (1, 3):
            second_far.append((p, p + half))
        else:
            second_far.append((p + half, p))
    late_near = [(2, 1), (4, 3)]
    first_pairs = first_far + [(0, 1), (half - 1, half - 2)]
    second_pairs = second_far + late_near
    near_pairs = [(d + 1, d) for d in range(1, count - 1) if d not in (1, 3, half - 2, half - 1)]
    near_pairs += [(0, half - 1), (half - 1, 0)]
    first_back = [(t, s) for s, t in first_far] + [(1, 0)]
    second_back = [(t, s) for s, t in second_far]
    side_pairs = [(0, half - 1), (half - 1, count - 1)]

    def among(devices):
        return functools.reduce(jnp.logical_or, [me == d for d in devices])

    def switch(on, other, *weights):
        flags = jnp.stack([jnp.asarray(on), jnp.asarray(other)]).astype(jnp.int32)
        return jnp.concatenate([flags, *weights])

    first_in = lax.ppermute(block, "chan", first_pairs)
    near_in = lax.ppermute(block, "chan", near_pairs)
    first_flags = lax.ppermute(quality, "chan", first_pairs)[0]
    near_flags = lax.ppermute(quality, "chan", near_pairs)[0]
    second_flags = lax.ppermute(quality, "chan", second_pairs)[0]
    coeffs = lag_rows(freq_count, window_count)
    own = turn(block, switch(True, False), "turn_own")
    halves = split(block)

    late_half, own, coeffs, first_in, near_in = lax.optimization_barrier((halves[0], own, coeffs, first_in, near_in))
    second_in = [lax.ppermute(late_half, "chan", second_pairs)]
    flags = quality[0]
    both = switch(True, False, flags * near_flags, flags * first_flags)
    near, first, first_mirror = corr(both, own, coeffs, [near_in, first_in], ["plain", "both"], "near_first")
    late_half, near = lax.optimization_barrier((halves[1], near))
    second_in.append(lax.ppermute(late_half, "chan", second_pairs))
    first_returned = lax.ppermute(first_mirror, "chan", first_back)

    side_switch = switch(among([0, half - 1]), me == half - 1, near_flags * first_flags)
    side_switch, near = lax.optimization_barrier((side_switch, near))
    side_turned = turn(near_in, side_switch, "turn_side", common=False)
    side, = corr(side_switch, side_turned, coeffs, [first_in], ["either"], "side", common=False)
    side_returned = lax.ppermute(side, "chan", side_pairs)

    second_switch = switch(among([t for _, t in second_pairs]), False, flags * second_flags)
    second_switch, side, first_returned = lax.optimization_barrier((second_switch, side, first_returned))
    total, = corr(second_switch, own, coeffs, second_in[:1], (), "second_a")
    middle = halves[0].shape[0]
    second, second_mirror = corr(second_switch, own, coeffs, second_in[1:], ["both"], "second_b", middle, total)
    second_returned = lax.ppermute(second_mirror, "chan", second_back)

    far = jnp.where(among([t for _, t in first_far]), first, second)
    far = jnp.where(among([s for s, _ in first_far]), first_returned, far)
    far = jnp.where(among([s for s, _ in second_far]), second_returned, far)
    near = jnp.where(among([t for _, t in late_near]), second, near)
    near = jnp.where(among([half - 1, count - 1]), side_returned, near)
    near = jnp.where(me == 0, first_returned, jnp.where(me == half - 2, first, near))
    return near[None], far[None]


def solution(mesh):
    return jax.shard_map(
        local,
        mesh=mesh,
        in_specs=(P(None, None, None, ("grp", "chan")), P(("grp", "chan"), None)),
        out_specs=(P(("grp", "chan"), None, None, None), P(("grp", "chan"), None, None, None)),
        check_vma=False,
    )
```

time: 104 us -> 78.4 us (0.75)
  Pallas kernels: 43.6 us -> 27.5 us
  starting transfers between devices: 44.1 us -> 28.9 us
  local copies, waits for them, and re-layouts: 0.89 us -> 6.82 us
  waiting for transfers between devices: 7.23 us -> 9.24 us
  other arithmetic: 5.87 us -> 4.35 us
    pallas_call x7, Pallas kernels: 43.6 us -> 27.5 us  [the longest x4 19.6 us: corr(): pl.pallas_call(functools.partial(corr_kernel, windows, count, acc is None...]
    ppermute x1, starting transfers between devices: 17 us -> 1.49 us  [local(): first_returned = lax.ppermute(first_mirror, 'chan', first_back)]
    unnamed x4 -> x30, local copies, waits for them, and re-layouts: 0.89 us -> 6.82 us
    ppermute x6 -> x7, waiting for transfers between devices: 0.02 us -> 2.01 us  [the longest x1 2 us: local(): second_in.append(lax.ppermute(late_half, 'chan', second_pairs))]
    convert_element_type x2, other arithmetic: 1.2 us -> 0.15 us  [switch(): flags = jnp.stack([jnp.asarray(on), jnp.asarray(other)]).astype(jnp.int32)]
    ppermute x6 -> x7, starting transfers between devices: 24.5 us -> 24.7 us  [the longest x1 11.8 us: local(): second_in = [lax.ppermute(late_half, 'chan', second_pairs)]]
  transfers between devices with their start and end apart: 9 -> 10, of which waited for: 1 -> 2; matrix products, arithmetic and copies ran while one was open for 4% -> 3% of each run, Pallas kernels for 37% -> 35%
where the time goes in v7:
time: 78.4 us; the launch traced here: 77.8 us
  starting transfers between devices  28.9 us (37%)
  Pallas kernels  27.5 us (35%)
  waiting for transfers between devices  9.24 us (12%)
  local copies, waits for them, and re-layouts  6.82 us (9%)
  other arithmetic  4.35 us (6%)
  between operations  0.99 us (1%)
    pallas_call x4, Pallas kernels, corr(): pl.pallas_call(functools.partial(corr_kernel, windows, count, acc is None...  19.6 us
    ppermute x1, starting transfers between devices, local(): second_in = [lax.ppermute(late_half, 'chan', second_pairs)]  11.8 us
    ppermute x1, waiting for transfers between devices, local(): second_returned = lax.ppermute(second_mirror, 'chan', second_back)  7.22 us
    ppermute x1, starting transfers between devices, local(): second_flags = lax.ppermute(quality, 'chan', second_pairs)[0]  6.97 us
    unnamed x30, local copies, waits for them, and re-layouts  6.82 us
    pallas_call x2, Pallas kernels, turn(): pl.pallas_call(turn_kernel, grid_spec=pltpu.PrefetchScalarGridSpec(num_sc...  4.76 us
    pallas_call x1, Pallas kernels, split(): pl.pallas_call(split_kernel, grid=(steps,), in_specs=[pl.BlockSpec((STEP,...  3.12 us
    broadcast_in_dim x1, other arithmetic, local(): return (near[None], far[None])  2.04 us
  transfers between devices with their start and end apart: 10, of which 2 were waited for; matrix products, arithmetic and copies ran while one was open for 3% of the time, Pallas kernels for 35%

profile of v7, /device:TPU:1, one launch (start us, length us, event | category | flops | bytes accessed | tf_op | source)
XLA Modules:
  0.0 77.8 jit_solution(17778678027969791973)
XLA Ops:
  0.6 1.3 %collective-permute-start.3 = (bf16[8192,128]{1,0:T(8,128)(2,1)}, bf16[8192,128]{1,0:T(8,128)(2,1)S(1)}, u32[]{:S(2)}, u32[]{:S(2)}) collective-permute-start(bf16[8192,128]{1,0:T(8,128)(2,1)} %bitcast.16), channel_id=1, source_target_pairs={{8,0},{4,12},{6,14},{15,7},{0,1},{7,6},{24,16},{20,28},{22,30},{31... | collective-permute-start | bytes 6291464 | tf_op jit(solution)/shard_map/ppermute | solution.py:237
  1.9 0.8 %collective-permute-start.4 = (bf16[8192,128]{1,0:T(8,128)(2,1)}, bf16[8192,128]{1,0:T(8,128)(2,1)S(1)}, u32[]{:S(2)}, u32[]{:S(2)}) collective-permute-start(bf16[8192,128]{1,0:T(8,128)(2,1)} %bitcast.17), channel_id=1, source_target_pairs={{3,2},{5,4},{6,5},{9,8},{10,9},{11,10},{12,11},{13,12},{14,13},{15... | collective-permute-start | bytes 6291464 | tf_op jit(solution)/shard_map/ppermute | solution.py:238
  2.7 7.0 %collective-permute-start = (s32[1,4]{1,0:T(1,128)}, s32[1,4]{1,0:T(1,128)S(1)}, u32[]{:S(2)}, u32[]{:S(2)}) collective-permute-start(s32[1,4]{1,0:T(1,128)} %param.3), channel_id=1, source_target_pairs={{1,9},{10,2},{3,11},{13,5},{2,1},{4,3},{17,25},{26,18},{19,27},{29... | collective-permute-start | bytes 56 | tf_op jit(solution)/shard_map/ppermute | solution.py:241
  10.4 1.3 %collective-permute-start.2 = (s32[1,4]{1,0:T(1,128)}, s32[1,4]{1,0:T(1,128)S(1)}, u32[]{:S(2)}, u32[]{:S(2)}) collective-permute-start(s32[1,4]{1,0:T(1,128)} %param.3), channel_id=1, source_target_pairs={{8,0},{4,12},{6,14},{15,7},{0,1},{7,6},{24,16},{20,28},{22,30},{31... | collective-permute-start | bytes 56 | tf_op jit(solution)/shard_map/ppermute | solution.py:239
  11.7 0.9 %multiply_convert_fusion = (bf16[5,8192]{1,0:T(8,128)(2,1)S(1)}, f32[5,8192]{1,0:T(8,128)S(1)}) fusion(f32[8192]{0:T(1024)S(1)} %fusion.9, f32[5]{0:T(128)S(1)} %iota_multiply_fusion), kind=kLoop, calls=%fused_computation.3 | loop fusion | flops 122880 | bytes 278548 | tf_op jit(solution)/shard_map/convert
  12.7 0.9 %fusion.2 = bf16[4,8192]{1,0:T(4,128)(2,1)S(1)} fusion(f32[5,8192]{1,0:T(8,128)S(1)} %get-tuple-element.51, f32[8192]{0:T(1024)S(1)} %select_multiply_fusion), kind=kLoop, calls=%fused_computation.7 | loop fusion | flops 98304 | bytes 229376 | tf_op jit(solution)/shard_map/convert.1
  13.6 1.6 %copy-done.2 = bf16[1024,2,4,128]{3,2,1,0:T(4,128)(2,1)S(1)} copy-done((bf16[1024,2,4,128]{3,2,1,0:T(4,128)(2,1)S(1)}, bf16[1024,2,4,128]{3,2,1,0:T(4,128)(2,1)}, u32[]{:S(2)}) %copy-start.2) | copy-done | bytes 2097176
  15.2 3.1 %split.1 = (bf16[4096,128]{1,0:T(8,128)(2,1)}, bf16[4096,128]{1,0:T(8,128)(2,1)}) custom-call(bf16[8192,128]{1,0:T(8,128)(2,1)S(1)} %bitcast.18), custom_call_target="tpu_custom_call" | custom-call | bytes 4194304 | tf_op jit(solution)/shard_map/split/pallas_call | solution.py:47
  18.3 3.9 %turn_own.1 = (bf16[128,8192]{1,0:T(8,128)(2,1)S(1)}, bf16[128,8192]{1,0:T(8,128)(2,1)S(1)}) custom-call(s32[2]{0:T(128)S(1)} %copy-done.11, bf16[8192,128]{1,0:T(8,128)(2,1)S(1)} %bitcast.19), custom_call_target="tpu_custom_call" | custom-call | bytes 6291456 | tf_op jit(solution)/shard_map/turn_own/pallas_call | solution.py:82
  22.5 11.8 %collective-permute-start.8 = (bf16[4096,128]{1,0:T(8,128)(2,1)}, bf16[4096,128]{1,0:T(8,128)(2,1)}, u32[]{:S(2)}, u32[]{:S(2)}) collective-permute-start(bf16[4096,128]{1,0:T(8,128)(2,1)} %get-tuple-element.44), channel_id=1, source_target_pairs={{1,9},{10,2},{3,11},{13,5},{2,1},{4,3},{17,25},{26,18},{19,27},{29... | collective-permute-start | bytes 3145736 | tf_op jit(solution)/shard_map/ppermute | solution.py:247
  34.3 7.9 %near_first.1 = (bf16[9,128,128]{2,1,0:T(8,128)(2,1)S(1)}, bf16[9,128,128]{2,1,0:T(8,128)(2,1)S(1)}, bf16[9,128,128]{2,1,0:T(8,128)(2,1)S(1)}) custom-call(s32[10]{0:T(128)S(1)} %pad_add_fusion.2.switch_ref, bf16[128,8192]{1,0:T(8,128)(2,1)S(1)} %get-tuple-element.29.plain_ref, bf16[128,8192]{1,0:T(8,128)(2,1)S(1)} %get-tuple-element.30.swapped_ref, ...), custom_call_target="tpu_custom_call" | custom-call | flops 4831838208 | bytes 8388608 | tf_op jit(solution)/shard_map/near_first/pallas_call | solution.py:184
  44.4 1.9 %collective-permute-start.7 = (bf16[4096,128]{1,0:T(8,128)(2,1)}, bf16[4096,128]{1,0:T(8,128)(2,1)S(1)}, u32[]{:S(2)}, u32[]{:S(2)}) collective-permute-start(bf16[4096,128]{1,0:T(8,128)(2,1)} %get-tuple-element.43), channel_id=1, source_target_pairs={{1,9},{10,2},{3,11},{13,5},{2,1},{4,3},{17,25},{26,18},{19,27},{29... | collective-permute-start | bytes 3145736 | tf_op jit(solution)/shard_map/ppermute | solution.py:252
  46.4 1.5 %collective-permute-start.5 = (bf16[9,128,128]{2,1,0:T(8,128)(2,1)}, bf16[9,128,128]{2,1,0:T(8,128)(2,1)S(1)}, u32[]{:S(2)}, u32[]{:S(2)}) collective-permute-start(bf16[9,128,128]{2,1,0:T(8,128)(2,1)} %copy-done.12), channel_id=1, source_target_pairs={{0,8},{12,4},{14,6},{7,15},{1,0},{16,24},{28,20},{30,22},{23,31},{... | collective-permute-start | bytes 884744 | tf_op jit(solution)/shard_map/ppermute | solution.py:253
  48.2 1.6 %copy-done.5 = bf16[8192,128]{1,0:T(8,128)(2,1)S(1)} copy-done((bf16[8192,128]{1,0:T(8,128)(2,1)S(1)}, bf16[8192,128]{1,0:T(8,128)(2,1)}, u32[]{:S(2)}) %copy-start.5) | copy-done | bytes 2097176
  49.8 0.8 %turn_side.1 = (bf16[128,8192]{1,0:T(8,128)(2,1)S(1)}, bf16[128,8192]{1,0:T(8,128)(2,1)S(1)}) custom-call(s32[6]{0:T(128)S(1)} %pad_add_fusion.1.active_ref.switch_ref, bf16[8192,128]{1,0:T(8,128)(2,1)S(1)} %copy-done.5), custom_call_target="tpu_custom_call" | custom-call | tf_op jit(solution)/shard_map/turn_side/pallas_call | solution.py:82
  50.6 0.8 copy-done.7
  51.4 1.7 %side.1 = bf16[9,128,128]{2,1,0:T(8,128)(2,1)} custom-call(s32[6]{0:T(128)S(1)} %pad_add_fusion.1.active_ref.switch_ref, bf16[128,8192]{1,0:T(8,128)(2,1)S(1)} %get-tuple-element.37.plain_ref, bf16[128,8192]{1,0:T(8,128)(2,1)S(1)} %get-tuple-element.38.swapped_ref, bf16[9,8192]{1,0:T(8,128)(2,1)S(1)} %pad_maximum_fusion.coeff_ref, ...), custom_call_target="tpu_custom_call" | custom-call | tf_op jit(solution)/shard_map/side/pallas_call | solution.py:184
  53.0 1.4 %collective-permute-start.6 = (bf16[9,128,128]{2,1,0:T(8,128)(2,1)}, bf16[9,128,128]{2,1,0:T(8,128)(2,1)}, u32[]{:S(2)}, u32[]{:S(2)}) collective-permute-start(bf16[9,128,128]{2,1,0:T(8,128)(2,1)} %side.1), channel_id=1, source_target_pairs={{0,7},{7,15},{16,23},{23,31}} | collective-permute-start | bytes 884744 | tf_op jit(solution)/shard_map/ppermute | solution.py:259
  54.4 5.1 %second_a.1.rest_1_ = f32[1152,128]{1,0:T(8,128)S(1)} custom-call(s32[6]{0:T(128)S(1)} %pad_add_fusion.switch_ref, bf16[128,8192]{1,0:T(8,128)(2,1)S(1)} %get-tuple-element.29.plain_ref, bf16[128,8192]{1,0:T(8,128)(2,1)S(1)} %copy-done.1, bf16[9,8192]{1,0:T(8,128)(2,1)S(1)} %pad_maximum_fusion.coeff_ref, bf16[4096,128]{1,0:T(8,128)(2,1)} %collective-permute-done.8.rest_0_), custom_call_target="tpu_custom_call" | custom-call | flops 1207959552 | bytes 3145728 | tf_op jit(solution)/shard_map/second_a/pallas_call | solution.py:184
  59.5 2.0 %collective-permute-done.7.rest_0_ = bf16[4096,128]{1,0:T(8,128)(2,1)S(1)} collective-permute-done((bf16[4096,128]{1,0:T(8,128)(2,1)}, bf16[4096,128]{1,0:T(8,128)(2,1)S(1)}, u32[]{:S(2)}, u32[]{:S(2)}) %collective-permute-start.7) | collective-permute-done | bytes 1048608 | tf_op jit(solution)/shard_map/ppermute | solution.py:252
  61.5 4.9 %second_b.1 = (bf16[9,128,128]{2,1,0:T(8,128)(2,1)S(1)}, bf16[9,128,128]{2,1,0:T(8,128)(2,1)}) custom-call(s32[6]{0:T(128)S(1)} %pad_add_fusion.switch_ref, bf16[128,8192]{1,0:T(8,128)(2,1)S(1)} %get-tuple-element.29.plain_ref, bf16[128,8192]{1,0:T(8,128)(2,1)S(1)} %copy-done.1, bf16[9,8192]{1,0:T(8,128)(2,1)S(1)} %pad_maximum_fusion.coeff_ref, ...), custom_call_target="tpu_custom_call" | custom-call | flops 1207959552 | bytes 3145728 | tf_op jit(solution)/shard_map/second_b/pallas_call | solution.py:184
  67.2 1.3 %collective-permute-start.9 = (bf16[9,128,128]{2,1,0:T(8,128)(2,1)}, bf16[9,128,128]{2,1,0:T(8,128)(2,1)S(1)}, u32[]{:S(2)}, u32[]{:S(2)}) collective-permute-start(bf16[9,128,128]{2,1,0:T(8,128)(2,1)} %get-tuple-element.47), channel_id=1, source_target_pairs={{9,1},{2,10},{11,3},{5,13},{25,17},{18,26},{27,19},{21,29}} | collective-permute-start | bytes 884744 | tf_op jit(solution)/shard_map/ppermute | solution.py:266
  68.5 7.2 %collective-permute-done.9 = bf16[9,128,128]{2,1,0:T(8,128)(2,1)S(1)} collective-permute-done((bf16[9,128,128]{2,1,0:T(8,128)(2,1)}, bf16[9,128,128]{2,1,0:T(8,128)(2,1)S(1)}, u32[]{:S(2)}, u32[]{:S(2)}) %collective-permute-start.9) | collective-permute-done | bytes 294944 | tf_op jit(solution)/shard_map/ppermute | solution.py:266
  75.7 2.0 %select_bitcast_fusion = (bf16[1,9,128,128]{3,2,1,0:T(8,128)(2,1)}, bf16[1,9,128,128]{3,2,1,0:T(8,128)(2,1)}) fusion(bf16[9,128,128]{2,1,0:T(8,128)(2,1)S(1)} %collective-permute-done.9, bf16[9,128,128]{2,1,0:T(8,128)(2,1)} %copy-done.13, bf16[9,128,128]{2,1,0:T(8,128)(2,1)} %copy-done.9, bf16[9,128,128]{2,1,0:T(8,128)(2,1)} %copy-done.10, pred[]{:T(512)S(6)} %or.67, ...), kind=kLoop, calls=%fused_computation | loop fusion | flops 1032192 | bytes 2359303 | tf_op jit(solution)/shard_map/broadcast_in_dim | solution.py:274
  (46 shorter events, 4.1 us)
Async XLA Ops:
  0.6 17.6 %copy-start.11 = (s32[2]{0:T(128)S(1)}, s32[2]{0:T(128)}, u32[]{:S(2)}) copy-start(s32[2]{0:T(128)} %constant.23.clone.1.active_ref) | copy-start | bytes 28
  0.6 21.8 %collective-permute-start.3 = (bf16[8192,128]{1,0:T(8,128)(2,1)}, bf16[8192,128]{1,0:T(8,128)(2,1)S(1)}, u32[]{:S(2)}, u32[]{:S(2)}) collective-permute-start(bf16[8192,128]{1,0:T(8,128)(2,1)} %bitcast.16), channel_id=1, source_target_pairs={{8,0},{4,12},{6,14},{15,7},{0,1},{7,6},{24,16},{20,28},{22,30},{31... | collective-permute-start | bytes 6291464 | tf_op jit(solution)/shard_map/ppermute | solution.py:237
  1.9 20.5 %collective-permute-start.4 = (bf16[8192,128]{1,0:T(8,128)(2,1)}, bf16[8192,128]{1,0:T(8,128)(2,1)S(1)}, u32[]{:S(2)}, u32[]{:S(2)}) collective-permute-start(bf16[8192,128]{1,0:T(8,128)(2,1)} %bitcast.17), channel_id=1, source_target_pairs={{3,2},{5,4},{6,5},{9,8},{10,9},{11,10},{12,11},{13,12},{14,13},{15... | collective-permute-start | bytes 6291464 | tf_op jit(solution)/shard_map/ppermute | solution.py:238
  2.7 19.6 %collective-permute-start = (s32[1,4]{1,0:T(1,128)}, s32[1,4]{1,0:T(1,128)S(1)}, u32[]{:S(2)}, u32[]{:S(2)}) collective-permute-start(s32[1,4]{1,0:T(1,128)} %param.3), channel_id=1, source_target_pairs={{1,9},{10,2},{3,11},{13,5},{2,1},{4,3},{17,25},{26,18},{19,27},{29... | collective-permute-start | bytes 56 | tf_op jit(solution)/shard_map/ppermute | solution.py:241
  9.7 12.6 %collective-permute-start.1 = (s32[1,4]{1,0:T(1,128)}, s32[1,4]{1,0:T(1,128)S(1)}, u32[]{:S(2)}, u32[]{:S(2)}) collective-permute-start(s32[1,4]{1,0:T(1,128)} %param.3), channel_id=1, source_target_pairs={{3,2},{5,4},{6,5},{9,8},{10,9},{11,10},{12,11},{13,12},{14,13},{15... | collective-permute-start | bytes 56 | tf_op jit(solution)/shard_map/ppermute | solution.py:240
  10.4 12.0 %collective-permute-start.2 = (s32[1,4]{1,0:T(1,128)}, s32[1,4]{1,0:T(1,128)S(1)}, u32[]{:S(2)}, u32[]{:S(2)}) collective-permute-start(s32[1,4]{1,0:T(1,128)} %param.3), channel_id=1, source_target_pairs={{8,0},{4,12},{6,14},{15,7},{0,1},{7,6},{24,16},{20,28},{22,30},{31... | collective-permute-start | bytes 56 | tf_op jit(solution)/shard_map/ppermute | solution.py:239
  13.6 1.6 %copy-start.2 = (bf16[1024,2,4,128]{3,2,1,0:T(4,128)(2,1)S(1)}, bf16[1024,2,4,128]{3,2,1,0:T(4,128)(2,1)}, u32[]{:S(2)}) copy-start(bf16[1024,2,4,128]{3,2,1,0:T(4,128)(2,1)} %param.2) | copy-start | bytes 6291460
  15.2 3.1 %copy-start.3 = (bf16[1024,2,4,128]{3,2,1,0:T(4,128)(2,1)S(1)}, bf16[1024,2,4,128]{3,2,1,0:T(4,128)(2,1)}, u32[]{:S(2)}) copy-start(bf16[1024,2,4,128]{3,2,1,0:T(4,128)(2,1)} %param.2) | copy-start | bytes 6291460
  15.2 7.2 %copy-start.14 = (s32[1,4]{1,0:T(1,128)S(1)}, s32[1,4]{1,0:T(1,128)}, u32[]{:S(2)}) copy-start(s32[1,4]{1,0:T(1,128)} %param.3) | copy-start | bytes 52
  22.2 20.0 %copy-start = (bf16[128,8192]{1,0:T(8,128)(2,1)}, bf16[128,8192]{1,0:T(8,128)(2,1)S(1)}, u32[]{:S(2)}) copy-start(bf16[128,8192]{1,0:T(8,128)(2,1)S(1)} %get-tuple-element.30.swapped_ref) | copy-start | bytes 6291460
  22.5 19.8 %copy-start.6 = (bf16[8192,128]{1,0:T(8,128)(2,1)}, bf16[8192,128]{1,0:T(8,128)(2,1)S(1)}, u32[]{:S(2)}) copy-start(bf16[8192,128]{1,0:T(8,128)(2,1)S(1)} %collective-permute-done.3.rest_1_.rest_0_) | copy-start | bytes 6291460
  22.5 19.8 %copy-start.4 = (bf16[8192,128]{1,0:T(8,128)(2,1)}, bf16[8192,128]{1,0:T(8,128)(2,1)S(1)}, u32[]{:S(2)}) copy-start(bf16[8192,128]{1,0:T(8,128)(2,1)S(1)} %collective-permute-done.4.rest_0_.x_ref) | copy-start | bytes 6291460
  22.5 31.9 %collective-permute-start.8 = (bf16[4096,128]{1,0:T(8,128)(2,1)}, bf16[4096,128]{1,0:T(8,128)(2,1)}, u32[]{:S(2)}, u32[]{:S(2)}) collective-permute-start(bf16[4096,128]{1,0:T(8,128)(2,1)} %get-tuple-element.44), channel_id=1, source_target_pairs={{1,9},{10,2},{3,11},{13,5},{2,1},{4,3},{17,25},{26,18},{19,27},{29... | collective-permute-start | bytes 3145736 | tf_op jit(solution)/shard_map/ppermute | solution.py:247
  43.0 0.7 copy-start.9
  43.7 0.7 copy-start.12
  44.4 17.1 %collective-permute-start.7 = (bf16[4096,128]{1,0:T(8,128)(2,1)}, bf16[4096,128]{1,0:T(8,128)(2,1)S(1)}, u32[]{:S(2)}, u32[]{:S(2)}) collective-permute-start(bf16[4096,128]{1,0:T(8,128)(2,1)} %get-tuple-element.43), channel_id=1, source_target_pairs={{1,9},{10,2},{3,11},{13,5},{2,1},{4,3},{17,25},{26,18},{19,27},{29... | collective-permute-start | bytes 3145736 | tf_op jit(solution)/shard_map/ppermute | solution.py:252
  46.4 7.9 %collective-permute-start.5 = (bf16[9,128,128]{2,1,0:T(8,128)(2,1)}, bf16[9,128,128]{2,1,0:T(8,128)(2,1)S(1)}, u32[]{:S(2)}, u32[]{:S(2)}) collective-permute-start(bf16[9,128,128]{2,1,0:T(8,128)(2,1)} %copy-done.12), channel_id=1, source_target_pairs={{0,8},{12,4},{14,6},{7,15},{1,0},{16,24},{28,20},{30,22},{23,31},{... | collective-permute-start | bytes 884744 | tf_op jit(solution)/shard_map/ppermute | solution.py:253
  48.2 1.6 %copy-start.5 = (bf16[8192,128]{1,0:T(8,128)(2,1)S(1)}, bf16[8192,128]{1,0:T(8,128)(2,1)}, u32[]{:S(2)}) copy-start(bf16[8192,128]{1,0:T(8,128)(2,1)} %copy-done.4) | copy-start | bytes 6291460
  49.8 1.6 %copy-start.7 = (bf16[8192,128]{1,0:T(8,128)(2,1)S(1)}, bf16[8192,128]{1,0:T(8,128)(2,1)}, u32[]{:S(2)}) copy-start(bf16[8192,128]{1,0:T(8,128)(2,1)} %copy-done.6) | copy-start | bytes 6291460
  51.4 3.0 %copy-start.1 = (bf16[128,8192]{1,0:T(8,128)(2,1)S(1)}, bf16[128,8192]{1,0:T(8,128)(2,1)}, u32[]{:S(2)}) copy-start(bf16[128,8192]{1,0:T(8,128)(2,1)} %copy-done) | copy-start | bytes 6291460
  53.0 15.5 %collective-permute-start.6 = (bf16[9,128,128]{2,1,0:T(8,128)(2,1)}, bf16[9,128,128]{2,1,0:T(8,128)(2,1)}, u32[]{:S(2)}, u32[]{:S(2)}) collective-permute-start(bf16[9,128,128]{2,1,0:T(8,128)(2,1)} %side.1), channel_id=1, source_target_pairs={{0,7},{7,15},{16,23},{23,31}} | collective-permute-start | bytes 884744 | tf_op jit(solution)/shard_map/ppermute | solution.py:259
  54.4 5.1 %copy-start.13 = (bf16[9,128,128]{2,1,0:T(8,128)(2,1)}, bf16[9,128,128]{2,1,0:T(8,128)(2,1)S(1)}, u32[]{:S(2)}) copy-start(bf16[9,128,128]{2,1,0:T(8,128)(2,1)S(1)} %collective-permute-done.5) | copy-start | bytes 884740
  66.5 0.7 copy-start.10
  67.2 8.6 %collective-permute-start.9 = (bf16[9,128,128]{2,1,0:T(8,128)(2,1)}, bf16[9,128,128]{2,1,0:T(8,128)(2,1)S(1)}, u32[]{:S(2)}, u32[]{:S(2)}) collective-permute-start(bf16[9,128,128]{2,1,0:T(8,128)(2,1)} %get-tuple-element.47), channel_id=1, source_target_pairs={{9,1},{2,10},{11,3},{5,13},{25,17},{18,26},{27,19},{21,29}} | collective-permute-start | bytes 884744 | tf_op jit(solution)/shard_map/ppermute | solution.py:266
  (1 other events, 0.7 us)

commit v8 on v7

v8 whole, which is shorter than its diff:
```python
import functools
import math

import jax
import jax.numpy as jnp
from jax import lax
from jax.experimental import pallas as pl
from jax.experimental.pallas import tpu as pltpu
from jax.sharding import PartitionSpec as P

HL = 4
LAGS = 2 * HL + 1
STEP = 1024
PARTS = (5, 8)
PARAMS = pltpu.CompilerParams(vmem_limit_bytes=16 * 1024 * 1024)


def lag_rows(freq_count, window_count):
    per_bin = 2 * window_count
    row = jnp.arange(freq_count * per_bin, dtype=jnp.int32)
    freq_values = (row // per_bin).astype(jnp.float32)
    sign = jnp.where(row % per_bin < window_count, 1.0, -1.0)
    lag_values = jnp.arange(HL + 1, dtype=jnp.float32)
    phases = jnp.pi / freq_count * lag_values[:, None] * freq_values[None, :]
    factor = 1.0 / math.sqrt(window_count * freq_count)
    cos_part = jnp.cos(phases) * factor
    sin_part = -jnp.sin(phases[1:]) * factor * sign[None, :]
    return jnp.concatenate([cos_part, sin_part], axis=0).astype(jnp.bfloat16)


def split_kernel(middle, x_ref, first_ref, last_ref):
    step = pl.program_id(0)

    @pl.when(step < middle)
    def _():
        first_ref[...] = x_ref[...]

    @pl.when(step >= middle)
    def _():
        last_ref[...] = x_ref[...]


def split(x):
    rows, cols = x.shape
    steps = rows // STEP
    middle = steps * PARTS[0] // PARTS[1]
    return pl.pallas_call(
        functools.partial(split_kernel, middle),
        grid=(steps,),
        in_specs=[pl.BlockSpec((STEP, cols), lambda s: (s, 0))],
        out_specs=[
            pl.BlockSpec((STEP, cols), lambda s: (jnp.minimum(s, middle - 1), 0)),
            pl.BlockSpec((STEP, cols), lambda s: (jnp.maximum(s - middle, 0), 0)),
        ],
        out_shape=[jax.ShapeDtypeStruct((n * STEP, cols), x.dtype) for n in (middle, steps - middle)],
        compiler_params=PARAMS,
        cost_estimate=pl.CostEstimate(flops=0, bytes_accessed=4 * rows * cols, transcendentals=0),
        name="split",
    )(x)


def turn_kernel(active_ref, x_ref, plain_ref, swapped_ref):
    @pl.when(active_ref[0] != 0)
    def _():
        rows, cols = x_ref.shape
        same = lax.broadcasted_iota(jnp.int32, (cols, cols), 0) == lax.broadcasted_iota(jnp.int32, (cols, cols), 1)
        eye = jnp.where(same, 1.0, 0.0).astype(jnp.bfloat16)
        source = lax.broadcasted_iota(jnp.int32, (2 * cols, 2 * cols), 0)
        target = lax.broadcasted_iota(jnp.int32, (2 * cols, 2 * cols), 1)
        exchange = jnp.where((source ^ 4) == target, 1.0, 0.0).astype(jnp.bfloat16)
        plain = lax.dot_general(eye, x_ref[...], (((1,), (1,)), ((), ())), preferred_element_type=jnp.float32)
        plain = plain.astype(jnp.bfloat16)
        plain_ref[...] = plain
        for t in range(0, rows, 2 * cols):
            swapped = jnp.dot(plain[:, t:t + 2 * cols], exchange, preferred_element_type=jnp.float32)
            swapped_ref[:, t:t + 2 * cols] = swapped.astype(jnp.bfloat16)


def turn(x, switch, name, common=True):
    rows, cols = x.shape
    out = jax.ShapeDtypeStruct((cols, rows), jnp.bfloat16)
    return pl.pallas_call(
        turn_kernel,
        grid_spec=pltpu.PrefetchScalarGridSpec(
            num_scalar_prefetch=1,
            grid=(rows // STEP,),
            in_specs=[pl.BlockSpec((STEP, cols), lambda s, on: (s * on[0], 0))],
            out_specs=[pl.BlockSpec((cols, STEP), lambda s, on: (0, s * on[0]))] * 2,
        ),
        out_shape=[out, out],
        compiler_params=PARAMS,
        cost_estimate=pl.CostEstimate(flops=0, bytes_accessed=6 * rows * cols if common else 0, transcendentals=0),
        name=name,
    )(switch, x)


def write_lags(out, acc, at, cols, mirrored):
    for lag in range(LAGS):
        k = abs(lag - HL)
        value = acc[k * cols:(k + 1) * cols, at]
        if k:
            odd = acc[(HL + k) * cols:(HL + k + 1) * cols, at]
            value = value + odd if lag > HL else value - odd
        value = value.astype(jnp.bfloat16)
        if mirrored:
            out[LAGS - 1 - lag] = value.T
        else:
            out[lag] = value


def scale(scaled, plain, swapped, coeff_ref):
    cols = plain.shape[0]
    for k in range(LAGS):
        part = plain if k <= HL else swapped
        scaled[k * cols:(k + 1) * cols, :] = part * coeff_ref[k:k + 1, :]


def weigh(x, switch_ref, begin, windows):
    rows, cols = x.shape
    window = lax.broadcasted_iota(jnp.int32, (16, cols), 0) % windows
    weights = jnp.zeros((16, cols), jnp.float32)
    for w in range(windows):
        weights = jnp.where(window == w, switch_ref[begin + w].astype(jnp.float32), weights)
    weights = jnp.broadcast_to(weights.astype(jnp.bfloat16)[None], (rows // 16, 16, cols))
    return x * weights.reshape(rows, cols)


def first_kernel(windows, switch_ref, plain_ref, swapped_ref, plain_alt, swapped_alt, coeff_ref, near_ref, first_ref,
                 own_ref, near_out, far_out, back_out, acc, scaled):
    step = pl.program_id(0)
    cols = plain_ref.shape[0]
    near_mirrored, special = switch_ref[0], switch_ref[1]

    @pl.when(step == 0)
    def _():
        acc[...] = jnp.zeros_like(acc)

    @pl.when(special == 0)
    def _():
        scale(scaled, plain_ref[...], swapped_ref[...], coeff_ref)

    @pl.when(special != 0)
    def _():
        scale(scaled, plain_alt[...], swapped_alt[...], coeff_ref)

    near = weigh(near_ref[...], switch_ref, 2, windows)
    far = weigh(jnp.where(special != 0, own_ref[...], first_ref[...]), switch_ref, 2 + windows, windows)
    acc[...] += jnp.dot(scaled[...], jnp.concatenate([near, far], axis=1), preferred_element_type=jnp.float32)

    @pl.when(step == pl.num_programs(0) - 1)
    def _():
        near_at, far_at = slice(0, cols), slice(cols, 2 * cols)

        @pl.when(special == 0)
        def _():
            write_lags(back_out, acc, far_at, cols, True)
            write_lags(far_out, acc, far_at, cols, False)

        @pl.when(special != 0)
        def _():
            write_lags(back_out, acc, far_at, cols, False)
            write_lags(far_out, acc, far_at, cols, True)

        pl.when(near_mirrored == 0)(lambda: write_lags(near_out, acc, near_at, cols, False))
        pl.when(near_mirrored != 0)(lambda: write_lags(near_out, acc, near_at, cols, True))


def first_sums(switch, own, alt, coeffs, near_in, first_in, block):
    rows, cols = block.shape
    windows = (switch.shape[0] - 2) // 2
    result = jax.ShapeDtypeStruct((LAGS, cols, cols), jnp.bfloat16)
    left = pl.BlockSpec((cols, STEP), lambda s, on: (0, s * (1 - on[1])))
    left_alt = pl.BlockSpec((cols, STEP), lambda s, on: (0, s * on[1]))
    right = pl.BlockSpec((STEP, cols), lambda s, on: (s, 0))
    right_usual = pl.BlockSpec((STEP, cols), lambda s, on: (s * (1 - on[1]), 0))
    right_special = pl.BlockSpec((STEP, cols), lambda s, on: (s * on[1], 0))
    return pl.pallas_call(
        functools.partial(first_kernel, windows),
        grid_spec=pltpu.PrefetchScalarGridSpec(
            num_scalar_prefetch=1,
            grid=(rows // STEP,),
            in_specs=[left, left, left_alt, left_alt, pl.BlockSpec((LAGS, STEP), lambda s, on: (0, s)),
                      right, right_usual, right_special],
            out_specs=[pl.BlockSpec(result.shape, lambda s, on: (0, 0, 0))] * 3,
            scratch_shapes=[pltpu.VMEM((LAGS * cols, 2 * cols), jnp.float32),
                            pltpu.VMEM((LAGS * cols, STEP), jnp.bfloat16)],
        ),
        out_shape=[result] * 3,
        compiler_params=PARAMS,
        cost_estimate=pl.CostEstimate(
            flops=4 * LAGS * cols * cols * rows, bytes_accessed=8 * rows * cols, transcendentals=0
        ),
        name="first_sums",
    )(switch, *own, *alt, coeffs, near_in, first_in, block)


def second_kernel(windows, first, switch_ref, plain_ref, swapped_ref, coeff_ref, partner_ref, *rest):
    on, late_near = switch_ref[0], switch_ref[1]
    step = pl.program_id(0)
    cols = plain_ref.shape[0]
    if first:
        acc, scaled = rest
    else:
        acc_in, near_in, far_in, near_out, far_out, back_out, acc, scaled = rest

    @pl.when(on != 0)
    def _():
        @pl.when(step == 0)
        def _():
            acc[...] = jnp.zeros_like(acc) if first else acc_in[...]

        scale(scaled, plain_ref[...], swapped_ref[...], coeff_ref)
        partner = weigh(partner_ref[...], switch_ref, 2, windows)
        acc[...] += jnp.dot(scaled[...], partner, preferred_element_type=jnp.float32)

    if not first:
        @pl.when(step == pl.num_programs(0) - 1)
        def _():
            here = slice(0, cols)

            @pl.when((on != 0) & (late_near == 0))
            def _():
                write_lags(back_out, acc, here, cols, True)
                write_lags(far_out, acc, here, cols, False)

            @pl.when((on == 0) | (late_near != 0))
            def _():
                far_out[...] = far_in[...]

            pl.when(late_near != 0)(lambda: write_lags(near_out, acc, here, cols, False))

            @pl.when(late_near == 0)
            def _():
                near_out[...] = near_in[...]


def second_sums(switch, own, coeffs, partner, start, earlier=None):
    rows, cols = partner.shape
    windows = switch.shape[0] - 2
    skip = start // STEP
    total = jax.ShapeDtypeStruct((LAGS * cols, cols), jnp.float32)
    total_spec = pl.BlockSpec(total.shape, lambda s, on: (0, 0))
    result = jax.ShapeDtypeStruct((LAGS, cols, cols), jnp.bfloat16)
    result_spec = pl.BlockSpec(result.shape, lambda s, on: (0, 0, 0))
    left = pl.BlockSpec((cols, STEP), lambda s, on: (0, s * on[0] + skip))
    in_specs = [left, left, pl.BlockSpec((LAGS, STEP), lambda s, on: (0, s * on[0] + skip)),
                pl.BlockSpec((STEP, cols), lambda s, on: (s * on[0], 0))]
    scratch = [pltpu.VMEM((LAGS * cols, STEP), jnp.bfloat16)]
    if earlier is None:
        out_shape, out_specs, earlier = [total], [total_spec], []
    else:
        out_shape, out_specs = [result] * 3, [result_spec] * 3
        in_specs += [total_spec, result_spec, result_spec]
        scratch = [pltpu.VMEM(total.shape, jnp.float32)] + scratch
    return pl.pallas_call(
        functools.partial(second_kernel, windows, not earlier),
        grid_spec=pltpu.PrefetchScalarGridSpec(
            num_scalar_prefetch=1,
            grid=(rows // STEP,),
            in_specs=in_specs,
            out_specs=out_specs,
            scratch_shapes=scratch,
        ),
        out_shape=out_shape,
        compiler_params=PARAMS,
        cost_estimate=pl.CostEstimate(
            flops=2 * LAGS * cols * cols * rows, bytes_accessed=6 * rows * cols, transcendentals=0
        ),
        name="second_last" if earlier else "second_part",
    )(switch, *own, coeffs, partner, *earlier)


def local(spectra, quality):
    count = lax.axis_size("chan")
    half = count // 2
    me = lax.axis_index("chan")
    freq_count, _, window_count, cols = spectra.shape
    block = spectra.reshape(-1, cols)

    first_far, second_far = [], []
    for p in range(half):
        if p in (0, half - 1):
            first_far.append((p + half, p))
        elif p % 2 == 0 and p >= half // 2:
            first_far.append((p, p + half))
        elif p in (1, 3):
            second_far.append((p, p + half))
        else:
            second_far.append((p + half, p))
    late_near = [(2, 1), (4, 3)]
    first_pairs = first_far + [(0, 1), (half - 1, half - 2)]
    second_pairs = second_far + late_near
    near_pairs = [(d + 1, d) for d in range(1, count - 1) if d not in (1, 3, half - 2, half - 1)]
    near_pairs += [(0, half - 1), (half - 1, 0)]
    first_back = [(t, s) for s, t in first_far] + [(1, 0)]
    second_back = [(t, s) for s, t in second_far]
    side_pairs = [(0, half - 1), (half - 1, count - 1)]

    def among(devices):
        return functools.reduce(jnp.logical_or, [me == d for d in devices])

    def switch(on, other, *weights):
        flags = jnp.stack([jnp.asarray(on), jnp.asarray(other)]).astype(jnp.int32)
        return jnp.concatenate([flags, *weights])

    first_in = lax.ppermute(block, "chan", first_pairs)
    near_in = lax.ppermute(block, "chan", near_pairs)
    coeffs = lag_rows(freq_count, window_count)
    own = turn(block, switch(True, False), "turn_own")
    parts = split(block)
    sent_flags, own = lax.optimization_barrier((quality, own))
    first_flags = lax.ppermute(sent_flags, "chan", first_pairs)[0]
    near_flags = lax.ppermute(sent_flags, "chan", near_pairs)[0]
    second_flags = lax.ppermute(sent_flags, "chan", second_pairs)[0]
    special = among([0, half - 1])
    usual_flags = quality[0]
    left_flags = jnp.where(special, first_flags, usual_flags)
    first_switch = switch(me == 0, special, left_flags * near_flags, usual_flags * first_flags)
    second_switch = switch(
        among([t for _, t in second_pairs]), among([t for _, t in late_near]), usual_flags * second_flags
    )

    late_part, own, coeffs, first_in, near_in = lax.optimization_barrier((parts[0], own, coeffs, first_in, near_in))
    second_first = lax.ppermute(late_part, "chan", second_pairs)
    alt = turn(first_in, switch(special, False), "turn_first", common=False)
    near, far, back = first_sums(first_switch, own, alt, coeffs, near_in, first_in, block)
    late_part, near = lax.optimization_barrier((parts[1], near))
    second_last = lax.ppermute(late_part, "chan", second_pairs)
    first_returned = lax.ppermute(back, "chan", first_back)
    side_returned = lax.ppermute(near, "chan", side_pairs)

    second_switch, first_returned = lax.optimization_barrier((second_switch, first_returned))
    total, = second_sums(second_switch, own, coeffs, second_first, 0)
    near = jnp.where(among([half - 1, count - 1]), side_returned, near)
    near = jnp.where(me == 0, first_returned, jnp.where(me == half - 2, far, near))
    far = jnp.where(among([s for s, _ in first_far]), first_returned, far)
    near, far, back = second_sums(
        second_switch, own, coeffs, second_last, parts[0].shape[0], [total, near, far]
    )
    second_returned = lax.ppermute(back, "chan", second_back)
    far = jnp.where(among([s for s, _ in second_far]), second_returned, far)
    return near[None], far[None]


def solution(mesh):
    return jax.shard_map(
        local,
        mesh=mesh,
        in_specs=(P(None, None, None, ("grp", "chan")), P(("grp", "chan"), None)),
        out_specs=(P(("grp", "chan"), None, None, None), P(("grp", "chan"), None, None, None)),
        check_vma=False,
    )
```

time: 78.4 us -> 97.9 us (1.25)
  starting transfers between devices: 28.9 us -> 44.7 us
  Pallas kernels: 27.5 us -> 34.7 us
  waiting for transfers between devices: 9.24 us -> 7.28 us
  local copies, waits for them, and re-layouts: 6.82 us -> 5.34 us
    ppermute x8, starting transfers between devices: 26.8 us -> 41.4 us  [the longest x1 21.2 us: local(): second_first = lax.ppermute(late_part, 'chan', second_pairs)]
    pallas_call x5 -> x4, Pallas kernels: 22.8 us -> 26.6 us  [the longest x1 11.6 us: first_sums(): pl.pallas_call(functools.partial(first_kernel, windows), grid_spec=pltpu....]
    pallas_call x2, Pallas kernels: 4.76 us -> 8.11 us  [turn(): pl.pallas_call(turn_kernel, grid_spec=pltpu.PrefetchScalarGridSpec(num_sc...]
    ppermute x8, waiting for transfers between devices: 9.23 us -> 7.28 us  [the longest x1 7.26 us: local(): second_returned = lax.ppermute(back, 'chan', second_back)]
    unnamed x30 -> x14, local copies, waits for them, and re-layouts: 6.82 us -> 5.34 us
    broadcast_in_dim x1, other arithmetic: 2.04 us -> 0.75 us  [local(): return (near[None], far[None])]
    ppermute x1, starting transfers between devices: 0.8 us -> 2 us  [local(): near_in = lax.ppermute(block, 'chan', near_pairs)]
    select_n x0 -> x1, other arithmetic: none -> 1.12 us  [local(): far = jnp.where(among([s for s, _ in first_far]), first_returned, far)]
  transfers between devices with their start and end apart: 10 -> 10, of which waited for: 2 -> 1; matrix products, arithmetic and copies ran while one was open for 3% -> 4% of each run, Pallas kernels for 35% -> 25%
where the time goes in v8:
time: 97.9 us; the launch traced here: 97.1 us
  starting transfers between devices  44.7 us (46%)
  Pallas kernels  34.7 us (35%)
  waiting for transfers between devices  7.28 us (7%)
  local copies, waits for them, and re-layouts  5.34 us (5%)
  other arithmetic  4.17 us (4%)
    ppermute x1, starting transfers between devices, local(): second_first = lax.ppermute(late_part, 'chan', second_pairs)  21.2 us
    pallas_call x1, Pallas kernels, first_sums(): pl.pallas_call(functools.partial(first_kernel, windows), grid_spec=pltpu....  11.6 us
    pallas_call x2, Pallas kernels, second_sums(): pl.pallas_call(functools.partial(second_kernel, windows, not earlier), gr...  10.1 us
    ppermute x1, starting transfers between devices, local(): first_returned = lax.ppermute(back, 'chan', first_back)  8.69 us
    pallas_call x2, Pallas kernels, turn(): pl.pallas_call(turn_kernel, grid_spec=pltpu.PrefetchScalarGridSpec(num_sc...  8.11 us
    ppermute x1, waiting for transfers between devices, local(): second_returned = lax.ppermute(back, 'chan', second_back)  7.26 us
    unnamed x14, local copies, waits for them, and re-layouts  5.34 us
    ppermute x1, starting transfers between devices, local(): second_flags = lax.ppermute(sent_flags, 'chan', second_pairs)[0]  5.04 us
  transfers between devices with their start and end apart: 10, of which 1 were waited for; matrix products, arithmetic and copies ran while one was open for 4% of the time, Pallas kernels for 25%

profile of v8, /device:TPU:1, one launch (start us, length us, event | category | flops | bytes accessed | tf_op | source)
XLA Modules:
  0.0 97.1 jit_solution(8368969981858270228)
XLA Ops:
  1.3 6.5 %turn_own.1 = (bf16[128,8192]{1,0:T(8,128)(2,1)S(1)}, bf16[128,8192]{1,0:T(8,128)(2,1)S(1)}) custom-call(s32[2]{0:T(128)S(1)} %copy-done.4, bf16[8192,128]{1,0:T(8,128)(2,1)} %bitcast.2.x_ref.own_ref), custom_call_target="tpu_custom_call" | custom-call | bytes 6291456 | tf_op jit(solution)/shard_map/turn_own/pallas_call | solution.py:82
  7.9 1.3 %copy-done = bf16[128,8192]{1,0:T(8,128)(2,1)} copy-done((bf16[128,8192]{1,0:T(8,128)(2,1)}, bf16[128,8192]{1,0:T(8,128)(2,1)S(1)}, u32[]{:S(2)}) %copy-start) | copy-done | bytes 2097176
  9.2 5.0 %collective-permute-start = (s32[1,4]{1,0:T(1,128)S(1)}, s32[1,4]{1,0:T(1,128)S(1)}, u32[]{:S(2)}, u32[]{:S(2)}) collective-permute-start(s32[1,4]{1,0:T(1,128)S(1)} %copy-done.6), channel_id=1, source_target_pairs={{1,9},{10,2},{3,11},{13,5},{2,1},{4,3},{17,25},{26,18},{19,27},{29... | collective-permute-start | bytes 56 | tf_op jit(solution)/shard_map/ppermute | solution.py:314
  14.2 1.3 %collective-permute-start.1 = (s32[1,4]{1,0:T(1,128)S(1)}, s32[1,4]{1,0:T(1,128)S(1)}, u32[]{:S(2)}, u32[]{:S(2)}) collective-permute-start(s32[1,4]{1,0:T(1,128)S(1)} %copy-done.6), channel_id=1, source_target_pairs={{8,0},{4,12},{6,14},{15,7},{0,1},{7,6},{24,16},{20,28},{22,30},{31... | collective-permute-start | bytes 56 | tf_op jit(solution)/shard_map/ppermute | solution.py:312
  16.2 1.3 %collective-permute-start.3 = (bf16[8192,128]{1,0:T(8,128)(2,1)}, bf16[8192,128]{1,0:T(8,128)(2,1)}, u32[]{:S(2)}, u32[]{:S(2)}) collective-permute-start(bf16[8192,128]{1,0:T(8,128)(2,1)} %bitcast.2.x_ref.own_ref), channel_id=1, source_target_pairs={{8,0},{4,12},{6,14},{15,7},{0,1},{7,6},{24,16},{20,28},{22,30},{31... | collective-permute-start | bytes 6291464 | tf_op jit(solution)/shard_map/ppermute | solution.py:306
  17.5 2.0 %collective-permute-start.4 = (bf16[8192,128]{1,0:T(8,128)(2,1)}, bf16[8192,128]{1,0:T(8,128)(2,1)}, u32[]{:S(2)}, u32[]{:S(2)}) collective-permute-start(bf16[8192,128]{1,0:T(8,128)(2,1)} %bitcast.2.x_ref.own_ref), channel_id=1, source_target_pairs={{3,2},{5,4},{6,5},{9,8},{10,9},{11,10},{12,11},{13,12},{14,13},{15... | collective-permute-start | bytes 6291464 | tf_op jit(solution)/shard_map/ppermute | solution.py:307
  19.5 4.9 %split.1 = (bf16[5120,128]{1,0:T(8,128)(2,1)S(1)}, bf16[3072,128]{1,0:T(8,128)(2,1)}) custom-call(bf16[8192,128]{1,0:T(8,128)(2,1)} %bitcast.2.x_ref.own_ref), custom_call_target="tpu_custom_call" | custom-call | bytes 4194304 | tf_op jit(solution)/shard_map/split/pallas_call | solution.py:47
  24.4 1.1 %copy-done.5 = bf16[5120,128]{1,0:T(8,128)(2,1)} copy-done((bf16[5120,128]{1,0:T(8,128)(2,1)}, bf16[5120,128]{1,0:T(8,128)(2,1)S(1)}, u32[]{:S(2)}) %copy-start.5) | copy-done | bytes 1310744
  25.6 0.9 multiply_convert_fusion
  26.6 0.9 fusion.2
  27.6 21.2 %collective-permute-start.7 = (bf16[5120,128]{1,0:T(8,128)(2,1)}, bf16[5120,128]{1,0:T(8,128)(2,1)}, u32[]{:S(2)}, u32[]{:S(2)}) collective-permute-start(bf16[5120,128]{1,0:T(8,128)(2,1)} %copy-done.5), channel_id=1, source_target_pairs={{1,9},{10,2},{3,11},{13,5},{2,1},{4,3},{17,25},{26,18},{19,27},{29... | collective-permute-start | bytes 3932168 | tf_op jit(solution)/shard_map/ppermute | solution.py:324
  48.9 1.6 %turn_first.1 = (bf16[128,8192]{1,0:T(8,128)(2,1)S(1)}, bf16[128,8192]{1,0:T(8,128)(2,1)S(1)}) custom-call(s32[2]{0:T(128)S(1)} %add_convert_fusion.2.active_ref, bf16[8192,128]{1,0:T(8,128)(2,1)} %collective-permute-done.3.x_ref.first_ref), custom_call_target="tpu_custom_call" | custom-call | tf_op jit(solution)/shard_map/turn_first/pallas_call | solution.py:82
  50.5 11.6 %first_sums.1 = (bf16[9,128,128]{2,1,0:T(8,128)(2,1)S(1)}, bf16[9,128,128]{2,1,0:T(8,128)(2,1)S(1)}, bf16[9,128,128]{2,1,0:T(8,128)(2,1)}) custom-call(s32[10]{0:T(128)S(1)} %pad_add_fusion.1.switch_ref, bf16[128,8192]{1,0:T(8,128)(2,1)S(1)} %get-tuple-element.33.plain_ref, bf16[128,8192]{1,0:T(8,128)(2,1)S(1)} %copy-done.1, ...), custom_call_target="tpu_custom_call" | custom-call | flops 4831838208 | bytes 8388608 | tf_op jit(solution)/shard_map/first_sums/pallas_call | solution.py:177
  62.1 0.7 copy-done.3
  62.8 1.9 %collective-permute-start.6 = (bf16[3072,128]{1,0:T(8,128)(2,1)}, bf16[3072,128]{1,0:T(8,128)(2,1)S(1)}, u32[]{:S(2)}, u32[]{:S(2)}) collective-permute-start(bf16[3072,128]{1,0:T(8,128)(2,1)} %get-tuple-element.44), channel_id=1, source_target_pairs={{1,9},{10,2},{3,11},{13,5},{2,1},{4,3},{17,25},{26,18},{19,27},{29... | collective-permute-start | bytes 2359304 | tf_op jit(solution)/shard_map/ppermute | solution.py:328
  64.7 8.7 %collective-permute-start.5 = (bf16[9,128,128]{2,1,0:T(8,128)(2,1)}, bf16[9,128,128]{2,1,0:T(8,128)(2,1)}, u32[]{:S(2)}, u32[]{:S(2)}) collective-permute-start(bf16[9,128,128]{2,1,0:T(8,128)(2,1)} %get-tuple-element.40), channel_id=1, source_target_pairs={{0,8},{12,4},{14,6},{7,15},{1,0},{16,24},{28,20},{30,22},{23,31},{... | collective-permute-start | bytes 884744 | tf_op jit(solution)/shard_map/ppermute | solution.py:329
  73.4 1.4 %collective-permute-start.8 = (bf16[9,128,128]{2,1,0:T(8,128)(2,1)S(1)}, bf16[9,128,128]{2,1,0:T(8,128)(2,1)}, u32[]{:S(2)}, u32[]{:S(2)}) collective-permute-start(bf16[9,128,128]{2,1,0:T(8,128)(2,1)S(1)} %get-tuple-element.48), channel_id=1, source_target_pairs={{0,7},{7,15},{16,23},{23,31}} | collective-permute-start | bytes 884744 | tf_op jit(solution)/shard_map/ppermute | solution.py:330
  75.0 1.1 %broadcast_select_fusion = (bf16[9,128,128]{2,1,0:T(8,128)(2,1)S(1)}, bf16[9,128,128]{2,1,0:T(8,128)(2,1)S(1)}) fusion(bf16[9,128,128]{2,1,0:T(8,128)(2,1)} %collective-permute-done.5, bf16[9,128,128]{2,1,0:T(8,128)(2,1)} %copy-done.3, pred[]{:T(512)S(6)} %or.52, bf16[9,128,128]{2,1,0:T(8,128)(2,1)} %collective-permute-done.8, ...), kind=kLoop, calls=%fused_computation.2 | loop fusion | flops 589824 | bytes 1769476 | tf_op jit(solution)/shard_map/jit(_where)/select_n | solution.py:336
  76.1 1.6 %copy-done.2 = bf16[128,8192]{1,0:T(8,128)(2,1)S(1)} copy-done((bf16[128,8192]{1,0:T(8,128)(2,1)S(1)}, bf16[128,8192]{1,0:T(8,128)(2,1)}, u32[]{:S(2)}) %copy-start.2) | copy-done | bytes 2097176
  77.7 6.0 %second_part.1.rest_0_ = f32[1152,128]{1,0:T(8,128)S(1)} custom-call(s32[6]{0:T(128)S(1)} %pad_add_fusion.switch_ref, bf16[128,8192]{1,0:T(8,128)(2,1)S(1)} %get-tuple-element.33.plain_ref, bf16[128,8192]{1,0:T(8,128)(2,1)S(1)} %copy-done.2, bf16[9,8192]{1,0:T(8,128)(2,1)S(1)} %pad_maximum_fusion.coeff_ref, bf16[5120,128]{1,0:T(8,128)(2,1)} %collective-permute-done.7.partner_ref), custom_call_target="tpu_custom_call" | custom-call | flops 1509949440 | bytes 3932160 | tf_op jit(solution)/shard_map/second_part/pallas_call | solution.py:255
  83.7 4.1 %second_last.1 = (bf16[9,128,128]{2,1,0:T(8,128)(2,1)}, bf16[9,128,128]{2,1,0:T(8,128)(2,1)S(1)}, bf16[9,128,128]{2,1,0:T(8,128)(2,1)}) custom-call(s32[6]{0:T(128)S(1)} %pad_add_fusion.switch_ref, bf16[128,8192]{1,0:T(8,128)(2,1)S(1)} %get-tuple-element.33.plain_ref, bf16[128,8192]{1,0:T(8,128)(2,1)S(1)} %copy-done.2, ...), custom_call_target="tpu_custom_call" | custom-call | flops 905969664 | bytes 2359296 | tf_op jit(solution)/shard_map/second_last/pallas_call | solution.py:255
  87.8 1.3 %collective-permute-start.9 = (bf16[9,128,128]{2,1,0:T(8,128)(2,1)}, bf16[9,128,128]{2,1,0:T(8,128)(2,1)S(1)}, u32[]{:S(2)}, u32[]{:S(2)}) collective-permute-start(bf16[9,128,128]{2,1,0:T(8,128)(2,1)} %get-tuple-element.50), channel_id=1, source_target_pairs={{9,1},{2,10},{11,3},{5,13},{25,17},{18,26},{27,19},{21,29}} | collective-permute-start | bytes 884744 | tf_op jit(solution)/shard_map/ppermute | solution.py:340
  89.1 7.3 %collective-permute-done.9 = bf16[9,128,128]{2,1,0:T(8,128)(2,1)S(1)} collective-permute-done((bf16[9,128,128]{2,1,0:T(8,128)(2,1)}, bf16[9,128,128]{2,1,0:T(8,128)(2,1)S(1)}, u32[]{:S(2)}, u32[]{:S(2)}) %collective-permute-start.9) | collective-permute-done | bytes 294944 | tf_op jit(solution)/shard_map/ppermute | solution.py:340
  96.4 0.7 select_bitcast_fusion
  (30 shorter events, 1.9 us)
Async XLA Ops:
  0.6 8.6 %copy-start.6 = (s32[1,4]{1,0:T(1,128)S(1)}, s32[1,4]{1,0:T(1,128)}, u32[]{:S(2)}) copy-start(s32[1,4]{1,0:T(1,128)} %param.3) | copy-start | bytes 52
  0.6 0.7 copy-start.4
  7.8 1.3 %copy-start = (bf16[128,8192]{1,0:T(8,128)(2,1)}, bf16[128,8192]{1,0:T(8,128)(2,1)S(1)}, u32[]{:S(2)}) copy-start(bf16[128,8192]{1,0:T(8,128)(2,1)S(1)} %get-tuple-element.34.swapped_ref) | copy-start | bytes 6291460
  9.2 39.6 %collective-permute-start = (s32[1,4]{1,0:T(1,128)S(1)}, s32[1,4]{1,0:T(1,128)S(1)}, u32[]{:S(2)}, u32[]{:S(2)}) collective-permute-start(s32[1,4]{1,0:T(1,128)S(1)} %copy-done.6), channel_id=1, source_target_pairs={{1,9},{10,2},{3,11},{13,5},{2,1},{4,3},{17,25},{26,18},{19,27},{29... | collective-permute-start | bytes 56 | tf_op jit(solution)/shard_map/ppermute | solution.py:314
  14.2 34.5 %collective-permute-start.1 = (s32[1,4]{1,0:T(1,128)S(1)}, s32[1,4]{1,0:T(1,128)S(1)}, u32[]{:S(2)}, u32[]{:S(2)}) collective-permute-start(s32[1,4]{1,0:T(1,128)S(1)} %copy-done.6), channel_id=1, source_target_pairs={{8,0},{4,12},{6,14},{15,7},{0,1},{7,6},{24,16},{20,28},{22,30},{31... | collective-permute-start | bytes 56 | tf_op jit(solution)/shard_map/ppermute | solution.py:312
  15.5 33.3 %collective-permute-start.2 = (s32[1,4]{1,0:T(1,128)S(1)}, s32[1,4]{1,0:T(1,128)S(1)}, u32[]{:S(2)}, u32[]{:S(2)}) collective-permute-start(s32[1,4]{1,0:T(1,128)S(1)} %copy-done.6), channel_id=1, source_target_pairs={{3,2},{5,4},{6,5},{9,8},{10,9},{11,10},{12,11},{13,12},{14,13},{15... | collective-permute-start | bytes 56 | tf_op jit(solution)/shard_map/ppermute | solution.py:313
  16.2 11.4 %collective-permute-start.3 = (bf16[8192,128]{1,0:T(8,128)(2,1)}, bf16[8192,128]{1,0:T(8,128)(2,1)}, u32[]{:S(2)}, u32[]{:S(2)}) collective-permute-start(bf16[8192,128]{1,0:T(8,128)(2,1)} %bitcast.2.x_ref.own_ref), channel_id=1, source_target_pairs={{8,0},{4,12},{6,14},{15,7},{0,1},{7,6},{24,16},{20,28},{22,30},{31... | collective-permute-start | bytes 6291464 | tf_op jit(solution)/shard_map/ppermute | solution.py:306
  17.5 10.1 %collective-permute-start.4 = (bf16[8192,128]{1,0:T(8,128)(2,1)}, bf16[8192,128]{1,0:T(8,128)(2,1)}, u32[]{:S(2)}, u32[]{:S(2)}) collective-permute-start(bf16[8192,128]{1,0:T(8,128)(2,1)} %bitcast.2.x_ref.own_ref), channel_id=1, source_target_pairs={{3,2},{5,4},{6,5},{9,8},{10,9},{11,10},{12,11},{13,12},{14,13},{15... | collective-permute-start | bytes 6291464 | tf_op jit(solution)/shard_map/ppermute | solution.py:307
  24.4 1.1 %copy-start.5 = (bf16[5120,128]{1,0:T(8,128)(2,1)}, bf16[5120,128]{1,0:T(8,128)(2,1)S(1)}, u32[]{:S(2)}) copy-start(bf16[5120,128]{1,0:T(8,128)(2,1)S(1)} %get-tuple-element.45) | copy-start | bytes 3932164
  25.5 25.0 %copy-start.1 = (bf16[128,8192]{1,0:T(8,128)(2,1)S(1)}, bf16[128,8192]{1,0:T(8,128)(2,1)}, u32[]{:S(2)}) copy-start(bf16[128,8192]{1,0:T(8,128)(2,1)} %copy-done) | copy-start | bytes 6291460
  27.6 48.5 %collective-permute-start.7 = (bf16[5120,128]{1,0:T(8,128)(2,1)}, bf16[5120,128]{1,0:T(8,128)(2,1)}, u32[]{:S(2)}, u32[]{:S(2)}) collective-permute-start(bf16[5120,128]{1,0:T(8,128)(2,1)} %copy-done.5), channel_id=1, source_target_pairs={{1,9},{10,2},{3,11},{13,5},{2,1},{4,3},{17,25},{26,18},{19,27},{29... | collective-permute-start | bytes 3932168 | tf_op jit(solution)/shard_map/ppermute | solution.py:324
  62.1 0.7 copy-start.3
  62.8 20.9 %collective-permute-start.6 = (bf16[3072,128]{1,0:T(8,128)(2,1)}, bf16[3072,128]{1,0:T(8,128)(2,1)S(1)}, u32[]{:S(2)}, u32[]{:S(2)}) collective-permute-start(bf16[3072,128]{1,0:T(8,128)(2,1)} %get-tuple-element.44), channel_id=1, source_target_pairs={{1,9},{10,2},{3,11},{13,5},{2,1},{4,3},{17,25},{26,18},{19,27},{29... | collective-permute-start | bytes 2359304 | tf_op jit(solution)/shard_map/ppermute | solution.py:328
  64.7 10.2 %collective-permute-start.5 = (bf16[9,128,128]{2,1,0:T(8,128)(2,1)}, bf16[9,128,128]{2,1,0:T(8,128)(2,1)}, u32[]{:S(2)}, u32[]{:S(2)}) collective-permute-start(bf16[9,128,128]{2,1,0:T(8,128)(2,1)} %get-tuple-element.40), channel_id=1, source_target_pairs={{0,8},{12,4},{14,6},{7,15},{1,0},{16,24},{28,20},{30,22},{23,31},{... | collective-permute-start | bytes 884744 | tf_op jit(solution)/shard_map/ppermute | solution.py:329
  73.4 1.5 %collective-permute-start.8 = (bf16[9,128,128]{2,1,0:T(8,128)(2,1)S(1)}, bf16[9,128,128]{2,1,0:T(8,128)(2,1)}, u32[]{:S(2)}, u32[]{:S(2)}) collective-permute-start(bf16[9,128,128]{2,1,0:T(8,128)(2,1)S(1)} %get-tuple-element.48), channel_id=1, source_target_pairs={{0,7},{7,15},{16,23},{23,31}} | collective-permute-start | bytes 884744 | tf_op jit(solution)/shard_map/ppermute | solution.py:330
  76.1 1.6 %copy-start.2 = (bf16[128,8192]{1,0:T(8,128)(2,1)S(1)}, bf16[128,8192]{1,0:T(8,128)(2,1)}, u32[]{:S(2)}) copy-start(bf16[128,8192]{1,0:T(8,128)(2,1)} %copy-done) | copy-start | bytes 6291460
  87.8 8.6 %collective-permute-start.9 = (bf16[9,128,128]{2,1,0:T(8,128)(2,1)}, bf16[9,128,128]{2,1,0:T(8,128)(2,1)S(1)}, u32[]{:S(2)}, u32[]{:S(2)}) collective-permute-start(bf16[9,128,128]{2,1,0:T(8,128)(2,1)} %get-tuple-element.50), channel_id=1, source_target_pairs={{9,1},{2,10},{11,3},{5,13},{25,17},{18,26},{27,19},{21,29}} | collective-permute-start | bytes 884744 | tf_op jit(solution)/shard_map/ppermute | solution.py:340

commit v9 on v8

--- a/solution.py
+++ b/solution.py
@@ -115,12 +115,12 @@
         scaled[k * cols:(k + 1) * cols, :] = part * coeff_ref[k:k + 1, :]
 
 
-def weigh(x, switch_ref, begin, windows):
+def weigh(x, window_weights):
     rows, cols = x.shape
-    window = lax.broadcasted_iota(jnp.int32, (16, cols), 0) % windows
+    window = lax.broadcasted_iota(jnp.int32, (16, cols), 0) % len(window_weights)
     weights = jnp.zeros((16, cols), jnp.float32)
-    for w in range(windows):
-        weights = jnp.where(window == w, switch_ref[begin + w].astype(jnp.float32), weights)
+    for w, weight in enumerate(window_weights):
+        weights = jnp.where(window == w, weight.astype(jnp.float32), weights)
     weights = jnp.broadcast_to(weights.astype(jnp.bfloat16)[None], (rows // 16, 16, cols))
     return x * weights.reshape(rows, cols)
 
@@ -135,16 +135,13 @@
     def _():
         acc[...] = jnp.zeros_like(acc)
 
-    @pl.when(special == 0)
-    def _():
-        scale(scaled, plain_ref[...], swapped_ref[...], coeff_ref)
-
-    @pl.when(special != 0)
-    def _():
-        scale(scaled, plain_alt[...], swapped_alt[...], coeff_ref)
-
-    near = weigh(near_ref[...], switch_ref, 2, windows)
-    far = weigh(jnp.where(special != 0, own_ref[...], first_ref[...]), switch_ref, 2 + windows, windows)
+    plain = jnp.where(special != 0, plain_alt[...], plain_ref[...])
+    swapped = jnp.where(special != 0, swapped_alt[...], swapped_ref[...])
+    scale(scaled, plain, swapped, coeff_ref)
+    flags = [[switch_ref[2 + part * windows + w] for w in range(windows)] for part in range(3)]
+    near_weights = [jnp.where(special != 0, first, own) * near for own, near, first in zip(*flags)]
+    near = weigh(near_ref[...], near_weights)
+    far = weigh(jnp.where(special != 0, own_ref[...], first_ref[...]), [own * first for own, _, first in zip(*flags)])
     acc[...] += jnp.dot(scaled[...], jnp.concatenate([near, far], axis=1), preferred_element_type=jnp.float32)
 
     @pl.when(step == pl.num_programs(0) - 1)
@@ -167,7 +164,7 @@
 
 def first_sums(switch, own, alt, coeffs, near_in, first_in, block):
     rows, cols = block.shape
-    windows = (switch.shape[0] - 2) // 2
+    windows = (switch.shape[0] - 2) // 3
     result = jax.ShapeDtypeStruct((LAGS, cols, cols), jnp.bfloat16)
     left = pl.BlockSpec((cols, STEP), lambda s, on: (0, s * (1 - on[1])))
     left_alt = pl.BlockSpec((cols, STEP), lambda s, on: (0, s * on[1]))
@@ -210,7 +207,7 @@
             acc[...] = jnp.zeros_like(acc) if first else acc_in[...]
 
         scale(scaled, plain_ref[...], swapped_ref[...], coeff_ref)
-        partner = weigh(partner_ref[...], switch_ref, 2, windows)
+        partner = weigh(partner_ref[...], [switch_ref[2 + w] for w in range(windows)])
         acc[...] += jnp.dot(scaled[...], partner, preferred_element_type=jnp.float32)
 
     if not first:
@@ -308,16 +305,13 @@
     coeffs = lag_rows(freq_count, window_count)
     own = turn(block, switch(True, False), "turn_own")
     parts = split(block)
-    sent_flags, own = lax.optimization_barrier((quality, own))
-    first_flags = lax.ppermute(sent_flags, "chan", first_pairs)[0]
-    near_flags = lax.ppermute(sent_flags, "chan", near_pairs)[0]
-    second_flags = lax.ppermute(sent_flags, "chan", second_pairs)[0]
+    first_flags = lax.ppermute(quality, "chan", first_pairs)[0]
+    near_flags = lax.ppermute(quality, "chan", near_pairs)[0]
+    second_flags = lax.ppermute(quality, "chan", second_pairs)[0]
     special = among([0, half - 1])
-    usual_flags = quality[0]
-    left_flags = jnp.where(special, first_flags, usual_flags)
-    first_switch = switch(me == 0, special, left_flags * near_flags, usual_flags * first_flags)
+    first_switch = switch(me == 0, special, quality[0], near_flags, first_flags)
     second_switch = switch(
-        among([t for _, t in second_pairs]), among([t for _, t in late_near]), usual_flags * second_flags
+        among([t for _, t in second_pairs]), among([t for _, t in late_near]), quality[0] * second_flags
     )
 
     late_part, own, coeffs, first_in, near_in = lax.optimization_barrier((parts[0], own, coeffs, first_in, near_in))

time: 97.9 us -> 84.9 us (0.87)
  starting transfers between devices: 44.7 us -> 35.2 us
  Pallas kernels: 34.7 us -> 26.9 us
  local copies, waits for them, and re-layouts: 5.34 us -> 8.58 us
  waiting for transfers between devices: 7.28 us -> 8.56 us
    ppermute x1, starting transfers between devices: 21.2 us -> 10.2 us  [local(): second_first = lax.ppermute(late_part, 'chan', second_pairs)]
    unnamed x14 -> x22, local copies, waits for them, and re-layouts: 5.34 us -> 8.58 us
    pallas_call x1, Pallas kernels: 4.87 us -> 1.68 us  [split(): pl.pallas_call(functools.partial(split_kernel, middle), grid=(steps,), in...]
    pallas_call x2, Pallas kernels: 8.11 us -> 5.52 us  [turn(): pl.pallas_call(turn_kernel, grid_spec=pltpu.PrefetchScalarGridSpec(num_sc...]
    ppermute x3, starting transfers between devices: 7 us -> 9.49 us  [the longest x1 7.54 us: local(): second_flags = lax.ppermute(quality, 'chan', second_pairs)[0]]
    pallas_call x1, Pallas kernels: 11.6 us -> 9.56 us  [first_sums(): pl.pallas_call(functools.partial(first_kernel, windows), grid_spec=pltpu....]
    ppermute x1, waiting for transfers between devices: 0.01 us -> 1.28 us  [local(): first_returned = lax.ppermute(back, 'chan', first_back)]
  transfers between devices with their start and end apart: 10 -> 10, of which waited for: 1 -> 2; matrix products, arithmetic and copies ran while one was open for 4% -> 4% of each run, Pallas kernels for 25% -> 27%
where the time goes in v9:
time: 84.9 us; the launch traced here: 84.2 us
  starting transfers between devices  35.2 us (41%)
  Pallas kernels  26.9 us (32%)
  local copies, waits for them, and re-layouts  8.58 us (10%)
  waiting for transfers between devices  8.56 us (10%)
  other arithmetic  4.09 us (5%)
  between operations  0.93 us (1%)
    ppermute x1, starting transfers between devices, local(): second_first = lax.ppermute(late_part, 'chan', second_pairs)  10.2 us
    pallas_call x2, Pallas kernels, second_sums(): pl.pallas_call(functools.partial(second_kernel, windows, not earlier), gr...  10.1 us
    pallas_call x1, Pallas kernels, first_sums(): pl.pallas_call(functools.partial(first_kernel, windows), grid_spec=pltpu....  9.56 us
    unnamed x22, local copies, waits for them, and re-layouts  8.58 us
    ppermute x1, starting transfers between devices, local(): first_returned = lax.ppermute(back, 'chan', first_back)  8.33 us
    ppermute x1, starting transfers between devices, local(): second_flags = lax.ppermute(quality, 'chan', second_pairs)[0]  7.54 us
    ppermute x1, waiting for transfers between devices, local(): second_returned = lax.ppermute(back, 'chan', second_back)  7.26 us
    pallas_call x2, Pallas kernels, turn(): pl.pallas_call(turn_kernel, grid_spec=pltpu.PrefetchScalarGridSpec(num_sc...  5.52 us
  transfers between devices with their start and end apart: 10, of which 2 were waited for; matrix products, arithmetic and copies ran while one was open for 4% of the time, Pallas kernels for 27%

profile of v9, /device:TPU:1, one launch (start us, length us, event | category | flops | bytes accessed | tf_op | source)
XLA Modules:
  0.0 84.2 jit_solution(17339409939472338340)
XLA Ops:
  0.6 1.3 %collective-permute-start.3 = (bf16[8192,128]{1,0:T(8,128)(2,1)}, bf16[8192,128]{1,0:T(8,128)(2,1)}, u32[]{:S(2)}, u32[]{:S(2)}) collective-permute-start(bf16[8192,128]{1,0:T(8,128)(2,1)} %bitcast.14), channel_id=1, source_target_pairs={{8,0},{4,12},{6,14},{15,7},{0,1},{7,6},{24,16},{20,28},{22,30},{31... | collective-permute-start | bytes 6291464 | tf_op jit(solution)/shard_map/ppermute | solution.py:303
  1.9 2.0 %collective-permute-start.4 = (bf16[8192,128]{1,0:T(8,128)(2,1)}, bf16[8192,128]{1,0:T(8,128)(2,1)}, u32[]{:S(2)}, u32[]{:S(2)}) collective-permute-start(bf16[8192,128]{1,0:T(8,128)(2,1)} %bitcast.15), channel_id=1, source_target_pairs={{3,2},{5,4},{6,5},{9,8},{10,9},{11,10},{12,11},{13,12},{14,13},{15... | collective-permute-start | bytes 6291464 | tf_op jit(solution)/shard_map/ppermute | solution.py:304
  4.6 1.3 %collective-permute-start.2 = (s32[1,4]{1,0:T(1,128)}, s32[1,4]{1,0:T(1,128)S(1)}, u32[]{:S(2)}, u32[]{:S(2)}) collective-permute-start(s32[1,4]{1,0:T(1,128)} %param.3), channel_id=1, source_target_pairs={{8,0},{4,12},{6,14},{15,7},{0,1},{7,6},{24,16},{20,28},{22,30},{31... | collective-permute-start | bytes 56 | tf_op jit(solution)/shard_map/ppermute | solution.py:308
  5.9 7.5 %collective-permute-start = (s32[1,4]{1,0:T(1,128)}, s32[1,4]{1,0:T(1,128)S(1)}, u32[]{:S(2)}, u32[]{:S(2)}) collective-permute-start(s32[1,4]{1,0:T(1,128)} %param.3), channel_id=1, source_target_pairs={{1,9},{10,2},{3,11},{13,5},{2,1},{4,3},{17,25},{26,18},{19,27},{29... | collective-permute-start | bytes 56 | tf_op jit(solution)/shard_map/ppermute | solution.py:310
  13.5 1.6 %copy-done.3 = bf16[1024,2,4,128]{3,2,1,0:T(4,128)(2,1)S(1)} copy-done((bf16[1024,2,4,128]{3,2,1,0:T(4,128)(2,1)S(1)}, bf16[1024,2,4,128]{3,2,1,0:T(4,128)(2,1)}, u32[]{:S(2)}) %copy-start.3) | copy-done | bytes 2097176
  15.1 1.7 %split.1 = (bf16[5120,128]{1,0:T(8,128)(2,1)S(1)}, bf16[3072,128]{1,0:T(8,128)(2,1)}) custom-call(bf16[8192,128]{1,0:T(8,128)(2,1)S(1)} %bitcast.16), custom_call_target="tpu_custom_call" | custom-call | bytes 4194304 | tf_op jit(solution)/shard_map/split/pallas_call | solution.py:47
  16.8 1.1 %copy-done.8 = bf16[5120,128]{1,0:T(8,128)(2,1)} copy-done((bf16[5120,128]{1,0:T(8,128)(2,1)}, bf16[5120,128]{1,0:T(8,128)(2,1)S(1)}, u32[]{:S(2)}) %copy-start.8) | copy-done | bytes 1310744
  17.9 3.9 %turn_own.1 = (bf16[128,8192]{1,0:T(8,128)(2,1)S(1)}, bf16[128,8192]{1,0:T(8,128)(2,1)S(1)}) custom-call(s32[2]{0:T(128)S(1)} %copy-done.7, bf16[8192,128]{1,0:T(8,128)(2,1)S(1)} %bitcast.17), custom_call_target="tpu_custom_call" | custom-call | bytes 6291456 | tf_op jit(solution)/shard_map/turn_own/pallas_call | solution.py:82
  21.8 1.3 %copy-done = bf16[128,8192]{1,0:T(8,128)(2,1)} copy-done((bf16[128,8192]{1,0:T(8,128)(2,1)}, bf16[128,8192]{1,0:T(8,128)(2,1)S(1)}, u32[]{:S(2)}) %copy-start) | copy-done | bytes 2097176
  23.2 0.9 %multiply_convert_fusion = (bf16[5,8192]{1,0:T(8,128)(2,1)S(1)}, f32[5,8192]{1,0:T(8,128)S(1)}) fusion(f32[8192]{0:T(1024)S(1)} %fusion.9, f32[5]{0:T(128)S(1)} %iota_multiply_fusion), kind=kLoop, calls=%fused_computation.4 | loop fusion | flops 122880 | bytes 278548 | tf_op jit(solution)/shard_map/convert
  24.2 0.9 %fusion.2 = bf16[4,8192]{1,0:T(4,128)(2,1)S(1)} fusion(f32[5,8192]{1,0:T(8,128)S(1)} %get-tuple-element.49, f32[8192]{0:T(1024)S(1)} %select_multiply_fusion), kind=kLoop, calls=%fused_computation.8 | loop fusion | flops 98304 | bytes 229376 | tf_op jit(solution)/shard_map/convert.1
  25.2 10.2 %collective-permute-start.7 = (bf16[5120,128]{1,0:T(8,128)(2,1)}, bf16[5120,128]{1,0:T(8,128)(2,1)}, u32[]{:S(2)}, u32[]{:S(2)}) collective-permute-start(bf16[5120,128]{1,0:T(8,128)(2,1)} %copy-done.8), channel_id=1, source_target_pairs={{1,9},{10,2},{3,11},{13,5},{2,1},{4,3},{17,25},{26,18},{19,27},{29... | collective-permute-start | bytes 3932168 | tf_op jit(solution)/shard_map/ppermute | solution.py:318
  35.6 1.6 %turn_first.1 = (bf16[128,8192]{1,0:T(8,128)(2,1)S(1)}, bf16[128,8192]{1,0:T(8,128)(2,1)S(1)}) custom-call(s32[2]{0:T(128)S(1)} %add_convert_fusion.2.active_ref, bf16[8192,128]{1,0:T(8,128)(2,1)} %collective-permute-done.3.x_ref.first_ref), custom_call_target="tpu_custom_call" | custom-call | tf_op jit(solution)/shard_map/turn_first/pallas_call | solution.py:82
  37.2 1.6 %copy-done.5 = bf16[1024,2,4,128]{3,2,1,0:T(4,128)(2,1)S(1)} copy-done((bf16[1024,2,4,128]{3,2,1,0:T(4,128)(2,1)S(1)}, bf16[1024,2,4,128]{3,2,1,0:T(4,128)(2,1)}, u32[]{:S(2)}) %copy-start.5) | copy-done | bytes 2097176
  38.7 9.6 %first_sums.1 = (bf16[9,128,128]{2,1,0:T(8,128)(2,1)S(1)}, bf16[9,128,128]{2,1,0:T(8,128)(2,1)S(1)}, bf16[9,128,128]{2,1,0:T(8,128)(2,1)S(1)}) custom-call(s32[14]{0:T(128)S(1)} %pad_add_fusion.1.switch_ref, bf16[128,8192]{1,0:T(8,128)(2,1)S(1)} %get-tuple-element.27.plain_ref, bf16[128,8192]{1,0:T(8,128)(2,1)S(1)} %copy-done.1, ...), custom_call_target="tpu_custom_call" | custom-call | flops 4831838208 | bytes 8388608 | tf_op jit(solution)/shard_map/first_sums/pallas_call | solution.py:174
  49.7 1.9 %collective-permute-start.6 = (bf16[3072,128]{1,0:T(8,128)(2,1)}, bf16[3072,128]{1,0:T(8,128)(2,1)S(1)}, u32[]{:S(2)}, u32[]{:S(2)}) collective-permute-start(bf16[3072,128]{1,0:T(8,128)(2,1)} %get-tuple-element.38), channel_id=1, source_target_pairs={{1,9},{10,2},{3,11},{13,5},{2,1},{4,3},{17,25},{26,18},{19,27},{29... | collective-permute-start | bytes 2359304 | tf_op jit(solution)/shard_map/ppermute | solution.py:322
  52.4 8.3 %collective-permute-start.5 = (bf16[9,128,128]{2,1,0:T(8,128)(2,1)}, bf16[9,128,128]{2,1,0:T(8,128)(2,1)S(1)}, u32[]{:S(2)}, u32[]{:S(2)}) collective-permute-start(bf16[9,128,128]{2,1,0:T(8,128)(2,1)} %copy-done.9), channel_id=1, source_target_pairs={{0,8},{12,4},{14,6},{7,15},{1,0},{16,24},{28,20},{30,22},{23,31},{... | collective-permute-start | bytes 884744 | tf_op jit(solution)/shard_map/ppermute | solution.py:323
  60.9 1.3 %collective-permute-done.5 = bf16[9,128,128]{2,1,0:T(8,128)(2,1)S(1)} collective-permute-done((bf16[9,128,128]{2,1,0:T(8,128)(2,1)}, bf16[9,128,128]{2,1,0:T(8,128)(2,1)S(1)}, u32[]{:S(2)}, u32[]{:S(2)}) %collective-permute-start.5) | collective-permute-done | bytes 294944 | tf_op jit(solution)/shard_map/ppermute | solution.py:323
  62.1 1.0 %broadcast_select_fusion = (bf16[9,128,128]{2,1,0:T(8,128)(2,1)S(1)}, bf16[9,128,128]{2,1,0:T(8,128)(2,1)S(1)}) fusion(bf16[9,128,128]{2,1,0:T(8,128)(2,1)S(1)} %collective-permute-done.5, bf16[9,128,128]{2,1,0:T(8,128)(2,1)} %copy-done.6, pred[]{:T(512)S(6)} %or.52, bf16[9,128,128]{2,1,0:T(8,128)(2,1)S(1)} %collective-permute-done.8, ...), kind=kLoop, calls=%fused_computation.2 | loop fusion | flops 589824 | bytes 1769476 | tf_op jit(solution)/shard_map/jit(_where)/select_n | solution.py:330
  63.2 1.6 %copy-done.2 = bf16[128,8192]{1,0:T(8,128)(2,1)S(1)} copy-done((bf16[128,8192]{1,0:T(8,128)(2,1)S(1)}, bf16[128,8192]{1,0:T(8,128)(2,1)}, u32[]{:S(2)}) %copy-start.2) | copy-done | bytes 2097176
  64.8 6.0 %second_part.1.rest_0_ = f32[1152,128]{1,0:T(8,128)S(1)} custom-call(s32[6]{0:T(128)S(1)} %pad_add_fusion.switch_ref, bf16[128,8192]{1,0:T(8,128)(2,1)S(1)} %get-tuple-element.27.plain_ref, bf16[128,8192]{1,0:T(8,128)(2,1)S(1)} %copy-done.2, bf16[9,8192]{1,0:T(8,128)(2,1)S(1)} %pad_maximum_fusion.coeff_ref, bf16[5120,128]{1,0:T(8,128)(2,1)} %collective-permute-done.7.partner_ref), custom_call_target="tpu_custom_call" | custom-call | flops 1509949440 | bytes 3932160 | tf_op jit(solution)/shard_map/second_part/pallas_call | solution.py:252
  70.8 4.1 %second_last.1 = (bf16[9,128,128]{2,1,0:T(8,128)(2,1)}, bf16[9,128,128]{2,1,0:T(8,128)(2,1)S(1)}, bf16[9,128,128]{2,1,0:T(8,128)(2,1)}) custom-call(s32[6]{0:T(128)S(1)} %pad_add_fusion.switch_ref, bf16[128,8192]{1,0:T(8,128)(2,1)S(1)} %get-tuple-element.27.plain_ref, bf16[128,8192]{1,0:T(8,128)(2,1)S(1)} %copy-done.2, ...), custom_call_target="tpu_custom_call" | custom-call | flops 905969664 | bytes 2359296 | tf_op jit(solution)/shard_map/second_last/pallas_call | solution.py:252
  74.9 1.3 %collective-permute-start.9 = (bf16[9,128,128]{2,1,0:T(8,128)(2,1)}, bf16[9,128,128]{2,1,0:T(8,128)(2,1)S(1)}, u32[]{:S(2)}, u32[]{:S(2)}) collective-permute-start(bf16[9,128,128]{2,1,0:T(8,128)(2,1)} %get-tuple-element.44), channel_id=1, source_target_pairs={{9,1},{2,10},{11,3},{5,13},{25,17},{18,26},{27,19},{21,29}} | collective-permute-start | bytes 884744 | tf_op jit(solution)/shard_map/ppermute | solution.py:334
  76.2 7.3 %collective-permute-done.9 = bf16[9,128,128]{2,1,0:T(8,128)(2,1)S(1)} collective-permute-done((bf16[9,128,128]{2,1,0:T(8,128)(2,1)}, bf16[9,128,128]{2,1,0:T(8,128)(2,1)S(1)}, u32[]{:S(2)}, u32[]{:S(2)}) %collective-permute-start.9) | collective-permute-done | bytes 294944 | tf_op jit(solution)/shard_map/ppermute | solution.py:334
  (38 shorter events, 4.0 us)
Async XLA Ops:
  0.6 17.2 %copy-start.7 = (s32[2]{0:T(128)S(1)}, s32[2]{0:T(128)}, u32[]{:S(2)}) copy-start(s32[2]{0:T(128)} %constant.58.clone.1.active_ref) | copy-start | bytes 28
  0.6 24.5 %collective-permute-start.3 = (bf16[8192,128]{1,0:T(8,128)(2,1)}, bf16[8192,128]{1,0:T(8,128)(2,1)}, u32[]{:S(2)}, u32[]{:S(2)}) collective-permute-start(bf16[8192,128]{1,0:T(8,128)(2,1)} %bitcast.14), channel_id=1, source_target_pairs={{8,0},{4,12},{6,14},{15,7},{0,1},{7,6},{24,16},{20,28},{22,30},{31... | collective-permute-start | bytes 6291464 | tf_op jit(solution)/shard_map/ppermute | solution.py:303
  1.9 23.2 %collective-permute-start.4 = (bf16[8192,128]{1,0:T(8,128)(2,1)}, bf16[8192,128]{1,0:T(8,128)(2,1)}, u32[]{:S(2)}, u32[]{:S(2)}) collective-permute-start(bf16[8192,128]{1,0:T(8,128)(2,1)} %bitcast.15), channel_id=1, source_target_pairs={{3,2},{5,4},{6,5},{9,8},{10,9},{11,10},{12,11},{13,12},{14,13},{15... | collective-permute-start | bytes 6291464 | tf_op jit(solution)/shard_map/ppermute | solution.py:304
  4.0 31.5 %collective-permute-start.1 = (s32[1,4]{1,0:T(1,128)}, s32[1,4]{1,0:T(1,128)S(1)}, u32[]{:S(2)}, u32[]{:S(2)}) collective-permute-start(s32[1,4]{1,0:T(1,128)} %param.3), channel_id=1, source_target_pairs={{3,2},{5,4},{6,5},{9,8},{10,9},{11,10},{12,11},{13,12},{14,13},{15... | collective-permute-start | bytes 56 | tf_op jit(solution)/shard_map/ppermute | solution.py:309
  4.6 30.8 %collective-permute-start.2 = (s32[1,4]{1,0:T(1,128)}, s32[1,4]{1,0:T(1,128)S(1)}, u32[]{:S(2)}, u32[]{:S(2)}) collective-permute-start(s32[1,4]{1,0:T(1,128)} %param.3), channel_id=1, source_target_pairs={{8,0},{4,12},{6,14},{15,7},{0,1},{7,6},{24,16},{20,28},{22,30},{31... | collective-permute-start | bytes 56 | tf_op jit(solution)/shard_map/ppermute | solution.py:308
  5.9 54.8 %collective-permute-start = (s32[1,4]{1,0:T(1,128)}, s32[1,4]{1,0:T(1,128)S(1)}, u32[]{:S(2)}, u32[]{:S(2)}) collective-permute-start(s32[1,4]{1,0:T(1,128)} %param.3), channel_id=1, source_target_pairs={{1,9},{10,2},{3,11},{13,5},{2,1},{4,3},{17,25},{26,18},{19,27},{29... | collective-permute-start | bytes 56 | tf_op jit(solution)/shard_map/ppermute | solution.py:310
  13.5 1.6 %copy-start.3 = (bf16[1024,2,4,128]{3,2,1,0:T(4,128)(2,1)S(1)}, bf16[1024,2,4,128]{3,2,1,0:T(4,128)(2,1)}, u32[]{:S(2)}) copy-start(bf16[1024,2,4,128]{3,2,1,0:T(4,128)(2,1)} %param.2) | copy-start | bytes 6291460
  15.1 2.8 %copy-start.4 = (bf16[1024,2,4,128]{3,2,1,0:T(4,128)(2,1)S(1)}, bf16[1024,2,4,128]{3,2,1,0:T(4,128)(2,1)}, u32[]{:S(2)}) copy-start(bf16[1024,2,4,128]{3,2,1,0:T(4,128)(2,1)} %param.2) | copy-start | bytes 6291460
  16.7 1.1 %copy-start.8 = (bf16[5120,128]{1,0:T(8,128)(2,1)}, bf16[5120,128]{1,0:T(8,128)(2,1)S(1)}, u32[]{:S(2)}) copy-start(bf16[5120,128]{1,0:T(8,128)(2,1)S(1)} %get-tuple-element.39) | copy-start | bytes 3932164
  17.8 17.7 %copy-start.10 = (s32[1,4]{1,0:T(1,128)S(1)}, s32[1,4]{1,0:T(1,128)}, u32[]{:S(2)}) copy-start(s32[1,4]{1,0:T(1,128)} %param.3) | copy-start | bytes 52
  21.8 1.3 %copy-start = (bf16[128,8192]{1,0:T(8,128)(2,1)}, bf16[128,8192]{1,0:T(8,128)(2,1)S(1)}, u32[]{:S(2)}) copy-start(bf16[128,8192]{1,0:T(8,128)(2,1)S(1)} %get-tuple-element.28.swapped_ref) | copy-start | bytes 6291460
  25.2 38.0 %collective-permute-start.7 = (bf16[5120,128]{1,0:T(8,128)(2,1)}, bf16[5120,128]{1,0:T(8,128)(2,1)}, u32[]{:S(2)}, u32[]{:S(2)}) collective-permute-start(bf16[5120,128]{1,0:T(8,128)(2,1)} %copy-done.8), channel_id=1, source_target_pairs={{1,9},{10,2},{3,11},{13,5},{2,1},{4,3},{17,25},{26,18},{19,27},{29... | collective-permute-start | bytes 3932168 | tf_op jit(solution)/shard_map/ppermute | solution.py:318
  35.5 1.7 %copy-start.1 = (bf16[128,8192]{1,0:T(8,128)(2,1)S(1)}, bf16[128,8192]{1,0:T(8,128)(2,1)}, u32[]{:S(2)}) copy-start(bf16[128,8192]{1,0:T(8,128)(2,1)} %copy-done) | copy-start | bytes 6291460
  37.1 1.6 %copy-start.5 = (bf16[1024,2,4,128]{3,2,1,0:T(4,128)(2,1)S(1)}, bf16[1024,2,4,128]{3,2,1,0:T(4,128)(2,1)}, u32[]{:S(2)}) copy-start(bf16[1024,2,4,128]{3,2,1,0:T(4,128)(2,1)} %param.2) | copy-start | bytes 6291460
  48.3 0.7 copy-start.6
  49.0 0.7 copy-start.9
  49.7 21.1 %collective-permute-start.6 = (bf16[3072,128]{1,0:T(8,128)(2,1)}, bf16[3072,128]{1,0:T(8,128)(2,1)S(1)}, u32[]{:S(2)}, u32[]{:S(2)}) collective-permute-start(bf16[3072,128]{1,0:T(8,128)(2,1)} %get-tuple-element.38), channel_id=1, source_target_pairs={{1,9},{10,2},{3,11},{13,5},{2,1},{4,3},{17,25},{26,18},{19,27},{29... | collective-permute-start | bytes 2359304 | tf_op jit(solution)/shard_map/ppermute | solution.py:322
  51.7 10.4 %collective-permute-start.8 = (bf16[9,128,128]{2,1,0:T(8,128)(2,1)S(1)}, bf16[9,128,128]{2,1,0:T(8,128)(2,1)S(1)}, u32[]{:S(2)}, u32[]{:S(2)}) collective-permute-start(bf16[9,128,128]{2,1,0:T(8,128)(2,1)S(1)} %get-tuple-element.42), channel_id=1, source_target_pairs={{0,7},{7,15},{16,23},{23,31}} | collective-permute-start | bytes 884744 | tf_op jit(solution)/shard_map/ppermute | solution.py:324
  52.4 9.7 %collective-permute-start.5 = (bf16[9,128,128]{2,1,0:T(8,128)(2,1)}, bf16[9,128,128]{2,1,0:T(8,128)(2,1)S(1)}, u32[]{:S(2)}, u32[]{:S(2)}) collective-permute-start(bf16[9,128,128]{2,1,0:T(8,128)(2,1)} %copy-done.9), channel_id=1, source_target_pairs={{0,8},{12,4},{14,6},{7,15},{1,0},{16,24},{28,20},{30,22},{23,31},{... | collective-permute-start | bytes 884744 | tf_op jit(solution)/shard_map/ppermute | solution.py:323
  63.2 1.6 %copy-start.2 = (bf16[128,8192]{1,0:T(8,128)(2,1)S(1)}, bf16[128,8192]{1,0:T(8,128)(2,1)}, u32[]{:S(2)}) copy-start(bf16[128,8192]{1,0:T(8,128)(2,1)} %copy-done) | copy-start | bytes 6291460
  74.9 8.6 %collective-permute-start.9 = (bf16[9,128,128]{2,1,0:T(8,128)(2,1)}, bf16[9,128,128]{2,1,0:T(8,128)(2,1)S(1)}, u32[]{:S(2)}, u32[]{:S(2)}) collective-permute-start(bf16[9,128,128]{2,1,0:T(8,128)(2,1)} %get-tuple-element.44), channel_id=1, source_target_pairs={{9,1},{2,10},{11,3},{5,13},{25,17},{18,26},{27,19},{21,29}} | collective-permute-start | bytes 884744 | tf_op jit(solution)/shard_map/ppermute | solution.py:334

commit v10 on v9

--- a/solution.py
+++ b/solution.py
@@ -12,7 +12,7 @@
 LAGS = 2 * HL + 1
 STEP = 1024
 PARTS = (5, 8)
-PARAMS = pltpu.CompilerParams(vmem_limit_bytes=16 * 1024 * 1024)
+PARAMS = pltpu.CompilerParams(vmem_limit_bytes=48 * 1024 * 1024)
 
 
 def lag_rows(freq_count, window_count):
@@ -59,8 +59,8 @@
     )(x)
 
 
-def turn_kernel(active_ref, x_ref, plain_ref, swapped_ref):
-    @pl.when(active_ref[0] != 0)
+def left_kernel(switch_ref, x_ref, coeff_ref, left_ref):
+    @pl.when(switch_ref[0] != 0)
     def _():
         rows, cols = x_ref.shape
         same = lax.broadcasted_iota(jnp.int32, (cols, cols), 0) == lax.broadcasted_iota(jnp.int32, (cols, cols), 1)
@@ -70,28 +70,32 @@
         exchange = jnp.where((source ^ 4) == target, 1.0, 0.0).astype(jnp.bfloat16)
         plain = lax.dot_general(eye, x_ref[...], (((1,), (1,)), ((), ())), preferred_element_type=jnp.float32)
         plain = plain.astype(jnp.bfloat16)
-        plain_ref[...] = plain
         for t in range(0, rows, 2 * cols):
-            swapped = jnp.dot(plain[:, t:t + 2 * cols], exchange, preferred_element_type=jnp.float32)
-            swapped_ref[:, t:t + 2 * cols] = swapped.astype(jnp.bfloat16)
-
-
-def turn(x, switch, name, common=True):
+            at = slice(t, t + 2 * cols)
+            swapped = jnp.dot(plain[:, at], exchange, preferred_element_type=jnp.float32).astype(jnp.bfloat16)
+            for k in range(LAGS):
+                part = plain[:, at] if k <= HL else swapped
+                left_ref[k * cols:(k + 1) * cols, at] = part * coeff_ref[k:k + 1, at]
+
+
+def left_factors(x, coeffs, switch, name, common=True):
     rows, cols = x.shape
-    out = jax.ShapeDtypeStruct((cols, rows), jnp.bfloat16)
     return pl.pallas_call(
-        turn_kernel,
+        left_kernel,
         grid_spec=pltpu.PrefetchScalarGridSpec(
             num_scalar_prefetch=1,
             grid=(rows // STEP,),
-            in_specs=[pl.BlockSpec((STEP, cols), lambda s, on: (s * on[0], 0))],
-            out_specs=[pl.BlockSpec((cols, STEP), lambda s, on: (0, s * on[0]))] * 2,
-        ),
-        out_shape=[out, out],
+            in_specs=[pl.BlockSpec((STEP, cols), lambda s, on: (s * on[0], 0)),
+                      pl.BlockSpec((LAGS, STEP), lambda s, on: (0, s * on[0]))],
+            out_specs=pl.BlockSpec((LAGS * cols, STEP), lambda s, on: (0, s * on[0])),
+        ),
+        out_shape=jax.ShapeDtypeStruct((LAGS * cols, rows), jnp.bfloat16),
         compiler_params=PARAMS,
-        cost_estimate=pl.CostEstimate(flops=0, bytes_accessed=6 * rows * cols if common else 0, transcendentals=0),
+        cost_estimate=pl.CostEstimate(
+            flops=0, bytes_accessed=2 * (LAGS + 1) * rows * cols if common else 0, transcendentals=0
+        ),
         name=name,
-    )(switch, x)
+    )(switch, x, coeffs)
 
 
 def write_lags(out, acc, at, cols, mirrored):
@@ -108,13 +112,6 @@
             out[lag] = value
 
 
-def scale(scaled, plain, swapped, coeff_ref):
-    cols = plain.shape[0]
-    for k in range(LAGS):
-        part = plain if k <= HL else swapped
-        scaled[k * cols:(k + 1) * cols, :] = part * coeff_ref[k:k + 1, :]
-
-
 def weigh(x, window_weights):
     rows, cols = x.shape
     window = lax.broadcasted_iota(jnp.int32, (16, cols), 0) % len(window_weights)
@@ -125,24 +122,28 @@
     return x * weights.reshape(rows, cols)
 
 
-def first_kernel(windows, switch_ref, plain_ref, swapped_ref, plain_alt, swapped_alt, coeff_ref, near_ref, first_ref,
-                 own_ref, near_out, far_out, back_out, acc, scaled):
+def first_kernel(windows, switch_ref, left_ref, left_alt, near_ref, first_ref, own_ref, near_out, far_out, back_out, acc):
     step = pl.program_id(0)
-    cols = plain_ref.shape[0]
+    cols = near_ref.shape[1]
     near_mirrored, special = switch_ref[0], switch_ref[1]
 
     @pl.when(step == 0)
     def _():
         acc[...] = jnp.zeros_like(acc)
 
-    plain = jnp.where(special != 0, plain_alt[...], plain_ref[...])
-    swapped = jnp.where(special != 0, swapped_alt[...], swapped_ref[...])
-    scale(scaled, plain, swapped, coeff_ref)
     flags = [[switch_ref[2 + part * windows + w] for w in range(windows)] for part in range(3)]
     near_weights = [jnp.where(special != 0, first, own) * near for own, near, first in zip(*flags)]
     near = weigh(near_ref[...], near_weights)
     far = weigh(jnp.where(special != 0, own_ref[...], first_ref[...]), [own * first for own, _, first in zip(*flags)])
-    acc[...] += jnp.dot(scaled[...], jnp.concatenate([near, far], axis=1), preferred_element_type=jnp.float32)
+    right = jnp.concatenate([near, far], axis=1)
+
+    @pl.when(special == 0)
+    def _():
+        acc[...] += jnp.dot(left_ref[...], right, preferred_element_type=jnp.float32)
+
+    @pl.when(special != 0)
+    def _():
+        acc[...] += jnp.dot(left_alt[...], right, preferred_element_type=jnp.float32)
 
     @pl.when(step == pl.num_programs(0) - 1)
     def _():
@@ -162,43 +163,42 @@
         pl.when(near_mirrored != 0)(lambda: write_lags(near_out, acc, near_at, cols, True))
 
 
-def first_sums(switch, own, alt, coeffs, near_in, first_in, block):
+def first_sums(switch, left, left_alt, near_in, first_in, block):
     rows, cols = block.shape
     windows = (switch.shape[0] - 2) // 3
     result = jax.ShapeDtypeStruct((LAGS, cols, cols), jnp.bfloat16)
-    left = pl.BlockSpec((cols, STEP), lambda s, on: (0, s * (1 - on[1])))
-    left_alt = pl.BlockSpec((cols, STEP), lambda s, on: (0, s * on[1]))
-    right = pl.BlockSpec((STEP, cols), lambda s, on: (s, 0))
-    right_usual = pl.BlockSpec((STEP, cols), lambda s, on: (s * (1 - on[1]), 0))
-    right_special = pl.BlockSpec((STEP, cols), lambda s, on: (s * on[1], 0))
     return pl.pallas_call(
         functools.partial(first_kernel, windows),
         grid_spec=pltpu.PrefetchScalarGridSpec(
             num_scalar_prefetch=1,
             grid=(rows // STEP,),
-            in_specs=[left, left, left_alt, left_alt, pl.BlockSpec((LAGS, STEP), lambda s, on: (0, s)),
-                      right, right_usual, right_special],
+            in_specs=[
+                pl.BlockSpec((LAGS * cols, STEP), lambda s, on: (0, s * (1 - on[1]))),
+                pl.BlockSpec((LAGS * cols, STEP), lambda s, on: (0, s * on[1])),
+                pl.BlockSpec((STEP, cols), lambda s, on: (s, 0)),
+                pl.BlockSpec((STEP, cols), lambda s, on: (s * (1 - on[1]), 0)),
+                pl.BlockSpec((STEP, cols), lambda s, on: (s * on[1], 0)),
+            ],
             out_specs=[pl.BlockSpec(result.shape, lambda s, on: (0, 0, 0))] * 3,
-            scratch_shapes=[pltpu.VMEM((LAGS * cols, 2 * cols), jnp.float32),
-                            pltpu.VMEM((LAGS * cols, STEP), jnp.bfloat16)],
+            scratch_shapes=[pltpu.VMEM((LAGS * cols, 2 * cols), jnp.float32)],
         ),
         out_shape=[result] * 3,
         compiler_params=PARAMS,
         cost_estimate=pl.CostEstimate(
-            flops=4 * LAGS * cols * cols * rows, bytes_accessed=8 * rows * cols, transcendentals=0
+            flops=4 * LAGS * cols * cols * rows, bytes_accessed=2 * (LAGS + 2) * rows * cols, transcendentals=0
         ),
         name="first_sums",
-    )(switch, *own, *alt, coeffs, near_in, first_in, block)
-
-
-def second_kernel(windows, first, switch_ref, plain_ref, swapped_ref, coeff_ref, partner_ref, *rest):
+    )(switch, left, left_alt, near_in, first_in, block)
+
+
+def second_kernel(windows, first, switch_ref, left_ref, partner_ref, *rest):
     on, late_near = switch_ref[0], switch_ref[1]
     step = pl.program_id(0)
-    cols = plain_ref.shape[0]
+    cols = partner_ref.shape[1]
     if first:
-        acc, scaled = rest
+        acc, = rest
     else:
-        acc_in, near_in, far_in, near_out, far_out, back_out, acc, scaled = rest
+        acc_in, near_in, far_in, back_in, near_out, far_out, back_out, acc = rest
 
     @pl.when(on != 0)
     def _():
@@ -206,9 +206,8 @@
         def _():
             acc[...] = jnp.zeros_like(acc) if first else acc_in[...]
 
-        scale(scaled, plain_ref[...], swapped_ref[...], coeff_ref)
         partner = weigh(partner_ref[...], [switch_ref[2 + w] for w in range(windows)])
-        acc[...] += jnp.dot(scaled[...], partner, preferred_element_type=jnp.float32)
+        acc[...] += jnp.dot(left_ref[...], partner, preferred_element_type=jnp.float32)
 
     if not first:
         @pl.when(step == pl.num_programs(0) - 1)
@@ -222,6 +221,7 @@
 
             @pl.when((on == 0) | (late_near != 0))
             def _():
+                back_out[...] = back_in[...]
                 far_out[...] = far_in[...]
 
             pl.when(late_near != 0)(lambda: write_lags(near_out, acc, here, cols, False))
@@ -231,7 +231,7 @@
                 near_out[...] = near_in[...]
 
 
-def second_sums(switch, own, coeffs, partner, start, earlier=None):
+def second_sums(switch, left, partner, start, earlier=None):
     rows, cols = partner.shape
     windows = switch.shape[0] - 2
     skip = start // STEP
@@ -239,16 +239,15 @@
     total_spec = pl.BlockSpec(total.shape, lambda s, on: (0, 0))
     result = jax.ShapeDtypeStruct((LAGS, cols, cols), jnp.bfloat16)
     result_spec = pl.BlockSpec(result.shape, lambda s, on: (0, 0, 0))
-    left = pl.BlockSpec((cols, STEP), lambda s, on: (0, s * on[0] + skip))
-    in_specs = [left, left, pl.BlockSpec((LAGS, STEP), lambda s, on: (0, s * on[0] + skip)),
+    in_specs = [pl.BlockSpec((LAGS * cols, STEP), lambda s, on: (0, s * on[0] + skip)),
                 pl.BlockSpec((STEP, cols), lambda s, on: (s * on[0], 0))]
-    scratch = [pltpu.VMEM((LAGS * cols, STEP), jnp.bfloat16)]
+    scratch = []
     if earlier is None:
         out_shape, out_specs, earlier = [total], [total_spec], []
     else:
         out_shape, out_specs = [result] * 3, [result_spec] * 3
-        in_specs += [total_spec, result_spec, result_spec]
-        scratch = [pltpu.VMEM(total.shape, jnp.float32)] + scratch
+        in_specs += [total_spec] + [result_spec] * 3
+        scratch = [pltpu.VMEM(total.shape, jnp.float32)]
     return pl.pallas_call(
         functools.partial(second_kernel, windows, not earlier),
         grid_spec=pltpu.PrefetchScalarGridSpec(
@@ -261,10 +260,10 @@
         out_shape=out_shape,
         compiler_params=PARAMS,
         cost_estimate=pl.CostEstimate(
-            flops=2 * LAGS * cols * cols * rows, bytes_accessed=6 * rows * cols, transcendentals=0
+            flops=2 * LAGS * cols * cols * rows, bytes_accessed=2 * (LAGS + 1) * rows * cols, transcendentals=0
         ),
         name="second_last" if earlier else "second_part",
-    )(switch, *own, coeffs, partner, *earlier)
+    )(switch, left, partner, *earlier)
 
 
 def local(spectra, quality):
@@ -289,8 +288,8 @@
     second_pairs = second_far + late_near
     near_pairs = [(d + 1, d) for d in range(1, count - 1) if d not in (1, 3, half - 2, half - 1)]
     near_pairs += [(0, half - 1), (half - 1, 0)]
-    first_back = [(t, s) for s, t in first_far] + [(1, 0)]
-    second_back = [(t, s) for s, t in second_far]
+    first_back = [(t, s) for s, t in first_far]
+    second_back = [(t, s) for s, t in second_far] + [(1, 0)]
     side_pairs = [(0, half - 1), (half - 1, count - 1)]
 
     def among(devices):
@@ -303,7 +302,7 @@
     first_in = lax.ppermute(block, "chan", first_pairs)
     near_in = lax.ppermute(block, "chan", near_pairs)
     coeffs = lag_rows(freq_count, window_count)
-    own = turn(block, switch(True, False), "turn_own")
+    left = left_factors(block, coeffs, switch(True, False), "left_own")
     parts = split(block)
     first_flags = lax.ppermute(quality, "chan", first_pairs)[0]
     near_flags = lax.ppermute(quality, "chan", near_pairs)[0]
@@ -314,24 +313,25 @@
         among([t for _, t in second_pairs]), among([t for _, t in late_near]), quality[0] * second_flags
     )
 
-    late_part, own, coeffs, first_in, near_in = lax.optimization_barrier((parts[0], own, coeffs, first_in, near_in))
+    late_part, left = lax.optimization_barrier((parts[0], left))
     second_first = lax.ppermute(late_part, "chan", second_pairs)
-    alt = turn(first_in, switch(special, False), "turn_first", common=False)
-    near, far, back = first_sums(first_switch, own, alt, coeffs, near_in, first_in, block)
+    left_alt = left_factors(first_in, coeffs, switch(special, False), "left_first", common=False)
+    near, far, back = first_sums(first_switch, left, left_alt, near_in, first_in, block)
     late_part, near = lax.optimization_barrier((parts[1], near))
     second_last = lax.ppermute(late_part, "chan", second_pairs)
     first_returned = lax.ppermute(back, "chan", first_back)
     side_returned = lax.ppermute(near, "chan", side_pairs)
 
     second_switch, first_returned = lax.optimization_barrier((second_switch, first_returned))
-    total, = second_sums(second_switch, own, coeffs, second_first, 0)
+    total, = second_sums(second_switch, left, second_first, 0)
     near = jnp.where(among([half - 1, count - 1]), side_returned, near)
-    near = jnp.where(me == 0, first_returned, jnp.where(me == half - 2, far, near))
+    near = jnp.where(me == half - 2, far, near)
     far = jnp.where(among([s for s, _ in first_far]), first_returned, far)
     near, far, back = second_sums(
-        second_switch, own, coeffs, second_last, parts[0].shape[0], [total, near, far]
+        second_switch, left, second_last, parts[0].shape[0], [total, near, far, back]
     )
     second_returned = lax.ppermute(back, "chan", second_back)
+    near = jnp.where(me == 0, second_returned, near)
     far = jnp.where(among([s for s, _ in second_far]), second_returned, far)
     return near[None], far[None]
 

time: 84.9 us -> 90.9 us (1.071)
  Pallas kernels: 26.9 us -> 42.5 us
  local copies, waits for them, and re-layouts: 8.58 us -> 1.6 us
  waiting for transfers between devices: 8.56 us -> 3.09 us
  starting transfers between devices: 35.2 us -> 38.8 us
    ppermute x1, starting transfers between devices: 1.28 us -> 16.3 us  [local(): second_returned = lax.ppermute(back, 'chan', second_back)]
    ppermute x1, starting transfers between devices: 8.33 us -> 0.68 us  [local(): first_returned = lax.ppermute(back, 'chan', first_back)]
    unnamed x22 -> x8, local copies, waits for them, and re-layouts: 8.58 us -> 1.6 us
    pallas_call x2, Pallas kernels: 5.52 us -> 11.7 us  [left_factors(): pl.pallas_call(left_kernel, grid_spec=pltpu.PrefetchScalarGridSpec(num_sc...]
    ppermute x1, waiting for transfers between devices: 7.26 us -> 1.17 us  [local(): second_returned = lax.ppermute(back, 'chan', second_back)]
    pallas_call x1, Pallas kernels: 9.56 us -> 14 us  [first_sums(): pl.pallas_call(functools.partial(first_kernel, windows), grid_spec=pltpu....]
    pallas_call x2, Pallas kernels: 10.1 us -> 13.6 us  [second_sums(): pl.pallas_call(functools.partial(second_kernel, windows, not earlier), gr...]
    ppermute x1, starting transfers between devices: 10.2 us -> 6.92 us  [local(): second_first = lax.ppermute(late_part, 'chan', second_pairs)]
  transfers between devices with their start and end apart: 10 -> 10, of which waited for: 2 -> 2; matrix products, arithmetic and copies ran while one was open for 4% -> 3% of each run, Pallas kernels for 27% -> 41%
where the time goes in v10:
time: 90.9 us; the launch traced here: 90 us
  Pallas kernels  42.5 us (47%)
  starting transfers between devices  38.8 us (43%)
  other arithmetic  3.19 us (4%)
  waiting for transfers between devices  3.09 us (3%)
  local copies, waits for them, and re-layouts  1.6 us (2%)
    ppermute x1, starting transfers between devices, local(): second_returned = lax.ppermute(back, 'chan', second_back)  16.3 us
    pallas_call x1, Pallas kernels, first_sums(): pl.pallas_call(functools.partial(first_kernel, windows), grid_spec=pltpu....  14 us
    pallas_call x2, Pallas kernels, second_sums(): pl.pallas_call(functools.partial(second_kernel, windows, not earlier), gr...  13.6 us
    pallas_call x2, Pallas kernels, left_factors(): pl.pallas_call(left_kernel, grid_spec=pltpu.PrefetchScalarGridSpec(num_sc...  11.7 us
    ppermute x1, starting transfers between devices, local(): second_flags = lax.ppermute(quality, 'chan', second_pairs)[0]  7.04 us
    ppermute x1, starting transfers between devices, local(): second_first = lax.ppermute(late_part, 'chan', second_pairs)  6.92 us
    pallas_call x1, Pallas kernels, split(): pl.pallas_call(functools.partial(split_kernel, middle), grid=(steps,), in...  3.11 us
    ppermute x1, starting transfers between devices, local(): near_in = lax.ppermute(block, 'chan', near_pairs)  2.02 us
  transfers between devices with their start and end apart: 10, of which 2 were waited for; matrix products, arithmetic and copies ran while one was open for 3% of the time, Pallas kernels for 41%

profile of v10, /device:TPU:1, one launch (start us, length us, event | category | flops | bytes accessed | tf_op | source)
XLA Modules:
  0.0 90.0 jit_solution(7938163591521857436)
XLA Ops:
  0.6 1.3 %collective-permute-start.3 = (bf16[8192,128]{1,0:T(8,128)(2,1)}, bf16[8192,128]{1,0:T(8,128)(2,1)}, u32[]{:S(2)}, u32[]{:S(2)}) collective-permute-start(bf16[8192,128]{1,0:T(8,128)(2,1)} %bitcast.15), channel_id=1, source_target_pairs={{8,0},{4,12},{6,14},{15,7},{0,1},{7,6},{24,16},{20,28},{22,30},{31... | collective-permute-start | bytes 6291464 | tf_op jit(solution)/shard_map/ppermute | solution.py:302
  1.9 2.0 %collective-permute-start.4 = (bf16[8192,128]{1,0:T(8,128)(2,1)}, bf16[8192,128]{1,0:T(8,128)(2,1)}, u32[]{:S(2)}, u32[]{:S(2)}) collective-permute-start(bf16[8192,128]{1,0:T(8,128)(2,1)} %bitcast.16), channel_id=1, source_target_pairs={{3,2},{5,4},{6,5},{9,8},{10,9},{11,10},{12,11},{13,12},{14,13},{15... | collective-permute-start | bytes 6291464 | tf_op jit(solution)/shard_map/ppermute | solution.py:303
  4.0 0.9 %multiply_convert_fusion = (bf16[5,8192]{1,0:T(8,128)(2,1)S(1)}, f32[5,8192]{1,0:T(8,128)S(1)}) fusion(f32[8192]{0:T(1024)S(1)} %fusion.9, f32[5]{0:T(128)S(1)} %iota_multiply_fusion), kind=kLoop, calls=%fused_computation.5 | loop fusion | flops 122880 | bytes 278548 | tf_op jit(solution)/shard_map/convert
  4.9 0.9 fusion.2
  5.8 1.6 %copy-done = bf16[1024,2,4,128]{3,2,1,0:T(4,128)(2,1)S(1)} copy-done((bf16[1024,2,4,128]{3,2,1,0:T(4,128)(2,1)S(1)}, bf16[1024,2,4,128]{3,2,1,0:T(4,128)(2,1)}, u32[]{:S(2)}) %copy-start) | copy-done | bytes 2097176
  7.4 3.1 %split.1 = (bf16[5120,128]{1,0:T(8,128)(2,1)}, bf16[3072,128]{1,0:T(8,128)(2,1)}) custom-call(bf16[8192,128]{1,0:T(8,128)(2,1)S(1)} %bitcast.18), custom_call_target="tpu_custom_call" | custom-call | bytes 4194304 | tf_op jit(solution)/shard_map/split/pallas_call | solution.py:47
  10.5 0.1 pad_maximum_fusion.coeff_ref
  10.6 8.7 %left_own.1.left_ref = bf16[1152,8192]{1,0:T(8,128)(2,1)} custom-call(s32[2]{0:T(128)S(1)} %copy-done.2, bf16[8192,128]{1,0:T(8,128)(2,1)S(1)} %bitcast.19, bf16[9,8192]{1,0:T(8,128)(2,1)S(1)} %pad_maximum_fusion.coeff_ref), custom_call_target="tpu_custom_call" | custom-call | bytes 20971520 | tf_op jit(solution)/shard_map/left_own/pallas_call | solution.py:83
  19.3 6.9 %collective-permute-start.7 = (bf16[5120,128]{1,0:T(8,128)(2,1)}, bf16[5120,128]{1,0:T(8,128)(2,1)S(1)}, u32[]{:S(2)}, u32[]{:S(2)}) collective-permute-start(bf16[5120,128]{1,0:T(8,128)(2,1)} %get-tuple-element.23), channel_id=1, source_target_pairs={{1,9},{10,2},{3,11},{13,5},{2,1},{4,3},{17,25},{26,18},{19,27},{29... | collective-permute-start | bytes 3932168 | tf_op jit(solution)/shard_map/ppermute | solution.py:317
  26.3 0.7 collective-permute-start.1
  26.9 1.3 %collective-permute-start.2 = (s32[1,4]{1,0:T(1,128)S(1)}, s32[1,4]{1,0:T(1,128)S(1)}, u32[]{:S(2)}, u32[]{:S(2)}) collective-permute-start(s32[1,4]{1,0:T(1,128)S(1)} %copy-done.3), channel_id=1, source_target_pairs={{8,0},{4,12},{6,14},{15,7},{0,1},{7,6},{24,16},{20,28},{22,30},{31... | collective-permute-start | bytes 56 | tf_op jit(solution)/shard_map/ppermute | solution.py:307
  28.3 7.0 %collective-permute-start = (s32[1,4]{1,0:T(1,128)S(1)}, s32[1,4]{1,0:T(1,128)S(1)}, u32[]{:S(2)}, u32[]{:S(2)}) collective-permute-start(s32[1,4]{1,0:T(1,128)S(1)} %copy-done.3), channel_id=1, source_target_pairs={{1,9},{10,2},{3,11},{13,5},{2,1},{4,3},{17,25},{26,18},{19,27},{29... | collective-permute-start | bytes 56 | tf_op jit(solution)/shard_map/ppermute | solution.py:309
  35.5 3.0 %left_first.1.left_alt = bf16[1152,8192]{1,0:T(8,128)(2,1)} custom-call(s32[2]{0:T(128)S(1)} %get-tuple-element.37.switch_ref, bf16[8192,128]{1,0:T(8,128)(2,1)} %collective-permute-done.3.x_ref.first_ref, bf16[9,8192]{1,0:T(8,128)(2,1)S(1)} %pad_maximum_fusion.coeff_ref), custom_call_target="tpu_custom_call" | custom-call | tf_op jit(solution)/shard_map/left_first/pallas_call | solution.py:83
  38.5 14.0 %first_sums.1 = (bf16[9,128,128]{2,1,0:T(8,128)(2,1)S(1)}, bf16[9,128,128]{2,1,0:T(8,128)(2,1)S(1)}, bf16[9,128,128]{2,1,0:T(8,128)(2,1)S(1)}) custom-call(s32[14]{0:T(128)S(1)} %pad_add_fusion.1.switch_ref, bf16[1152,8192]{1,0:T(8,128)(2,1)} %left_own.1.left_ref, bf16[1152,8192]{1,0:T(8,128)(2,1)} %left_first.1.left_alt, ...), custom_call_target="tpu_custom_call" | custom-call | flops 4831838208 | bytes 23068672 | tf_op jit(solution)/shard_map/first_sums/pallas_call | solution.py:170
  52.5 1.9 %collective-permute-start.6 = (bf16[3072,128]{1,0:T(8,128)(2,1)}, bf16[3072,128]{1,0:T(8,128)(2,1)S(1)}, u32[]{:S(2)}, u32[]{:S(2)}) collective-permute-start(bf16[3072,128]{1,0:T(8,128)(2,1)} %get-tuple-element.22), channel_id=1, source_target_pairs={{1,9},{10,2},{3,11},{13,5},{2,1},{4,3},{17,25},{26,18},{19,27},{29... | collective-permute-start | bytes 2359304 | tf_op jit(solution)/shard_map/ppermute | solution.py:321
  54.5 0.7 collective-permute-start.8
  55.2 0.7 collective-permute-start.5
  56.0 8.0 %second_part.1.rest_0_ = f32[1152,128]{1,0:T(8,128)S(1)} custom-call(s32[6]{0:T(128)S(1)} %pad_add_fusion.switch_ref, bf16[1152,8192]{1,0:T(8,128)(2,1)} %left_own.1.left_ref, bf16[5120,128]{1,0:T(8,128)(2,1)S(1)} %collective-permute-done.7.partner_ref), custom_call_target="tpu_custom_call" | custom-call | flops 1509949440 | bytes 13107200 | tf_op jit(solution)/shard_map/second_part/pallas_call | solution.py:251
  64.1 0.1 broadcast_select_fusion
  64.1 1.9 %collective-permute-done.6.partner_ref = bf16[3072,128]{1,0:T(8,128)(2,1)S(1)} collective-permute-done((bf16[3072,128]{1,0:T(8,128)(2,1)}, bf16[3072,128]{1,0:T(8,128)(2,1)S(1)}, u32[]{:S(2)}, u32[]{:S(2)}) %collective-permute-start.6) | collective-permute-done | bytes 786464 | tf_op jit(solution)/shard_map/ppermute | solution.py:321
  66.0 5.6 %second_last.1 = (bf16[9,128,128]{2,1,0:T(8,128)(2,1)S(1)}, bf16[9,128,128]{2,1,0:T(8,128)(2,1)S(1)}, bf16[9,128,128]{2,1,0:T(8,128)(2,1)S(1)}) custom-call(s32[6]{0:T(128)S(1)} %pad_add_fusion.switch_ref, bf16[1152,8192]{1,0:T(8,128)(2,1)} %left_own.1.left_ref, bf16[3072,128]{1,0:T(8,128)(2,1)S(1)} %collective-permute-done.6.partner_ref, ...), custom_call_target="tpu_custom_call" | custom-call | flops 905969664 | bytes 7864320 | tf_op jit(solution)/shard_map/second_last/pallas_call | solution.py:251
  71.7 16.3 %collective-permute-start.9 = (bf16[9,128,128]{2,1,0:T(8,128)(2,1)S(1)}, bf16[9,128,128]{2,1,0:T(8,128)(2,1)S(1)}, u32[]{:S(2)}, u32[]{:S(2)}) collective-permute-start(bf16[9,128,128]{2,1,0:T(8,128)(2,1)S(1)} %get-tuple-element.27), channel_id=1, source_target_pairs={{9,1},{2,10},{11,3},{5,13},{1,0},{25,17},{18,26},{27,19},{21,29},{... | collective-permute-start | bytes 884744 | tf_op jit(solution)/shard_map/ppermute | solution.py:333
  88.0 1.2 %collective-permute-done.9 = bf16[9,128,128]{2,1,0:T(8,128)(2,1)S(1)} collective-permute-done((bf16[9,128,128]{2,1,0:T(8,128)(2,1)S(1)}, bf16[9,128,128]{2,1,0:T(8,128)(2,1)S(1)}, u32[]{:S(2)}, u32[]{:S(2)}) %collective-permute-start.9) | collective-permute-done | bytes 294944 | tf_op jit(solution)/shard_map/ppermute | solution.py:333
  89.1 0.9 select_bitcast_fusion
  (23 shorter events, 0.4 us)
Async XLA Ops:
  0.6 10.0 %copy-start.2 = (s32[2]{0:T(128)S(1)}, s32[2]{0:T(128)}, u32[]{:S(2)}) copy-start(s32[2]{0:T(128)} %constant.58.clone.1.switch_ref) | copy-start | bytes 28
  0.6 34.8 %collective-permute-start.3 = (bf16[8192,128]{1,0:T(8,128)(2,1)}, bf16[8192,128]{1,0:T(8,128)(2,1)}, u32[]{:S(2)}, u32[]{:S(2)}) collective-permute-start(bf16[8192,128]{1,0:T(8,128)(2,1)} %bitcast.15), channel_id=1, source_target_pairs={{8,0},{4,12},{6,14},{15,7},{0,1},{7,6},{24,16},{20,28},{22,30},{31... | collective-permute-start | bytes 6291464 | tf_op jit(solution)/shard_map/ppermute | solution.py:302
  1.9 36.5 %collective-permute-start.4 = (bf16[8192,128]{1,0:T(8,128)(2,1)}, bf16[8192,128]{1,0:T(8,128)(2,1)}, u32[]{:S(2)}, u32[]{:S(2)}) collective-permute-start(bf16[8192,128]{1,0:T(8,128)(2,1)} %bitcast.16), channel_id=1, source_target_pairs={{3,2},{5,4},{6,5},{9,8},{10,9},{11,10},{12,11},{13,12},{14,13},{15... | collective-permute-start | bytes 6291464 | tf_op jit(solution)/shard_map/ppermute | solution.py:303
  5.8 1.6 %copy-start = (bf16[1024,2,4,128]{3,2,1,0:T(4,128)(2,1)S(1)}, bf16[1024,2,4,128]{3,2,1,0:T(4,128)(2,1)}, u32[]{:S(2)}) copy-start(bf16[1024,2,4,128]{3,2,1,0:T(4,128)(2,1)} %param.2) | copy-start | bytes 6291460
  7.4 3.2 %copy-start.1 = (bf16[1024,2,4,128]{3,2,1,0:T(4,128)(2,1)S(1)}, bf16[1024,2,4,128]{3,2,1,0:T(4,128)(2,1)}, u32[]{:S(2)}) copy-start(bf16[1024,2,4,128]{3,2,1,0:T(4,128)(2,1)} %param.2) | copy-start | bytes 6291460
  10.6 15.6 %copy-start.3 = (s32[1,4]{1,0:T(1,128)S(1)}, s32[1,4]{1,0:T(1,128)}, u32[]{:S(2)}) copy-start(s32[1,4]{1,0:T(1,128)} %param.3) | copy-start | bytes 52
  19.3 36.7 %collective-permute-start.7 = (bf16[5120,128]{1,0:T(8,128)(2,1)}, bf16[5120,128]{1,0:T(8,128)(2,1)S(1)}, u32[]{:S(2)}, u32[]{:S(2)}) collective-permute-start(bf16[5120,128]{1,0:T(8,128)(2,1)} %get-tuple-element.23), channel_id=1, source_target_pairs={{1,9},{10,2},{3,11},{13,5},{2,1},{4,3},{17,25},{26,18},{19,27},{29... | collective-permute-start | bytes 3932168 | tf_op jit(solution)/shard_map/ppermute | solution.py:317
  26.3 2.1 %collective-permute-start.1 = (s32[1,4]{1,0:T(1,128)S(1)}, s32[1,4]{1,0:T(1,128)S(1)}, u32[]{:S(2)}, u32[]{:S(2)}) collective-permute-start(s32[1,4]{1,0:T(1,128)S(1)} %copy-done.3), channel_id=1, source_target_pairs={{3,2},{5,4},{6,5},{9,8},{10,9},{11,10},{12,11},{13,12},{14,13},{15... | collective-permute-start | bytes 56 | tf_op jit(solution)/shard_map/ppermute | solution.py:308
  26.9 8.5 %collective-permute-start.2 = (s32[1,4]{1,0:T(1,128)S(1)}, s32[1,4]{1,0:T(1,128)S(1)}, u32[]{:S(2)}, u32[]{:S(2)}) collective-permute-start(s32[1,4]{1,0:T(1,128)S(1)} %copy-done.3), channel_id=1, source_target_pairs={{8,0},{4,12},{6,14},{15,7},{0,1},{7,6},{24,16},{20,28},{22,30},{31... | collective-permute-start | bytes 56 | tf_op jit(solution)/shard_map/ppermute | solution.py:307
  28.3 27.6 %collective-permute-start = (s32[1,4]{1,0:T(1,128)S(1)}, s32[1,4]{1,0:T(1,128)S(1)}, u32[]{:S(2)}, u32[]{:S(2)}) collective-permute-start(s32[1,4]{1,0:T(1,128)S(1)} %copy-done.3), channel_id=1, source_target_pairs={{1,9},{10,2},{3,11},{13,5},{2,1},{4,3},{17,25},{26,18},{19,27},{29... | collective-permute-start | bytes 56 | tf_op jit(solution)/shard_map/ppermute | solution.py:309
  52.5 13.5 %collective-permute-start.6 = (bf16[3072,128]{1,0:T(8,128)(2,1)}, bf16[3072,128]{1,0:T(8,128)(2,1)S(1)}, u32[]{:S(2)}, u32[]{:S(2)}) collective-permute-start(bf16[3072,128]{1,0:T(8,128)(2,1)} %get-tuple-element.22), channel_id=1, source_target_pairs={{1,9},{10,2},{3,11},{13,5},{2,1},{4,3},{17,25},{26,18},{19,27},{29... | collective-permute-start | bytes 2359304 | tf_op jit(solution)/shard_map/ppermute | solution.py:321
  54.5 9.5 %collective-permute-start.8 = (bf16[9,128,128]{2,1,0:T(8,128)(2,1)S(1)}, bf16[9,128,128]{2,1,0:T(8,128)(2,1)S(1)}, u32[]{:S(2)}, u32[]{:S(2)}) collective-permute-start(bf16[9,128,128]{2,1,0:T(8,128)(2,1)S(1)} %get-tuple-element.25), channel_id=1, source_target_pairs={{0,7},{7,15},{16,23},{23,31}} | collective-permute-start | bytes 884744 | tf_op jit(solution)/shard_map/ppermute | solution.py:323
  55.2 0.8 collective-permute-start.5
  71.7 17.5 %collective-permute-start.9 = (bf16[9,128,128]{2,1,0:T(8,128)(2,1)S(1)}, bf16[9,128,128]{2,1,0:T(8,128)(2,1)S(1)}, u32[]{:S(2)}, u32[]{:S(2)}) collective-permute-start(bf16[9,128,128]{2,1,0:T(8,128)(2,1)S(1)} %get-tuple-element.27), channel_id=1, source_target_pairs={{9,1},{2,10},{11,3},{5,13},{1,0},{25,17},{18,26},{27,19},{21,29},{... | collective-permute-start | bytes 884744 | tf_op jit(solution)/shard_map/ppermute | solution.py:333

commit v11 on v9

--- a/solution.py
+++ b/solution.py
@@ -11,7 +11,7 @@
 HL = 4
 LAGS = 2 * HL + 1
 STEP = 1024
-PARTS = (5, 8)
+PARTS = (3, 8)
 PARAMS = pltpu.CompilerParams(vmem_limit_bytes=16 * 1024 * 1024)
 
 
@@ -198,7 +198,7 @@
     if first:
         acc, scaled = rest
     else:
-        acc_in, near_in, far_in, near_out, far_out, back_out, acc, scaled = rest
+        acc_in, near_in, far_in, back_in, near_out, far_out, back_out, acc, scaled = rest
 
     @pl.when(on != 0)
     def _():
@@ -222,6 +222,7 @@
 
             @pl.when((on == 0) | (late_near != 0))
             def _():
+                back_out[...] = back_in[...]
                 far_out[...] = far_in[...]
 
             pl.when(late_near != 0)(lambda: write_lags(near_out, acc, here, cols, False))
@@ -247,7 +248,7 @@
         out_shape, out_specs, earlier = [total], [total_spec], []
     else:
         out_shape, out_specs = [result] * 3, [result_spec] * 3
-        in_specs += [total_spec, result_spec, result_spec]
+        in_specs += [total_spec] + [result_spec] * 3
         scratch = [pltpu.VMEM(total.shape, jnp.float32)] + scratch
     return pl.pallas_call(
         functools.partial(second_kernel, windows, not earlier),
@@ -289,8 +290,7 @@
     second_pairs = second_far + late_near
     near_pairs = [(d + 1, d) for d in range(1, count - 1) if d not in (1, 3, half - 2, half - 1)]
     near_pairs += [(0, half - 1), (half - 1, 0)]
-    first_back = [(t, s) for s, t in first_far] + [(1, 0)]
-    second_back = [(t, s) for s, t in second_far]
+    back_pairs = [(t, s) for s, t in first_far + second_far] + [(1, 0)]
     side_pairs = [(0, half - 1), (half - 1, count - 1)]
 
     def among(devices):
@@ -300,8 +300,8 @@
         flags = jnp.stack([jnp.asarray(on), jnp.asarray(other)]).astype(jnp.int32)
         return jnp.concatenate([flags, *weights])
 
+    near_in = lax.ppermute(block, "chan", near_pairs)
     first_in = lax.ppermute(block, "chan", first_pairs)
-    near_in = lax.ppermute(block, "chan", near_pairs)
     coeffs = lag_rows(freq_count, window_count)
     own = turn(block, switch(True, False), "turn_own")
     parts = split(block)
@@ -314,25 +314,22 @@
         among([t for _, t in second_pairs]), among([t for _, t in late_near]), quality[0] * second_flags
     )
 
-    late_part, own, coeffs, first_in, near_in = lax.optimization_barrier((parts[0], own, coeffs, first_in, near_in))
-    second_first = lax.ppermute(late_part, "chan", second_pairs)
+    near_in, parts, own, coeffs, first_in = lax.optimization_barrier((near_in, parts, own, coeffs, first_in))
+    second_in = [lax.ppermute(part, "chan", second_pairs) for part in parts]
     alt = turn(first_in, switch(special, False), "turn_first", common=False)
     near, far, back = first_sums(first_switch, own, alt, coeffs, near_in, first_in, block)
-    late_part, near = lax.optimization_barrier((parts[1], near))
-    second_last = lax.ppermute(late_part, "chan", second_pairs)
-    first_returned = lax.ppermute(back, "chan", first_back)
     side_returned = lax.ppermute(near, "chan", side_pairs)
-
-    second_switch, first_returned = lax.optimization_barrier((second_switch, first_returned))
-    total, = second_sums(second_switch, own, coeffs, second_first, 0)
+    second_switch, near = lax.optimization_barrier((second_switch, near))
+    total, = second_sums(second_switch, own, coeffs, second_in[0], 0)
+
     near = jnp.where(among([half - 1, count - 1]), side_returned, near)
-    near = jnp.where(me == 0, first_returned, jnp.where(me == half - 2, far, near))
-    far = jnp.where(among([s for s, _ in first_far]), first_returned, far)
+    near = jnp.where(me == half - 2, far, near)
     near, far, back = second_sums(
-        second_switch, own, coeffs, second_last, parts[0].shape[0], [total, near, far]
+        second_switch, own, coeffs, second_in[1], parts[0].shape[0], [total, near, far, back]
     )
-    second_returned = lax.ppermute(back, "chan", second_back)
-    far = jnp.where(among([s for s, _ in second_far]), second_returned, far)
+    returned = lax.ppermute(back, "chan", back_pairs)
+    near = jnp.where(me == 0, returned, near)
+    far = jnp.where(among([s for s, _ in first_far + second_far]), returned, far)
     return near[None], far[None]
 
 

time: 84.9 us -> 76.7 us (0.903)
  the two profiles are of different devices: /device:TPU:1 before, /device:TPU:5 now
where the time goes in v11:
time: 76.7 us; the launch traced here: 76.1 us
  starting transfers between devices  25.8 us (34%)
  Pallas kernels  23.7 us (31%)
  waiting for transfers between devices  16.5 us (22%)
  local copies, waits for them, and re-layouts  6.05 us (8%)
  other arithmetic  3.22 us (4%)
  between operations  0.91 us (1%)
    ppermute x2, starting transfers between devices, local(): second_in = [lax.ppermute(part, 'chan', second_pairs) for part in parts]  12.4 us
    pallas_call x1, Pallas kernels, first_sums(): pl.pallas_call(functools.partial(first_kernel, windows), grid_spec=pltpu....  9.58 us
    ppermute x2, waiting for transfers between devices, local(): second_in = [lax.ppermute(part, 'chan', second_pairs) for part in parts]  9.41 us
    pallas_call x2, Pallas kernels, second_sums(): pl.pallas_call(functools.partial(second_kernel, windows, not earlier), gr...  8.29 us
    ppermute x1, waiting for transfers between devices, local(): returned = lax.ppermute(back, 'chan', back_pairs)  7.03 us
    unnamed x16, local copies, waits for them, and re-layouts  6.05 us
    pallas_call x2, Pallas kernels, turn(): pl.pallas_call(turn_kernel, grid_spec=pltpu.PrefetchScalarGridSpec(num_sc...  5.51 us
    ppermute x1, starting transfers between devices, local(): near_in = lax.ppermute(block, 'chan', near_pairs)  3.89 us
  transfers between devices with their start and end apart: 9, of which 2 were waited for; matrix products, arithmetic and copies ran while one was open for 3% of the time, Pallas kernels for 24%

profile of v11, /device:TPU:5, one launch (start us, length us, event | category | flops | bytes accessed | tf_op | source)
XLA Modules:
  0.0 76.1 jit_solution(17393090396626660611)
XLA Ops:
  0.6 3.9 %collective-permute-start.3 = (bf16[8192,128]{1,0:T(8,128)(2,1)}, bf16[8192,128]{1,0:T(8,128)(2,1)}, u32[]{:S(2)}, u32[]{:S(2)}) collective-permute-start(bf16[8192,128]{1,0:T(8,128)(2,1)} %bitcast.15), channel_id=1, source_target_pairs={{3,2},{5,4},{6,5},{9,8},{10,9},{11,10},{12,11},{13,12},{14,13},{15... | collective-permute-start | bytes 6291464 | tf_op jit(solution)/shard_map/ppermute | solution.py:303
  4.5 2.0 %collective-permute-start.4 = (bf16[8192,128]{1,0:T(8,128)(2,1)}, bf16[8192,128]{1,0:T(8,128)(2,1)}, u32[]{:S(2)}, u32[]{:S(2)}) collective-permute-start(bf16[8192,128]{1,0:T(8,128)(2,1)} %bitcast.16), channel_id=1, source_target_pairs={{8,0},{4,12},{6,14},{15,7},{0,1},{7,6},{24,16},{20,28},{22,30},{31... | collective-permute-start | bytes 6291464 | tf_op jit(solution)/shard_map/ppermute | solution.py:304
  6.5 1.3 %collective-permute-start.1 = (s32[1,4]{1,0:T(1,128)}, s32[1,4]{1,0:T(1,128)S(1)}, u32[]{:S(2)}, u32[]{:S(2)}) collective-permute-start(s32[1,4]{1,0:T(1,128)} %param.3), channel_id=1, source_target_pairs={{3,2},{5,4},{6,5},{9,8},{10,9},{11,10},{12,11},{13,12},{14,13},{15... | collective-permute-start | bytes 56 | tf_op jit(solution)/shard_map/ppermute | solution.py:309
  7.8 0.7 collective-permute-start.2
  8.5 3.6 %collective-permute-start = (s32[1,4]{1,0:T(1,128)}, s32[1,4]{1,0:T(1,128)S(1)}, u32[]{:S(2)}, u32[]{:S(2)}) collective-permute-start(s32[1,4]{1,0:T(1,128)} %param.3), channel_id=1, source_target_pairs={{1,9},{10,2},{3,11},{13,5},{2,1},{4,3},{17,25},{26,18},{19,27},{29... | collective-permute-start | bytes 56 | tf_op jit(solution)/shard_map/ppermute | solution.py:310
  12.1 1.6 %copy-done.2 = bf16[1024,2,4,128]{3,2,1,0:T(4,128)(2,1)S(1)} copy-done((bf16[1024,2,4,128]{3,2,1,0:T(4,128)(2,1)S(1)}, bf16[1024,2,4,128]{3,2,1,0:T(4,128)(2,1)}, u32[]{:S(2)}) %copy-start.2) | copy-done | bytes 2097176
  13.9 0.9 %copy-done.6 = bf16[3072,128]{1,0:T(8,128)(2,1)} copy-done((bf16[3072,128]{1,0:T(8,128)(2,1)}, bf16[3072,128]{1,0:T(8,128)(2,1)S(1)}, u32[]{:S(2)}) %copy-start.6) | copy-done | bytes 786456
  14.9 0.6 copy-done.3
  15.5 3.9 %turn_own.1 = (bf16[128,8192]{1,0:T(8,128)(2,1)S(1)}, bf16[128,8192]{1,0:T(8,128)(2,1)S(1)}) custom-call(s32[2]{0:T(128)S(1)} %copy-done.5, bf16[8192,128]{1,0:T(8,128)(2,1)S(1)} %bitcast.18), custom_call_target="tpu_custom_call" | custom-call | bytes 6291456 | tf_op jit(solution)/shard_map/turn_own/pallas_call | solution.py:82
  19.5 1.3 %copy-done = bf16[128,8192]{1,0:T(8,128)(2,1)} copy-done((bf16[128,8192]{1,0:T(8,128)(2,1)}, bf16[128,8192]{1,0:T(8,128)(2,1)S(1)}, u32[]{:S(2)}) %copy-start) | copy-done | bytes 2097176
  21.0 0.9 %multiply_convert_fusion = (bf16[5,8192]{1,0:T(8,128)(2,1)S(1)}, f32[5,8192]{1,0:T(8,128)S(1)}) fusion(f32[8192]{0:T(1024)S(1)} %fusion.9, f32[5]{0:T(128)S(1)} %iota_multiply_fusion), kind=kLoop, calls=%fused_computation.4 | loop fusion | flops 122880 | bytes 278548 | tf_op jit(solution)/shard_map/convert
  21.9 0.9 %fusion.2 = bf16[4,8192]{1,0:T(4,128)(2,1)S(1)} fusion(f32[5,8192]{1,0:T(8,128)S(1)} %get-tuple-element.47, f32[8192]{0:T(1024)S(1)} %select_multiply_fusion), kind=kLoop, calls=%fused_computation.8 | loop fusion | flops 98304 | bytes 229376 | tf_op jit(solution)/shard_map/convert.1
  22.9 10.5 %collective-permute-start.5 = (bf16[5120,128]{1,0:T(8,128)(2,1)S(1)}, bf16[5120,128]{1,0:T(8,128)(2,1)S(1)}, u32[]{:S(2)}, u32[]{:S(2)}) collective-permute-start(bf16[5120,128]{1,0:T(8,128)(2,1)S(1)} %get-tuple-element.36), channel_id=1, source_target_pairs={{1,9},{10,2},{3,11},{13,5},{2,1},{4,3},{17,25},{26,18},{19,27},{29... | collective-permute-start | bytes 3932168 | tf_op jit(solution)/shard_map/ppermute | solution.py:318
  33.6 1.9 %collective-permute-start.6 = (bf16[3072,128]{1,0:T(8,128)(2,1)}, bf16[3072,128]{1,0:T(8,128)(2,1)S(1)}, u32[]{:S(2)}, u32[]{:S(2)}) collective-permute-start(bf16[3072,128]{1,0:T(8,128)(2,1)} %copy-done.6), channel_id=1, source_target_pairs={{1,9},{10,2},{3,11},{13,5},{2,1},{4,3},{17,25},{26,18},{19,27},{29... | collective-permute-start | bytes 2359304 | tf_op jit(solution)/shard_map/ppermute | solution.py:318
  35.5 1.6 %turn_first.1 = (bf16[128,8192]{1,0:T(8,128)(2,1)S(1)}, bf16[128,8192]{1,0:T(8,128)(2,1)S(1)}) custom-call(s32[2]{0:T(128)S(1)} %add_convert_fusion.2.active_ref, bf16[8192,128]{1,0:T(8,128)(2,1)} %collective-permute-done.4.x_ref.first_ref), custom_call_target="tpu_custom_call" | custom-call | tf_op jit(solution)/shard_map/turn_first/pallas_call | solution.py:82
  37.1 1.6 %copy-done.4 = bf16[1024,2,4,128]{3,2,1,0:T(4,128)(2,1)S(1)} copy-done((bf16[1024,2,4,128]{3,2,1,0:T(4,128)(2,1)S(1)}, bf16[1024,2,4,128]{3,2,1,0:T(4,128)(2,1)}, u32[]{:S(2)}) %copy-start.4) | copy-done | bytes 2097176
  38.7 9.6 %first_sums.1 = (bf16[9,128,128]{2,1,0:T(8,128)(2,1)S(1)}, bf16[9,128,128]{2,1,0:T(8,128)(2,1)S(1)}, bf16[9,128,128]{2,1,0:T(8,128)(2,1)S(1)}) custom-call(s32[14]{0:T(128)S(1)} %pad_add_fusion.1.switch_ref, bf16[128,8192]{1,0:T(8,128)(2,1)S(1)} %get-tuple-element.27.plain_ref, bf16[128,8192]{1,0:T(8,128)(2,1)S(1)} %copy-done.1, ...), custom_call_target="tpu_custom_call" | custom-call | flops 4831838208 | bytes 8388608 | tf_op jit(solution)/shard_map/first_sums/pallas_call | solution.py:174
  48.3 0.7 collective-permute-start.7
  49.1 9.4 %collective-permute-done.6.partner_ref = bf16[3072,128]{1,0:T(8,128)(2,1)S(1)} collective-permute-done((bf16[3072,128]{1,0:T(8,128)(2,1)}, bf16[3072,128]{1,0:T(8,128)(2,1)S(1)}, u32[]{:S(2)}, u32[]{:S(2)}) %collective-permute-start.6) | collective-permute-done | bytes 786464 | tf_op jit(solution)/shard_map/ppermute | solution.py:318
  58.5 3.2 %second_part.1.rest_0_ = f32[1152,128]{1,0:T(8,128)S(1)} custom-call(s32[6]{0:T(128)S(1)} %pad_add_fusion.switch_ref, bf16[128,8192]{1,0:T(8,128)(2,1)S(1)} %get-tuple-element.27.plain_ref, bf16[128,8192]{1,0:T(8,128)(2,1)S(1)} %copy-done.1, bf16[9,8192]{1,0:T(8,128)(2,1)S(1)} %pad_maximum_fusion.coeff_ref, ...), custom_call_target="tpu_custom_call" | custom-call | flops 905969664 | bytes 2359296 | tf_op jit(solution)/shard_map/second_part/pallas_call | solution.py:253
  61.8 5.1 %second_last.1 = (bf16[9,128,128]{2,1,0:T(8,128)(2,1)S(1)}, bf16[9,128,128]{2,1,0:T(8,128)(2,1)S(1)}, bf16[9,128,128]{2,1,0:T(8,128)(2,1)S(1)}) custom-call(s32[6]{0:T(128)S(1)} %pad_add_fusion.switch_ref, bf16[128,8192]{1,0:T(8,128)(2,1)S(1)} %get-tuple-element.27.plain_ref, bf16[128,8192]{1,0:T(8,128)(2,1)S(1)} %copy-done.1, ...), custom_call_target="tpu_custom_call" | custom-call | flops 1509949440 | bytes 3932160 | tf_op jit(solution)/shard_map/second_last/pallas_call | solution.py:253
  66.9 1.3 %collective-permute-start.8 = (bf16[9,128,128]{2,1,0:T(8,128)(2,1)S(1)}, bf16[9,128,128]{2,1,0:T(8,128)(2,1)S(1)}, u32[]{:S(2)}, u32[]{:S(2)}) collective-permute-start(bf16[9,128,128]{2,1,0:T(8,128)(2,1)S(1)} %get-tuple-element.41), channel_id=1, source_target_pairs={{0,8},{12,4},{14,6},{7,15},{9,1},{2,10},{11,3},{5,13},{1,0},{16,24... | collective-permute-start | bytes 884744 | tf_op jit(solution)/shard_map/ppermute | solution.py:330
  68.2 7.0 %collective-permute-done.8 = bf16[9,128,128]{2,1,0:T(8,128)(2,1)S(1)} collective-permute-done((bf16[9,128,128]{2,1,0:T(8,128)(2,1)S(1)}, bf16[9,128,128]{2,1,0:T(8,128)(2,1)S(1)}, u32[]{:S(2)}, u32[]{:S(2)}) %collective-permute-start.8) | collective-permute-done | bytes 294944 | tf_op jit(solution)/shard_map/ppermute | solution.py:330
  75.2 0.9 %select_bitcast_fusion = (bf16[1,9,128,128]{3,2,1,0:T(8,128)(2,1)}, bf16[1,9,128,128]{3,2,1,0:T(8,128)(2,1)}) fusion(bf16[9,128,128]{2,1,0:T(8,128)(2,1)S(1)} %collective-permute-done.8, bf16[9,128,128]{2,1,0:T(8,128)(2,1)S(1)} %get-tuple-element.43, pred[]{:T(512)S(6)} %or.59, bf16[9,128,128]{2,1,0:T(8,128)(2,1)S(1)} %get-tuple-element.42, pred[]{:T(512)} %eq.53), kind=kLoop, calls=%fused_computation | loop fusion | flops 294912 | bytes 1474562 | tf_op jit(solution)/shard_map/broadcast_in_dim | solution.py:333
  (30 shorter events, 0.9 us)
Async XLA Ops:
  0.6 14.2 %copy-start.5 = (s32[2]{0:T(128)S(1)}, s32[2]{0:T(128)}, u32[]{:S(2)}) copy-start(s32[2]{0:T(128)} %constant.58.clone.1.active_ref) | copy-start | bytes 28
  0.6 22.2 %collective-permute-start.3 = (bf16[8192,128]{1,0:T(8,128)(2,1)}, bf16[8192,128]{1,0:T(8,128)(2,1)}, u32[]{:S(2)}, u32[]{:S(2)}) collective-permute-start(bf16[8192,128]{1,0:T(8,128)(2,1)} %bitcast.15), channel_id=1, source_target_pairs={{3,2},{5,4},{6,5},{9,8},{10,9},{11,10},{12,11},{13,12},{14,13},{15... | collective-permute-start | bytes 6291464 | tf_op jit(solution)/shard_map/ppermute | solution.py:303
  4.5 18.4 %collective-permute-start.4 = (bf16[8192,128]{1,0:T(8,128)(2,1)}, bf16[8192,128]{1,0:T(8,128)(2,1)}, u32[]{:S(2)}, u32[]{:S(2)}) collective-permute-start(bf16[8192,128]{1,0:T(8,128)(2,1)} %bitcast.16), channel_id=1, source_target_pairs={{8,0},{4,12},{6,14},{15,7},{0,1},{7,6},{24,16},{20,28},{22,30},{31... | collective-permute-start | bytes 6291464 | tf_op jit(solution)/shard_map/ppermute | solution.py:304
  6.5 27.0 %collective-permute-start.1 = (s32[1,4]{1,0:T(1,128)}, s32[1,4]{1,0:T(1,128)S(1)}, u32[]{:S(2)}, u32[]{:S(2)}) collective-permute-start(s32[1,4]{1,0:T(1,128)} %param.3), channel_id=1, source_target_pairs={{3,2},{5,4},{6,5},{9,8},{10,9},{11,10},{12,11},{13,12},{14,13},{15... | collective-permute-start | bytes 56 | tf_op jit(solution)/shard_map/ppermute | solution.py:309
  7.8 25.7 %collective-permute-start.2 = (s32[1,4]{1,0:T(1,128)}, s32[1,4]{1,0:T(1,128)S(1)}, u32[]{:S(2)}, u32[]{:S(2)}) collective-permute-start(s32[1,4]{1,0:T(1,128)} %param.3), channel_id=1, source_target_pairs={{8,0},{4,12},{6,14},{15,7},{0,1},{7,6},{24,16},{20,28},{22,30},{31... | collective-permute-start | bytes 56 | tf_op jit(solution)/shard_map/ppermute | solution.py:308
  8.5 40.5 %collective-permute-start = (s32[1,4]{1,0:T(1,128)}, s32[1,4]{1,0:T(1,128)S(1)}, u32[]{:S(2)}, u32[]{:S(2)}) collective-permute-start(s32[1,4]{1,0:T(1,128)} %param.3), channel_id=1, source_target_pairs={{1,9},{10,2},{3,11},{13,5},{2,1},{4,3},{17,25},{26,18},{19,27},{29... | collective-permute-start | bytes 56 | tf_op jit(solution)/shard_map/ppermute | solution.py:310
  12.0 1.6 %copy-start.2 = (bf16[1024,2,4,128]{3,2,1,0:T(4,128)(2,1)S(1)}, bf16[1024,2,4,128]{3,2,1,0:T(4,128)(2,1)}, u32[]{:S(2)}) copy-start(bf16[1024,2,4,128]{3,2,1,0:T(4,128)(2,1)} %param.2) | copy-start | bytes 6291460
  13.6 1.9 %copy-start.3 = (bf16[1024,2,4,128]{3,2,1,0:T(4,128)(2,1)S(1)}, bf16[1024,2,4,128]{3,2,1,0:T(4,128)(2,1)}, u32[]{:S(2)}) copy-start(bf16[1024,2,4,128]{3,2,1,0:T(4,128)(2,1)} %param.2) | copy-start | bytes 6291460
  13.9 0.9 %copy-start.6 = (bf16[3072,128]{1,0:T(8,128)(2,1)}, bf16[3072,128]{1,0:T(8,128)(2,1)S(1)}, u32[]{:S(2)}) copy-start(bf16[3072,128]{1,0:T(8,128)(2,1)S(1)} %get-tuple-element.37) | copy-start | bytes 2359300
  14.8 18.7 %copy-start.7 = (s32[1,4]{1,0:T(1,128)S(1)}, s32[1,4]{1,0:T(1,128)}, u32[]{:S(2)}) copy-start(s32[1,4]{1,0:T(1,128)} %param.3) | copy-start | bytes 52
  19.5 1.3 %copy-start = (bf16[128,8192]{1,0:T(8,128)(2,1)}, bf16[128,8192]{1,0:T(8,128)(2,1)S(1)}, u32[]{:S(2)}) copy-start(bf16[128,8192]{1,0:T(8,128)(2,1)S(1)} %get-tuple-element.28.swapped_ref) | copy-start | bytes 6291460
  20.9 16.2 %copy-start.1 = (bf16[128,8192]{1,0:T(8,128)(2,1)S(1)}, bf16[128,8192]{1,0:T(8,128)(2,1)}, u32[]{:S(2)}) copy-start(bf16[128,8192]{1,0:T(8,128)(2,1)} %copy-done) | copy-start | bytes 6291460
  22.9 38.9 %collective-permute-start.5 = (bf16[5120,128]{1,0:T(8,128)(2,1)S(1)}, bf16[5120,128]{1,0:T(8,128)(2,1)S(1)}, u32[]{:S(2)}, u32[]{:S(2)}) collective-permute-start(bf16[5120,128]{1,0:T(8,128)(2,1)S(1)} %get-tuple-element.36), channel_id=1, source_target_pairs={{1,9},{10,2},{3,11},{13,5},{2,1},{4,3},{17,25},{26,18},{19,27},{29... | collective-permute-start | bytes 3932168 | tf_op jit(solution)/shard_map/ppermute | solution.py:318
  33.6 24.9 %collective-permute-start.6 = (bf16[3072,128]{1,0:T(8,128)(2,1)}, bf16[3072,128]{1,0:T(8,128)(2,1)S(1)}, u32[]{:S(2)}, u32[]{:S(2)}) collective-permute-start(bf16[3072,128]{1,0:T(8,128)(2,1)} %copy-done.6), channel_id=1, source_target_pairs={{1,9},{10,2},{3,11},{13,5},{2,1},{4,3},{17,25},{26,18},{19,27},{29... | collective-permute-start | bytes 2359304 | tf_op jit(solution)/shard_map/ppermute | solution.py:318
  37.1 1.6 %copy-start.4 = (bf16[1024,2,4,128]{3,2,1,0:T(4,128)(2,1)S(1)}, bf16[1024,2,4,128]{3,2,1,0:T(4,128)(2,1)}, u32[]{:S(2)}) copy-start(bf16[1024,2,4,128]{3,2,1,0:T(4,128)(2,1)} %param.2) | copy-start | bytes 6291460
  48.3 0.8 %collective-permute-start.7 = (bf16[9,128,128]{2,1,0:T(8,128)(2,1)S(1)}, bf16[9,128,128]{2,1,0:T(8,128)(2,1)S(1)}, u32[]{:S(2)}, u32[]{:S(2)}) collective-permute-start(bf16[9,128,128]{2,1,0:T(8,128)(2,1)S(1)} %get-tuple-element.39), channel_id=1, source_target_pairs={{0,7},{7,15},{16,23},{23,31}} | collective-permute-start | bytes 884744 | tf_op jit(solution)/shard_map/ppermute | solution.py:321
  66.9 8.4 %collective-permute-start.8 = (bf16[9,128,128]{2,1,0:T(8,128)(2,1)S(1)}, bf16[9,128,128]{2,1,0:T(8,128)(2,1)S(1)}, u32[]{:S(2)}, u32[]{:S(2)}) collective-permute-start(bf16[9,128,128]{2,1,0:T(8,128)(2,1)S(1)} %get-tuple-element.41), channel_id=1, source_target_pairs={{0,8},{12,4},{14,6},{7,15},{9,1},{2,10},{11,3},{5,13},{1,0},{16,24... | collective-permute-start | bytes 884744 | tf_op jit(solution)/shard_map/ppermute | solution.py:330

commit v12 on v11

--- a/solution.py
+++ b/solution.py
@@ -28,35 +28,39 @@
     return jnp.concatenate([cos_part, sin_part], axis=0).astype(jnp.bfloat16)
 
 
-def split_kernel(middle, x_ref, first_ref, last_ref):
+def split_kernel(middle, windows, flags_ref, x_ref, first_ref, last_ref):
     step = pl.program_id(0)
+    masked = weigh(x_ref[...], [flags_ref[w] for w in range(windows)])
 
     @pl.when(step < middle)
     def _():
-        first_ref[...] = x_ref[...]
+        first_ref[...] = masked
 
     @pl.when(step >= middle)
     def _():
-        last_ref[...] = x_ref[...]
-
-
-def split(x):
+        last_ref[...] = masked
+
+
+def split(flags, x):
     rows, cols = x.shape
     steps = rows // STEP
     middle = steps * PARTS[0] // PARTS[1]
     return pl.pallas_call(
-        functools.partial(split_kernel, middle),
-        grid=(steps,),
-        in_specs=[pl.BlockSpec((STEP, cols), lambda s: (s, 0))],
-        out_specs=[
-            pl.BlockSpec((STEP, cols), lambda s: (jnp.minimum(s, middle - 1), 0)),
-            pl.BlockSpec((STEP, cols), lambda s: (jnp.maximum(s - middle, 0), 0)),
-        ],
+        functools.partial(split_kernel, middle, flags.shape[0]),
+        grid_spec=pltpu.PrefetchScalarGridSpec(
+            num_scalar_prefetch=1,
+            grid=(steps,),
+            in_specs=[pl.BlockSpec((STEP, cols), lambda s, on: (s, 0))],
+            out_specs=[
+                pl.BlockSpec((STEP, cols), lambda s, on: (jnp.minimum(s, middle - 1), 0)),
+                pl.BlockSpec((STEP, cols), lambda s, on: (jnp.maximum(s - middle, 0), 0)),
+            ],
+        ),
         out_shape=[jax.ShapeDtypeStruct((n * STEP, cols), x.dtype) for n in (middle, steps - middle)],
         compiler_params=PARAMS,
-        cost_estimate=pl.CostEstimate(flops=0, bytes_accessed=4 * rows * cols, transcendentals=0),
+        cost_estimate=pl.CostEstimate(flops=rows * cols, bytes_accessed=4 * rows * cols, transcendentals=0),
         name="split",
-    )(x)
+    )(flags, x)
 
 
 def turn_kernel(active_ref, x_ref, plain_ref, swapped_ref):
@@ -125,11 +129,11 @@
     return x * weights.reshape(rows, cols)
 
 
-def first_kernel(windows, switch_ref, plain_ref, swapped_ref, plain_alt, swapped_alt, coeff_ref, near_ref, first_ref,
-                 own_ref, near_out, far_out, back_out, acc, scaled):
+def first_kernel(windows, switch_ref, plain_ref, swapped_ref, plain_alt, swapped_alt, coeff_ref, near_ref, near_alt,
+                 first_ref, own_ref, near_out, far_out, back_out, acc, scaled):
     step = pl.program_id(0)
     cols = plain_ref.shape[0]
-    near_mirrored, special = switch_ref[0], switch_ref[1]
+    near_mirrored, special, near_second = switch_ref[0], switch_ref[1], switch_ref[2]
 
     @pl.when(step == 0)
     def _():
@@ -138,9 +142,9 @@
     plain = jnp.where(special != 0, plain_alt[...], plain_ref[...])
     swapped = jnp.where(special != 0, swapped_alt[...], swapped_ref[...])
     scale(scaled, plain, swapped, coeff_ref)
-    flags = [[switch_ref[2 + part * windows + w] for w in range(windows)] for part in range(3)]
+    flags = [[switch_ref[3 + part * windows + w] for w in range(windows)] for part in range(3)]
     near_weights = [jnp.where(special != 0, first, own) * near for own, near, first in zip(*flags)]
-    near = weigh(near_ref[...], near_weights)
+    near = weigh(jnp.where(near_second != 0, near_alt[...], near_ref[...]), near_weights)
     far = weigh(jnp.where(special != 0, own_ref[...], first_ref[...]), [own * first for own, _, first in zip(*flags)])
     acc[...] += jnp.dot(scaled[...], jnp.concatenate([near, far], axis=1), preferred_element_type=jnp.float32)
 
@@ -162,13 +166,14 @@
         pl.when(near_mirrored != 0)(lambda: write_lags(near_out, acc, near_at, cols, True))
 
 
-def first_sums(switch, own, alt, coeffs, near_in, first_in, block):
+def first_sums(switch, own, alt, coeffs, near_in, near_alt, first_in, block):
     rows, cols = block.shape
-    windows = (switch.shape[0] - 2) // 3
+    windows = (switch.shape[0] - 3) // 3
     result = jax.ShapeDtypeStruct((LAGS, cols, cols), jnp.bfloat16)
     left = pl.BlockSpec((cols, STEP), lambda s, on: (0, s * (1 - on[1])))
     left_alt = pl.BlockSpec((cols, STEP), lambda s, on: (0, s * on[1]))
-    right = pl.BlockSpec((STEP, cols), lambda s, on: (s, 0))
+    right_near = pl.BlockSpec((STEP, cols), lambda s, on: (s * (1 - on[2]), 0))
+    right_near_alt = pl.BlockSpec((STEP, cols), lambda s, on: (s * on[2], 0))
     right_usual = pl.BlockSpec((STEP, cols), lambda s, on: (s * (1 - on[1]), 0))
     right_special = pl.BlockSpec((STEP, cols), lambda s, on: (s * on[1], 0))
     return pl.pallas_call(
@@ -177,7 +182,7 @@
             num_scalar_prefetch=1,
             grid=(rows // STEP,),
             in_specs=[left, left, left_alt, left_alt, pl.BlockSpec((LAGS, STEP), lambda s, on: (0, s)),
-                      right, right_usual, right_special],
+                      right_near, right_near_alt, right_usual, right_special],
             out_specs=[pl.BlockSpec(result.shape, lambda s, on: (0, 0, 0))] * 3,
             scratch_shapes=[pltpu.VMEM((LAGS * cols, 2 * cols), jnp.float32),
                             pltpu.VMEM((LAGS * cols, STEP), jnp.bfloat16)],
@@ -188,19 +193,18 @@
             flops=4 * LAGS * cols * cols * rows, bytes_accessed=8 * rows * cols, transcendentals=0
         ),
         name="first_sums",
-    )(switch, *own, *alt, coeffs, near_in, first_in, block)
+    )(switch, *own, *alt, coeffs, near_in, near_alt, first_in, block)
 
 
 def second_kernel(windows, first, switch_ref, plain_ref, swapped_ref, coeff_ref, partner_ref, *rest):
-    on, late_near = switch_ref[0], switch_ref[1]
     step = pl.program_id(0)
     cols = plain_ref.shape[0]
     if first:
         acc, scaled = rest
     else:
-        acc_in, near_in, far_in, back_in, near_out, far_out, back_out, acc, scaled = rest
-
-    @pl.when(on != 0)
+        acc_in, far_in, back_in, far_out, back_out, acc, scaled = rest
+
+    @pl.when(switch_ref[0] != 0)
     def _():
         @pl.when(step == 0)
         def _():
@@ -215,26 +219,19 @@
         def _():
             here = slice(0, cols)
 
-            @pl.when((on != 0) & (late_near == 0))
+            @pl.when(switch_ref[0] != 0)
             def _():
                 write_lags(back_out, acc, here, cols, True)
                 write_lags(far_out, acc, here, cols, False)
 
-            @pl.when((on == 0) | (late_near != 0))
+            @pl.when(switch_ref[0] == 0)
             def _():
                 back_out[...] = back_in[...]
                 far_out[...] = far_in[...]
 
-            pl.when(late_near != 0)(lambda: write_lags(near_out, acc, here, cols, False))
-
-            @pl.when(late_near == 0)
-            def _():
-                near_out[...] = near_in[...]
-
 
 def second_sums(switch, own, coeffs, partner, start, earlier=None):
     rows, cols = partner.shape
-    windows = switch.shape[0] - 2
     skip = start // STEP
     total = jax.ShapeDtypeStruct((LAGS * cols, cols), jnp.float32)
     total_spec = pl.BlockSpec(total.shape, lambda s, on: (0, 0))
@@ -247,11 +244,11 @@
     if earlier is None:
         out_shape, out_specs, earlier = [total], [total_spec], []
     else:
-        out_shape, out_specs = [result] * 3, [result_spec] * 3
-        in_specs += [total_spec] + [result_spec] * 3
+        out_shape, out_specs = [result] * 2, [result_spec] * 2
+        in_specs += [total_spec] + [result_spec] * 2
         scratch = [pltpu.VMEM(total.shape, jnp.float32)] + scratch
     return pl.pallas_call(
-        functools.partial(second_kernel, windows, not earlier),
+        functools.partial(second_kernel, switch.shape[0] - 2, not earlier),
         grid_spec=pltpu.PrefetchScalarGridSpec(
             num_scalar_prefetch=1,
             grid=(rows // STEP,),
@@ -266,6 +263,47 @@
         ),
         name="second_last" if earlier else "second_part",
     )(switch, *own, coeffs, partner, *earlier)
+
+
+def late_kernel(windows, middle, switch_ref, plain_ref, swapped_ref, coeff_ref, first_ref, last_ref, near_out, acc, scaled):
+    step = pl.program_id(0)
+    cols = plain_ref.shape[0]
+
+    @pl.when(switch_ref[0] != 0)
+    def _():
+        @pl.when(step == 0)
+        def _():
+            acc[...] = jnp.zeros_like(acc)
+
+        scale(scaled, plain_ref[...], swapped_ref[...], coeff_ref)
+        partner = jnp.where(step < middle, first_ref[...], last_ref[...])
+        partner = weigh(partner, [switch_ref[2 + w] for w in range(windows)])
+        acc[...] += jnp.dot(scaled[...], partner, preferred_element_type=jnp.float32)
+        pl.when(step == pl.num_programs(0) - 1)(lambda: write_lags(near_out, acc, slice(0, cols), cols, False))
+
+
+def late_sums(switch, own, coeffs, parts):
+    cols, rows = own[0].shape
+    middle = parts[0].shape[0] // STEP
+    left = pl.BlockSpec((cols, STEP), lambda s, on: (0, s * on[0]))
+    result = jax.ShapeDtypeStruct((LAGS, cols, cols), jnp.bfloat16)
+    return pl.pallas_call(
+        functools.partial(late_kernel, switch.shape[0] - 2, middle),
+        grid_spec=pltpu.PrefetchScalarGridSpec(
+            num_scalar_prefetch=1,
+            grid=(rows // STEP,),
+            in_specs=[left, left, pl.BlockSpec((LAGS, STEP), lambda s, on: (0, s * on[0])),
+                      pl.BlockSpec((STEP, cols), lambda s, on: (jnp.minimum(s, middle - 1) * on[0], 0)),
+                      pl.BlockSpec((STEP, cols), lambda s, on: (jnp.maximum(s - middle, 0) * on[0], 0))],
+            out_specs=pl.BlockSpec(result.shape, lambda s, on: (0, 0, 0)),
+            scratch_shapes=[pltpu.VMEM((LAGS * cols, cols), jnp.float32),
+                            pltpu.VMEM((LAGS * cols, STEP), jnp.bfloat16)],
+        ),
+        out_shape=result,
+        compiler_params=PARAMS,
+        cost_estimate=pl.CostEstimate(flops=0, bytes_accessed=0, transcendentals=0),
+        name="late_near",
+    )(switch, *own, coeffs, *parts)
 
 
 def local(spectra, quality):
@@ -290,6 +328,9 @@
     second_pairs = second_far + late_near
     near_pairs = [(d + 1, d) for d in range(1, count - 1) if d not in (1, 3, half - 2, half - 1)]
     near_pairs += [(0, half - 1), (half - 1, 0)]
+    receivers = {t for _, t in first_far}
+    later_pairs = [pair for pair in near_pairs if receivers.intersection(pair)]
+    early_pairs = [pair for pair in near_pairs if not receivers.intersection(pair)]
     back_pairs = [(t, s) for s, t in first_far + second_far] + [(1, 0)]
     side_pairs = [(0, half - 1), (half - 1, count - 1)]
 
@@ -300,34 +341,39 @@
         flags = jnp.stack([jnp.asarray(on), jnp.asarray(other)]).astype(jnp.int32)
         return jnp.concatenate([flags, *weights])
 
-    near_in = lax.ppermute(block, "chan", near_pairs)
+    near_in = lax.ppermute(block, "chan", early_pairs)
     first_in = lax.ppermute(block, "chan", first_pairs)
+    near_alt = lax.ppermute(block, "chan", later_pairs)
     coeffs = lag_rows(freq_count, window_count)
     own = turn(block, switch(True, False), "turn_own")
-    parts = split(block)
+    parts = split(quality[0], block)
     first_flags = lax.ppermute(quality, "chan", first_pairs)[0]
     near_flags = lax.ppermute(quality, "chan", near_pairs)[0]
-    second_flags = lax.ppermute(quality, "chan", second_pairs)[0]
     special = among([0, half - 1])
-    first_switch = switch(me == 0, special, quality[0], near_flags, first_flags)
-    second_switch = switch(
-        among([t for _, t in second_pairs]), among([t for _, t in late_near]), quality[0] * second_flags
+    near_later = among([t for _, t in later_pairs])
+    first_switch = jnp.concatenate(
+        [jnp.stack([me == 0, special, near_later]).astype(jnp.int32), quality[0], near_flags, first_flags]
     )
-
-    near_in, parts, own, coeffs, first_in = lax.optimization_barrier((near_in, parts, own, coeffs, first_in))
+    second_switch = switch(among([t for _, t in second_far]), False, quality[0])
+    late_switch = switch(among([t for _, t in late_near]), False, quality[0])
+
+    near_in, first_in, near_alt, parts, own, coeffs, first_switch = lax.optimization_barrier(
+        (near_in, first_in, near_alt, parts, own, coeffs, first_switch)
+    )
     second_in = [lax.ppermute(part, "chan", second_pairs) for part in parts]
     alt = turn(first_in, switch(special, False), "turn_first", common=False)
-    near, far, back = first_sums(first_switch, own, alt, coeffs, near_in, first_in, block)
+    near, far, back = first_sums(first_switch, own, alt, coeffs, near_in, near_alt, first_in, block)
     side_returned = lax.ppermute(near, "chan", side_pairs)
     second_switch, near = lax.optimization_barrier((second_switch, near))
     total, = second_sums(second_switch, own, coeffs, second_in[0], 0)
+    far, back = second_sums(second_switch, own, coeffs, second_in[1], parts[0].shape[0], [total, far, back])
+    returned = lax.ppermute(back, "chan", back_pairs)
+    late_switch, far = lax.optimization_barrier((late_switch, far))
+    late = late_sums(late_switch, own, coeffs, second_in)
 
     near = jnp.where(among([half - 1, count - 1]), side_returned, near)
     near = jnp.where(me == half - 2, far, near)
-    near, far, back = second_sums(
-        second_switch, own, coeffs, second_in[1], parts[0].shape[0], [total, near, far, back]
-    )
-    returned = lax.ppermute(back, "chan", back_pairs)
+    near = jnp.where(among([t for _, t in late_near]), late, near)
     near = jnp.where(me == 0, returned, near)
     far = jnp.where(among([s for s, _ in first_far + second_far]), returned, far)
     return near[None], far[None]

time: 76.7 us -> 107 us (1.40)
  the two profiles are of different devices: /device:TPU:5 before, /device:TPU:1 now
where the time goes in v12:
time: 107 us; the launch traced here: 106 us
  starting transfers between devices  50.7 us (47%)
  Pallas kernels  29 us (27%)
  local copies, waits for them, and re-layouts  11.6 us (11%)
  waiting for transfers between devices  8.76 us (8%)
  other arithmetic  4.98 us (5%)
    ppermute x1, starting transfers between devices, local(): returned = lax.ppermute(back, 'chan', back_pairs)  25.8 us
    ppermute x2, starting transfers between devices, local(): second_in = [lax.ppermute(part, 'chan', second_pairs) for part in parts]  16.2 us
    unnamed x32, local copies, waits for them, and re-layouts  11.6 us
    pallas_call x1, Pallas kernels, first_sums(): pl.pallas_call(functools.partial(first_kernel, windows), grid_spec=pltpu....  10.5 us
    ppermute x2, waiting for transfers between devices, local(): second_in = [lax.ppermute(part, 'chan', second_pairs) for part in parts]  8.74 us
    pallas_call x1, Pallas kernels, late_sums(): pl.pallas_call(functools.partial(late_kernel, switch.shape[0] - 2, middle...  7.56 us
    pallas_call x2, Pallas kernels, turn(): pl.pallas_call(turn_kernel, grid_spec=pltpu.PrefetchScalarGridSpec(num_sc...  5.52 us
    pallas_call x1, Pallas kernels, split(): pl.pallas_call(functools.partial(split_kernel, middle, flags.shape[0]), g...  3.14 us
  transfers between devices with their start and end apart: 9, of which 1 were waited for; matrix products, arithmetic and copies ran while one was open for 3% of the time, Pallas kernels for 27%

profile of v12, /device:TPU:1, one launch (start us, length us, event | category | flops | bytes accessed | tf_op | source)
XLA Modules:
  0.0 105.9 jit_solution(8723057095753404567)
XLA Ops:
  1.3 1.3 %collective-permute-start.4 = (s32[1,4]{1,0:T(1,128)}, s32[1,4]{1,0:T(1,128)S(1)}, u32[]{:S(2)}, u32[]{:S(2)}) collective-permute-start(s32[1,4]{1,0:T(1,128)} %param.3), channel_id=1, source_target_pairs={{8,0},{4,12},{6,14},{15,7},{0,1},{7,6},{24,16},{20,28},{22,30},{31... | collective-permute-start | bytes 56 | tf_op jit(solution)/shard_map/ppermute | solution.py:350
  2.6 2.1 %collective-permute-start = (bf16[8192,128]{1,0:T(8,128)(2,1)}, bf16[8192,128]{1,0:T(8,128)(2,1)}, u32[]{:S(2)}, u32[]{:S(2)}) collective-permute-start(bf16[8192,128]{1,0:T(8,128)(2,1)} %bitcast.13), channel_id=1, source_target_pairs={{3,2},{5,4},{6,5},{9,8},{10,9},{11,10},{19,18},{21,20},{22,21},{25... | collective-permute-start | bytes 6291464 | tf_op jit(solution)/shard_map/ppermute | solution.py:344
  4.7 1.3 %collective-permute-start.1 = (bf16[8192,128]{1,0:T(8,128)(2,1)}, bf16[8192,128]{1,0:T(8,128)(2,1)}, u32[]{:S(2)}, u32[]{:S(2)}) collective-permute-start(bf16[8192,128]{1,0:T(8,128)(2,1)} %bitcast.14), channel_id=1, source_target_pairs={{8,0},{4,12},{6,14},{15,7},{0,1},{7,6},{24,16},{20,28},{22,30},{31... | collective-permute-start | bytes 6291464 | tf_op jit(solution)/shard_map/ppermute | solution.py:345
  5.9 2.1 %collective-permute-start.2 = (bf16[8192,128]{1,0:T(8,128)(2,1)}, bf16[8192,128]{1,0:T(8,128)(2,1)}, u32[]{:S(2)}, u32[]{:S(2)}) collective-permute-start(bf16[8192,128]{1,0:T(8,128)(2,1)} %bitcast.15), channel_id=1, source_target_pairs={{12,11},{13,12},{14,13},{15,14},{0,7},{7,0},{28,27},{29,28},{30,29... | collective-permute-start | bytes 6291464 | tf_op jit(solution)/shard_map/ppermute | solution.py:346
  8.1 1.6 %copy-done.3 = bf16[1024,2,4,128]{3,2,1,0:T(4,128)(2,1)S(1)} copy-done((bf16[1024,2,4,128]{3,2,1,0:T(4,128)(2,1)S(1)}, bf16[1024,2,4,128]{3,2,1,0:T(4,128)(2,1)}, u32[]{:S(2)}) %copy-start.3) | copy-done | bytes 2097176
  10.3 3.1 %split.1 = (bf16[3072,128]{1,0:T(8,128)(2,1)S(1)}, bf16[5120,128]{1,0:T(8,128)(2,1)}) custom-call(s32[4]{0:T(128)S(1)} %bitcast.19, bf16[8192,128]{1,0:T(8,128)(2,1)S(1)} %bitcast.16), custom_call_target="tpu_custom_call" | custom-call | flops 1048576 | bytes 4194304 | tf_op jit(solution)/shard_map/split/pallas_call | solution.py:48
  14.4 3.9 %turn_own.1 = (bf16[128,8192]{1,0:T(8,128)(2,1)S(1)}, bf16[128,8192]{1,0:T(8,128)(2,1)S(1)}) custom-call(s32[2]{0:T(128)S(1)} %copy-done.14, bf16[8192,128]{1,0:T(8,128)(2,1)S(1)} %bitcast.17), custom_call_target="tpu_custom_call" | custom-call | bytes 6291456 | tf_op jit(solution)/shard_map/turn_own/pallas_call | solution.py:86
  18.3 1.3 %copy-done = bf16[128,8192]{1,0:T(8,128)(2,1)} copy-done((bf16[128,8192]{1,0:T(8,128)(2,1)}, bf16[128,8192]{1,0:T(8,128)(2,1)S(1)}, u32[]{:S(2)}) %copy-start) | copy-done | bytes 2097176
  19.7 0.9 multiply_convert_fusion
  22.5 14.1 %collective-permute-start.5 = (bf16[5120,128]{1,0:T(8,128)(2,1)}, bf16[5120,128]{1,0:T(8,128)(2,1)S(1)}, u32[]{:S(2)}, u32[]{:S(2)}) collective-permute-start(bf16[5120,128]{1,0:T(8,128)(2,1)} %get-tuple-element.41), channel_id=1, source_target_pairs={{1,9},{10,2},{3,11},{13,5},{2,1},{4,3},{17,25},{26,18},{19,27},{29... | collective-permute-start | bytes 3932168 | tf_op jit(solution)/shard_map/ppermute | solution.py:363
  36.7 2.1 %collective-permute-start.6 = (bf16[3072,128]{1,0:T(8,128)(2,1)}, bf16[3072,128]{1,0:T(8,128)(2,1)S(1)}, u32[]{:S(2)}, u32[]{:S(2)}) collective-permute-start(bf16[3072,128]{1,0:T(8,128)(2,1)} %copy-done.15), channel_id=1, source_target_pairs={{1,9},{10,2},{3,11},{13,5},{2,1},{4,3},{17,25},{26,18},{19,27},{29... | collective-permute-start | bytes 2359304 | tf_op jit(solution)/shard_map/ppermute | solution.py:363
  39.0 1.6 %turn_first.1 = (bf16[128,8192]{1,0:T(8,128)(2,1)S(1)}, bf16[128,8192]{1,0:T(8,128)(2,1)S(1)}) custom-call(s32[2]{0:T(128)S(1)} %get-tuple-element.57.active_ref, bf16[8192,128]{1,0:T(8,128)(2,1)} %collective-permute-done.1.x_ref.first_ref), custom_call_target="tpu_custom_call" | custom-call | tf_op jit(solution)/shard_map/turn_first/pallas_call | solution.py:86
  40.6 1.6 %copy-done.5 = bf16[1024,2,4,128]{3,2,1,0:T(4,128)(2,1)S(1)} copy-done((bf16[1024,2,4,128]{3,2,1,0:T(4,128)(2,1)S(1)}, bf16[1024,2,4,128]{3,2,1,0:T(4,128)(2,1)}, u32[]{:S(2)}) %copy-start.5) | copy-done | bytes 2097176
  42.1 0.9 copy-done.6
  43.1 10.5 %first_sums.1 = (bf16[9,128,128]{2,1,0:T(8,128)(2,1)}, bf16[9,128,128]{2,1,0:T(8,128)(2,1)S(1)}, bf16[9,128,128]{2,1,0:T(8,128)(2,1)S(1)}) custom-call(s32[15]{0:T(128)S(1)} %pad_add_fusion.4.switch_ref, bf16[128,8192]{1,0:T(8,128)(2,1)S(1)} %get-tuple-element.31.plain_ref, bf16[128,8192]{1,0:T(8,128)(2,1)S(1)} %copy-done.1, ...), custom_call_target="tpu_custom_call" | custom-call | flops 4831838208 | bytes 8388608 | tf_op jit(solution)/shard_map/first_sums/pallas_call | solution.py:179
  53.5 1.4 %collective-permute-start.8 = (bf16[9,128,128]{2,1,0:T(8,128)(2,1)}, bf16[9,128,128]{2,1,0:T(8,128)(2,1)}, u32[]{:S(2)}, u32[]{:S(2)}) collective-permute-start(bf16[9,128,128]{2,1,0:T(8,128)(2,1)} %get-tuple-element.49), channel_id=1, source_target_pairs={{0,7},{7,15},{16,23},{23,31}} | collective-permute-start | bytes 884744 | tf_op jit(solution)/shard_map/ppermute | solution.py:366
  54.9 8.7 %collective-permute-done.6.partner_ref.first_ref = bf16[3072,128]{1,0:T(8,128)(2,1)S(1)} collective-permute-done((bf16[3072,128]{1,0:T(8,128)(2,1)}, bf16[3072,128]{1,0:T(8,128)(2,1)S(1)}, u32[]{:S(2)}, u32[]{:S(2)}) %collective-permute-start.6) | collective-permute-done | bytes 786464 | tf_op jit(solution)/shard_map/ppermute | solution.py:363
  64.5 1.6 %second_last.1 = (bf16[9,128,128]{2,1,0:T(8,128)(2,1)S(1)}, bf16[9,128,128]{2,1,0:T(8,128)(2,1)}) custom-call(s32[6]{0:T(128)S(1)} %get-tuple-element.40.switch_ref, bf16[128,8192]{1,0:T(8,128)(2,1)S(1)} %get-tuple-element.31.plain_ref, bf16[128,8192]{1,0:T(8,128)(2,1)S(1)} %copy-done.1, bf16[9,8192]{1,0:T(8,128)(2,1)S(1)} %copy-done.6, ...), custom_call_target="tpu_custom_call" | custom-call | flops 1509949440 | bytes 3932160 | tf_op jit(solution)/shard_map/second_last/pallas_call | solution.py:250
  66.8 25.8 %collective-permute-start.7 = (bf16[9,128,128]{2,1,0:T(8,128)(2,1)}, bf16[9,128,128]{2,1,0:T(8,128)(2,1)}, u32[]{:S(2)}, u32[]{:S(2)}) collective-permute-start(bf16[9,128,128]{2,1,0:T(8,128)(2,1)} %get-tuple-element.45), channel_id=1, source_target_pairs={{0,8},{12,4},{14,6},{7,15},{9,1},{2,10},{11,3},{5,13},{1,0},{16,24... | collective-permute-start | bytes 884744 | tf_op jit(solution)/shard_map/ppermute | solution.py:370
  92.7 1.6 %copy-done.2 = bf16[128,8192]{1,0:T(8,128)(2,1)S(1)} copy-done((bf16[128,8192]{1,0:T(8,128)(2,1)S(1)}, bf16[128,8192]{1,0:T(8,128)(2,1)}, u32[]{:S(2)}) %copy-start.2) | copy-done | bytes 2097176
  94.3 0.9 copy-done.7
  95.3 1.1 %copy-done.9 = bf16[3072,128]{1,0:T(8,128)(2,1)S(1)} copy-done((bf16[3072,128]{1,0:T(8,128)(2,1)S(1)}, bf16[3072,128]{1,0:T(8,128)(2,1)}, u32[]{:S(2)}) %copy-start.9) | copy-done | bytes 786456
  96.4 7.6 %late_near.1 = bf16[9,128,128]{2,1,0:T(8,128)(2,1)S(1)} custom-call(s32[6]{0:T(128)S(1)} %get-tuple-element.47.switch_ref, bf16[128,8192]{1,0:T(8,128)(2,1)S(1)} %get-tuple-element.31.plain_ref, bf16[128,8192]{1,0:T(8,128)(2,1)S(1)} %copy-done.2, bf16[9,8192]{1,0:T(8,128)(2,1)S(1)} %copy-done.7, bf16[3072,128]{1,0:T(8,128)(2,1)S(1)} %copy-done.9, ...), custom_call_target="tpu_custom_call" | custom-call | tf_op jit(solution)/shard_map/late_near/pallas_call | solution.py:290
  104.0 1.9 %select_bitcast_fusion = (bf16[1,9,128,128]{3,2,1,0:T(8,128)(2,1)}, bf16[1,9,128,128]{3,2,1,0:T(8,128)(2,1)}) fusion(bf16[9,128,128]{2,1,0:T(8,128)(2,1)} %collective-permute-done.7, bf16[9,128,128]{2,1,0:T(8,128)(2,1)S(1)} %copy-done.11, pred[]{:T(512)S(6)} %or.72, bf16[9,128,128]{2,1,0:T(8,128)(2,1)S(1)} %late_near.1, ...), kind=kLoop, calls=%fused_computation | loop fusion | flops 737280 | bytes 2064389 | tf_op jit(solution)/shard_map/broadcast_in_dim | solution.py:379
  (45 shorter events, 6.0 us)
Async XLA Ops:
  0.6 13.8 %copy-start.14 = (s32[2]{0:T(128)S(1)}, s32[2]{0:T(128)}, u32[]{:S(2)}) copy-start(s32[2]{0:T(128)} %constant.31.clone.1.active_ref) | copy-start | bytes 28
  0.6 21.8 %collective-permute-start.3 = (s32[1,4]{1,0:T(1,128)}, s32[1,4]{1,0:T(1,128)S(1)}, u32[]{:S(2)}, u32[]{:S(2)}) collective-permute-start(s32[1,4]{1,0:T(1,128)} %param.3), channel_id=1, source_target_pairs={{3,2},{5,4},{6,5},{9,8},{10,9},{11,10},{12,11},{13,12},{14,13},{15... | collective-permute-start | bytes 56 | tf_op jit(solution)/shard_map/ppermute | solution.py:351
  1.3 21.1 %collective-permute-start.4 = (s32[1,4]{1,0:T(1,128)}, s32[1,4]{1,0:T(1,128)S(1)}, u32[]{:S(2)}, u32[]{:S(2)}) collective-permute-start(s32[1,4]{1,0:T(1,128)} %param.3), channel_id=1, source_target_pairs={{8,0},{4,12},{6,14},{15,7},{0,1},{7,6},{24,16},{20,28},{22,30},{31... | collective-permute-start | bytes 56 | tf_op jit(solution)/shard_map/ppermute | solution.py:350
  2.6 19.9 %collective-permute-start = (bf16[8192,128]{1,0:T(8,128)(2,1)}, bf16[8192,128]{1,0:T(8,128)(2,1)}, u32[]{:S(2)}, u32[]{:S(2)}) collective-permute-start(bf16[8192,128]{1,0:T(8,128)(2,1)} %bitcast.13), channel_id=1, source_target_pairs={{3,2},{5,4},{6,5},{9,8},{10,9},{11,10},{19,18},{21,20},{22,21},{25... | collective-permute-start | bytes 6291464 | tf_op jit(solution)/shard_map/ppermute | solution.py:344
  4.7 17.8 %collective-permute-start.1 = (bf16[8192,128]{1,0:T(8,128)(2,1)}, bf16[8192,128]{1,0:T(8,128)(2,1)}, u32[]{:S(2)}, u32[]{:S(2)}) collective-permute-start(bf16[8192,128]{1,0:T(8,128)(2,1)} %bitcast.14), channel_id=1, source_target_pairs={{8,0},{4,12},{6,14},{15,7},{0,1},{7,6},{24,16},{20,28},{22,30},{31... | collective-permute-start | bytes 6291464 | tf_op jit(solution)/shard_map/ppermute | solution.py:345
  5.9 16.5 %collective-permute-start.2 = (bf16[8192,128]{1,0:T(8,128)(2,1)}, bf16[8192,128]{1,0:T(8,128)(2,1)}, u32[]{:S(2)}, u32[]{:S(2)}) collective-permute-start(bf16[8192,128]{1,0:T(8,128)(2,1)} %bitcast.15), channel_id=1, source_target_pairs={{12,11},{13,12},{14,13},{15,14},{0,7},{7,0},{28,27},{29,28},{30,29... | collective-permute-start | bytes 6291464 | tf_op jit(solution)/shard_map/ppermute | solution.py:346
  8.1 1.6 %copy-start.3 = (bf16[1024,2,4,128]{3,2,1,0:T(4,128)(2,1)S(1)}, bf16[1024,2,4,128]{3,2,1,0:T(4,128)(2,1)}, u32[]{:S(2)}) copy-start(bf16[1024,2,4,128]{3,2,1,0:T(4,128)(2,1)} %param.2) | copy-start | bytes 6291460
  10.3 4.1 %copy-start.4 = (bf16[1024,2,4,128]{3,2,1,0:T(4,128)(2,1)S(1)}, bf16[1024,2,4,128]{3,2,1,0:T(4,128)(2,1)}, u32[]{:S(2)}) copy-start(bf16[1024,2,4,128]{3,2,1,0:T(4,128)(2,1)} %param.2) | copy-start | bytes 6291460
  13.5 0.9 copy-start.15
  14.4 24.5 %copy-start.13 = (s32[1,4]{1,0:T(1,128)S(1)}, s32[1,4]{1,0:T(1,128)}, u32[]{:S(2)}) copy-start(s32[1,4]{1,0:T(1,128)} %param.3) | copy-start | bytes 52
  18.3 1.4 %copy-start = (bf16[128,8192]{1,0:T(8,128)(2,1)}, bf16[128,8192]{1,0:T(8,128)(2,1)S(1)}, u32[]{:S(2)}) copy-start(bf16[128,8192]{1,0:T(8,128)(2,1)S(1)} %get-tuple-element.32.swapped_ref) | copy-start | bytes 6291460
  22.5 42.0 %collective-permute-start.5 = (bf16[5120,128]{1,0:T(8,128)(2,1)}, bf16[5120,128]{1,0:T(8,128)(2,1)S(1)}, u32[]{:S(2)}, u32[]{:S(2)}) collective-permute-start(bf16[5120,128]{1,0:T(8,128)(2,1)} %get-tuple-element.41), channel_id=1, source_target_pairs={{1,9},{10,2},{3,11},{13,5},{2,1},{4,3},{17,25},{26,18},{19,27},{29... | collective-permute-start | bytes 3932168 | tf_op jit(solution)/shard_map/ppermute | solution.py:363
  36.7 3.9 %copy-start.1 = (bf16[128,8192]{1,0:T(8,128)(2,1)S(1)}, bf16[128,8192]{1,0:T(8,128)(2,1)}, u32[]{:S(2)}) copy-start(bf16[128,8192]{1,0:T(8,128)(2,1)} %copy-done) | copy-start | bytes 6291460
  36.7 27.0 %collective-permute-start.6 = (bf16[3072,128]{1,0:T(8,128)(2,1)}, bf16[3072,128]{1,0:T(8,128)(2,1)S(1)}, u32[]{:S(2)}, u32[]{:S(2)}) collective-permute-start(bf16[3072,128]{1,0:T(8,128)(2,1)} %copy-done.15), channel_id=1, source_target_pairs={{1,9},{10,2},{3,11},{13,5},{2,1},{4,3},{17,25},{26,18},{19,27},{29... | collective-permute-start | bytes 2359304 | tf_op jit(solution)/shard_map/ppermute | solution.py:363
  40.5 1.6 %copy-start.5 = (bf16[1024,2,4,128]{3,2,1,0:T(4,128)(2,1)S(1)}, bf16[1024,2,4,128]{3,2,1,0:T(4,128)(2,1)}, u32[]{:S(2)}) copy-start(bf16[1024,2,4,128]{3,2,1,0:T(4,128)(2,1)} %param.2) | copy-start | bytes 6291460
  42.1 0.9 copy-start.6
  53.5 50.4 %collective-permute-start.8 = (bf16[9,128,128]{2,1,0:T(8,128)(2,1)}, bf16[9,128,128]{2,1,0:T(8,128)(2,1)}, u32[]{:S(2)}, u32[]{:S(2)}) collective-permute-start(bf16[9,128,128]{2,1,0:T(8,128)(2,1)} %get-tuple-element.49), channel_id=1, source_target_pairs={{0,7},{7,15},{16,23},{23,31}} | collective-permute-start | bytes 884744 | tf_op jit(solution)/shard_map/ppermute | solution.py:366
  63.7 0.9 copy-start.8
  66.1 0.7 copy-start.10
  66.8 37.1 %collective-permute-start.7 = (bf16[9,128,128]{2,1,0:T(8,128)(2,1)}, bf16[9,128,128]{2,1,0:T(8,128)(2,1)}, u32[]{:S(2)}, u32[]{:S(2)}) collective-permute-start(bf16[9,128,128]{2,1,0:T(8,128)(2,1)} %get-tuple-element.45), channel_id=1, source_target_pairs={{0,8},{12,4},{14,6},{7,15},{9,1},{2,10},{11,3},{5,13},{1,0},{16,24... | collective-permute-start | bytes 884744 | tf_op jit(solution)/shard_map/ppermute | solution.py:370
  92.7 1.6 %copy-start.2 = (bf16[128,8192]{1,0:T(8,128)(2,1)S(1)}, bf16[128,8192]{1,0:T(8,128)(2,1)}, u32[]{:S(2)}) copy-start(bf16[128,8192]{1,0:T(8,128)(2,1)} %copy-done) | copy-start | bytes 6291460
  94.3 0.9 copy-start.7
  95.3 1.1 %copy-start.9 = (bf16[3072,128]{1,0:T(8,128)(2,1)S(1)}, bf16[3072,128]{1,0:T(8,128)(2,1)}, u32[]{:S(2)}) copy-start(bf16[3072,128]{1,0:T(8,128)(2,1)} %copy-done.8) | copy-start | bytes 2359300
  96.4 7.6 %copy-start.11 = (bf16[9,128,128]{2,1,0:T(8,128)(2,1)S(1)}, bf16[9,128,128]{2,1,0:T(8,128)(2,1)}, u32[]{:S(2)}) copy-start(bf16[9,128,128]{2,1,0:T(8,128)(2,1)} %copy-done.10) | copy-start | bytes 884740
  (1 other events, 0.7 us)

commit v13 on v11

--- a/solution.py
+++ b/solution.py
@@ -192,15 +192,14 @@
 
 
 def second_kernel(windows, first, switch_ref, plain_ref, swapped_ref, coeff_ref, partner_ref, *rest):
-    on, late_near = switch_ref[0], switch_ref[1]
     step = pl.program_id(0)
     cols = plain_ref.shape[0]
     if first:
         acc, scaled = rest
     else:
-        acc_in, near_in, far_in, back_in, near_out, far_out, back_out, acc, scaled = rest
-
-    @pl.when(on != 0)
+        acc_in, far_in, back_in, far_out, back_out, acc, scaled = rest
+
+    @pl.when(switch_ref[0] != 0)
     def _():
         @pl.when(step == 0)
         def _():
@@ -215,26 +214,19 @@
         def _():
             here = slice(0, cols)
 
-            @pl.when((on != 0) & (late_near == 0))
+            @pl.when(switch_ref[0] != 0)
             def _():
                 write_lags(back_out, acc, here, cols, True)
                 write_lags(far_out, acc, here, cols, False)
 
-            @pl.when((on == 0) | (late_near != 0))
+            @pl.when(switch_ref[0] == 0)
             def _():
                 back_out[...] = back_in[...]
                 far_out[...] = far_in[...]
 
-            pl.when(late_near != 0)(lambda: write_lags(near_out, acc, here, cols, False))
-
-            @pl.when(late_near == 0)
-            def _():
-                near_out[...] = near_in[...]
-
 
 def second_sums(switch, own, coeffs, partner, start, earlier=None):
     rows, cols = partner.shape
-    windows = switch.shape[0] - 2
     skip = start // STEP
     total = jax.ShapeDtypeStruct((LAGS * cols, cols), jnp.float32)
     total_spec = pl.BlockSpec(total.shape, lambda s, on: (0, 0))
@@ -247,11 +239,11 @@
     if earlier is None:
         out_shape, out_specs, earlier = [total], [total_spec], []
     else:
-        out_shape, out_specs = [result] * 3, [result_spec] * 3
-        in_specs += [total_spec] + [result_spec] * 3
+        out_shape, out_specs = [result] * 2, [result_spec] * 2
+        in_specs += [total_spec] + [result_spec] * 2
         scratch = [pltpu.VMEM(total.shape, jnp.float32)] + scratch
     return pl.pallas_call(
-        functools.partial(second_kernel, windows, not earlier),
+        functools.partial(second_kernel, switch.shape[0] - 2, not earlier),
         grid_spec=pltpu.PrefetchScalarGridSpec(
             num_scalar_prefetch=1,
             grid=(rows // STEP,),
@@ -268,6 +260,47 @@
     )(switch, *own, coeffs, partner, *earlier)
 
 
+def late_kernel(windows, middle, switch_ref, plain_ref, swapped_ref, coeff_ref, first_ref, last_ref, near_out, acc, scaled):
+    step = pl.program_id(0)
+    cols = plain_ref.shape[0]
+
+    @pl.when(switch_ref[0] != 0)
+    def _():
+        @pl.when(step == 0)
+        def _():
+            acc[...] = jnp.zeros_like(acc)
+
+        scale(scaled, plain_ref[...], swapped_ref[...], coeff_ref)
+        partner = jnp.where(step < middle, first_ref[...], last_ref[...])
+        partner = weigh(partner, [switch_ref[2 + w] for w in range(windows)])
+        acc[...] += jnp.dot(scaled[...], partner, preferred_element_type=jnp.float32)
+        pl.when(step == pl.num_programs(0) - 1)(lambda: write_lags(near_out, acc, slice(0, cols), cols, False))
+
+
+def late_sums(switch, own, coeffs, parts):
+    cols, rows = own[0].shape
+    middle = parts[0].shape[0] // STEP
+    left = pl.BlockSpec((cols, STEP), lambda s, on: (0, s * on[0]))
+    result = jax.ShapeDtypeStruct((LAGS, cols, cols), jnp.bfloat16)
+    return pl.pallas_call(
+        functools.partial(late_kernel, switch.shape[0] - 2, middle),
+        grid_spec=pltpu.PrefetchScalarGridSpec(
+            num_scalar_prefetch=1,
+            grid=(rows // STEP,),
+            in_specs=[left, left, pl.BlockSpec((LAGS, STEP), lambda s, on: (0, s * on[0])),
+                      pl.BlockSpec((STEP, cols), lambda s, on: (jnp.minimum(s, middle - 1) * on[0], 0)),
+                      pl.BlockSpec((STEP, cols), lambda s, on: (jnp.maximum(s - middle, 0) * on[0], 0))],
+            out_specs=pl.BlockSpec(result.shape, lambda s, on: (0, 0, 0)),
+            scratch_shapes=[pltpu.VMEM((LAGS * cols, cols), jnp.float32),
+                            pltpu.VMEM((LAGS * cols, STEP), jnp.bfloat16)],
+        ),
+        out_shape=result,
+        compiler_params=PARAMS,
+        cost_estimate=pl.CostEstimate(flops=0, bytes_accessed=0, transcendentals=0),
+        name="late_near",
+    )(switch, *own, coeffs, *parts)
+
+
 def local(spectra, quality):
     count = lax.axis_size("chan")
     half = count // 2
@@ -279,9 +312,9 @@
     for p in range(half):
         if p in (0, half - 1):
             first_far.append((p + half, p))
-        elif p % 2 == 0 and p >= half // 2:
+        elif p % 2 == 1 and p != 1:
             first_far.append((p, p + half))
-        elif p in (1, 3):
+        elif p in (1, half - 2):
             second_far.append((p, p + half))
         else:
             second_far.append((p + half, p))
@@ -310,24 +343,27 @@
     second_flags = lax.ppermute(quality, "chan", second_pairs)[0]
     special = among([0, half - 1])
     first_switch = switch(me == 0, special, quality[0], near_flags, first_flags)
-    second_switch = switch(
-        among([t for _, t in second_pairs]), among([t for _, t in late_near]), quality[0] * second_flags
-    )
+    second_weights = quality[0] * second_flags
+    second_switch = switch(among([t for _, t in second_far]), False, second_weights)
+    late_switch = switch(among([t for _, t in late_near]), False, second_weights)
 
     near_in, parts, own, coeffs, first_in = lax.optimization_barrier((near_in, parts, own, coeffs, first_in))
     second_in = [lax.ppermute(part, "chan", second_pairs) for part in parts]
     alt = turn(first_in, switch(special, False), "turn_first", common=False)
     near, far, back = first_sums(first_switch, own, alt, coeffs, near_in, first_in, block)
+    near_pair = far
     side_returned = lax.ppermute(near, "chan", side_pairs)
     second_switch, near = lax.optimization_barrier((second_switch, near))
     total, = second_sums(second_switch, own, coeffs, second_in[0], 0)
 
+    far, back = second_sums(second_switch, own, coeffs, second_in[1], parts[0].shape[0], [total, far, back])
+    returned = lax.ppermute(back, "chan", back_pairs)
+    late_switch, far = lax.optimization_barrier((late_switch, far))
+    late = late_sums(late_switch, own, coeffs, second_in)
+
     near = jnp.where(among([half - 1, count - 1]), side_returned, near)
-    near = jnp.where(me == half - 2, far, near)
-    near, far, back = second_sums(
-        second_switch, own, coeffs, second_in[1], parts[0].shape[0], [total, near, far, back]
-    )
-    returned = lax.ppermute(back, "chan", back_pairs)
+    near = jnp.where(me == half - 2, near_pair, near)
+    near = jnp.where(among([t for _, t in late_near]), late, near)
     near = jnp.where(me == 0, returned, near)
     far = jnp.where(among([s for s, _ in first_far + second_far]), returned, far)
     return near[None], far[None]

time: 76.7 us -> 77.7 us (1.013)
  the two profiles are of different devices: /device:TPU:5 before, /device:TPU:1 now
where the time goes in v13:
time: 77.7 us; the launch traced here: 76.9 us
  starting transfers between devices  28.1 us (36%)
  Pallas kernels  26 us (33%)
  local copies, waits for them, and re-layouts  11.1 us (14%)
  waiting for transfers between devices  6.5 us (8%)
  other arithmetic  4.26 us (5%)
  between operations  0.96 us (1%)
    unnamed x36, local copies, waits for them, and re-layouts  11.1 us
    ppermute x1, starting transfers between devices, local(): second_flags = lax.ppermute(quality, 'chan', second_pairs)[0]  10.5 us
    pallas_call x1, Pallas kernels, first_sums(): pl.pallas_call(functools.partial(first_kernel, windows), grid_spec=pltpu....  10.3 us
    ppermute x2, starting transfers between devices, local(): second_in = [lax.ppermute(part, 'chan', second_pairs) for part in parts]  7.67 us
    pallas_call x1, Pallas kernels, late_sums(): pl.pallas_call(functools.partial(late_kernel, switch.shape[0] - 2, middle...  7.55 us
    ppermute x2, waiting for transfers between devices, local(): second_in = [lax.ppermute(part, 'chan', second_pairs) for part in parts]  6.07 us
    pallas_call x2, Pallas kernels, turn(): pl.pallas_call(turn_kernel, grid_spec=pltpu.PrefetchScalarGridSpec(num_sc...  5.52 us
    ppermute x1, starting transfers between devices, local(): returned = lax.ppermute(back, 'chan', back_pairs)  3.36 us
  transfers between devices with their start and end apart: 9, of which 2 were waited for; matrix products, arithmetic and copies ran while one was open for 3% of the time, Pallas kernels for 34%

profile of v13, /device:TPU:1, one launch (start us, length us, event | category | flops | bytes accessed | tf_op | source)
XLA Modules:
  0.0 76.9 jit_solution(13351876601646319190)
XLA Ops:
  0.6 2.0 %collective-permute-start.3 = (bf16[8192,128]{1,0:T(8,128)(2,1)}, bf16[8192,128]{1,0:T(8,128)(2,1)}, u32[]{:S(2)}, u32[]{:S(2)}) collective-permute-start(bf16[8192,128]{1,0:T(8,128)(2,1)} %bitcast.15), channel_id=1, source_target_pairs={{3,2},{5,4},{6,5},{9,8},{10,9},{11,10},{12,11},{13,12},{14,13},{15... | collective-permute-start | bytes 6291464 | tf_op jit(solution)/shard_map/ppermute | solution.py:336
  2.7 1.3 %collective-permute-start.4 = (bf16[8192,128]{1,0:T(8,128)(2,1)}, bf16[8192,128]{1,0:T(8,128)(2,1)}, u32[]{:S(2)}, u32[]{:S(2)}) collective-permute-start(bf16[8192,128]{1,0:T(8,128)(2,1)} %bitcast.16), channel_id=1, source_target_pairs={{8,0},{3,11},{5,13},{15,7},{0,1},{7,6},{24,16},{19,27},{21,29},{31... | collective-permute-start | bytes 6291464 | tf_op jit(solution)/shard_map/ppermute | solution.py:337
  4.6 1.3 %collective-permute-start.2 = (s32[1,4]{1,0:T(1,128)}, s32[1,4]{1,0:T(1,128)S(1)}, u32[]{:S(2)}, u32[]{:S(2)}) collective-permute-start(s32[1,4]{1,0:T(1,128)} %param.3), channel_id=1, source_target_pairs={{8,0},{3,11},{5,13},{15,7},{0,1},{7,6},{24,16},{19,27},{21,29},{31... | collective-permute-start | bytes 56 | tf_op jit(solution)/shard_map/ppermute | solution.py:341
  5.9 10.5 %collective-permute-start = (s32[1,4]{1,0:T(1,128)}, s32[1,4]{1,0:T(1,128)S(1)}, u32[]{:S(2)}, u32[]{:S(2)}) collective-permute-start(s32[1,4]{1,0:T(1,128)} %param.3), channel_id=1, source_target_pairs={{1,9},{10,2},{12,4},{6,14},{2,1},{4,3},{17,25},{26,18},{28,20},{22... | collective-permute-start | bytes 56 | tf_op jit(solution)/shard_map/ppermute | solution.py:343
  16.4 1.6 %copy-done.3 = bf16[1024,2,4,128]{3,2,1,0:T(4,128)(2,1)S(1)} copy-done((bf16[1024,2,4,128]{3,2,1,0:T(4,128)(2,1)S(1)}, bf16[1024,2,4,128]{3,2,1,0:T(4,128)(2,1)}, u32[]{:S(2)}) %copy-start.3) | copy-done | bytes 2097176
  18.3 1.1 %copy-done.15 = bf16[5120,128]{1,0:T(8,128)(2,1)} copy-done((bf16[5120,128]{1,0:T(8,128)(2,1)}, bf16[5120,128]{1,0:T(8,128)(2,1)S(1)}, u32[]{:S(2)}) %copy-start.15) | copy-done | bytes 1310744
  19.4 0.9 %copy-done.16 = bf16[3072,128]{1,0:T(8,128)(2,1)} copy-done((bf16[3072,128]{1,0:T(8,128)(2,1)}, bf16[3072,128]{1,0:T(8,128)(2,1)S(1)}, u32[]{:S(2)}) %copy-start.16) | copy-done | bytes 786456
  20.4 3.9 %turn_own.1 = (bf16[128,8192]{1,0:T(8,128)(2,1)S(1)}, bf16[128,8192]{1,0:T(8,128)(2,1)S(1)}) custom-call(s32[2]{0:T(128)S(1)} %copy-done.14, bf16[8192,128]{1,0:T(8,128)(2,1)S(1)} %bitcast.18), custom_call_target="tpu_custom_call" | custom-call | bytes 6291456 | tf_op jit(solution)/shard_map/turn_own/pallas_call | solution.py:82
  24.3 1.3 %copy-done = bf16[128,8192]{1,0:T(8,128)(2,1)} copy-done((bf16[128,8192]{1,0:T(8,128)(2,1)}, bf16[128,8192]{1,0:T(8,128)(2,1)S(1)}, u32[]{:S(2)}) %copy-start) | copy-done | bytes 2097176
  25.7 0.9 %multiply_convert_fusion = (bf16[5,8192]{1,0:T(8,128)(2,1)S(1)}, f32[5,8192]{1,0:T(8,128)S(1)}) fusion(f32[8192]{0:T(1024)S(1)} %fusion.9, f32[5]{0:T(128)S(1)} %iota_multiply_fusion), kind=kLoop, calls=%fused_computation.3 | loop fusion | flops 122880 | bytes 278548 | tf_op jit(solution)/shard_map/convert
  27.7 5.8 %collective-permute-start.5 = (bf16[5120,128]{1,0:T(8,128)(2,1)}, bf16[5120,128]{1,0:T(8,128)(2,1)S(1)}, u32[]{:S(2)}, u32[]{:S(2)}) collective-permute-start(bf16[5120,128]{1,0:T(8,128)(2,1)} %copy-done.15), channel_id=1, source_target_pairs={{1,9},{10,2},{12,4},{6,14},{2,1},{4,3},{17,25},{26,18},{28,20},{22... | collective-permute-start | bytes 3932168 | tf_op jit(solution)/shard_map/ppermute | solution.py:351
  33.7 1.9 %collective-permute-start.6 = (bf16[3072,128]{1,0:T(8,128)(2,1)}, bf16[3072,128]{1,0:T(8,128)(2,1)S(1)}, u32[]{:S(2)}, u32[]{:S(2)}) collective-permute-start(bf16[3072,128]{1,0:T(8,128)(2,1)} %copy-done.16), channel_id=1, source_target_pairs={{1,9},{10,2},{12,4},{6,14},{2,1},{4,3},{17,25},{26,18},{28,20},{22... | collective-permute-start | bytes 2359304 | tf_op jit(solution)/shard_map/ppermute | solution.py:351
  35.8 1.6 %turn_first.1 = (bf16[128,8192]{1,0:T(8,128)(2,1)S(1)}, bf16[128,8192]{1,0:T(8,128)(2,1)S(1)}) custom-call(s32[2]{0:T(128)S(1)} %fusion.13.active_ref, bf16[8192,128]{1,0:T(8,128)(2,1)} %collective-permute-done.4.x_ref.first_ref), custom_call_target="tpu_custom_call" | custom-call | tf_op jit(solution)/shard_map/turn_first/pallas_call | solution.py:82
  37.4 1.6 %copy-done.5 = bf16[1024,2,4,128]{3,2,1,0:T(4,128)(2,1)S(1)} copy-done((bf16[1024,2,4,128]{3,2,1,0:T(4,128)(2,1)S(1)}, bf16[1024,2,4,128]{3,2,1,0:T(4,128)(2,1)}, u32[]{:S(2)}) %copy-start.5) | copy-done | bytes 2097176
  39.0 10.3 %first_sums.1 = (bf16[9,128,128]{2,1,0:T(8,128)(2,1)}, bf16[9,128,128]{2,1,0:T(8,128)(2,1)S(1)}, bf16[9,128,128]{2,1,0:T(8,128)(2,1)S(1)}) custom-call(s32[14]{0:T(128)S(1)} %pad_add_fusion.4.switch_ref, bf16[128,8192]{1,0:T(8,128)(2,1)S(1)} %get-tuple-element.28.plain_ref, bf16[128,8192]{1,0:T(8,128)(2,1)S(1)} %copy-done.1, ...), custom_call_target="tpu_custom_call" | custom-call | flops 4831838208 | bytes 8388608 | tf_op jit(solution)/shard_map/first_sums/pallas_call | solution.py:174
  49.3 1.4 %collective-permute-start.8 = (bf16[9,128,128]{2,1,0:T(8,128)(2,1)}, bf16[9,128,128]{2,1,0:T(8,128)(2,1)}, u32[]{:S(2)}, u32[]{:S(2)}) collective-permute-start(bf16[9,128,128]{2,1,0:T(8,128)(2,1)} %get-tuple-element.44), channel_id=1, source_target_pairs={{0,7},{7,15},{16,23},{23,31}} | collective-permute-start | bytes 884744 | tf_op jit(solution)/shard_map/ppermute | solution.py:355
  50.6 6.1 %collective-permute-done.6.partner_ref.first_ref = bf16[3072,128]{1,0:T(8,128)(2,1)S(1)} collective-permute-done((bf16[3072,128]{1,0:T(8,128)(2,1)}, bf16[3072,128]{1,0:T(8,128)(2,1)S(1)}, u32[]{:S(2)}, u32[]{:S(2)}) %collective-permute-start.6) | collective-permute-done | bytes 786464 | tf_op jit(solution)/shard_map/ppermute | solution.py:351
  57.6 1.6 %second_last.1 = (bf16[9,128,128]{2,1,0:T(8,128)(2,1)S(1)}, bf16[9,128,128]{2,1,0:T(8,128)(2,1)}) custom-call(s32[6]{0:T(128)S(1)} %get-tuple-element.36.switch_ref, bf16[128,8192]{1,0:T(8,128)(2,1)S(1)} %get-tuple-element.28.plain_ref, bf16[128,8192]{1,0:T(8,128)(2,1)S(1)} %copy-done.1, bf16[9,8192]{1,0:T(8,128)(2,1)S(1)} %pad_maximum_fusion.coeff_ref, ...), custom_call_target="tpu_custom_call" | custom-call | flops 1509949440 | bytes 3932160 | tf_op jit(solution)/shard_map/second_last/pallas_call | solution.py:245
  59.9 3.4 %collective-permute-start.7 = (bf16[9,128,128]{2,1,0:T(8,128)(2,1)}, bf16[9,128,128]{2,1,0:T(8,128)(2,1)}, u32[]{:S(2)}, u32[]{:S(2)}) collective-permute-start(bf16[9,128,128]{2,1,0:T(8,128)(2,1)} %get-tuple-element.41), channel_id=1, source_target_pairs={{0,8},{11,3},{13,5},{7,15},{9,1},{2,10},{4,12},{14,6},{1,0},{16,24... | collective-permute-start | bytes 884744 | tf_op jit(solution)/shard_map/ppermute | solution.py:360
  63.3 1.6 %copy-done.2 = bf16[128,8192]{1,0:T(8,128)(2,1)S(1)} copy-done((bf16[128,8192]{1,0:T(8,128)(2,1)S(1)}, bf16[128,8192]{1,0:T(8,128)(2,1)}, u32[]{:S(2)}) %copy-start.2) | copy-done | bytes 2097176
  64.9 0.9 %copy-done.7 = bf16[9,8192]{1,0:T(8,128)(2,1)S(1)} copy-done((bf16[9,8192]{1,0:T(8,128)(2,1)S(1)}, bf16[9,8192]{1,0:T(8,128)(2,1)}, u32[]{:S(2)}) %copy-start.7) | copy-done | bytes 147480
  65.8 1.1 %copy-done.9 = bf16[3072,128]{1,0:T(8,128)(2,1)S(1)} copy-done((bf16[3072,128]{1,0:T(8,128)(2,1)S(1)}, bf16[3072,128]{1,0:T(8,128)(2,1)}, u32[]{:S(2)}) %copy-start.9) | copy-done | bytes 786456
  67.0 7.5 %late_near.1 = bf16[9,128,128]{2,1,0:T(8,128)(2,1)S(1)} custom-call(s32[6]{0:T(128)S(1)} %get-tuple-element.43.switch_ref, bf16[128,8192]{1,0:T(8,128)(2,1)S(1)} %get-tuple-element.28.plain_ref, bf16[128,8192]{1,0:T(8,128)(2,1)S(1)} %copy-done.2, bf16[9,8192]{1,0:T(8,128)(2,1)S(1)} %copy-done.7, bf16[3072,128]{1,0:T(8,128)(2,1)S(1)} %copy-done.9, ...), custom_call_target="tpu_custom_call" | custom-call | tf_op jit(solution)/shard_map/late_near/pallas_call | solution.py:285
  75.0 1.9 %select_bitcast_fusion = (bf16[1,9,128,128]{3,2,1,0:T(8,128)(2,1)}, bf16[1,9,128,128]{3,2,1,0:T(8,128)(2,1)}) fusion(bf16[9,128,128]{2,1,0:T(8,128)(2,1)} %collective-permute-done.7, bf16[9,128,128]{2,1,0:T(8,128)(2,1)S(1)} %copy-done.13, pred[]{:T(512)S(6)} %or.52, bf16[9,128,128]{2,1,0:T(8,128)(2,1)S(1)} %late_near.1, bf16[9,128,128]{2,1,0:T(8,128)(2,1)S(1)} %copy-done.11, ...), kind=kLoop, calls=%fused_computation | loop fusion | flops 737280 | bytes 2359301 | tf_op jit(solution)/shard_map/broadcast_in_dim | solution.py:369
  (50 shorter events, 4.4 us)
Async XLA Ops:
  0.6 19.7 %copy-start.14 = (s32[2]{0:T(128)S(1)}, s32[2]{0:T(128)}, u32[]{:S(2)}) copy-start(s32[2]{0:T(128)} %constant.30.clone.1.active_ref) | copy-start | bytes 28
  0.6 27.0 %collective-permute-start.3 = (bf16[8192,128]{1,0:T(8,128)(2,1)}, bf16[8192,128]{1,0:T(8,128)(2,1)}, u32[]{:S(2)}, u32[]{:S(2)}) collective-permute-start(bf16[8192,128]{1,0:T(8,128)(2,1)} %bitcast.15), channel_id=1, source_target_pairs={{3,2},{5,4},{6,5},{9,8},{10,9},{11,10},{12,11},{13,12},{14,13},{15... | collective-permute-start | bytes 6291464 | tf_op jit(solution)/shard_map/ppermute | solution.py:336
  2.7 25.0 %collective-permute-start.4 = (bf16[8192,128]{1,0:T(8,128)(2,1)}, bf16[8192,128]{1,0:T(8,128)(2,1)}, u32[]{:S(2)}, u32[]{:S(2)}) collective-permute-start(bf16[8192,128]{1,0:T(8,128)(2,1)} %bitcast.16), channel_id=1, source_target_pairs={{8,0},{3,11},{5,13},{15,7},{0,1},{7,6},{24,16},{19,27},{21,29},{31... | collective-permute-start | bytes 6291464 | tf_op jit(solution)/shard_map/ppermute | solution.py:337
  4.0 29.7 %collective-permute-start.1 = (s32[1,4]{1,0:T(1,128)}, s32[1,4]{1,0:T(1,128)S(1)}, u32[]{:S(2)}, u32[]{:S(2)}) collective-permute-start(s32[1,4]{1,0:T(1,128)} %param.3), channel_id=1, source_target_pairs={{3,2},{5,4},{6,5},{9,8},{10,9},{11,10},{12,11},{13,12},{14,13},{15... | collective-permute-start | bytes 56 | tf_op jit(solution)/shard_map/ppermute | solution.py:342
  4.6 29.0 %collective-permute-start.2 = (s32[1,4]{1,0:T(1,128)}, s32[1,4]{1,0:T(1,128)S(1)}, u32[]{:S(2)}, u32[]{:S(2)}) collective-permute-start(s32[1,4]{1,0:T(1,128)} %param.3), channel_id=1, source_target_pairs={{8,0},{3,11},{5,13},{15,7},{0,1},{7,6},{24,16},{19,27},{21,29},{31... | collective-permute-start | bytes 56 | tf_op jit(solution)/shard_map/ppermute | solution.py:341
  5.9 29.7 %collective-permute-start = (s32[1,4]{1,0:T(1,128)}, s32[1,4]{1,0:T(1,128)S(1)}, u32[]{:S(2)}, u32[]{:S(2)}) collective-permute-start(s32[1,4]{1,0:T(1,128)} %param.3), channel_id=1, source_target_pairs={{1,9},{10,2},{12,4},{6,14},{2,1},{4,3},{17,25},{26,18},{28,20},{22... | collective-permute-start | bytes 56 | tf_op jit(solution)/shard_map/ppermute | solution.py:343
  16.4 1.6 %copy-start.3 = (bf16[1024,2,4,128]{3,2,1,0:T(4,128)(2,1)S(1)}, bf16[1024,2,4,128]{3,2,1,0:T(4,128)(2,1)}, u32[]{:S(2)}) copy-start(bf16[1024,2,4,128]{3,2,1,0:T(4,128)(2,1)} %param.2) | copy-start | bytes 6291460
  18.0 2.4 %copy-start.4 = (bf16[1024,2,4,128]{3,2,1,0:T(4,128)(2,1)S(1)}, bf16[1024,2,4,128]{3,2,1,0:T(4,128)(2,1)}, u32[]{:S(2)}) copy-start(bf16[1024,2,4,128]{3,2,1,0:T(4,128)(2,1)} %param.2) | copy-start | bytes 6291460
  18.3 1.1 %copy-start.15 = (bf16[5120,128]{1,0:T(8,128)(2,1)}, bf16[5120,128]{1,0:T(8,128)(2,1)S(1)}, u32[]{:S(2)}) copy-start(bf16[5120,128]{1,0:T(8,128)(2,1)S(1)} %get-tuple-element.37) | copy-start | bytes 3932164
  20.3 13.3 %copy-start.17 = (s32[1,4]{1,0:T(1,128)S(1)}, s32[1,4]{1,0:T(1,128)}, u32[]{:S(2)}) copy-start(s32[1,4]{1,0:T(1,128)} %param.3) | copy-start | bytes 52
  24.3 1.3 %copy-start = (bf16[128,8192]{1,0:T(8,128)(2,1)}, bf16[128,8192]{1,0:T(8,128)(2,1)S(1)}, u32[]{:S(2)}) copy-start(bf16[128,8192]{1,0:T(8,128)(2,1)S(1)} %get-tuple-element.29.swapped_ref) | copy-start | bytes 6291460
  26.6 10.7 %copy-start.1 = (bf16[128,8192]{1,0:T(8,128)(2,1)S(1)}, bf16[128,8192]{1,0:T(8,128)(2,1)}, u32[]{:S(2)}) copy-start(bf16[128,8192]{1,0:T(8,128)(2,1)} %copy-done) | copy-start | bytes 6291460
  27.6 30.0 %copy-start.6 = (bf16[9,8192]{1,0:T(8,128)(2,1)}, bf16[9,8192]{1,0:T(8,128)(2,1)S(1)}, u32[]{:S(2)}) copy-start(bf16[9,8192]{1,0:T(8,128)(2,1)S(1)} %pad_maximum_fusion.coeff_ref) | copy-start | bytes 442372
  27.7 29.9 %collective-permute-start.5 = (bf16[5120,128]{1,0:T(8,128)(2,1)}, bf16[5120,128]{1,0:T(8,128)(2,1)S(1)}, u32[]{:S(2)}, u32[]{:S(2)}) collective-permute-start(bf16[5120,128]{1,0:T(8,128)(2,1)} %copy-done.15), channel_id=1, source_target_pairs={{1,9},{10,2},{12,4},{6,14},{2,1},{4,3},{17,25},{26,18},{28,20},{22... | collective-permute-start | bytes 3932168 | tf_op jit(solution)/shard_map/ppermute | solution.py:351
  33.7 23.0 %collective-permute-start.6 = (bf16[3072,128]{1,0:T(8,128)(2,1)}, bf16[3072,128]{1,0:T(8,128)(2,1)S(1)}, u32[]{:S(2)}, u32[]{:S(2)}) collective-permute-start(bf16[3072,128]{1,0:T(8,128)(2,1)} %copy-done.16), channel_id=1, source_target_pairs={{1,9},{10,2},{12,4},{6,14},{2,1},{4,3},{17,25},{26,18},{28,20},{22... | collective-permute-start | bytes 2359304 | tf_op jit(solution)/shard_map/ppermute | solution.py:351
  37.4 1.6 %copy-start.5 = (bf16[1024,2,4,128]{3,2,1,0:T(4,128)(2,1)S(1)}, bf16[1024,2,4,128]{3,2,1,0:T(4,128)(2,1)}, u32[]{:S(2)}) copy-start(bf16[1024,2,4,128]{3,2,1,0:T(4,128)(2,1)} %param.2) | copy-start | bytes 6291460
  49.3 8.3 %copy-start.10 = (bf16[9,128,128]{2,1,0:T(8,128)(2,1)}, bf16[9,128,128]{2,1,0:T(8,128)(2,1)S(1)}, u32[]{:S(2)}) copy-start(bf16[9,128,128]{2,1,0:T(8,128)(2,1)S(1)} %get-tuple-element.39.rest_1_) | copy-start | bytes 884740
  49.3 25.3 %collective-permute-start.8 = (bf16[9,128,128]{2,1,0:T(8,128)(2,1)}, bf16[9,128,128]{2,1,0:T(8,128)(2,1)}, u32[]{:S(2)}, u32[]{:S(2)}) collective-permute-start(bf16[9,128,128]{2,1,0:T(8,128)(2,1)} %get-tuple-element.44), channel_id=1, source_target_pairs={{0,7},{7,15},{16,23},{23,31}} | collective-permute-start | bytes 884744 | tf_op jit(solution)/shard_map/ppermute | solution.py:355
  59.9 15.1 %collective-permute-start.7 = (bf16[9,128,128]{2,1,0:T(8,128)(2,1)}, bf16[9,128,128]{2,1,0:T(8,128)(2,1)}, u32[]{:S(2)}, u32[]{:S(2)}) collective-permute-start(bf16[9,128,128]{2,1,0:T(8,128)(2,1)} %get-tuple-element.41), channel_id=1, source_target_pairs={{0,8},{11,3},{13,5},{7,15},{9,1},{2,10},{4,12},{14,6},{1,0},{16,24... | collective-permute-start | bytes 884744 | tf_op jit(solution)/shard_map/ppermute | solution.py:360
  63.3 1.6 %copy-start.2 = (bf16[128,8192]{1,0:T(8,128)(2,1)S(1)}, bf16[128,8192]{1,0:T(8,128)(2,1)}, u32[]{:S(2)}) copy-start(bf16[128,8192]{1,0:T(8,128)(2,1)} %copy-done) | copy-start | bytes 6291460
  64.9 0.9 %copy-start.7 = (bf16[9,8192]{1,0:T(8,128)(2,1)S(1)}, bf16[9,8192]{1,0:T(8,128)(2,1)}, u32[]{:S(2)}) copy-start(bf16[9,8192]{1,0:T(8,128)(2,1)} %copy-done.6) | copy-start | bytes 442372
  65.8 1.1 %copy-start.9 = (bf16[3072,128]{1,0:T(8,128)(2,1)S(1)}, bf16[3072,128]{1,0:T(8,128)(2,1)}, u32[]{:S(2)}) copy-start(bf16[3072,128]{1,0:T(8,128)(2,1)} %copy-done.8) | copy-start | bytes 2359300
  67.0 8.0 %copy-start.11 = (bf16[9,128,128]{2,1,0:T(8,128)(2,1)S(1)}, bf16[9,128,128]{2,1,0:T(8,128)(2,1)}, u32[]{:S(2)}) copy-start(bf16[9,128,128]{2,1,0:T(8,128)(2,1)} %copy-done.10) | copy-start | bytes 884740
  67.0 8.0 %copy-start.13 = (bf16[9,128,128]{2,1,0:T(8,128)(2,1)S(1)}, bf16[9,128,128]{2,1,0:T(8,128)(2,1)}, u32[]{:S(2)}) copy-start(bf16[9,128,128]{2,1,0:T(8,128)(2,1)} %copy-done.12) | copy-start | bytes 884740
  (3 other events, 2.5 us)

commit v14 on v11

--- a/solution.py
+++ b/solution.py
@@ -11,7 +11,7 @@
 HL = 4
 LAGS = 2 * HL + 1
 STEP = 1024
-PARTS = (3, 8)
+PARTS = (5, 8)
 PARAMS = pltpu.CompilerParams(vmem_limit_bytes=16 * 1024 * 1024)
 
 
@@ -125,15 +125,23 @@
     return x * weights.reshape(rows, cols)
 
 
-def first_kernel(windows, switch_ref, plain_ref, swapped_ref, plain_alt, swapped_alt, coeff_ref, near_ref, first_ref,
-                 own_ref, near_out, far_out, back_out, acc, scaled):
+def first_kernel(windows, last, switch_ref, plain_ref, swapped_ref, plain_alt, swapped_alt, coeff_ref, near_ref, first_ref,
+                 own_ref, *rest):
     step = pl.program_id(0)
     cols = plain_ref.shape[0]
     near_mirrored, special = switch_ref[0], switch_ref[1]
+    if last:
+        acc_in, _, near_out, far_out, back_out, acc, scaled = rest
+    else:
+        acc, token_out, scaled = rest
 
     @pl.when(step == 0)
     def _():
-        acc[...] = jnp.zeros_like(acc)
+        if last:
+            acc[...] = acc_in[...]
+        else:
+            acc[...] = jnp.zeros_like(acc)
+            token_out[...] = jnp.zeros_like(token_out)
 
     plain = jnp.where(special != 0, plain_alt[...], plain_ref[...])
     swapped = jnp.where(special != 0, swapped_alt[...], swapped_ref[...])
@@ -144,51 +152,66 @@
     far = weigh(jnp.where(special != 0, own_ref[...], first_ref[...]), [own * first for own, _, first in zip(*flags)])
     acc[...] += jnp.dot(scaled[...], jnp.concatenate([near, far], axis=1), preferred_element_type=jnp.float32)
 
-    @pl.when(step == pl.num_programs(0) - 1)
-    def _():
-        near_at, far_at = slice(0, cols), slice(cols, 2 * cols)
-
-        @pl.when(special == 0)
+    if last:
+        @pl.when(step == pl.num_programs(0) - 1)
         def _():
-            write_lags(back_out, acc, far_at, cols, True)
-            write_lags(far_out, acc, far_at, cols, False)
-
-        @pl.when(special != 0)
-        def _():
-            write_lags(back_out, acc, far_at, cols, False)
-            write_lags(far_out, acc, far_at, cols, True)
-
-        pl.when(near_mirrored == 0)(lambda: write_lags(near_out, acc, near_at, cols, False))
-        pl.when(near_mirrored != 0)(lambda: write_lags(near_out, acc, near_at, cols, True))
-
-
-def first_sums(switch, own, alt, coeffs, near_in, first_in, block):
+            near_at, far_at = slice(0, cols), slice(cols, 2 * cols)
+
+            @pl.when(special == 0)
+            def _():
+                write_lags(back_out, acc, far_at, cols, True)
+                write_lags(far_out, acc, far_at, cols, False)
+
+            @pl.when(special != 0)
+            def _():
+                write_lags(back_out, acc, far_at, cols, False)
+                write_lags(far_out, acc, far_at, cols, True)
+
+            pl.when(near_mirrored == 0)(lambda: write_lags(near_out, acc, near_at, cols, False))
+            pl.when(near_mirrored != 0)(lambda: write_lags(near_out, acc, near_at, cols, True))
+
+
+def first_sums(switch, own, alt, coeffs, near_in, first_in, block, earlier=None):
     rows, cols = block.shape
+    steps = rows // STEP // 2
+    skip = 0 if earlier is None else steps
     windows = (switch.shape[0] - 2) // 3
     result = jax.ShapeDtypeStruct((LAGS, cols, cols), jnp.bfloat16)
-    left = pl.BlockSpec((cols, STEP), lambda s, on: (0, s * (1 - on[1])))
-    left_alt = pl.BlockSpec((cols, STEP), lambda s, on: (0, s * on[1]))
-    right = pl.BlockSpec((STEP, cols), lambda s, on: (s, 0))
-    right_usual = pl.BlockSpec((STEP, cols), lambda s, on: (s * (1 - on[1]), 0))
-    right_special = pl.BlockSpec((STEP, cols), lambda s, on: (s * on[1], 0))
+    total = jax.ShapeDtypeStruct((LAGS * cols, 2 * cols), jnp.float32)
+    total_spec = pl.BlockSpec(total.shape, lambda s, on: (0, 0))
+    token = jax.ShapeDtypeStruct((8, cols), jnp.float32)
+    token_spec = pl.BlockSpec(token.shape, lambda s, on: (0, 0))
+    left = pl.BlockSpec((cols, STEP), lambda s, on: (0, (s + skip) * (1 - on[1])))
+    left_alt = pl.BlockSpec((cols, STEP), lambda s, on: (0, (s + skip) * on[1]))
+    right = pl.BlockSpec((STEP, cols), lambda s, on: (s + skip, 0))
+    right_usual = pl.BlockSpec((STEP, cols), lambda s, on: ((s + skip) * (1 - on[1]), 0))
+    right_special = pl.BlockSpec((STEP, cols), lambda s, on: ((s + skip) * on[1], 0))
+    in_specs = [left, left, left_alt, left_alt, pl.BlockSpec((LAGS, STEP), lambda s, on: (0, s + skip)),
+                right, right_usual, right_special]
+    scratch = [pltpu.VMEM((LAGS * cols, STEP), jnp.bfloat16)]
+    if earlier is None:
+        out_shape, out_specs, earlier = [total, token], [total_spec, token_spec], []
+    else:
+        in_specs += [total_spec, token_spec]
+        out_shape = [result] * 3
+        out_specs = [pl.BlockSpec(result.shape, lambda s, on: (0, 0, 0))] * 3
+        scratch = [pltpu.VMEM(total.shape, jnp.float32)] + scratch
     return pl.pallas_call(
-        functools.partial(first_kernel, windows),
+        functools.partial(first_kernel, windows, bool(earlier)),
         grid_spec=pltpu.PrefetchScalarGridSpec(
             num_scalar_prefetch=1,
-            grid=(rows // STEP,),
-            in_specs=[left, left, left_alt, left_alt, pl.BlockSpec((LAGS, STEP), lambda s, on: (0, s)),
-                      right, right_usual, right_special],
-            out_specs=[pl.BlockSpec(result.shape, lambda s, on: (0, 0, 0))] * 3,
-            scratch_shapes=[pltpu.VMEM((LAGS * cols, 2 * cols), jnp.float32),
-                            pltpu.VMEM((LAGS * cols, STEP), jnp.bfloat16)],
-        ),
-        out_shape=[result] * 3,
+            grid=(steps,),
+            in_specs=in_specs,
+            out_specs=out_specs,
+            scratch_shapes=scratch,
+        ),
+        out_shape=out_shape,
         compiler_params=PARAMS,
         cost_estimate=pl.CostEstimate(
-            flops=4 * LAGS * cols * cols * rows, bytes_accessed=8 * rows * cols, transcendentals=0
-        ),
-        name="first_sums",
-    )(switch, *own, *alt, coeffs, near_in, first_in, block)
+            flops=2 * LAGS * cols * cols * rows, bytes_accessed=4 * rows * cols, transcendentals=0
+        ),
+        name="first_last" if earlier else "first_half",
+    )(switch, *own, *alt, coeffs, near_in, first_in, block, *earlier)
 
 
 def second_kernel(windows, first, switch_ref, plain_ref, swapped_ref, coeff_ref, partner_ref, *rest):
@@ -314,10 +337,14 @@
         among([t for _, t in second_pairs]), among([t for _, t in late_near]), quality[0] * second_flags
     )
 
-    near_in, parts, own, coeffs, first_in = lax.optimization_barrier((near_in, parts, own, coeffs, first_in))
-    second_in = [lax.ppermute(part, "chan", second_pairs) for part in parts]
+    near_in, first_part, own, coeffs, first_in = lax.optimization_barrier((near_in, parts[0], own, coeffs, first_in))
+    second_in = [lax.ppermute(first_part, "chan", second_pairs)]
     alt = turn(first_in, switch(special, False), "turn_first", common=False)
-    near, far, back = first_sums(first_switch, own, alt, coeffs, near_in, first_in, block)
+    operands = first_switch, own, alt, coeffs, near_in, first_in, block
+    total, token = first_sums(*operands)
+    last_part, token = lax.optimization_barrier((parts[1], token))
+    second_in.append(lax.ppermute(last_part, "chan", second_pairs))
+    near, far, back = first_sums(*operands, [total, token])
     side_returned = lax.ppermute(near, "chan", side_pairs)
     second_switch, near = lax.optimization_barrier((second_switch, near))
     total, = second_sums(second_switch, own, coeffs, second_in[0], 0)

time: 76.7 us -> 73.5 us (0.958)
  the two profiles are of different devices: /device:TPU:5 before, /device:TPU:1 now
where the time goes in v14:
time: 73.5 us; the launch traced here: 72.6 us
  starting transfers between devices  30.5 us (41%)
  Pallas kernels  26.3 us (36%)
  local copies, waits for them, and re-layouts  7.62 us (10%)
  waiting for transfers between devices  3.99 us (5%)
  other arithmetic  3.25 us (4%)
  between operations  0.93 us (1%)
    pallas_call x2, Pallas kernels, first_sums(): pl.pallas_call(functools.partial(first_kernel, windows, bool(earlier)), g...  11.2 us
    ppermute x1, starting transfers between devices, local(): second_flags = lax.ppermute(quality, 'chan', second_pairs)[0]  10.5 us
    pallas_call x2, Pallas kernels, second_sums(): pl.pallas_call(functools.partial(second_kernel, windows, not earlier), gr...  9.36 us
    unnamed x18, local copies, waits for them, and re-layouts  7.62 us
    ppermute x1, starting transfers between devices, local(): returned = lax.ppermute(back, 'chan', back_pairs)  7.52 us
    pallas_call x2, Pallas kernels, turn(): pl.pallas_call(turn_kernel, grid_spec=pltpu.PrefetchScalarGridSpec(num_sc...  5.51 us
    ppermute x1, starting transfers between devices, local(): second_in = [lax.ppermute(first_part, 'chan', second_pairs)]  4.65 us
    ppermute x1, waiting for transfers between devices, local(): returned = lax.ppermute(back, 'chan', back_pairs)  3.96 us
  transfers between devices with their start and end apart: 9, of which 1 were waited for; matrix products, arithmetic and copies ran while one was open for 3% of the time, Pallas kernels for 32%

profile of v14, /device:TPU:1, one launch (start us, length us, event | category | flops | bytes accessed | tf_op | source)
XLA Modules:
  0.0 72.6 jit_solution(5890462916857438804)
XLA Ops:
  0.6 2.0 %collective-permute-start.3 = (bf16[8192,128]{1,0:T(8,128)(2,1)}, bf16[8192,128]{1,0:T(8,128)(2,1)}, u32[]{:S(2)}, u32[]{:S(2)}) collective-permute-start(bf16[8192,128]{1,0:T(8,128)(2,1)} %bitcast.15), channel_id=1, source_target_pairs={{3,2},{5,4},{6,5},{9,8},{10,9},{11,10},{12,11},{13,12},{14,13},{15... | collective-permute-start | bytes 6291464 | tf_op jit(solution)/shard_map/ppermute | solution.py:326
  2.6 1.3 %collective-permute-start.4 = (bf16[8192,128]{1,0:T(8,128)(2,1)}, bf16[8192,128]{1,0:T(8,128)(2,1)}, u32[]{:S(2)}, u32[]{:S(2)}) collective-permute-start(bf16[8192,128]{1,0:T(8,128)(2,1)} %bitcast.16), channel_id=1, source_target_pairs={{8,0},{4,12},{6,14},{15,7},{0,1},{7,6},{24,16},{20,28},{22,30},{31... | collective-permute-start | bytes 6291464 | tf_op jit(solution)/shard_map/ppermute | solution.py:327
  3.9 0.7 collective-permute-start.1
  4.6 1.3 %collective-permute-start.2 = (s32[1,4]{1,0:T(1,128)}, s32[1,4]{1,0:T(1,128)S(1)}, u32[]{:S(2)}, u32[]{:S(2)}) collective-permute-start(s32[1,4]{1,0:T(1,128)} %param.3), channel_id=1, source_target_pairs={{8,0},{4,12},{6,14},{15,7},{0,1},{7,6},{24,16},{20,28},{22,30},{31... | collective-permute-start | bytes 56 | tf_op jit(solution)/shard_map/ppermute | solution.py:331
  5.9 10.5 %collective-permute-start = (s32[1,4]{1,0:T(1,128)}, s32[1,4]{1,0:T(1,128)S(1)}, u32[]{:S(2)}, u32[]{:S(2)}) collective-permute-start(s32[1,4]{1,0:T(1,128)} %param.3), channel_id=1, source_target_pairs={{1,9},{10,2},{3,11},{13,5},{2,1},{4,3},{17,25},{26,18},{19,27},{29... | collective-permute-start | bytes 56 | tf_op jit(solution)/shard_map/ppermute | solution.py:333
  16.4 1.6 %copy-done = bf16[1024,2,4,128]{3,2,1,0:T(4,128)(2,1)S(1)} copy-done((bf16[1024,2,4,128]{3,2,1,0:T(4,128)(2,1)S(1)}, bf16[1024,2,4,128]{3,2,1,0:T(4,128)(2,1)}, u32[]{:S(2)}) %copy-start) | copy-done | bytes 2097176
  18.3 1.1 %copy-done.7 = bf16[5120,128]{1,0:T(8,128)(2,1)} copy-done((bf16[5120,128]{1,0:T(8,128)(2,1)}, bf16[5120,128]{1,0:T(8,128)(2,1)S(1)}, u32[]{:S(2)}) %copy-start.7) | copy-done | bytes 1310744
  20.1 3.9 %turn_own.1 = (bf16[128,8192]{1,0:T(8,128)(2,1)S(1)}, bf16[128,8192]{1,0:T(8,128)(2,1)S(1)}) custom-call(s32[2]{0:T(128)S(1)} %copy-done.6, bf16[8192,128]{1,0:T(8,128)(2,1)S(1)} %bitcast.18), custom_call_target="tpu_custom_call" | custom-call | bytes 6291456 | tf_op jit(solution)/shard_map/turn_own/pallas_call | solution.py:82
  24.0 1.3 %copy-done.2 = bf16[128,8192]{1,0:T(8,128)(2,1)} copy-done((bf16[128,8192]{1,0:T(8,128)(2,1)}, bf16[128,8192]{1,0:T(8,128)(2,1)S(1)}, u32[]{:S(2)}) %copy-start.2) | copy-done | bytes 2097176
  25.4 1.4 %copy-done.4 = bf16[128,8192]{1,0:T(8,128)(2,1)} copy-done((bf16[128,8192]{1,0:T(8,128)(2,1)}, bf16[128,8192]{1,0:T(8,128)(2,1)S(1)}, u32[]{:S(2)}) %copy-start.4) | copy-done | bytes 2097176
  26.8 0.9 %multiply_convert_fusion = (bf16[5,8192]{1,0:T(8,128)(2,1)S(1)}, f32[5,8192]{1,0:T(8,128)S(1)}) fusion(f32[8192]{0:T(1024)S(1)} %fusion.9, f32[5]{0:T(128)S(1)} %iota_multiply_fusion), kind=kLoop, calls=%fused_computation.4 | loop fusion | flops 122880 | bytes 278548 | tf_op jit(solution)/shard_map/convert
  27.8 0.9 %fusion.2 = bf16[4,8192]{1,0:T(4,128)(2,1)S(1)} fusion(f32[5,8192]{1,0:T(8,128)S(1)} %get-tuple-element.53, f32[8192]{0:T(1024)S(1)} %select_multiply_fusion), kind=kLoop, calls=%fused_computation.8 | loop fusion | flops 98304 | bytes 229376 | tf_op jit(solution)/shard_map/convert.1
  28.8 4.6 %collective-permute-start.6 = (bf16[5120,128]{1,0:T(8,128)(2,1)}, bf16[5120,128]{1,0:T(8,128)(2,1)}, u32[]{:S(2)}, u32[]{:S(2)}) collective-permute-start(bf16[5120,128]{1,0:T(8,128)(2,1)} %copy-done.7), channel_id=1, source_target_pairs={{1,9},{10,2},{3,11},{13,5},{2,1},{4,3},{17,25},{26,18},{19,27},{29... | collective-permute-start | bytes 3932168 | tf_op jit(solution)/shard_map/ppermute | solution.py:341
  33.7 1.6 %turn_first.1 = (bf16[128,8192]{1,0:T(8,128)(2,1)S(1)}, bf16[128,8192]{1,0:T(8,128)(2,1)S(1)}) custom-call(s32[2]{0:T(128)S(1)} %add_convert_fusion.2.active_ref, bf16[8192,128]{1,0:T(8,128)(2,1)} %collective-permute-done.4.x_ref.first_ref), custom_call_target="tpu_custom_call" | custom-call | tf_op jit(solution)/shard_map/turn_first/pallas_call | solution.py:82
  35.3 1.6 %copy-done.5 = bf16[128,8192]{1,0:T(8,128)(2,1)S(1)} copy-done((bf16[128,8192]{1,0:T(8,128)(2,1)S(1)}, bf16[128,8192]{1,0:T(8,128)(2,1)}, u32[]{:S(2)}) %copy-start.5) | copy-done | bytes 2097176
  36.9 5.5 %first_half.1 = (f32[1152,256]{1,0:T(8,128)S(1)}, f32[8,128]{1,0:T(8,128)S(1)}) custom-call(s32[14]{0:T(128)S(1)} %pad_add_fusion.1.switch_ref, bf16[128,8192]{1,0:T(8,128)(2,1)S(1)} %copy-done.3, bf16[128,8192]{1,0:T(8,128)(2,1)S(1)} %copy-done.5, bf16[128,8192]{1,0:T(8,128)(2,1)S(1)} %get-tuple-element.32.plain_alt, ...), custom_call_target="tpu_custom_call" | custom-call | flops 2415919104 | bytes 4194304 | tf_op jit(solution)/shard_map/first_half/pallas_call | solution.py:199
  42.4 1.9 %collective-permute-start.5 = (bf16[3072,128]{1,0:T(8,128)(2,1)S(1)}, bf16[3072,128]{1,0:T(8,128)(2,1)S(1)}, u32[]{:S(2)}, u32[]{:S(2)}) collective-permute-start(bf16[3072,128]{1,0:T(8,128)(2,1)S(1)} %get-tuple-element.42), channel_id=1, source_target_pairs={{1,9},{10,2},{3,11},{13,5},{2,1},{4,3},{17,25},{26,18},{19,27},{29... | collective-permute-start | bytes 2359304 | tf_op jit(solution)/shard_map/ppermute | solution.py:346
  44.3 5.7 %first_last.1 = (bf16[9,128,128]{2,1,0:T(8,128)(2,1)S(1)}, bf16[9,128,128]{2,1,0:T(8,128)(2,1)S(1)}, bf16[9,128,128]{2,1,0:T(8,128)(2,1)S(1)}) custom-call(s32[14]{0:T(128)S(1)} %pad_add_fusion.1.switch_ref, bf16[128,8192]{1,0:T(8,128)(2,1)S(1)} %copy-done.3, bf16[128,8192]{1,0:T(8,128)(2,1)S(1)} %copy-done.5, ...), custom_call_target="tpu_custom_call" | custom-call | flops 2415919104 | bytes 4194304 | tf_op jit(solution)/shard_map/first_last/pallas_call | solution.py:199
  50.0 0.7 collective-permute-start.7
  50.9 6.0 %second_part.1.rest_0_ = f32[1152,128]{1,0:T(8,128)S(1)} custom-call(s32[6]{0:T(128)S(1)} %pad_add_fusion.switch_ref, bf16[128,8192]{1,0:T(8,128)(2,1)S(1)} %copy-done.3, bf16[128,8192]{1,0:T(8,128)(2,1)S(1)} %copy-done.5, bf16[9,8192]{1,0:T(8,128)(2,1)S(1)} %pad_maximum_fusion.coeff_ref, bf16[5120,128]{1,0:T(8,128)(2,1)} %collective-permute-done.6.partner_ref), custom_call_target="tpu_custom_call" | custom-call | flops 1509949440 | bytes 3932160 | tf_op jit(solution)/shard_map/second_part/pallas_call | solution.py:276
  56.9 3.3 %second_last.1 = (bf16[9,128,128]{2,1,0:T(8,128)(2,1)S(1)}, bf16[9,128,128]{2,1,0:T(8,128)(2,1)S(1)}, bf16[9,128,128]{2,1,0:T(8,128)(2,1)S(1)}) custom-call(s32[6]{0:T(128)S(1)} %pad_add_fusion.switch_ref, bf16[128,8192]{1,0:T(8,128)(2,1)S(1)} %copy-done.3, bf16[128,8192]{1,0:T(8,128)(2,1)S(1)} %copy-done.5, bf16[9,8192]{1,0:T(8,128)(2,1)S(1)} %pad_maximum_fusion.coeff_ref, ...), custom_call_target="tpu_custom_call" | custom-call | flops 905969664 | bytes 2359296 | tf_op jit(solution)/shard_map/second_last/pallas_call | solution.py:276
  60.2 7.5 %collective-permute-start.8 = (bf16[9,128,128]{2,1,0:T(8,128)(2,1)S(1)}, bf16[9,128,128]{2,1,0:T(8,128)(2,1)S(1)}, u32[]{:S(2)}, u32[]{:S(2)}) collective-permute-start(bf16[9,128,128]{2,1,0:T(8,128)(2,1)S(1)} %get-tuple-element.47), channel_id=1, source_target_pairs={{0,8},{12,4},{14,6},{7,15},{9,1},{2,10},{11,3},{5,13},{1,0},{16,24... | collective-permute-start | bytes 884744 | tf_op jit(solution)/shard_map/ppermute | solution.py:357
  67.8 4.0 %collective-permute-done.8 = bf16[9,128,128]{2,1,0:T(8,128)(2,1)S(1)} collective-permute-done((bf16[9,128,128]{2,1,0:T(8,128)(2,1)S(1)}, bf16[9,128,128]{2,1,0:T(8,128)(2,1)S(1)}, u32[]{:S(2)}, u32[]{:S(2)}) %collective-permute-start.8) | collective-permute-done | bytes 294944 | tf_op jit(solution)/shard_map/ppermute | solution.py:357
  71.8 0.9 %select_bitcast_fusion = (bf16[1,9,128,128]{3,2,1,0:T(8,128)(2,1)}, bf16[1,9,128,128]{3,2,1,0:T(8,128)(2,1)}) fusion(bf16[9,128,128]{2,1,0:T(8,128)(2,1)S(1)} %collective-permute-done.8, bf16[9,128,128]{2,1,0:T(8,128)(2,1)S(1)} %get-tuple-element.49, pred[]{:T(512)S(6)} %or.59, bf16[9,128,128]{2,1,0:T(8,128)(2,1)S(1)} %get-tuple-element.48, pred[]{:T(512)} %eq.53), kind=kLoop, calls=%fused_computation | loop fusion | flops 294912 | bytes 1474562 | tf_op jit(solution)/shard_map/broadcast_in_dim | solution.py:360
  (33 shorter events, 1.5 us)
Async XLA Ops:
  0.6 18.8 %copy-start.6 = (s32[2]{0:T(128)S(1)}, s32[2]{0:T(128)}, u32[]{:S(2)}) copy-start(s32[2]{0:T(128)} %constant.58.clone.1.active_ref) | copy-start | bytes 28
  0.6 28.1 %collective-permute-start.3 = (bf16[8192,128]{1,0:T(8,128)(2,1)}, bf16[8192,128]{1,0:T(8,128)(2,1)}, u32[]{:S(2)}, u32[]{:S(2)}) collective-permute-start(bf16[8192,128]{1,0:T(8,128)(2,1)} %bitcast.15), channel_id=1, source_target_pairs={{3,2},{5,4},{6,5},{9,8},{10,9},{11,10},{12,11},{13,12},{14,13},{15... | collective-permute-start | bytes 6291464 | tf_op jit(solution)/shard_map/ppermute | solution.py:326
  2.6 26.1 %collective-permute-start.4 = (bf16[8192,128]{1,0:T(8,128)(2,1)}, bf16[8192,128]{1,0:T(8,128)(2,1)}, u32[]{:S(2)}, u32[]{:S(2)}) collective-permute-start(bf16[8192,128]{1,0:T(8,128)(2,1)} %bitcast.16), channel_id=1, source_target_pairs={{8,0},{4,12},{6,14},{15,7},{0,1},{7,6},{24,16},{20,28},{22,30},{31... | collective-permute-start | bytes 6291464 | tf_op jit(solution)/shard_map/ppermute | solution.py:327
  3.9 29.7 %collective-permute-start.1 = (s32[1,4]{1,0:T(1,128)}, s32[1,4]{1,0:T(1,128)S(1)}, u32[]{:S(2)}, u32[]{:S(2)}) collective-permute-start(s32[1,4]{1,0:T(1,128)} %param.3), channel_id=1, source_target_pairs={{3,2},{5,4},{6,5},{9,8},{10,9},{11,10},{12,11},{13,12},{14,13},{15... | collective-permute-start | bytes 56 | tf_op jit(solution)/shard_map/ppermute | solution.py:332
  4.6 29.0 %collective-permute-start.2 = (s32[1,4]{1,0:T(1,128)}, s32[1,4]{1,0:T(1,128)S(1)}, u32[]{:S(2)}, u32[]{:S(2)}) collective-permute-start(s32[1,4]{1,0:T(1,128)} %param.3), channel_id=1, source_target_pairs={{8,0},{4,12},{6,14},{15,7},{0,1},{7,6},{24,16},{20,28},{22,30},{31... | collective-permute-start | bytes 56 | tf_op jit(solution)/shard_map/ppermute | solution.py:331
  5.9 44.8 %collective-permute-start = (s32[1,4]{1,0:T(1,128)}, s32[1,4]{1,0:T(1,128)S(1)}, u32[]{:S(2)}, u32[]{:S(2)}) collective-permute-start(s32[1,4]{1,0:T(1,128)} %param.3), channel_id=1, source_target_pairs={{1,9},{10,2},{3,11},{13,5},{2,1},{4,3},{17,25},{26,18},{19,27},{29... | collective-permute-start | bytes 56 | tf_op jit(solution)/shard_map/ppermute | solution.py:333
  16.4 1.6 %copy-start = (bf16[1024,2,4,128]{3,2,1,0:T(4,128)(2,1)S(1)}, bf16[1024,2,4,128]{3,2,1,0:T(4,128)(2,1)}, u32[]{:S(2)}) copy-start(bf16[1024,2,4,128]{3,2,1,0:T(4,128)(2,1)} %param.2) | copy-start | bytes 6291460
  18.0 2.1 %copy-start.1 = (bf16[1024,2,4,128]{3,2,1,0:T(4,128)(2,1)S(1)}, bf16[1024,2,4,128]{3,2,1,0:T(4,128)(2,1)}, u32[]{:S(2)}) copy-start(bf16[1024,2,4,128]{3,2,1,0:T(4,128)(2,1)} %param.2) | copy-start | bytes 6291460
  18.3 1.1 %copy-start.7 = (bf16[5120,128]{1,0:T(8,128)(2,1)}, bf16[5120,128]{1,0:T(8,128)(2,1)S(1)}, u32[]{:S(2)}) copy-start(bf16[5120,128]{1,0:T(8,128)(2,1)S(1)} %get-tuple-element.43) | copy-start | bytes 3932164
  19.4 14.2 %copy-start.8 = (s32[1,4]{1,0:T(1,128)S(1)}, s32[1,4]{1,0:T(1,128)}, u32[]{:S(2)}) copy-start(s32[1,4]{1,0:T(1,128)} %param.3) | copy-start | bytes 52
  24.0 1.3 %copy-start.2 = (bf16[128,8192]{1,0:T(8,128)(2,1)}, bf16[128,8192]{1,0:T(8,128)(2,1)S(1)}, u32[]{:S(2)}) copy-start(bf16[128,8192]{1,0:T(8,128)(2,1)S(1)} %get-tuple-element.29.plain_ref) | copy-start | bytes 6291460
  25.4 1.4 %copy-start.4 = (bf16[128,8192]{1,0:T(8,128)(2,1)}, bf16[128,8192]{1,0:T(8,128)(2,1)S(1)}, u32[]{:S(2)}) copy-start(bf16[128,8192]{1,0:T(8,128)(2,1)S(1)} %get-tuple-element.30.swapped_ref) | copy-start | bytes 6291460
  28.8 22.1 %collective-permute-start.6 = (bf16[5120,128]{1,0:T(8,128)(2,1)}, bf16[5120,128]{1,0:T(8,128)(2,1)}, u32[]{:S(2)}, u32[]{:S(2)}) collective-permute-start(bf16[5120,128]{1,0:T(8,128)(2,1)} %copy-done.7), channel_id=1, source_target_pairs={{1,9},{10,2},{3,11},{13,5},{2,1},{4,3},{17,25},{26,18},{19,27},{29... | collective-permute-start | bytes 3932168 | tf_op jit(solution)/shard_map/ppermute | solution.py:341
  33.5 1.8 %copy-start.3 = (bf16[128,8192]{1,0:T(8,128)(2,1)S(1)}, bf16[128,8192]{1,0:T(8,128)(2,1)}, u32[]{:S(2)}) copy-start(bf16[128,8192]{1,0:T(8,128)(2,1)} %copy-done.2) | copy-start | bytes 6291460
  35.3 1.6 %copy-start.5 = (bf16[128,8192]{1,0:T(8,128)(2,1)S(1)}, bf16[128,8192]{1,0:T(8,128)(2,1)}, u32[]{:S(2)}) copy-start(bf16[128,8192]{1,0:T(8,128)(2,1)} %copy-done.4) | copy-start | bytes 6291460
  42.4 14.6 %collective-permute-start.5 = (bf16[3072,128]{1,0:T(8,128)(2,1)S(1)}, bf16[3072,128]{1,0:T(8,128)(2,1)S(1)}, u32[]{:S(2)}, u32[]{:S(2)}) collective-permute-start(bf16[3072,128]{1,0:T(8,128)(2,1)S(1)} %get-tuple-element.42), channel_id=1, source_target_pairs={{1,9},{10,2},{3,11},{13,5},{2,1},{4,3},{17,25},{26,18},{19,27},{29... | collective-permute-start | bytes 2359304 | tf_op jit(solution)/shard_map/ppermute | solution.py:346
  50.0 0.8 %collective-permute-start.7 = (bf16[9,128,128]{2,1,0:T(8,128)(2,1)S(1)}, bf16[9,128,128]{2,1,0:T(8,128)(2,1)S(1)}, u32[]{:S(2)}, u32[]{:S(2)}) collective-permute-start(bf16[9,128,128]{2,1,0:T(8,128)(2,1)S(1)} %get-tuple-element.45), channel_id=1, source_target_pairs={{0,7},{7,15},{16,23},{23,31}} | collective-permute-start | bytes 884744 | tf_op jit(solution)/shard_map/ppermute | solution.py:348
  60.2 11.5 %collective-permute-start.8 = (bf16[9,128,128]{2,1,0:T(8,128)(2,1)S(1)}, bf16[9,128,128]{2,1,0:T(8,128)(2,1)S(1)}, u32[]{:S(2)}, u32[]{:S(2)}) collective-permute-start(bf16[9,128,128]{2,1,0:T(8,128)(2,1)S(1)} %get-tuple-element.47), channel_id=1, source_target_pairs={{0,8},{12,4},{14,6},{7,15},{9,1},{2,10},{11,3},{5,13},{1,0},{16,24... | collective-permute-start | bytes 884744 | tf_op jit(solution)/shard_map/ppermute | solution.py:357

commit v15 on v14

--- a/solution.py
+++ b/solution.py
@@ -59,39 +59,39 @@
     )(x)
 
 
-def turn_kernel(active_ref, x_ref, plain_ref, swapped_ref):
-    @pl.when(active_ref[0] != 0)
-    def _():
-        rows, cols = x_ref.shape
-        same = lax.broadcasted_iota(jnp.int32, (cols, cols), 0) == lax.broadcasted_iota(jnp.int32, (cols, cols), 1)
-        eye = jnp.where(same, 1.0, 0.0).astype(jnp.bfloat16)
-        source = lax.broadcasted_iota(jnp.int32, (2 * cols, 2 * cols), 0)
-        target = lax.broadcasted_iota(jnp.int32, (2 * cols, 2 * cols), 1)
-        exchange = jnp.where((source ^ 4) == target, 1.0, 0.0).astype(jnp.bfloat16)
-        plain = lax.dot_general(eye, x_ref[...], (((1,), (1,)), ((), ())), preferred_element_type=jnp.float32)
-        plain = plain.astype(jnp.bfloat16)
-        plain_ref[...] = plain
-        for t in range(0, rows, 2 * cols):
-            swapped = jnp.dot(plain[:, t:t + 2 * cols], exchange, preferred_element_type=jnp.float32)
-            swapped_ref[:, t:t + 2 * cols] = swapped.astype(jnp.bfloat16)
-
-
-def turn(x, switch, name, common=True):
+def turned(x):
+    rows, cols = x.shape
+    same = lax.broadcasted_iota(jnp.int32, (cols, cols), 0) == lax.broadcasted_iota(jnp.int32, (cols, cols), 1)
+    eye = jnp.where(same, 1.0, 0.0).astype(jnp.bfloat16)
+    source = lax.broadcasted_iota(jnp.int32, (2 * cols, 2 * cols), 0)
+    target = lax.broadcasted_iota(jnp.int32, (2 * cols, 2 * cols), 1)
+    exchange = jnp.where((source ^ 4) == target, 1.0, 0.0).astype(jnp.bfloat16)
+    plain = lax.dot_general(eye, x, (((1,), (1,)), ((), ())), preferred_element_type=jnp.float32)
+    plain = plain.astype(jnp.bfloat16)
+    swapped = [
+        jnp.dot(plain[:, t:t + 2 * cols], exchange, preferred_element_type=jnp.float32).astype(jnp.bfloat16)
+        for t in range(0, rows, 2 * cols)
+    ]
+    return plain, jnp.concatenate(swapped, axis=1)
+
+
+def turn_kernel(x_ref, plain_ref, swapped_ref):
+    plain_ref[...], swapped_ref[...] = turned(x_ref[...])
+
+
+def turn(x):
     rows, cols = x.shape
     out = jax.ShapeDtypeStruct((cols, rows), jnp.bfloat16)
     return pl.pallas_call(
         turn_kernel,
-        grid_spec=pltpu.PrefetchScalarGridSpec(
-            num_scalar_prefetch=1,
-            grid=(rows // STEP,),
-            in_specs=[pl.BlockSpec((STEP, cols), lambda s, on: (s * on[0], 0))],
-            out_specs=[pl.BlockSpec((cols, STEP), lambda s, on: (0, s * on[0]))] * 2,
-        ),
+        grid=(rows // STEP,),
+        in_specs=[pl.BlockSpec((STEP, cols), lambda s: (s, 0))],
+        out_specs=[pl.BlockSpec((cols, STEP), lambda s: (0, s))] * 2,
         out_shape=[out, out],
         compiler_params=PARAMS,
-        cost_estimate=pl.CostEstimate(flops=0, bytes_accessed=6 * rows * cols if common else 0, transcendentals=0),
-        name=name,
-    )(switch, x)
+        cost_estimate=pl.CostEstimate(flops=0, bytes_accessed=6 * rows * cols, transcendentals=0),
+        name="turn",
+    )(x)
 
 
 def write_lags(out, acc, at, cols, mirrored):
@@ -125,15 +125,14 @@
     return x * weights.reshape(rows, cols)
 
 
-def first_kernel(windows, last, switch_ref, plain_ref, swapped_ref, plain_alt, swapped_alt, coeff_ref, near_ref, first_ref,
-                 own_ref, *rest):
+def first_kernel(windows, last, switch_ref, plain_ref, swapped_ref, coeff_ref, near_ref, first_ref, own_ref, *rest):
     step = pl.program_id(0)
     cols = plain_ref.shape[0]
     near_mirrored, special = switch_ref[0], switch_ref[1]
     if last:
-        acc_in, _, near_out, far_out, back_out, acc, scaled = rest
+        acc_in, _, near_out, far_out, back_out, acc, scaled, plain, swapped = rest
     else:
-        acc, token_out, scaled = rest
+        acc, token_out, scaled, plain, swapped = rest
 
     @pl.when(step == 0)
     def _():
@@ -143,9 +142,15 @@
             acc[...] = jnp.zeros_like(acc)
             token_out[...] = jnp.zeros_like(token_out)
 
-    plain = jnp.where(special != 0, plain_alt[...], plain_ref[...])
-    swapped = jnp.where(special != 0, swapped_alt[...], swapped_ref[...])
-    scale(scaled, plain, swapped, coeff_ref)
+    @pl.when(special == 0)
+    def _():
+        plain[...], swapped[...] = plain_ref[...], swapped_ref[...]
+
+    @pl.when(special != 0)
+    def _():
+        plain[...], swapped[...] = turned(first_ref[...])
+
+    scale(scaled, plain[...], swapped[...], coeff_ref)
     flags = [[switch_ref[2 + part * windows + w] for w in range(windows)] for part in range(3)]
     near_weights = [jnp.where(special != 0, first, own) * near for own, near, first in zip(*flags)]
     near = weigh(near_ref[...], near_weights)
@@ -171,7 +176,7 @@
             pl.when(near_mirrored != 0)(lambda: write_lags(near_out, acc, near_at, cols, True))
 
 
-def first_sums(switch, own, alt, coeffs, near_in, first_in, block, earlier=None):
+def first_sums(switch, own, coeffs, near_in, first_in, block, earlier=None):
     rows, cols = block.shape
     steps = rows // STEP // 2
     skip = 0 if earlier is None else steps
@@ -182,13 +187,10 @@
     token = jax.ShapeDtypeStruct((8, cols), jnp.float32)
     token_spec = pl.BlockSpec(token.shape, lambda s, on: (0, 0))
     left = pl.BlockSpec((cols, STEP), lambda s, on: (0, (s + skip) * (1 - on[1])))
-    left_alt = pl.BlockSpec((cols, STEP), lambda s, on: (0, (s + skip) * on[1]))
     right = pl.BlockSpec((STEP, cols), lambda s, on: (s + skip, 0))
-    right_usual = pl.BlockSpec((STEP, cols), lambda s, on: ((s + skip) * (1 - on[1]), 0))
     right_special = pl.BlockSpec((STEP, cols), lambda s, on: ((s + skip) * on[1], 0))
-    in_specs = [left, left, left_alt, left_alt, pl.BlockSpec((LAGS, STEP), lambda s, on: (0, s + skip)),
-                right, right_usual, right_special]
-    scratch = [pltpu.VMEM((LAGS * cols, STEP), jnp.bfloat16)]
+    in_specs = [left, left, pl.BlockSpec((LAGS, STEP), lambda s, on: (0, s + skip)), right, right, right_special]
+    scratch = [pltpu.VMEM((LAGS * cols, STEP), jnp.bfloat16)] + [pltpu.VMEM((cols, STEP), jnp.bfloat16)] * 2
     if earlier is None:
         out_shape, out_specs, earlier = [total, token], [total_spec, token_spec], []
     else:
@@ -211,7 +213,7 @@
             flops=2 * LAGS * cols * cols * rows, bytes_accessed=4 * rows * cols, transcendentals=0
         ),
         name="first_last" if earlier else "first_half",
-    )(switch, *own, *alt, coeffs, near_in, first_in, block, *earlier)
+    )(switch, *own, coeffs, near_in, first_in, block, *earlier)
 
 
 def second_kernel(windows, first, switch_ref, plain_ref, swapped_ref, coeff_ref, partner_ref, *rest):
@@ -326,7 +328,7 @@
     near_in = lax.ppermute(block, "chan", near_pairs)
     first_in = lax.ppermute(block, "chan", first_pairs)
     coeffs = lag_rows(freq_count, window_count)
-    own = turn(block, switch(True, False), "turn_own")
+    own = turn(block)
     parts = split(block)
     first_flags = lax.ppermute(quality, "chan", first_pairs)[0]
     near_flags = lax.ppermute(quality, "chan", near_pairs)[0]
@@ -337,24 +339,25 @@
         among([t for _, t in second_pairs]), among([t for _, t in late_near]), quality[0] * second_flags
     )
 
-    near_in, first_part, own, coeffs, first_in = lax.optimization_barrier((near_in, parts[0], own, coeffs, first_in))
+    near_in, first_part, last_part, own, coeffs, first_in = lax.optimization_barrier(
+        (near_in, *parts, own, coeffs, first_in)
+    )
     second_in = [lax.ppermute(first_part, "chan", second_pairs)]
-    alt = turn(first_in, switch(special, False), "turn_first", common=False)
-    operands = first_switch, own, alt, coeffs, near_in, first_in, block
+    operands = first_switch, own, coeffs, near_in, first_in, block
     total, token = first_sums(*operands)
-    last_part, token = lax.optimization_barrier((parts[1], token))
+    last_part, token = lax.optimization_barrier((last_part, token))
     second_in.append(lax.ppermute(last_part, "chan", second_pairs))
     near, far, back = first_sums(*operands, [total, token])
     side_returned = lax.ppermute(near, "chan", side_pairs)
     second_switch, near = lax.optimization_barrier((second_switch, near))
     total, = second_sums(second_switch, own, coeffs, second_in[0], 0)
 
-    near = jnp.where(among([half - 1, count - 1]), side_returned, near)
     near = jnp.where(me == half - 2, far, near)
     near, far, back = second_sums(
         second_switch, own, coeffs, second_in[1], parts[0].shape[0], [total, near, far, back]
     )
     returned = lax.ppermute(back, "chan", back_pairs)
+    near = jnp.where(among([half - 1, count - 1]), side_returned, near)
     near = jnp.where(me == 0, returned, near)
     far = jnp.where(among([s for s, _ in first_far + second_far]), returned, far)
     return near[None], far[None]

time: 73.5 us -> 73.5 us (level)
  waiting for transfers between devices: 3.99 us -> 9.29 us
  Pallas kernels: 26.3 us -> 24 us
  starting transfers between devices: 30.5 us -> 28.5 us
    ppermute x1, starting transfers between devices: 7.52 us -> 1.92 us  [local(): returned = lax.ppermute(back, 'chan', back_pairs)]
    ppermute x1, waiting for transfers between devices: 3.96 us -> 9.27 us  [local(): returned = lax.ppermute(back, 'chan', back_pairs)]
    ppermute x1, starting transfers between devices: 4.65 us -> 7.59 us  [local(): second_in = [lax.ppermute(first_part, 'chan', second_pairs)]]
    pallas_call x2 -> x1, Pallas kernels: 5.51 us -> 3.15 us  [turn(): pl.pallas_call(turn_kernel, grid=(rows // STEP,), in_specs=[pl.BlockSpec(...]
    unnamed x18 -> x12, local copies, waits for them, and re-layouts: 7.62 us -> 7.16 us
  transfers between devices with their start and end apart: 9 -> 9, of which waited for: 1 -> 1; matrix products, arithmetic and copies ran while one was open for 3% -> 3% of each run, Pallas kernels for 32% -> 33%
where the time goes in v15:
time: 73.5 us; the launch traced here: 73 us
  starting transfers between devices  28.5 us (39%)
  Pallas kernels  24 us (33%)
  waiting for transfers between devices  9.29 us (13%)
  local copies, waits for them, and re-layouts  7.16 us (10%)
  other arithmetic  3.15 us (4%)
  between operations  0.9 us (1%)
    pallas_call x2, Pallas kernels, first_sums(): pl.pallas_call(functools.partial(first_kernel, windows, bool(earlier)), g...  11.2 us
    ppermute x1, starting transfers between devices, local(): second_flags = lax.ppermute(quality, 'chan', second_pairs)[0]  10.5 us
    pallas_call x2, Pallas kernels, second_sums(): pl.pallas_call(functools.partial(second_kernel, windows, not earlier), gr...  9.37 us
    ppermute x1, waiting for transfers between devices, local(): returned = lax.ppermute(back, 'chan', back_pairs)  9.27 us
    ppermute x1, starting transfers between devices, local(): second_in = [lax.ppermute(first_part, 'chan', second_pairs)]  7.59 us
    unnamed x12, local copies, waits for them, and re-layouts  7.16 us
    pallas_call x1, Pallas kernels, turn(): pl.pallas_call(turn_kernel, grid=(rows // STEP,), in_specs=[pl.BlockSpec(...  3.15 us
    ppermute x1, starting transfers between devices, local(): near_in = lax.ppermute(block, 'chan', near_pairs)  2 us
  transfers between devices with their start and end apart: 9, of which 1 were waited for; matrix products, arithmetic and copies ran while one was open for 3% of the time, Pallas kernels for 33%

profile of v15, /device:TPU:1, one launch (start us, length us, event | category | flops | bytes accessed | tf_op | source)
XLA Modules:
  0.0 73.0 jit_solution(17964203834647994010)
XLA Ops:
  0.6 2.0 %collective-permute-start.3 = (bf16[8192,128]{1,0:T(8,128)(2,1)}, bf16[8192,128]{1,0:T(8,128)(2,1)}, u32[]{:S(2)}, u32[]{:S(2)}) collective-permute-start(bf16[8192,128]{1,0:T(8,128)(2,1)} %bitcast.15), channel_id=1, source_target_pairs={{3,2},{5,4},{6,5},{9,8},{10,9},{11,10},{12,11},{13,12},{14,13},{15... | collective-permute-start | bytes 6291464 | tf_op jit(solution)/shard_map/ppermute | solution.py:328
  2.6 1.3 %collective-permute-start.4 = (bf16[8192,128]{1,0:T(8,128)(2,1)}, bf16[8192,128]{1,0:T(8,128)(2,1)}, u32[]{:S(2)}, u32[]{:S(2)}) collective-permute-start(bf16[8192,128]{1,0:T(8,128)(2,1)} %bitcast.16), channel_id=1, source_target_pairs={{8,0},{4,12},{6,14},{15,7},{0,1},{7,6},{24,16},{20,28},{22,30},{31... | collective-permute-start | bytes 6291464 | tf_op jit(solution)/shard_map/ppermute | solution.py:329
  3.9 0.7 collective-permute-start.1
  4.6 1.3 %collective-permute-start.2 = (s32[1,4]{1,0:T(1,128)}, s32[1,4]{1,0:T(1,128)S(1)}, u32[]{:S(2)}, u32[]{:S(2)}) collective-permute-start(s32[1,4]{1,0:T(1,128)} %param.3), channel_id=1, source_target_pairs={{8,0},{4,12},{6,14},{15,7},{0,1},{7,6},{24,16},{20,28},{22,30},{31... | collective-permute-start | bytes 56 | tf_op jit(solution)/shard_map/ppermute | solution.py:333
  5.9 10.5 %collective-permute-start = (s32[1,4]{1,0:T(1,128)}, s32[1,4]{1,0:T(1,128)S(1)}, u32[]{:S(2)}, u32[]{:S(2)}) collective-permute-start(s32[1,4]{1,0:T(1,128)} %param.3), channel_id=1, source_target_pairs={{1,9},{10,2},{3,11},{13,5},{2,1},{4,3},{17,25},{26,18},{19,27},{29... | collective-permute-start | bytes 56 | tf_op jit(solution)/shard_map/ppermute | solution.py:335
  16.4 1.6 %copy-done.2 = bf16[1024,2,4,128]{3,2,1,0:T(4,128)(2,1)S(1)} copy-done((bf16[1024,2,4,128]{3,2,1,0:T(4,128)(2,1)S(1)}, bf16[1024,2,4,128]{3,2,1,0:T(4,128)(2,1)}, u32[]{:S(2)}) %copy-start.2) | copy-done | bytes 2097176
  18.0 3.2 %turn.1 = (bf16[128,8192]{1,0:T(8,128)(2,1)S(1)}, bf16[128,8192]{1,0:T(8,128)(2,1)S(1)}) custom-call(bf16[8192,128]{1,0:T(8,128)(2,1)S(1)} %bitcast.17), custom_call_target="tpu_custom_call" | custom-call | bytes 6291456 | tf_op jit(solution)/shard_map/turn/pallas_call | solution.py:85
  21.1 1.3 %copy-done = bf16[128,8192]{1,0:T(8,128)(2,1)} copy-done((bf16[128,8192]{1,0:T(8,128)(2,1)}, bf16[128,8192]{1,0:T(8,128)(2,1)S(1)}, u32[]{:S(2)}) %copy-start) | copy-done | bytes 2097176
  22.5 0.3 split.1
  22.8 1.0 %copy-done.4 = bf16[5120,128]{1,0:T(8,128)(2,1)} copy-done((bf16[5120,128]{1,0:T(8,128)(2,1)}, bf16[5120,128]{1,0:T(8,128)(2,1)S(1)}, u32[]{:S(2)}) %copy-start.4) | copy-done | bytes 1310744
  23.9 0.9 %multiply_convert_fusion = (bf16[5,8192]{1,0:T(8,128)(2,1)S(1)}, f32[5,8192]{1,0:T(8,128)S(1)}) fusion(f32[8192]{0:T(1024)S(1)} %fusion.9, f32[5]{0:T(128)S(1)} %iota_multiply_fusion), kind=kLoop, calls=%fused_computation.4 | loop fusion | flops 122880 | bytes 278548 | tf_op jit(solution)/shard_map/convert
  24.8 0.9 %fusion.2 = bf16[4,8192]{1,0:T(4,128)(2,1)S(1)} fusion(f32[5,8192]{1,0:T(8,128)S(1)} %get-tuple-element.51, f32[8192]{0:T(1024)S(1)} %select_multiply_fusion), kind=kLoop, calls=%fused_computation.8 | loop fusion | flops 98304 | bytes 229376 | tf_op jit(solution)/shard_map/convert.1
  25.8 7.6 %collective-permute-start.6 = (bf16[5120,128]{1,0:T(8,128)(2,1)}, bf16[5120,128]{1,0:T(8,128)(2,1)}, u32[]{:S(2)}, u32[]{:S(2)}) collective-permute-start(bf16[5120,128]{1,0:T(8,128)(2,1)} %copy-done.4), channel_id=1, source_target_pairs={{1,9},{10,2},{3,11},{13,5},{2,1},{4,3},{17,25},{26,18},{19,27},{29... | collective-permute-start | bytes 3932168 | tf_op jit(solution)/shard_map/ppermute | solution.py:345
  33.7 1.6 %copy-done.1 = bf16[128,8192]{1,0:T(8,128)(2,1)S(1)} copy-done((bf16[128,8192]{1,0:T(8,128)(2,1)S(1)}, bf16[128,8192]{1,0:T(8,128)(2,1)}, u32[]{:S(2)}) %copy-start.1) | copy-done | bytes 2097176
  35.3 1.6 %copy-done.3 = bf16[1024,2,4,128]{3,2,1,0:T(4,128)(2,1)S(1)} copy-done((bf16[1024,2,4,128]{3,2,1,0:T(4,128)(2,1)S(1)}, bf16[1024,2,4,128]{3,2,1,0:T(4,128)(2,1)}, u32[]{:S(2)}) %copy-start.3) | copy-done | bytes 2097176
  36.8 5.5 %first_half.1 = (f32[1152,256]{1,0:T(8,128)S(1)}, f32[8,128]{1,0:T(8,128)S(1)}) custom-call(s32[14]{0:T(128)S(1)} %pad_add_fusion.1.switch_ref, bf16[128,8192]{1,0:T(8,128)(2,1)S(1)} %get-tuple-element.29.plain_ref, bf16[128,8192]{1,0:T(8,128)(2,1)S(1)} %copy-done.1, bf16[9,8192]{1,0:T(8,128)(2,1)S(1)} %pad_maximum_fusion.coeff_ref, ...), custom_call_target="tpu_custom_call" | custom-call | flops 2415919104 | bytes 4194304 | tf_op jit(solution)/shard_map/first_half/pallas_call | solution.py:201
  42.3 1.9 %collective-permute-start.5 = (bf16[3072,128]{1,0:T(8,128)(2,1)S(1)}, bf16[3072,128]{1,0:T(8,128)(2,1)S(1)}, u32[]{:S(2)}, u32[]{:S(2)}) collective-permute-start(bf16[3072,128]{1,0:T(8,128)(2,1)S(1)} %get-tuple-element.40), channel_id=1, source_target_pairs={{1,9},{10,2},{3,11},{13,5},{2,1},{4,3},{17,25},{26,18},{19,27},{29... | collective-permute-start | bytes 2359304 | tf_op jit(solution)/shard_map/ppermute | solution.py:349
  44.4 5.7 %first_last.1 = (bf16[9,128,128]{2,1,0:T(8,128)(2,1)S(1)}, bf16[9,128,128]{2,1,0:T(8,128)(2,1)S(1)}, bf16[9,128,128]{2,1,0:T(8,128)(2,1)S(1)}) custom-call(s32[14]{0:T(128)S(1)} %pad_add_fusion.1.switch_ref, bf16[128,8192]{1,0:T(8,128)(2,1)S(1)} %get-tuple-element.29.plain_ref, bf16[128,8192]{1,0:T(8,128)(2,1)S(1)} %copy-done.1, ...), custom_call_target="tpu_custom_call" | custom-call | flops 2415919104 | bytes 4194304 | tf_op jit(solution)/shard_map/first_last/pallas_call | solution.py:201
  50.0 1.4 %collective-permute-start.8 = (bf16[9,128,128]{2,1,0:T(8,128)(2,1)S(1)}, bf16[9,128,128]{2,1,0:T(8,128)(2,1)}, u32[]{:S(2)}, u32[]{:S(2)}) collective-permute-start(bf16[9,128,128]{2,1,0:T(8,128)(2,1)S(1)} %get-tuple-element.43), channel_id=1, source_target_pairs={{0,7},{7,15},{16,23},{23,31}} | collective-permute-start | bytes 884744 | tf_op jit(solution)/shard_map/ppermute | solution.py:351
  51.5 6.1 %second_part.1.rest_0_ = f32[1152,128]{1,0:T(8,128)S(1)} custom-call(s32[6]{0:T(128)S(1)} %pad_add_fusion.switch_ref, bf16[128,8192]{1,0:T(8,128)(2,1)S(1)} %get-tuple-element.29.plain_ref, bf16[128,8192]{1,0:T(8,128)(2,1)S(1)} %copy-done.1, bf16[9,8192]{1,0:T(8,128)(2,1)S(1)} %pad_maximum_fusion.coeff_ref, bf16[5120,128]{1,0:T(8,128)(2,1)} %collective-permute-done.6.partner_ref), custom_call_target="tpu_custom_call" | custom-call | flops 1509949440 | bytes 3932160 | tf_op jit(solution)/shard_map/second_part/pallas_call | solution.py:278
  57.5 3.3 %second_last.1 = (bf16[9,128,128]{2,1,0:T(8,128)(2,1)S(1)}, bf16[9,128,128]{2,1,0:T(8,128)(2,1)S(1)}, bf16[9,128,128]{2,1,0:T(8,128)(2,1)S(1)}) custom-call(s32[6]{0:T(128)S(1)} %pad_add_fusion.switch_ref, bf16[128,8192]{1,0:T(8,128)(2,1)S(1)} %get-tuple-element.29.plain_ref, bf16[128,8192]{1,0:T(8,128)(2,1)S(1)} %copy-done.1, ...), custom_call_target="tpu_custom_call" | custom-call | flops 905969664 | bytes 2359296 | tf_op jit(solution)/shard_map/second_last/pallas_call | solution.py:278
  60.9 1.9 %collective-permute-start.7 = (bf16[9,128,128]{2,1,0:T(8,128)(2,1)S(1)}, bf16[9,128,128]{2,1,0:T(8,128)(2,1)S(1)}, u32[]{:S(2)}, u32[]{:S(2)}) collective-permute-start(bf16[9,128,128]{2,1,0:T(8,128)(2,1)S(1)} %get-tuple-element.45), channel_id=1, source_target_pairs={{0,8},{12,4},{14,6},{7,15},{9,1},{2,10},{11,3},{5,13},{1,0},{16,24... | collective-permute-start | bytes 884744 | tf_op jit(solution)/shard_map/ppermute | solution.py:359
  62.9 9.3 %collective-permute-done.7 = bf16[9,128,128]{2,1,0:T(8,128)(2,1)S(1)} collective-permute-done((bf16[9,128,128]{2,1,0:T(8,128)(2,1)S(1)}, bf16[9,128,128]{2,1,0:T(8,128)(2,1)S(1)}, u32[]{:S(2)}, u32[]{:S(2)}) %collective-permute-start.7) | collective-permute-done | bytes 294944 | tf_op jit(solution)/shard_map/ppermute | solution.py:359
  72.1 0.9 %select_bitcast_fusion = (bf16[1,9,128,128]{3,2,1,0:T(8,128)(2,1)}, bf16[1,9,128,128]{3,2,1,0:T(8,128)(2,1)}) fusion(bf16[9,128,128]{2,1,0:T(8,128)(2,1)S(1)} %collective-permute-done.7, bf16[9,128,128]{2,1,0:T(8,128)(2,1)S(1)} %get-tuple-element.47, pred[]{:T(512)S(6)} %or.59, bf16[9,128,128]{2,1,0:T(8,128)(2,1)} %collective-permute-done.8, ...), kind=kLoop, calls=%fused_computation | loop fusion | flops 442368 | bytes 1769475 | tf_op jit(solution)/shard_map/broadcast_in_dim | solution.py:363
  (25 shorter events, 0.5 us)
Async XLA Ops:
  0.6 25.2 %collective-permute-start.3 = (bf16[8192,128]{1,0:T(8,128)(2,1)}, bf16[8192,128]{1,0:T(8,128)(2,1)}, u32[]{:S(2)}, u32[]{:S(2)}) collective-permute-start(bf16[8192,128]{1,0:T(8,128)(2,1)} %bitcast.15), channel_id=1, source_target_pairs={{3,2},{5,4},{6,5},{9,8},{10,9},{11,10},{12,11},{13,12},{14,13},{15... | collective-permute-start | bytes 6291464 | tf_op jit(solution)/shard_map/ppermute | solution.py:328
  2.6 23.2 %collective-permute-start.4 = (bf16[8192,128]{1,0:T(8,128)(2,1)}, bf16[8192,128]{1,0:T(8,128)(2,1)}, u32[]{:S(2)}, u32[]{:S(2)}) collective-permute-start(bf16[8192,128]{1,0:T(8,128)(2,1)} %bitcast.16), channel_id=1, source_target_pairs={{8,0},{4,12},{6,14},{15,7},{0,1},{7,6},{24,16},{20,28},{22,30},{31... | collective-permute-start | bytes 6291464 | tf_op jit(solution)/shard_map/ppermute | solution.py:329
  3.9 29.7 %collective-permute-start.1 = (s32[1,4]{1,0:T(1,128)}, s32[1,4]{1,0:T(1,128)S(1)}, u32[]{:S(2)}, u32[]{:S(2)}) collective-permute-start(s32[1,4]{1,0:T(1,128)} %param.3), channel_id=1, source_target_pairs={{3,2},{5,4},{6,5},{9,8},{10,9},{11,10},{12,11},{13,12},{14,13},{15... | collective-permute-start | bytes 56 | tf_op jit(solution)/shard_map/ppermute | solution.py:334
  4.6 29.0 %collective-permute-start.2 = (s32[1,4]{1,0:T(1,128)}, s32[1,4]{1,0:T(1,128)S(1)}, u32[]{:S(2)}, u32[]{:S(2)}) collective-permute-start(s32[1,4]{1,0:T(1,128)} %param.3), channel_id=1, source_target_pairs={{8,0},{4,12},{6,14},{15,7},{0,1},{7,6},{24,16},{20,28},{22,30},{31... | collective-permute-start | bytes 56 | tf_op jit(solution)/shard_map/ppermute | solution.py:333
  5.9 38.4 %collective-permute-start = (s32[1,4]{1,0:T(1,128)}, s32[1,4]{1,0:T(1,128)S(1)}, u32[]{:S(2)}, u32[]{:S(2)}) collective-permute-start(s32[1,4]{1,0:T(1,128)} %param.3), channel_id=1, source_target_pairs={{1,9},{10,2},{3,11},{13,5},{2,1},{4,3},{17,25},{26,18},{19,27},{29... | collective-permute-start | bytes 56 | tf_op jit(solution)/shard_map/ppermute | solution.py:335
  16.4 1.6 %copy-start.2 = (bf16[1024,2,4,128]{3,2,1,0:T(4,128)(2,1)S(1)}, bf16[1024,2,4,128]{3,2,1,0:T(4,128)(2,1)}, u32[]{:S(2)}) copy-start(bf16[1024,2,4,128]{3,2,1,0:T(4,128)(2,1)} %param.2) | copy-start | bytes 6291460
  21.1 1.3 %copy-start = (bf16[128,8192]{1,0:T(8,128)(2,1)}, bf16[128,8192]{1,0:T(8,128)(2,1)S(1)}, u32[]{:S(2)}) copy-start(bf16[128,8192]{1,0:T(8,128)(2,1)S(1)} %get-tuple-element.30.swapped_ref) | copy-start | bytes 6291460
  22.5 11.1 %copy-start.5 = (s32[1,4]{1,0:T(1,128)S(1)}, s32[1,4]{1,0:T(1,128)}, u32[]{:S(2)}) copy-start(s32[1,4]{1,0:T(1,128)} %param.3) | copy-start | bytes 52
  22.8 1.1 %copy-start.4 = (bf16[5120,128]{1,0:T(8,128)(2,1)}, bf16[5120,128]{1,0:T(8,128)(2,1)S(1)}, u32[]{:S(2)}) copy-start(bf16[5120,128]{1,0:T(8,128)(2,1)S(1)} %get-tuple-element.41) | copy-start | bytes 3932164
  25.8 25.7 %collective-permute-start.6 = (bf16[5120,128]{1,0:T(8,128)(2,1)}, bf16[5120,128]{1,0:T(8,128)(2,1)}, u32[]{:S(2)}, u32[]{:S(2)}) collective-permute-start(bf16[5120,128]{1,0:T(8,128)(2,1)} %copy-done.4), channel_id=1, source_target_pairs={{1,9},{10,2},{3,11},{13,5},{2,1},{4,3},{17,25},{26,18},{19,27},{29... | collective-permute-start | bytes 3932168 | tf_op jit(solution)/shard_map/ppermute | solution.py:345
  33.7 1.6 %copy-start.1 = (bf16[128,8192]{1,0:T(8,128)(2,1)S(1)}, bf16[128,8192]{1,0:T(8,128)(2,1)}, u32[]{:S(2)}) copy-start(bf16[128,8192]{1,0:T(8,128)(2,1)} %copy-done) | copy-start | bytes 6291460
  35.3 1.6 %copy-start.3 = (bf16[1024,2,4,128]{3,2,1,0:T(4,128)(2,1)S(1)}, bf16[1024,2,4,128]{3,2,1,0:T(4,128)(2,1)}, u32[]{:S(2)}) copy-start(bf16[1024,2,4,128]{3,2,1,0:T(4,128)(2,1)} %param.2) | copy-start | bytes 6291460
  42.3 15.2 %collective-permute-start.5 = (bf16[3072,128]{1,0:T(8,128)(2,1)S(1)}, bf16[3072,128]{1,0:T(8,128)(2,1)S(1)}, u32[]{:S(2)}, u32[]{:S(2)}) collective-permute-start(bf16[3072,128]{1,0:T(8,128)(2,1)S(1)} %get-tuple-element.40), channel_id=1, source_target_pairs={{1,9},{10,2},{3,11},{13,5},{2,1},{4,3},{17,25},{26,18},{19,27},{29... | collective-permute-start | bytes 2359304 | tf_op jit(solution)/shard_map/ppermute | solution.py:349
  50.0 12.8 %collective-permute-start.8 = (bf16[9,128,128]{2,1,0:T(8,128)(2,1)S(1)}, bf16[9,128,128]{2,1,0:T(8,128)(2,1)}, u32[]{:S(2)}, u32[]{:S(2)}) collective-permute-start(bf16[9,128,128]{2,1,0:T(8,128)(2,1)S(1)} %get-tuple-element.43), channel_id=1, source_target_pairs={{0,7},{7,15},{16,23},{23,31}} | collective-permute-start | bytes 884744 | tf_op jit(solution)/shard_map/ppermute | solution.py:351
  60.9 11.2 %collective-permute-start.7 = (bf16[9,128,128]{2,1,0:T(8,128)(2,1)S(1)}, bf16[9,128,128]{2,1,0:T(8,128)(2,1)S(1)}, u32[]{:S(2)}, u32[]{:S(2)}) collective-permute-start(bf16[9,128,128]{2,1,0:T(8,128)(2,1)S(1)} %get-tuple-element.45), channel_id=1, source_target_pairs={{0,8},{12,4},{14,6},{7,15},{9,1},{2,10},{11,3},{5,13},{1,0},{16,24... | collective-permute-start | bytes 884744 | tf_op jit(solution)/shard_map/ppermute | solution.py:359

commit v16 on v15

--- a/solution.py
+++ b/solution.py
@@ -12,7 +12,7 @@
 LAGS = 2 * HL + 1
 STEP = 1024
 PARTS = (5, 8)
-PARAMS = pltpu.CompilerParams(vmem_limit_bytes=16 * 1024 * 1024)
+PARAMS = pltpu.CompilerParams(vmem_limit_bytes=12 * 1024 * 1024)
 
 
 def lag_rows(freq_count, window_count):
@@ -28,35 +28,39 @@
     return jnp.concatenate([cos_part, sin_part], axis=0).astype(jnp.bfloat16)
 
 
-def split_kernel(middle, x_ref, first_ref, last_ref):
+def split_kernel(middle, windows, flags_ref, x_ref, first_ref, last_ref):
     step = pl.program_id(0)
+    masked = weigh(x_ref[...], [flags_ref[w] for w in range(windows)])
 
     @pl.when(step < middle)
     def _():
-        first_ref[...] = x_ref[...]
+        first_ref[...] = masked
 
     @pl.when(step >= middle)
     def _():
-        last_ref[...] = x_ref[...]
-
-
-def split(x):
+        last_ref[...] = masked
+
+
+def split(flags, x):
     rows, cols = x.shape
     steps = rows // STEP
     middle = steps * PARTS[0] // PARTS[1]
     return pl.pallas_call(
-        functools.partial(split_kernel, middle),
-        grid=(steps,),
-        in_specs=[pl.BlockSpec((STEP, cols), lambda s: (s, 0))],
-        out_specs=[
-            pl.BlockSpec((STEP, cols), lambda s: (jnp.minimum(s, middle - 1), 0)),
-            pl.BlockSpec((STEP, cols), lambda s: (jnp.maximum(s - middle, 0), 0)),
-        ],
+        functools.partial(split_kernel, middle, flags.shape[0]),
+        grid_spec=pltpu.PrefetchScalarGridSpec(
+            num_scalar_prefetch=1,
+            grid=(steps,),
+            in_specs=[pl.BlockSpec((STEP, cols), lambda s, on: (s, 0))],
+            out_specs=[
+                pl.BlockSpec((STEP, cols), lambda s, on: (jnp.minimum(s, middle - 1), 0)),
+                pl.BlockSpec((STEP, cols), lambda s, on: (jnp.maximum(s - middle, 0), 0)),
+            ],
+        ),
         out_shape=[jax.ShapeDtypeStruct((n * STEP, cols), x.dtype) for n in (middle, steps - middle)],
         compiler_params=PARAMS,
-        cost_estimate=pl.CostEstimate(flops=0, bytes_accessed=4 * rows * cols, transcendentals=0),
+        cost_estimate=pl.CostEstimate(flops=rows * cols, bytes_accessed=4 * rows * cols, transcendentals=0),
         name="split",
-    )(x)
+    )(flags, x)
 
 
 def turned(x):
@@ -130,9 +134,11 @@
     cols = plain_ref.shape[0]
     near_mirrored, special = switch_ref[0], switch_ref[1]
     if last:
-        acc_in, _, near_out, far_out, back_out, acc, scaled, plain, swapped = rest
+        acc_in, _, near_out, far_out, back_out, acc, scaled, plain, swapped, own_rows, arrived = rest
     else:
-        acc, token_out, scaled, plain, swapped = rest
+        acc, token_out, scaled, plain, swapped, own_rows, arrived = rest
+    size = own_rows.shape[0]
+    begin = size if last else 0
 
     @pl.when(step == 0)
     def _():
@@ -146,6 +152,12 @@
     def _():
         plain[...], swapped[...] = plain_ref[...], swapped_ref[...]
 
+    @pl.when((special != 0) & (step == 0))
+    def _():
+        copy = pltpu.make_async_copy(own_ref.at[pl.ds(begin, size)], own_rows, arrived)
+        copy.start()
+        copy.wait()
+
     @pl.when(special != 0)
     def _():
         plain[...], swapped[...] = turned(first_ref[...])
@@ -154,7 +166,8 @@
     flags = [[switch_ref[2 + part * windows + w] for w in range(windows)] for part in range(3)]
     near_weights = [jnp.where(special != 0, first, own) * near for own, near, first in zip(*flags)]
     near = weigh(near_ref[...], near_weights)
-    far = weigh(jnp.where(special != 0, own_ref[...], first_ref[...]), [own * first for own, _, first in zip(*flags)])
+    own_tile = own_rows[pl.ds(pl.multiple_of(step * STEP, STEP), STEP), :]
+    far = weigh(jnp.where(special != 0, own_tile, first_ref[...]), [own * first for own, _, first in zip(*flags)])
     acc[...] += jnp.dot(scaled[...], jnp.concatenate([near, far], axis=1), preferred_element_type=jnp.float32)
 
     if last:
@@ -188,9 +201,10 @@
     token_spec = pl.BlockSpec(token.shape, lambda s, on: (0, 0))
     left = pl.BlockSpec((cols, STEP), lambda s, on: (0, (s + skip) * (1 - on[1])))
     right = pl.BlockSpec((STEP, cols), lambda s, on: (s + skip, 0))
-    right_special = pl.BlockSpec((STEP, cols), lambda s, on: ((s + skip) * on[1], 0))
-    in_specs = [left, left, pl.BlockSpec((LAGS, STEP), lambda s, on: (0, s + skip)), right, right, right_special]
+    in_specs = [left, left, pl.BlockSpec((LAGS, STEP), lambda s, on: (0, s + skip)), right, right,
+                pl.BlockSpec(memory_space=pltpu.HBM)]
     scratch = [pltpu.VMEM((LAGS * cols, STEP), jnp.bfloat16)] + [pltpu.VMEM((cols, STEP), jnp.bfloat16)] * 2
+    scratch += [pltpu.VMEM((steps * STEP, cols), jnp.bfloat16), pltpu.SemaphoreType.DMA(())]
     if earlier is None:
         out_shape, out_specs, earlier = [total, token], [total_spec, token_spec], []
     else:
@@ -315,7 +329,8 @@
     second_pairs = second_far + late_near
     near_pairs = [(d + 1, d) for d in range(1, count - 1) if d not in (1, 3, half - 2, half - 1)]
     near_pairs += [(0, half - 1), (half - 1, 0)]
-    back_pairs = [(t, s) for s, t in first_far + second_far] + [(1, 0)]
+    first_back = [(t, s) for s, t in first_far]
+    second_back = [(t, s) for s, t in second_far] + [(1, 0)]
     side_pairs = [(0, half - 1), (half - 1, count - 1)]
 
     def among(devices):
@@ -329,20 +344,19 @@
     first_in = lax.ppermute(block, "chan", first_pairs)
     coeffs = lag_rows(freq_count, window_count)
     own = turn(block)
-    parts = split(block)
+    parts = split(quality[0], block)
     first_flags = lax.ppermute(quality, "chan", first_pairs)[0]
     near_flags = lax.ppermute(quality, "chan", near_pairs)[0]
-    second_flags = lax.ppermute(quality, "chan", second_pairs)[0]
     special = among([0, half - 1])
-    first_switch = switch(me == 0, special, quality[0], near_flags, first_flags)
     second_switch = switch(
-        among([t for _, t in second_pairs]), among([t for _, t in late_near]), quality[0] * second_flags
+        among([t for _, t in second_pairs]), among([t for _, t in late_near]), quality[0]
     )
 
-    near_in, first_part, last_part, own, coeffs, first_in = lax.optimization_barrier(
-        (near_in, *parts, own, coeffs, first_in)
+    near_in, first_part, last_part, own, coeffs, first_in, near_flags, first_flags = lax.optimization_barrier(
+        (near_in, *parts, own, coeffs, first_in, near_flags, first_flags)
     )
     second_in = [lax.ppermute(first_part, "chan", second_pairs)]
+    first_switch = switch(me == 0, special, quality[0], near_flags, first_flags)
     operands = first_switch, own, coeffs, near_in, first_in, block
     total, token = first_sums(*operands)
     last_part, token = lax.optimization_barrier((last_part, token))
@@ -351,15 +365,18 @@
     side_returned = lax.ppermute(near, "chan", side_pairs)
     second_switch, near = lax.optimization_barrier((second_switch, near))
     total, = second_sums(second_switch, own, coeffs, second_in[0], 0)
-
+    total, back = lax.optimization_barrier((total, back))
+    first_returned = lax.ppermute(back, "chan", first_back)
+
+    near = jnp.where(among([half - 1, count - 1]), side_returned, near)
     near = jnp.where(me == half - 2, far, near)
+    far = jnp.where(among([s for s, _ in first_far]), first_returned, far)
     near, far, back = second_sums(
         second_switch, own, coeffs, second_in[1], parts[0].shape[0], [total, near, far, back]
     )
-    returned = lax.ppermute(back, "chan", back_pairs)
-    near = jnp.where(among([half - 1, count - 1]), side_returned, near)
-    near = jnp.where(me == 0, returned, near)
-    far = jnp.where(among([s for s, _ in first_far + second_far]), returned, far)
+    second_returned = lax.ppermute(back, "chan", second_back)
+    near = jnp.where(me == 0, second_returned, near)
+    far = jnp.where(among([s for s, _ in second_far]), second_returned, far)
     return near[None], far[None]
 
 

time: 73.5 us -> 80 us (1.088)
  local copies, waits for them, and re-layouts: 7.16 us -> 13.5 us
  waiting for transfers between devices: 9.29 us -> 2.98 us
  Pallas kernels: 24 us -> 27.9 us
  starting transfers between devices: 28.5 us -> 31 us
    ppermute x1, starting transfers between devices: 7.59 us -> 16.7 us  [local(): second_in = [lax.ppermute(first_part, 'chan', second_pairs)]]
    unnamed x12 -> x20, local copies, waits for them, and re-layouts: 7.16 us -> 13.5 us
    ppermute x2, waiting for transfers between devices: 9.27 us -> 2.97 us  [the longest x1 2.96 us: local(): second_returned = lax.ppermute(back, 'chan', second_back)]
    ppermute x2, starting transfers between devices: 12.4 us -> 6.95 us  [the longest x1 5.57 us: local(): second_returned = lax.ppermute(back, 'chan', second_back)]
    pallas_call x1, Pallas kernels: 0.28 us -> 3.86 us  [split(): pl.pallas_call(functools.partial(split_kernel, middle, flags.shape[0]), g...]
    pallas_call x2, Pallas kernels: 9.37 us -> 11.1 us  [second_sums(): pl.pallas_call(functools.partial(second_kernel, windows, not earlier), gr...]
    pallas_call x2, Pallas kernels: 11.2 us -> 9.74 us  [first_sums(): pl.pallas_call(functools.partial(first_kernel, windows, bool(earlier)), g...]
    ppermute x1, starting transfers between devices: 2 us -> 0.8 us  [local(): near_in = lax.ppermute(block, 'chan', near_pairs)]
  transfers between devices with their start and end apart: 9 -> 9, of which waited for: 1 -> 1; matrix products, arithmetic and copies ran while one was open for 3% -> 3% of each run, Pallas kernels for 33% -> 29%
where the time goes in v16:
time: 80 us; the launch traced here: 79.5 us
  starting transfers between devices  31 us (39%)
  Pallas kernels  27.9 us (35%)
  local copies, waits for them, and re-layouts  13.5 us (17%)
  other arithmetic  3.17 us (4%)
  waiting for transfers between devices  2.98 us (4%)
  between operations  0.89 us (1%)
    ppermute x1, starting transfers between devices, local(): second_in = [lax.ppermute(first_part, 'chan', second_pairs)]  16.7 us
    unnamed x20, local copies, waits for them, and re-layouts  13.5 us
    pallas_call x2, Pallas kernels, second_sums(): pl.pallas_call(functools.partial(second_kernel, windows, not earlier), gr...  11.1 us
    pallas_call x2, Pallas kernels, first_sums(): pl.pallas_call(functools.partial(first_kernel, windows, bool(earlier)), g...  9.74 us
    ppermute x1, starting transfers between devices, local(): second_returned = lax.ppermute(back, 'chan', second_back)  5.57 us
    pallas_call x1, Pallas kernels, split(): pl.pallas_call(functools.partial(split_kernel, middle, flags.shape[0]), g...  3.86 us
    pallas_call x1, Pallas kernels, turn(): pl.pallas_call(turn_kernel, grid=(rows // STEP,), in_specs=[pl.BlockSpec(...  3.15 us
    ppermute x1, waiting for transfers between devices, local(): second_returned = lax.ppermute(back, 'chan', second_back)  2.96 us
  transfers between devices with their start and end apart: 9, of which 1 were waited for; matrix products, arithmetic and copies ran while one was open for 3% of the time, Pallas kernels for 29%

profile of v16, /device:TPU:1, one launch (start us, length us, event | category | flops | bytes accessed | tf_op | source)
XLA Modules:
  0.0 79.5 jit_solution(11594158993676758035)
XLA Ops:
  1.4 1.3 %collective-permute-start.1 = (bf16[8192,128]{1,0:T(8,128)(2,1)}, bf16[8192,128]{1,0:T(8,128)(2,1)S(1)}, u32[]{:S(2)}, u32[]{:S(2)}) collective-permute-start(bf16[8192,128]{1,0:T(8,128)(2,1)} %bitcast.13), channel_id=1, source_target_pairs={{8,0},{4,12},{6,14},{15,7},{0,1},{7,6},{24,16},{20,28},{22,30},{31... | collective-permute-start | bytes 6291464 | tf_op jit(solution)/shard_map/ppermute | solution.py:344
  3.4 1.3 %collective-permute-start.3 = (s32[1,4]{1,0:T(1,128)}, s32[1,4]{1,0:T(1,128)S(1)}, u32[]{:S(2)}, u32[]{:S(2)}) collective-permute-start(s32[1,4]{1,0:T(1,128)} %param.3), channel_id=1, source_target_pairs={{8,0},{4,12},{6,14},{15,7},{0,1},{7,6},{24,16},{20,28},{22,30},{31... | collective-permute-start | bytes 56 | tf_op jit(solution)/shard_map/ppermute | solution.py:348
  4.7 1.6 %copy-done.3 = bf16[1024,2,4,128]{3,2,1,0:T(4,128)(2,1)S(1)} copy-done((bf16[1024,2,4,128]{3,2,1,0:T(4,128)(2,1)S(1)}, bf16[1024,2,4,128]{3,2,1,0:T(4,128)(2,1)}, u32[]{:S(2)}) %copy-start.3) | copy-done | bytes 2097176
  6.3 3.1 %turn.1 = (bf16[128,8192]{1,0:T(8,128)(2,1)S(1)}, bf16[128,8192]{1,0:T(8,128)(2,1)S(1)}) custom-call(bf16[8192,128]{1,0:T(8,128)(2,1)S(1)} %bitcast.14), custom_call_target="tpu_custom_call" | custom-call | bytes 6291456 | tf_op jit(solution)/shard_map/turn/pallas_call | solution.py:89
  9.5 1.3 %copy-done = bf16[128,8192]{1,0:T(8,128)(2,1)} copy-done((bf16[128,8192]{1,0:T(8,128)(2,1)}, bf16[128,8192]{1,0:T(8,128)(2,1)S(1)}, u32[]{:S(2)}) %copy-start) | copy-done | bytes 2097176
  10.8 3.9 %split.1 = (bf16[5120,128]{1,0:T(8,128)(2,1)}, bf16[3072,128]{1,0:T(8,128)(2,1)}) custom-call(s32[4]{0:T(128)S(1)} %bitcast.18, bf16[8192,128]{1,0:T(8,128)(2,1)S(1)} %bitcast.15), custom_call_target="tpu_custom_call" | custom-call | flops 1048576 | bytes 4194304 | tf_op jit(solution)/shard_map/split/pallas_call | solution.py:48
  14.7 0.9 %multiply_convert_fusion = (bf16[5,8192]{1,0:T(8,128)(2,1)S(1)}, f32[5,8192]{1,0:T(8,128)S(1)}) fusion(f32[8192]{0:T(1024)S(1)} %fusion.9, f32[5]{0:T(128)S(1)} %iota_multiply_fusion), kind=kLoop, calls=%fused_computation.5 | loop fusion | flops 122880 | bytes 278548 | tf_op jit(solution)/shard_map/convert
  16.6 1.3 %copy-done.5 = bf16[8192,128]{1,0:T(8,128)(2,1)} copy-done((bf16[8192,128]{1,0:T(8,128)(2,1)}, bf16[8192,128]{1,0:T(8,128)(2,1)S(1)}, u32[]{:S(2)}) %copy-start.5) | copy-done | bytes 2097176
  17.9 1.4 %copy-done.7 = bf16[8192,128]{1,0:T(8,128)(2,1)} copy-done((bf16[8192,128]{1,0:T(8,128)(2,1)}, bf16[8192,128]{1,0:T(8,128)(2,1)S(1)}, u32[]{:S(2)}) %copy-start.7) | copy-done | bytes 2097176
  19.3 16.7 %collective-permute-start.5 = (bf16[5120,128]{1,0:T(8,128)(2,1)}, bf16[5120,128]{1,0:T(8,128)(2,1)}, u32[]{:S(2)}, u32[]{:S(2)}) collective-permute-start(bf16[5120,128]{1,0:T(8,128)(2,1)} %get-tuple-element.47), channel_id=1, source_target_pairs={{1,9},{10,2},{3,11},{13,5},{2,1},{4,3},{17,25},{26,18},{19,27},{29... | collective-permute-start | bytes 3932168 | tf_op jit(solution)/shard_map/ppermute | solution.py:358
  36.4 1.6 %copy-done.1 = bf16[128,8192]{1,0:T(8,128)(2,1)S(1)} copy-done((bf16[128,8192]{1,0:T(8,128)(2,1)S(1)}, bf16[128,8192]{1,0:T(8,128)(2,1)}, u32[]{:S(2)}) %copy-start.1) | copy-done | bytes 2097176
  38.0 1.6 %copy-done.4 = bf16[1024,2,4,128]{3,2,1,0:T(4,128)(2,1)S(1)} copy-done((bf16[1024,2,4,128]{3,2,1,0:T(4,128)(2,1)S(1)}, bf16[1024,2,4,128]{3,2,1,0:T(4,128)(2,1)}, u32[]{:S(2)}) %copy-start.4) | copy-done | bytes 2097176
  39.6 1.6 %copy-done.6 = bf16[8192,128]{1,0:T(8,128)(2,1)S(1)} copy-done((bf16[8192,128]{1,0:T(8,128)(2,1)S(1)}, bf16[8192,128]{1,0:T(8,128)(2,1)}, u32[]{:S(2)}) %copy-start.6) | copy-done | bytes 2097176
  41.2 1.6 %copy-done.8 = bf16[8192,128]{1,0:T(8,128)(2,1)S(1)} copy-done((bf16[8192,128]{1,0:T(8,128)(2,1)S(1)}, bf16[8192,128]{1,0:T(8,128)(2,1)}, u32[]{:S(2)}) %copy-start.8) | copy-done | bytes 2097176
  42.8 4.4 %first_half.1 = (f32[1152,256]{1,0:T(8,128)S(1)}, f32[8,128]{1,0:T(8,128)S(1)}) custom-call(s32[14]{0:T(128)S(1)} %pad_add_fusion.1.switch_ref, bf16[128,8192]{1,0:T(8,128)(2,1)S(1)} %get-tuple-element.35.plain_ref, bf16[128,8192]{1,0:T(8,128)(2,1)S(1)} %copy-done.1, bf16[9,8192]{1,0:T(8,128)(2,1)S(1)} %pad_maximum_fusion.coeff_ref, ...), custom_call_target="tpu_custom_call" | custom-call | flops 2415919104 | bytes 4194304 | tf_op jit(solution)/shard_map/first_half/pallas_call | solution.py:215
  47.2 1.9 %collective-permute-start.4 = (bf16[3072,128]{1,0:T(8,128)(2,1)}, bf16[3072,128]{1,0:T(8,128)(2,1)}, u32[]{:S(2)}, u32[]{:S(2)}) collective-permute-start(bf16[3072,128]{1,0:T(8,128)(2,1)} %get-tuple-element.46), channel_id=1, source_target_pairs={{1,9},{10,2},{3,11},{13,5},{2,1},{4,3},{17,25},{26,18},{19,27},{29... | collective-permute-start | bytes 2359304 | tf_op jit(solution)/shard_map/ppermute | solution.py:363
  49.1 5.3 %first_last.1 = (bf16[9,128,128]{2,1,0:T(8,128)(2,1)S(1)}, bf16[9,128,128]{2,1,0:T(8,128)(2,1)S(1)}, bf16[9,128,128]{2,1,0:T(8,128)(2,1)}) custom-call(s32[14]{0:T(128)S(1)} %pad_add_fusion.1.switch_ref, bf16[128,8192]{1,0:T(8,128)(2,1)S(1)} %get-tuple-element.35.plain_ref, bf16[128,8192]{1,0:T(8,128)(2,1)S(1)} %copy-done.1, ...), custom_call_target="tpu_custom_call" | custom-call | flops 2415919104 | bytes 4194304 | tf_op jit(solution)/shard_map/first_last/pallas_call | solution.py:215
  54.4 1.4 %collective-permute-start.6 = (bf16[9,128,128]{2,1,0:T(8,128)(2,1)S(1)}, bf16[9,128,128]{2,1,0:T(8,128)(2,1)}, u32[]{:S(2)}, u32[]{:S(2)}) collective-permute-start(bf16[9,128,128]{2,1,0:T(8,128)(2,1)S(1)} %get-tuple-element.51), channel_id=1, source_target_pairs={{0,7},{7,15},{16,23},{23,31}} | collective-permute-start | bytes 884744 | tf_op jit(solution)/shard_map/ppermute | solution.py:365
  55.8 6.0 %second_part.1.rest_0_ = f32[1152,128]{1,0:T(8,128)S(1)} custom-call(s32[6]{0:T(128)S(1)} %pad_add_fusion.switch_ref, bf16[128,8192]{1,0:T(8,128)(2,1)S(1)} %get-tuple-element.35.plain_ref, bf16[128,8192]{1,0:T(8,128)(2,1)S(1)} %copy-done.1, bf16[9,8192]{1,0:T(8,128)(2,1)S(1)} %pad_maximum_fusion.coeff_ref, bf16[5120,128]{1,0:T(8,128)(2,1)} %collective-permute-done.5.partner_ref), custom_call_target="tpu_custom_call" | custom-call | flops 1509949440 | bytes 3932160 | tf_op jit(solution)/shard_map/second_part/pallas_call | solution.py:292
  61.9 1.4 %collective-permute-start.7 = (bf16[9,128,128]{2,1,0:T(8,128)(2,1)}, bf16[9,128,128]{2,1,0:T(8,128)(2,1)}, u32[]{:S(2)}, u32[]{:S(2)}) collective-permute-start(bf16[9,128,128]{2,1,0:T(8,128)(2,1)} %get-tuple-element.52.rest_3_), channel_id=1, source_target_pairs={{0,8},{12,4},{14,6},{7,15},{16,24},{28,20},{30,22},{23,31}} | collective-permute-start | bytes 884744 | tf_op jit(solution)/shard_map/ppermute | solution.py:369
  63.4 1.6 %copy-done.2 = bf16[128,8192]{1,0:T(8,128)(2,1)S(1)} copy-done((bf16[128,8192]{1,0:T(8,128)(2,1)S(1)}, bf16[128,8192]{1,0:T(8,128)(2,1)}, u32[]{:S(2)}) %copy-start.2) | copy-done | bytes 2097176
  64.9 5.1 %second_last.1 = (bf16[9,128,128]{2,1,0:T(8,128)(2,1)S(1)}, bf16[9,128,128]{2,1,0:T(8,128)(2,1)S(1)}, bf16[9,128,128]{2,1,0:T(8,128)(2,1)}) custom-call(s32[6]{0:T(128)S(1)} %pad_add_fusion.switch_ref, bf16[128,8192]{1,0:T(8,128)(2,1)S(1)} %get-tuple-element.35.plain_ref, bf16[128,8192]{1,0:T(8,128)(2,1)S(1)} %copy-done.2, ...), custom_call_target="tpu_custom_call" | custom-call | flops 905969664 | bytes 2359296 | tf_op jit(solution)/shard_map/second_last/pallas_call | solution.py:292
  70.0 5.6 %collective-permute-start.8 = (bf16[9,128,128]{2,1,0:T(8,128)(2,1)}, bf16[9,128,128]{2,1,0:T(8,128)(2,1)S(1)}, u32[]{:S(2)}, u32[]{:S(2)}) collective-permute-start(bf16[9,128,128]{2,1,0:T(8,128)(2,1)} %get-tuple-element.53), channel_id=1, source_target_pairs={{9,1},{2,10},{11,3},{5,13},{1,0},{25,17},{18,26},{27,19},{21,29},{... | collective-permute-start | bytes 884744 | tf_op jit(solution)/shard_map/ppermute | solution.py:377
  75.6 3.0 %collective-permute-done.8 = bf16[9,128,128]{2,1,0:T(8,128)(2,1)S(1)} collective-permute-done((bf16[9,128,128]{2,1,0:T(8,128)(2,1)}, bf16[9,128,128]{2,1,0:T(8,128)(2,1)S(1)}, u32[]{:S(2)}, u32[]{:S(2)}) %collective-permute-start.8) | collective-permute-done | bytes 294944 | tf_op jit(solution)/shard_map/ppermute | solution.py:377
  (32 shorter events, 3.7 us)
Async XLA Ops:
  0.6 10.2 %copy-start.9 = (s32[1,4]{1,0:T(1,128)S(1)}, s32[1,4]{1,0:T(1,128)}, u32[]{:S(2)}) copy-start(s32[1,4]{1,0:T(1,128)} %param.3) | copy-start | bytes 52
  0.6 16.0 %collective-permute-start = (bf16[8192,128]{1,0:T(8,128)(2,1)}, bf16[8192,128]{1,0:T(8,128)(2,1)S(1)}, u32[]{:S(2)}, u32[]{:S(2)}) collective-permute-start(bf16[8192,128]{1,0:T(8,128)(2,1)} %bitcast.12), channel_id=1, source_target_pairs={{3,2},{5,4},{6,5},{9,8},{10,9},{11,10},{12,11},{13,12},{14,13},{15... | collective-permute-start | bytes 6291464 | tf_op jit(solution)/shard_map/ppermute | solution.py:343
  1.4 16.5 %collective-permute-start.1 = (bf16[8192,128]{1,0:T(8,128)(2,1)}, bf16[8192,128]{1,0:T(8,128)(2,1)S(1)}, u32[]{:S(2)}, u32[]{:S(2)}) collective-permute-start(bf16[8192,128]{1,0:T(8,128)(2,1)} %bitcast.13), channel_id=1, source_target_pairs={{8,0},{4,12},{6,14},{15,7},{0,1},{7,6},{24,16},{20,28},{22,30},{31... | collective-permute-start | bytes 6291464 | tf_op jit(solution)/shard_map/ppermute | solution.py:344
  2.7 13.9 %collective-permute-start.2 = (s32[1,4]{1,0:T(1,128)}, s32[1,4]{1,0:T(1,128)S(1)}, u32[]{:S(2)}, u32[]{:S(2)}) collective-permute-start(s32[1,4]{1,0:T(1,128)} %param.3), channel_id=1, source_target_pairs={{3,2},{5,4},{6,5},{9,8},{10,9},{11,10},{12,11},{13,12},{14,13},{15... | collective-permute-start | bytes 56 | tf_op jit(solution)/shard_map/ppermute | solution.py:349
  3.4 13.2 %collective-permute-start.3 = (s32[1,4]{1,0:T(1,128)}, s32[1,4]{1,0:T(1,128)S(1)}, u32[]{:S(2)}, u32[]{:S(2)}) collective-permute-start(s32[1,4]{1,0:T(1,128)} %param.3), channel_id=1, source_target_pairs={{8,0},{4,12},{6,14},{15,7},{0,1},{7,6},{24,16},{20,28},{22,30},{31... | collective-permute-start | bytes 56 | tf_op jit(solution)/shard_map/ppermute | solution.py:348
  4.7 1.6 %copy-start.3 = (bf16[1024,2,4,128]{3,2,1,0:T(4,128)(2,1)S(1)}, bf16[1024,2,4,128]{3,2,1,0:T(4,128)(2,1)}, u32[]{:S(2)}) copy-start(bf16[1024,2,4,128]{3,2,1,0:T(4,128)(2,1)} %param.2) | copy-start | bytes 6291460
  9.5 1.3 %copy-start = (bf16[128,8192]{1,0:T(8,128)(2,1)}, bf16[128,8192]{1,0:T(8,128)(2,1)S(1)}, u32[]{:S(2)}) copy-start(bf16[128,8192]{1,0:T(8,128)(2,1)S(1)} %get-tuple-element.36.swapped_ref) | copy-start | bytes 6291460
  16.6 1.3 %copy-start.5 = (bf16[8192,128]{1,0:T(8,128)(2,1)}, bf16[8192,128]{1,0:T(8,128)(2,1)S(1)}, u32[]{:S(2)}) copy-start(bf16[8192,128]{1,0:T(8,128)(2,1)S(1)} %collective-permute-done.near_ref) | copy-start | bytes 6291460
  17.9 1.4 %copy-start.7 = (bf16[8192,128]{1,0:T(8,128)(2,1)}, bf16[8192,128]{1,0:T(8,128)(2,1)S(1)}, u32[]{:S(2)}) copy-start(bf16[8192,128]{1,0:T(8,128)(2,1)S(1)} %collective-permute-done.1.first_ref) | copy-start | bytes 6291460
  19.3 36.5 %collective-permute-start.5 = (bf16[5120,128]{1,0:T(8,128)(2,1)}, bf16[5120,128]{1,0:T(8,128)(2,1)}, u32[]{:S(2)}, u32[]{:S(2)}) collective-permute-start(bf16[5120,128]{1,0:T(8,128)(2,1)} %get-tuple-element.47), channel_id=1, source_target_pairs={{1,9},{10,2},{3,11},{13,5},{2,1},{4,3},{17,25},{26,18},{19,27},{29... | collective-permute-start | bytes 3932168 | tf_op jit(solution)/shard_map/ppermute | solution.py:358
  36.4 1.6 %copy-start.1 = (bf16[128,8192]{1,0:T(8,128)(2,1)S(1)}, bf16[128,8192]{1,0:T(8,128)(2,1)}, u32[]{:S(2)}) copy-start(bf16[128,8192]{1,0:T(8,128)(2,1)} %copy-done) | copy-start | bytes 6291460
  38.0 1.6 %copy-start.4 = (bf16[1024,2,4,128]{3,2,1,0:T(4,128)(2,1)S(1)}, bf16[1024,2,4,128]{3,2,1,0:T(4,128)(2,1)}, u32[]{:S(2)}) copy-start(bf16[1024,2,4,128]{3,2,1,0:T(4,128)(2,1)} %param.2) | copy-start | bytes 6291460
  39.6 1.6 %copy-start.6 = (bf16[8192,128]{1,0:T(8,128)(2,1)S(1)}, bf16[8192,128]{1,0:T(8,128)(2,1)}, u32[]{:S(2)}) copy-start(bf16[8192,128]{1,0:T(8,128)(2,1)} %copy-done.5) | copy-start | bytes 6291460
  41.2 1.6 %copy-start.8 = (bf16[8192,128]{1,0:T(8,128)(2,1)S(1)}, bf16[8192,128]{1,0:T(8,128)(2,1)}, u32[]{:S(2)}) copy-start(bf16[8192,128]{1,0:T(8,128)(2,1)} %copy-done.7) | copy-start | bytes 6291460
  47.2 16.2 %collective-permute-start.4 = (bf16[3072,128]{1,0:T(8,128)(2,1)}, bf16[3072,128]{1,0:T(8,128)(2,1)}, u32[]{:S(2)}, u32[]{:S(2)}) collective-permute-start(bf16[3072,128]{1,0:T(8,128)(2,1)} %get-tuple-element.46), channel_id=1, source_target_pairs={{1,9},{10,2},{3,11},{13,5},{2,1},{4,3},{17,25},{26,18},{19,27},{29... | collective-permute-start | bytes 2359304 | tf_op jit(solution)/shard_map/ppermute | solution.py:363
  54.4 8.8 %collective-permute-start.6 = (bf16[9,128,128]{2,1,0:T(8,128)(2,1)S(1)}, bf16[9,128,128]{2,1,0:T(8,128)(2,1)}, u32[]{:S(2)}, u32[]{:S(2)}) collective-permute-start(bf16[9,128,128]{2,1,0:T(8,128)(2,1)S(1)} %get-tuple-element.51), channel_id=1, source_target_pairs={{0,7},{7,15},{16,23},{23,31}} | collective-permute-start | bytes 884744 | tf_op jit(solution)/shard_map/ppermute | solution.py:365
  61.9 1.4 %collective-permute-start.7 = (bf16[9,128,128]{2,1,0:T(8,128)(2,1)}, bf16[9,128,128]{2,1,0:T(8,128)(2,1)}, u32[]{:S(2)}, u32[]{:S(2)}) collective-permute-start(bf16[9,128,128]{2,1,0:T(8,128)(2,1)} %get-tuple-element.52.rest_3_), channel_id=1, source_target_pairs={{0,8},{12,4},{14,6},{7,15},{16,24},{28,20},{30,22},{23,31}} | collective-permute-start | bytes 884744 | tf_op jit(solution)/shard_map/ppermute | solution.py:369
  63.3 1.6 %copy-start.2 = (bf16[128,8192]{1,0:T(8,128)(2,1)S(1)}, bf16[128,8192]{1,0:T(8,128)(2,1)}, u32[]{:S(2)}) copy-start(bf16[128,8192]{1,0:T(8,128)(2,1)} %copy-done) | copy-start | bytes 6291460
  70.0 8.6 %collective-permute-start.8 = (bf16[9,128,128]{2,1,0:T(8,128)(2,1)}, bf16[9,128,128]{2,1,0:T(8,128)(2,1)S(1)}, u32[]{:S(2)}, u32[]{:S(2)}) collective-permute-start(bf16[9,128,128]{2,1,0:T(8,128)(2,1)} %get-tuple-element.53), channel_id=1, source_target_pairs={{9,1},{2,10},{11,3},{5,13},{1,0},{25,17},{18,26},{27,19},{21,29},{... | collective-permute-start | bytes 884744 | tf_op jit(solution)/shard_map/ppermute | solution.py:377

commit v17 on v16

--- a/solution.py
+++ b/solution.py
@@ -12,7 +12,7 @@
 LAGS = 2 * HL + 1
 STEP = 1024
 PARTS = (5, 8)
-PARAMS = pltpu.CompilerParams(vmem_limit_bytes=12 * 1024 * 1024)
+PARAMS = pltpu.CompilerParams(vmem_limit_bytes=16 * 1024 * 1024)
 
 
 def lag_rows(freq_count, window_count):
@@ -79,8 +79,9 @@
     return plain, jnp.concatenate(swapped, axis=1)
 
 
-def turn_kernel(x_ref, plain_ref, swapped_ref):
+def turn_kernel(x_ref, plain_ref, swapped_ref, token_ref):
     plain_ref[...], swapped_ref[...] = turned(x_ref[...])
+    token_ref[...] = x_ref[:16, :]
 
 
 def turn(x):
@@ -90,8 +91,8 @@
         turn_kernel,
         grid=(rows // STEP,),
         in_specs=[pl.BlockSpec((STEP, cols), lambda s: (s, 0))],
-        out_specs=[pl.BlockSpec((cols, STEP), lambda s: (0, s))] * 2,
-        out_shape=[out, out],
+        out_specs=[pl.BlockSpec((cols, STEP), lambda s: (0, s))] * 2 + [pl.BlockSpec((16, cols), lambda s: (0, 0))],
+        out_shape=[out, out, jax.ShapeDtypeStruct((16, cols), jnp.bfloat16)],
         compiler_params=PARAMS,
         cost_estimate=pl.CostEstimate(flops=0, bytes_accessed=6 * rows * cols, transcendentals=0),
         name="turn",
@@ -136,7 +137,7 @@
     if last:
         acc_in, _, near_out, far_out, back_out, acc, scaled, plain, swapped, own_rows, arrived = rest
     else:
-        acc, token_out, scaled, plain, swapped, own_rows, arrived = rest
+        _, _, _, acc, token_out, scaled, plain, swapped, own_rows, arrived = rest
     size = own_rows.shape[0]
     begin = size if last else 0
 
@@ -189,10 +190,10 @@
             pl.when(near_mirrored != 0)(lambda: write_lags(near_out, acc, near_at, cols, True))
 
 
-def first_sums(switch, own, coeffs, near_in, first_in, block, earlier=None):
+def first_sums(switch, own, coeffs, near_in, first_in, block, earlier, last):
     rows, cols = block.shape
     steps = rows // STEP // 2
-    skip = 0 if earlier is None else steps
+    skip = steps if last else 0
     windows = (switch.shape[0] - 2) // 3
     result = jax.ShapeDtypeStruct((LAGS, cols, cols), jnp.bfloat16)
     total = jax.ShapeDtypeStruct((LAGS * cols, 2 * cols), jnp.float32)
@@ -205,15 +206,16 @@
                 pl.BlockSpec(memory_space=pltpu.HBM)]
     scratch = [pltpu.VMEM((LAGS * cols, STEP), jnp.bfloat16)] + [pltpu.VMEM((cols, STEP), jnp.bfloat16)] * 2
     scratch += [pltpu.VMEM((steps * STEP, cols), jnp.bfloat16), pltpu.SemaphoreType.DMA(())]
-    if earlier is None:
-        out_shape, out_specs, earlier = [total, token], [total_spec, token_spec], []
+    if not last:
+        in_specs += [pl.BlockSpec((16, cols), lambda s, on: (0, 0))] * 3
+        out_shape, out_specs = [total, token], [total_spec, token_spec]
     else:
         in_specs += [total_spec, token_spec]
         out_shape = [result] * 3
         out_specs = [pl.BlockSpec(result.shape, lambda s, on: (0, 0, 0))] * 3
         scratch = [pltpu.VMEM(total.shape, jnp.float32)] + scratch
     return pl.pallas_call(
-        functools.partial(first_kernel, windows, bool(earlier)),
+        functools.partial(first_kernel, windows, last),
         grid_spec=pltpu.PrefetchScalarGridSpec(
             num_scalar_prefetch=1,
             grid=(steps,),
@@ -226,7 +228,7 @@
         cost_estimate=pl.CostEstimate(
             flops=2 * LAGS * cols * cols * rows, bytes_accessed=4 * rows * cols, transcendentals=0
         ),
-        name="first_last" if earlier else "first_half",
+        name="first_last" if last else "first_half",
     )(switch, *own, coeffs, near_in, first_in, block, *earlier)
 
 
@@ -343,7 +345,7 @@
     near_in = lax.ppermute(block, "chan", near_pairs)
     first_in = lax.ppermute(block, "chan", first_pairs)
     coeffs = lag_rows(freq_count, window_count)
-    own = turn(block)
+    *own, token = turn(block)
     parts = split(quality[0], block)
     first_flags = lax.ppermute(quality, "chan", first_pairs)[0]
     near_flags = lax.ppermute(quality, "chan", near_pairs)[0]
@@ -352,16 +354,16 @@
         among([t for _, t in second_pairs]), among([t for _, t in late_near]), quality[0]
     )
 
-    near_in, first_part, last_part, own, coeffs, first_in, near_flags, first_flags = lax.optimization_barrier(
-        (near_in, *parts, own, coeffs, first_in, near_flags, first_flags)
+    first_part, coeffs, near_flags, first_flags, *tokens = lax.optimization_barrier(
+        (parts[0], coeffs, near_flags, first_flags, near_in[:16], first_in[:16], token)
     )
     second_in = [lax.ppermute(first_part, "chan", second_pairs)]
     first_switch = switch(me == 0, special, quality[0], near_flags, first_flags)
     operands = first_switch, own, coeffs, near_in, first_in, block
-    total, token = first_sums(*operands)
-    last_part, token = lax.optimization_barrier((last_part, token))
+    total, token = first_sums(*operands, tokens, False)
+    last_part, token = lax.optimization_barrier((parts[1], token))
     second_in.append(lax.ppermute(last_part, "chan", second_pairs))
-    near, far, back = first_sums(*operands, [total, token])
+    near, far, back = first_sums(*operands, [total, token], True)
     side_returned = lax.ppermute(near, "chan", side_pairs)
     second_switch, near = lax.optimization_barrier((second_switch, near))
     total, = second_sums(second_switch, own, coeffs, second_in[0], 0)

time: 80 us -> 79.9 us (level)
  waiting for transfers between devices: 2.98 us -> 4.29 us
  starting transfers between devices: 31 us -> 29.7 us
    ppermute x1, starting transfers between devices: 5.57 us -> 4.27 us  [local(): second_returned = lax.ppermute(back, 'chan', second_back)]
    ppermute x1, waiting for transfers between devices: 2.96 us -> 4.27 us  [local(): second_returned = lax.ppermute(back, 'chan', second_back)]
where the time goes in v17:
time: 79.9 us; the launch traced here: 79.4 us
  starting transfers between devices  29.7 us (37%)
  Pallas kernels  27.8 us (35%)
  local copies, waits for them, and re-layouts  13.5 us (17%)
  waiting for transfers between devices  4.29 us (5%)
  other arithmetic  3.17 us (4%)
  between operations  0.88 us (1%)
    ppermute x1, starting transfers between devices, local(): second_in = [lax.ppermute(first_part, 'chan', second_pairs)]  16.7 us
    unnamed x20, local copies, waits for them, and re-layouts  13.5 us
    pallas_call x2, Pallas kernels, second_sums(): pl.pallas_call(functools.partial(second_kernel, windows, not earlier), gr...  11.1 us
    pallas_call x2, Pallas kernels, first_sums(): pl.pallas_call(functools.partial(first_kernel, windows, last), grid_spec=...  9.68 us
    ppermute x1, starting transfers between devices, local(): second_returned = lax.ppermute(back, 'chan', second_back)  4.27 us
    ppermute x1, waiting for transfers between devices, local(): second_returned = lax.ppermute(back, 'chan', second_back)  4.27 us
    pallas_call x1, Pallas kernels, split(): pl.pallas_call(functools.partial(split_kernel, middle, flags.shape[0]), g...  3.86 us
    pallas_call x1, Pallas kernels, turn(): pl.pallas_call(turn_kernel, grid=(rows // STEP,), in_specs=[pl.BlockSpec(...  3.15 us
  transfers between devices with their start and end apart: 9, of which 1 were waited for; matrix products, arithmetic and copies ran while one was open for 3% of the time, Pallas kernels for 29%

profile of v17, /device:TPU:1, one launch (start us, length us, event | category | flops | bytes accessed | tf_op | source)
XLA Modules:
  0.0 79.4 jit_solution(14898337932111226551)
XLA Ops:
  1.4 1.3 %collective-permute-start.3 = (bf16[8192,128]{1,0:T(8,128)(2,1)}, bf16[8192,128]{1,0:T(8,128)(2,1)S(1)}, u32[]{:S(2)}, u32[]{:S(2)}) collective-permute-start(bf16[8192,128]{1,0:T(8,128)(2,1)} %bitcast.13), channel_id=1, source_target_pairs={{8,0},{4,12},{6,14},{15,7},{0,1},{7,6},{24,16},{20,28},{22,30},{31... | collective-permute-start | bytes 6291464 | tf_op jit(solution)/shard_map/ppermute | solution.py:346
  3.4 1.3 %collective-permute-start.1 = (s32[1,4]{1,0:T(1,128)}, s32[1,4]{1,0:T(1,128)S(1)}, u32[]{:S(2)}, u32[]{:S(2)}) collective-permute-start(s32[1,4]{1,0:T(1,128)} %param.3), channel_id=1, source_target_pairs={{8,0},{4,12},{6,14},{15,7},{0,1},{7,6},{24,16},{20,28},{22,30},{31... | collective-permute-start | bytes 56 | tf_op jit(solution)/shard_map/ppermute | solution.py:350
  4.7 1.6 %copy-done.3 = bf16[1024,2,4,128]{3,2,1,0:T(4,128)(2,1)S(1)} copy-done((bf16[1024,2,4,128]{3,2,1,0:T(4,128)(2,1)S(1)}, bf16[1024,2,4,128]{3,2,1,0:T(4,128)(2,1)}, u32[]{:S(2)}) %copy-start.3) | copy-done | bytes 2097176
  6.3 3.1 %turn.1 = (bf16[128,8192]{1,0:T(8,128)(2,1)S(1)}, bf16[128,8192]{1,0:T(8,128)(2,1)S(1)}, bf16[16,128]{1,0:T(8,128)(2,1)S(1)}) custom-call(bf16[8192,128]{1,0:T(8,128)(2,1)S(1)} %bitcast.14), custom_call_target="tpu_custom_call" | custom-call | bytes 6291456 | tf_op jit(solution)/shard_map/turn/pallas_call | solution.py:90
  9.5 1.3 %copy-done = bf16[128,8192]{1,0:T(8,128)(2,1)} copy-done((bf16[128,8192]{1,0:T(8,128)(2,1)}, bf16[128,8192]{1,0:T(8,128)(2,1)S(1)}, u32[]{:S(2)}) %copy-start) | copy-done | bytes 2097176
  10.8 3.9 %split.1 = (bf16[5120,128]{1,0:T(8,128)(2,1)}, bf16[3072,128]{1,0:T(8,128)(2,1)}) custom-call(s32[4]{0:T(128)S(1)} %bitcast.18, bf16[8192,128]{1,0:T(8,128)(2,1)S(1)} %bitcast.15), custom_call_target="tpu_custom_call" | custom-call | flops 1048576 | bytes 4194304 | tf_op jit(solution)/shard_map/split/pallas_call | solution.py:48
  14.7 0.9 %multiply_convert_fusion = (bf16[5,8192]{1,0:T(8,128)(2,1)S(1)}, f32[5,8192]{1,0:T(8,128)S(1)}) fusion(f32[8192]{0:T(1024)S(1)} %fusion.9, f32[5]{0:T(128)S(1)} %iota_multiply_fusion), kind=kLoop, calls=%fused_computation.5 | loop fusion | flops 122880 | bytes 278548 | tf_op jit(solution)/shard_map/convert
  16.6 1.3 %copy-done.5 = bf16[8192,128]{1,0:T(8,128)(2,1)} copy-done((bf16[8192,128]{1,0:T(8,128)(2,1)}, bf16[8192,128]{1,0:T(8,128)(2,1)S(1)}, u32[]{:S(2)}) %copy-start.5) | copy-done | bytes 2097176
  17.9 1.4 %copy-done.7 = bf16[8192,128]{1,0:T(8,128)(2,1)} copy-done((bf16[8192,128]{1,0:T(8,128)(2,1)}, bf16[8192,128]{1,0:T(8,128)(2,1)S(1)}, u32[]{:S(2)}) %copy-start.7) | copy-done | bytes 2097176
  19.3 16.7 %collective-permute-start.5 = (bf16[5120,128]{1,0:T(8,128)(2,1)}, bf16[5120,128]{1,0:T(8,128)(2,1)}, u32[]{:S(2)}, u32[]{:S(2)}) collective-permute-start(bf16[5120,128]{1,0:T(8,128)(2,1)} %get-tuple-element.45), channel_id=1, source_target_pairs={{1,9},{10,2},{3,11},{13,5},{2,1},{4,3},{17,25},{26,18},{19,27},{29... | collective-permute-start | bytes 3932168 | tf_op jit(solution)/shard_map/ppermute | solution.py:360
  36.3 1.6 %copy-done.1 = bf16[128,8192]{1,0:T(8,128)(2,1)S(1)} copy-done((bf16[128,8192]{1,0:T(8,128)(2,1)S(1)}, bf16[128,8192]{1,0:T(8,128)(2,1)}, u32[]{:S(2)}) %copy-start.1) | copy-done | bytes 2097176
  37.9 1.6 %copy-done.4 = bf16[1024,2,4,128]{3,2,1,0:T(4,128)(2,1)S(1)} copy-done((bf16[1024,2,4,128]{3,2,1,0:T(4,128)(2,1)S(1)}, bf16[1024,2,4,128]{3,2,1,0:T(4,128)(2,1)}, u32[]{:S(2)}) %copy-start.4) | copy-done | bytes 2097176
  39.5 1.6 %copy-done.6 = bf16[8192,128]{1,0:T(8,128)(2,1)S(1)} copy-done((bf16[8192,128]{1,0:T(8,128)(2,1)S(1)}, bf16[8192,128]{1,0:T(8,128)(2,1)}, u32[]{:S(2)}) %copy-start.6) | copy-done | bytes 2097176
  41.1 1.6 %copy-done.8 = bf16[8192,128]{1,0:T(8,128)(2,1)S(1)} copy-done((bf16[8192,128]{1,0:T(8,128)(2,1)S(1)}, bf16[8192,128]{1,0:T(8,128)(2,1)}, u32[]{:S(2)}) %copy-start.8) | copy-done | bytes 2097176
  42.7 4.4 %first_half.1 = (f32[1152,256]{1,0:T(8,128)S(1)}, f32[8,128]{1,0:T(8,128)S(1)}) custom-call(s32[14]{0:T(128)S(1)} %pad_add_fusion.1.switch_ref, bf16[128,8192]{1,0:T(8,128)(2,1)S(1)} %get-tuple-element.32.plain_ref, bf16[128,8192]{1,0:T(8,128)(2,1)S(1)} %copy-done.1, bf16[9,8192]{1,0:T(8,128)(2,1)S(1)} %pad_maximum_fusion.coeff_ref, ...), custom_call_target="tpu_custom_call" | custom-call | flops 2415919104 | bytes 4194304 | tf_op jit(solution)/shard_map/first_half/pallas_call | solution.py:217
  47.1 1.9 %collective-permute-start.4 = (bf16[3072,128]{1,0:T(8,128)(2,1)}, bf16[3072,128]{1,0:T(8,128)(2,1)}, u32[]{:S(2)}, u32[]{:S(2)}) collective-permute-start(bf16[3072,128]{1,0:T(8,128)(2,1)} %get-tuple-element.44), channel_id=1, source_target_pairs={{1,9},{10,2},{3,11},{13,5},{2,1},{4,3},{17,25},{26,18},{19,27},{29... | collective-permute-start | bytes 2359304 | tf_op jit(solution)/shard_map/ppermute | solution.py:365
  49.0 5.3 %first_last.1 = (bf16[9,128,128]{2,1,0:T(8,128)(2,1)S(1)}, bf16[9,128,128]{2,1,0:T(8,128)(2,1)S(1)}, bf16[9,128,128]{2,1,0:T(8,128)(2,1)}) custom-call(s32[14]{0:T(128)S(1)} %pad_add_fusion.1.switch_ref, bf16[128,8192]{1,0:T(8,128)(2,1)S(1)} %get-tuple-element.32.plain_ref, bf16[128,8192]{1,0:T(8,128)(2,1)S(1)} %copy-done.1, ...), custom_call_target="tpu_custom_call" | custom-call | flops 2415919104 | bytes 4194304 | tf_op jit(solution)/shard_map/first_last/pallas_call | solution.py:217
  54.3 1.4 %collective-permute-start.6 = (bf16[9,128,128]{2,1,0:T(8,128)(2,1)S(1)}, bf16[9,128,128]{2,1,0:T(8,128)(2,1)}, u32[]{:S(2)}, u32[]{:S(2)}) collective-permute-start(bf16[9,128,128]{2,1,0:T(8,128)(2,1)S(1)} %get-tuple-element.49), channel_id=1, source_target_pairs={{0,7},{7,15},{16,23},{23,31}} | collective-permute-start | bytes 884744 | tf_op jit(solution)/shard_map/ppermute | solution.py:367
  55.7 6.0 %second_part.1.rest_0_ = f32[1152,128]{1,0:T(8,128)S(1)} custom-call(s32[6]{0:T(128)S(1)} %pad_add_fusion.switch_ref, bf16[128,8192]{1,0:T(8,128)(2,1)S(1)} %get-tuple-element.32.plain_ref, bf16[128,8192]{1,0:T(8,128)(2,1)S(1)} %copy-done.1, bf16[9,8192]{1,0:T(8,128)(2,1)S(1)} %pad_maximum_fusion.coeff_ref, bf16[5120,128]{1,0:T(8,128)(2,1)} %collective-permute-done.5.partner_ref), custom_call_target="tpu_custom_call" | custom-call | flops 1509949440 | bytes 3932160 | tf_op jit(solution)/shard_map/second_part/pallas_call | solution.py:294
  61.8 1.4 %collective-permute-start.7 = (bf16[9,128,128]{2,1,0:T(8,128)(2,1)}, bf16[9,128,128]{2,1,0:T(8,128)(2,1)}, u32[]{:S(2)}, u32[]{:S(2)}) collective-permute-start(bf16[9,128,128]{2,1,0:T(8,128)(2,1)} %get-tuple-element.50.rest_3_), channel_id=1, source_target_pairs={{0,8},{12,4},{14,6},{7,15},{16,24},{28,20},{30,22},{23,31}} | collective-permute-start | bytes 884744 | tf_op jit(solution)/shard_map/ppermute | solution.py:371
  63.2 1.6 %copy-done.2 = bf16[128,8192]{1,0:T(8,128)(2,1)S(1)} copy-done((bf16[128,8192]{1,0:T(8,128)(2,1)S(1)}, bf16[128,8192]{1,0:T(8,128)(2,1)}, u32[]{:S(2)}) %copy-start.2) | copy-done | bytes 2097176
  64.8 5.1 %second_last.1 = (bf16[9,128,128]{2,1,0:T(8,128)(2,1)S(1)}, bf16[9,128,128]{2,1,0:T(8,128)(2,1)S(1)}, bf16[9,128,128]{2,1,0:T(8,128)(2,1)}) custom-call(s32[6]{0:T(128)S(1)} %pad_add_fusion.switch_ref, bf16[128,8192]{1,0:T(8,128)(2,1)S(1)} %get-tuple-element.32.plain_ref, bf16[128,8192]{1,0:T(8,128)(2,1)S(1)} %copy-done.2, ...), custom_call_target="tpu_custom_call" | custom-call | flops 905969664 | bytes 2359296 | tf_op jit(solution)/shard_map/second_last/pallas_call | solution.py:294
  69.9 4.3 %collective-permute-start.8 = (bf16[9,128,128]{2,1,0:T(8,128)(2,1)}, bf16[9,128,128]{2,1,0:T(8,128)(2,1)S(1)}, u32[]{:S(2)}, u32[]{:S(2)}) collective-permute-start(bf16[9,128,128]{2,1,0:T(8,128)(2,1)} %get-tuple-element.51), channel_id=1, source_target_pairs={{9,1},{2,10},{11,3},{5,13},{1,0},{25,17},{18,26},{27,19},{21,29},{... | collective-permute-start | bytes 884744 | tf_op jit(solution)/shard_map/ppermute | solution.py:379
  74.2 4.3 %collective-permute-done.8 = bf16[9,128,128]{2,1,0:T(8,128)(2,1)S(1)} collective-permute-done((bf16[9,128,128]{2,1,0:T(8,128)(2,1)}, bf16[9,128,128]{2,1,0:T(8,128)(2,1)S(1)}, u32[]{:S(2)}, u32[]{:S(2)}) %collective-permute-start.8) | collective-permute-done | bytes 294944 | tf_op jit(solution)/shard_map/ppermute | solution.py:379
  (34 shorter events, 3.7 us)
Async XLA Ops:
  0.6 10.2 %copy-start.9 = (s32[1,4]{1,0:T(1,128)S(1)}, s32[1,4]{1,0:T(1,128)}, u32[]{:S(2)}) copy-start(s32[1,4]{1,0:T(1,128)} %param.3) | copy-start | bytes 52
  0.6 16.0 %collective-permute-start.2 = (bf16[8192,128]{1,0:T(8,128)(2,1)}, bf16[8192,128]{1,0:T(8,128)(2,1)S(1)}, u32[]{:S(2)}, u32[]{:S(2)}) collective-permute-start(bf16[8192,128]{1,0:T(8,128)(2,1)} %bitcast.12), channel_id=1, source_target_pairs={{3,2},{5,4},{6,5},{9,8},{10,9},{11,10},{12,11},{13,12},{14,13},{15... | collective-permute-start | bytes 6291464 | tf_op jit(solution)/shard_map/ppermute | solution.py:345
  1.4 16.5 %collective-permute-start.3 = (bf16[8192,128]{1,0:T(8,128)(2,1)}, bf16[8192,128]{1,0:T(8,128)(2,1)S(1)}, u32[]{:S(2)}, u32[]{:S(2)}) collective-permute-start(bf16[8192,128]{1,0:T(8,128)(2,1)} %bitcast.13), channel_id=1, source_target_pairs={{8,0},{4,12},{6,14},{15,7},{0,1},{7,6},{24,16},{20,28},{22,30},{31... | collective-permute-start | bytes 6291464 | tf_op jit(solution)/shard_map/ppermute | solution.py:346
  2.7 16.6 %collective-permute-start = (s32[1,4]{1,0:T(1,128)}, s32[1,4]{1,0:T(1,128)S(1)}, u32[]{:S(2)}, u32[]{:S(2)}) collective-permute-start(s32[1,4]{1,0:T(1,128)} %param.3), channel_id=1, source_target_pairs={{3,2},{5,4},{6,5},{9,8},{10,9},{11,10},{12,11},{13,12},{14,13},{15... | collective-permute-start | bytes 56 | tf_op jit(solution)/shard_map/ppermute | solution.py:351
  3.4 15.9 %collective-permute-start.1 = (s32[1,4]{1,0:T(1,128)}, s32[1,4]{1,0:T(1,128)S(1)}, u32[]{:S(2)}, u32[]{:S(2)}) collective-permute-start(s32[1,4]{1,0:T(1,128)} %param.3), channel_id=1, source_target_pairs={{8,0},{4,12},{6,14},{15,7},{0,1},{7,6},{24,16},{20,28},{22,30},{31... | collective-permute-start | bytes 56 | tf_op jit(solution)/shard_map/ppermute | solution.py:350
  4.7 1.6 %copy-start.3 = (bf16[1024,2,4,128]{3,2,1,0:T(4,128)(2,1)S(1)}, bf16[1024,2,4,128]{3,2,1,0:T(4,128)(2,1)}, u32[]{:S(2)}) copy-start(bf16[1024,2,4,128]{3,2,1,0:T(4,128)(2,1)} %param.2) | copy-start | bytes 6291460
  9.5 1.3 %copy-start = (bf16[128,8192]{1,0:T(8,128)(2,1)}, bf16[128,8192]{1,0:T(8,128)(2,1)S(1)}, u32[]{:S(2)}) copy-start(bf16[128,8192]{1,0:T(8,128)(2,1)S(1)} %get-tuple-element.33.swapped_ref) | copy-start | bytes 6291460
  16.6 1.3 %copy-start.5 = (bf16[8192,128]{1,0:T(8,128)(2,1)}, bf16[8192,128]{1,0:T(8,128)(2,1)S(1)}, u32[]{:S(2)}) copy-start(bf16[8192,128]{1,0:T(8,128)(2,1)S(1)} %collective-permute-done.2.near_ref) | copy-start | bytes 6291460
  17.9 1.4 %copy-start.7 = (bf16[8192,128]{1,0:T(8,128)(2,1)}, bf16[8192,128]{1,0:T(8,128)(2,1)S(1)}, u32[]{:S(2)}) copy-start(bf16[8192,128]{1,0:T(8,128)(2,1)S(1)} %collective-permute-done.3.first_ref) | copy-start | bytes 6291460
  19.3 36.4 %collective-permute-start.5 = (bf16[5120,128]{1,0:T(8,128)(2,1)}, bf16[5120,128]{1,0:T(8,128)(2,1)}, u32[]{:S(2)}, u32[]{:S(2)}) collective-permute-start(bf16[5120,128]{1,0:T(8,128)(2,1)} %get-tuple-element.45), channel_id=1, source_target_pairs={{1,9},{10,2},{3,11},{13,5},{2,1},{4,3},{17,25},{26,18},{19,27},{29... | collective-permute-start | bytes 3932168 | tf_op jit(solution)/shard_map/ppermute | solution.py:360
  36.3 1.6 %copy-start.1 = (bf16[128,8192]{1,0:T(8,128)(2,1)S(1)}, bf16[128,8192]{1,0:T(8,128)(2,1)}, u32[]{:S(2)}) copy-start(bf16[128,8192]{1,0:T(8,128)(2,1)} %copy-done) | copy-start | bytes 6291460
  37.9 1.6 %copy-start.4 = (bf16[1024,2,4,128]{3,2,1,0:T(4,128)(2,1)S(1)}, bf16[1024,2,4,128]{3,2,1,0:T(4,128)(2,1)}, u32[]{:S(2)}) copy-start(bf16[1024,2,4,128]{3,2,1,0:T(4,128)(2,1)} %param.2) | copy-start | bytes 6291460
  39.5 1.6 %copy-start.6 = (bf16[8192,128]{1,0:T(8,128)(2,1)S(1)}, bf16[8192,128]{1,0:T(8,128)(2,1)}, u32[]{:S(2)}) copy-start(bf16[8192,128]{1,0:T(8,128)(2,1)} %copy-done.5) | copy-start | bytes 6291460
  41.1 1.6 %copy-start.8 = (bf16[8192,128]{1,0:T(8,128)(2,1)S(1)}, bf16[8192,128]{1,0:T(8,128)(2,1)}, u32[]{:S(2)}) copy-start(bf16[8192,128]{1,0:T(8,128)(2,1)} %copy-done.7) | copy-start | bytes 6291460
  47.1 16.1 %collective-permute-start.4 = (bf16[3072,128]{1,0:T(8,128)(2,1)}, bf16[3072,128]{1,0:T(8,128)(2,1)}, u32[]{:S(2)}, u32[]{:S(2)}) collective-permute-start(bf16[3072,128]{1,0:T(8,128)(2,1)} %get-tuple-element.44), channel_id=1, source_target_pairs={{1,9},{10,2},{3,11},{13,5},{2,1},{4,3},{17,25},{26,18},{19,27},{29... | collective-permute-start | bytes 2359304 | tf_op jit(solution)/shard_map/ppermute | solution.py:365
  54.3 8.8 %collective-permute-start.6 = (bf16[9,128,128]{2,1,0:T(8,128)(2,1)S(1)}, bf16[9,128,128]{2,1,0:T(8,128)(2,1)}, u32[]{:S(2)}, u32[]{:S(2)}) collective-permute-start(bf16[9,128,128]{2,1,0:T(8,128)(2,1)S(1)} %get-tuple-element.49), channel_id=1, source_target_pairs={{0,7},{7,15},{16,23},{23,31}} | collective-permute-start | bytes 884744 | tf_op jit(solution)/shard_map/ppermute | solution.py:367
  61.8 1.4 %collective-permute-start.7 = (bf16[9,128,128]{2,1,0:T(8,128)(2,1)}, bf16[9,128,128]{2,1,0:T(8,128)(2,1)}, u32[]{:S(2)}, u32[]{:S(2)}) collective-permute-start(bf16[9,128,128]{2,1,0:T(8,128)(2,1)} %get-tuple-element.50.rest_3_), channel_id=1, source_target_pairs={{0,8},{12,4},{14,6},{7,15},{16,24},{28,20},{30,22},{23,31}} | collective-permute-start | bytes 884744 | tf_op jit(solution)/shard_map/ppermute | solution.py:371
  63.2 1.6 %copy-start.2 = (bf16[128,8192]{1,0:T(8,128)(2,1)S(1)}, bf16[128,8192]{1,0:T(8,128)(2,1)}, u32[]{:S(2)}) copy-start(bf16[128,8192]{1,0:T(8,128)(2,1)} %copy-done) | copy-start | bytes 6291460
  69.9 8.6 %collective-permute-start.8 = (bf16[9,128,128]{2,1,0:T(8,128)(2,1)}, bf16[9,128,128]{2,1,0:T(8,128)(2,1)S(1)}, u32[]{:S(2)}, u32[]{:S(2)}) collective-permute-start(bf16[9,128,128]{2,1,0:T(8,128)(2,1)} %get-tuple-element.51), channel_id=1, source_target_pairs={{9,1},{2,10},{11,3},{5,13},{1,0},{25,17},{18,26},{27,19},{21,29},{... | collective-permute-start | bytes 884744 | tf_op jit(solution)/shard_map/ppermute | solution.py:379

commit v18 on v16

--- a/solution.py
+++ b/solution.py
@@ -12,7 +12,7 @@
 LAGS = 2 * HL + 1
 STEP = 1024
 PARTS = (5, 8)
-PARAMS = pltpu.CompilerParams(vmem_limit_bytes=12 * 1024 * 1024)
+PARAMS = pltpu.CompilerParams(vmem_limit_bytes=16 * 1024 * 1024)
 
 
 def lag_rows(freq_count, window_count):
@@ -134,11 +134,9 @@
     cols = plain_ref.shape[0]
     near_mirrored, special = switch_ref[0], switch_ref[1]
     if last:
-        acc_in, _, near_out, far_out, back_out, acc, scaled, plain, swapped, own_rows, arrived = rest
+        acc_in, _, near_out, far_out, back_out, acc, scaled, plain, swapped = rest
     else:
-        acc, token_out, scaled, plain, swapped, own_rows, arrived = rest
-    size = own_rows.shape[0]
-    begin = size if last else 0
+        acc, token_out, scaled, plain, swapped = rest
 
     @pl.when(step == 0)
     def _():
@@ -152,12 +150,6 @@
     def _():
         plain[...], swapped[...] = plain_ref[...], swapped_ref[...]
 
-    @pl.when((special != 0) & (step == 0))
-    def _():
-        copy = pltpu.make_async_copy(own_ref.at[pl.ds(begin, size)], own_rows, arrived)
-        copy.start()
-        copy.wait()
-
     @pl.when(special != 0)
     def _():
         plain[...], swapped[...] = turned(first_ref[...])
@@ -166,8 +158,7 @@
     flags = [[switch_ref[2 + part * windows + w] for w in range(windows)] for part in range(3)]
     near_weights = [jnp.where(special != 0, first, own) * near for own, near, first in zip(*flags)]
     near = weigh(near_ref[...], near_weights)
-    own_tile = own_rows[pl.ds(pl.multiple_of(step * STEP, STEP), STEP), :]
-    far = weigh(jnp.where(special != 0, own_tile, first_ref[...]), [own * first for own, _, first in zip(*flags)])
+    far = weigh(jnp.where(special != 0, own_ref[...], first_ref[...]), [own * first for own, _, first in zip(*flags)])
     acc[...] += jnp.dot(scaled[...], jnp.concatenate([near, far], axis=1), preferred_element_type=jnp.float32)
 
     if last:
@@ -201,10 +192,9 @@
     token_spec = pl.BlockSpec(token.shape, lambda s, on: (0, 0))
     left = pl.BlockSpec((cols, STEP), lambda s, on: (0, (s + skip) * (1 - on[1])))
     right = pl.BlockSpec((STEP, cols), lambda s, on: (s + skip, 0))
-    in_specs = [left, left, pl.BlockSpec((LAGS, STEP), lambda s, on: (0, s + skip)), right, right,
-                pl.BlockSpec(memory_space=pltpu.HBM)]
+    right_special = pl.BlockSpec((STEP, cols), lambda s, on: ((s + skip) * on[1], 0))
+    in_specs = [left, left, pl.BlockSpec((LAGS, STEP), lambda s, on: (0, s + skip)), right, right, right_special]
     scratch = [pltpu.VMEM((LAGS * cols, STEP), jnp.bfloat16)] + [pltpu.VMEM((cols, STEP), jnp.bfloat16)] * 2
-    scratch += [pltpu.VMEM((steps * STEP, cols), jnp.bfloat16), pltpu.SemaphoreType.DMA(())]
     if earlier is None:
         out_shape, out_specs, earlier = [total, token], [total_spec, token_spec], []
     else:

time: 80 us -> 80 us (level)
  no operation moved by 1% of the time
where the time goes in v18:
time: 80 us; the launch traced here: 79.4 us
  starting transfers between devices  30.9 us (39%)
  Pallas kernels  27.9 us (35%)
  local copies, waits for them, and re-layouts  13.5 us (17%)
  other arithmetic  3.17 us (4%)
  waiting for transfers between devices  3.13 us (4%)
  between operations  0.88 us (1%)
    ppermute x1, starting transfers between devices, local(): second_in = [lax.ppermute(first_part, 'chan', second_pairs)]  16.7 us
    unnamed x20, local copies, waits for them, and re-layouts  13.5 us
    pallas_call x2, Pallas kernels, second_sums(): pl.pallas_call(functools.partial(second_kernel, windows, not earlier), gr...  11.2 us
    pallas_call x2, Pallas kernels, first_sums(): pl.pallas_call(functools.partial(first_kernel, windows, bool(earlier)), g...  9.71 us
    ppermute x1, starting transfers between devices, local(): second_returned = lax.ppermute(back, 'chan', second_back)  5.43 us
    pallas_call x1, Pallas kernels, split(): pl.pallas_call(functools.partial(split_kernel, middle, flags.shape[0]), g...  3.86 us
    pallas_call x1, Pallas kernels, turn(): pl.pallas_call(turn_kernel, grid=(rows // STEP,), in_specs=[pl.BlockSpec(...  3.15 us
    ppermute x1, waiting for transfers between devices, local(): second_returned = lax.ppermute(back, 'chan', second_back)  3.11 us
  transfers between devices with their start and end apart: 9, of which 1 were waited for; matrix products, arithmetic and copies ran while one was open for 3% of the time, Pallas kernels for 29%

profile of v18, /device:TPU:1, one launch (start us, length us, event | category | flops | bytes accessed | tf_op | source)
XLA Modules:
  0.0 79.4 jit_solution(3389730373702880236)
XLA Ops:
  1.4 1.3 %collective-permute-start.1 = (bf16[8192,128]{1,0:T(8,128)(2,1)}, bf16[8192,128]{1,0:T(8,128)(2,1)S(1)}, u32[]{:S(2)}, u32[]{:S(2)}) collective-permute-start(bf16[8192,128]{1,0:T(8,128)(2,1)} %bitcast.13), channel_id=1, source_target_pairs={{8,0},{4,12},{6,14},{15,7},{0,1},{7,6},{24,16},{20,28},{22,30},{31... | collective-permute-start | bytes 6291464 | tf_op jit(solution)/shard_map/ppermute | solution.py:334
  3.4 1.3 %collective-permute-start.3 = (s32[1,4]{1,0:T(1,128)}, s32[1,4]{1,0:T(1,128)S(1)}, u32[]{:S(2)}, u32[]{:S(2)}) collective-permute-start(s32[1,4]{1,0:T(1,128)} %param.3), channel_id=1, source_target_pairs={{8,0},{4,12},{6,14},{15,7},{0,1},{7,6},{24,16},{20,28},{22,30},{31... | collective-permute-start | bytes 56 | tf_op jit(solution)/shard_map/ppermute | solution.py:338
  4.7 1.6 %copy-done.3 = bf16[1024,2,4,128]{3,2,1,0:T(4,128)(2,1)S(1)} copy-done((bf16[1024,2,4,128]{3,2,1,0:T(4,128)(2,1)S(1)}, bf16[1024,2,4,128]{3,2,1,0:T(4,128)(2,1)}, u32[]{:S(2)}) %copy-start.3) | copy-done | bytes 2097176
  6.3 3.1 %turn.1 = (bf16[128,8192]{1,0:T(8,128)(2,1)S(1)}, bf16[128,8192]{1,0:T(8,128)(2,1)S(1)}) custom-call(bf16[8192,128]{1,0:T(8,128)(2,1)S(1)} %bitcast.14), custom_call_target="tpu_custom_call" | custom-call | bytes 6291456 | tf_op jit(solution)/shard_map/turn/pallas_call | solution.py:89
  9.5 1.3 %copy-done = bf16[128,8192]{1,0:T(8,128)(2,1)} copy-done((bf16[128,8192]{1,0:T(8,128)(2,1)}, bf16[128,8192]{1,0:T(8,128)(2,1)S(1)}, u32[]{:S(2)}) %copy-start) | copy-done | bytes 2097176
  10.8 3.9 %split.1 = (bf16[5120,128]{1,0:T(8,128)(2,1)}, bf16[3072,128]{1,0:T(8,128)(2,1)}) custom-call(s32[4]{0:T(128)S(1)} %bitcast.18, bf16[8192,128]{1,0:T(8,128)(2,1)S(1)} %bitcast.15), custom_call_target="tpu_custom_call" | custom-call | flops 1048576 | bytes 4194304 | tf_op jit(solution)/shard_map/split/pallas_call | solution.py:48
  14.7 0.9 %multiply_convert_fusion = (bf16[5,8192]{1,0:T(8,128)(2,1)S(1)}, f32[5,8192]{1,0:T(8,128)S(1)}) fusion(f32[8192]{0:T(1024)S(1)} %fusion.9, f32[5]{0:T(128)S(1)} %iota_multiply_fusion), kind=kLoop, calls=%fused_computation.5 | loop fusion | flops 122880 | bytes 278548 | tf_op jit(solution)/shard_map/convert
  16.6 1.3 %copy-done.5 = bf16[8192,128]{1,0:T(8,128)(2,1)} copy-done((bf16[8192,128]{1,0:T(8,128)(2,1)}, bf16[8192,128]{1,0:T(8,128)(2,1)S(1)}, u32[]{:S(2)}) %copy-start.5) | copy-done | bytes 2097176
  17.9 1.4 %copy-done.7 = bf16[8192,128]{1,0:T(8,128)(2,1)} copy-done((bf16[8192,128]{1,0:T(8,128)(2,1)}, bf16[8192,128]{1,0:T(8,128)(2,1)S(1)}, u32[]{:S(2)}) %copy-start.7) | copy-done | bytes 2097176
  19.3 16.7 %collective-permute-start.5 = (bf16[5120,128]{1,0:T(8,128)(2,1)}, bf16[5120,128]{1,0:T(8,128)(2,1)}, u32[]{:S(2)}, u32[]{:S(2)}) collective-permute-start(bf16[5120,128]{1,0:T(8,128)(2,1)} %get-tuple-element.47), channel_id=1, source_target_pairs={{1,9},{10,2},{3,11},{13,5},{2,1},{4,3},{17,25},{26,18},{19,27},{29... | collective-permute-start | bytes 3932168 | tf_op jit(solution)/shard_map/ppermute | solution.py:348
  36.4 1.6 %copy-done.1 = bf16[128,8192]{1,0:T(8,128)(2,1)S(1)} copy-done((bf16[128,8192]{1,0:T(8,128)(2,1)S(1)}, bf16[128,8192]{1,0:T(8,128)(2,1)}, u32[]{:S(2)}) %copy-start.1) | copy-done | bytes 2097176
  38.0 1.6 %copy-done.4 = bf16[1024,2,4,128]{3,2,1,0:T(4,128)(2,1)S(1)} copy-done((bf16[1024,2,4,128]{3,2,1,0:T(4,128)(2,1)S(1)}, bf16[1024,2,4,128]{3,2,1,0:T(4,128)(2,1)}, u32[]{:S(2)}) %copy-start.4) | copy-done | bytes 2097176
  39.6 1.6 %copy-done.6 = bf16[8192,128]{1,0:T(8,128)(2,1)S(1)} copy-done((bf16[8192,128]{1,0:T(8,128)(2,1)S(1)}, bf16[8192,128]{1,0:T(8,128)(2,1)}, u32[]{:S(2)}) %copy-start.6) | copy-done | bytes 2097176
  41.2 1.6 %copy-done.8 = bf16[8192,128]{1,0:T(8,128)(2,1)S(1)} copy-done((bf16[8192,128]{1,0:T(8,128)(2,1)S(1)}, bf16[8192,128]{1,0:T(8,128)(2,1)}, u32[]{:S(2)}) %copy-start.8) | copy-done | bytes 2097176
  42.8 4.4 %first_half.1 = (f32[1152,256]{1,0:T(8,128)S(1)}, f32[8,128]{1,0:T(8,128)S(1)}) custom-call(s32[14]{0:T(128)S(1)} %pad_add_fusion.1.switch_ref, bf16[128,8192]{1,0:T(8,128)(2,1)S(1)} %get-tuple-element.35.plain_ref, bf16[128,8192]{1,0:T(8,128)(2,1)S(1)} %copy-done.1, bf16[9,8192]{1,0:T(8,128)(2,1)S(1)} %pad_maximum_fusion.coeff_ref, ...), custom_call_target="tpu_custom_call" | custom-call | flops 2415919104 | bytes 4194304 | tf_op jit(solution)/shard_map/first_half/pallas_call | solution.py:205
  47.2 1.9 %collective-permute-start.4 = (bf16[3072,128]{1,0:T(8,128)(2,1)}, bf16[3072,128]{1,0:T(8,128)(2,1)}, u32[]{:S(2)}, u32[]{:S(2)}) collective-permute-start(bf16[3072,128]{1,0:T(8,128)(2,1)} %get-tuple-element.46), channel_id=1, source_target_pairs={{1,9},{10,2},{3,11},{13,5},{2,1},{4,3},{17,25},{26,18},{19,27},{29... | collective-permute-start | bytes 2359304 | tf_op jit(solution)/shard_map/ppermute | solution.py:353
  49.1 5.3 %first_last.1 = (bf16[9,128,128]{2,1,0:T(8,128)(2,1)S(1)}, bf16[9,128,128]{2,1,0:T(8,128)(2,1)S(1)}, bf16[9,128,128]{2,1,0:T(8,128)(2,1)}) custom-call(s32[14]{0:T(128)S(1)} %pad_add_fusion.1.switch_ref, bf16[128,8192]{1,0:T(8,128)(2,1)S(1)} %get-tuple-element.35.plain_ref, bf16[128,8192]{1,0:T(8,128)(2,1)S(1)} %copy-done.1, ...), custom_call_target="tpu_custom_call" | custom-call | flops 2415919104 | bytes 4194304 | tf_op jit(solution)/shard_map/first_last/pallas_call | solution.py:205
  54.4 1.4 %collective-permute-start.6 = (bf16[9,128,128]{2,1,0:T(8,128)(2,1)S(1)}, bf16[9,128,128]{2,1,0:T(8,128)(2,1)}, u32[]{:S(2)}, u32[]{:S(2)}) collective-permute-start(bf16[9,128,128]{2,1,0:T(8,128)(2,1)S(1)} %get-tuple-element.51), channel_id=1, source_target_pairs={{0,7},{7,15},{16,23},{23,31}} | collective-permute-start | bytes 884744 | tf_op jit(solution)/shard_map/ppermute | solution.py:355
  55.8 6.1 %second_part.1.rest_0_ = f32[1152,128]{1,0:T(8,128)S(1)} custom-call(s32[6]{0:T(128)S(1)} %pad_add_fusion.switch_ref, bf16[128,8192]{1,0:T(8,128)(2,1)S(1)} %get-tuple-element.35.plain_ref, bf16[128,8192]{1,0:T(8,128)(2,1)S(1)} %copy-done.1, bf16[9,8192]{1,0:T(8,128)(2,1)S(1)} %pad_maximum_fusion.coeff_ref, bf16[5120,128]{1,0:T(8,128)(2,1)} %collective-permute-done.5.partner_ref), custom_call_target="tpu_custom_call" | custom-call | flops 1509949440 | bytes 3932160 | tf_op jit(solution)/shard_map/second_part/pallas_call | solution.py:282
  61.9 1.4 %collective-permute-start.7 = (bf16[9,128,128]{2,1,0:T(8,128)(2,1)}, bf16[9,128,128]{2,1,0:T(8,128)(2,1)}, u32[]{:S(2)}, u32[]{:S(2)}) collective-permute-start(bf16[9,128,128]{2,1,0:T(8,128)(2,1)} %get-tuple-element.52.rest_3_), channel_id=1, source_target_pairs={{0,8},{12,4},{14,6},{7,15},{16,24},{28,20},{30,22},{23,31}} | collective-permute-start | bytes 884744 | tf_op jit(solution)/shard_map/ppermute | solution.py:359
  63.3 1.6 %copy-done.2 = bf16[128,8192]{1,0:T(8,128)(2,1)S(1)} copy-done((bf16[128,8192]{1,0:T(8,128)(2,1)S(1)}, bf16[128,8192]{1,0:T(8,128)(2,1)}, u32[]{:S(2)}) %copy-start.2) | copy-done | bytes 2097176
  64.9 5.1 %second_last.1 = (bf16[9,128,128]{2,1,0:T(8,128)(2,1)S(1)}, bf16[9,128,128]{2,1,0:T(8,128)(2,1)S(1)}, bf16[9,128,128]{2,1,0:T(8,128)(2,1)}) custom-call(s32[6]{0:T(128)S(1)} %pad_add_fusion.switch_ref, bf16[128,8192]{1,0:T(8,128)(2,1)S(1)} %get-tuple-element.35.plain_ref, bf16[128,8192]{1,0:T(8,128)(2,1)S(1)} %copy-done.2, ...), custom_call_target="tpu_custom_call" | custom-call | flops 905969664 | bytes 2359296 | tf_op jit(solution)/shard_map/second_last/pallas_call | solution.py:282
  70.0 5.4 %collective-permute-start.8 = (bf16[9,128,128]{2,1,0:T(8,128)(2,1)}, bf16[9,128,128]{2,1,0:T(8,128)(2,1)S(1)}, u32[]{:S(2)}, u32[]{:S(2)}) collective-permute-start(bf16[9,128,128]{2,1,0:T(8,128)(2,1)} %get-tuple-element.53), channel_id=1, source_target_pairs={{9,1},{2,10},{11,3},{5,13},{1,0},{25,17},{18,26},{27,19},{21,29},{... | collective-permute-start | bytes 884744 | tf_op jit(solution)/shard_map/ppermute | solution.py:367
  75.5 3.1 %collective-permute-done.8 = bf16[9,128,128]{2,1,0:T(8,128)(2,1)S(1)} collective-permute-done((bf16[9,128,128]{2,1,0:T(8,128)(2,1)}, bf16[9,128,128]{2,1,0:T(8,128)(2,1)S(1)}, u32[]{:S(2)}, u32[]{:S(2)}) %collective-permute-start.8) | collective-permute-done | bytes 294944 | tf_op jit(solution)/shard_map/ppermute | solution.py:367
  (32 shorter events, 3.7 us)
Async XLA Ops:
  0.6 10.2 %copy-start.9 = (s32[1,4]{1,0:T(1,128)S(1)}, s32[1,4]{1,0:T(1,128)}, u32[]{:S(2)}) copy-start(s32[1,4]{1,0:T(1,128)} %param.3) | copy-start | bytes 52
  0.6 16.0 %collective-permute-start = (bf16[8192,128]{1,0:T(8,128)(2,1)}, bf16[8192,128]{1,0:T(8,128)(2,1)S(1)}, u32[]{:S(2)}, u32[]{:S(2)}) collective-permute-start(bf16[8192,128]{1,0:T(8,128)(2,1)} %bitcast.12), channel_id=1, source_target_pairs={{3,2},{5,4},{6,5},{9,8},{10,9},{11,10},{12,11},{13,12},{14,13},{15... | collective-permute-start | bytes 6291464 | tf_op jit(solution)/shard_map/ppermute | solution.py:333
  1.4 16.5 %collective-permute-start.1 = (bf16[8192,128]{1,0:T(8,128)(2,1)}, bf16[8192,128]{1,0:T(8,128)(2,1)S(1)}, u32[]{:S(2)}, u32[]{:S(2)}) collective-permute-start(bf16[8192,128]{1,0:T(8,128)(2,1)} %bitcast.13), channel_id=1, source_target_pairs={{8,0},{4,12},{6,14},{15,7},{0,1},{7,6},{24,16},{20,28},{22,30},{31... | collective-permute-start | bytes 6291464 | tf_op jit(solution)/shard_map/ppermute | solution.py:334
  2.7 13.9 %collective-permute-start.2 = (s32[1,4]{1,0:T(1,128)}, s32[1,4]{1,0:T(1,128)S(1)}, u32[]{:S(2)}, u32[]{:S(2)}) collective-permute-start(s32[1,4]{1,0:T(1,128)} %param.3), channel_id=1, source_target_pairs={{3,2},{5,4},{6,5},{9,8},{10,9},{11,10},{12,11},{13,12},{14,13},{15... | collective-permute-start | bytes 56 | tf_op jit(solution)/shard_map/ppermute | solution.py:339
  3.4 13.2 %collective-permute-start.3 = (s32[1,4]{1,0:T(1,128)}, s32[1,4]{1,0:T(1,128)S(1)}, u32[]{:S(2)}, u32[]{:S(2)}) collective-permute-start(s32[1,4]{1,0:T(1,128)} %param.3), channel_id=1, source_target_pairs={{8,0},{4,12},{6,14},{15,7},{0,1},{7,6},{24,16},{20,28},{22,30},{31... | collective-permute-start | bytes 56 | tf_op jit(solution)/shard_map/ppermute | solution.py:338
  4.7 1.6 %copy-start.3 = (bf16[1024,2,4,128]{3,2,1,0:T(4,128)(2,1)S(1)}, bf16[1024,2,4,128]{3,2,1,0:T(4,128)(2,1)}, u32[]{:S(2)}) copy-start(bf16[1024,2,4,128]{3,2,1,0:T(4,128)(2,1)} %param.2) | copy-start | bytes 6291460
  9.5 1.3 %copy-start = (bf16[128,8192]{1,0:T(8,128)(2,1)}, bf16[128,8192]{1,0:T(8,128)(2,1)S(1)}, u32[]{:S(2)}) copy-start(bf16[128,8192]{1,0:T(8,128)(2,1)S(1)} %get-tuple-element.36.swapped_ref) | copy-start | bytes 6291460
  16.6 1.3 %copy-start.5 = (bf16[8192,128]{1,0:T(8,128)(2,1)}, bf16[8192,128]{1,0:T(8,128)(2,1)S(1)}, u32[]{:S(2)}) copy-start(bf16[8192,128]{1,0:T(8,128)(2,1)S(1)} %collective-permute-done.near_ref) | copy-start | bytes 6291460
  17.9 1.4 %copy-start.7 = (bf16[8192,128]{1,0:T(8,128)(2,1)}, bf16[8192,128]{1,0:T(8,128)(2,1)S(1)}, u32[]{:S(2)}) copy-start(bf16[8192,128]{1,0:T(8,128)(2,1)S(1)} %collective-permute-done.1.first_ref) | copy-start | bytes 6291460
  19.3 36.5 %collective-permute-start.5 = (bf16[5120,128]{1,0:T(8,128)(2,1)}, bf16[5120,128]{1,0:T(8,128)(2,1)}, u32[]{:S(2)}, u32[]{:S(2)}) collective-permute-start(bf16[5120,128]{1,0:T(8,128)(2,1)} %get-tuple-element.47), channel_id=1, source_target_pairs={{1,9},{10,2},{3,11},{13,5},{2,1},{4,3},{17,25},{26,18},{19,27},{29... | collective-permute-start | bytes 3932168 | tf_op jit(solution)/shard_map/ppermute | solution.py:348
  36.4 1.6 %copy-start.1 = (bf16[128,8192]{1,0:T(8,128)(2,1)S(1)}, bf16[128,8192]{1,0:T(8,128)(2,1)}, u32[]{:S(2)}) copy-start(bf16[128,8192]{1,0:T(8,128)(2,1)} %copy-done) | copy-start | bytes 6291460
  38.0 1.6 %copy-start.4 = (bf16[1024,2,4,128]{3,2,1,0:T(4,128)(2,1)S(1)}, bf16[1024,2,4,128]{3,2,1,0:T(4,128)(2,1)}, u32[]{:S(2)}) copy-start(bf16[1024,2,4,128]{3,2,1,0:T(4,128)(2,1)} %param.2) | copy-start | bytes 6291460
  39.6 1.6 %copy-start.6 = (bf16[8192,128]{1,0:T(8,128)(2,1)S(1)}, bf16[8192,128]{1,0:T(8,128)(2,1)}, u32[]{:S(2)}) copy-start(bf16[8192,128]{1,0:T(8,128)(2,1)} %copy-done.5) | copy-start | bytes 6291460
  41.2 1.6 %copy-start.8 = (bf16[8192,128]{1,0:T(8,128)(2,1)S(1)}, bf16[8192,128]{1,0:T(8,128)(2,1)}, u32[]{:S(2)}) copy-start(bf16[8192,128]{1,0:T(8,128)(2,1)} %copy-done.7) | copy-start | bytes 6291460
  47.2 16.2 %collective-permute-start.4 = (bf16[3072,128]{1,0:T(8,128)(2,1)}, bf16[3072,128]{1,0:T(8,128)(2,1)}, u32[]{:S(2)}, u32[]{:S(2)}) collective-permute-start(bf16[3072,128]{1,0:T(8,128)(2,1)} %get-tuple-element.46), channel_id=1, source_target_pairs={{1,9},{10,2},{3,11},{13,5},{2,1},{4,3},{17,25},{26,18},{19,27},{29... | collective-permute-start | bytes 2359304 | tf_op jit(solution)/shard_map/ppermute | solution.py:353
  54.4 8.8 %collective-permute-start.6 = (bf16[9,128,128]{2,1,0:T(8,128)(2,1)S(1)}, bf16[9,128,128]{2,1,0:T(8,128)(2,1)}, u32[]{:S(2)}, u32[]{:S(2)}) collective-permute-start(bf16[9,128,128]{2,1,0:T(8,128)(2,1)S(1)} %get-tuple-element.51), channel_id=1, source_target_pairs={{0,7},{7,15},{16,23},{23,31}} | collective-permute-start | bytes 884744 | tf_op jit(solution)/shard_map/ppermute | solution.py:355
  61.9 1.4 %collective-permute-start.7 = (bf16[9,128,128]{2,1,0:T(8,128)(2,1)}, bf16[9,128,128]{2,1,0:T(8,128)(2,1)}, u32[]{:S(2)}, u32[]{:S(2)}) collective-permute-start(bf16[9,128,128]{2,1,0:T(8,128)(2,1)} %get-tuple-element.52.rest_3_), channel_id=1, source_target_pairs={{0,8},{12,4},{14,6},{7,15},{16,24},{28,20},{30,22},{23,31}} | collective-permute-start | bytes 884744 | tf_op jit(solution)/shard_map/ppermute | solution.py:359
  63.3 1.6 %copy-start.2 = (bf16[128,8192]{1,0:T(8,128)(2,1)S(1)}, bf16[128,8192]{1,0:T(8,128)(2,1)}, u32[]{:S(2)}) copy-start(bf16[128,8192]{1,0:T(8,128)(2,1)} %copy-done) | copy-start | bytes 6291460
  70.0 8.6 %collective-permute-start.8 = (bf16[9,128,128]{2,1,0:T(8,128)(2,1)}, bf16[9,128,128]{2,1,0:T(8,128)(2,1)S(1)}, u32[]{:S(2)}, u32[]{:S(2)}) collective-permute-start(bf16[9,128,128]{2,1,0:T(8,128)(2,1)} %get-tuple-element.53), channel_id=1, source_target_pairs={{9,1},{2,10},{11,3},{5,13},{1,0},{25,17},{18,26},{27,19},{21,29},{... | collective-permute-start | bytes 884744 | tf_op jit(solution)/shard_map/ppermute | solution.py:367

commit v19 on v15

--- a/solution.py
+++ b/solution.py
@@ -304,9 +304,9 @@
     for p in range(half):
         if p in (0, half - 1):
             first_far.append((p + half, p))
-        elif p % 2 == 0 and p >= half // 2:
+        elif p > half // 2:
             first_far.append((p, p + half))
-        elif p in (1, 3):
+        elif p % 2 == 1:
             second_far.append((p, p + half))
         else:
             second_far.append((p + half, p))

time: 73.5 us -> 70.7 us (0.962)
  waiting for transfers between devices: 9.29 us -> 6.41 us
    ppermute x1, waiting for transfers between devices: 9.27 us -> 6.39 us  [local(): returned = lax.ppermute(back, 'chan', back_pairs)]
  transfers between devices with their start and end apart: 9 -> 9, of which waited for: 1 -> 1; matrix products, arithmetic and copies ran while one was open for 3% -> 3% of each run, Pallas kernels for 33% -> 34%
where the time goes in v19:
time: 70.7 us; the launch traced here: 70.1 us
  starting transfers between devices  28.5 us (40%)
  Pallas kernels  24 us (34%)
  local copies, waits for them, and re-layouts  7.16 us (10%)
  waiting for transfers between devices  6.41 us (9%)
  other arithmetic  3.15 us (4%)
  between operations  0.9 us (1%)
    pallas_call x2, Pallas kernels, first_sums(): pl.pallas_call(functools.partial(first_kernel, windows, bool(earlier)), g...  11.2 us
    ppermute x1, starting transfers between devices, local(): second_flags = lax.ppermute(quality, 'chan', second_pairs)[0]  10.5 us
    pallas_call x2, Pallas kernels, second_sums(): pl.pallas_call(functools.partial(second_kernel, windows, not earlier), gr...  9.37 us
    ppermute x1, starting transfers between devices, local(): second_in = [lax.ppermute(first_part, 'chan', second_pairs)]  7.59 us
    unnamed x12, local copies, waits for them, and re-layouts  7.16 us
    ppermute x1, waiting for transfers between devices, local(): returned = lax.ppermute(back, 'chan', back_pairs)  6.39 us
    pallas_call x1, Pallas kernels, turn(): pl.pallas_call(turn_kernel, grid=(rows // STEP,), in_specs=[pl.BlockSpec(...  3.15 us
    ppermute x1, starting transfers between devices, local(): near_in = lax.ppermute(block, 'chan', near_pairs)  2 us
  transfers between devices with their start and end apart: 9, of which 1 were waited for; matrix products, arithmetic and copies ran while one was open for 3% of the time, Pallas kernels for 34%

profile of v19, /device:TPU:1, one launch (start us, length us, event | category | flops | bytes accessed | tf_op | source)
XLA Modules:
  0.0 70.1 jit_solution(14435174890389317081)
XLA Ops:
  0.6 2.0 %collective-permute-start.3 = (bf16[8192,128]{1,0:T(8,128)(2,1)}, bf16[8192,128]{1,0:T(8,128)(2,1)}, u32[]{:S(2)}, u32[]{:S(2)}) collective-permute-start(bf16[8192,128]{1,0:T(8,128)(2,1)} %bitcast.15), channel_id=1, source_target_pairs={{3,2},{5,4},{6,5},{9,8},{10,9},{11,10},{12,11},{13,12},{14,13},{15... | collective-permute-start | bytes 6291464 | tf_op jit(solution)/shard_map/ppermute | solution.py:328
  2.6 1.3 %collective-permute-start.4 = (bf16[8192,128]{1,0:T(8,128)(2,1)}, bf16[8192,128]{1,0:T(8,128)(2,1)}, u32[]{:S(2)}, u32[]{:S(2)}) collective-permute-start(bf16[8192,128]{1,0:T(8,128)(2,1)} %bitcast.16), channel_id=1, source_target_pairs={{8,0},{5,13},{6,14},{15,7},{0,1},{7,6},{24,16},{21,29},{22,30},{31... | collective-permute-start | bytes 6291464 | tf_op jit(solution)/shard_map/ppermute | solution.py:329
  3.9 0.7 collective-permute-start.1
  4.6 1.3 %collective-permute-start.2 = (s32[1,4]{1,0:T(1,128)}, s32[1,4]{1,0:T(1,128)S(1)}, u32[]{:S(2)}, u32[]{:S(2)}) collective-permute-start(s32[1,4]{1,0:T(1,128)} %param.3), channel_id=1, source_target_pairs={{8,0},{5,13},{6,14},{15,7},{0,1},{7,6},{24,16},{21,29},{22,30},{31... | collective-permute-start | bytes 56 | tf_op jit(solution)/shard_map/ppermute | solution.py:333
  5.9 10.5 %collective-permute-start = (s32[1,4]{1,0:T(1,128)}, s32[1,4]{1,0:T(1,128)S(1)}, u32[]{:S(2)}, u32[]{:S(2)}) collective-permute-start(s32[1,4]{1,0:T(1,128)} %param.3), channel_id=1, source_target_pairs={{1,9},{10,2},{3,11},{12,4},{2,1},{4,3},{17,25},{26,18},{19,27},{28... | collective-permute-start | bytes 56 | tf_op jit(solution)/shard_map/ppermute | solution.py:335
  16.4 1.6 %copy-done.2 = bf16[1024,2,4,128]{3,2,1,0:T(4,128)(2,1)S(1)} copy-done((bf16[1024,2,4,128]{3,2,1,0:T(4,128)(2,1)S(1)}, bf16[1024,2,4,128]{3,2,1,0:T(4,128)(2,1)}, u32[]{:S(2)}) %copy-start.2) | copy-done | bytes 2097176
  18.0 3.2 %turn.1 = (bf16[128,8192]{1,0:T(8,128)(2,1)S(1)}, bf16[128,8192]{1,0:T(8,128)(2,1)S(1)}) custom-call(bf16[8192,128]{1,0:T(8,128)(2,1)S(1)} %bitcast.17), custom_call_target="tpu_custom_call" | custom-call | bytes 6291456 | tf_op jit(solution)/shard_map/turn/pallas_call | solution.py:85
  21.1 1.3 %copy-done = bf16[128,8192]{1,0:T(8,128)(2,1)} copy-done((bf16[128,8192]{1,0:T(8,128)(2,1)}, bf16[128,8192]{1,0:T(8,128)(2,1)S(1)}, u32[]{:S(2)}) %copy-start) | copy-done | bytes 2097176
  22.5 0.3 split.1
  22.8 1.0 %copy-done.4 = bf16[5120,128]{1,0:T(8,128)(2,1)} copy-done((bf16[5120,128]{1,0:T(8,128)(2,1)}, bf16[5120,128]{1,0:T(8,128)(2,1)S(1)}, u32[]{:S(2)}) %copy-start.4) | copy-done | bytes 1310744
  23.9 0.9 %multiply_convert_fusion = (bf16[5,8192]{1,0:T(8,128)(2,1)S(1)}, f32[5,8192]{1,0:T(8,128)S(1)}) fusion(f32[8192]{0:T(1024)S(1)} %fusion.9, f32[5]{0:T(128)S(1)} %iota_multiply_fusion), kind=kLoop, calls=%fused_computation.4 | loop fusion | flops 122880 | bytes 278548 | tf_op jit(solution)/shard_map/convert
  24.8 0.9 %fusion.2 = bf16[4,8192]{1,0:T(4,128)(2,1)S(1)} fusion(f32[5,8192]{1,0:T(8,128)S(1)} %get-tuple-element.51, f32[8192]{0:T(1024)S(1)} %select_multiply_fusion), kind=kLoop, calls=%fused_computation.8 | loop fusion | flops 98304 | bytes 229376 | tf_op jit(solution)/shard_map/convert.1
  25.8 7.6 %collective-permute-start.6 = (bf16[5120,128]{1,0:T(8,128)(2,1)}, bf16[5120,128]{1,0:T(8,128)(2,1)}, u32[]{:S(2)}, u32[]{:S(2)}) collective-permute-start(bf16[5120,128]{1,0:T(8,128)(2,1)} %copy-done.4), channel_id=1, source_target_pairs={{1,9},{10,2},{3,11},{12,4},{2,1},{4,3},{17,25},{26,18},{19,27},{28... | collective-permute-start | bytes 3932168 | tf_op jit(solution)/shard_map/ppermute | solution.py:345
  33.7 1.6 %copy-done.1 = bf16[128,8192]{1,0:T(8,128)(2,1)S(1)} copy-done((bf16[128,8192]{1,0:T(8,128)(2,1)S(1)}, bf16[128,8192]{1,0:T(8,128)(2,1)}, u32[]{:S(2)}) %copy-start.1) | copy-done | bytes 2097176
  35.3 1.6 %copy-done.3 = bf16[1024,2,4,128]{3,2,1,0:T(4,128)(2,1)S(1)} copy-done((bf16[1024,2,4,128]{3,2,1,0:T(4,128)(2,1)S(1)}, bf16[1024,2,4,128]{3,2,1,0:T(4,128)(2,1)}, u32[]{:S(2)}) %copy-start.3) | copy-done | bytes 2097176
  36.8 5.5 %first_half.1 = (f32[1152,256]{1,0:T(8,128)S(1)}, f32[8,128]{1,0:T(8,128)S(1)}) custom-call(s32[14]{0:T(128)S(1)} %pad_add_fusion.1.switch_ref, bf16[128,8192]{1,0:T(8,128)(2,1)S(1)} %get-tuple-element.29.plain_ref, bf16[128,8192]{1,0:T(8,128)(2,1)S(1)} %copy-done.1, bf16[9,8192]{1,0:T(8,128)(2,1)S(1)} %pad_maximum_fusion.coeff_ref, ...), custom_call_target="tpu_custom_call" | custom-call | flops 2415919104 | bytes 4194304 | tf_op jit(solution)/shard_map/first_half/pallas_call | solution.py:201
  42.3 1.9 %collective-permute-start.5 = (bf16[3072,128]{1,0:T(8,128)(2,1)S(1)}, bf16[3072,128]{1,0:T(8,128)(2,1)S(1)}, u32[]{:S(2)}, u32[]{:S(2)}) collective-permute-start(bf16[3072,128]{1,0:T(8,128)(2,1)S(1)} %get-tuple-element.40), channel_id=1, source_target_pairs={{1,9},{10,2},{3,11},{12,4},{2,1},{4,3},{17,25},{26,18},{19,27},{28... | collective-permute-start | bytes 2359304 | tf_op jit(solution)/shard_map/ppermute | solution.py:349
  44.4 5.7 %first_last.1 = (bf16[9,128,128]{2,1,0:T(8,128)(2,1)S(1)}, bf16[9,128,128]{2,1,0:T(8,128)(2,1)S(1)}, bf16[9,128,128]{2,1,0:T(8,128)(2,1)S(1)}) custom-call(s32[14]{0:T(128)S(1)} %pad_add_fusion.1.switch_ref, bf16[128,8192]{1,0:T(8,128)(2,1)S(1)} %get-tuple-element.29.plain_ref, bf16[128,8192]{1,0:T(8,128)(2,1)S(1)} %copy-done.1, ...), custom_call_target="tpu_custom_call" | custom-call | flops 2415919104 | bytes 4194304 | tf_op jit(solution)/shard_map/first_last/pallas_call | solution.py:201
  50.0 1.4 %collective-permute-start.8 = (bf16[9,128,128]{2,1,0:T(8,128)(2,1)S(1)}, bf16[9,128,128]{2,1,0:T(8,128)(2,1)}, u32[]{:S(2)}, u32[]{:S(2)}) collective-permute-start(bf16[9,128,128]{2,1,0:T(8,128)(2,1)S(1)} %get-tuple-element.43), channel_id=1, source_target_pairs={{0,7},{7,15},{16,23},{23,31}} | collective-permute-start | bytes 884744 | tf_op jit(solution)/shard_map/ppermute | solution.py:351
  51.5 6.1 %second_part.1.rest_0_ = f32[1152,128]{1,0:T(8,128)S(1)} custom-call(s32[6]{0:T(128)S(1)} %pad_add_fusion.switch_ref, bf16[128,8192]{1,0:T(8,128)(2,1)S(1)} %get-tuple-element.29.plain_ref, bf16[128,8192]{1,0:T(8,128)(2,1)S(1)} %copy-done.1, bf16[9,8192]{1,0:T(8,128)(2,1)S(1)} %pad_maximum_fusion.coeff_ref, bf16[5120,128]{1,0:T(8,128)(2,1)} %collective-permute-done.6.partner_ref), custom_call_target="tpu_custom_call" | custom-call | flops 1509949440 | bytes 3932160 | tf_op jit(solution)/shard_map/second_part/pallas_call | solution.py:278
  57.5 3.3 %second_last.1 = (bf16[9,128,128]{2,1,0:T(8,128)(2,1)S(1)}, bf16[9,128,128]{2,1,0:T(8,128)(2,1)S(1)}, bf16[9,128,128]{2,1,0:T(8,128)(2,1)S(1)}) custom-call(s32[6]{0:T(128)S(1)} %pad_add_fusion.switch_ref, bf16[128,8192]{1,0:T(8,128)(2,1)S(1)} %get-tuple-element.29.plain_ref, bf16[128,8192]{1,0:T(8,128)(2,1)S(1)} %copy-done.1, ...), custom_call_target="tpu_custom_call" | custom-call | flops 905969664 | bytes 2359296 | tf_op jit(solution)/shard_map/second_last/pallas_call | solution.py:278
  60.9 1.9 %collective-permute-start.7 = (bf16[9,128,128]{2,1,0:T(8,128)(2,1)S(1)}, bf16[9,128,128]{2,1,0:T(8,128)(2,1)S(1)}, u32[]{:S(2)}, u32[]{:S(2)}) collective-permute-start(bf16[9,128,128]{2,1,0:T(8,128)(2,1)S(1)} %get-tuple-element.45), channel_id=1, source_target_pairs={{0,8},{13,5},{14,6},{7,15},{9,1},{2,10},{11,3},{4,12},{1,0},{16,24... | collective-permute-start | bytes 884744 | tf_op jit(solution)/shard_map/ppermute | solution.py:359
  62.9 6.4 %collective-permute-done.7 = bf16[9,128,128]{2,1,0:T(8,128)(2,1)S(1)} collective-permute-done((bf16[9,128,128]{2,1,0:T(8,128)(2,1)S(1)}, bf16[9,128,128]{2,1,0:T(8,128)(2,1)S(1)}, u32[]{:S(2)}, u32[]{:S(2)}) %collective-permute-start.7) | collective-permute-done | bytes 294944 | tf_op jit(solution)/shard_map/ppermute | solution.py:359
  69.2 0.9 %select_bitcast_fusion = (bf16[1,9,128,128]{3,2,1,0:T(8,128)(2,1)}, bf16[1,9,128,128]{3,2,1,0:T(8,128)(2,1)}) fusion(bf16[9,128,128]{2,1,0:T(8,128)(2,1)S(1)} %collective-permute-done.7, bf16[9,128,128]{2,1,0:T(8,128)(2,1)S(1)} %get-tuple-element.47, pred[]{:T(512)S(6)} %or.59, bf16[9,128,128]{2,1,0:T(8,128)(2,1)} %collective-permute-done.8, ...), kind=kLoop, calls=%fused_computation | loop fusion | flops 442368 | bytes 1769475 | tf_op jit(solution)/shard_map/broadcast_in_dim | solution.py:363
  (25 shorter events, 0.5 us)
Async XLA Ops:
  0.6 25.2 %collective-permute-start.3 = (bf16[8192,128]{1,0:T(8,128)(2,1)}, bf16[8192,128]{1,0:T(8,128)(2,1)}, u32[]{:S(2)}, u32[]{:S(2)}) collective-permute-start(bf16[8192,128]{1,0:T(8,128)(2,1)} %bitcast.15), channel_id=1, source_target_pairs={{3,2},{5,4},{6,5},{9,8},{10,9},{11,10},{12,11},{13,12},{14,13},{15... | collective-permute-start | bytes 6291464 | tf_op jit(solution)/shard_map/ppermute | solution.py:328
  2.6 23.2 %collective-permute-start.4 = (bf16[8192,128]{1,0:T(8,128)(2,1)}, bf16[8192,128]{1,0:T(8,128)(2,1)}, u32[]{:S(2)}, u32[]{:S(2)}) collective-permute-start(bf16[8192,128]{1,0:T(8,128)(2,1)} %bitcast.16), channel_id=1, source_target_pairs={{8,0},{5,13},{6,14},{15,7},{0,1},{7,6},{24,16},{21,29},{22,30},{31... | collective-permute-start | bytes 6291464 | tf_op jit(solution)/shard_map/ppermute | solution.py:329
  3.9 29.7 %collective-permute-start.1 = (s32[1,4]{1,0:T(1,128)}, s32[1,4]{1,0:T(1,128)S(1)}, u32[]{:S(2)}, u32[]{:S(2)}) collective-permute-start(s32[1,4]{1,0:T(1,128)} %param.3), channel_id=1, source_target_pairs={{3,2},{5,4},{6,5},{9,8},{10,9},{11,10},{12,11},{13,12},{14,13},{15... | collective-permute-start | bytes 56 | tf_op jit(solution)/shard_map/ppermute | solution.py:334
  4.6 29.0 %collective-permute-start.2 = (s32[1,4]{1,0:T(1,128)}, s32[1,4]{1,0:T(1,128)S(1)}, u32[]{:S(2)}, u32[]{:S(2)}) collective-permute-start(s32[1,4]{1,0:T(1,128)} %param.3), channel_id=1, source_target_pairs={{8,0},{5,13},{6,14},{15,7},{0,1},{7,6},{24,16},{21,29},{22,30},{31... | collective-permute-start | bytes 56 | tf_op jit(solution)/shard_map/ppermute | solution.py:333
  5.9 38.4 %collective-permute-start = (s32[1,4]{1,0:T(1,128)}, s32[1,4]{1,0:T(1,128)S(1)}, u32[]{:S(2)}, u32[]{:S(2)}) collective-permute-start(s32[1,4]{1,0:T(1,128)} %param.3), channel_id=1, source_target_pairs={{1,9},{10,2},{3,11},{12,4},{2,1},{4,3},{17,25},{26,18},{19,27},{28... | collective-permute-start | bytes 56 | tf_op jit(solution)/shard_map/ppermute | solution.py:335
  16.4 1.6 %copy-start.2 = (bf16[1024,2,4,128]{3,2,1,0:T(4,128)(2,1)S(1)}, bf16[1024,2,4,128]{3,2,1,0:T(4,128)(2,1)}, u32[]{:S(2)}) copy-start(bf16[1024,2,4,128]{3,2,1,0:T(4,128)(2,1)} %param.2) | copy-start | bytes 6291460
  21.1 1.3 %copy-start = (bf16[128,8192]{1,0:T(8,128)(2,1)}, bf16[128,8192]{1,0:T(8,128)(2,1)S(1)}, u32[]{:S(2)}) copy-start(bf16[128,8192]{1,0:T(8,128)(2,1)S(1)} %get-tuple-element.30.swapped_ref) | copy-start | bytes 6291460
  22.5 11.1 %copy-start.5 = (s32[1,4]{1,0:T(1,128)S(1)}, s32[1,4]{1,0:T(1,128)}, u32[]{:S(2)}) copy-start(s32[1,4]{1,0:T(1,128)} %param.3) | copy-start | bytes 52
  22.8 1.1 %copy-start.4 = (bf16[5120,128]{1,0:T(8,128)(2,1)}, bf16[5120,128]{1,0:T(8,128)(2,1)S(1)}, u32[]{:S(2)}) copy-start(bf16[5120,128]{1,0:T(8,128)(2,1)S(1)} %get-tuple-element.41) | copy-start | bytes 3932164
  25.8 25.7 %collective-permute-start.6 = (bf16[5120,128]{1,0:T(8,128)(2,1)}, bf16[5120,128]{1,0:T(8,128)(2,1)}, u32[]{:S(2)}, u32[]{:S(2)}) collective-permute-start(bf16[5120,128]{1,0:T(8,128)(2,1)} %copy-done.4), channel_id=1, source_target_pairs={{1,9},{10,2},{3,11},{12,4},{2,1},{4,3},{17,25},{26,18},{19,27},{28... | collective-permute-start | bytes 3932168 | tf_op jit(solution)/shard_map/ppermute | solution.py:345
  33.7 1.6 %copy-start.1 = (bf16[128,8192]{1,0:T(8,128)(2,1)S(1)}, bf16[128,8192]{1,0:T(8,128)(2,1)}, u32[]{:S(2)}) copy-start(bf16[128,8192]{1,0:T(8,128)(2,1)} %copy-done) | copy-start | bytes 6291460
  35.3 1.6 %copy-start.3 = (bf16[1024,2,4,128]{3,2,1,0:T(4,128)(2,1)S(1)}, bf16[1024,2,4,128]{3,2,1,0:T(4,128)(2,1)}, u32[]{:S(2)}) copy-start(bf16[1024,2,4,128]{3,2,1,0:T(4,128)(2,1)} %param.2) | copy-start | bytes 6291460
  42.3 15.2 %collective-permute-start.5 = (bf16[3072,128]{1,0:T(8,128)(2,1)S(1)}, bf16[3072,128]{1,0:T(8,128)(2,1)S(1)}, u32[]{:S(2)}, u32[]{:S(2)}) collective-permute-start(bf16[3072,128]{1,0:T(8,128)(2,1)S(1)} %get-tuple-element.40), channel_id=1, source_target_pairs={{1,9},{10,2},{3,11},{12,4},{2,1},{4,3},{17,25},{26,18},{19,27},{28... | collective-permute-start | bytes 2359304 | tf_op jit(solution)/shard_map/ppermute | solution.py:349
  50.0 12.8 %collective-permute-start.8 = (bf16[9,128,128]{2,1,0:T(8,128)(2,1)S(1)}, bf16[9,128,128]{2,1,0:T(8,128)(2,1)}, u32[]{:S(2)}, u32[]{:S(2)}) collective-permute-start(bf16[9,128,128]{2,1,0:T(8,128)(2,1)S(1)} %get-tuple-element.43), channel_id=1, source_target_pairs={{0,7},{7,15},{16,23},{23,31}} | collective-permute-start | bytes 884744 | tf_op jit(solution)/shard_map/ppermute | solution.py:351
  60.9 8.4 %collective-permute-start.7 = (bf16[9,128,128]{2,1,0:T(8,128)(2,1)S(1)}, bf16[9,128,128]{2,1,0:T(8,128)(2,1)S(1)}, u32[]{:S(2)}, u32[]{:S(2)}) collective-permute-start(bf16[9,128,128]{2,1,0:T(8,128)(2,1)S(1)} %get-tuple-element.45), channel_id=1, source_target_pairs={{0,8},{13,5},{14,6},{7,15},{9,1},{2,10},{11,3},{4,12},{1,0},{16,24... | collective-permute-start | bytes 884744 | tf_op jit(solution)/shard_map/ppermute | solution.py:359

commit v20 on v19

--- a/solution.py
+++ b/solution.py
@@ -130,9 +130,11 @@
     cols = plain_ref.shape[0]
     near_mirrored, special = switch_ref[0], switch_ref[1]
     if last:
-        acc_in, _, near_out, far_out, back_out, acc, scaled, plain, swapped = rest
+        acc_in, _, near_out, far_out, back_out, acc, scaled, plain, swapped, own_rows, arrived = rest
     else:
-        acc, token_out, scaled, plain, swapped = rest
+        acc, token_out, scaled, plain, swapped, own_rows, arrived = rest
+    size = own_rows.shape[0]
+    begin = size if last else 0
 
     @pl.when(step == 0)
     def _():
@@ -146,6 +148,12 @@
     def _():
         plain[...], swapped[...] = plain_ref[...], swapped_ref[...]
 
+    @pl.when((special != 0) & (step == 0))
+    def _():
+        copy = pltpu.make_async_copy(own_ref.at[pl.ds(begin, size)], own_rows, arrived)
+        copy.start()
+        copy.wait()
+
     @pl.when(special != 0)
     def _():
         plain[...], swapped[...] = turned(first_ref[...])
@@ -154,7 +162,8 @@
     flags = [[switch_ref[2 + part * windows + w] for w in range(windows)] for part in range(3)]
     near_weights = [jnp.where(special != 0, first, own) * near for own, near, first in zip(*flags)]
     near = weigh(near_ref[...], near_weights)
-    far = weigh(jnp.where(special != 0, own_ref[...], first_ref[...]), [own * first for own, _, first in zip(*flags)])
+    own_tile = own_rows[pl.ds(pl.multiple_of(step * STEP, STEP), STEP), :]
+    far = weigh(jnp.where(special != 0, own_tile, first_ref[...]), [own * first for own, _, first in zip(*flags)])
     acc[...] += jnp.dot(scaled[...], jnp.concatenate([near, far], axis=1), preferred_element_type=jnp.float32)
 
     if last:
@@ -188,9 +197,10 @@
     token_spec = pl.BlockSpec(token.shape, lambda s, on: (0, 0))
     left = pl.BlockSpec((cols, STEP), lambda s, on: (0, (s + skip) * (1 - on[1])))
     right = pl.BlockSpec((STEP, cols), lambda s, on: (s + skip, 0))
-    right_special = pl.BlockSpec((STEP, cols), lambda s, on: ((s + skip) * on[1], 0))
-    in_specs = [left, left, pl.BlockSpec((LAGS, STEP), lambda s, on: (0, s + skip)), right, right, right_special]
+    in_specs = [left, left, pl.BlockSpec((LAGS, STEP), lambda s, on: (0, s + skip)), right, right,
+                pl.BlockSpec(memory_space=pltpu.HBM)]
     scratch = [pltpu.VMEM((LAGS * cols, STEP), jnp.bfloat16)] + [pltpu.VMEM((cols, STEP), jnp.bfloat16)] * 2
+    scratch += [pltpu.VMEM((steps * STEP, cols), jnp.bfloat16), pltpu.SemaphoreType.DMA(())]
     if earlier is None:
         out_shape, out_specs, earlier = [total, token], [total_spec, token_spec], []
     else:

time: 70.7 us -> 70.7 us (level)
  no operation moved by 1% of the time
where the time goes in v20:
time: 70.7 us; the launch traced here: 70.2 us
  starting transfers between devices  28.5 us (40%)
  Pallas kernels  24 us (34%)
  local copies, waits for them, and re-layouts  7.16 us (10%)
  waiting for transfers between devices  6.41 us (9%)
  other arithmetic  3.15 us (4%)
  between operations  0.9 us (1%)
    pallas_call x2, Pallas kernels, first_sums(): pl.pallas_call(functools.partial(first_kernel, windows, bool(earlier)), g...  11.2 us
    ppermute x1, starting transfers between devices, local(): second_flags = lax.ppermute(quality, 'chan', second_pairs)[0]  10.5 us
    pallas_call x2, Pallas kernels, second_sums(): pl.pallas_call(functools.partial(second_kernel, windows, not earlier), gr...  9.37 us
    ppermute x1, starting transfers between devices, local(): second_in = [lax.ppermute(first_part, 'chan', second_pairs)]  7.59 us
    unnamed x12, local copies, waits for them, and re-layouts  7.16 us
    ppermute x1, waiting for transfers between devices, local(): returned = lax.ppermute(back, 'chan', back_pairs)  6.39 us
    pallas_call x1, Pallas kernels, turn(): pl.pallas_call(turn_kernel, grid=(rows // STEP,), in_specs=[pl.BlockSpec(...  3.15 us
    ppermute x1, starting transfers between devices, local(): near_in = lax.ppermute(block, 'chan', near_pairs)  2 us
  transfers between devices with their start and end apart: 9, of which 1 were waited for; matrix products, arithmetic and copies ran while one was open for 3% of the time, Pallas kernels for 34%

profile of v20, /device:TPU:1, one launch (start us, length us, event | category | flops | bytes accessed | tf_op | source)
XLA Modules:
  0.0 70.2 jit_solution(10195133865135869434)
XLA Ops:
  0.6 2.0 %collective-permute-start.3 = (bf16[8192,128]{1,0:T(8,128)(2,1)}, bf16[8192,128]{1,0:T(8,128)(2,1)}, u32[]{:S(2)}, u32[]{:S(2)}) collective-permute-start(bf16[8192,128]{1,0:T(8,128)(2,1)} %bitcast.15), channel_id=1, source_target_pairs={{3,2},{5,4},{6,5},{9,8},{10,9},{11,10},{12,11},{13,12},{14,13},{15... | collective-permute-start | bytes 6291464 | tf_op jit(solution)/shard_map/ppermute | solution.py:338
  2.6 1.3 %collective-permute-start.4 = (bf16[8192,128]{1,0:T(8,128)(2,1)}, bf16[8192,128]{1,0:T(8,128)(2,1)}, u32[]{:S(2)}, u32[]{:S(2)}) collective-permute-start(bf16[8192,128]{1,0:T(8,128)(2,1)} %bitcast.16), channel_id=1, source_target_pairs={{8,0},{5,13},{6,14},{15,7},{0,1},{7,6},{24,16},{21,29},{22,30},{31... | collective-permute-start | bytes 6291464 | tf_op jit(solution)/shard_map/ppermute | solution.py:339
  3.9 0.7 collective-permute-start.1
  4.6 1.3 %collective-permute-start.2 = (s32[1,4]{1,0:T(1,128)}, s32[1,4]{1,0:T(1,128)S(1)}, u32[]{:S(2)}, u32[]{:S(2)}) collective-permute-start(s32[1,4]{1,0:T(1,128)} %param.3), channel_id=1, source_target_pairs={{8,0},{5,13},{6,14},{15,7},{0,1},{7,6},{24,16},{21,29},{22,30},{31... | collective-permute-start | bytes 56 | tf_op jit(solution)/shard_map/ppermute | solution.py:343
  5.9 10.5 %collective-permute-start = (s32[1,4]{1,0:T(1,128)}, s32[1,4]{1,0:T(1,128)S(1)}, u32[]{:S(2)}, u32[]{:S(2)}) collective-permute-start(s32[1,4]{1,0:T(1,128)} %param.3), channel_id=1, source_target_pairs={{1,9},{10,2},{3,11},{12,4},{2,1},{4,3},{17,25},{26,18},{19,27},{28... | collective-permute-start | bytes 56 | tf_op jit(solution)/shard_map/ppermute | solution.py:345
  16.4 1.6 %copy-done.2 = bf16[1024,2,4,128]{3,2,1,0:T(4,128)(2,1)S(1)} copy-done((bf16[1024,2,4,128]{3,2,1,0:T(4,128)(2,1)S(1)}, bf16[1024,2,4,128]{3,2,1,0:T(4,128)(2,1)}, u32[]{:S(2)}) %copy-start.2) | copy-done | bytes 2097176
  18.0 3.2 %turn.1 = (bf16[128,8192]{1,0:T(8,128)(2,1)S(1)}, bf16[128,8192]{1,0:T(8,128)(2,1)S(1)}) custom-call(bf16[8192,128]{1,0:T(8,128)(2,1)S(1)} %bitcast.17), custom_call_target="tpu_custom_call" | custom-call | bytes 6291456 | tf_op jit(solution)/shard_map/turn/pallas_call | solution.py:85
  21.1 1.3 %copy-done = bf16[128,8192]{1,0:T(8,128)(2,1)} copy-done((bf16[128,8192]{1,0:T(8,128)(2,1)}, bf16[128,8192]{1,0:T(8,128)(2,1)S(1)}, u32[]{:S(2)}) %copy-start) | copy-done | bytes 2097176
  22.5 0.3 split.1
  22.8 1.0 %copy-done.4 = bf16[5120,128]{1,0:T(8,128)(2,1)} copy-done((bf16[5120,128]{1,0:T(8,128)(2,1)}, bf16[5120,128]{1,0:T(8,128)(2,1)S(1)}, u32[]{:S(2)}) %copy-start.4) | copy-done | bytes 1310744
  23.9 0.9 %multiply_convert_fusion = (bf16[5,8192]{1,0:T(8,128)(2,1)S(1)}, f32[5,8192]{1,0:T(8,128)S(1)}) fusion(f32[8192]{0:T(1024)S(1)} %fusion.9, f32[5]{0:T(128)S(1)} %iota_multiply_fusion), kind=kLoop, calls=%fused_computation.4 | loop fusion | flops 122880 | bytes 278548 | tf_op jit(solution)/shard_map/convert
  24.8 0.9 %fusion.2 = bf16[4,8192]{1,0:T(4,128)(2,1)S(1)} fusion(f32[5,8192]{1,0:T(8,128)S(1)} %get-tuple-element.51, f32[8192]{0:T(1024)S(1)} %select_multiply_fusion), kind=kLoop, calls=%fused_computation.8 | loop fusion | flops 98304 | bytes 229376 | tf_op jit(solution)/shard_map/convert.1
  25.8 7.6 %collective-permute-start.6 = (bf16[5120,128]{1,0:T(8,128)(2,1)}, bf16[5120,128]{1,0:T(8,128)(2,1)}, u32[]{:S(2)}, u32[]{:S(2)}) collective-permute-start(bf16[5120,128]{1,0:T(8,128)(2,1)} %copy-done.4), channel_id=1, source_target_pairs={{1,9},{10,2},{3,11},{12,4},{2,1},{4,3},{17,25},{26,18},{19,27},{28... | collective-permute-start | bytes 3932168 | tf_op jit(solution)/shard_map/ppermute | solution.py:355
  33.7 1.6 %copy-done.1 = bf16[128,8192]{1,0:T(8,128)(2,1)S(1)} copy-done((bf16[128,8192]{1,0:T(8,128)(2,1)S(1)}, bf16[128,8192]{1,0:T(8,128)(2,1)}, u32[]{:S(2)}) %copy-start.1) | copy-done | bytes 2097176
  35.3 1.6 %copy-done.3 = bf16[1024,2,4,128]{3,2,1,0:T(4,128)(2,1)S(1)} copy-done((bf16[1024,2,4,128]{3,2,1,0:T(4,128)(2,1)S(1)}, bf16[1024,2,4,128]{3,2,1,0:T(4,128)(2,1)}, u32[]{:S(2)}) %copy-start.3) | copy-done | bytes 2097176
  36.8 5.5 %first_half.1 = (f32[1152,256]{1,0:T(8,128)S(1)}, f32[8,128]{1,0:T(8,128)S(1)}) custom-call(s32[14]{0:T(128)S(1)} %pad_add_fusion.1.switch_ref, bf16[128,8192]{1,0:T(8,128)(2,1)S(1)} %get-tuple-element.29.plain_ref, bf16[128,8192]{1,0:T(8,128)(2,1)S(1)} %copy-done.1, bf16[9,8192]{1,0:T(8,128)(2,1)S(1)} %pad_maximum_fusion.coeff_ref, ...), custom_call_target="tpu_custom_call" | custom-call | flops 2415919104 | bytes 4194304 | tf_op jit(solution)/shard_map/first_half/pallas_call | solution.py:211
  42.3 1.9 %collective-permute-start.5 = (bf16[3072,128]{1,0:T(8,128)(2,1)S(1)}, bf16[3072,128]{1,0:T(8,128)(2,1)S(1)}, u32[]{:S(2)}, u32[]{:S(2)}) collective-permute-start(bf16[3072,128]{1,0:T(8,128)(2,1)S(1)} %get-tuple-element.40), channel_id=1, source_target_pairs={{1,9},{10,2},{3,11},{12,4},{2,1},{4,3},{17,25},{26,18},{19,27},{28... | collective-permute-start | bytes 2359304 | tf_op jit(solution)/shard_map/ppermute | solution.py:359
  44.4 5.7 %first_last.1 = (bf16[9,128,128]{2,1,0:T(8,128)(2,1)S(1)}, bf16[9,128,128]{2,1,0:T(8,128)(2,1)S(1)}, bf16[9,128,128]{2,1,0:T(8,128)(2,1)S(1)}) custom-call(s32[14]{0:T(128)S(1)} %pad_add_fusion.1.switch_ref, bf16[128,8192]{1,0:T(8,128)(2,1)S(1)} %get-tuple-element.29.plain_ref, bf16[128,8192]{1,0:T(8,128)(2,1)S(1)} %copy-done.1, ...), custom_call_target="tpu_custom_call" | custom-call | flops 2415919104 | bytes 4194304 | tf_op jit(solution)/shard_map/first_last/pallas_call | solution.py:211
  50.1 1.4 %collective-permute-start.8 = (bf16[9,128,128]{2,1,0:T(8,128)(2,1)S(1)}, bf16[9,128,128]{2,1,0:T(8,128)(2,1)}, u32[]{:S(2)}, u32[]{:S(2)}) collective-permute-start(bf16[9,128,128]{2,1,0:T(8,128)(2,1)S(1)} %get-tuple-element.43), channel_id=1, source_target_pairs={{0,7},{7,15},{16,23},{23,31}} | collective-permute-start | bytes 884744 | tf_op jit(solution)/shard_map/ppermute | solution.py:361
  51.5 6.1 %second_part.1.rest_0_ = f32[1152,128]{1,0:T(8,128)S(1)} custom-call(s32[6]{0:T(128)S(1)} %pad_add_fusion.switch_ref, bf16[128,8192]{1,0:T(8,128)(2,1)S(1)} %get-tuple-element.29.plain_ref, bf16[128,8192]{1,0:T(8,128)(2,1)S(1)} %copy-done.1, bf16[9,8192]{1,0:T(8,128)(2,1)S(1)} %pad_maximum_fusion.coeff_ref, bf16[5120,128]{1,0:T(8,128)(2,1)} %collective-permute-done.6.partner_ref), custom_call_target="tpu_custom_call" | custom-call | flops 1509949440 | bytes 3932160 | tf_op jit(solution)/shard_map/second_part/pallas_call | solution.py:288
  57.6 3.3 %second_last.1 = (bf16[9,128,128]{2,1,0:T(8,128)(2,1)S(1)}, bf16[9,128,128]{2,1,0:T(8,128)(2,1)S(1)}, bf16[9,128,128]{2,1,0:T(8,128)(2,1)S(1)}) custom-call(s32[6]{0:T(128)S(1)} %pad_add_fusion.switch_ref, bf16[128,8192]{1,0:T(8,128)(2,1)S(1)} %get-tuple-element.29.plain_ref, bf16[128,8192]{1,0:T(8,128)(2,1)S(1)} %copy-done.1, ...), custom_call_target="tpu_custom_call" | custom-call | flops 905969664 | bytes 2359296 | tf_op jit(solution)/shard_map/second_last/pallas_call | solution.py:288
  60.9 1.9 %collective-permute-start.7 = (bf16[9,128,128]{2,1,0:T(8,128)(2,1)S(1)}, bf16[9,128,128]{2,1,0:T(8,128)(2,1)S(1)}, u32[]{:S(2)}, u32[]{:S(2)}) collective-permute-start(bf16[9,128,128]{2,1,0:T(8,128)(2,1)S(1)} %get-tuple-element.45), channel_id=1, source_target_pairs={{0,8},{13,5},{14,6},{7,15},{9,1},{2,10},{11,3},{4,12},{1,0},{16,24... | collective-permute-start | bytes 884744 | tf_op jit(solution)/shard_map/ppermute | solution.py:369
  62.9 6.4 %collective-permute-done.7 = bf16[9,128,128]{2,1,0:T(8,128)(2,1)S(1)} collective-permute-done((bf16[9,128,128]{2,1,0:T(8,128)(2,1)S(1)}, bf16[9,128,128]{2,1,0:T(8,128)(2,1)S(1)}, u32[]{:S(2)}, u32[]{:S(2)}) %collective-permute-start.7) | collective-permute-done | bytes 294944 | tf_op jit(solution)/shard_map/ppermute | solution.py:369
  69.3 0.9 %select_bitcast_fusion = (bf16[1,9,128,128]{3,2,1,0:T(8,128)(2,1)}, bf16[1,9,128,128]{3,2,1,0:T(8,128)(2,1)}) fusion(bf16[9,128,128]{2,1,0:T(8,128)(2,1)S(1)} %collective-permute-done.7, bf16[9,128,128]{2,1,0:T(8,128)(2,1)S(1)} %get-tuple-element.47, pred[]{:T(512)S(6)} %or.59, bf16[9,128,128]{2,1,0:T(8,128)(2,1)} %collective-permute-done.8, ...), kind=kLoop, calls=%fused_computation | loop fusion | flops 442368 | bytes 1769475 | tf_op jit(solution)/shard_map/broadcast_in_dim | solution.py:373
  (25 shorter events, 0.5 us)
Async XLA Ops:
  0.6 25.2 %collective-permute-start.3 = (bf16[8192,128]{1,0:T(8,128)(2,1)}, bf16[8192,128]{1,0:T(8,128)(2,1)}, u32[]{:S(2)}, u32[]{:S(2)}) collective-permute-start(bf16[8192,128]{1,0:T(8,128)(2,1)} %bitcast.15), channel_id=1, source_target_pairs={{3,2},{5,4},{6,5},{9,8},{10,9},{11,10},{12,11},{13,12},{14,13},{15... | collective-permute-start | bytes 6291464 | tf_op jit(solution)/shard_map/ppermute | solution.py:338
  2.6 23.2 %collective-permute-start.4 = (bf16[8192,128]{1,0:T(8,128)(2,1)}, bf16[8192,128]{1,0:T(8,128)(2,1)}, u32[]{:S(2)}, u32[]{:S(2)}) collective-permute-start(bf16[8192,128]{1,0:T(8,128)(2,1)} %bitcast.16), channel_id=1, source_target_pairs={{8,0},{5,13},{6,14},{15,7},{0,1},{7,6},{24,16},{21,29},{22,30},{31... | collective-permute-start | bytes 6291464 | tf_op jit(solution)/shard_map/ppermute | solution.py:339
  3.9 29.7 %collective-permute-start.1 = (s32[1,4]{1,0:T(1,128)}, s32[1,4]{1,0:T(1,128)S(1)}, u32[]{:S(2)}, u32[]{:S(2)}) collective-permute-start(s32[1,4]{1,0:T(1,128)} %param.3), channel_id=1, source_target_pairs={{3,2},{5,4},{6,5},{9,8},{10,9},{11,10},{12,11},{13,12},{14,13},{15... | collective-permute-start | bytes 56 | tf_op jit(solution)/shard_map/ppermute | solution.py:344
  4.6 29.0 %collective-permute-start.2 = (s32[1,4]{1,0:T(1,128)}, s32[1,4]{1,0:T(1,128)S(1)}, u32[]{:S(2)}, u32[]{:S(2)}) collective-permute-start(s32[1,4]{1,0:T(1,128)} %param.3), channel_id=1, source_target_pairs={{8,0},{5,13},{6,14},{15,7},{0,1},{7,6},{24,16},{21,29},{22,30},{31... | collective-permute-start | bytes 56 | tf_op jit(solution)/shard_map/ppermute | solution.py:343
  5.9 38.4 %collective-permute-start = (s32[1,4]{1,0:T(1,128)}, s32[1,4]{1,0:T(1,128)S(1)}, u32[]{:S(2)}, u32[]{:S(2)}) collective-permute-start(s32[1,4]{1,0:T(1,128)} %param.3), channel_id=1, source_target_pairs={{1,9},{10,2},{3,11},{12,4},{2,1},{4,3},{17,25},{26,18},{19,27},{28... | collective-permute-start | bytes 56 | tf_op jit(solution)/shard_map/ppermute | solution.py:345
  16.4 1.6 %copy-start.2 = (bf16[1024,2,4,128]{3,2,1,0:T(4,128)(2,1)S(1)}, bf16[1024,2,4,128]{3,2,1,0:T(4,128)(2,1)}, u32[]{:S(2)}) copy-start(bf16[1024,2,4,128]{3,2,1,0:T(4,128)(2,1)} %param.2) | copy-start | bytes 6291460
  21.1 1.3 %copy-start = (bf16[128,8192]{1,0:T(8,128)(2,1)}, bf16[128,8192]{1,0:T(8,128)(2,1)S(1)}, u32[]{:S(2)}) copy-start(bf16[128,8192]{1,0:T(8,128)(2,1)S(1)} %get-tuple-element.30.swapped_ref) | copy-start | bytes 6291460
  22.5 11.1 %copy-start.5 = (s32[1,4]{1,0:T(1,128)S(1)}, s32[1,4]{1,0:T(1,128)}, u32[]{:S(2)}) copy-start(s32[1,4]{1,0:T(1,128)} %param.3) | copy-start | bytes 52
  22.8 1.1 %copy-start.4 = (bf16[5120,128]{1,0:T(8,128)(2,1)}, bf16[5120,128]{1,0:T(8,128)(2,1)S(1)}, u32[]{:S(2)}) copy-start(bf16[5120,128]{1,0:T(8,128)(2,1)S(1)} %get-tuple-element.41) | copy-start | bytes 3932164
  25.8 25.7 %collective-permute-start.6 = (bf16[5120,128]{1,0:T(8,128)(2,1)}, bf16[5120,128]{1,0:T(8,128)(2,1)}, u32[]{:S(2)}, u32[]{:S(2)}) collective-permute-start(bf16[5120,128]{1,0:T(8,128)(2,1)} %copy-done.4), channel_id=1, source_target_pairs={{1,9},{10,2},{3,11},{12,4},{2,1},{4,3},{17,25},{26,18},{19,27},{28... | collective-permute-start | bytes 3932168 | tf_op jit(solution)/shard_map/ppermute | solution.py:355
  33.7 1.6 %copy-start.1 = (bf16[128,8192]{1,0:T(8,128)(2,1)S(1)}, bf16[128,8192]{1,0:T(8,128)(2,1)}, u32[]{:S(2)}) copy-start(bf16[128,8192]{1,0:T(8,128)(2,1)} %copy-done) | copy-start | bytes 6291460
  35.3 1.6 %copy-start.3 = (bf16[1024,2,4,128]{3,2,1,0:T(4,128)(2,1)S(1)}, bf16[1024,2,4,128]{3,2,1,0:T(4,128)(2,1)}, u32[]{:S(2)}) copy-start(bf16[1024,2,4,128]{3,2,1,0:T(4,128)(2,1)} %param.2) | copy-start | bytes 6291460
  42.3 15.2 %collective-permute-start.5 = (bf16[3072,128]{1,0:T(8,128)(2,1)S(1)}, bf16[3072,128]{1,0:T(8,128)(2,1)S(1)}, u32[]{:S(2)}, u32[]{:S(2)}) collective-permute-start(bf16[3072,128]{1,0:T(8,128)(2,1)S(1)} %get-tuple-element.40), channel_id=1, source_target_pairs={{1,9},{10,2},{3,11},{12,4},{2,1},{4,3},{17,25},{26,18},{19,27},{28... | collective-permute-start | bytes 2359304 | tf_op jit(solution)/shard_map/ppermute | solution.py:359
  50.1 12.8 %collective-permute-start.8 = (bf16[9,128,128]{2,1,0:T(8,128)(2,1)S(1)}, bf16[9,128,128]{2,1,0:T(8,128)(2,1)}, u32[]{:S(2)}, u32[]{:S(2)}) collective-permute-start(bf16[9,128,128]{2,1,0:T(8,128)(2,1)S(1)} %get-tuple-element.43), channel_id=1, source_target_pairs={{0,7},{7,15},{16,23},{23,31}} | collective-permute-start | bytes 884744 | tf_op jit(solution)/shard_map/ppermute | solution.py:361
  60.9 8.4 %collective-permute-start.7 = (bf16[9,128,128]{2,1,0:T(8,128)(2,1)S(1)}, bf16[9,128,128]{2,1,0:T(8,128)(2,1)S(1)}, u32[]{:S(2)}, u32[]{:S(2)}) collective-permute-start(bf16[9,128,128]{2,1,0:T(8,128)(2,1)S(1)} %get-tuple-element.45), channel_id=1, source_target_pairs={{0,8},{13,5},{14,6},{7,15},{9,1},{2,10},{11,3},{4,12},{1,0},{16,24... | collective-permute-start | bytes 884744 | tf_op jit(solution)/shard_map/ppermute | solution.py:369

commit v21 on v19

--- a/solution.py
+++ b/solution.py
@@ -125,14 +125,14 @@
     return x * weights.reshape(rows, cols)
 
 
-def first_kernel(windows, last, switch_ref, plain_ref, swapped_ref, coeff_ref, near_ref, first_ref, own_ref, *rest):
+def first_kernel(windows, last, switch_ref, plain_ref, swapped_ref, coeff_ref, near_ref, first_ref, *rest):
     step = pl.program_id(0)
     cols = plain_ref.shape[0]
     near_mirrored, special = switch_ref[0], switch_ref[1]
     if last:
-        acc_in, _, near_out, far_out, back_out, acc, scaled, plain, swapped = rest
+        acc_in, _, near_out, far_out, back_out, acc, scaled, plain, swapped, right = rest
     else:
-        acc, token_out, scaled, plain, swapped = rest
+        acc, token_out, scaled, plain, swapped, right = rest
 
     @pl.when(step == 0)
     def _():
@@ -145,16 +145,19 @@
     @pl.when(special == 0)
     def _():
         plain[...], swapped[...] = plain_ref[...], swapped_ref[...]
+        right[...] = first_ref[...]
 
     @pl.when(special != 0)
     def _():
         plain[...], swapped[...] = turned(first_ref[...])
+        for t in range(0, STEP, cols):
+            right[t:t + cols, :] = plain_ref[:, t:t + cols].T
 
     scale(scaled, plain[...], swapped[...], coeff_ref)
     flags = [[switch_ref[2 + part * windows + w] for w in range(windows)] for part in range(3)]
     near_weights = [jnp.where(special != 0, first, own) * near for own, near, first in zip(*flags)]
     near = weigh(near_ref[...], near_weights)
-    far = weigh(jnp.where(special != 0, own_ref[...], first_ref[...]), [own * first for own, _, first in zip(*flags)])
+    far = weigh(right[...], [own * first for own, _, first in zip(*flags)])
     acc[...] += jnp.dot(scaled[...], jnp.concatenate([near, far], axis=1), preferred_element_type=jnp.float32)
 
     if last:
@@ -176,8 +179,8 @@
             pl.when(near_mirrored != 0)(lambda: write_lags(near_out, acc, near_at, cols, True))
 
 
-def first_sums(switch, own, coeffs, near_in, first_in, block, earlier=None):
-    rows, cols = block.shape
+def first_sums(switch, own, coeffs, near_in, first_in, earlier=None):
+    rows, cols = near_in.shape
     steps = rows // STEP // 2
     skip = 0 if earlier is None else steps
     windows = (switch.shape[0] - 2) // 3
@@ -186,11 +189,11 @@
     total_spec = pl.BlockSpec(total.shape, lambda s, on: (0, 0))
     token = jax.ShapeDtypeStruct((8, cols), jnp.float32)
     token_spec = pl.BlockSpec(token.shape, lambda s, on: (0, 0))
-    left = pl.BlockSpec((cols, STEP), lambda s, on: (0, (s + skip) * (1 - on[1])))
+    left = pl.BlockSpec((cols, STEP), lambda s, on: (0, s + skip))
     right = pl.BlockSpec((STEP, cols), lambda s, on: (s + skip, 0))
-    right_special = pl.BlockSpec((STEP, cols), lambda s, on: ((s + skip) * on[1], 0))
-    in_specs = [left, left, pl.BlockSpec((LAGS, STEP), lambda s, on: (0, s + skip)), right, right, right_special]
+    in_specs = [left, left, pl.BlockSpec((LAGS, STEP), lambda s, on: (0, s + skip)), right, right]
     scratch = [pltpu.VMEM((LAGS * cols, STEP), jnp.bfloat16)] + [pltpu.VMEM((cols, STEP), jnp.bfloat16)] * 2
+    scratch += [pltpu.VMEM((STEP, cols), jnp.bfloat16)]
     if earlier is None:
         out_shape, out_specs, earlier = [total, token], [total_spec, token_spec], []
     else:
@@ -213,7 +216,7 @@
             flops=2 * LAGS * cols * cols * rows, bytes_accessed=4 * rows * cols, transcendentals=0
         ),
         name="first_last" if earlier else "first_half",
-    )(switch, *own, coeffs, near_in, first_in, block, *earlier)
+    )(switch, *own, coeffs, near_in, first_in, *earlier)
 
 
 def second_kernel(windows, first, switch_ref, plain_ref, swapped_ref, coeff_ref, partner_ref, *rest):
@@ -334,16 +337,16 @@
     near_flags = lax.ppermute(quality, "chan", near_pairs)[0]
     second_flags = lax.ppermute(quality, "chan", second_pairs)[0]
     special = among([0, half - 1])
-    first_switch = switch(me == 0, special, quality[0], near_flags, first_flags)
     second_switch = switch(
         among([t for _, t in second_pairs]), among([t for _, t in late_near]), quality[0] * second_flags
     )
 
-    near_in, first_part, last_part, own, coeffs, first_in = lax.optimization_barrier(
-        (near_in, *parts, own, coeffs, first_in)
+    near_in, first_part, last_part, own, coeffs, first_in, near_flags, first_flags, second_flags = lax.optimization_barrier(
+        (near_in, *parts, own, coeffs, first_in, near_flags, first_flags, second_flags)
     )
     second_in = [lax.ppermute(first_part, "chan", second_pairs)]
-    operands = first_switch, own, coeffs, near_in, first_in, block
+    first_switch = switch(me == 0, special, quality[0], near_flags, first_flags)
+    operands = first_switch, own, coeffs, near_in, first_in
     total, token = first_sums(*operands)
     last_part, token = lax.optimization_barrier((last_part, token))
     second_in.append(lax.ppermute(last_part, "chan", second_pairs))

time: 70.7 us -> 70.4 us (level)
  local copies, waits for them, and re-layouts: 7.16 us -> 5.57 us
  waiting for transfers between devices: 6.41 us -> 7.81 us
    unnamed x12 -> x10, local copies, waits for them, and re-layouts: 7.16 us -> 5.57 us
    ppermute x1, waiting for transfers between devices: 0.01 us -> 1.41 us  [local(): second_in.append(lax.ppermute(last_part, 'chan', second_pairs))]
  transfers between devices with their start and end apart: 9 -> 9, of which waited for: 1 -> 2; matrix products, arithmetic and copies ran while one was open for 3% -> 3% of each run, Pallas kernels for 34% -> 34%
where the time goes in v21:
time: 70.4 us; the launch traced here: 69.9 us
  starting transfers between devices  28.5 us (40%)
  Pallas kernels  23.9 us (34%)
  waiting for transfers between devices  7.81 us (11%)
  local copies, waits for them, and re-layouts  5.57 us (8%)
  other arithmetic  3.15 us (4%)
  between operations  0.9 us (1%)
    pallas_call x2, Pallas kernels, first_sums(): pl.pallas_call(functools.partial(first_kernel, windows, bool(earlier)), g...  11.1 us
    ppermute x1, starting transfers between devices, local(): second_flags = lax.ppermute(quality, 'chan', second_pairs)[0]  10.5 us
    pallas_call x2, Pallas kernels, second_sums(): pl.pallas_call(functools.partial(second_kernel, windows, not earlier), gr...  9.37 us
    ppermute x1, starting transfers between devices, local(): second_in = [lax.ppermute(first_part, 'chan', second_pairs)]  7.59 us
    ppermute x1, waiting for transfers between devices, local(): returned = lax.ppermute(back, 'chan', back_pairs)  6.39 us
    unnamed x10, local copies, waits for them, and re-layouts  5.57 us
    pallas_call x1, Pallas kernels, turn(): pl.pallas_call(turn_kernel, grid=(rows // STEP,), in_specs=[pl.BlockSpec(...  3.15 us
    ppermute x1, starting transfers between devices, local(): near_in = lax.ppermute(block, 'chan', near_pairs)  2.01 us
  transfers between devices with their start and end apart: 9, of which 2 were waited for; matrix products, arithmetic and copies ran while one was open for 3% of the time, Pallas kernels for 34%

profile of v21, /device:TPU:1, one launch (start us, length us, event | category | flops | bytes accessed | tf_op | source)
XLA Modules:
  0.0 69.9 jit_solution(6392014371882342078)
XLA Ops:
  0.6 2.0 %collective-permute-start.1 = (bf16[8192,128]{1,0:T(8,128)(2,1)}, bf16[8192,128]{1,0:T(8,128)(2,1)}, u32[]{:S(2)}, u32[]{:S(2)}) collective-permute-start(bf16[8192,128]{1,0:T(8,128)(2,1)} %bitcast.15), channel_id=1, source_target_pairs={{3,2},{5,4},{6,5},{9,8},{10,9},{11,10},{12,11},{13,12},{14,13},{15... | collective-permute-start | bytes 6291464 | tf_op jit(solution)/shard_map/ppermute | solution.py:331
  2.6 1.3 %collective-permute-start.2 = (bf16[8192,128]{1,0:T(8,128)(2,1)}, bf16[8192,128]{1,0:T(8,128)(2,1)}, u32[]{:S(2)}, u32[]{:S(2)}) collective-permute-start(bf16[8192,128]{1,0:T(8,128)(2,1)} %bitcast.16), channel_id=1, source_target_pairs={{8,0},{5,13},{6,14},{15,7},{0,1},{7,6},{24,16},{21,29},{22,30},{31... | collective-permute-start | bytes 6291464 | tf_op jit(solution)/shard_map/ppermute | solution.py:332
  3.9 0.7 collective-permute-start.3
  4.6 1.3 %collective-permute-start.4 = (s32[1,4]{1,0:T(1,128)}, s32[1,4]{1,0:T(1,128)S(1)}, u32[]{:S(2)}, u32[]{:S(2)}) collective-permute-start(s32[1,4]{1,0:T(1,128)} %param.3), channel_id=1, source_target_pairs={{8,0},{5,13},{6,14},{15,7},{0,1},{7,6},{24,16},{21,29},{22,30},{31... | collective-permute-start | bytes 56 | tf_op jit(solution)/shard_map/ppermute | solution.py:336
  5.9 10.5 %collective-permute-start = (s32[1,4]{1,0:T(1,128)}, s32[1,4]{1,0:T(1,128)S(1)}, u32[]{:S(2)}, u32[]{:S(2)}) collective-permute-start(s32[1,4]{1,0:T(1,128)} %param.3), channel_id=1, source_target_pairs={{1,9},{10,2},{3,11},{12,4},{2,1},{4,3},{17,25},{26,18},{19,27},{28... | collective-permute-start | bytes 56 | tf_op jit(solution)/shard_map/ppermute | solution.py:338
  16.4 1.6 %copy-done.2 = bf16[1024,2,4,128]{3,2,1,0:T(4,128)(2,1)S(1)} copy-done((bf16[1024,2,4,128]{3,2,1,0:T(4,128)(2,1)S(1)}, bf16[1024,2,4,128]{3,2,1,0:T(4,128)(2,1)}, u32[]{:S(2)}) %copy-start.2) | copy-done | bytes 2097176
  18.0 3.2 %turn.1 = (bf16[128,8192]{1,0:T(8,128)(2,1)S(1)}, bf16[128,8192]{1,0:T(8,128)(2,1)S(1)}) custom-call(bf16[8192,128]{1,0:T(8,128)(2,1)S(1)} %bitcast.17), custom_call_target="tpu_custom_call" | custom-call | bytes 6291456 | tf_op jit(solution)/shard_map/turn/pallas_call | solution.py:85
  21.2 1.3 %copy-done = bf16[128,8192]{1,0:T(8,128)(2,1)} copy-done((bf16[128,8192]{1,0:T(8,128)(2,1)}, bf16[128,8192]{1,0:T(8,128)(2,1)S(1)}, u32[]{:S(2)}) %copy-start) | copy-done | bytes 2097176
  22.5 0.3 split.1
  22.8 1.0 %copy-done.3 = bf16[5120,128]{1,0:T(8,128)(2,1)} copy-done((bf16[5120,128]{1,0:T(8,128)(2,1)}, bf16[5120,128]{1,0:T(8,128)(2,1)S(1)}, u32[]{:S(2)}) %copy-start.3) | copy-done | bytes 1310744
  23.9 0.9 %multiply_convert_fusion = (bf16[5,8192]{1,0:T(8,128)(2,1)S(1)}, f32[5,8192]{1,0:T(8,128)S(1)}) fusion(f32[8192]{0:T(1024)S(1)} %fusion.9, f32[5]{0:T(128)S(1)} %iota_multiply_fusion), kind=kLoop, calls=%fused_computation.4 | loop fusion | flops 122880 | bytes 278548 | tf_op jit(solution)/shard_map/convert
  24.8 0.9 %fusion.2 = bf16[4,8192]{1,0:T(4,128)(2,1)S(1)} fusion(f32[5,8192]{1,0:T(8,128)S(1)} %get-tuple-element.55, f32[8192]{0:T(1024)S(1)} %select_multiply_fusion), kind=kLoop, calls=%fused_computation.8 | loop fusion | flops 98304 | bytes 229376 | tf_op jit(solution)/shard_map/convert.1
  25.8 7.6 %collective-permute-start.6 = (bf16[5120,128]{1,0:T(8,128)(2,1)}, bf16[5120,128]{1,0:T(8,128)(2,1)}, u32[]{:S(2)}, u32[]{:S(2)}) collective-permute-start(bf16[5120,128]{1,0:T(8,128)(2,1)} %copy-done.3), channel_id=1, source_target_pairs={{1,9},{10,2},{3,11},{12,4},{2,1},{4,3},{17,25},{26,18},{19,27},{28... | collective-permute-start | bytes 3932168 | tf_op jit(solution)/shard_map/ppermute | solution.py:347
  33.7 1.6 %copy-done.1 = bf16[128,8192]{1,0:T(8,128)(2,1)S(1)} copy-done((bf16[128,8192]{1,0:T(8,128)(2,1)S(1)}, bf16[128,8192]{1,0:T(8,128)(2,1)}, u32[]{:S(2)}) %copy-start.1) | copy-done | bytes 2097176
  35.3 5.5 %first_half.1 = (f32[1152,256]{1,0:T(8,128)S(1)}, f32[8,128]{1,0:T(8,128)S(1)}) custom-call(s32[14]{0:T(128)S(1)} %pad_add_fusion.1.switch_ref, bf16[128,8192]{1,0:T(8,128)(2,1)S(1)} %get-tuple-element.33.plain_ref, bf16[128,8192]{1,0:T(8,128)(2,1)S(1)} %copy-done.1, bf16[9,8192]{1,0:T(8,128)(2,1)S(1)} %pad_maximum_fusion.coeff_ref, ...), custom_call_target="tpu_custom_call" | custom-call | flops 2415919104 | bytes 4194304 | tf_op jit(solution)/shard_map/first_half/pallas_call | solution.py:204
  40.7 1.9 %collective-permute-start.5 = (bf16[3072,128]{1,0:T(8,128)(2,1)S(1)}, bf16[3072,128]{1,0:T(8,128)(2,1)S(1)}, u32[]{:S(2)}, u32[]{:S(2)}) collective-permute-start(bf16[3072,128]{1,0:T(8,128)(2,1)S(1)} %get-tuple-element.44), channel_id=1, source_target_pairs={{1,9},{10,2},{3,11},{12,4},{2,1},{4,3},{17,25},{26,18},{19,27},{28... | collective-permute-start | bytes 2359304 | tf_op jit(solution)/shard_map/ppermute | solution.py:352
  42.8 5.7 %first_last.1 = (bf16[9,128,128]{2,1,0:T(8,128)(2,1)S(1)}, bf16[9,128,128]{2,1,0:T(8,128)(2,1)S(1)}, bf16[9,128,128]{2,1,0:T(8,128)(2,1)S(1)}) custom-call(s32[14]{0:T(128)S(1)} %pad_add_fusion.1.switch_ref, bf16[128,8192]{1,0:T(8,128)(2,1)S(1)} %get-tuple-element.33.plain_ref, bf16[128,8192]{1,0:T(8,128)(2,1)S(1)} %copy-done.1, ...), custom_call_target="tpu_custom_call" | custom-call | flops 2415919104 | bytes 4194304 | tf_op jit(solution)/shard_map/first_last/pallas_call | solution.py:204
  48.4 1.4 %collective-permute-start.8 = (bf16[9,128,128]{2,1,0:T(8,128)(2,1)S(1)}, bf16[9,128,128]{2,1,0:T(8,128)(2,1)}, u32[]{:S(2)}, u32[]{:S(2)}) collective-permute-start(bf16[9,128,128]{2,1,0:T(8,128)(2,1)S(1)} %get-tuple-element.47), channel_id=1, source_target_pairs={{0,7},{7,15},{16,23},{23,31}} | collective-permute-start | bytes 884744 | tf_op jit(solution)/shard_map/ppermute | solution.py:354
  49.9 6.0 %second_part.1.rest_0_ = f32[1152,128]{1,0:T(8,128)S(1)} custom-call(s32[6]{0:T(128)S(1)} %pad_add_fusion.switch_ref, bf16[128,8192]{1,0:T(8,128)(2,1)S(1)} %get-tuple-element.33.plain_ref, bf16[128,8192]{1,0:T(8,128)(2,1)S(1)} %copy-done.1, bf16[9,8192]{1,0:T(8,128)(2,1)S(1)} %pad_maximum_fusion.coeff_ref, bf16[5120,128]{1,0:T(8,128)(2,1)} %collective-permute-done.6.partner_ref), custom_call_target="tpu_custom_call" | custom-call | flops 1509949440 | bytes 3932160 | tf_op jit(solution)/shard_map/second_part/pallas_call | solution.py:281
  55.9 1.4 %collective-permute-done.5.partner_ref = bf16[3072,128]{1,0:T(8,128)(2,1)S(1)} collective-permute-done((bf16[3072,128]{1,0:T(8,128)(2,1)S(1)}, bf16[3072,128]{1,0:T(8,128)(2,1)S(1)}, u32[]{:S(2)}, u32[]{:S(2)}) %collective-permute-start.5) | collective-permute-done | bytes 786464 | tf_op jit(solution)/shard_map/ppermute | solution.py:352
  57.3 3.3 %second_last.1 = (bf16[9,128,128]{2,1,0:T(8,128)(2,1)S(1)}, bf16[9,128,128]{2,1,0:T(8,128)(2,1)S(1)}, bf16[9,128,128]{2,1,0:T(8,128)(2,1)S(1)}) custom-call(s32[6]{0:T(128)S(1)} %pad_add_fusion.switch_ref, bf16[128,8192]{1,0:T(8,128)(2,1)S(1)} %get-tuple-element.33.plain_ref, bf16[128,8192]{1,0:T(8,128)(2,1)S(1)} %copy-done.1, ...), custom_call_target="tpu_custom_call" | custom-call | flops 905969664 | bytes 2359296 | tf_op jit(solution)/shard_map/second_last/pallas_call | solution.py:281
  60.6 1.9 %collective-permute-start.7 = (bf16[9,128,128]{2,1,0:T(8,128)(2,1)S(1)}, bf16[9,128,128]{2,1,0:T(8,128)(2,1)S(1)}, u32[]{:S(2)}, u32[]{:S(2)}) collective-permute-start(bf16[9,128,128]{2,1,0:T(8,128)(2,1)S(1)} %get-tuple-element.49), channel_id=1, source_target_pairs={{0,8},{13,5},{14,6},{7,15},{9,1},{2,10},{11,3},{4,12},{1,0},{16,24... | collective-permute-start | bytes 884744 | tf_op jit(solution)/shard_map/ppermute | solution.py:362
  62.6 6.4 %collective-permute-done.7 = bf16[9,128,128]{2,1,0:T(8,128)(2,1)S(1)} collective-permute-done((bf16[9,128,128]{2,1,0:T(8,128)(2,1)S(1)}, bf16[9,128,128]{2,1,0:T(8,128)(2,1)S(1)}, u32[]{:S(2)}, u32[]{:S(2)}) %collective-permute-start.7) | collective-permute-done | bytes 294944 | tf_op jit(solution)/shard_map/ppermute | solution.py:362
  69.0 0.9 %select_bitcast_fusion = (bf16[1,9,128,128]{3,2,1,0:T(8,128)(2,1)}, bf16[1,9,128,128]{3,2,1,0:T(8,128)(2,1)}) fusion(bf16[9,128,128]{2,1,0:T(8,128)(2,1)S(1)} %collective-permute-done.7, bf16[9,128,128]{2,1,0:T(8,128)(2,1)S(1)} %get-tuple-element.51, pred[]{:T(512)S(6)} %or.59, bf16[9,128,128]{2,1,0:T(8,128)(2,1)} %collective-permute-done.8, ...), kind=kLoop, calls=%fused_computation | loop fusion | flops 442368 | bytes 1769475 | tf_op jit(solution)/shard_map/broadcast_in_dim | solution.py:366
  (23 shorter events, 0.5 us)
Async XLA Ops:
  0.6 25.2 %collective-permute-start.1 = (bf16[8192,128]{1,0:T(8,128)(2,1)}, bf16[8192,128]{1,0:T(8,128)(2,1)}, u32[]{:S(2)}, u32[]{:S(2)}) collective-permute-start(bf16[8192,128]{1,0:T(8,128)(2,1)} %bitcast.15), channel_id=1, source_target_pairs={{3,2},{5,4},{6,5},{9,8},{10,9},{11,10},{12,11},{13,12},{14,13},{15... | collective-permute-start | bytes 6291464 | tf_op jit(solution)/shard_map/ppermute | solution.py:331
  2.6 23.2 %collective-permute-start.2 = (bf16[8192,128]{1,0:T(8,128)(2,1)}, bf16[8192,128]{1,0:T(8,128)(2,1)}, u32[]{:S(2)}, u32[]{:S(2)}) collective-permute-start(bf16[8192,128]{1,0:T(8,128)(2,1)} %bitcast.16), channel_id=1, source_target_pairs={{8,0},{5,13},{6,14},{15,7},{0,1},{7,6},{24,16},{21,29},{22,30},{31... | collective-permute-start | bytes 6291464 | tf_op jit(solution)/shard_map/ppermute | solution.py:332
  3.9 21.9 %collective-permute-start.3 = (s32[1,4]{1,0:T(1,128)}, s32[1,4]{1,0:T(1,128)S(1)}, u32[]{:S(2)}, u32[]{:S(2)}) collective-permute-start(s32[1,4]{1,0:T(1,128)} %param.3), channel_id=1, source_target_pairs={{3,2},{5,4},{6,5},{9,8},{10,9},{11,10},{12,11},{13,12},{14,13},{15... | collective-permute-start | bytes 56 | tf_op jit(solution)/shard_map/ppermute | solution.py:337
  4.6 21.2 %collective-permute-start.4 = (s32[1,4]{1,0:T(1,128)}, s32[1,4]{1,0:T(1,128)S(1)}, u32[]{:S(2)}, u32[]{:S(2)}) collective-permute-start(s32[1,4]{1,0:T(1,128)} %param.3), channel_id=1, source_target_pairs={{8,0},{5,13},{6,14},{15,7},{0,1},{7,6},{24,16},{21,29},{22,30},{31... | collective-permute-start | bytes 56 | tf_op jit(solution)/shard_map/ppermute | solution.py:336
  5.9 36.8 %collective-permute-start = (s32[1,4]{1,0:T(1,128)}, s32[1,4]{1,0:T(1,128)S(1)}, u32[]{:S(2)}, u32[]{:S(2)}) collective-permute-start(s32[1,4]{1,0:T(1,128)} %param.3), channel_id=1, source_target_pairs={{1,9},{10,2},{3,11},{12,4},{2,1},{4,3},{17,25},{26,18},{19,27},{28... | collective-permute-start | bytes 56 | tf_op jit(solution)/shard_map/ppermute | solution.py:338
  16.4 1.6 %copy-start.2 = (bf16[1024,2,4,128]{3,2,1,0:T(4,128)(2,1)S(1)}, bf16[1024,2,4,128]{3,2,1,0:T(4,128)(2,1)}, u32[]{:S(2)}) copy-start(bf16[1024,2,4,128]{3,2,1,0:T(4,128)(2,1)} %param.2) | copy-start | bytes 6291460
  21.1 1.4 %copy-start = (bf16[128,8192]{1,0:T(8,128)(2,1)}, bf16[128,8192]{1,0:T(8,128)(2,1)S(1)}, u32[]{:S(2)}) copy-start(bf16[128,8192]{1,0:T(8,128)(2,1)S(1)} %get-tuple-element.34.swapped_ref) | copy-start | bytes 6291460
  22.5 11.1 %copy-start.4 = (s32[1,4]{1,0:T(1,128)S(1)}, s32[1,4]{1,0:T(1,128)}, u32[]{:S(2)}) copy-start(s32[1,4]{1,0:T(1,128)} %param.3) | copy-start | bytes 52
  22.8 1.0 %copy-start.3 = (bf16[5120,128]{1,0:T(8,128)(2,1)}, bf16[5120,128]{1,0:T(8,128)(2,1)S(1)}, u32[]{:S(2)}) copy-start(bf16[5120,128]{1,0:T(8,128)(2,1)S(1)} %get-tuple-element.45) | copy-start | bytes 3932164
  25.8 24.0 %collective-permute-start.6 = (bf16[5120,128]{1,0:T(8,128)(2,1)}, bf16[5120,128]{1,0:T(8,128)(2,1)}, u32[]{:S(2)}, u32[]{:S(2)}) collective-permute-start(bf16[5120,128]{1,0:T(8,128)(2,1)} %copy-done.3), channel_id=1, source_target_pairs={{1,9},{10,2},{3,11},{12,4},{2,1},{4,3},{17,25},{26,18},{19,27},{28... | collective-permute-start | bytes 3932168 | tf_op jit(solution)/shard_map/ppermute | solution.py:347
  33.7 1.6 %copy-start.1 = (bf16[128,8192]{1,0:T(8,128)(2,1)S(1)}, bf16[128,8192]{1,0:T(8,128)(2,1)}, u32[]{:S(2)}) copy-start(bf16[128,8192]{1,0:T(8,128)(2,1)} %copy-done) | copy-start | bytes 6291460
  40.7 16.6 %collective-permute-start.5 = (bf16[3072,128]{1,0:T(8,128)(2,1)S(1)}, bf16[3072,128]{1,0:T(8,128)(2,1)S(1)}, u32[]{:S(2)}, u32[]{:S(2)}) collective-permute-start(bf16[3072,128]{1,0:T(8,128)(2,1)S(1)} %get-tuple-element.44), channel_id=1, source_target_pairs={{1,9},{10,2},{3,11},{12,4},{2,1},{4,3},{17,25},{26,18},{19,27},{28... | collective-permute-start | bytes 2359304 | tf_op jit(solution)/shard_map/ppermute | solution.py:352
  48.4 14.2 %collective-permute-start.8 = (bf16[9,128,128]{2,1,0:T(8,128)(2,1)S(1)}, bf16[9,128,128]{2,1,0:T(8,128)(2,1)}, u32[]{:S(2)}, u32[]{:S(2)}) collective-permute-start(bf16[9,128,128]{2,1,0:T(8,128)(2,1)S(1)} %get-tuple-element.47), channel_id=1, source_target_pairs={{0,7},{7,15},{16,23},{23,31}} | collective-permute-start | bytes 884744 | tf_op jit(solution)/shard_map/ppermute | solution.py:354
  60.6 8.4 %collective-permute-start.7 = (bf16[9,128,128]{2,1,0:T(8,128)(2,1)S(1)}, bf16[9,128,128]{2,1,0:T(8,128)(2,1)S(1)}, u32[]{:S(2)}, u32[]{:S(2)}) collective-permute-start(bf16[9,128,128]{2,1,0:T(8,128)(2,1)S(1)} %get-tuple-element.49), channel_id=1, source_target_pairs={{0,8},{13,5},{14,6},{7,15},{9,1},{2,10},{11,3},{4,12},{1,0},{16,24... | collective-permute-start | bytes 884744 | tf_op jit(solution)/shard_map/ppermute | solution.py:362

commit v22 on v21

--- a/solution.py
+++ b/solution.py
@@ -328,8 +328,8 @@
         flags = jnp.stack([jnp.asarray(on), jnp.asarray(other)]).astype(jnp.int32)
         return jnp.concatenate([flags, *weights])
 
+    first_in = lax.ppermute(block, "chan", first_pairs)
     near_in = lax.ppermute(block, "chan", near_pairs)
-    first_in = lax.ppermute(block, "chan", first_pairs)
     coeffs = lag_rows(freq_count, window_count)
     own = turn(block)
     parts = split(block)
@@ -341,8 +341,8 @@
         among([t for _, t in second_pairs]), among([t for _, t in late_near]), quality[0] * second_flags
     )
 
-    near_in, first_part, last_part, own, coeffs, first_in, near_flags, first_flags, second_flags = lax.optimization_barrier(
-        (near_in, *parts, own, coeffs, first_in, near_flags, first_flags, second_flags)
+    first_in, near_in, first_part, last_part, own, coeffs, first_flags, near_flags, second_flags = lax.optimization_barrier(
+        (first_in, near_in, *parts, own, coeffs, first_flags, near_flags, second_flags)
     )
     second_in = [lax.ppermute(first_part, "chan", second_pairs)]
     first_switch = switch(me == 0, special, quality[0], near_flags, first_flags)

time: 70.4 us -> 74.5 us (1.058)
  waiting for transfers between devices: 7.81 us -> 9.94 us
  starting transfers between devices: 28.5 us -> 30.5 us
    ppermute x1, waiting for transfers between devices: 1.41 us -> 3.53 us  [local(): second_in.append(lax.ppermute(last_part, 'chan', second_pairs))]
    ppermute x1, starting transfers between devices: 7.59 us -> 8.91 us  [local(): second_in = [lax.ppermute(first_part, 'chan', second_pairs)]]
  transfers between devices with their start and end apart: 9 -> 9, of which waited for: 2 -> 2; matrix products, arithmetic and copies ran while one was open for 3% -> 3% of each run, Pallas kernels for 34% -> 32%
where the time goes in v22:
time: 74.5 us; the launch traced here: 74 us
  starting transfers between devices  30.5 us (41%)
  Pallas kernels  23.9 us (32%)
  waiting for transfers between devices  9.94 us (13%)
  local copies, waits for them, and re-layouts  5.57 us (7%)
  other arithmetic  3.15 us (4%)
  between operations  0.9 us (1%)
    pallas_call x2, Pallas kernels, first_sums(): pl.pallas_call(functools.partial(first_kernel, windows, bool(earlier)), g...  11.1 us
    ppermute x1, starting transfers between devices, local(): second_flags = lax.ppermute(quality, 'chan', second_pairs)[0]  11.1 us
    pallas_call x2, Pallas kernels, second_sums(): pl.pallas_call(functools.partial(second_kernel, windows, not earlier), gr...  9.37 us
    ppermute x1, starting transfers between devices, local(): second_in = [lax.ppermute(first_part, 'chan', second_pairs)]  8.91 us
    ppermute x1, waiting for transfers between devices, local(): returned = lax.ppermute(back, 'chan', back_pairs)  6.39 us
    unnamed x10, local copies, waits for them, and re-layouts  5.57 us
    ppermute x1, waiting for transfers between devices, local(): second_in.append(lax.ppermute(last_part, 'chan', second_pairs))  3.53 us
    pallas_call x1, Pallas kernels, turn(): pl.pallas_call(turn_kernel, grid=(rows // STEP,), in_specs=[pl.BlockSpec(...  3.15 us
  transfers between devices with their start and end apart: 9, of which 2 were waited for; matrix products, arithmetic and copies ran while one was open for 3% of the time, Pallas kernels for 32%

profile of v22, /device:TPU:1, one launch (start us, length us, event | category | flops | bytes accessed | tf_op | source)
XLA Modules:
  0.0 74.0 jit_solution(17077107539321503581)
XLA Ops:
  0.6 1.3 %collective-permute-start.1 = (bf16[8192,128]{1,0:T(8,128)(2,1)}, bf16[8192,128]{1,0:T(8,128)(2,1)}, u32[]{:S(2)}, u32[]{:S(2)}) collective-permute-start(bf16[8192,128]{1,0:T(8,128)(2,1)} %bitcast.15), channel_id=1, source_target_pairs={{8,0},{5,13},{6,14},{15,7},{0,1},{7,6},{24,16},{21,29},{22,30},{31... | collective-permute-start | bytes 6291464 | tf_op jit(solution)/shard_map/ppermute | solution.py:331
  1.9 2.0 %collective-permute-start.2 = (bf16[8192,128]{1,0:T(8,128)(2,1)}, bf16[8192,128]{1,0:T(8,128)(2,1)}, u32[]{:S(2)}, u32[]{:S(2)}) collective-permute-start(bf16[8192,128]{1,0:T(8,128)(2,1)} %bitcast.16), channel_id=1, source_target_pairs={{3,2},{5,4},{6,5},{9,8},{10,9},{11,10},{12,11},{13,12},{14,13},{15... | collective-permute-start | bytes 6291464 | tf_op jit(solution)/shard_map/ppermute | solution.py:332
  3.9 1.3 %collective-permute-start.3 = (s32[1,4]{1,0:T(1,128)}, s32[1,4]{1,0:T(1,128)S(1)}, u32[]{:S(2)}, u32[]{:S(2)}) collective-permute-start(s32[1,4]{1,0:T(1,128)} %param.3), channel_id=1, source_target_pairs={{8,0},{5,13},{6,14},{15,7},{0,1},{7,6},{24,16},{21,29},{22,30},{31... | collective-permute-start | bytes 56 | tf_op jit(solution)/shard_map/ppermute | solution.py:336
  5.2 0.7 collective-permute-start.4
  5.9 11.1 %collective-permute-start = (s32[1,4]{1,0:T(1,128)}, s32[1,4]{1,0:T(1,128)S(1)}, u32[]{:S(2)}, u32[]{:S(2)}) collective-permute-start(s32[1,4]{1,0:T(1,128)} %param.3), channel_id=1, source_target_pairs={{1,9},{10,2},{3,11},{12,4},{2,1},{4,3},{17,25},{26,18},{19,27},{28... | collective-permute-start | bytes 56 | tf_op jit(solution)/shard_map/ppermute | solution.py:338
  17.0 1.6 %copy-done.2 = bf16[1024,2,4,128]{3,2,1,0:T(4,128)(2,1)S(1)} copy-done((bf16[1024,2,4,128]{3,2,1,0:T(4,128)(2,1)S(1)}, bf16[1024,2,4,128]{3,2,1,0:T(4,128)(2,1)}, u32[]{:S(2)}) %copy-start.2) | copy-done | bytes 2097176
  18.6 3.2 %turn.1 = (bf16[128,8192]{1,0:T(8,128)(2,1)S(1)}, bf16[128,8192]{1,0:T(8,128)(2,1)S(1)}) custom-call(bf16[8192,128]{1,0:T(8,128)(2,1)S(1)} %bitcast.17), custom_call_target="tpu_custom_call" | custom-call | bytes 6291456 | tf_op jit(solution)/shard_map/turn/pallas_call | solution.py:85
  21.8 1.3 %copy-done = bf16[128,8192]{1,0:T(8,128)(2,1)} copy-done((bf16[128,8192]{1,0:T(8,128)(2,1)}, bf16[128,8192]{1,0:T(8,128)(2,1)S(1)}, u32[]{:S(2)}) %copy-start) | copy-done | bytes 2097176
  23.1 0.3 split.1
  23.4 1.0 %copy-done.3 = bf16[5120,128]{1,0:T(8,128)(2,1)} copy-done((bf16[5120,128]{1,0:T(8,128)(2,1)}, bf16[5120,128]{1,0:T(8,128)(2,1)S(1)}, u32[]{:S(2)}) %copy-start.3) | copy-done | bytes 1310744
  24.5 0.9 %multiply_convert_fusion = (bf16[5,8192]{1,0:T(8,128)(2,1)S(1)}, f32[5,8192]{1,0:T(8,128)S(1)}) fusion(f32[8192]{0:T(1024)S(1)} %fusion.9, f32[5]{0:T(128)S(1)} %iota_multiply_fusion), kind=kLoop, calls=%fused_computation.4 | loop fusion | flops 122880 | bytes 278548 | tf_op jit(solution)/shard_map/convert
  25.4 0.9 %fusion.2 = bf16[4,8192]{1,0:T(4,128)(2,1)S(1)} fusion(f32[5,8192]{1,0:T(8,128)S(1)} %get-tuple-element.55, f32[8192]{0:T(1024)S(1)} %select_multiply_fusion), kind=kLoop, calls=%fused_computation.8 | loop fusion | flops 98304 | bytes 229376 | tf_op jit(solution)/shard_map/convert.1
  26.5 8.9 %collective-permute-start.6 = (bf16[5120,128]{1,0:T(8,128)(2,1)}, bf16[5120,128]{1,0:T(8,128)(2,1)}, u32[]{:S(2)}, u32[]{:S(2)}) collective-permute-start(bf16[5120,128]{1,0:T(8,128)(2,1)} %copy-done.3), channel_id=1, source_target_pairs={{1,9},{10,2},{3,11},{12,4},{2,1},{4,3},{17,25},{26,18},{19,27},{28... | collective-permute-start | bytes 3932168 | tf_op jit(solution)/shard_map/ppermute | solution.py:347
  35.6 1.6 %copy-done.1 = bf16[128,8192]{1,0:T(8,128)(2,1)S(1)} copy-done((bf16[128,8192]{1,0:T(8,128)(2,1)S(1)}, bf16[128,8192]{1,0:T(8,128)(2,1)}, u32[]{:S(2)}) %copy-start.1) | copy-done | bytes 2097176
  37.2 5.5 %first_half.1 = (f32[1152,256]{1,0:T(8,128)S(1)}, f32[8,128]{1,0:T(8,128)S(1)}) custom-call(s32[14]{0:T(128)S(1)} %pad_add_fusion.1.switch_ref, bf16[128,8192]{1,0:T(8,128)(2,1)S(1)} %get-tuple-element.33.plain_ref, bf16[128,8192]{1,0:T(8,128)(2,1)S(1)} %copy-done.1, bf16[9,8192]{1,0:T(8,128)(2,1)S(1)} %pad_maximum_fusion.coeff_ref, ...), custom_call_target="tpu_custom_call" | custom-call | flops 2415919104 | bytes 4194304 | tf_op jit(solution)/shard_map/first_half/pallas_call | solution.py:204
  42.7 1.9 %collective-permute-start.5 = (bf16[3072,128]{1,0:T(8,128)(2,1)S(1)}, bf16[3072,128]{1,0:T(8,128)(2,1)S(1)}, u32[]{:S(2)}, u32[]{:S(2)}) collective-permute-start(bf16[3072,128]{1,0:T(8,128)(2,1)S(1)} %get-tuple-element.44), channel_id=1, source_target_pairs={{1,9},{10,2},{3,11},{12,4},{2,1},{4,3},{17,25},{26,18},{19,27},{28... | collective-permute-start | bytes 2359304 | tf_op jit(solution)/shard_map/ppermute | solution.py:352
  44.7 5.7 %first_last.1 = (bf16[9,128,128]{2,1,0:T(8,128)(2,1)S(1)}, bf16[9,128,128]{2,1,0:T(8,128)(2,1)S(1)}, bf16[9,128,128]{2,1,0:T(8,128)(2,1)S(1)}) custom-call(s32[14]{0:T(128)S(1)} %pad_add_fusion.1.switch_ref, bf16[128,8192]{1,0:T(8,128)(2,1)S(1)} %get-tuple-element.33.plain_ref, bf16[128,8192]{1,0:T(8,128)(2,1)S(1)} %copy-done.1, ...), custom_call_target="tpu_custom_call" | custom-call | flops 2415919104 | bytes 4194304 | tf_op jit(solution)/shard_map/first_last/pallas_call | solution.py:204
  50.4 1.4 %collective-permute-start.8 = (bf16[9,128,128]{2,1,0:T(8,128)(2,1)S(1)}, bf16[9,128,128]{2,1,0:T(8,128)(2,1)}, u32[]{:S(2)}, u32[]{:S(2)}) collective-permute-start(bf16[9,128,128]{2,1,0:T(8,128)(2,1)S(1)} %get-tuple-element.47), channel_id=1, source_target_pairs={{0,7},{7,15},{16,23},{23,31}} | collective-permute-start | bytes 884744 | tf_op jit(solution)/shard_map/ppermute | solution.py:354
  51.8 6.1 %second_part.1.rest_0_ = f32[1152,128]{1,0:T(8,128)S(1)} custom-call(s32[6]{0:T(128)S(1)} %pad_add_fusion.switch_ref, bf16[128,8192]{1,0:T(8,128)(2,1)S(1)} %get-tuple-element.33.plain_ref, bf16[128,8192]{1,0:T(8,128)(2,1)S(1)} %copy-done.1, bf16[9,8192]{1,0:T(8,128)(2,1)S(1)} %pad_maximum_fusion.coeff_ref, bf16[5120,128]{1,0:T(8,128)(2,1)} %collective-permute-done.6.partner_ref), custom_call_target="tpu_custom_call" | custom-call | flops 1509949440 | bytes 3932160 | tf_op jit(solution)/shard_map/second_part/pallas_call | solution.py:281
  57.9 3.5 %collective-permute-done.5.partner_ref = bf16[3072,128]{1,0:T(8,128)(2,1)S(1)} collective-permute-done((bf16[3072,128]{1,0:T(8,128)(2,1)S(1)}, bf16[3072,128]{1,0:T(8,128)(2,1)S(1)}, u32[]{:S(2)}, u32[]{:S(2)}) %collective-permute-start.5) | collective-permute-done | bytes 786464 | tf_op jit(solution)/shard_map/ppermute | solution.py:352
  61.4 3.3 %second_last.1 = (bf16[9,128,128]{2,1,0:T(8,128)(2,1)S(1)}, bf16[9,128,128]{2,1,0:T(8,128)(2,1)S(1)}, bf16[9,128,128]{2,1,0:T(8,128)(2,1)S(1)}) custom-call(s32[6]{0:T(128)S(1)} %pad_add_fusion.switch_ref, bf16[128,8192]{1,0:T(8,128)(2,1)S(1)} %get-tuple-element.33.plain_ref, bf16[128,8192]{1,0:T(8,128)(2,1)S(1)} %copy-done.1, ...), custom_call_target="tpu_custom_call" | custom-call | flops 905969664 | bytes 2359296 | tf_op jit(solution)/shard_map/second_last/pallas_call | solution.py:281
  64.7 1.9 %collective-permute-start.7 = (bf16[9,128,128]{2,1,0:T(8,128)(2,1)S(1)}, bf16[9,128,128]{2,1,0:T(8,128)(2,1)S(1)}, u32[]{:S(2)}, u32[]{:S(2)}) collective-permute-start(bf16[9,128,128]{2,1,0:T(8,128)(2,1)S(1)} %get-tuple-element.49), channel_id=1, source_target_pairs={{0,8},{13,5},{14,6},{7,15},{9,1},{2,10},{11,3},{4,12},{1,0},{16,24... | collective-permute-start | bytes 884744 | tf_op jit(solution)/shard_map/ppermute | solution.py:362
  66.7 6.4 %collective-permute-done.7 = bf16[9,128,128]{2,1,0:T(8,128)(2,1)S(1)} collective-permute-done((bf16[9,128,128]{2,1,0:T(8,128)(2,1)S(1)}, bf16[9,128,128]{2,1,0:T(8,128)(2,1)S(1)}, u32[]{:S(2)}, u32[]{:S(2)}) %collective-permute-start.7) | collective-permute-done | bytes 294944 | tf_op jit(solution)/shard_map/ppermute | solution.py:362
  73.1 0.9 %select_bitcast_fusion = (bf16[1,9,128,128]{3,2,1,0:T(8,128)(2,1)}, bf16[1,9,128,128]{3,2,1,0:T(8,128)(2,1)}) fusion(bf16[9,128,128]{2,1,0:T(8,128)(2,1)S(1)} %collective-permute-done.7, bf16[9,128,128]{2,1,0:T(8,128)(2,1)S(1)} %get-tuple-element.51, pred[]{:T(512)S(6)} %or.59, bf16[9,128,128]{2,1,0:T(8,128)(2,1)} %collective-permute-done.8, ...), kind=kLoop, calls=%fused_computation | loop fusion | flops 442368 | bytes 1769475 | tf_op jit(solution)/shard_map/broadcast_in_dim | solution.py:366
  (23 shorter events, 0.5 us)
Async XLA Ops:
  0.6 25.8 %collective-permute-start.1 = (bf16[8192,128]{1,0:T(8,128)(2,1)}, bf16[8192,128]{1,0:T(8,128)(2,1)}, u32[]{:S(2)}, u32[]{:S(2)}) collective-permute-start(bf16[8192,128]{1,0:T(8,128)(2,1)} %bitcast.15), channel_id=1, source_target_pairs={{8,0},{5,13},{6,14},{15,7},{0,1},{7,6},{24,16},{21,29},{22,30},{31... | collective-permute-start | bytes 6291464 | tf_op jit(solution)/shard_map/ppermute | solution.py:331
  1.9 24.5 %collective-permute-start.2 = (bf16[8192,128]{1,0:T(8,128)(2,1)}, bf16[8192,128]{1,0:T(8,128)(2,1)}, u32[]{:S(2)}, u32[]{:S(2)}) collective-permute-start(bf16[8192,128]{1,0:T(8,128)(2,1)} %bitcast.16), channel_id=1, source_target_pairs={{3,2},{5,4},{6,5},{9,8},{10,9},{11,10},{12,11},{13,12},{14,13},{15... | collective-permute-start | bytes 6291464 | tf_op jit(solution)/shard_map/ppermute | solution.py:332
  3.9 22.5 %collective-permute-start.3 = (s32[1,4]{1,0:T(1,128)}, s32[1,4]{1,0:T(1,128)S(1)}, u32[]{:S(2)}, u32[]{:S(2)}) collective-permute-start(s32[1,4]{1,0:T(1,128)} %param.3), channel_id=1, source_target_pairs={{8,0},{5,13},{6,14},{15,7},{0,1},{7,6},{24,16},{21,29},{22,30},{31... | collective-permute-start | bytes 56 | tf_op jit(solution)/shard_map/ppermute | solution.py:336
  5.2 21.2 %collective-permute-start.4 = (s32[1,4]{1,0:T(1,128)}, s32[1,4]{1,0:T(1,128)S(1)}, u32[]{:S(2)}, u32[]{:S(2)}) collective-permute-start(s32[1,4]{1,0:T(1,128)} %param.3), channel_id=1, source_target_pairs={{3,2},{5,4},{6,5},{9,8},{10,9},{11,10},{12,11},{13,12},{14,13},{15... | collective-permute-start | bytes 56 | tf_op jit(solution)/shard_map/ppermute | solution.py:337
  5.9 38.7 %collective-permute-start = (s32[1,4]{1,0:T(1,128)}, s32[1,4]{1,0:T(1,128)S(1)}, u32[]{:S(2)}, u32[]{:S(2)}) collective-permute-start(s32[1,4]{1,0:T(1,128)} %param.3), channel_id=1, source_target_pairs={{1,9},{10,2},{3,11},{12,4},{2,1},{4,3},{17,25},{26,18},{19,27},{28... | collective-permute-start | bytes 56 | tf_op jit(solution)/shard_map/ppermute | solution.py:338
  17.0 1.6 %copy-start.2 = (bf16[1024,2,4,128]{3,2,1,0:T(4,128)(2,1)S(1)}, bf16[1024,2,4,128]{3,2,1,0:T(4,128)(2,1)}, u32[]{:S(2)}) copy-start(bf16[1024,2,4,128]{3,2,1,0:T(4,128)(2,1)} %param.2) | copy-start | bytes 6291460
  21.8 1.4 %copy-start = (bf16[128,8192]{1,0:T(8,128)(2,1)}, bf16[128,8192]{1,0:T(8,128)(2,1)S(1)}, u32[]{:S(2)}) copy-start(bf16[128,8192]{1,0:T(8,128)(2,1)S(1)} %get-tuple-element.34.swapped_ref) | copy-start | bytes 6291460
  23.1 12.4 %copy-start.4 = (s32[1,4]{1,0:T(1,128)S(1)}, s32[1,4]{1,0:T(1,128)}, u32[]{:S(2)}) copy-start(s32[1,4]{1,0:T(1,128)} %param.3) | copy-start | bytes 52
  23.4 1.0 %copy-start.3 = (bf16[5120,128]{1,0:T(8,128)(2,1)}, bf16[5120,128]{1,0:T(8,128)(2,1)S(1)}, u32[]{:S(2)}) copy-start(bf16[5120,128]{1,0:T(8,128)(2,1)S(1)} %get-tuple-element.45) | copy-start | bytes 3932164
  26.5 25.3 %collective-permute-start.6 = (bf16[5120,128]{1,0:T(8,128)(2,1)}, bf16[5120,128]{1,0:T(8,128)(2,1)}, u32[]{:S(2)}, u32[]{:S(2)}) collective-permute-start(bf16[5120,128]{1,0:T(8,128)(2,1)} %copy-done.3), channel_id=1, source_target_pairs={{1,9},{10,2},{3,11},{12,4},{2,1},{4,3},{17,25},{26,18},{19,27},{28... | collective-permute-start | bytes 3932168 | tf_op jit(solution)/shard_map/ppermute | solution.py:347
  35.6 1.6 %copy-start.1 = (bf16[128,8192]{1,0:T(8,128)(2,1)S(1)}, bf16[128,8192]{1,0:T(8,128)(2,1)}, u32[]{:S(2)}) copy-start(bf16[128,8192]{1,0:T(8,128)(2,1)} %copy-done) | copy-start | bytes 6291460
  42.7 18.7 %collective-permute-start.5 = (bf16[3072,128]{1,0:T(8,128)(2,1)S(1)}, bf16[3072,128]{1,0:T(8,128)(2,1)S(1)}, u32[]{:S(2)}, u32[]{:S(2)}) collective-permute-start(bf16[3072,128]{1,0:T(8,128)(2,1)S(1)} %get-tuple-element.44), channel_id=1, source_target_pairs={{1,9},{10,2},{3,11},{12,4},{2,1},{4,3},{17,25},{26,18},{19,27},{28... | collective-permute-start | bytes 2359304 | tf_op jit(solution)/shard_map/ppermute | solution.py:352
  50.4 16.3 %collective-permute-start.8 = (bf16[9,128,128]{2,1,0:T(8,128)(2,1)S(1)}, bf16[9,128,128]{2,1,0:T(8,128)(2,1)}, u32[]{:S(2)}, u32[]{:S(2)}) collective-permute-start(bf16[9,128,128]{2,1,0:T(8,128)(2,1)S(1)} %get-tuple-element.47), channel_id=1, source_target_pairs={{0,7},{7,15},{16,23},{23,31}} | collective-permute-start | bytes 884744 | tf_op jit(solution)/shard_map/ppermute | solution.py:354
  64.7 8.4 %collective-permute-start.7 = (bf16[9,128,128]{2,1,0:T(8,128)(2,1)S(1)}, bf16[9,128,128]{2,1,0:T(8,128)(2,1)S(1)}, u32[]{:S(2)}, u32[]{:S(2)}) collective-permute-start(bf16[9,128,128]{2,1,0:T(8,128)(2,1)S(1)} %get-tuple-element.49), channel_id=1, source_target_pairs={{0,8},{13,5},{14,6},{7,15},{9,1},{2,10},{11,3},{4,12},{1,0},{16,24... | collective-permute-start | bytes 884744 | tf_op jit(solution)/shard_map/ppermute | solution.py:362

commit v23 on v21

--- a/solution.py
+++ b/solution.py
@@ -351,7 +351,6 @@
     last_part, token = lax.optimization_barrier((last_part, token))
     second_in.append(lax.ppermute(last_part, "chan", second_pairs))
     near, far, back = first_sums(*operands, [total, token])
-    side_returned = lax.ppermute(near, "chan", side_pairs)
     second_switch, near = lax.optimization_barrier((second_switch, near))
     total, = second_sums(second_switch, own, coeffs, second_in[0], 0)
 
@@ -360,6 +359,7 @@
         second_switch, own, coeffs, second_in[1], parts[0].shape[0], [total, near, far, back]
     )
     returned = lax.ppermute(back, "chan", back_pairs)
+    side_returned = lax.ppermute(near, "chan", side_pairs)
     near = jnp.where(among([half - 1, count - 1]), side_returned, near)
     near = jnp.where(me == 0, returned, near)
     far = jnp.where(among([s for s, _ in first_far + second_far]), returned, far)

time: 70.4 us -> 69.7 us (0.990)
  transfers between devices with their start and end apart: 9 -> 9, of which waited for: 2 -> 2; matrix products, arithmetic and copies ran while one was open for 3% -> 3% of each run, Pallas kernels for 34% -> 30%
where the time goes in v23:
time: 69.7 us; the launch traced here: 69.2 us
  starting transfers between devices  27.8 us (40%)
  Pallas kernels  23.9 us (34%)
  waiting for transfers between devices  7.78 us (11%)
  local copies, waits for them, and re-layouts  5.57 us (8%)
  other arithmetic  3.15 us (5%)
  between operations  0.9 us (1%)
    pallas_call x2, Pallas kernels, first_sums(): pl.pallas_call(functools.partial(first_kernel, windows, bool(earlier)), g...  11.1 us
    ppermute x1, starting transfers between devices, local(): second_flags = lax.ppermute(quality, 'chan', second_pairs)[0]  10.5 us
    pallas_call x2, Pallas kernels, second_sums(): pl.pallas_call(functools.partial(second_kernel, windows, not earlier), gr...  9.36 us
    ppermute x1, starting transfers between devices, local(): second_in = [lax.ppermute(first_part, 'chan', second_pairs)]  7.59 us
    ppermute x1, waiting for transfers between devices, local(): returned = lax.ppermute(back, 'chan', back_pairs)  5.71 us
    unnamed x10, local copies, waits for them, and re-layouts  5.57 us
    pallas_call x1, Pallas kernels, turn(): pl.pallas_call(turn_kernel, grid=(rows // STEP,), in_specs=[pl.BlockSpec(...  3.15 us
    ppermute x1, waiting for transfers between devices, local(): second_in.append(lax.ppermute(last_part, 'chan', second_pairs))  2.05 us
  transfers between devices with their start and end apart: 9, of which 2 were waited for; matrix products, arithmetic and copies ran while one was open for 3% of the time, Pallas kernels for 30%

profile of v23, /device:TPU:1, one launch (start us, length us, event | category | flops | bytes accessed | tf_op | source)
XLA Modules:
  0.0 69.2 jit_solution(16994815317482343074)
XLA Ops:
  0.6 2.0 %collective-permute-start.1 = (bf16[8192,128]{1,0:T(8,128)(2,1)}, bf16[8192,128]{1,0:T(8,128)(2,1)}, u32[]{:S(2)}, u32[]{:S(2)}) collective-permute-start(bf16[8192,128]{1,0:T(8,128)(2,1)} %bitcast.15), channel_id=1, source_target_pairs={{3,2},{5,4},{6,5},{9,8},{10,9},{11,10},{12,11},{13,12},{14,13},{15... | collective-permute-start | bytes 6291464 | tf_op jit(solution)/shard_map/ppermute | solution.py:331
  2.6 1.3 %collective-permute-start.2 = (bf16[8192,128]{1,0:T(8,128)(2,1)}, bf16[8192,128]{1,0:T(8,128)(2,1)}, u32[]{:S(2)}, u32[]{:S(2)}) collective-permute-start(bf16[8192,128]{1,0:T(8,128)(2,1)} %bitcast.16), channel_id=1, source_target_pairs={{8,0},{5,13},{6,14},{15,7},{0,1},{7,6},{24,16},{21,29},{22,30},{31... | collective-permute-start | bytes 6291464 | tf_op jit(solution)/shard_map/ppermute | solution.py:332
  3.9 0.7 collective-permute-start.3
  4.6 1.3 %collective-permute-start.4 = (s32[1,4]{1,0:T(1,128)}, s32[1,4]{1,0:T(1,128)S(1)}, u32[]{:S(2)}, u32[]{:S(2)}) collective-permute-start(s32[1,4]{1,0:T(1,128)} %param.3), channel_id=1, source_target_pairs={{8,0},{5,13},{6,14},{15,7},{0,1},{7,6},{24,16},{21,29},{22,30},{31... | collective-permute-start | bytes 56 | tf_op jit(solution)/shard_map/ppermute | solution.py:336
  5.9 10.5 %collective-permute-start = (s32[1,4]{1,0:T(1,128)}, s32[1,4]{1,0:T(1,128)S(1)}, u32[]{:S(2)}, u32[]{:S(2)}) collective-permute-start(s32[1,4]{1,0:T(1,128)} %param.3), channel_id=1, source_target_pairs={{1,9},{10,2},{3,11},{12,4},{2,1},{4,3},{17,25},{26,18},{19,27},{28... | collective-permute-start | bytes 56 | tf_op jit(solution)/shard_map/ppermute | solution.py:338
  16.4 1.6 %copy-done.2 = bf16[1024,2,4,128]{3,2,1,0:T(4,128)(2,1)S(1)} copy-done((bf16[1024,2,4,128]{3,2,1,0:T(4,128)(2,1)S(1)}, bf16[1024,2,4,128]{3,2,1,0:T(4,128)(2,1)}, u32[]{:S(2)}) %copy-start.2) | copy-done | bytes 2097176
  18.0 3.2 %turn.1 = (bf16[128,8192]{1,0:T(8,128)(2,1)S(1)}, bf16[128,8192]{1,0:T(8,128)(2,1)S(1)}) custom-call(bf16[8192,128]{1,0:T(8,128)(2,1)S(1)} %bitcast.17), custom_call_target="tpu_custom_call" | custom-call | bytes 6291456 | tf_op jit(solution)/shard_map/turn/pallas_call | solution.py:85
  21.2 1.3 %copy-done = bf16[128,8192]{1,0:T(8,128)(2,1)} copy-done((bf16[128,8192]{1,0:T(8,128)(2,1)}, bf16[128,8192]{1,0:T(8,128)(2,1)S(1)}, u32[]{:S(2)}) %copy-start) | copy-done | bytes 2097176
  22.5 0.3 split.1
  22.8 1.0 %copy-done.3 = bf16[5120,128]{1,0:T(8,128)(2,1)} copy-done((bf16[5120,128]{1,0:T(8,128)(2,1)}, bf16[5120,128]{1,0:T(8,128)(2,1)S(1)}, u32[]{:S(2)}) %copy-start.3) | copy-done | bytes 1310744
  23.9 0.9 %multiply_convert_fusion = (bf16[5,8192]{1,0:T(8,128)(2,1)S(1)}, f32[5,8192]{1,0:T(8,128)S(1)}) fusion(f32[8192]{0:T(1024)S(1)} %fusion.9, f32[5]{0:T(128)S(1)} %iota_multiply_fusion), kind=kLoop, calls=%fused_computation.4 | loop fusion | flops 122880 | bytes 278548 | tf_op jit(solution)/shard_map/convert
  24.8 0.9 %fusion.2 = bf16[4,8192]{1,0:T(4,128)(2,1)S(1)} fusion(f32[5,8192]{1,0:T(8,128)S(1)} %get-tuple-element.55, f32[8192]{0:T(1024)S(1)} %select_multiply_fusion), kind=kLoop, calls=%fused_computation.8 | loop fusion | flops 98304 | bytes 229376 | tf_op jit(solution)/shard_map/convert.1
  25.8 7.6 %collective-permute-start.6 = (bf16[5120,128]{1,0:T(8,128)(2,1)}, bf16[5120,128]{1,0:T(8,128)(2,1)}, u32[]{:S(2)}, u32[]{:S(2)}) collective-permute-start(bf16[5120,128]{1,0:T(8,128)(2,1)} %copy-done.3), channel_id=1, source_target_pairs={{1,9},{10,2},{3,11},{12,4},{2,1},{4,3},{17,25},{26,18},{19,27},{28... | collective-permute-start | bytes 3932168 | tf_op jit(solution)/shard_map/ppermute | solution.py:347
  33.7 1.6 %copy-done.1 = bf16[128,8192]{1,0:T(8,128)(2,1)S(1)} copy-done((bf16[128,8192]{1,0:T(8,128)(2,1)S(1)}, bf16[128,8192]{1,0:T(8,128)(2,1)}, u32[]{:S(2)}) %copy-start.1) | copy-done | bytes 2097176
  35.3 5.5 %first_half.1 = (f32[1152,256]{1,0:T(8,128)S(1)}, f32[8,128]{1,0:T(8,128)S(1)}) custom-call(s32[14]{0:T(128)S(1)} %pad_add_fusion.1.switch_ref, bf16[128,8192]{1,0:T(8,128)(2,1)S(1)} %get-tuple-element.33.plain_ref, bf16[128,8192]{1,0:T(8,128)(2,1)S(1)} %copy-done.1, bf16[9,8192]{1,0:T(8,128)(2,1)S(1)} %pad_maximum_fusion.coeff_ref, ...), custom_call_target="tpu_custom_call" | custom-call | flops 2415919104 | bytes 4194304 | tf_op jit(solution)/shard_map/first_half/pallas_call | solution.py:204
  40.7 1.9 %collective-permute-start.5 = (bf16[3072,128]{1,0:T(8,128)(2,1)S(1)}, bf16[3072,128]{1,0:T(8,128)(2,1)S(1)}, u32[]{:S(2)}, u32[]{:S(2)}) collective-permute-start(bf16[3072,128]{1,0:T(8,128)(2,1)S(1)} %get-tuple-element.44), channel_id=1, source_target_pairs={{1,9},{10,2},{3,11},{12,4},{2,1},{4,3},{17,25},{26,18},{19,27},{28... | collective-permute-start | bytes 2359304 | tf_op jit(solution)/shard_map/ppermute | solution.py:352
  42.8 5.7 %first_last.1 = (bf16[9,128,128]{2,1,0:T(8,128)(2,1)S(1)}, bf16[9,128,128]{2,1,0:T(8,128)(2,1)S(1)}, bf16[9,128,128]{2,1,0:T(8,128)(2,1)S(1)}) custom-call(s32[14]{0:T(128)S(1)} %pad_add_fusion.1.switch_ref, bf16[128,8192]{1,0:T(8,128)(2,1)S(1)} %get-tuple-element.33.plain_ref, bf16[128,8192]{1,0:T(8,128)(2,1)S(1)} %copy-done.1, ...), custom_call_target="tpu_custom_call" | custom-call | flops 2415919104 | bytes 4194304 | tf_op jit(solution)/shard_map/first_last/pallas_call | solution.py:204
  48.5 6.1 %second_part.1.rest_0_ = f32[1152,128]{1,0:T(8,128)S(1)} custom-call(s32[6]{0:T(128)S(1)} %pad_add_fusion.switch_ref, bf16[128,8192]{1,0:T(8,128)(2,1)S(1)} %get-tuple-element.33.plain_ref, bf16[128,8192]{1,0:T(8,128)(2,1)S(1)} %copy-done.1, bf16[9,8192]{1,0:T(8,128)(2,1)S(1)} %pad_maximum_fusion.coeff_ref, bf16[5120,128]{1,0:T(8,128)(2,1)} %collective-permute-done.6.partner_ref), custom_call_target="tpu_custom_call" | custom-call | flops 1509949440 | bytes 3932160 | tf_op jit(solution)/shard_map/second_part/pallas_call | solution.py:281
  54.5 2.1 %collective-permute-done.5.partner_ref = bf16[3072,128]{1,0:T(8,128)(2,1)S(1)} collective-permute-done((bf16[3072,128]{1,0:T(8,128)(2,1)S(1)}, bf16[3072,128]{1,0:T(8,128)(2,1)S(1)}, u32[]{:S(2)}, u32[]{:S(2)}) %collective-permute-start.5) | collective-permute-done | bytes 786464 | tf_op jit(solution)/shard_map/ppermute | solution.py:352
  56.6 3.3 %second_last.1 = (bf16[9,128,128]{2,1,0:T(8,128)(2,1)S(1)}, bf16[9,128,128]{2,1,0:T(8,128)(2,1)S(1)}, bf16[9,128,128]{2,1,0:T(8,128)(2,1)S(1)}) custom-call(s32[6]{0:T(128)S(1)} %pad_add_fusion.switch_ref, bf16[128,8192]{1,0:T(8,128)(2,1)S(1)} %get-tuple-element.33.plain_ref, bf16[128,8192]{1,0:T(8,128)(2,1)S(1)} %copy-done.1, ...), custom_call_target="tpu_custom_call" | custom-call | flops 905969664 | bytes 2359296 | tf_op jit(solution)/shard_map/second_last/pallas_call | solution.py:281
  59.9 1.9 %collective-permute-start.7 = (bf16[9,128,128]{2,1,0:T(8,128)(2,1)S(1)}, bf16[9,128,128]{2,1,0:T(8,128)(2,1)S(1)}, u32[]{:S(2)}, u32[]{:S(2)}) collective-permute-start(bf16[9,128,128]{2,1,0:T(8,128)(2,1)S(1)} %get-tuple-element.49), channel_id=1, source_target_pairs={{0,8},{13,5},{14,6},{7,15},{9,1},{2,10},{11,3},{4,12},{1,0},{16,24... | collective-permute-start | bytes 884744 | tf_op jit(solution)/shard_map/ppermute | solution.py:361
  61.8 0.7 collective-permute-start.8
  62.6 5.7 %collective-permute-done.7 = bf16[9,128,128]{2,1,0:T(8,128)(2,1)S(1)} collective-permute-done((bf16[9,128,128]{2,1,0:T(8,128)(2,1)S(1)}, bf16[9,128,128]{2,1,0:T(8,128)(2,1)S(1)}, u32[]{:S(2)}, u32[]{:S(2)}) %collective-permute-start.7) | collective-permute-done | bytes 294944 | tf_op jit(solution)/shard_map/ppermute | solution.py:361
  68.3 0.9 %select_bitcast_fusion = (bf16[1,9,128,128]{3,2,1,0:T(8,128)(2,1)}, bf16[1,9,128,128]{3,2,1,0:T(8,128)(2,1)}) fusion(bf16[9,128,128]{2,1,0:T(8,128)(2,1)S(1)} %collective-permute-done.7, bf16[9,128,128]{2,1,0:T(8,128)(2,1)S(1)} %get-tuple-element.51, pred[]{:T(512)S(6)} %or.59, bf16[9,128,128]{2,1,0:T(8,128)(2,1)S(1)} %collective-permute-done.8, ...), kind=kLoop, calls=%fused_computation | loop fusion | flops 442368 | bytes 1769475 | tf_op jit(solution)/shard_map/broadcast_in_dim | solution.py:366
  (23 shorter events, 0.5 us)
Async XLA Ops:
  0.6 25.2 %collective-permute-start.1 = (bf16[8192,128]{1,0:T(8,128)(2,1)}, bf16[8192,128]{1,0:T(8,128)(2,1)}, u32[]{:S(2)}, u32[]{:S(2)}) collective-permute-start(bf16[8192,128]{1,0:T(8,128)(2,1)} %bitcast.15), channel_id=1, source_target_pairs={{3,2},{5,4},{6,5},{9,8},{10,9},{11,10},{12,11},{13,12},{14,13},{15... | collective-permute-start | bytes 6291464 | tf_op jit(solution)/shard_map/ppermute | solution.py:331
  2.6 23.2 %collective-permute-start.2 = (bf16[8192,128]{1,0:T(8,128)(2,1)}, bf16[8192,128]{1,0:T(8,128)(2,1)}, u32[]{:S(2)}, u32[]{:S(2)}) collective-permute-start(bf16[8192,128]{1,0:T(8,128)(2,1)} %bitcast.16), channel_id=1, source_target_pairs={{8,0},{5,13},{6,14},{15,7},{0,1},{7,6},{24,16},{21,29},{22,30},{31... | collective-permute-start | bytes 6291464 | tf_op jit(solution)/shard_map/ppermute | solution.py:332
  3.9 21.9 %collective-permute-start.3 = (s32[1,4]{1,0:T(1,128)}, s32[1,4]{1,0:T(1,128)S(1)}, u32[]{:S(2)}, u32[]{:S(2)}) collective-permute-start(s32[1,4]{1,0:T(1,128)} %param.3), channel_id=1, source_target_pairs={{3,2},{5,4},{6,5},{9,8},{10,9},{11,10},{12,11},{13,12},{14,13},{15... | collective-permute-start | bytes 56 | tf_op jit(solution)/shard_map/ppermute | solution.py:337
  4.6 21.2 %collective-permute-start.4 = (s32[1,4]{1,0:T(1,128)}, s32[1,4]{1,0:T(1,128)S(1)}, u32[]{:S(2)}, u32[]{:S(2)}) collective-permute-start(s32[1,4]{1,0:T(1,128)} %param.3), channel_id=1, source_target_pairs={{8,0},{5,13},{6,14},{15,7},{0,1},{7,6},{24,16},{21,29},{22,30},{31... | collective-permute-start | bytes 56 | tf_op jit(solution)/shard_map/ppermute | solution.py:336
  5.9 36.8 %collective-permute-start = (s32[1,4]{1,0:T(1,128)}, s32[1,4]{1,0:T(1,128)S(1)}, u32[]{:S(2)}, u32[]{:S(2)}) collective-permute-start(s32[1,4]{1,0:T(1,128)} %param.3), channel_id=1, source_target_pairs={{1,9},{10,2},{3,11},{12,4},{2,1},{4,3},{17,25},{26,18},{19,27},{28... | collective-permute-start | bytes 56 | tf_op jit(solution)/shard_map/ppermute | solution.py:338
  16.4 1.6 %copy-start.2 = (bf16[1024,2,4,128]{3,2,1,0:T(4,128)(2,1)S(1)}, bf16[1024,2,4,128]{3,2,1,0:T(4,128)(2,1)}, u32[]{:S(2)}) copy-start(bf16[1024,2,4,128]{3,2,1,0:T(4,128)(2,1)} %param.2) | copy-start | bytes 6291460
  21.1 1.4 %copy-start = (bf16[128,8192]{1,0:T(8,128)(2,1)}, bf16[128,8192]{1,0:T(8,128)(2,1)S(1)}, u32[]{:S(2)}) copy-start(bf16[128,8192]{1,0:T(8,128)(2,1)S(1)} %get-tuple-element.34.swapped_ref) | copy-start | bytes 6291460
  22.5 11.1 %copy-start.4 = (s32[1,4]{1,0:T(1,128)S(1)}, s32[1,4]{1,0:T(1,128)}, u32[]{:S(2)}) copy-start(s32[1,4]{1,0:T(1,128)} %param.3) | copy-start | bytes 52
  22.8 1.0 %copy-start.3 = (bf16[5120,128]{1,0:T(8,128)(2,1)}, bf16[5120,128]{1,0:T(8,128)(2,1)S(1)}, u32[]{:S(2)}) copy-start(bf16[5120,128]{1,0:T(8,128)(2,1)S(1)} %get-tuple-element.45) | copy-start | bytes 3932164
  25.8 22.6 %collective-permute-start.6 = (bf16[5120,128]{1,0:T(8,128)(2,1)}, bf16[5120,128]{1,0:T(8,128)(2,1)}, u32[]{:S(2)}, u32[]{:S(2)}) collective-permute-start(bf16[5120,128]{1,0:T(8,128)(2,1)} %copy-done.3), channel_id=1, source_target_pairs={{1,9},{10,2},{3,11},{12,4},{2,1},{4,3},{17,25},{26,18},{19,27},{28... | collective-permute-start | bytes 3932168 | tf_op jit(solution)/shard_map/ppermute | solution.py:347
  33.7 1.6 %copy-start.1 = (bf16[128,8192]{1,0:T(8,128)(2,1)S(1)}, bf16[128,8192]{1,0:T(8,128)(2,1)}, u32[]{:S(2)}) copy-start(bf16[128,8192]{1,0:T(8,128)(2,1)} %copy-done) | copy-start | bytes 6291460
  40.7 15.9 %collective-permute-start.5 = (bf16[3072,128]{1,0:T(8,128)(2,1)S(1)}, bf16[3072,128]{1,0:T(8,128)(2,1)S(1)}, u32[]{:S(2)}, u32[]{:S(2)}) collective-permute-start(bf16[3072,128]{1,0:T(8,128)(2,1)S(1)} %get-tuple-element.44), channel_id=1, source_target_pairs={{1,9},{10,2},{3,11},{12,4},{2,1},{4,3},{17,25},{26,18},{19,27},{28... | collective-permute-start | bytes 2359304 | tf_op jit(solution)/shard_map/ppermute | solution.py:352
  59.9 8.4 %collective-permute-start.7 = (bf16[9,128,128]{2,1,0:T(8,128)(2,1)S(1)}, bf16[9,128,128]{2,1,0:T(8,128)(2,1)S(1)}, u32[]{:S(2)}, u32[]{:S(2)}) collective-permute-start(bf16[9,128,128]{2,1,0:T(8,128)(2,1)S(1)} %get-tuple-element.49), channel_id=1, source_target_pairs={{0,8},{13,5},{14,6},{7,15},{9,1},{2,10},{11,3},{4,12},{1,0},{16,24... | collective-permute-start | bytes 884744 | tf_op jit(solution)/shard_map/ppermute | solution.py:361
  61.8 6.4 %collective-permute-start.8 = (bf16[9,128,128]{2,1,0:T(8,128)(2,1)S(1)}, bf16[9,128,128]{2,1,0:T(8,128)(2,1)S(1)}, u32[]{:S(2)}, u32[]{:S(2)}) collective-permute-start(bf16[9,128,128]{2,1,0:T(8,128)(2,1)S(1)} %get-tuple-element.50), channel_id=1, source_target_pairs={{0,7},{7,15},{16,23},{23,31}} | collective-permute-start | bytes 884744 | tf_op jit(solution)/shard_map/ppermute | solution.py:362

commit v24 on v23

--- a/solution.py
+++ b/solution.py
@@ -11,7 +11,7 @@
 HL = 4
 LAGS = 2 * HL + 1
 STEP = 1024
-PARTS = (5, 8)
+ENDS = (4, 6, 8)
 PARAMS = pltpu.CompilerParams(vmem_limit_bytes=16 * 1024 * 1024)
 
 
@@ -28,31 +28,29 @@
     return jnp.concatenate([cos_part, sin_part], axis=0).astype(jnp.bfloat16)
 
 
-def split_kernel(middle, x_ref, first_ref, last_ref):
+def split_kernel(ends, x_ref, *part_refs):
     step = pl.program_id(0)
-
-    @pl.when(step < middle)
-    def _():
-        first_ref[...] = x_ref[...]
-
-    @pl.when(step >= middle)
-    def _():
-        last_ref[...] = x_ref[...]
+    for begin, end, part_ref in zip((0, *ends), ends, part_refs):
+        @pl.when((step >= begin) & (step < end))
+        def _():
+            part_ref[...] = x_ref[...]
 
 
 def split(x):
     rows, cols = x.shape
     steps = rows // STEP
-    middle = steps * PARTS[0] // PARTS[1]
+    ends = [steps * e // ENDS[-1] for e in ENDS]
+    sizes = [e - b for b, e in zip([0] + ends, ends)]
+
+    def place(end, size):
+        return lambda s: (jnp.clip(s - end + size, 0, size - 1), 0)
+
     return pl.pallas_call(
-        functools.partial(split_kernel, middle),
+        functools.partial(split_kernel, ends),
         grid=(steps,),
         in_specs=[pl.BlockSpec((STEP, cols), lambda s: (s, 0))],
-        out_specs=[
-            pl.BlockSpec((STEP, cols), lambda s: (jnp.minimum(s, middle - 1), 0)),
-            pl.BlockSpec((STEP, cols), lambda s: (jnp.maximum(s - middle, 0), 0)),
-        ],
-        out_shape=[jax.ShapeDtypeStruct((n * STEP, cols), x.dtype) for n in (middle, steps - middle)],
+        out_specs=[pl.BlockSpec((STEP, cols), place(e, n)) for e, n in zip(ends, sizes)],
+        out_shape=[jax.ShapeDtypeStruct((n * STEP, cols), x.dtype) for n in sizes],
         compiler_params=PARAMS,
         cost_estimate=pl.CostEstimate(flops=0, bytes_accessed=4 * rows * cols, transcendentals=0),
         name="split",
@@ -219,12 +217,14 @@
     )(switch, *own, coeffs, near_in, first_in, *earlier)
 
 
-def second_kernel(windows, first, switch_ref, plain_ref, swapped_ref, coeff_ref, partner_ref, *rest):
+def second_kernel(windows, first, last, switch_ref, plain_ref, swapped_ref, coeff_ref, partner_ref, *rest):
     on, late_near = switch_ref[0], switch_ref[1]
     step = pl.program_id(0)
     cols = plain_ref.shape[0]
     if first:
         acc, scaled = rest
+    elif not last:
+        acc_in, acc, scaled = rest
     else:
         acc_in, near_in, far_in, back_in, near_out, far_out, back_out, acc, scaled = rest
 
@@ -238,7 +238,7 @@
         partner = weigh(partner_ref[...], [switch_ref[2 + w] for w in range(windows)])
         acc[...] += jnp.dot(scaled[...], partner, preferred_element_type=jnp.float32)
 
-    if not first:
+    if last:
         @pl.when(step == pl.num_programs(0) - 1)
         def _():
             here = slice(0, cols)
@@ -260,7 +260,7 @@
                 near_out[...] = near_in[...]
 
 
-def second_sums(switch, own, coeffs, partner, start, earlier=None):
+def second_sums(switch, own, coeffs, partner, start, earlier=()):
     rows, cols = partner.shape
     windows = switch.shape[0] - 2
     skip = start // STEP
@@ -272,14 +272,15 @@
     in_specs = [left, left, pl.BlockSpec((LAGS, STEP), lambda s, on: (0, s * on[0] + skip)),
                 pl.BlockSpec((STEP, cols), lambda s, on: (s * on[0], 0))]
     scratch = [pltpu.VMEM((LAGS * cols, STEP), jnp.bfloat16)]
-    if earlier is None:
-        out_shape, out_specs, earlier = [total], [total_spec], []
+    last = len(earlier) > 1
+    in_specs += [total_spec, result_spec, result_spec, result_spec][:len(earlier)]
+    if not last:
+        out_shape, out_specs = [total], [total_spec]
     else:
         out_shape, out_specs = [result] * 3, [result_spec] * 3
-        in_specs += [total_spec] + [result_spec] * 3
         scratch = [pltpu.VMEM(total.shape, jnp.float32)] + scratch
     return pl.pallas_call(
-        functools.partial(second_kernel, windows, not earlier),
+        functools.partial(second_kernel, windows, not earlier, last),
         grid_spec=pltpu.PrefetchScalarGridSpec(
             num_scalar_prefetch=1,
             grid=(rows // STEP,),
@@ -292,7 +293,7 @@
         cost_estimate=pl.CostEstimate(
             flops=2 * LAGS * cols * cols * rows, bytes_accessed=6 * rows * cols, transcendentals=0
         ),
-        name="second_last" if earlier else "second_part",
+        name="second_last" if last else "second_part",
     )(switch, *own, coeffs, partner, *earlier)
 
 
@@ -341,22 +342,25 @@
         among([t for _, t in second_pairs]), among([t for _, t in late_near]), quality[0] * second_flags
     )
 
-    near_in, first_part, last_part, own, coeffs, first_in, near_flags, first_flags, second_flags = lax.optimization_barrier(
+    near_in, *parts, own, coeffs, first_in, near_flags, first_flags, second_flags = lax.optimization_barrier(
         (near_in, *parts, own, coeffs, first_in, near_flags, first_flags, second_flags)
     )
-    second_in = [lax.ppermute(first_part, "chan", second_pairs)]
+    second_in = [lax.ppermute(parts[0], "chan", second_pairs)]
     first_switch = switch(me == 0, special, quality[0], near_flags, first_flags)
     operands = first_switch, own, coeffs, near_in, first_in
     total, token = first_sums(*operands)
-    last_part, token = lax.optimization_barrier((last_part, token))
-    second_in.append(lax.ppermute(last_part, "chan", second_pairs))
+    part, token = lax.optimization_barrier((parts[1], token))
+    second_in.append(lax.ppermute(part, "chan", second_pairs))
     near, far, back = first_sums(*operands, [total, token])
-    second_switch, near = lax.optimization_barrier((second_switch, near))
-    total, = second_sums(second_switch, own, coeffs, second_in[0], 0)
+    second_switch, near, part = lax.optimization_barrier((second_switch, near, parts[2]))
+    second_in.append(lax.ppermute(part, "chan", second_pairs))
+    starts = [0, parts[0].shape[0], parts[0].shape[0] + parts[1].shape[0]]
+    total = second_sums(second_switch, own, coeffs, second_in[0], starts[0])
+    total, = second_sums(second_switch, own, coeffs, second_in[1], starts[1], total)
 
     near = jnp.where(me == half - 2, far, near)
     near, far, back = second_sums(
-        second_switch, own, coeffs, second_in[1], parts[0].shape[0], [total, near, far, back]
+        second_switch, own, coeffs, second_in[2], starts[2], [total, near, far, back]
     )
     returned = lax.ppermute(back, "chan", back_pairs)
     side_returned = lax.ppermute(near, "chan", side_pairs)

time: 69.7 us -> 76.9 us (1.10)
  Pallas kernels: 23.9 us -> 29.2 us
  local copies, waits for them, and re-layouts: 5.57 us -> 7.52 us
  other arithmetic: 3.15 us -> 5.08 us
  waiting for transfers between devices: 7.78 us -> 5.95 us
    pallas_call x3 -> x4, Pallas kernels: 9.64 us -> 14.9 us  [the longest x3 11.6 us: second_sums(): pl.pallas_call(functools.partial(second_kernel, windows, not earlier, las...]
    ppermute x2 -> x3, waiting for transfers between devices: 2.05 us -> 0.01 us  [the longest x2 0.01 us: local(): second_in.append(lax.ppermute(part, 'chan', second_pairs))]
    unnamed x10 -> x14, local copies, waits for them, and re-layouts: 5.57 us -> 7.52 us
    broadcast_in_dim x1, other arithmetic: 0.87 us -> 1.84 us  [local(): return (near[None], far[None])]
    select_n x1, other arithmetic: 0.04 us -> 1 us  [local(): near = jnp.where(me == half - 2, far, near)]
    ppermute x2 -> x3, starting transfers between devices: 9.51 us -> 9.35 us  [the longest x1 5.52 us: local(): second_in = [lax.ppermute(parts[0], 'chan', second_pairs)]]
  transfers between devices with their start and end apart: 9 -> 10, of which waited for: 2 -> 1; matrix products, arithmetic and copies ran while one was open for 3% -> 4% of each run, Pallas kernels for 30% -> 34%
where the time goes in v24:
time: 76.9 us; the launch traced here: 76.3 us
  Pallas kernels  29.2 us (38%)
  starting transfers between devices  27.6 us (36%)
  local copies, waits for them, and re-layouts  7.52 us (10%)
  waiting for transfers between devices  5.95 us (8%)
  other arithmetic  5.08 us (7%)
  between operations  0.96 us (1%)
    pallas_call x3, Pallas kernels, second_sums(): pl.pallas_call(functools.partial(second_kernel, windows, not earlier, las...  11.6 us
    pallas_call x2, Pallas kernels, first_sums(): pl.pallas_call(functools.partial(first_kernel, windows, bool(earlier)), g...  11.1 us
    ppermute x1, starting transfers between devices, local(): second_flags = lax.ppermute(quality, 'chan', second_pairs)[0]  10.5 us
    unnamed x14, local copies, waits for them, and re-layouts  7.52 us
    ppermute x1, waiting for transfers between devices, local(): returned = lax.ppermute(back, 'chan', back_pairs)  5.92 us
    ppermute x1, starting transfers between devices, local(): second_in = [lax.ppermute(parts[0], 'chan', second_pairs)]  5.52 us
    ppermute x2, starting transfers between devices, local(): second_in.append(lax.ppermute(part, 'chan', second_pairs))  3.83 us
    pallas_call x1, Pallas kernels, split(): pl.pallas_call(functools.partial(split_kernel, ends), grid=(steps,), in_s...  3.26 us
  transfers between devices with their start and end apart: 10, of which 1 were waited for; matrix products, arithmetic and copies ran while one was open for 4% of the time, Pallas kernels for 34%

profile of v24, /device:TPU:1, one launch (start us, length us, event | category | flops | bytes accessed | tf_op | source)
XLA Modules:
  0.0 76.3 jit_solution(11056545154754886349)
XLA Ops:
  0.6 2.0 %collective-permute-start.1 = (bf16[8192,128]{1,0:T(8,128)(2,1)}, bf16[8192,128]{1,0:T(8,128)(2,1)}, u32[]{:S(2)}, u32[]{:S(2)}) collective-permute-start(bf16[8192,128]{1,0:T(8,128)(2,1)} %bitcast.15), channel_id=1, source_target_pairs={{3,2},{5,4},{6,5},{9,8},{10,9},{11,10},{12,11},{13,12},{14,13},{15... | collective-permute-start | bytes 6291464 | tf_op jit(solution)/shard_map/ppermute | solution.py:332
  2.6 1.3 %collective-permute-start.2 = (bf16[8192,128]{1,0:T(8,128)(2,1)}, bf16[8192,128]{1,0:T(8,128)(2,1)}, u32[]{:S(2)}, u32[]{:S(2)}) collective-permute-start(bf16[8192,128]{1,0:T(8,128)(2,1)} %bitcast.16), channel_id=1, source_target_pairs={{8,0},{5,13},{6,14},{15,7},{0,1},{7,6},{24,16},{21,29},{22,30},{31... | collective-permute-start | bytes 6291464 | tf_op jit(solution)/shard_map/ppermute | solution.py:333
  4.6 1.3 %collective-permute-start.4 = (s32[1,4]{1,0:T(1,128)}, s32[1,4]{1,0:T(1,128)S(1)}, u32[]{:S(2)}, u32[]{:S(2)}) collective-permute-start(s32[1,4]{1,0:T(1,128)} %param.3), channel_id=1, source_target_pairs={{8,0},{5,13},{6,14},{15,7},{0,1},{7,6},{24,16},{21,29},{22,30},{31... | collective-permute-start | bytes 56 | tf_op jit(solution)/shard_map/ppermute | solution.py:337
  5.9 10.5 %collective-permute-start = (s32[1,4]{1,0:T(1,128)}, s32[1,4]{1,0:T(1,128)S(1)}, u32[]{:S(2)}, u32[]{:S(2)}) collective-permute-start(s32[1,4]{1,0:T(1,128)} %param.3), channel_id=1, source_target_pairs={{1,9},{10,2},{3,11},{12,4},{2,1},{4,3},{17,25},{26,18},{19,27},{28... | collective-permute-start | bytes 56 | tf_op jit(solution)/shard_map/ppermute | solution.py:339
  16.4 1.6 %copy-done.3 = bf16[1024,2,4,128]{3,2,1,0:T(4,128)(2,1)S(1)} copy-done((bf16[1024,2,4,128]{3,2,1,0:T(4,128)(2,1)S(1)}, bf16[1024,2,4,128]{3,2,1,0:T(4,128)(2,1)}, u32[]{:S(2)}) %copy-start.3) | copy-done | bytes 2097176
  18.0 3.3 %split.1 = (bf16[4096,128]{1,0:T(8,128)(2,1)}, bf16[2048,128]{1,0:T(8,128)(2,1)}, bf16[2048,128]{1,0:T(8,128)(2,1)}) custom-call(bf16[8192,128]{1,0:T(8,128)(2,1)S(1)} %bitcast.17), custom_call_target="tpu_custom_call" | custom-call | bytes 4194304 | tf_op jit(solution)/shard_map/split/pallas_call | solution.py:48
  21.2 3.2 %turn.1 = (bf16[128,8192]{1,0:T(8,128)(2,1)S(1)}, bf16[128,8192]{1,0:T(8,128)(2,1)S(1)}) custom-call(bf16[8192,128]{1,0:T(8,128)(2,1)S(1)} %bitcast.18), custom_call_target="tpu_custom_call" | custom-call | bytes 6291456 | tf_op jit(solution)/shard_map/turn/pallas_call | solution.py:83
  24.4 1.3 %copy-done = bf16[128,8192]{1,0:T(8,128)(2,1)} copy-done((bf16[128,8192]{1,0:T(8,128)(2,1)}, bf16[128,8192]{1,0:T(8,128)(2,1)S(1)}, u32[]{:S(2)}) %copy-start) | copy-done | bytes 2097176
  25.9 0.9 %multiply_convert_fusion = (bf16[5,8192]{1,0:T(8,128)(2,1)S(1)}, f32[5,8192]{1,0:T(8,128)S(1)}) fusion(f32[8192]{0:T(1024)S(1)} %fusion.9, f32[5]{0:T(128)S(1)} %iota_multiply_fusion), kind=kLoop, calls=%fused_computation.4 | loop fusion | flops 122880 | bytes 278548 | tf_op jit(solution)/shard_map/convert
  26.9 0.9 %fusion.2 = bf16[4,8192]{1,0:T(4,128)(2,1)S(1)} fusion(f32[5,8192]{1,0:T(8,128)S(1)} %get-tuple-element.61, f32[8192]{0:T(1024)S(1)} %select_multiply_fusion), kind=kLoop, calls=%fused_computation.8 | loop fusion | flops 98304 | bytes 229376 | tf_op jit(solution)/shard_map/convert.1
  27.9 5.5 %collective-permute-start.7 = (bf16[4096,128]{1,0:T(8,128)(2,1)}, bf16[4096,128]{1,0:T(8,128)(2,1)}, u32[]{:S(2)}, u32[]{:S(2)}) collective-permute-start(bf16[4096,128]{1,0:T(8,128)(2,1)} %get-tuple-element.51), channel_id=1, source_target_pairs={{1,9},{10,2},{3,11},{12,4},{2,1},{4,3},{17,25},{26,18},{19,27},{28... | collective-permute-start | bytes 3145736 | tf_op jit(solution)/shard_map/ppermute | solution.py:348
  33.6 1.6 %copy-done.1 = bf16[128,8192]{1,0:T(8,128)(2,1)S(1)} copy-done((bf16[128,8192]{1,0:T(8,128)(2,1)S(1)}, bf16[128,8192]{1,0:T(8,128)(2,1)}, u32[]{:S(2)}) %copy-start.1) | copy-done | bytes 2097176
  35.2 5.4 %first_half.1 = (f32[1152,256]{1,0:T(8,128)S(1)}, f32[8,128]{1,0:T(8,128)S(1)}) custom-call(s32[14]{0:T(128)S(1)} %pad_add_fusion.1.switch_ref, bf16[128,8192]{1,0:T(8,128)(2,1)S(1)} %get-tuple-element.37.plain_ref, bf16[128,8192]{1,0:T(8,128)(2,1)S(1)} %copy-done.1, bf16[9,8192]{1,0:T(8,128)(2,1)S(1)} %pad_maximum_fusion.coeff_ref, ...), custom_call_target="tpu_custom_call" | custom-call | flops 2415919104 | bytes 4194304 | tf_op jit(solution)/shard_map/first_half/pallas_call | solution.py:202
  40.7 1.9 %collective-permute-start.6 = (bf16[2048,128]{1,0:T(8,128)(2,1)}, bf16[2048,128]{1,0:T(8,128)(2,1)}, u32[]{:S(2)}, u32[]{:S(2)}) collective-permute-start(bf16[2048,128]{1,0:T(8,128)(2,1)} %get-tuple-element.50), channel_id=1, source_target_pairs={{1,9},{10,2},{3,11},{12,4},{2,1},{4,3},{17,25},{26,18},{19,27},{28... | collective-permute-start | bytes 1572872 | tf_op jit(solution)/shard_map/ppermute | solution.py:353
  42.6 5.7 %first_last.1 = (bf16[9,128,128]{2,1,0:T(8,128)(2,1)S(1)}, bf16[9,128,128]{2,1,0:T(8,128)(2,1)S(1)}, bf16[9,128,128]{2,1,0:T(8,128)(2,1)S(1)}) custom-call(s32[14]{0:T(128)S(1)} %pad_add_fusion.1.switch_ref, bf16[128,8192]{1,0:T(8,128)(2,1)S(1)} %get-tuple-element.37.plain_ref, bf16[128,8192]{1,0:T(8,128)(2,1)S(1)} %copy-done.1, ...), custom_call_target="tpu_custom_call" | custom-call | flops 2415919104 | bytes 4194304 | tf_op jit(solution)/shard_map/first_last/pallas_call | solution.py:202
  49.0 1.9 %collective-permute-start.5 = (bf16[2048,128]{1,0:T(8,128)(2,1)}, bf16[2048,128]{1,0:T(8,128)(2,1)S(1)}, u32[]{:S(2)}, u32[]{:S(2)}) collective-permute-start(bf16[2048,128]{1,0:T(8,128)(2,1)} %get-tuple-element.49), channel_id=1, source_target_pairs={{1,9},{10,2},{3,11},{12,4},{2,1},{4,3},{17,25},{26,18},{19,27},{28... | collective-permute-start | bytes 1572872 | tf_op jit(solution)/shard_map/ppermute | solution.py:356
  50.9 1.0 %broadcast_select_fusion.rest_1_ = bf16[9,128,128]{2,1,0:T(8,128)(2,1)S(1)} fusion(bf16[9,128,128]{2,1,0:T(8,128)(2,1)S(1)} %get-tuple-element.52.rest_2_, bf16[9,128,128]{2,1,0:T(8,128)(2,1)} %copy-done.5, pred[]{:T(512)S(6)} %eq.61), kind=kLoop, calls=%fused_computation.2 | loop fusion | flops 147456 | bytes 884737 | tf_op jit(solution)/shard_map/jit(_where)/select_n | solution.py:361
  51.9 1.6 %copy-done.2 = bf16[128,8192]{1,0:T(8,128)(2,1)S(1)} copy-done((bf16[128,8192]{1,0:T(8,128)(2,1)S(1)}, bf16[128,8192]{1,0:T(8,128)(2,1)}, u32[]{:S(2)}) %copy-start.2) | copy-done | bytes 2097176
  53.5 5.1 %second_part.2.rest_0_ = f32[1152,128]{1,0:T(8,128)S(1)} custom-call(s32[6]{0:T(128)S(1)} %pad_add_fusion.switch_ref, bf16[128,8192]{1,0:T(8,128)(2,1)S(1)} %get-tuple-element.37.plain_ref, bf16[128,8192]{1,0:T(8,128)(2,1)S(1)} %copy-done.2, bf16[9,8192]{1,0:T(8,128)(2,1)S(1)} %pad_maximum_fusion.coeff_ref, bf16[4096,128]{1,0:T(8,128)(2,1)} %collective-permute-done.7.partner_ref), custom_call_target="tpu_custom_call" | custom-call | flops 1207959552 | bytes 3145728 | tf_op jit(solution)/shard_map/second_part/pallas_call | solution.py:282
  58.7 3.2 %second_part.3.rest_0_ = f32[1152,128]{1,0:T(8,128)S(1)} custom-call(s32[6]{0:T(128)S(1)} %pad_add_fusion.switch_ref, bf16[128,8192]{1,0:T(8,128)(2,1)S(1)} %get-tuple-element.37.plain_ref, bf16[128,8192]{1,0:T(8,128)(2,1)S(1)} %copy-done.2, bf16[9,8192]{1,0:T(8,128)(2,1)S(1)} %pad_maximum_fusion.coeff_ref, ...), custom_call_target="tpu_custom_call" | custom-call | flops 603979776 | bytes 1572864 | tf_op jit(solution)/shard_map/second_part/pallas_call | solution.py:282
  62.0 3.2 %second_last.1 = (bf16[9,128,128]{2,1,0:T(8,128)(2,1)}, bf16[9,128,128]{2,1,0:T(8,128)(2,1)S(1)}, bf16[9,128,128]{2,1,0:T(8,128)(2,1)}) custom-call(s32[6]{0:T(128)S(1)} %pad_add_fusion.switch_ref, bf16[128,8192]{1,0:T(8,128)(2,1)S(1)} %get-tuple-element.37.plain_ref, bf16[128,8192]{1,0:T(8,128)(2,1)S(1)} %copy-done.2, ...), custom_call_target="tpu_custom_call" | custom-call | flops 603979776 | bytes 1572864 | tf_op jit(solution)/shard_map/second_last/pallas_call | solution.py:282
  65.9 1.9 %collective-permute-start.8 = (bf16[9,128,128]{2,1,0:T(8,128)(2,1)}, bf16[9,128,128]{2,1,0:T(8,128)(2,1)S(1)}, u32[]{:S(2)}, u32[]{:S(2)}) collective-permute-start(bf16[9,128,128]{2,1,0:T(8,128)(2,1)} %get-tuple-element.55), channel_id=1, source_target_pairs={{0,8},{13,5},{14,6},{7,15},{9,1},{2,10},{11,3},{4,12},{1,0},{16,24... | collective-permute-start | bytes 884744 | tf_op jit(solution)/shard_map/ppermute | solution.py:365
  68.5 5.9 %collective-permute-done.8 = bf16[9,128,128]{2,1,0:T(8,128)(2,1)S(1)} collective-permute-done((bf16[9,128,128]{2,1,0:T(8,128)(2,1)}, bf16[9,128,128]{2,1,0:T(8,128)(2,1)S(1)}, u32[]{:S(2)}, u32[]{:S(2)}) %collective-permute-start.8) | collective-permute-done | bytes 294944 | tf_op jit(solution)/shard_map/ppermute | solution.py:365
  74.5 1.8 %select_bitcast_fusion = (bf16[1,9,128,128]{3,2,1,0:T(8,128)(2,1)}, bf16[1,9,128,128]{3,2,1,0:T(8,128)(2,1)}) fusion(bf16[9,128,128]{2,1,0:T(8,128)(2,1)S(1)} %collective-permute-done.8, bf16[9,128,128]{2,1,0:T(8,128)(2,1)} %copy-done.4, pred[]{:T(512)S(6)} %or.59, bf16[9,128,128]{2,1,0:T(8,128)(2,1)S(1)} %collective-permute-done.9, ...), kind=kLoop, calls=%fused_computation | loop fusion | flops 442368 | bytes 1769475 | tf_op jit(solution)/shard_map/broadcast_in_dim | solution.py:370
  (30 shorter events, 3.2 us)
Async XLA Ops:
  0.6 27.3 %collective-permute-start.1 = (bf16[8192,128]{1,0:T(8,128)(2,1)}, bf16[8192,128]{1,0:T(8,128)(2,1)}, u32[]{:S(2)}, u32[]{:S(2)}) collective-permute-start(bf16[8192,128]{1,0:T(8,128)(2,1)} %bitcast.15), channel_id=1, source_target_pairs={{3,2},{5,4},{6,5},{9,8},{10,9},{11,10},{12,11},{13,12},{14,13},{15... | collective-permute-start | bytes 6291464 | tf_op jit(solution)/shard_map/ppermute | solution.py:332
  2.6 25.3 %collective-permute-start.2 = (bf16[8192,128]{1,0:T(8,128)(2,1)}, bf16[8192,128]{1,0:T(8,128)(2,1)}, u32[]{:S(2)}, u32[]{:S(2)}) collective-permute-start(bf16[8192,128]{1,0:T(8,128)(2,1)} %bitcast.16), channel_id=1, source_target_pairs={{8,0},{5,13},{6,14},{15,7},{0,1},{7,6},{24,16},{21,29},{22,30},{31... | collective-permute-start | bytes 6291464 | tf_op jit(solution)/shard_map/ppermute | solution.py:333
  3.9 24.0 %collective-permute-start.3 = (s32[1,4]{1,0:T(1,128)}, s32[1,4]{1,0:T(1,128)S(1)}, u32[]{:S(2)}, u32[]{:S(2)}) collective-permute-start(s32[1,4]{1,0:T(1,128)} %param.3), channel_id=1, source_target_pairs={{3,2},{5,4},{6,5},{9,8},{10,9},{11,10},{12,11},{13,12},{14,13},{15... | collective-permute-start | bytes 56 | tf_op jit(solution)/shard_map/ppermute | solution.py:338
  4.6 23.3 %collective-permute-start.4 = (s32[1,4]{1,0:T(1,128)}, s32[1,4]{1,0:T(1,128)S(1)}, u32[]{:S(2)}, u32[]{:S(2)}) collective-permute-start(s32[1,4]{1,0:T(1,128)} %param.3), channel_id=1, source_target_pairs={{8,0},{5,13},{6,14},{15,7},{0,1},{7,6},{24,16},{21,29},{22,30},{31... | collective-permute-start | bytes 56 | tf_op jit(solution)/shard_map/ppermute | solution.py:337
  5.9 27.6 %collective-permute-start = (s32[1,4]{1,0:T(1,128)}, s32[1,4]{1,0:T(1,128)S(1)}, u32[]{:S(2)}, u32[]{:S(2)}) collective-permute-start(s32[1,4]{1,0:T(1,128)} %param.3), channel_id=1, source_target_pairs={{1,9},{10,2},{3,11},{12,4},{2,1},{4,3},{17,25},{26,18},{19,27},{28... | collective-permute-start | bytes 56 | tf_op jit(solution)/shard_map/ppermute | solution.py:339
  16.4 1.6 %copy-start.3 = (bf16[1024,2,4,128]{3,2,1,0:T(4,128)(2,1)S(1)}, bf16[1024,2,4,128]{3,2,1,0:T(4,128)(2,1)}, u32[]{:S(2)}) copy-start(bf16[1024,2,4,128]{3,2,1,0:T(4,128)(2,1)} %param.2) | copy-start | bytes 6291460
  21.2 12.2 %copy-start.6 = (s32[1,4]{1,0:T(1,128)S(1)}, s32[1,4]{1,0:T(1,128)}, u32[]{:S(2)}) copy-start(s32[1,4]{1,0:T(1,128)} %param.3) | copy-start | bytes 52
  24.4 1.3 %copy-start = (bf16[128,8192]{1,0:T(8,128)(2,1)}, bf16[128,8192]{1,0:T(8,128)(2,1)S(1)}, u32[]{:S(2)}) copy-start(bf16[128,8192]{1,0:T(8,128)(2,1)S(1)} %get-tuple-element.38.swapped_ref) | copy-start | bytes 6291460
  27.9 24.0 %collective-permute-start.7 = (bf16[4096,128]{1,0:T(8,128)(2,1)}, bf16[4096,128]{1,0:T(8,128)(2,1)}, u32[]{:S(2)}, u32[]{:S(2)}) collective-permute-start(bf16[4096,128]{1,0:T(8,128)(2,1)} %get-tuple-element.51), channel_id=1, source_target_pairs={{1,9},{10,2},{3,11},{12,4},{2,1},{4,3},{17,25},{26,18},{19,27},{28... | collective-permute-start | bytes 3145736 | tf_op jit(solution)/shard_map/ppermute | solution.py:348
  33.6 1.6 %copy-start.1 = (bf16[128,8192]{1,0:T(8,128)(2,1)S(1)}, bf16[128,8192]{1,0:T(8,128)(2,1)}, u32[]{:S(2)}) copy-start(bf16[128,8192]{1,0:T(8,128)(2,1)} %copy-done) | copy-start | bytes 6291460
  40.7 18.0 %collective-permute-start.6 = (bf16[2048,128]{1,0:T(8,128)(2,1)}, bf16[2048,128]{1,0:T(8,128)(2,1)}, u32[]{:S(2)}, u32[]{:S(2)}) collective-permute-start(bf16[2048,128]{1,0:T(8,128)(2,1)} %get-tuple-element.50), channel_id=1, source_target_pairs={{1,9},{10,2},{3,11},{12,4},{2,1},{4,3},{17,25},{26,18},{19,27},{28... | collective-permute-start | bytes 1572872 | tf_op jit(solution)/shard_map/ppermute | solution.py:353
  48.3 0.7 copy-start.5
  49.0 13.0 %collective-permute-start.5 = (bf16[2048,128]{1,0:T(8,128)(2,1)}, bf16[2048,128]{1,0:T(8,128)(2,1)S(1)}, u32[]{:S(2)}, u32[]{:S(2)}) collective-permute-start(bf16[2048,128]{1,0:T(8,128)(2,1)} %get-tuple-element.49), channel_id=1, source_target_pairs={{1,9},{10,2},{3,11},{12,4},{2,1},{4,3},{17,25},{26,18},{19,27},{28... | collective-permute-start | bytes 1572872 | tf_op jit(solution)/shard_map/ppermute | solution.py:356
  51.9 1.6 %copy-start.2 = (bf16[128,8192]{1,0:T(8,128)(2,1)S(1)}, bf16[128,8192]{1,0:T(8,128)(2,1)}, u32[]{:S(2)}) copy-start(bf16[128,8192]{1,0:T(8,128)(2,1)} %copy-done) | copy-start | bytes 6291460
  65.2 0.7 copy-start.4
  65.9 8.6 %collective-permute-start.8 = (bf16[9,128,128]{2,1,0:T(8,128)(2,1)}, bf16[9,128,128]{2,1,0:T(8,128)(2,1)S(1)}, u32[]{:S(2)}, u32[]{:S(2)}) collective-permute-start(bf16[9,128,128]{2,1,0:T(8,128)(2,1)} %get-tuple-element.55), channel_id=1, source_target_pairs={{0,8},{13,5},{14,6},{7,15},{9,1},{2,10},{11,3},{4,12},{1,0},{16,24... | collective-permute-start | bytes 884744 | tf_op jit(solution)/shard_map/ppermute | solution.py:365
  67.8 6.7 %collective-permute-start.9 = (bf16[9,128,128]{2,1,0:T(8,128)(2,1)}, bf16[9,128,128]{2,1,0:T(8,128)(2,1)S(1)}, u32[]{:S(2)}, u32[]{:S(2)}) collective-permute-start(bf16[9,128,128]{2,1,0:T(8,128)(2,1)} %get-tuple-element.56), channel_id=1, source_target_pairs={{0,7},{7,15},{16,23},{23,31}} | collective-permute-start | bytes 884744 | tf_op jit(solution)/shard_map/ppermute | solution.py:366

commit v25 on v23

--- a/solution.py
+++ b/solution.py
@@ -307,7 +307,7 @@
     for p in range(half):
         if p in (0, half - 1):
             first_far.append((p + half, p))
-        elif p > half // 2:
+        elif p == 2 or p % 2 == 1 and p > 3:
             first_far.append((p, p + half))
         elif p % 2 == 1:
             second_far.append((p, p + half))

time: 69.7 us -> 71.8 us (1.030)
  waiting for transfers between devices: 7.78 us -> 9.94 us
    ppermute x1, waiting for transfers between devices: 0.01 us -> 1.95 us  [local(): second_in = [lax.ppermute(first_part, 'chan', second_pairs)]]
  transfers between devices with their start and end apart: 9 -> 9, of which waited for: 2 -> 3; matrix products, arithmetic and copies ran while one was open for 3% -> 3% of each run, Pallas kernels for 30% -> 29%
where the time goes in v25:
time: 71.8 us; the launch traced here: 71.3 us
  starting transfers between devices  27.8 us (39%)
  Pallas kernels  23.9 us (33%)
  waiting for transfers between devices  9.94 us (14%)
  local copies, waits for them, and re-layouts  5.57 us (8%)
  other arithmetic  3.15 us (4%)
  between operations  0.89 us (1%)
    pallas_call x2, Pallas kernels, first_sums(): pl.pallas_call(functools.partial(first_kernel, windows, bool(earlier)), g...  11.1 us
    ppermute x1, starting transfers between devices, local(): second_flags = lax.ppermute(quality, 'chan', second_pairs)[0]  10.5 us
    pallas_call x2, Pallas kernels, second_sums(): pl.pallas_call(functools.partial(second_kernel, windows, not earlier), gr...  9.36 us
    ppermute x1, starting transfers between devices, local(): second_in = [lax.ppermute(first_part, 'chan', second_pairs)]  7.59 us
    ppermute x1, waiting for transfers between devices, local(): returned = lax.ppermute(back, 'chan', back_pairs)  5.72 us
    unnamed x10, local copies, waits for them, and re-layouts  5.57 us
    pallas_call x1, Pallas kernels, turn(): pl.pallas_call(turn_kernel, grid=(rows // STEP,), in_specs=[pl.BlockSpec(...  3.15 us
    ppermute x1, waiting for transfers between devices, local(): second_in.append(lax.ppermute(last_part, 'chan', second_pairs))  2.25 us
  transfers between devices with their start and end apart: 9, of which 3 were waited for; matrix products, arithmetic and copies ran while one was open for 3% of the time, Pallas kernels for 29%

profile of v25, /device:TPU:1, one launch (start us, length us, event | category | flops | bytes accessed | tf_op | source)
XLA Modules:
  0.0 71.3 jit_solution(12643310335426230690)
XLA Ops:
  0.6 2.0 %collective-permute-start.1 = (bf16[8192,128]{1,0:T(8,128)(2,1)}, bf16[8192,128]{1,0:T(8,128)(2,1)}, u32[]{:S(2)}, u32[]{:S(2)}) collective-permute-start(bf16[8192,128]{1,0:T(8,128)(2,1)} %bitcast.15), channel_id=1, source_target_pairs={{3,2},{5,4},{6,5},{9,8},{10,9},{11,10},{12,11},{13,12},{14,13},{15... | collective-permute-start | bytes 6291464 | tf_op jit(solution)/shard_map/ppermute | solution.py:331
  2.6 1.3 %collective-permute-start.2 = (bf16[8192,128]{1,0:T(8,128)(2,1)}, bf16[8192,128]{1,0:T(8,128)(2,1)}, u32[]{:S(2)}, u32[]{:S(2)}) collective-permute-start(bf16[8192,128]{1,0:T(8,128)(2,1)} %bitcast.16), channel_id=1, source_target_pairs={{8,0},{2,10},{5,13},{15,7},{0,1},{7,6},{24,16},{18,26},{21,29},{31... | collective-permute-start | bytes 6291464 | tf_op jit(solution)/shard_map/ppermute | solution.py:332
  3.9 0.7 collective-permute-start.3
  4.6 1.3 %collective-permute-start.4 = (s32[1,4]{1,0:T(1,128)}, s32[1,4]{1,0:T(1,128)S(1)}, u32[]{:S(2)}, u32[]{:S(2)}) collective-permute-start(s32[1,4]{1,0:T(1,128)} %param.3), channel_id=1, source_target_pairs={{8,0},{2,10},{5,13},{15,7},{0,1},{7,6},{24,16},{18,26},{21,29},{31... | collective-permute-start | bytes 56 | tf_op jit(solution)/shard_map/ppermute | solution.py:336
  5.9 10.5 %collective-permute-start = (s32[1,4]{1,0:T(1,128)}, s32[1,4]{1,0:T(1,128)S(1)}, u32[]{:S(2)}, u32[]{:S(2)}) collective-permute-start(s32[1,4]{1,0:T(1,128)} %param.3), channel_id=1, source_target_pairs={{1,9},{3,11},{12,4},{14,6},{2,1},{4,3},{17,25},{19,27},{28,20},{30... | collective-permute-start | bytes 56 | tf_op jit(solution)/shard_map/ppermute | solution.py:338
  16.4 1.6 %copy-done.2 = bf16[1024,2,4,128]{3,2,1,0:T(4,128)(2,1)S(1)} copy-done((bf16[1024,2,4,128]{3,2,1,0:T(4,128)(2,1)S(1)}, bf16[1024,2,4,128]{3,2,1,0:T(4,128)(2,1)}, u32[]{:S(2)}) %copy-start.2) | copy-done | bytes 2097176
  18.0 3.2 %turn.1 = (bf16[128,8192]{1,0:T(8,128)(2,1)S(1)}, bf16[128,8192]{1,0:T(8,128)(2,1)S(1)}) custom-call(bf16[8192,128]{1,0:T(8,128)(2,1)S(1)} %bitcast.17), custom_call_target="tpu_custom_call" | custom-call | bytes 6291456 | tf_op jit(solution)/shard_map/turn/pallas_call | solution.py:85
  21.2 1.3 %copy-done = bf16[128,8192]{1,0:T(8,128)(2,1)} copy-done((bf16[128,8192]{1,0:T(8,128)(2,1)}, bf16[128,8192]{1,0:T(8,128)(2,1)S(1)}, u32[]{:S(2)}) %copy-start) | copy-done | bytes 2097176
  22.8 1.0 %copy-done.3 = bf16[5120,128]{1,0:T(8,128)(2,1)} copy-done((bf16[5120,128]{1,0:T(8,128)(2,1)}, bf16[5120,128]{1,0:T(8,128)(2,1)S(1)}, u32[]{:S(2)}) %copy-start.3) | copy-done | bytes 1310744
  23.9 0.9 %multiply_convert_fusion = (bf16[5,8192]{1,0:T(8,128)(2,1)S(1)}, f32[5,8192]{1,0:T(8,128)S(1)}) fusion(f32[8192]{0:T(1024)S(1)} %fusion.9, f32[5]{0:T(128)S(1)} %iota_multiply_fusion), kind=kLoop, calls=%fused_computation.4 | loop fusion | flops 122880 | bytes 278548 | tf_op jit(solution)/shard_map/convert
  24.8 0.9 %fusion.2 = bf16[4,8192]{1,0:T(4,128)(2,1)S(1)} fusion(f32[5,8192]{1,0:T(8,128)S(1)} %get-tuple-element.55, f32[8192]{0:T(1024)S(1)} %select_multiply_fusion), kind=kLoop, calls=%fused_computation.8 | loop fusion | flops 98304 | bytes 229376 | tf_op jit(solution)/shard_map/convert.1
  25.8 7.6 %collective-permute-start.6 = (bf16[5120,128]{1,0:T(8,128)(2,1)}, bf16[5120,128]{1,0:T(8,128)(2,1)}, u32[]{:S(2)}, u32[]{:S(2)}) collective-permute-start(bf16[5120,128]{1,0:T(8,128)(2,1)} %copy-done.3), channel_id=1, source_target_pairs={{1,9},{3,11},{12,4},{14,6},{2,1},{4,3},{17,25},{19,27},{28,20},{30... | collective-permute-start | bytes 3932168 | tf_op jit(solution)/shard_map/ppermute | solution.py:347
  33.7 1.6 %copy-done.1 = bf16[128,8192]{1,0:T(8,128)(2,1)S(1)} copy-done((bf16[128,8192]{1,0:T(8,128)(2,1)S(1)}, bf16[128,8192]{1,0:T(8,128)(2,1)}, u32[]{:S(2)}) %copy-start.1) | copy-done | bytes 2097176
  35.3 5.5 %first_half.1 = (f32[1152,256]{1,0:T(8,128)S(1)}, f32[8,128]{1,0:T(8,128)S(1)}) custom-call(s32[14]{0:T(128)S(1)} %pad_add_fusion.1.switch_ref, bf16[128,8192]{1,0:T(8,128)(2,1)S(1)} %get-tuple-element.33.plain_ref, bf16[128,8192]{1,0:T(8,128)(2,1)S(1)} %copy-done.1, bf16[9,8192]{1,0:T(8,128)(2,1)S(1)} %pad_maximum_fusion.coeff_ref, ...), custom_call_target="tpu_custom_call" | custom-call | flops 2415919104 | bytes 4194304 | tf_op jit(solution)/shard_map/first_half/pallas_call | solution.py:204
  40.7 1.9 %collective-permute-start.5 = (bf16[3072,128]{1,0:T(8,128)(2,1)S(1)}, bf16[3072,128]{1,0:T(8,128)(2,1)S(1)}, u32[]{:S(2)}, u32[]{:S(2)}) collective-permute-start(bf16[3072,128]{1,0:T(8,128)(2,1)S(1)} %get-tuple-element.44), channel_id=1, source_target_pairs={{1,9},{3,11},{12,4},{14,6},{2,1},{4,3},{17,25},{19,27},{28,20},{30... | collective-permute-start | bytes 2359304 | tf_op jit(solution)/shard_map/ppermute | solution.py:352
  42.8 5.7 %first_last.1 = (bf16[9,128,128]{2,1,0:T(8,128)(2,1)S(1)}, bf16[9,128,128]{2,1,0:T(8,128)(2,1)S(1)}, bf16[9,128,128]{2,1,0:T(8,128)(2,1)S(1)}) custom-call(s32[14]{0:T(128)S(1)} %pad_add_fusion.1.switch_ref, bf16[128,8192]{1,0:T(8,128)(2,1)S(1)} %get-tuple-element.33.plain_ref, bf16[128,8192]{1,0:T(8,128)(2,1)S(1)} %copy-done.1, ...), custom_call_target="tpu_custom_call" | custom-call | flops 2415919104 | bytes 4194304 | tf_op jit(solution)/shard_map/first_last/pallas_call | solution.py:204
  48.5 2.0 %collective-permute-done.6.partner_ref = bf16[5120,128]{1,0:T(8,128)(2,1)} collective-permute-done((bf16[5120,128]{1,0:T(8,128)(2,1)}, bf16[5120,128]{1,0:T(8,128)(2,1)}, u32[]{:S(2)}, u32[]{:S(2)}) %collective-permute-start.6) | collective-permute-done | bytes 1310752 | tf_op jit(solution)/shard_map/ppermute | solution.py:347
  50.4 6.1 %second_part.1.rest_0_ = f32[1152,128]{1,0:T(8,128)S(1)} custom-call(s32[6]{0:T(128)S(1)} %pad_add_fusion.switch_ref, bf16[128,8192]{1,0:T(8,128)(2,1)S(1)} %get-tuple-element.33.plain_ref, bf16[128,8192]{1,0:T(8,128)(2,1)S(1)} %copy-done.1, bf16[9,8192]{1,0:T(8,128)(2,1)S(1)} %pad_maximum_fusion.coeff_ref, bf16[5120,128]{1,0:T(8,128)(2,1)} %collective-permute-done.6.partner_ref), custom_call_target="tpu_custom_call" | custom-call | flops 1509949440 | bytes 3932160 | tf_op jit(solution)/shard_map/second_part/pallas_call | solution.py:281
  56.5 2.3 %collective-permute-done.5.partner_ref = bf16[3072,128]{1,0:T(8,128)(2,1)S(1)} collective-permute-done((bf16[3072,128]{1,0:T(8,128)(2,1)S(1)}, bf16[3072,128]{1,0:T(8,128)(2,1)S(1)}, u32[]{:S(2)}, u32[]{:S(2)}) %collective-permute-start.5) | collective-permute-done | bytes 786464 | tf_op jit(solution)/shard_map/ppermute | solution.py:352
  58.7 3.3 %second_last.1 = (bf16[9,128,128]{2,1,0:T(8,128)(2,1)S(1)}, bf16[9,128,128]{2,1,0:T(8,128)(2,1)S(1)}, bf16[9,128,128]{2,1,0:T(8,128)(2,1)S(1)}) custom-call(s32[6]{0:T(128)S(1)} %pad_add_fusion.switch_ref, bf16[128,8192]{1,0:T(8,128)(2,1)S(1)} %get-tuple-element.33.plain_ref, bf16[128,8192]{1,0:T(8,128)(2,1)S(1)} %copy-done.1, ...), custom_call_target="tpu_custom_call" | custom-call | flops 905969664 | bytes 2359296 | tf_op jit(solution)/shard_map/second_last/pallas_call | solution.py:281
  62.1 1.9 %collective-permute-start.7 = (bf16[9,128,128]{2,1,0:T(8,128)(2,1)S(1)}, bf16[9,128,128]{2,1,0:T(8,128)(2,1)S(1)}, u32[]{:S(2)}, u32[]{:S(2)}) collective-permute-start(bf16[9,128,128]{2,1,0:T(8,128)(2,1)S(1)} %get-tuple-element.49), channel_id=1, source_target_pairs={{0,8},{10,2},{13,5},{7,15},{9,1},{11,3},{4,12},{6,14},{1,0},{16,24... | collective-permute-start | bytes 884744 | tf_op jit(solution)/shard_map/ppermute | solution.py:361
  64.0 0.7 collective-permute-start.8
  64.7 5.7 %collective-permute-done.7 = bf16[9,128,128]{2,1,0:T(8,128)(2,1)S(1)} collective-permute-done((bf16[9,128,128]{2,1,0:T(8,128)(2,1)S(1)}, bf16[9,128,128]{2,1,0:T(8,128)(2,1)S(1)}, u32[]{:S(2)}, u32[]{:S(2)}) %collective-permute-start.7) | collective-permute-done | bytes 294944 | tf_op jit(solution)/shard_map/ppermute | solution.py:361
  70.4 0.9 %select_bitcast_fusion = (bf16[1,9,128,128]{3,2,1,0:T(8,128)(2,1)}, bf16[1,9,128,128]{3,2,1,0:T(8,128)(2,1)}) fusion(bf16[9,128,128]{2,1,0:T(8,128)(2,1)S(1)} %collective-permute-done.7, bf16[9,128,128]{2,1,0:T(8,128)(2,1)S(1)} %get-tuple-element.51, pred[]{:T(512)S(6)} %or.59, bf16[9,128,128]{2,1,0:T(8,128)(2,1)S(1)} %collective-permute-done.8, ...), kind=kLoop, calls=%fused_computation | loop fusion | flops 442368 | bytes 1769475 | tf_op jit(solution)/shard_map/broadcast_in_dim | solution.py:366
  (23 shorter events, 0.8 us)
Async XLA Ops:
  0.6 25.2 %collective-permute-start.1 = (bf16[8192,128]{1,0:T(8,128)(2,1)}, bf16[8192,128]{1,0:T(8,128)(2,1)}, u32[]{:S(2)}, u32[]{:S(2)}) collective-permute-start(bf16[8192,128]{1,0:T(8,128)(2,1)} %bitcast.15), channel_id=1, source_target_pairs={{3,2},{5,4},{6,5},{9,8},{10,9},{11,10},{12,11},{13,12},{14,13},{15... | collective-permute-start | bytes 6291464 | tf_op jit(solution)/shard_map/ppermute | solution.py:331
  2.6 23.2 %collective-permute-start.2 = (bf16[8192,128]{1,0:T(8,128)(2,1)}, bf16[8192,128]{1,0:T(8,128)(2,1)}, u32[]{:S(2)}, u32[]{:S(2)}) collective-permute-start(bf16[8192,128]{1,0:T(8,128)(2,1)} %bitcast.16), channel_id=1, source_target_pairs={{8,0},{2,10},{5,13},{15,7},{0,1},{7,6},{24,16},{18,26},{21,29},{31... | collective-permute-start | bytes 6291464 | tf_op jit(solution)/shard_map/ppermute | solution.py:332
  3.9 21.9 %collective-permute-start.3 = (s32[1,4]{1,0:T(1,128)}, s32[1,4]{1,0:T(1,128)S(1)}, u32[]{:S(2)}, u32[]{:S(2)}) collective-permute-start(s32[1,4]{1,0:T(1,128)} %param.3), channel_id=1, source_target_pairs={{3,2},{5,4},{6,5},{9,8},{10,9},{11,10},{12,11},{13,12},{14,13},{15... | collective-permute-start | bytes 56 | tf_op jit(solution)/shard_map/ppermute | solution.py:337
  4.6 21.2 %collective-permute-start.4 = (s32[1,4]{1,0:T(1,128)}, s32[1,4]{1,0:T(1,128)S(1)}, u32[]{:S(2)}, u32[]{:S(2)}) collective-permute-start(s32[1,4]{1,0:T(1,128)} %param.3), channel_id=1, source_target_pairs={{8,0},{2,10},{5,13},{15,7},{0,1},{7,6},{24,16},{18,26},{21,29},{31... | collective-permute-start | bytes 56 | tf_op jit(solution)/shard_map/ppermute | solution.py:336
  5.9 36.8 %collective-permute-start = (s32[1,4]{1,0:T(1,128)}, s32[1,4]{1,0:T(1,128)S(1)}, u32[]{:S(2)}, u32[]{:S(2)}) collective-permute-start(s32[1,4]{1,0:T(1,128)} %param.3), channel_id=1, source_target_pairs={{1,9},{3,11},{12,4},{14,6},{2,1},{4,3},{17,25},{19,27},{28,20},{30... | collective-permute-start | bytes 56 | tf_op jit(solution)/shard_map/ppermute | solution.py:338
  16.4 1.6 %copy-start.2 = (bf16[1024,2,4,128]{3,2,1,0:T(4,128)(2,1)S(1)}, bf16[1024,2,4,128]{3,2,1,0:T(4,128)(2,1)}, u32[]{:S(2)}) copy-start(bf16[1024,2,4,128]{3,2,1,0:T(4,128)(2,1)} %param.2) | copy-start | bytes 6291460
  21.1 1.4 %copy-start = (bf16[128,8192]{1,0:T(8,128)(2,1)}, bf16[128,8192]{1,0:T(8,128)(2,1)S(1)}, u32[]{:S(2)}) copy-start(bf16[128,8192]{1,0:T(8,128)(2,1)S(1)} %get-tuple-element.34.swapped_ref) | copy-start | bytes 6291460
  22.5 11.1 %copy-start.4 = (s32[1,4]{1,0:T(1,128)S(1)}, s32[1,4]{1,0:T(1,128)}, u32[]{:S(2)}) copy-start(s32[1,4]{1,0:T(1,128)} %param.3) | copy-start | bytes 52
  22.8 1.0 %copy-start.3 = (bf16[5120,128]{1,0:T(8,128)(2,1)}, bf16[5120,128]{1,0:T(8,128)(2,1)S(1)}, u32[]{:S(2)}) copy-start(bf16[5120,128]{1,0:T(8,128)(2,1)S(1)} %get-tuple-element.45) | copy-start | bytes 3932164
  25.8 24.6 %collective-permute-start.6 = (bf16[5120,128]{1,0:T(8,128)(2,1)}, bf16[5120,128]{1,0:T(8,128)(2,1)}, u32[]{:S(2)}, u32[]{:S(2)}) collective-permute-start(bf16[5120,128]{1,0:T(8,128)(2,1)} %copy-done.3), channel_id=1, source_target_pairs={{1,9},{3,11},{12,4},{14,6},{2,1},{4,3},{17,25},{19,27},{28,20},{30... | collective-permute-start | bytes 3932168 | tf_op jit(solution)/shard_map/ppermute | solution.py:347
  33.7 1.6 %copy-start.1 = (bf16[128,8192]{1,0:T(8,128)(2,1)S(1)}, bf16[128,8192]{1,0:T(8,128)(2,1)}, u32[]{:S(2)}) copy-start(bf16[128,8192]{1,0:T(8,128)(2,1)} %copy-done) | copy-start | bytes 6291460
  40.7 18.0 %collective-permute-start.5 = (bf16[3072,128]{1,0:T(8,128)(2,1)S(1)}, bf16[3072,128]{1,0:T(8,128)(2,1)S(1)}, u32[]{:S(2)}, u32[]{:S(2)}) collective-permute-start(bf16[3072,128]{1,0:T(8,128)(2,1)S(1)} %get-tuple-element.44), channel_id=1, source_target_pairs={{1,9},{3,11},{12,4},{14,6},{2,1},{4,3},{17,25},{19,27},{28,20},{30... | collective-permute-start | bytes 2359304 | tf_op jit(solution)/shard_map/ppermute | solution.py:352
  62.1 8.4 %collective-permute-start.7 = (bf16[9,128,128]{2,1,0:T(8,128)(2,1)S(1)}, bf16[9,128,128]{2,1,0:T(8,128)(2,1)S(1)}, u32[]{:S(2)}, u32[]{:S(2)}) collective-permute-start(bf16[9,128,128]{2,1,0:T(8,128)(2,1)S(1)} %get-tuple-element.49), channel_id=1, source_target_pairs={{0,8},{10,2},{13,5},{7,15},{9,1},{11,3},{4,12},{6,14},{1,0},{16,24... | collective-permute-start | bytes 884744 | tf_op jit(solution)/shard_map/ppermute | solution.py:361
  64.0 6.4 %collective-permute-start.8 = (bf16[9,128,128]{2,1,0:T(8,128)(2,1)S(1)}, bf16[9,128,128]{2,1,0:T(8,128)(2,1)S(1)}, u32[]{:S(2)}, u32[]{:S(2)}) collective-permute-start(bf16[9,128,128]{2,1,0:T(8,128)(2,1)S(1)} %get-tuple-element.50), channel_id=1, source_target_pairs={{0,7},{7,15},{16,23},{23,31}} | collective-permute-start | bytes 884744 | tf_op jit(solution)/shard_map/ppermute | solution.py:362

commit v26 on v23

--- a/solution.py
+++ b/solution.py
@@ -12,7 +12,7 @@
 LAGS = 2 * HL + 1
 STEP = 1024
 PARTS = (5, 8)
-PARAMS = pltpu.CompilerParams(vmem_limit_bytes=16 * 1024 * 1024)
+PARAMS = pltpu.CompilerParams(vmem_limit_bytes=28 * 1024 * 1024)
 
 
 def lag_rows(freq_count, window_count):

time: 69.7 us -> 69.7 us (level)
  no operation moved by 1% of the time
where the time goes in v26:
time: 69.7 us; the launch traced here: 69.2 us
  starting transfers between devices  27.8 us (40%)
  Pallas kernels  23.9 us (34%)
  waiting for transfers between devices  7.78 us (11%)
  local copies, waits for them, and re-layouts  5.57 us (8%)
  other arithmetic  3.15 us (5%)
  between operations  0.9 us (1%)
    pallas_call x2, Pallas kernels, first_sums(): pl.pallas_call(functools.partial(first_kernel, windows, bool(earlier)), g...  11.1 us
    ppermute x1, starting transfers between devices, local(): second_flags = lax.ppermute(quality, 'chan', second_pairs)[0]  10.5 us
    pallas_call x2, Pallas kernels, second_sums(): pl.pallas_call(functools.partial(second_kernel, windows, not earlier), gr...  9.36 us
    ppermute x1, starting transfers between devices, local(): second_in = [lax.ppermute(first_part, 'chan', second_pairs)]  7.59 us
    ppermute x1, waiting for transfers between devices, local(): returned = lax.ppermute(back, 'chan', back_pairs)  5.71 us
    unnamed x10, local copies, waits for them, and re-layouts  5.57 us
    pallas_call x1, Pallas kernels, turn(): pl.pallas_call(turn_kernel, grid=(rows // STEP,), in_specs=[pl.BlockSpec(...  3.15 us
    ppermute x1, waiting for transfers between devices, local(): second_in.append(lax.ppermute(last_part, 'chan', second_pairs))  2.05 us
  transfers between devices with their start and end apart: 9, of which 2 were waited for; matrix products, arithmetic and copies ran while one was open for 3% of the time, Pallas kernels for 30%

profile of v26, /device:TPU:1, one launch (start us, length us, event | category | flops | bytes accessed | tf_op | source)
XLA Modules:
  0.0 69.2 jit_solution(16170797134604733283)
XLA Ops:
  0.6 2.0 %collective-permute-start.1 = (bf16[8192,128]{1,0:T(8,128)(2,1)}, bf16[8192,128]{1,0:T(8,128)(2,1)}, u32[]{:S(2)}, u32[]{:S(2)}) collective-permute-start(bf16[8192,128]{1,0:T(8,128)(2,1)} %bitcast.15), channel_id=1, source_target_pairs={{3,2},{5,4},{6,5},{9,8},{10,9},{11,10},{12,11},{13,12},{14,13},{15... | collective-permute-start | bytes 6291464 | tf_op jit(solution)/shard_map/ppermute | solution.py:331
  2.6 1.3 %collective-permute-start.2 = (bf16[8192,128]{1,0:T(8,128)(2,1)}, bf16[8192,128]{1,0:T(8,128)(2,1)}, u32[]{:S(2)}, u32[]{:S(2)}) collective-permute-start(bf16[8192,128]{1,0:T(8,128)(2,1)} %bitcast.16), channel_id=1, source_target_pairs={{8,0},{5,13},{6,14},{15,7},{0,1},{7,6},{24,16},{21,29},{22,30},{31... | collective-permute-start | bytes 6291464 | tf_op jit(solution)/shard_map/ppermute | solution.py:332
  3.9 0.7 collective-permute-start.3
  4.6 1.3 %collective-permute-start.4 = (s32[1,4]{1,0:T(1,128)}, s32[1,4]{1,0:T(1,128)S(1)}, u32[]{:S(2)}, u32[]{:S(2)}) collective-permute-start(s32[1,4]{1,0:T(1,128)} %param.3), channel_id=1, source_target_pairs={{8,0},{5,13},{6,14},{15,7},{0,1},{7,6},{24,16},{21,29},{22,30},{31... | collective-permute-start | bytes 56 | tf_op jit(solution)/shard_map/ppermute | solution.py:336
  5.9 10.5 %collective-permute-start = (s32[1,4]{1,0:T(1,128)}, s32[1,4]{1,0:T(1,128)S(1)}, u32[]{:S(2)}, u32[]{:S(2)}) collective-permute-start(s32[1,4]{1,0:T(1,128)} %param.3), channel_id=1, source_target_pairs={{1,9},{10,2},{3,11},{12,4},{2,1},{4,3},{17,25},{26,18},{19,27},{28... | collective-permute-start | bytes 56 | tf_op jit(solution)/shard_map/ppermute | solution.py:338
  16.4 1.6 %copy-done.2 = bf16[1024,2,4,128]{3,2,1,0:T(4,128)(2,1)S(1)} copy-done((bf16[1024,2,4,128]{3,2,1,0:T(4,128)(2,1)S(1)}, bf16[1024,2,4,128]{3,2,1,0:T(4,128)(2,1)}, u32[]{:S(2)}) %copy-start.2) | copy-done | bytes 2097176
  18.0 3.2 %turn.1 = (bf16[128,8192]{1,0:T(8,128)(2,1)S(1)}, bf16[128,8192]{1,0:T(8,128)(2,1)S(1)}) custom-call(bf16[8192,128]{1,0:T(8,128)(2,1)S(1)} %bitcast.17), custom_call_target="tpu_custom_call" | custom-call | bytes 6291456 | tf_op jit(solution)/shard_map/turn/pallas_call | solution.py:85
  21.2 1.3 %copy-done = bf16[128,8192]{1,0:T(8,128)(2,1)} copy-done((bf16[128,8192]{1,0:T(8,128)(2,1)}, bf16[128,8192]{1,0:T(8,128)(2,1)S(1)}, u32[]{:S(2)}) %copy-start) | copy-done | bytes 2097176
  22.5 0.3 split.1
  22.8 1.0 %copy-done.3 = bf16[5120,128]{1,0:T(8,128)(2,1)} copy-done((bf16[5120,128]{1,0:T(8,128)(2,1)}, bf16[5120,128]{1,0:T(8,128)(2,1)S(1)}, u32[]{:S(2)}) %copy-start.3) | copy-done | bytes 1310744
  23.9 0.9 %multiply_convert_fusion = (bf16[5,8192]{1,0:T(8,128)(2,1)S(1)}, f32[5,8192]{1,0:T(8,128)S(1)}) fusion(f32[8192]{0:T(1024)S(1)} %fusion.9, f32[5]{0:T(128)S(1)} %iota_multiply_fusion), kind=kLoop, calls=%fused_computation.4 | loop fusion | flops 122880 | bytes 278548 | tf_op jit(solution)/shard_map/convert
  24.8 0.9 %fusion.2 = bf16[4,8192]{1,0:T(4,128)(2,1)S(1)} fusion(f32[5,8192]{1,0:T(8,128)S(1)} %get-tuple-element.55, f32[8192]{0:T(1024)S(1)} %select_multiply_fusion), kind=kLoop, calls=%fused_computation.8 | loop fusion | flops 98304 | bytes 229376 | tf_op jit(solution)/shard_map/convert.1
  25.8 7.6 %collective-permute-start.6 = (bf16[5120,128]{1,0:T(8,128)(2,1)}, bf16[5120,128]{1,0:T(8,128)(2,1)}, u32[]{:S(2)}, u32[]{:S(2)}) collective-permute-start(bf16[5120,128]{1,0:T(8,128)(2,1)} %copy-done.3), channel_id=1, source_target_pairs={{1,9},{10,2},{3,11},{12,4},{2,1},{4,3},{17,25},{26,18},{19,27},{28... | collective-permute-start | bytes 3932168 | tf_op jit(solution)/shard_map/ppermute | solution.py:347
  33.7 1.6 %copy-done.1 = bf16[128,8192]{1,0:T(8,128)(2,1)S(1)} copy-done((bf16[128,8192]{1,0:T(8,128)(2,1)S(1)}, bf16[128,8192]{1,0:T(8,128)(2,1)}, u32[]{:S(2)}) %copy-start.1) | copy-done | bytes 2097176
  35.3 5.5 %first_half.1 = (f32[1152,256]{1,0:T(8,128)S(1)}, f32[8,128]{1,0:T(8,128)S(1)}) custom-call(s32[14]{0:T(128)S(1)} %pad_add_fusion.1.switch_ref, bf16[128,8192]{1,0:T(8,128)(2,1)S(1)} %get-tuple-element.33.plain_ref, bf16[128,8192]{1,0:T(8,128)(2,1)S(1)} %copy-done.1, bf16[9,8192]{1,0:T(8,128)(2,1)S(1)} %pad_maximum_fusion.coeff_ref, ...), custom_call_target="tpu_custom_call" | custom-call | flops 2415919104 | bytes 4194304 | tf_op jit(solution)/shard_map/first_half/pallas_call | solution.py:204
  40.7 1.9 %collective-permute-start.5 = (bf16[3072,128]{1,0:T(8,128)(2,1)S(1)}, bf16[3072,128]{1,0:T(8,128)(2,1)S(1)}, u32[]{:S(2)}, u32[]{:S(2)}) collective-permute-start(bf16[3072,128]{1,0:T(8,128)(2,1)S(1)} %get-tuple-element.44), channel_id=1, source_target_pairs={{1,9},{10,2},{3,11},{12,4},{2,1},{4,3},{17,25},{26,18},{19,27},{28... | collective-permute-start | bytes 2359304 | tf_op jit(solution)/shard_map/ppermute | solution.py:352
  42.8 5.7 %first_last.1 = (bf16[9,128,128]{2,1,0:T(8,128)(2,1)S(1)}, bf16[9,128,128]{2,1,0:T(8,128)(2,1)S(1)}, bf16[9,128,128]{2,1,0:T(8,128)(2,1)S(1)}) custom-call(s32[14]{0:T(128)S(1)} %pad_add_fusion.1.switch_ref, bf16[128,8192]{1,0:T(8,128)(2,1)S(1)} %get-tuple-element.33.plain_ref, bf16[128,8192]{1,0:T(8,128)(2,1)S(1)} %copy-done.1, ...), custom_call_target="tpu_custom_call" | custom-call | flops 2415919104 | bytes 4194304 | tf_op jit(solution)/shard_map/first_last/pallas_call | solution.py:204
  48.5 6.1 %second_part.1.rest_0_ = f32[1152,128]{1,0:T(8,128)S(1)} custom-call(s32[6]{0:T(128)S(1)} %pad_add_fusion.switch_ref, bf16[128,8192]{1,0:T(8,128)(2,1)S(1)} %get-tuple-element.33.plain_ref, bf16[128,8192]{1,0:T(8,128)(2,1)S(1)} %copy-done.1, bf16[9,8192]{1,0:T(8,128)(2,1)S(1)} %pad_maximum_fusion.coeff_ref, bf16[5120,128]{1,0:T(8,128)(2,1)} %collective-permute-done.6.partner_ref), custom_call_target="tpu_custom_call" | custom-call | flops 1509949440 | bytes 3932160 | tf_op jit(solution)/shard_map/second_part/pallas_call | solution.py:281
  54.5 2.1 %collective-permute-done.5.partner_ref = bf16[3072,128]{1,0:T(8,128)(2,1)S(1)} collective-permute-done((bf16[3072,128]{1,0:T(8,128)(2,1)S(1)}, bf16[3072,128]{1,0:T(8,128)(2,1)S(1)}, u32[]{:S(2)}, u32[]{:S(2)}) %collective-permute-start.5) | collective-permute-done | bytes 786464 | tf_op jit(solution)/shard_map/ppermute | solution.py:352
  56.6 3.3 %second_last.1 = (bf16[9,128,128]{2,1,0:T(8,128)(2,1)S(1)}, bf16[9,128,128]{2,1,0:T(8,128)(2,1)S(1)}, bf16[9,128,128]{2,1,0:T(8,128)(2,1)S(1)}) custom-call(s32[6]{0:T(128)S(1)} %pad_add_fusion.switch_ref, bf16[128,8192]{1,0:T(8,128)(2,1)S(1)} %get-tuple-element.33.plain_ref, bf16[128,8192]{1,0:T(8,128)(2,1)S(1)} %copy-done.1, ...), custom_call_target="tpu_custom_call" | custom-call | flops 905969664 | bytes 2359296 | tf_op jit(solution)/shard_map/second_last/pallas_call | solution.py:281
  59.9 1.9 %collective-permute-start.7 = (bf16[9,128,128]{2,1,0:T(8,128)(2,1)S(1)}, bf16[9,128,128]{2,1,0:T(8,128)(2,1)S(1)}, u32[]{:S(2)}, u32[]{:S(2)}) collective-permute-start(bf16[9,128,128]{2,1,0:T(8,128)(2,1)S(1)} %get-tuple-element.49), channel_id=1, source_target_pairs={{0,8},{13,5},{14,6},{7,15},{9,1},{2,10},{11,3},{4,12},{1,0},{16,24... | collective-permute-start | bytes 884744 | tf_op jit(solution)/shard_map/ppermute | solution.py:361
  61.8 0.7 collective-permute-start.8
  62.6 5.7 %collective-permute-done.7 = bf16[9,128,128]{2,1,0:T(8,128)(2,1)S(1)} collective-permute-done((bf16[9,128,128]{2,1,0:T(8,128)(2,1)S(1)}, bf16[9,128,128]{2,1,0:T(8,128)(2,1)S(1)}, u32[]{:S(2)}, u32[]{:S(2)}) %collective-permute-start.7) | collective-permute-done | bytes 294944 | tf_op jit(solution)/shard_map/ppermute | solution.py:361
  68.3 0.9 %select_bitcast_fusion = (bf16[1,9,128,128]{3,2,1,0:T(8,128)(2,1)}, bf16[1,9,128,128]{3,2,1,0:T(8,128)(2,1)}) fusion(bf16[9,128,128]{2,1,0:T(8,128)(2,1)S(1)} %collective-permute-done.7, bf16[9,128,128]{2,1,0:T(8,128)(2,1)S(1)} %get-tuple-element.51, pred[]{:T(512)S(6)} %or.59, bf16[9,128,128]{2,1,0:T(8,128)(2,1)S(1)} %collective-permute-done.8, ...), kind=kLoop, calls=%fused_computation | loop fusion | flops 442368 | bytes 1769475 | tf_op jit(solution)/shard_map/broadcast_in_dim | solution.py:366
  (23 shorter events, 0.5 us)
Async XLA Ops:
  0.6 25.2 %collective-permute-start.1 = (bf16[8192,128]{1,0:T(8,128)(2,1)}, bf16[8192,128]{1,0:T(8,128)(2,1)}, u32[]{:S(2)}, u32[]{:S(2)}) collective-permute-start(bf16[8192,128]{1,0:T(8,128)(2,1)} %bitcast.15), channel_id=1, source_target_pairs={{3,2},{5,4},{6,5},{9,8},{10,9},{11,10},{12,11},{13,12},{14,13},{15... | collective-permute-start | bytes 6291464 | tf_op jit(solution)/shard_map/ppermute | solution.py:331
  2.6 23.2 %collective-permute-start.2 = (bf16[8192,128]{1,0:T(8,128)(2,1)}, bf16[8192,128]{1,0:T(8,128)(2,1)}, u32[]{:S(2)}, u32[]{:S(2)}) collective-permute-start(bf16[8192,128]{1,0:T(8,128)(2,1)} %bitcast.16), channel_id=1, source_target_pairs={{8,0},{5,13},{6,14},{15,7},{0,1},{7,6},{24,16},{21,29},{22,30},{31... | collective-permute-start | bytes 6291464 | tf_op jit(solution)/shard_map/ppermute | solution.py:332
  3.9 21.9 %collective-permute-start.3 = (s32[1,4]{1,0:T(1,128)}, s32[1,4]{1,0:T(1,128)S(1)}, u32[]{:S(2)}, u32[]{:S(2)}) collective-permute-start(s32[1,4]{1,0:T(1,128)} %param.3), channel_id=1, source_target_pairs={{3,2},{5,4},{6,5},{9,8},{10,9},{11,10},{12,11},{13,12},{14,13},{15... | collective-permute-start | bytes 56 | tf_op jit(solution)/shard_map/ppermute | solution.py:337
  4.6 21.2 %collective-permute-start.4 = (s32[1,4]{1,0:T(1,128)}, s32[1,4]{1,0:T(1,128)S(1)}, u32[]{:S(2)}, u32[]{:S(2)}) collective-permute-start(s32[1,4]{1,0:T(1,128)} %param.3), channel_id=1, source_target_pairs={{8,0},{5,13},{6,14},{15,7},{0,1},{7,6},{24,16},{21,29},{22,30},{31... | collective-permute-start | bytes 56 | tf_op jit(solution)/shard_map/ppermute | solution.py:336
  5.9 36.8 %collective-permute-start = (s32[1,4]{1,0:T(1,128)}, s32[1,4]{1,0:T(1,128)S(1)}, u32[]{:S(2)}, u32[]{:S(2)}) collective-permute-start(s32[1,4]{1,0:T(1,128)} %param.3), channel_id=1, source_target_pairs={{1,9},{10,2},{3,11},{12,4},{2,1},{4,3},{17,25},{26,18},{19,27},{28... | collective-permute-start | bytes 56 | tf_op jit(solution)/shard_map/ppermute | solution.py:338
  16.4 1.6 %copy-start.2 = (bf16[1024,2,4,128]{3,2,1,0:T(4,128)(2,1)S(1)}, bf16[1024,2,4,128]{3,2,1,0:T(4,128)(2,1)}, u32[]{:S(2)}) copy-start(bf16[1024,2,4,128]{3,2,1,0:T(4,128)(2,1)} %param.2) | copy-start | bytes 6291460
  21.1 1.4 %copy-start = (bf16[128,8192]{1,0:T(8,128)(2,1)}, bf16[128,8192]{1,0:T(8,128)(2,1)S(1)}, u32[]{:S(2)}) copy-start(bf16[128,8192]{1,0:T(8,128)(2,1)S(1)} %get-tuple-element.34.swapped_ref) | copy-start | bytes 6291460
  22.5 11.1 %copy-start.4 = (s32[1,4]{1,0:T(1,128)S(1)}, s32[1,4]{1,0:T(1,128)}, u32[]{:S(2)}) copy-start(s32[1,4]{1,0:T(1,128)} %param.3) | copy-start | bytes 52
  22.8 1.0 %copy-start.3 = (bf16[5120,128]{1,0:T(8,128)(2,1)}, bf16[5120,128]{1,0:T(8,128)(2,1)S(1)}, u32[]{:S(2)}) copy-start(bf16[5120,128]{1,0:T(8,128)(2,1)S(1)} %get-tuple-element.45) | copy-start | bytes 3932164
  25.8 22.6 %collective-permute-start.6 = (bf16[5120,128]{1,0:T(8,128)(2,1)}, bf16[5120,128]{1,0:T(8,128)(2,1)}, u32[]{:S(2)}, u32[]{:S(2)}) collective-permute-start(bf16[5120,128]{1,0:T(8,128)(2,1)} %copy-done.3), channel_id=1, source_target_pairs={{1,9},{10,2},{3,11},{12,4},{2,1},{4,3},{17,25},{26,18},{19,27},{28... | collective-permute-start | bytes 3932168 | tf_op jit(solution)/shard_map/ppermute | solution.py:347
  33.7 1.6 %copy-start.1 = (bf16[128,8192]{1,0:T(8,128)(2,1)S(1)}, bf16[128,8192]{1,0:T(8,128)(2,1)}, u32[]{:S(2)}) copy-start(bf16[128,8192]{1,0:T(8,128)(2,1)} %copy-done) | copy-start | bytes 6291460
  40.7 15.9 %collective-permute-start.5 = (bf16[3072,128]{1,0:T(8,128)(2,1)S(1)}, bf16[3072,128]{1,0:T(8,128)(2,1)S(1)}, u32[]{:S(2)}, u32[]{:S(2)}) collective-permute-start(bf16[3072,128]{1,0:T(8,128)(2,1)S(1)} %get-tuple-element.44), channel_id=1, source_target_pairs={{1,9},{10,2},{3,11},{12,4},{2,1},{4,3},{17,25},{26,18},{19,27},{28... | collective-permute-start | bytes 2359304 | tf_op jit(solution)/shard_map/ppermute | solution.py:352
  59.9 8.4 %collective-permute-start.7 = (bf16[9,128,128]{2,1,0:T(8,128)(2,1)S(1)}, bf16[9,128,128]{2,1,0:T(8,128)(2,1)S(1)}, u32[]{:S(2)}, u32[]{:S(2)}) collective-permute-start(bf16[9,128,128]{2,1,0:T(8,128)(2,1)S(1)} %get-tuple-element.49), channel_id=1, source_target_pairs={{0,8},{13,5},{14,6},{7,15},{9,1},{2,10},{11,3},{4,12},{1,0},{16,24... | collective-permute-start | bytes 884744 | tf_op jit(solution)/shard_map/ppermute | solution.py:361
  61.8 6.4 %collective-permute-start.8 = (bf16[9,128,128]{2,1,0:T(8,128)(2,1)S(1)}, bf16[9,128,128]{2,1,0:T(8,128)(2,1)S(1)}, u32[]{:S(2)}, u32[]{:S(2)}) collective-permute-start(bf16[9,128,128]{2,1,0:T(8,128)(2,1)S(1)} %get-tuple-element.50), channel_id=1, source_target_pairs={{0,7},{7,15},{16,23},{23,31}} | collective-permute-start | bytes 884744 | tf_op jit(solution)/shard_map/ppermute | solution.py:362

commit v27 on v23

--- a/solution.py
+++ b/solution.py
@@ -59,15 +59,21 @@
     )(x)
 
 
+def identity(size):
+    same = lax.broadcasted_iota(jnp.int32, (size, size), 0) == lax.broadcasted_iota(jnp.int32, (size, size), 1)
+    return jnp.where(same, 1.0, 0.0).astype(jnp.bfloat16)
+
+
+def across(a, b):
+    return lax.dot_general(a, b, (((1,), (1,)), ((), ())), preferred_element_type=jnp.float32)
+
+
 def turned(x):
     rows, cols = x.shape
-    same = lax.broadcasted_iota(jnp.int32, (cols, cols), 0) == lax.broadcasted_iota(jnp.int32, (cols, cols), 1)
-    eye = jnp.where(same, 1.0, 0.0).astype(jnp.bfloat16)
     source = lax.broadcasted_iota(jnp.int32, (2 * cols, 2 * cols), 0)
     target = lax.broadcasted_iota(jnp.int32, (2 * cols, 2 * cols), 1)
     exchange = jnp.where((source ^ 4) == target, 1.0, 0.0).astype(jnp.bfloat16)
-    plain = lax.dot_general(eye, x, (((1,), (1,)), ((), ())), preferred_element_type=jnp.float32)
-    plain = plain.astype(jnp.bfloat16)
+    plain = across(identity(cols), x).astype(jnp.bfloat16)
     swapped = [
         jnp.dot(plain[:, t:t + 2 * cols], exchange, preferred_element_type=jnp.float32).astype(jnp.bfloat16)
         for t in range(0, rows, 2 * cols)
@@ -219,6 +225,20 @@
     )(switch, *own, coeffs, near_in, first_in, *earlier)
 
 
+def write_turned_lags(out, acc, cols, mirrored):
+    for lag in range(LAGS):
+        k = abs(lag - HL)
+        value = acc[:, k * cols:(k + 1) * cols]
+        if k:
+            odd = acc[:, (HL + k) * cols:(HL + k + 1) * cols]
+            value = value + odd if lag > HL else value - odd
+        value = value.astype(jnp.bfloat16)
+        if mirrored:
+            out[LAGS - 1 - lag] = value
+        else:
+            out[lag] = value.T
+
+
 def second_kernel(windows, first, switch_ref, plain_ref, swapped_ref, coeff_ref, partner_ref, *rest):
     on, late_near = switch_ref[0], switch_ref[1]
     step = pl.program_id(0)
@@ -236,24 +256,23 @@
 
         scale(scaled, plain_ref[...], swapped_ref[...], coeff_ref)
         partner = weigh(partner_ref[...], [switch_ref[2 + w] for w in range(windows)])
-        acc[...] += jnp.dot(scaled[...], partner, preferred_element_type=jnp.float32)
+        columns = across(identity(cols), partner).astype(jnp.bfloat16)
+        acc[...] += across(columns, scaled[...])
 
     if not first:
         @pl.when(step == pl.num_programs(0) - 1)
         def _():
-            here = slice(0, cols)
-
             @pl.when((on != 0) & (late_near == 0))
             def _():
-                write_lags(back_out, acc, here, cols, True)
-                write_lags(far_out, acc, here, cols, False)
+                write_turned_lags(back_out, acc, cols, True)
+                write_turned_lags(far_out, acc, cols, False)
 
             @pl.when((on == 0) | (late_near != 0))
             def _():
                 back_out[...] = back_in[...]
                 far_out[...] = far_in[...]
 
-            pl.when(late_near != 0)(lambda: write_lags(near_out, acc, here, cols, False))
+            pl.when(late_near != 0)(lambda: write_turned_lags(near_out, acc, cols, False))
 
             @pl.when(late_near == 0)
             def _():
@@ -264,7 +283,7 @@
     rows, cols = partner.shape
     windows = switch.shape[0] - 2
     skip = start // STEP
-    total = jax.ShapeDtypeStruct((LAGS * cols, cols), jnp.float32)
+    total = jax.ShapeDtypeStruct((cols, LAGS * cols), jnp.float32)
     total_spec = pl.BlockSpec(total.shape, lambda s, on: (0, 0))
     result = jax.ShapeDtypeStruct((LAGS, cols, cols), jnp.bfloat16)
     result_spec = pl.BlockSpec(result.shape, lambda s, on: (0, 0, 0))

time: 69.7 us -> 70.4 us (1.010)
  Pallas kernels: 23.9 us -> 25.6 us
  waiting for transfers between devices: 7.78 us -> 6.88 us
    pallas_call x2, Pallas kernels: 9.36 us -> 11 us  [second_sums(): pl.pallas_call(functools.partial(second_kernel, windows, not earlier), gr...]
    ppermute x1, waiting for transfers between devices: 2.05 us -> 1.15 us  [local(): second_in.append(lax.ppermute(last_part, 'chan', second_pairs))]
  transfers between devices with their start and end apart: 9 -> 9, of which waited for: 2 -> 2; matrix products, arithmetic and copies ran while one was open for 3% -> 3% of each run, Pallas kernels for 30% -> 31%
where the time goes in v27:
time: 70.4 us; the launch traced here: 69.9 us
  starting transfers between devices  27.8 us (39%)
  Pallas kernels  25.6 us (36%)
  waiting for transfers between devices  6.88 us (10%)
  local copies, waits for them, and re-layouts  5.57 us (8%)
  other arithmetic  3.15 us (4%)
  between operations  0.9 us (1%)
    pallas_call x2, Pallas kernels, first_sums(): pl.pallas_call(functools.partial(first_kernel, windows, bool(earlier)), g...  11.1 us
    pallas_call x2, Pallas kernels, second_sums(): pl.pallas_call(functools.partial(second_kernel, windows, not earlier), gr...  11 us
    ppermute x1, starting transfers between devices, local(): second_flags = lax.ppermute(quality, 'chan', second_pairs)[0]  10.5 us
    ppermute x1, starting transfers between devices, local(): second_in = [lax.ppermute(first_part, 'chan', second_pairs)]  7.59 us
    ppermute x1, waiting for transfers between devices, local(): returned = lax.ppermute(back, 'chan', back_pairs)  5.71 us
    unnamed x10, local copies, waits for them, and re-layouts  5.57 us
    pallas_call x1, Pallas kernels, turn(): pl.pallas_call(turn_kernel, grid=(rows // STEP,), in_specs=[pl.BlockSpec(...  3.15 us
    ppermute x1, starting transfers between devices, local(): near_in = lax.ppermute(block, 'chan', near_pairs)  2.01 us
  transfers between devices with their start and end apart: 9, of which 2 were waited for; matrix products, arithmetic and copies ran while one was open for 3% of the time, Pallas kernels for 31%

profile of v27, /device:TPU:1, one launch (start us, length us, event | category | flops | bytes accessed | tf_op | source)
XLA Modules:
  0.0 69.9 jit_solution(12245683094205778030)
XLA Ops:
  0.6 2.0 %collective-permute-start.1 = (bf16[8192,128]{1,0:T(8,128)(2,1)}, bf16[8192,128]{1,0:T(8,128)(2,1)}, u32[]{:S(2)}, u32[]{:S(2)}) collective-permute-start(bf16[8192,128]{1,0:T(8,128)(2,1)} %bitcast.15), channel_id=1, source_target_pairs={{3,2},{5,4},{6,5},{9,8},{10,9},{11,10},{12,11},{13,12},{14,13},{15... | collective-permute-start | bytes 6291464 | tf_op jit(solution)/shard_map/ppermute | solution.py:350
  2.6 1.3 %collective-permute-start.2 = (bf16[8192,128]{1,0:T(8,128)(2,1)}, bf16[8192,128]{1,0:T(8,128)(2,1)}, u32[]{:S(2)}, u32[]{:S(2)}) collective-permute-start(bf16[8192,128]{1,0:T(8,128)(2,1)} %bitcast.16), channel_id=1, source_target_pairs={{8,0},{5,13},{6,14},{15,7},{0,1},{7,6},{24,16},{21,29},{22,30},{31... | collective-permute-start | bytes 6291464 | tf_op jit(solution)/shard_map/ppermute | solution.py:351
  3.9 0.7 collective-permute-start.3
  4.6 1.3 %collective-permute-start.4 = (s32[1,4]{1,0:T(1,128)}, s32[1,4]{1,0:T(1,128)S(1)}, u32[]{:S(2)}, u32[]{:S(2)}) collective-permute-start(s32[1,4]{1,0:T(1,128)} %param.3), channel_id=1, source_target_pairs={{8,0},{5,13},{6,14},{15,7},{0,1},{7,6},{24,16},{21,29},{22,30},{31... | collective-permute-start | bytes 56 | tf_op jit(solution)/shard_map/ppermute | solution.py:355
  5.9 10.5 %collective-permute-start = (s32[1,4]{1,0:T(1,128)}, s32[1,4]{1,0:T(1,128)S(1)}, u32[]{:S(2)}, u32[]{:S(2)}) collective-permute-start(s32[1,4]{1,0:T(1,128)} %param.3), channel_id=1, source_target_pairs={{1,9},{10,2},{3,11},{12,4},{2,1},{4,3},{17,25},{26,18},{19,27},{28... | collective-permute-start | bytes 56 | tf_op jit(solution)/shard_map/ppermute | solution.py:357
  16.4 1.6 %copy-done.2 = bf16[1024,2,4,128]{3,2,1,0:T(4,128)(2,1)S(1)} copy-done((bf16[1024,2,4,128]{3,2,1,0:T(4,128)(2,1)S(1)}, bf16[1024,2,4,128]{3,2,1,0:T(4,128)(2,1)}, u32[]{:S(2)}) %copy-start.2) | copy-done | bytes 2097176
  18.0 3.2 %turn.1 = (bf16[128,8192]{1,0:T(8,128)(2,1)S(1)}, bf16[128,8192]{1,0:T(8,128)(2,1)S(1)}) custom-call(bf16[8192,128]{1,0:T(8,128)(2,1)S(1)} %bitcast.17), custom_call_target="tpu_custom_call" | custom-call | bytes 6291456 | tf_op jit(solution)/shard_map/turn/pallas_call | solution.py:91
  21.2 1.3 %copy-done = bf16[128,8192]{1,0:T(8,128)(2,1)} copy-done((bf16[128,8192]{1,0:T(8,128)(2,1)}, bf16[128,8192]{1,0:T(8,128)(2,1)S(1)}, u32[]{:S(2)}) %copy-start) | copy-done | bytes 2097176
  22.5 0.3 split.1
  22.8 1.0 %copy-done.3 = bf16[5120,128]{1,0:T(8,128)(2,1)} copy-done((bf16[5120,128]{1,0:T(8,128)(2,1)}, bf16[5120,128]{1,0:T(8,128)(2,1)S(1)}, u32[]{:S(2)}) %copy-start.3) | copy-done | bytes 1310744
  23.9 0.9 %multiply_convert_fusion = (bf16[5,8192]{1,0:T(8,128)(2,1)S(1)}, f32[5,8192]{1,0:T(8,128)S(1)}) fusion(f32[8192]{0:T(1024)S(1)} %fusion.9, f32[5]{0:T(128)S(1)} %iota_multiply_fusion), kind=kLoop, calls=%fused_computation.4 | loop fusion | flops 122880 | bytes 278548 | tf_op jit(solution)/shard_map/convert
  24.8 0.9 %fusion.2 = bf16[4,8192]{1,0:T(4,128)(2,1)S(1)} fusion(f32[5,8192]{1,0:T(8,128)S(1)} %get-tuple-element.55, f32[8192]{0:T(1024)S(1)} %select_multiply_fusion), kind=kLoop, calls=%fused_computation.8 | loop fusion | flops 98304 | bytes 229376 | tf_op jit(solution)/shard_map/convert.1
  25.8 7.6 %collective-permute-start.6 = (bf16[5120,128]{1,0:T(8,128)(2,1)}, bf16[5120,128]{1,0:T(8,128)(2,1)}, u32[]{:S(2)}, u32[]{:S(2)}) collective-permute-start(bf16[5120,128]{1,0:T(8,128)(2,1)} %copy-done.3), channel_id=1, source_target_pairs={{1,9},{10,2},{3,11},{12,4},{2,1},{4,3},{17,25},{26,18},{19,27},{28... | collective-permute-start | bytes 3932168 | tf_op jit(solution)/shard_map/ppermute | solution.py:366
  33.7 1.6 %copy-done.1 = bf16[128,8192]{1,0:T(8,128)(2,1)S(1)} copy-done((bf16[128,8192]{1,0:T(8,128)(2,1)S(1)}, bf16[128,8192]{1,0:T(8,128)(2,1)}, u32[]{:S(2)}) %copy-start.1) | copy-done | bytes 2097176
  35.3 5.5 %first_half.1 = (f32[1152,256]{1,0:T(8,128)S(1)}, f32[8,128]{1,0:T(8,128)S(1)}) custom-call(s32[14]{0:T(128)S(1)} %pad_add_fusion.1.switch_ref, bf16[128,8192]{1,0:T(8,128)(2,1)S(1)} %get-tuple-element.33.plain_ref, bf16[128,8192]{1,0:T(8,128)(2,1)S(1)} %copy-done.1, bf16[9,8192]{1,0:T(8,128)(2,1)S(1)} %pad_maximum_fusion.coeff_ref, ...), custom_call_target="tpu_custom_call" | custom-call | flops 2415919104 | bytes 4194304 | tf_op jit(solution)/shard_map/first_half/pallas_call | solution.py:210
  40.7 1.9 %collective-permute-start.5 = (bf16[3072,128]{1,0:T(8,128)(2,1)S(1)}, bf16[3072,128]{1,0:T(8,128)(2,1)S(1)}, u32[]{:S(2)}, u32[]{:S(2)}) collective-permute-start(bf16[3072,128]{1,0:T(8,128)(2,1)S(1)} %get-tuple-element.44), channel_id=1, source_target_pairs={{1,9},{10,2},{3,11},{12,4},{2,1},{4,3},{17,25},{26,18},{19,27},{28... | collective-permute-start | bytes 2359304 | tf_op jit(solution)/shard_map/ppermute | solution.py:371
  42.8 5.7 %first_last.1 = (bf16[9,128,128]{2,1,0:T(8,128)(2,1)S(1)}, bf16[9,128,128]{2,1,0:T(8,128)(2,1)S(1)}, bf16[9,128,128]{2,1,0:T(8,128)(2,1)S(1)}) custom-call(s32[14]{0:T(128)S(1)} %pad_add_fusion.1.switch_ref, bf16[128,8192]{1,0:T(8,128)(2,1)S(1)} %get-tuple-element.33.plain_ref, bf16[128,8192]{1,0:T(8,128)(2,1)S(1)} %copy-done.1, ...), custom_call_target="tpu_custom_call" | custom-call | flops 2415919104 | bytes 4194304 | tf_op jit(solution)/shard_map/first_last/pallas_call | solution.py:210
  48.5 7.0 %second_part.1.rest_0_ = f32[128,1152]{1,0:T(8,128)S(1)} custom-call(s32[6]{0:T(128)S(1)} %pad_add_fusion.switch_ref, bf16[128,8192]{1,0:T(8,128)(2,1)S(1)} %get-tuple-element.33.plain_ref, bf16[128,8192]{1,0:T(8,128)(2,1)S(1)} %copy-done.1, bf16[9,8192]{1,0:T(8,128)(2,1)S(1)} %pad_maximum_fusion.coeff_ref, bf16[5120,128]{1,0:T(8,128)(2,1)} %collective-permute-done.6.partner_ref), custom_call_target="tpu_custom_call" | custom-call | flops 1509949440 | bytes 3932160 | tf_op jit(solution)/shard_map/second_part/pallas_call | solution.py:300
  55.4 1.2 %collective-permute-done.5.partner_ref = bf16[3072,128]{1,0:T(8,128)(2,1)S(1)} collective-permute-done((bf16[3072,128]{1,0:T(8,128)(2,1)S(1)}, bf16[3072,128]{1,0:T(8,128)(2,1)S(1)}, u32[]{:S(2)}, u32[]{:S(2)}) %collective-permute-start.5) | collective-permute-done | bytes 786464 | tf_op jit(solution)/shard_map/ppermute | solution.py:371
  56.6 4.1 %second_last.1 = (bf16[9,128,128]{2,1,0:T(8,128)(2,1)S(1)}, bf16[9,128,128]{2,1,0:T(8,128)(2,1)S(1)}, bf16[9,128,128]{2,1,0:T(8,128)(2,1)S(1)}) custom-call(s32[6]{0:T(128)S(1)} %pad_add_fusion.switch_ref, bf16[128,8192]{1,0:T(8,128)(2,1)S(1)} %get-tuple-element.33.plain_ref, bf16[128,8192]{1,0:T(8,128)(2,1)S(1)} %copy-done.1, ...), custom_call_target="tpu_custom_call" | custom-call | flops 905969664 | bytes 2359296 | tf_op jit(solution)/shard_map/second_last/pallas_call | solution.py:300
  60.7 1.9 %collective-permute-start.7 = (bf16[9,128,128]{2,1,0:T(8,128)(2,1)S(1)}, bf16[9,128,128]{2,1,0:T(8,128)(2,1)S(1)}, u32[]{:S(2)}, u32[]{:S(2)}) collective-permute-start(bf16[9,128,128]{2,1,0:T(8,128)(2,1)S(1)} %get-tuple-element.49), channel_id=1, source_target_pairs={{0,8},{13,5},{14,6},{7,15},{9,1},{2,10},{11,3},{4,12},{1,0},{16,24... | collective-permute-start | bytes 884744 | tf_op jit(solution)/shard_map/ppermute | solution.py:380
  62.6 0.7 collective-permute-start.8
  63.3 5.7 %collective-permute-done.7 = bf16[9,128,128]{2,1,0:T(8,128)(2,1)S(1)} collective-permute-done((bf16[9,128,128]{2,1,0:T(8,128)(2,1)S(1)}, bf16[9,128,128]{2,1,0:T(8,128)(2,1)S(1)}, u32[]{:S(2)}, u32[]{:S(2)}) %collective-permute-start.7) | collective-permute-done | bytes 294944 | tf_op jit(solution)/shard_map/ppermute | solution.py:380
  69.0 0.9 %select_bitcast_fusion = (bf16[1,9,128,128]{3,2,1,0:T(8,128)(2,1)}, bf16[1,9,128,128]{3,2,1,0:T(8,128)(2,1)}) fusion(bf16[9,128,128]{2,1,0:T(8,128)(2,1)S(1)} %collective-permute-done.7, bf16[9,128,128]{2,1,0:T(8,128)(2,1)S(1)} %get-tuple-element.51, pred[]{:T(512)S(6)} %or.59, bf16[9,128,128]{2,1,0:T(8,128)(2,1)S(1)} %collective-permute-done.8, ...), kind=kLoop, calls=%fused_computation | loop fusion | flops 442368 | bytes 1769475 | tf_op jit(solution)/shard_map/broadcast_in_dim | solution.py:385
  (23 shorter events, 0.5 us)
Async XLA Ops:
  0.6 25.2 %collective-permute-start.1 = (bf16[8192,128]{1,0:T(8,128)(2,1)}, bf16[8192,128]{1,0:T(8,128)(2,1)}, u32[]{:S(2)}, u32[]{:S(2)}) collective-permute-start(bf16[8192,128]{1,0:T(8,128)(2,1)} %bitcast.15), channel_id=1, source_target_pairs={{3,2},{5,4},{6,5},{9,8},{10,9},{11,10},{12,11},{13,12},{14,13},{15... | collective-permute-start | bytes 6291464 | tf_op jit(solution)/shard_map/ppermute | solution.py:350
  2.6 23.2 %collective-permute-start.2 = (bf16[8192,128]{1,0:T(8,128)(2,1)}, bf16[8192,128]{1,0:T(8,128)(2,1)}, u32[]{:S(2)}, u32[]{:S(2)}) collective-permute-start(bf16[8192,128]{1,0:T(8,128)(2,1)} %bitcast.16), channel_id=1, source_target_pairs={{8,0},{5,13},{6,14},{15,7},{0,1},{7,6},{24,16},{21,29},{22,30},{31... | collective-permute-start | bytes 6291464 | tf_op jit(solution)/shard_map/ppermute | solution.py:351
  3.9 21.9 %collective-permute-start.3 = (s32[1,4]{1,0:T(1,128)}, s32[1,4]{1,0:T(1,128)S(1)}, u32[]{:S(2)}, u32[]{:S(2)}) collective-permute-start(s32[1,4]{1,0:T(1,128)} %param.3), channel_id=1, source_target_pairs={{3,2},{5,4},{6,5},{9,8},{10,9},{11,10},{12,11},{13,12},{14,13},{15... | collective-permute-start | bytes 56 | tf_op jit(solution)/shard_map/ppermute | solution.py:356
  4.6 21.2 %collective-permute-start.4 = (s32[1,4]{1,0:T(1,128)}, s32[1,4]{1,0:T(1,128)S(1)}, u32[]{:S(2)}, u32[]{:S(2)}) collective-permute-start(s32[1,4]{1,0:T(1,128)} %param.3), channel_id=1, source_target_pairs={{8,0},{5,13},{6,14},{15,7},{0,1},{7,6},{24,16},{21,29},{22,30},{31... | collective-permute-start | bytes 56 | tf_op jit(solution)/shard_map/ppermute | solution.py:355
  5.9 36.8 %collective-permute-start = (s32[1,4]{1,0:T(1,128)}, s32[1,4]{1,0:T(1,128)S(1)}, u32[]{:S(2)}, u32[]{:S(2)}) collective-permute-start(s32[1,4]{1,0:T(1,128)} %param.3), channel_id=1, source_target_pairs={{1,9},{10,2},{3,11},{12,4},{2,1},{4,3},{17,25},{26,18},{19,27},{28... | collective-permute-start | bytes 56 | tf_op jit(solution)/shard_map/ppermute | solution.py:357
  16.4 1.6 %copy-start.2 = (bf16[1024,2,4,128]{3,2,1,0:T(4,128)(2,1)S(1)}, bf16[1024,2,4,128]{3,2,1,0:T(4,128)(2,1)}, u32[]{:S(2)}) copy-start(bf16[1024,2,4,128]{3,2,1,0:T(4,128)(2,1)} %param.2) | copy-start | bytes 6291460
  21.1 1.4 %copy-start = (bf16[128,8192]{1,0:T(8,128)(2,1)}, bf16[128,8192]{1,0:T(8,128)(2,1)S(1)}, u32[]{:S(2)}) copy-start(bf16[128,8192]{1,0:T(8,128)(2,1)S(1)} %get-tuple-element.34.swapped_ref) | copy-start | bytes 6291460
  22.5 11.1 %copy-start.4 = (s32[1,4]{1,0:T(1,128)S(1)}, s32[1,4]{1,0:T(1,128)}, u32[]{:S(2)}) copy-start(s32[1,4]{1,0:T(1,128)} %param.3) | copy-start | bytes 52
  22.8 1.0 %copy-start.3 = (bf16[5120,128]{1,0:T(8,128)(2,1)}, bf16[5120,128]{1,0:T(8,128)(2,1)S(1)}, u32[]{:S(2)}) copy-start(bf16[5120,128]{1,0:T(8,128)(2,1)S(1)} %get-tuple-element.45) | copy-start | bytes 3932164
  25.8 22.6 %collective-permute-start.6 = (bf16[5120,128]{1,0:T(8,128)(2,1)}, bf16[5120,128]{1,0:T(8,128)(2,1)}, u32[]{:S(2)}, u32[]{:S(2)}) collective-permute-start(bf16[5120,128]{1,0:T(8,128)(2,1)} %copy-done.3), channel_id=1, source_target_pairs={{1,9},{10,2},{3,11},{12,4},{2,1},{4,3},{17,25},{26,18},{19,27},{28... | collective-permute-start | bytes 3932168 | tf_op jit(solution)/shard_map/ppermute | solution.py:366
  33.7 1.6 %copy-start.1 = (bf16[128,8192]{1,0:T(8,128)(2,1)S(1)}, bf16[128,8192]{1,0:T(8,128)(2,1)}, u32[]{:S(2)}) copy-start(bf16[128,8192]{1,0:T(8,128)(2,1)} %copy-done) | copy-start | bytes 6291460
  40.7 15.9 %collective-permute-start.5 = (bf16[3072,128]{1,0:T(8,128)(2,1)S(1)}, bf16[3072,128]{1,0:T(8,128)(2,1)S(1)}, u32[]{:S(2)}, u32[]{:S(2)}) collective-permute-start(bf16[3072,128]{1,0:T(8,128)(2,1)S(1)} %get-tuple-element.44), channel_id=1, source_target_pairs={{1,9},{10,2},{3,11},{12,4},{2,1},{4,3},{17,25},{26,18},{19,27},{28... | collective-permute-start | bytes 2359304 | tf_op jit(solution)/shard_map/ppermute | solution.py:371
  60.7 8.4 %collective-permute-start.7 = (bf16[9,128,128]{2,1,0:T(8,128)(2,1)S(1)}, bf16[9,128,128]{2,1,0:T(8,128)(2,1)S(1)}, u32[]{:S(2)}, u32[]{:S(2)}) collective-permute-start(bf16[9,128,128]{2,1,0:T(8,128)(2,1)S(1)} %get-tuple-element.49), channel_id=1, source_target_pairs={{0,8},{13,5},{14,6},{7,15},{9,1},{2,10},{11,3},{4,12},{1,0},{16,24... | collective-permute-start | bytes 884744 | tf_op jit(solution)/shard_map/ppermute | solution.py:380
  62.6 6.4 %collective-permute-start.8 = (bf16[9,128,128]{2,1,0:T(8,128)(2,1)S(1)}, bf16[9,128,128]{2,1,0:T(8,128)(2,1)S(1)}, u32[]{:S(2)}, u32[]{:S(2)}) collective-permute-start(bf16[9,128,128]{2,1,0:T(8,128)(2,1)S(1)} %get-tuple-element.50), channel_id=1, source_target_pairs={{0,7},{7,15},{16,23},{23,31}} | collective-permute-start | bytes 884744 | tf_op jit(solution)/shard_map/ppermute | solution.py:381

commit v28 on v23

--- a/solution.py
+++ b/solution.py
@@ -344,12 +344,10 @@
     near_in, first_part, last_part, own, coeffs, first_in, near_flags, first_flags, second_flags = lax.optimization_barrier(
         (near_in, *parts, own, coeffs, first_in, near_flags, first_flags, second_flags)
     )
-    second_in = [lax.ppermute(first_part, "chan", second_pairs)]
     first_switch = switch(me == 0, special, quality[0], near_flags, first_flags)
+    second_in = [lax.ppermute(part, "chan", second_pairs) for part in (first_part, last_part)]
     operands = first_switch, own, coeffs, near_in, first_in
     total, token = first_sums(*operands)
-    last_part, token = lax.optimization_barrier((last_part, token))
-    second_in.append(lax.ppermute(last_part, "chan", second_pairs))
     near, far, back = first_sums(*operands, [total, token])
     second_switch, near = lax.optimization_barrier((second_switch, near))
     total, = second_sums(second_switch, own, coeffs, second_in[0], 0)

time: 69.7 us -> 69.7 us (level)
  no operation moved by 1% of the time
where the time goes in v28:
time: 69.7 us; the launch traced here: 69.2 us
  starting transfers between devices  27.8 us (40%)
  Pallas kernels  23.9 us (34%)
  waiting for transfers between devices  7.8 us (11%)
  local copies, waits for them, and re-layouts  5.57 us (8%)
  other arithmetic  3.16 us (5%)
  between operations  0.89 us (1%)
    pallas_call x2, Pallas kernels, first_sums(): pl.pallas_call(functools.partial(first_kernel, windows, bool(earlier)), g...  11.1 us
    ppermute x1, starting transfers between devices, local(): second_flags = lax.ppermute(quality, 'chan', second_pairs)[0]  10.5 us
    ppermute x2, starting transfers between devices, local(): lax.ppermute(part, 'chan', second_pairs)  9.5 us
    pallas_call x2, Pallas kernels, second_sums(): pl.pallas_call(functools.partial(second_kernel, windows, not earlier), gr...  9.37 us
    ppermute x1, waiting for transfers between devices, local(): returned = lax.ppermute(back, 'chan', back_pairs)  5.71 us
    unnamed x10, local copies, waits for them, and re-layouts  5.57 us
    pallas_call x1, Pallas kernels, turn(): pl.pallas_call(turn_kernel, grid=(rows // STEP,), in_specs=[pl.BlockSpec(...  3.15 us
    ppermute x2, waiting for transfers between devices, local(): lax.ppermute(part, 'chan', second_pairs)  2.07 us
  transfers between devices with their start and end apart: 9, of which 2 were waited for; matrix products, arithmetic and copies ran while one was open for 3% of the time, Pallas kernels for 30%

profile of v28, /device:TPU:1, one launch (start us, length us, event | category | flops | bytes accessed | tf_op | source)
XLA Modules:
  0.0 69.2 jit_solution(1157103643119189649)
XLA Ops:
  0.6 2.0 %collective-permute-start.1 = (bf16[8192,128]{1,0:T(8,128)(2,1)}, bf16[8192,128]{1,0:T(8,128)(2,1)}, u32[]{:S(2)}, u32[]{:S(2)}) collective-permute-start(bf16[8192,128]{1,0:T(8,128)(2,1)} %bitcast.15), channel_id=1, source_target_pairs={{3,2},{5,4},{6,5},{9,8},{10,9},{11,10},{12,11},{13,12},{14,13},{15... | collective-permute-start | bytes 6291464 | tf_op jit(solution)/shard_map/ppermute | solution.py:331
  2.6 1.3 %collective-permute-start.2 = (bf16[8192,128]{1,0:T(8,128)(2,1)}, bf16[8192,128]{1,0:T(8,128)(2,1)}, u32[]{:S(2)}, u32[]{:S(2)}) collective-permute-start(bf16[8192,128]{1,0:T(8,128)(2,1)} %bitcast.16), channel_id=1, source_target_pairs={{8,0},{5,13},{6,14},{15,7},{0,1},{7,6},{24,16},{21,29},{22,30},{31... | collective-permute-start | bytes 6291464 | tf_op jit(solution)/shard_map/ppermute | solution.py:332
  3.9 0.7 collective-permute-start.3
  4.6 1.3 %collective-permute-start.4 = (s32[1,4]{1,0:T(1,128)}, s32[1,4]{1,0:T(1,128)S(1)}, u32[]{:S(2)}, u32[]{:S(2)}) collective-permute-start(s32[1,4]{1,0:T(1,128)} %param.3), channel_id=1, source_target_pairs={{8,0},{5,13},{6,14},{15,7},{0,1},{7,6},{24,16},{21,29},{22,30},{31... | collective-permute-start | bytes 56 | tf_op jit(solution)/shard_map/ppermute | solution.py:336
  5.9 10.5 %collective-permute-start = (s32[1,4]{1,0:T(1,128)}, s32[1,4]{1,0:T(1,128)S(1)}, u32[]{:S(2)}, u32[]{:S(2)}) collective-permute-start(s32[1,4]{1,0:T(1,128)} %param.3), channel_id=1, source_target_pairs={{1,9},{10,2},{3,11},{12,4},{2,1},{4,3},{17,25},{26,18},{19,27},{28... | collective-permute-start | bytes 56 | tf_op jit(solution)/shard_map/ppermute | solution.py:338
  16.4 1.6 %copy-done.2 = bf16[1024,2,4,128]{3,2,1,0:T(4,128)(2,1)S(1)} copy-done((bf16[1024,2,4,128]{3,2,1,0:T(4,128)(2,1)S(1)}, bf16[1024,2,4,128]{3,2,1,0:T(4,128)(2,1)}, u32[]{:S(2)}) %copy-start.2) | copy-done | bytes 2097176
  18.0 3.2 %turn.1 = (bf16[128,8192]{1,0:T(8,128)(2,1)S(1)}, bf16[128,8192]{1,0:T(8,128)(2,1)S(1)}) custom-call(bf16[8192,128]{1,0:T(8,128)(2,1)S(1)} %bitcast.17), custom_call_target="tpu_custom_call" | custom-call | bytes 6291456 | tf_op jit(solution)/shard_map/turn/pallas_call | solution.py:85
  21.2 1.3 %copy-done = bf16[128,8192]{1,0:T(8,128)(2,1)} copy-done((bf16[128,8192]{1,0:T(8,128)(2,1)}, bf16[128,8192]{1,0:T(8,128)(2,1)S(1)}, u32[]{:S(2)}) %copy-start) | copy-done | bytes 2097176
  22.5 0.3 split.1
  22.8 1.0 %copy-done.3 = bf16[5120,128]{1,0:T(8,128)(2,1)} copy-done((bf16[5120,128]{1,0:T(8,128)(2,1)}, bf16[5120,128]{1,0:T(8,128)(2,1)S(1)}, u32[]{:S(2)}) %copy-start.3) | copy-done | bytes 1310744
  23.9 0.9 %multiply_convert_fusion = (bf16[5,8192]{1,0:T(8,128)(2,1)S(1)}, f32[5,8192]{1,0:T(8,128)S(1)}) fusion(f32[8192]{0:T(1024)S(1)} %fusion.9, f32[5]{0:T(128)S(1)} %iota_multiply_fusion), kind=kLoop, calls=%fused_computation.4 | loop fusion | flops 122880 | bytes 278548 | tf_op jit(solution)/shard_map/convert
  24.8 0.9 %fusion.2 = bf16[4,8192]{1,0:T(4,128)(2,1)S(1)} fusion(f32[5,8192]{1,0:T(8,128)S(1)} %get-tuple-element.51, f32[8192]{0:T(1024)S(1)} %select_multiply_fusion), kind=kLoop, calls=%fused_computation.8 | loop fusion | flops 98304 | bytes 229376 | tf_op jit(solution)/shard_map/convert.1
  25.8 7.6 %collective-permute-start.6 = (bf16[5120,128]{1,0:T(8,128)(2,1)}, bf16[5120,128]{1,0:T(8,128)(2,1)}, u32[]{:S(2)}, u32[]{:S(2)}) collective-permute-start(bf16[5120,128]{1,0:T(8,128)(2,1)} %copy-done.3), channel_id=1, source_target_pairs={{1,9},{10,2},{3,11},{12,4},{2,1},{4,3},{17,25},{26,18},{19,27},{28... | collective-permute-start | bytes 3932168 | tf_op jit(solution)/shard_map/ppermute | solution.py:348
  33.7 1.9 %collective-permute-start.5 = (bf16[3072,128]{1,0:T(8,128)(2,1)S(1)}, bf16[3072,128]{1,0:T(8,128)(2,1)S(1)}, u32[]{:S(2)}, u32[]{:S(2)}) collective-permute-start(bf16[3072,128]{1,0:T(8,128)(2,1)S(1)} %get-tuple-element.40), channel_id=1, source_target_pairs={{1,9},{10,2},{3,11},{12,4},{2,1},{4,3},{17,25},{26,18},{19,27},{28... | collective-permute-start | bytes 2359304 | tf_op jit(solution)/shard_map/ppermute | solution.py:348
  35.7 1.6 %copy-done.1 = bf16[128,8192]{1,0:T(8,128)(2,1)S(1)} copy-done((bf16[128,8192]{1,0:T(8,128)(2,1)S(1)}, bf16[128,8192]{1,0:T(8,128)(2,1)}, u32[]{:S(2)}) %copy-start.1) | copy-done | bytes 2097176
  37.3 5.5 %first_half.1 = (f32[1152,256]{1,0:T(8,128)S(1)}, f32[8,128]{1,0:T(8,128)S(1)}) custom-call(s32[14]{0:T(128)S(1)} %pad_add_fusion.1.switch_ref, bf16[128,8192]{1,0:T(8,128)(2,1)S(1)} %get-tuple-element.31.plain_ref, bf16[128,8192]{1,0:T(8,128)(2,1)S(1)} %copy-done.1, bf16[9,8192]{1,0:T(8,128)(2,1)S(1)} %pad_maximum_fusion.coeff_ref, ...), custom_call_target="tpu_custom_call" | custom-call | flops 2415919104 | bytes 4194304 | tf_op jit(solution)/shard_map/first_half/pallas_call | solution.py:204
  42.7 5.7 %first_last.1 = (bf16[9,128,128]{2,1,0:T(8,128)(2,1)S(1)}, bf16[9,128,128]{2,1,0:T(8,128)(2,1)S(1)}, bf16[9,128,128]{2,1,0:T(8,128)(2,1)S(1)}) custom-call(s32[14]{0:T(128)S(1)} %pad_add_fusion.1.switch_ref, bf16[128,8192]{1,0:T(8,128)(2,1)S(1)} %get-tuple-element.31.plain_ref, bf16[128,8192]{1,0:T(8,128)(2,1)S(1)} %copy-done.1, ...), custom_call_target="tpu_custom_call" | custom-call | flops 2415919104 | bytes 4194304 | tf_op jit(solution)/shard_map/first_last/pallas_call | solution.py:204
  48.5 6.1 %second_part.1.rest_0_ = f32[1152,128]{1,0:T(8,128)S(1)} custom-call(s32[6]{0:T(128)S(1)} %pad_add_fusion.switch_ref, bf16[128,8192]{1,0:T(8,128)(2,1)S(1)} %get-tuple-element.31.plain_ref, bf16[128,8192]{1,0:T(8,128)(2,1)S(1)} %copy-done.1, bf16[9,8192]{1,0:T(8,128)(2,1)S(1)} %pad_maximum_fusion.coeff_ref, bf16[5120,128]{1,0:T(8,128)(2,1)} %collective-permute-done.6.partner_ref), custom_call_target="tpu_custom_call" | custom-call | flops 1509949440 | bytes 3932160 | tf_op jit(solution)/shard_map/second_part/pallas_call | solution.py:281
  54.5 2.1 %collective-permute-done.5.partner_ref = bf16[3072,128]{1,0:T(8,128)(2,1)S(1)} collective-permute-done((bf16[3072,128]{1,0:T(8,128)(2,1)S(1)}, bf16[3072,128]{1,0:T(8,128)(2,1)S(1)}, u32[]{:S(2)}, u32[]{:S(2)}) %collective-permute-start.5) | collective-permute-done | bytes 786464 | tf_op jit(solution)/shard_map/ppermute | solution.py:348
  56.6 3.3 %second_last.1 = (bf16[9,128,128]{2,1,0:T(8,128)(2,1)S(1)}, bf16[9,128,128]{2,1,0:T(8,128)(2,1)S(1)}, bf16[9,128,128]{2,1,0:T(8,128)(2,1)S(1)}) custom-call(s32[6]{0:T(128)S(1)} %pad_add_fusion.switch_ref, bf16[128,8192]{1,0:T(8,128)(2,1)S(1)} %get-tuple-element.31.plain_ref, bf16[128,8192]{1,0:T(8,128)(2,1)S(1)} %copy-done.1, ...), custom_call_target="tpu_custom_call" | custom-call | flops 905969664 | bytes 2359296 | tf_op jit(solution)/shard_map/second_last/pallas_call | solution.py:281
  59.9 1.9 %collective-permute-start.7 = (bf16[9,128,128]{2,1,0:T(8,128)(2,1)S(1)}, bf16[9,128,128]{2,1,0:T(8,128)(2,1)S(1)}, u32[]{:S(2)}, u32[]{:S(2)}) collective-permute-start(bf16[9,128,128]{2,1,0:T(8,128)(2,1)S(1)} %get-tuple-element.45), channel_id=1, source_target_pairs={{0,8},{13,5},{14,6},{7,15},{9,1},{2,10},{11,3},{4,12},{1,0},{16,24... | collective-permute-start | bytes 884744 | tf_op jit(solution)/shard_map/ppermute | solution.py:359
  61.8 0.7 collective-permute-start.8
  62.6 5.7 %collective-permute-done.7 = bf16[9,128,128]{2,1,0:T(8,128)(2,1)S(1)} collective-permute-done((bf16[9,128,128]{2,1,0:T(8,128)(2,1)S(1)}, bf16[9,128,128]{2,1,0:T(8,128)(2,1)S(1)}, u32[]{:S(2)}, u32[]{:S(2)}) %collective-permute-start.7) | collective-permute-done | bytes 294944 | tf_op jit(solution)/shard_map/ppermute | solution.py:359
  68.3 0.9 %select_bitcast_fusion = (bf16[1,9,128,128]{3,2,1,0:T(8,128)(2,1)}, bf16[1,9,128,128]{3,2,1,0:T(8,128)(2,1)}) fusion(bf16[9,128,128]{2,1,0:T(8,128)(2,1)S(1)} %collective-permute-done.7, bf16[9,128,128]{2,1,0:T(8,128)(2,1)S(1)} %get-tuple-element.47, pred[]{:T(512)S(6)} %or.59, bf16[9,128,128]{2,1,0:T(8,128)(2,1)S(1)} %collective-permute-done.8, ...), kind=kLoop, calls=%fused_computation | loop fusion | flops 442368 | bytes 1769475 | tf_op jit(solution)/shard_map/broadcast_in_dim | solution.py:364
  (23 shorter events, 0.5 us)
Async XLA Ops:
  0.6 25.2 %collective-permute-start.1 = (bf16[8192,128]{1,0:T(8,128)(2,1)}, bf16[8192,128]{1,0:T(8,128)(2,1)}, u32[]{:S(2)}, u32[]{:S(2)}) collective-permute-start(bf16[8192,128]{1,0:T(8,128)(2,1)} %bitcast.15), channel_id=1, source_target_pairs={{3,2},{5,4},{6,5},{9,8},{10,9},{11,10},{12,11},{13,12},{14,13},{15... | collective-permute-start | bytes 6291464 | tf_op jit(solution)/shard_map/ppermute | solution.py:331
  2.6 23.2 %collective-permute-start.2 = (bf16[8192,128]{1,0:T(8,128)(2,1)}, bf16[8192,128]{1,0:T(8,128)(2,1)}, u32[]{:S(2)}, u32[]{:S(2)}) collective-permute-start(bf16[8192,128]{1,0:T(8,128)(2,1)} %bitcast.16), channel_id=1, source_target_pairs={{8,0},{5,13},{6,14},{15,7},{0,1},{7,6},{24,16},{21,29},{22,30},{31... | collective-permute-start | bytes 6291464 | tf_op jit(solution)/shard_map/ppermute | solution.py:332
  3.9 21.9 %collective-permute-start.3 = (s32[1,4]{1,0:T(1,128)}, s32[1,4]{1,0:T(1,128)S(1)}, u32[]{:S(2)}, u32[]{:S(2)}) collective-permute-start(s32[1,4]{1,0:T(1,128)} %param.3), channel_id=1, source_target_pairs={{3,2},{5,4},{6,5},{9,8},{10,9},{11,10},{12,11},{13,12},{14,13},{15... | collective-permute-start | bytes 56 | tf_op jit(solution)/shard_map/ppermute | solution.py:337
  4.6 21.2 %collective-permute-start.4 = (s32[1,4]{1,0:T(1,128)}, s32[1,4]{1,0:T(1,128)S(1)}, u32[]{:S(2)}, u32[]{:S(2)}) collective-permute-start(s32[1,4]{1,0:T(1,128)} %param.3), channel_id=1, source_target_pairs={{8,0},{5,13},{6,14},{15,7},{0,1},{7,6},{24,16},{21,29},{22,30},{31... | collective-permute-start | bytes 56 | tf_op jit(solution)/shard_map/ppermute | solution.py:336
  5.9 27.7 %collective-permute-start = (s32[1,4]{1,0:T(1,128)}, s32[1,4]{1,0:T(1,128)S(1)}, u32[]{:S(2)}, u32[]{:S(2)}) collective-permute-start(s32[1,4]{1,0:T(1,128)} %param.3), channel_id=1, source_target_pairs={{1,9},{10,2},{3,11},{12,4},{2,1},{4,3},{17,25},{26,18},{19,27},{28... | collective-permute-start | bytes 56 | tf_op jit(solution)/shard_map/ppermute | solution.py:338
  16.4 1.6 %copy-start.2 = (bf16[1024,2,4,128]{3,2,1,0:T(4,128)(2,1)S(1)}, bf16[1024,2,4,128]{3,2,1,0:T(4,128)(2,1)}, u32[]{:S(2)}) copy-start(bf16[1024,2,4,128]{3,2,1,0:T(4,128)(2,1)} %param.2) | copy-start | bytes 6291460
  21.1 1.4 %copy-start = (bf16[128,8192]{1,0:T(8,128)(2,1)}, bf16[128,8192]{1,0:T(8,128)(2,1)S(1)}, u32[]{:S(2)}) copy-start(bf16[128,8192]{1,0:T(8,128)(2,1)S(1)} %get-tuple-element.32.swapped_ref) | copy-start | bytes 6291460
  22.5 11.1 %copy-start.4 = (s32[1,4]{1,0:T(1,128)S(1)}, s32[1,4]{1,0:T(1,128)}, u32[]{:S(2)}) copy-start(s32[1,4]{1,0:T(1,128)} %param.3) | copy-start | bytes 52
  22.8 1.0 %copy-start.3 = (bf16[5120,128]{1,0:T(8,128)(2,1)}, bf16[5120,128]{1,0:T(8,128)(2,1)S(1)}, u32[]{:S(2)}) copy-start(bf16[5120,128]{1,0:T(8,128)(2,1)S(1)} %get-tuple-element.41) | copy-start | bytes 3932164
  25.8 22.6 %collective-permute-start.6 = (bf16[5120,128]{1,0:T(8,128)(2,1)}, bf16[5120,128]{1,0:T(8,128)(2,1)}, u32[]{:S(2)}, u32[]{:S(2)}) collective-permute-start(bf16[5120,128]{1,0:T(8,128)(2,1)} %copy-done.3), channel_id=1, source_target_pairs={{1,9},{10,2},{3,11},{12,4},{2,1},{4,3},{17,25},{26,18},{19,27},{28... | collective-permute-start | bytes 3932168 | tf_op jit(solution)/shard_map/ppermute | solution.py:348
  33.7 22.9 %collective-permute-start.5 = (bf16[3072,128]{1,0:T(8,128)(2,1)S(1)}, bf16[3072,128]{1,0:T(8,128)(2,1)S(1)}, u32[]{:S(2)}, u32[]{:S(2)}) collective-permute-start(bf16[3072,128]{1,0:T(8,128)(2,1)S(1)} %get-tuple-element.40), channel_id=1, source_target_pairs={{1,9},{10,2},{3,11},{12,4},{2,1},{4,3},{17,25},{26,18},{19,27},{28... | collective-permute-start | bytes 2359304 | tf_op jit(solution)/shard_map/ppermute | solution.py:348
  35.7 1.6 %copy-start.1 = (bf16[128,8192]{1,0:T(8,128)(2,1)S(1)}, bf16[128,8192]{1,0:T(8,128)(2,1)}, u32[]{:S(2)}) copy-start(bf16[128,8192]{1,0:T(8,128)(2,1)} %copy-done) | copy-start | bytes 6291460
  59.9 8.4 %collective-permute-start.7 = (bf16[9,128,128]{2,1,0:T(8,128)(2,1)S(1)}, bf16[9,128,128]{2,1,0:T(8,128)(2,1)S(1)}, u32[]{:S(2)}, u32[]{:S(2)}) collective-permute-start(bf16[9,128,128]{2,1,0:T(8,128)(2,1)S(1)} %get-tuple-element.45), channel_id=1, source_target_pairs={{0,8},{13,5},{14,6},{7,15},{9,1},{2,10},{11,3},{4,12},{1,0},{16,24... | collective-permute-start | bytes 884744 | tf_op jit(solution)/shard_map/ppermute | solution.py:359
  61.8 6.4 %collective-permute-start.8 = (bf16[9,128,128]{2,1,0:T(8,128)(2,1)S(1)}, bf16[9,128,128]{2,1,0:T(8,128)(2,1)S(1)}, u32[]{:S(2)}, u32[]{:S(2)}) collective-permute-start(bf16[9,128,128]{2,1,0:T(8,128)(2,1)S(1)} %get-tuple-element.46), channel_id=1, source_target_pairs={{0,7},{7,15},{16,23},{23,31}} | collective-permute-start | bytes 884744 | tf_op jit(solution)/shard_map/ppermute | solution.py:360

commit v29 on v24

--- a/solution.py
+++ b/solution.py
@@ -345,15 +345,12 @@
     near_in, *parts, own, coeffs, first_in, near_flags, first_flags, second_flags = lax.optimization_barrier(
         (near_in, *parts, own, coeffs, first_in, near_flags, first_flags, second_flags)
     )
-    second_in = [lax.ppermute(parts[0], "chan", second_pairs)]
     first_switch = switch(me == 0, special, quality[0], near_flags, first_flags)
+    second_in = [lax.ppermute(part, "chan", second_pairs) for part in parts]
     operands = first_switch, own, coeffs, near_in, first_in
     total, token = first_sums(*operands)
-    part, token = lax.optimization_barrier((parts[1], token))
-    second_in.append(lax.ppermute(part, "chan", second_pairs))
     near, far, back = first_sums(*operands, [total, token])
-    second_switch, near, part = lax.optimization_barrier((second_switch, near, parts[2]))
-    second_in.append(lax.ppermute(part, "chan", second_pairs))
+    second_switch, near = lax.optimization_barrier((second_switch, near))
     starts = [0, parts[0].shape[0], parts[0].shape[0] + parts[1].shape[0]]
     total = second_sums(second_switch, own, coeffs, second_in[0], starts[0])
     total, = second_sums(second_switch, own, coeffs, second_in[1], starts[1], total)

time: 76.9 us -> 68.9 us (0.90)
  Pallas kernels: 29.2 us -> 23.5 us
  other arithmetic: 5.08 us -> 3.16 us
  local copies, waits for them, and re-layouts: 7.52 us -> 6.1 us
  starting transfers between devices: 27.6 us -> 29 us
    pallas_call x1, Pallas kernels: 3.26 us -> 0.35 us  [split(): pl.pallas_call(functools.partial(split_kernel, ends), grid=(steps,), in_s...]
    pallas_call x3, Pallas kernels: 11.6 us -> 8.87 us  [second_sums(): pl.pallas_call(functools.partial(second_kernel, windows, not earlier, las...]
    unnamed x14 -> x12, local copies, waits for them, and re-layouts: 7.52 us -> 6.1 us
    ppermute x3, starting transfers between devices: 9.35 us -> 10.6 us  [local(): second_in = [lax.ppermute(part, 'chan', second_pairs) for part in parts]]
    broadcast_in_dim x1, other arithmetic: 1.84 us -> 0.87 us  [local(): return (near[None], far[None])]
    select_n x1, other arithmetic: 1 us -> 0.04 us  [local(): near = jnp.where(me == half - 2, far, near)]
  transfers between devices with their start and end apart: 10 -> 10, of which waited for: 1 -> 1; matrix products, arithmetic and copies ran while one was open for 4% -> 3% of each run, Pallas kernels for 34% -> 31%
where the time goes in v29:
time: 68.9 us; the launch traced here: 68.4 us
  starting transfers between devices  29 us (42%)
  Pallas kernels  23.5 us (34%)
  local copies, waits for them, and re-layouts  6.1 us (9%)
  waiting for transfers between devices  5.74 us (8%)
  other arithmetic  3.16 us (5%)
  between operations  0.96 us (1%)
    pallas_call x2, Pallas kernels, first_sums(): pl.pallas_call(functools.partial(first_kernel, windows, bool(earlier)), g...  11.1 us
    ppermute x3, starting transfers between devices, local(): second_in = [lax.ppermute(part, 'chan', second_pairs) for part in parts]  10.6 us
    ppermute x1, starting transfers between devices, local(): second_flags = lax.ppermute(quality, 'chan', second_pairs)[0]  10.5 us
    pallas_call x3, Pallas kernels, second_sums(): pl.pallas_call(functools.partial(second_kernel, windows, not earlier, las...  8.87 us
    unnamed x12, local copies, waits for them, and re-layouts  6.1 us
    ppermute x1, waiting for transfers between devices, local(): returned = lax.ppermute(back, 'chan', back_pairs)  5.71 us
    pallas_call x1, Pallas kernels, turn(): pl.pallas_call(turn_kernel, grid=(rows // STEP,), in_specs=[pl.BlockSpec(...  3.15 us
    ppermute x1, starting transfers between devices, local(): near_in = lax.ppermute(block, 'chan', near_pairs)  2 us
  transfers between devices with their start and end apart: 10, of which 1 were waited for; matrix products, arithmetic and copies ran while one was open for 3% of the time, Pallas kernels for 31%

profile of v29, /device:TPU:1, one launch (start us, length us, event | category | flops | bytes accessed | tf_op | source)
XLA Modules:
  0.0 68.4 jit_solution(8567599678446300425)
XLA Ops:
  0.6 2.0 %collective-permute-start.1 = (bf16[8192,128]{1,0:T(8,128)(2,1)}, bf16[8192,128]{1,0:T(8,128)(2,1)}, u32[]{:S(2)}, u32[]{:S(2)}) collective-permute-start(bf16[8192,128]{1,0:T(8,128)(2,1)} %bitcast.15), channel_id=1, source_target_pairs={{3,2},{5,4},{6,5},{9,8},{10,9},{11,10},{12,11},{13,12},{14,13},{15... | collective-permute-start | bytes 6291464 | tf_op jit(solution)/shard_map/ppermute | solution.py:332
  2.6 1.3 %collective-permute-start.2 = (bf16[8192,128]{1,0:T(8,128)(2,1)}, bf16[8192,128]{1,0:T(8,128)(2,1)}, u32[]{:S(2)}, u32[]{:S(2)}) collective-permute-start(bf16[8192,128]{1,0:T(8,128)(2,1)} %bitcast.16), channel_id=1, source_target_pairs={{8,0},{5,13},{6,14},{15,7},{0,1},{7,6},{24,16},{21,29},{22,30},{31... | collective-permute-start | bytes 6291464 | tf_op jit(solution)/shard_map/ppermute | solution.py:333
  4.6 1.3 %collective-permute-start.4 = (s32[1,4]{1,0:T(1,128)}, s32[1,4]{1,0:T(1,128)S(1)}, u32[]{:S(2)}, u32[]{:S(2)}) collective-permute-start(s32[1,4]{1,0:T(1,128)} %param.3), channel_id=1, source_target_pairs={{8,0},{5,13},{6,14},{15,7},{0,1},{7,6},{24,16},{21,29},{22,30},{31... | collective-permute-start | bytes 56 | tf_op jit(solution)/shard_map/ppermute | solution.py:337
  5.9 10.5 %collective-permute-start = (s32[1,4]{1,0:T(1,128)}, s32[1,4]{1,0:T(1,128)S(1)}, u32[]{:S(2)}, u32[]{:S(2)}) collective-permute-start(s32[1,4]{1,0:T(1,128)} %param.3), channel_id=1, source_target_pairs={{1,9},{10,2},{3,11},{12,4},{2,1},{4,3},{17,25},{26,18},{19,27},{28... | collective-permute-start | bytes 56 | tf_op jit(solution)/shard_map/ppermute | solution.py:339
  16.4 1.6 %copy-done.2 = bf16[1024,2,4,128]{3,2,1,0:T(4,128)(2,1)S(1)} copy-done((bf16[1024,2,4,128]{3,2,1,0:T(4,128)(2,1)S(1)}, bf16[1024,2,4,128]{3,2,1,0:T(4,128)(2,1)}, u32[]{:S(2)}) %copy-start.2) | copy-done | bytes 2097176
  18.3 0.8 %copy-done.3 = bf16[2048,128]{1,0:T(8,128)(2,1)} copy-done((bf16[2048,128]{1,0:T(8,128)(2,1)}, bf16[2048,128]{1,0:T(8,128)(2,1)S(1)}, u32[]{:S(2)}) %copy-start.3) | copy-done | bytes 524312
  19.1 0.8 %copy-done.4 = bf16[2048,128]{1,0:T(8,128)(2,1)} copy-done((bf16[2048,128]{1,0:T(8,128)(2,1)}, bf16[2048,128]{1,0:T(8,128)(2,1)S(1)}, u32[]{:S(2)}) %copy-start.4) | copy-done | bytes 524312
  19.9 3.2 %turn.1 = (bf16[128,8192]{1,0:T(8,128)(2,1)S(1)}, bf16[128,8192]{1,0:T(8,128)(2,1)S(1)}) custom-call(bf16[8192,128]{1,0:T(8,128)(2,1)S(1)} %bitcast.18), custom_call_target="tpu_custom_call" | custom-call | bytes 6291456 | tf_op jit(solution)/shard_map/turn/pallas_call | solution.py:83
  23.1 1.3 %copy-done = bf16[128,8192]{1,0:T(8,128)(2,1)} copy-done((bf16[128,8192]{1,0:T(8,128)(2,1)}, bf16[128,8192]{1,0:T(8,128)(2,1)S(1)}, u32[]{:S(2)}) %copy-start) | copy-done | bytes 2097176
  24.6 0.9 %multiply_convert_fusion = (bf16[5,8192]{1,0:T(8,128)(2,1)S(1)}, f32[5,8192]{1,0:T(8,128)S(1)}) fusion(f32[8192]{0:T(1024)S(1)} %fusion.9, f32[5]{0:T(128)S(1)} %iota_multiply_fusion), kind=kLoop, calls=%fused_computation.4 | loop fusion | flops 122880 | bytes 278548 | tf_op jit(solution)/shard_map/convert
  25.6 0.9 %fusion.2 = bf16[4,8192]{1,0:T(4,128)(2,1)S(1)} fusion(f32[5,8192]{1,0:T(8,128)S(1)} %get-tuple-element.55, f32[8192]{0:T(1024)S(1)} %select_multiply_fusion), kind=kLoop, calls=%fused_computation.8 | loop fusion | flops 98304 | bytes 229376 | tf_op jit(solution)/shard_map/convert.1
  26.6 6.8 %collective-permute-start.7 = (bf16[4096,128]{1,0:T(8,128)(2,1)S(1)}, bf16[4096,128]{1,0:T(8,128)(2,1)S(1)}, u32[]{:S(2)}, u32[]{:S(2)}) collective-permute-start(bf16[4096,128]{1,0:T(8,128)(2,1)S(1)} %get-tuple-element.45), channel_id=1, source_target_pairs={{1,9},{10,2},{3,11},{12,4},{2,1},{4,3},{17,25},{26,18},{19,27},{28... | collective-permute-start | bytes 3145736 | tf_op jit(solution)/shard_map/ppermute | solution.py:349
  33.5 1.9 %collective-permute-start.6 = (bf16[2048,128]{1,0:T(8,128)(2,1)}, bf16[2048,128]{1,0:T(8,128)(2,1)S(1)}, u32[]{:S(2)}, u32[]{:S(2)}) collective-permute-start(bf16[2048,128]{1,0:T(8,128)(2,1)} %copy-done.4), channel_id=1, source_target_pairs={{1,9},{10,2},{3,11},{12,4},{2,1},{4,3},{17,25},{26,18},{19,27},{28... | collective-permute-start | bytes 1572872 | tf_op jit(solution)/shard_map/ppermute | solution.py:349
  35.5 1.9 %collective-permute-start.5 = (bf16[2048,128]{1,0:T(8,128)(2,1)}, bf16[2048,128]{1,0:T(8,128)(2,1)S(1)}, u32[]{:S(2)}, u32[]{:S(2)}) collective-permute-start(bf16[2048,128]{1,0:T(8,128)(2,1)} %copy-done.3), channel_id=1, source_target_pairs={{1,9},{10,2},{3,11},{12,4},{2,1},{4,3},{17,25},{26,18},{19,27},{28... | collective-permute-start | bytes 1572872 | tf_op jit(solution)/shard_map/ppermute | solution.py:349
  37.5 1.6 %copy-done.1 = bf16[128,8192]{1,0:T(8,128)(2,1)S(1)} copy-done((bf16[128,8192]{1,0:T(8,128)(2,1)S(1)}, bf16[128,8192]{1,0:T(8,128)(2,1)}, u32[]{:S(2)}) %copy-start.1) | copy-done | bytes 2097176
  39.1 5.5 %first_half.1 = (f32[1152,256]{1,0:T(8,128)S(1)}, f32[8,128]{1,0:T(8,128)S(1)}) custom-call(s32[14]{0:T(128)S(1)} %pad_add_fusion.1.switch_ref, bf16[128,8192]{1,0:T(8,128)(2,1)S(1)} %get-tuple-element.34.plain_ref, bf16[128,8192]{1,0:T(8,128)(2,1)S(1)} %copy-done.1, bf16[9,8192]{1,0:T(8,128)(2,1)S(1)} %pad_maximum_fusion.coeff_ref, ...), custom_call_target="tpu_custom_call" | custom-call | flops 2415919104 | bytes 4194304 | tf_op jit(solution)/shard_map/first_half/pallas_call | solution.py:202
  44.5 5.7 %first_last.1 = (bf16[9,128,128]{2,1,0:T(8,128)(2,1)S(1)}, bf16[9,128,128]{2,1,0:T(8,128)(2,1)S(1)}, bf16[9,128,128]{2,1,0:T(8,128)(2,1)S(1)}) custom-call(s32[14]{0:T(128)S(1)} %pad_add_fusion.1.switch_ref, bf16[128,8192]{1,0:T(8,128)(2,1)S(1)} %get-tuple-element.34.plain_ref, bf16[128,8192]{1,0:T(8,128)(2,1)S(1)} %copy-done.1, ...), custom_call_target="tpu_custom_call" | custom-call | flops 2415919104 | bytes 4194304 | tf_op jit(solution)/shard_map/first_last/pallas_call | solution.py:202
  50.3 4.1 %second_part.2.rest_0_ = f32[1152,128]{1,0:T(8,128)S(1)} custom-call(s32[6]{0:T(128)S(1)} %pad_add_fusion.switch_ref, bf16[128,8192]{1,0:T(8,128)(2,1)S(1)} %get-tuple-element.34.plain_ref, bf16[128,8192]{1,0:T(8,128)(2,1)S(1)} %copy-done.1, bf16[9,8192]{1,0:T(8,128)(2,1)S(1)} %pad_maximum_fusion.coeff_ref, ...), custom_call_target="tpu_custom_call" | custom-call | flops 1207959552 | bytes 3145728 | tf_op jit(solution)/shard_map/second_part/pallas_call | solution.py:282
  54.4 2.4 %second_part.3.rest_0_ = f32[1152,128]{1,0:T(8,128)S(1)} custom-call(s32[6]{0:T(128)S(1)} %pad_add_fusion.switch_ref, bf16[128,8192]{1,0:T(8,128)(2,1)S(1)} %get-tuple-element.34.plain_ref, bf16[128,8192]{1,0:T(8,128)(2,1)S(1)} %copy-done.1, bf16[9,8192]{1,0:T(8,128)(2,1)S(1)} %pad_maximum_fusion.coeff_ref, ...), custom_call_target="tpu_custom_call" | custom-call | flops 603979776 | bytes 1572864 | tf_op jit(solution)/shard_map/second_part/pallas_call | solution.py:282
  56.7 2.4 %second_last.1 = (bf16[9,128,128]{2,1,0:T(8,128)(2,1)S(1)}, bf16[9,128,128]{2,1,0:T(8,128)(2,1)S(1)}, bf16[9,128,128]{2,1,0:T(8,128)(2,1)S(1)}) custom-call(s32[6]{0:T(128)S(1)} %pad_add_fusion.switch_ref, bf16[128,8192]{1,0:T(8,128)(2,1)S(1)} %get-tuple-element.34.plain_ref, bf16[128,8192]{1,0:T(8,128)(2,1)S(1)} %copy-done.1, ...), custom_call_target="tpu_custom_call" | custom-call | flops 603979776 | bytes 1572864 | tf_op jit(solution)/shard_map/second_last/pallas_call | solution.py:282
  59.2 1.9 %collective-permute-start.8 = (bf16[9,128,128]{2,1,0:T(8,128)(2,1)S(1)}, bf16[9,128,128]{2,1,0:T(8,128)(2,1)S(1)}, u32[]{:S(2)}, u32[]{:S(2)}) collective-permute-start(bf16[9,128,128]{2,1,0:T(8,128)(2,1)S(1)} %get-tuple-element.49), channel_id=1, source_target_pairs={{0,8},{13,5},{14,6},{7,15},{9,1},{2,10},{11,3},{4,12},{1,0},{16,24... | collective-permute-start | bytes 884744 | tf_op jit(solution)/shard_map/ppermute | solution.py:362
  61.1 0.7 collective-permute-start.9
  61.8 5.7 %collective-permute-done.8 = bf16[9,128,128]{2,1,0:T(8,128)(2,1)S(1)} collective-permute-done((bf16[9,128,128]{2,1,0:T(8,128)(2,1)S(1)}, bf16[9,128,128]{2,1,0:T(8,128)(2,1)S(1)}, u32[]{:S(2)}, u32[]{:S(2)}) %collective-permute-start.8) | collective-permute-done | bytes 294944 | tf_op jit(solution)/shard_map/ppermute | solution.py:362
  67.5 0.9 %select_bitcast_fusion = (bf16[1,9,128,128]{3,2,1,0:T(8,128)(2,1)}, bf16[1,9,128,128]{3,2,1,0:T(8,128)(2,1)}) fusion(bf16[9,128,128]{2,1,0:T(8,128)(2,1)S(1)} %collective-permute-done.8, bf16[9,128,128]{2,1,0:T(8,128)(2,1)S(1)} %get-tuple-element.51, pred[]{:T(512)S(6)} %or.59, bf16[9,128,128]{2,1,0:T(8,128)(2,1)S(1)} %collective-permute-done.9, ...), kind=kLoop, calls=%fused_computation | loop fusion | flops 442368 | bytes 1769475 | tf_op jit(solution)/shard_map/broadcast_in_dim | solution.py:367
  (28 shorter events, 1.5 us)
Async XLA Ops:
  0.6 26.0 %collective-permute-start.1 = (bf16[8192,128]{1,0:T(8,128)(2,1)}, bf16[8192,128]{1,0:T(8,128)(2,1)}, u32[]{:S(2)}, u32[]{:S(2)}) collective-permute-start(bf16[8192,128]{1,0:T(8,128)(2,1)} %bitcast.15), channel_id=1, source_target_pairs={{3,2},{5,4},{6,5},{9,8},{10,9},{11,10},{12,11},{13,12},{14,13},{15... | collective-permute-start | bytes 6291464 | tf_op jit(solution)/shard_map/ppermute | solution.py:332
  2.6 24.0 %collective-permute-start.2 = (bf16[8192,128]{1,0:T(8,128)(2,1)}, bf16[8192,128]{1,0:T(8,128)(2,1)}, u32[]{:S(2)}, u32[]{:S(2)}) collective-permute-start(bf16[8192,128]{1,0:T(8,128)(2,1)} %bitcast.16), channel_id=1, source_target_pairs={{8,0},{5,13},{6,14},{15,7},{0,1},{7,6},{24,16},{21,29},{22,30},{31... | collective-permute-start | bytes 6291464 | tf_op jit(solution)/shard_map/ppermute | solution.py:333
  3.9 22.7 %collective-permute-start.3 = (s32[1,4]{1,0:T(1,128)}, s32[1,4]{1,0:T(1,128)S(1)}, u32[]{:S(2)}, u32[]{:S(2)}) collective-permute-start(s32[1,4]{1,0:T(1,128)} %param.3), channel_id=1, source_target_pairs={{3,2},{5,4},{6,5},{9,8},{10,9},{11,10},{12,11},{13,12},{14,13},{15... | collective-permute-start | bytes 56 | tf_op jit(solution)/shard_map/ppermute | solution.py:338
  4.6 22.0 %collective-permute-start.4 = (s32[1,4]{1,0:T(1,128)}, s32[1,4]{1,0:T(1,128)S(1)}, u32[]{:S(2)}, u32[]{:S(2)}) collective-permute-start(s32[1,4]{1,0:T(1,128)} %param.3), channel_id=1, source_target_pairs={{8,0},{5,13},{6,14},{15,7},{0,1},{7,6},{24,16},{21,29},{22,30},{31... | collective-permute-start | bytes 56 | tf_op jit(solution)/shard_map/ppermute | solution.py:337
  5.9 27.6 %collective-permute-start = (s32[1,4]{1,0:T(1,128)}, s32[1,4]{1,0:T(1,128)S(1)}, u32[]{:S(2)}, u32[]{:S(2)}) collective-permute-start(s32[1,4]{1,0:T(1,128)} %param.3), channel_id=1, source_target_pairs={{1,9},{10,2},{3,11},{12,4},{2,1},{4,3},{17,25},{26,18},{19,27},{28... | collective-permute-start | bytes 56 | tf_op jit(solution)/shard_map/ppermute | solution.py:339
  16.4 1.6 %copy-start.2 = (bf16[1024,2,4,128]{3,2,1,0:T(4,128)(2,1)S(1)}, bf16[1024,2,4,128]{3,2,1,0:T(4,128)(2,1)}, u32[]{:S(2)}) copy-start(bf16[1024,2,4,128]{3,2,1,0:T(4,128)(2,1)} %param.2) | copy-start | bytes 6291460
  18.3 0.8 %copy-start.3 = (bf16[2048,128]{1,0:T(8,128)(2,1)}, bf16[2048,128]{1,0:T(8,128)(2,1)S(1)}, u32[]{:S(2)}) copy-start(bf16[2048,128]{1,0:T(8,128)(2,1)S(1)} %get-tuple-element.43) | copy-start | bytes 1572868
  19.1 0.8 %copy-start.4 = (bf16[2048,128]{1,0:T(8,128)(2,1)}, bf16[2048,128]{1,0:T(8,128)(2,1)S(1)}, u32[]{:S(2)}) copy-start(bf16[2048,128]{1,0:T(8,128)(2,1)S(1)} %get-tuple-element.44) | copy-start | bytes 1572868
  19.9 13.5 %copy-start.5 = (s32[1,4]{1,0:T(1,128)S(1)}, s32[1,4]{1,0:T(1,128)}, u32[]{:S(2)}) copy-start(s32[1,4]{1,0:T(1,128)} %param.3) | copy-start | bytes 52
  23.1 1.3 %copy-start = (bf16[128,8192]{1,0:T(8,128)(2,1)}, bf16[128,8192]{1,0:T(8,128)(2,1)S(1)}, u32[]{:S(2)}) copy-start(bf16[128,8192]{1,0:T(8,128)(2,1)S(1)} %get-tuple-element.35.swapped_ref) | copy-start | bytes 6291460
  26.6 23.6 %collective-permute-start.7 = (bf16[4096,128]{1,0:T(8,128)(2,1)S(1)}, bf16[4096,128]{1,0:T(8,128)(2,1)S(1)}, u32[]{:S(2)}, u32[]{:S(2)}) collective-permute-start(bf16[4096,128]{1,0:T(8,128)(2,1)S(1)} %get-tuple-element.45), channel_id=1, source_target_pairs={{1,9},{10,2},{3,11},{12,4},{2,1},{4,3},{17,25},{26,18},{19,27},{28... | collective-permute-start | bytes 3145736 | tf_op jit(solution)/shard_map/ppermute | solution.py:349
  33.5 20.8 %collective-permute-start.6 = (bf16[2048,128]{1,0:T(8,128)(2,1)}, bf16[2048,128]{1,0:T(8,128)(2,1)S(1)}, u32[]{:S(2)}, u32[]{:S(2)}) collective-permute-start(bf16[2048,128]{1,0:T(8,128)(2,1)} %copy-done.4), channel_id=1, source_target_pairs={{1,9},{10,2},{3,11},{12,4},{2,1},{4,3},{17,25},{26,18},{19,27},{28... | collective-permute-start | bytes 1572872 | tf_op jit(solution)/shard_map/ppermute | solution.py:349
  35.5 21.3 %collective-permute-start.5 = (bf16[2048,128]{1,0:T(8,128)(2,1)}, bf16[2048,128]{1,0:T(8,128)(2,1)S(1)}, u32[]{:S(2)}, u32[]{:S(2)}) collective-permute-start(bf16[2048,128]{1,0:T(8,128)(2,1)} %copy-done.3), channel_id=1, source_target_pairs={{1,9},{10,2},{3,11},{12,4},{2,1},{4,3},{17,25},{26,18},{19,27},{28... | collective-permute-start | bytes 1572872 | tf_op jit(solution)/shard_map/ppermute | solution.py:349
  37.5 1.6 %copy-start.1 = (bf16[128,8192]{1,0:T(8,128)(2,1)S(1)}, bf16[128,8192]{1,0:T(8,128)(2,1)}, u32[]{:S(2)}) copy-start(bf16[128,8192]{1,0:T(8,128)(2,1)} %copy-done) | copy-start | bytes 6291460
  59.2 8.4 %collective-permute-start.8 = (bf16[9,128,128]{2,1,0:T(8,128)(2,1)S(1)}, bf16[9,128,128]{2,1,0:T(8,128)(2,1)S(1)}, u32[]{:S(2)}, u32[]{:S(2)}) collective-permute-start(bf16[9,128,128]{2,1,0:T(8,128)(2,1)S(1)} %get-tuple-element.49), channel_id=1, source_target_pairs={{0,8},{13,5},{14,6},{7,15},{9,1},{2,10},{11,3},{4,12},{1,0},{16,24... | collective-permute-start | bytes 884744 | tf_op jit(solution)/shard_map/ppermute | solution.py:362
  61.1 6.4 %collective-permute-start.9 = (bf16[9,128,128]{2,1,0:T(8,128)(2,1)S(1)}, bf16[9,128,128]{2,1,0:T(8,128)(2,1)S(1)}, u32[]{:S(2)}, u32[]{:S(2)}) collective-permute-start(bf16[9,128,128]{2,1,0:T(8,128)(2,1)S(1)} %get-tuple-element.50), channel_id=1, source_target_pairs={{0,7},{7,15},{16,23},{23,31}} | collective-permute-start | bytes 884744 | tf_op jit(solution)/shard_map/ppermute | solution.py:363

commit v30 on v29

--- a/solution.py
+++ b/solution.py
@@ -123,22 +123,15 @@
     return x * weights.reshape(rows, cols)
 
 
-def first_kernel(windows, last, switch_ref, plain_ref, swapped_ref, coeff_ref, near_ref, first_ref, *rest):
+def first_kernel(windows, switch_ref, plain_ref, swapped_ref, coeff_ref, near_ref, first_ref, *rest):
     step = pl.program_id(0)
     cols = plain_ref.shape[0]
     near_mirrored, special = switch_ref[0], switch_ref[1]
-    if last:
-        acc_in, _, near_out, far_out, back_out, acc, scaled, plain, swapped, right = rest
-    else:
-        acc, token_out, scaled, plain, swapped, right = rest
+    near_out, far_out, back_out, acc, scaled, plain, swapped, right = rest
 
     @pl.when(step == 0)
     def _():
-        if last:
-            acc[...] = acc_in[...]
-        else:
-            acc[...] = jnp.zeros_like(acc)
-            token_out[...] = jnp.zeros_like(token_out)
+        acc[...] = jnp.zeros_like(acc)
 
     @pl.when(special == 0)
     def _():
@@ -158,63 +151,52 @@
     far = weigh(right[...], [own * first for own, _, first in zip(*flags)])
     acc[...] += jnp.dot(scaled[...], jnp.concatenate([near, far], axis=1), preferred_element_type=jnp.float32)
 
-    if last:
-        @pl.when(step == pl.num_programs(0) - 1)
-        def _():
-            near_at, far_at = slice(0, cols), slice(cols, 2 * cols)
-
-            @pl.when(special == 0)
-            def _():
-                write_lags(back_out, acc, far_at, cols, True)
-                write_lags(far_out, acc, far_at, cols, False)
-
-            @pl.when(special != 0)
-            def _():
-                write_lags(back_out, acc, far_at, cols, False)
-                write_lags(far_out, acc, far_at, cols, True)
-
-            pl.when(near_mirrored == 0)(lambda: write_lags(near_out, acc, near_at, cols, False))
-            pl.when(near_mirrored != 0)(lambda: write_lags(near_out, acc, near_at, cols, True))
-
-
-def first_sums(switch, own, coeffs, near_in, first_in, earlier=None):
+    @pl.when(step == pl.num_programs(0) - 1)
+    def _():
+        near_at, far_at = slice(0, cols), slice(cols, 2 * cols)
+
+        @pl.when(special == 0)
+        def _():
+            write_lags(back_out, acc, far_at, cols, True)
+            write_lags(far_out, acc, far_at, cols, False)
+
+        @pl.when(special != 0)
+        def _():
+            write_lags(back_out, acc, far_at, cols, False)
+            write_lags(far_out, acc, far_at, cols, True)
+
+        pl.when(near_mirrored == 0)(lambda: write_lags(near_out, acc, near_at, cols, False))
+        pl.when(near_mirrored != 0)(lambda: write_lags(near_out, acc, near_at, cols, True))
+
+
+def first_sums(switch, own, coeffs, near_in, first_in):
     rows, cols = near_in.shape
-    steps = rows // STEP // 2
-    skip = 0 if earlier is None else steps
     windows = (switch.shape[0] - 2) // 3
     result = jax.ShapeDtypeStruct((LAGS, cols, cols), jnp.bfloat16)
-    total = jax.ShapeDtypeStruct((LAGS * cols, 2 * cols), jnp.float32)
-    total_spec = pl.BlockSpec(total.shape, lambda s, on: (0, 0))
-    token = jax.ShapeDtypeStruct((8, cols), jnp.float32)
-    token_spec = pl.BlockSpec(token.shape, lambda s, on: (0, 0))
-    left = pl.BlockSpec((cols, STEP), lambda s, on: (0, s + skip))
-    right = pl.BlockSpec((STEP, cols), lambda s, on: (s + skip, 0))
-    in_specs = [left, left, pl.BlockSpec((LAGS, STEP), lambda s, on: (0, s + skip)), right, right]
-    scratch = [pltpu.VMEM((LAGS * cols, STEP), jnp.bfloat16)] + [pltpu.VMEM((cols, STEP), jnp.bfloat16)] * 2
-    scratch += [pltpu.VMEM((STEP, cols), jnp.bfloat16)]
-    if earlier is None:
-        out_shape, out_specs, earlier = [total, token], [total_spec, token_spec], []
-    else:
-        in_specs += [total_spec, token_spec]
-        out_shape = [result] * 3
-        out_specs = [pl.BlockSpec(result.shape, lambda s, on: (0, 0, 0))] * 3
-        scratch = [pltpu.VMEM(total.shape, jnp.float32)] + scratch
+    left = pl.BlockSpec((cols, STEP), lambda s, on: (0, s))
+    right = pl.BlockSpec((STEP, cols), lambda s, on: (s, 0))
     return pl.pallas_call(
-        functools.partial(first_kernel, windows, bool(earlier)),
+        functools.partial(first_kernel, windows),
         grid_spec=pltpu.PrefetchScalarGridSpec(
             num_scalar_prefetch=1,
-            grid=(steps,),
-            in_specs=in_specs,
-            out_specs=out_specs,
-            scratch_shapes=scratch,
+            grid=(rows // STEP,),
+            in_specs=[left, left, pl.BlockSpec((LAGS, STEP), lambda s, on: (0, s)), right, right],
+            out_specs=[pl.BlockSpec(result.shape, lambda s, on: (0, 0, 0))] * 3,
+            scratch_shapes=[
+                pltpu.VMEM((LAGS * cols, 2 * cols), jnp.float32),
+                pltpu.VMEM((LAGS * cols, STEP), jnp.bfloat16),
+                pltpu.VMEM((cols, STEP), jnp.bfloat16),
+                pltpu.VMEM((cols, STEP), jnp.bfloat16),
+                pltpu.VMEM((STEP, cols), jnp.bfloat16),
+            ],
         ),
-        out_shape=out_shape,
+        out_shape=[result] * 3,
         compiler_params=PARAMS,
         cost_estimate=pl.CostEstimate(
-            flops=2 * LAGS * cols * cols * rows, bytes_accessed=4 * rows * cols, transcendentals=0
+            flops=4 * LAGS * cols * cols * rows, bytes_accessed=8 * rows * cols, transcendentals=0
         ),
-        name="first_last" if earlier else "first_half",
-    )(switch, *own, coeffs, near_in, first_in, *earlier)
+        name="first_sums",
+    )(switch, *own, coeffs, near_in, first_in)
 
 
 def second_kernel(windows, first, last, switch_ref, plain_ref, swapped_ref, coeff_ref, partner_ref, *rest):
@@ -347,9 +329,7 @@
     )
     first_switch = switch(me == 0, special, quality[0], near_flags, first_flags)
     second_in = [lax.ppermute(part, "chan", second_pairs) for part in parts]
-    operands = first_switch, own, coeffs, near_in, first_in
-    total, token = first_sums(*operands)
-    near, far, back = first_sums(*operands, [total, token])
+    near, far, back = first_sums(first_switch, own, coeffs, near_in, first_in)
     second_switch, near = lax.optimization_barrier((second_switch, near))
     starts = [0, parts[0].shape[0], parts[0].shape[0] + parts[1].shape[0]]
     total = second_sums(second_switch, own, coeffs, second_in[0], starts[0])

time: 68.9 us -> 69.2 us (level)
  waiting for transfers between devices: 5.74 us -> 7.57 us
  Pallas kernels: 23.5 us -> 22 us
    ppermute x3, waiting for transfers between devices: 0.01 us -> 1.74 us  [local(): second_in = [lax.ppermute(part, 'chan', second_pairs) for part in parts]]
    pallas_call x2 -> x1, Pallas kernels: 11.1 us -> 9.57 us  [first_sums(): pl.pallas_call(functools.partial(first_kernel, windows), grid_spec=pltpu....]
  transfers between devices with their start and end apart: 10 -> 10, of which waited for: 1 -> 2; matrix products, arithmetic and copies ran while one was open for 3% -> 3% of each run, Pallas kernels for 31% -> 28%
where the time goes in v30:
time: 69.2 us; the launch traced here: 68.7 us
  starting transfers between devices  29 us (42%)
  Pallas kernels  22 us (32%)
  waiting for transfers between devices  7.57 us (11%)
  local copies, waits for them, and re-layouts  6.1 us (9%)
  other arithmetic  3.15 us (5%)
  between operations  0.95 us (1%)
    ppermute x3, starting transfers between devices, local(): second_in = [lax.ppermute(part, 'chan', second_pairs) for part in parts]  10.6 us
    ppermute x1, starting transfers between devices, local(): second_flags = lax.ppermute(quality, 'chan', second_pairs)[0]  10.5 us
    pallas_call x1, Pallas kernels, first_sums(): pl.pallas_call(functools.partial(first_kernel, windows), grid_spec=pltpu....  9.57 us
    pallas_call x3, Pallas kernels, second_sums(): pl.pallas_call(functools.partial(second_kernel, windows, not earlier, las...  8.89 us
    unnamed x12, local copies, waits for them, and re-layouts  6.1 us
    ppermute x1, waiting for transfers between devices, local(): returned = lax.ppermute(back, 'chan', back_pairs)  5.82 us
    pallas_call x1, Pallas kernels, turn(): pl.pallas_call(turn_kernel, grid=(rows // STEP,), in_specs=[pl.BlockSpec(...  3.15 us
    ppermute x1, starting transfers between devices, local(): near_in = lax.ppermute(block, 'chan', near_pairs)  2 us
  transfers between devices with their start and end apart: 10, of which 2 were waited for; matrix products, arithmetic and copies ran while one was open for 3% of the time, Pallas kernels for 28%

profile of v30, /device:TPU:1, one launch (start us, length us, event | category | flops | bytes accessed | tf_op | source)
XLA Modules:
  0.0 68.7 jit_solution(10701045267039501760)
XLA Ops:
  0.6 2.0 %collective-permute-start.1 = (bf16[8192,128]{1,0:T(8,128)(2,1)}, bf16[8192,128]{1,0:T(8,128)(2,1)}, u32[]{:S(2)}, u32[]{:S(2)}) collective-permute-start(bf16[8192,128]{1,0:T(8,128)(2,1)} %bitcast.15), channel_id=1, source_target_pairs={{3,2},{5,4},{6,5},{9,8},{10,9},{11,10},{12,11},{13,12},{14,13},{15... | collective-permute-start | bytes 6291464 | tf_op jit(solution)/shard_map/ppermute | solution.py:314
  2.6 1.3 %collective-permute-start.2 = (bf16[8192,128]{1,0:T(8,128)(2,1)}, bf16[8192,128]{1,0:T(8,128)(2,1)}, u32[]{:S(2)}, u32[]{:S(2)}) collective-permute-start(bf16[8192,128]{1,0:T(8,128)(2,1)} %bitcast.16), channel_id=1, source_target_pairs={{8,0},{5,13},{6,14},{15,7},{0,1},{7,6},{24,16},{21,29},{22,30},{31... | collective-permute-start | bytes 6291464 | tf_op jit(solution)/shard_map/ppermute | solution.py:315
  4.6 1.3 %collective-permute-start.4 = (s32[1,4]{1,0:T(1,128)}, s32[1,4]{1,0:T(1,128)S(1)}, u32[]{:S(2)}, u32[]{:S(2)}) collective-permute-start(s32[1,4]{1,0:T(1,128)} %param.3), channel_id=1, source_target_pairs={{8,0},{5,13},{6,14},{15,7},{0,1},{7,6},{24,16},{21,29},{22,30},{31... | collective-permute-start | bytes 56 | tf_op jit(solution)/shard_map/ppermute | solution.py:319
  5.9 10.5 %collective-permute-start = (s32[1,4]{1,0:T(1,128)}, s32[1,4]{1,0:T(1,128)S(1)}, u32[]{:S(2)}, u32[]{:S(2)}) collective-permute-start(s32[1,4]{1,0:T(1,128)} %param.3), channel_id=1, source_target_pairs={{1,9},{10,2},{3,11},{12,4},{2,1},{4,3},{17,25},{26,18},{19,27},{28... | collective-permute-start | bytes 56 | tf_op jit(solution)/shard_map/ppermute | solution.py:321
  16.4 1.6 %copy-done.2 = bf16[1024,2,4,128]{3,2,1,0:T(4,128)(2,1)S(1)} copy-done((bf16[1024,2,4,128]{3,2,1,0:T(4,128)(2,1)S(1)}, bf16[1024,2,4,128]{3,2,1,0:T(4,128)(2,1)}, u32[]{:S(2)}) %copy-start.2) | copy-done | bytes 2097176
  18.3 0.8 %copy-done.3 = bf16[2048,128]{1,0:T(8,128)(2,1)} copy-done((bf16[2048,128]{1,0:T(8,128)(2,1)}, bf16[2048,128]{1,0:T(8,128)(2,1)S(1)}, u32[]{:S(2)}) %copy-start.3) | copy-done | bytes 524312
  19.1 0.8 %copy-done.4 = bf16[2048,128]{1,0:T(8,128)(2,1)} copy-done((bf16[2048,128]{1,0:T(8,128)(2,1)}, bf16[2048,128]{1,0:T(8,128)(2,1)S(1)}, u32[]{:S(2)}) %copy-start.4) | copy-done | bytes 524312
  19.9 3.2 %turn.1 = (bf16[128,8192]{1,0:T(8,128)(2,1)S(1)}, bf16[128,8192]{1,0:T(8,128)(2,1)S(1)}) custom-call(bf16[8192,128]{1,0:T(8,128)(2,1)S(1)} %bitcast.18), custom_call_target="tpu_custom_call" | custom-call | bytes 6291456 | tf_op jit(solution)/shard_map/turn/pallas_call | solution.py:83
  23.1 1.3 %copy-done = bf16[128,8192]{1,0:T(8,128)(2,1)} copy-done((bf16[128,8192]{1,0:T(8,128)(2,1)}, bf16[128,8192]{1,0:T(8,128)(2,1)S(1)}, u32[]{:S(2)}) %copy-start) | copy-done | bytes 2097176
  24.6 0.9 %multiply_convert_fusion = (bf16[5,8192]{1,0:T(8,128)(2,1)S(1)}, f32[5,8192]{1,0:T(8,128)S(1)}) fusion(f32[8192]{0:T(1024)S(1)} %fusion.9, f32[5]{0:T(128)S(1)} %iota_multiply_fusion), kind=kLoop, calls=%fused_computation.4 | loop fusion | flops 122880 | bytes 278548 | tf_op jit(solution)/shard_map/convert
  25.6 0.9 %fusion.2 = bf16[4,8192]{1,0:T(4,128)(2,1)S(1)} fusion(f32[5,8192]{1,0:T(8,128)S(1)} %get-tuple-element.51, f32[8192]{0:T(1024)S(1)} %select_multiply_fusion), kind=kLoop, calls=%fused_computation.8 | loop fusion | flops 98304 | bytes 229376 | tf_op jit(solution)/shard_map/convert.1
  26.6 6.8 %collective-permute-start.7 = (bf16[4096,128]{1,0:T(8,128)(2,1)S(1)}, bf16[4096,128]{1,0:T(8,128)(2,1)S(1)}, u32[]{:S(2)}, u32[]{:S(2)}) collective-permute-start(bf16[4096,128]{1,0:T(8,128)(2,1)S(1)} %get-tuple-element.41), channel_id=1, source_target_pairs={{1,9},{10,2},{3,11},{12,4},{2,1},{4,3},{17,25},{26,18},{19,27},{28... | collective-permute-start | bytes 3145736 | tf_op jit(solution)/shard_map/ppermute | solution.py:331
  33.5 1.9 %collective-permute-start.6 = (bf16[2048,128]{1,0:T(8,128)(2,1)}, bf16[2048,128]{1,0:T(8,128)(2,1)S(1)}, u32[]{:S(2)}, u32[]{:S(2)}) collective-permute-start(bf16[2048,128]{1,0:T(8,128)(2,1)} %copy-done.4), channel_id=1, source_target_pairs={{1,9},{10,2},{3,11},{12,4},{2,1},{4,3},{17,25},{26,18},{19,27},{28... | collective-permute-start | bytes 1572872 | tf_op jit(solution)/shard_map/ppermute | solution.py:331
  35.5 1.9 %collective-permute-start.5 = (bf16[2048,128]{1,0:T(8,128)(2,1)}, bf16[2048,128]{1,0:T(8,128)(2,1)S(1)}, u32[]{:S(2)}, u32[]{:S(2)}) collective-permute-start(bf16[2048,128]{1,0:T(8,128)(2,1)} %copy-done.3), channel_id=1, source_target_pairs={{1,9},{10,2},{3,11},{12,4},{2,1},{4,3},{17,25},{26,18},{19,27},{28... | collective-permute-start | bytes 1572872 | tf_op jit(solution)/shard_map/ppermute | solution.py:331
  37.5 1.6 %copy-done.1 = bf16[128,8192]{1,0:T(8,128)(2,1)S(1)} copy-done((bf16[128,8192]{1,0:T(8,128)(2,1)S(1)}, bf16[128,8192]{1,0:T(8,128)(2,1)}, u32[]{:S(2)}) %copy-start.1) | copy-done | bytes 2097176
  39.1 9.6 %first_sums.1 = (bf16[9,128,128]{2,1,0:T(8,128)(2,1)S(1)}, bf16[9,128,128]{2,1,0:T(8,128)(2,1)S(1)}, bf16[9,128,128]{2,1,0:T(8,128)(2,1)S(1)}) custom-call(s32[14]{0:T(128)S(1)} %pad_add_fusion.1.switch_ref, bf16[128,8192]{1,0:T(8,128)(2,1)S(1)} %get-tuple-element.32.plain_ref, bf16[128,8192]{1,0:T(8,128)(2,1)S(1)} %copy-done.1, ...), custom_call_target="tpu_custom_call" | custom-call | flops 4831838208 | bytes 8388608 | tf_op jit(solution)/shard_map/first_sums/pallas_call | solution.py:178
  48.7 4.1 %second_part.2.rest_0_ = f32[1152,128]{1,0:T(8,128)S(1)} custom-call(s32[6]{0:T(128)S(1)} %pad_add_fusion.switch_ref, bf16[128,8192]{1,0:T(8,128)(2,1)S(1)} %get-tuple-element.32.plain_ref, bf16[128,8192]{1,0:T(8,128)(2,1)S(1)} %copy-done.1, bf16[9,8192]{1,0:T(8,128)(2,1)S(1)} %pad_maximum_fusion.coeff_ref, ...), custom_call_target="tpu_custom_call" | custom-call | flops 1207959552 | bytes 3145728 | tf_op jit(solution)/shard_map/second_part/pallas_call | solution.py:264
  52.8 2.3 %second_part.3.rest_0_ = f32[1152,128]{1,0:T(8,128)S(1)} custom-call(s32[6]{0:T(128)S(1)} %pad_add_fusion.switch_ref, bf16[128,8192]{1,0:T(8,128)(2,1)S(1)} %get-tuple-element.32.plain_ref, bf16[128,8192]{1,0:T(8,128)(2,1)S(1)} %copy-done.1, bf16[9,8192]{1,0:T(8,128)(2,1)S(1)} %pad_maximum_fusion.coeff_ref, ...), custom_call_target="tpu_custom_call" | custom-call | flops 603979776 | bytes 1572864 | tf_op jit(solution)/shard_map/second_part/pallas_call | solution.py:264
  55.2 1.7 %collective-permute-done.5.partner_ref = bf16[2048,128]{1,0:T(8,128)(2,1)S(1)} collective-permute-done((bf16[2048,128]{1,0:T(8,128)(2,1)}, bf16[2048,128]{1,0:T(8,128)(2,1)S(1)}, u32[]{:S(2)}, u32[]{:S(2)}) %collective-permute-start.5) | collective-permute-done | bytes 524320 | tf_op jit(solution)/shard_map/ppermute | solution.py:331
  56.9 2.4 %second_last.1 = (bf16[9,128,128]{2,1,0:T(8,128)(2,1)S(1)}, bf16[9,128,128]{2,1,0:T(8,128)(2,1)S(1)}, bf16[9,128,128]{2,1,0:T(8,128)(2,1)S(1)}) custom-call(s32[6]{0:T(128)S(1)} %pad_add_fusion.switch_ref, bf16[128,8192]{1,0:T(8,128)(2,1)S(1)} %get-tuple-element.32.plain_ref, bf16[128,8192]{1,0:T(8,128)(2,1)S(1)} %copy-done.1, ...), custom_call_target="tpu_custom_call" | custom-call | flops 603979776 | bytes 1572864 | tf_op jit(solution)/shard_map/second_last/pallas_call | solution.py:264
  59.3 1.9 %collective-permute-start.8 = (bf16[9,128,128]{2,1,0:T(8,128)(2,1)S(1)}, bf16[9,128,128]{2,1,0:T(8,128)(2,1)S(1)}, u32[]{:S(2)}, u32[]{:S(2)}) collective-permute-start(bf16[9,128,128]{2,1,0:T(8,128)(2,1)S(1)} %get-tuple-element.45), channel_id=1, source_target_pairs={{0,8},{13,5},{14,6},{7,15},{9,1},{2,10},{11,3},{4,12},{1,0},{16,24... | collective-permute-start | bytes 884744 | tf_op jit(solution)/shard_map/ppermute | solution.py:342
  61.3 0.7 collective-permute-start.9
  62.0 5.8 %collective-permute-done.8 = bf16[9,128,128]{2,1,0:T(8,128)(2,1)S(1)} collective-permute-done((bf16[9,128,128]{2,1,0:T(8,128)(2,1)S(1)}, bf16[9,128,128]{2,1,0:T(8,128)(2,1)S(1)}, u32[]{:S(2)}, u32[]{:S(2)}) %collective-permute-start.8) | collective-permute-done | bytes 294944 | tf_op jit(solution)/shard_map/ppermute | solution.py:342
  67.8 0.9 %select_bitcast_fusion = (bf16[1,9,128,128]{3,2,1,0:T(8,128)(2,1)}, bf16[1,9,128,128]{3,2,1,0:T(8,128)(2,1)}) fusion(bf16[9,128,128]{2,1,0:T(8,128)(2,1)S(1)} %collective-permute-done.8, bf16[9,128,128]{2,1,0:T(8,128)(2,1)S(1)} %get-tuple-element.47, pred[]{:T(512)S(6)} %or.59, bf16[9,128,128]{2,1,0:T(8,128)(2,1)S(1)} %collective-permute-done.9, ...), kind=kLoop, calls=%fused_computation | loop fusion | flops 442368 | bytes 1769475 | tf_op jit(solution)/shard_map/broadcast_in_dim | solution.py:347
  (27 shorter events, 1.5 us)
Async XLA Ops:
  0.6 26.0 %collective-permute-start.1 = (bf16[8192,128]{1,0:T(8,128)(2,1)}, bf16[8192,128]{1,0:T(8,128)(2,1)}, u32[]{:S(2)}, u32[]{:S(2)}) collective-permute-start(bf16[8192,128]{1,0:T(8,128)(2,1)} %bitcast.15), channel_id=1, source_target_pairs={{3,2},{5,4},{6,5},{9,8},{10,9},{11,10},{12,11},{13,12},{14,13},{15... | collective-permute-start | bytes 6291464 | tf_op jit(solution)/shard_map/ppermute | solution.py:314
  2.6 24.0 %collective-permute-start.2 = (bf16[8192,128]{1,0:T(8,128)(2,1)}, bf16[8192,128]{1,0:T(8,128)(2,1)}, u32[]{:S(2)}, u32[]{:S(2)}) collective-permute-start(bf16[8192,128]{1,0:T(8,128)(2,1)} %bitcast.16), channel_id=1, source_target_pairs={{8,0},{5,13},{6,14},{15,7},{0,1},{7,6},{24,16},{21,29},{22,30},{31... | collective-permute-start | bytes 6291464 | tf_op jit(solution)/shard_map/ppermute | solution.py:315
  3.9 22.7 %collective-permute-start.3 = (s32[1,4]{1,0:T(1,128)}, s32[1,4]{1,0:T(1,128)S(1)}, u32[]{:S(2)}, u32[]{:S(2)}) collective-permute-start(s32[1,4]{1,0:T(1,128)} %param.3), channel_id=1, source_target_pairs={{3,2},{5,4},{6,5},{9,8},{10,9},{11,10},{12,11},{13,12},{14,13},{15... | collective-permute-start | bytes 56 | tf_op jit(solution)/shard_map/ppermute | solution.py:320
  4.6 22.0 %collective-permute-start.4 = (s32[1,4]{1,0:T(1,128)}, s32[1,4]{1,0:T(1,128)S(1)}, u32[]{:S(2)}, u32[]{:S(2)}) collective-permute-start(s32[1,4]{1,0:T(1,128)} %param.3), channel_id=1, source_target_pairs={{8,0},{5,13},{6,14},{15,7},{0,1},{7,6},{24,16},{21,29},{22,30},{31... | collective-permute-start | bytes 56 | tf_op jit(solution)/shard_map/ppermute | solution.py:319
  5.9 27.5 %collective-permute-start = (s32[1,4]{1,0:T(1,128)}, s32[1,4]{1,0:T(1,128)S(1)}, u32[]{:S(2)}, u32[]{:S(2)}) collective-permute-start(s32[1,4]{1,0:T(1,128)} %param.3), channel_id=1, source_target_pairs={{1,9},{10,2},{3,11},{12,4},{2,1},{4,3},{17,25},{26,18},{19,27},{28... | collective-permute-start | bytes 56 | tf_op jit(solution)/shard_map/ppermute | solution.py:321
  16.4 1.6 %copy-start.2 = (bf16[1024,2,4,128]{3,2,1,0:T(4,128)(2,1)S(1)}, bf16[1024,2,4,128]{3,2,1,0:T(4,128)(2,1)}, u32[]{:S(2)}) copy-start(bf16[1024,2,4,128]{3,2,1,0:T(4,128)(2,1)} %param.2) | copy-start | bytes 6291460
  18.3 0.8 %copy-start.3 = (bf16[2048,128]{1,0:T(8,128)(2,1)}, bf16[2048,128]{1,0:T(8,128)(2,1)S(1)}, u32[]{:S(2)}) copy-start(bf16[2048,128]{1,0:T(8,128)(2,1)S(1)} %get-tuple-element.39) | copy-start | bytes 1572868
  19.1 0.8 %copy-start.4 = (bf16[2048,128]{1,0:T(8,128)(2,1)}, bf16[2048,128]{1,0:T(8,128)(2,1)S(1)}, u32[]{:S(2)}) copy-start(bf16[2048,128]{1,0:T(8,128)(2,1)S(1)} %get-tuple-element.40) | copy-start | bytes 1572868
  19.9 13.5 %copy-start.5 = (s32[1,4]{1,0:T(1,128)S(1)}, s32[1,4]{1,0:T(1,128)}, u32[]{:S(2)}) copy-start(s32[1,4]{1,0:T(1,128)} %param.3) | copy-start | bytes 52
  23.1 1.3 %copy-start = (bf16[128,8192]{1,0:T(8,128)(2,1)}, bf16[128,8192]{1,0:T(8,128)(2,1)S(1)}, u32[]{:S(2)}) copy-start(bf16[128,8192]{1,0:T(8,128)(2,1)S(1)} %get-tuple-element.33.swapped_ref) | copy-start | bytes 6291460
  26.6 22.1 %collective-permute-start.7 = (bf16[4096,128]{1,0:T(8,128)(2,1)S(1)}, bf16[4096,128]{1,0:T(8,128)(2,1)S(1)}, u32[]{:S(2)}, u32[]{:S(2)}) collective-permute-start(bf16[4096,128]{1,0:T(8,128)(2,1)S(1)} %get-tuple-element.41), channel_id=1, source_target_pairs={{1,9},{10,2},{3,11},{12,4},{2,1},{4,3},{17,25},{26,18},{19,27},{28... | collective-permute-start | bytes 3145736 | tf_op jit(solution)/shard_map/ppermute | solution.py:331
  33.5 19.3 %collective-permute-start.6 = (bf16[2048,128]{1,0:T(8,128)(2,1)}, bf16[2048,128]{1,0:T(8,128)(2,1)S(1)}, u32[]{:S(2)}, u32[]{:S(2)}) collective-permute-start(bf16[2048,128]{1,0:T(8,128)(2,1)} %copy-done.4), channel_id=1, source_target_pairs={{1,9},{10,2},{3,11},{12,4},{2,1},{4,3},{17,25},{26,18},{19,27},{28... | collective-permute-start | bytes 1572872 | tf_op jit(solution)/shard_map/ppermute | solution.py:331
  35.5 21.4 %collective-permute-start.5 = (bf16[2048,128]{1,0:T(8,128)(2,1)}, bf16[2048,128]{1,0:T(8,128)(2,1)S(1)}, u32[]{:S(2)}, u32[]{:S(2)}) collective-permute-start(bf16[2048,128]{1,0:T(8,128)(2,1)} %copy-done.3), channel_id=1, source_target_pairs={{1,9},{10,2},{3,11},{12,4},{2,1},{4,3},{17,25},{26,18},{19,27},{28... | collective-permute-start | bytes 1572872 | tf_op jit(solution)/shard_map/ppermute | solution.py:331
  37.5 1.6 %copy-start.1 = (bf16[128,8192]{1,0:T(8,128)(2,1)S(1)}, bf16[128,8192]{1,0:T(8,128)(2,1)}, u32[]{:S(2)}) copy-start(bf16[128,8192]{1,0:T(8,128)(2,1)} %copy-done) | copy-start | bytes 6291460
  59.3 8.5 %collective-permute-start.8 = (bf16[9,128,128]{2,1,0:T(8,128)(2,1)S(1)}, bf16[9,128,128]{2,1,0:T(8,128)(2,1)S(1)}, u32[]{:S(2)}, u32[]{:S(2)}) collective-permute-start(bf16[9,128,128]{2,1,0:T(8,128)(2,1)S(1)} %get-tuple-element.45), channel_id=1, source_target_pairs={{0,8},{13,5},{14,6},{7,15},{9,1},{2,10},{11,3},{4,12},{1,0},{16,24... | collective-permute-start | bytes 884744 | tf_op jit(solution)/shard_map/ppermute | solution.py:342
  61.3 6.5 %collective-permute-start.9 = (bf16[9,128,128]{2,1,0:T(8,128)(2,1)S(1)}, bf16[9,128,128]{2,1,0:T(8,128)(2,1)S(1)}, u32[]{:S(2)}, u32[]{:S(2)}) collective-permute-start(bf16[9,128,128]{2,1,0:T(8,128)(2,1)S(1)} %get-tuple-element.46), channel_id=1, source_target_pairs={{0,7},{7,15},{16,23},{23,31}} | collective-permute-start | bytes 884744 | tf_op jit(solution)/shard_map/ppermute | solution.py:343

commit v31 on v30

--- a/solution.py
+++ b/solution.py
@@ -11,7 +11,7 @@
 HL = 4
 LAGS = 2 * HL + 1
 STEP = 1024
-ENDS = (4, 6, 8)
+ENDS = (5, 7, 8)
 PARAMS = pltpu.CompilerParams(vmem_limit_bytes=16 * 1024 * 1024)
 
 

time: 69.2 us -> 68.9 us (level)
  waiting for transfers between devices: 7.57 us -> 5.74 us
  Pallas kernels: 22 us -> 22.9 us
  starting transfers between devices: 29 us -> 29.7 us
    ppermute x3, waiting for transfers between devices: 1.74 us -> 0.01 us  [local(): second_in = [lax.ppermute(part, 'chan', second_pairs) for part in parts]]
    pallas_call x3, Pallas kernels: 8.89 us -> 9.87 us  [second_sums(): pl.pallas_call(functools.partial(second_kernel, windows, not earlier, las...]
    ppermute x3, starting transfers between devices: 10.6 us -> 11.4 us  [local(): second_in = [lax.ppermute(part, 'chan', second_pairs) for part in parts]]
    unnamed x12 -> x10, local copies, waits for them, and re-layouts: 6.1 us -> 5.57 us
  transfers between devices with their start and end apart: 10 -> 10, of which waited for: 2 -> 1; matrix products, arithmetic and copies ran while one was open for 3% -> 3% of each run, Pallas kernels for 28% -> 32%
where the time goes in v31:
time: 68.9 us; the launch traced here: 68 us
  starting transfers between devices  29.7 us (43%)
  Pallas kernels  22.9 us (33%)
  waiting for transfers between devices  5.74 us (8%)
  local copies, waits for them, and re-layouts  5.57 us (8%)
  other arithmetic  3.15 us (5%)
  between operations  0.92 us (1%)
    ppermute x3, starting transfers between devices, local(): second_in = [lax.ppermute(part, 'chan', second_pairs) for part in parts]  11.4 us
    ppermute x1, starting transfers between devices, local(): second_flags = lax.ppermute(quality, 'chan', second_pairs)[0]  10.5 us
    pallas_call x3, Pallas kernels, second_sums(): pl.pallas_call(functools.partial(second_kernel, windows, not earlier, las...  9.87 us
    pallas_call x1, Pallas kernels, first_sums(): pl.pallas_call(functools.partial(first_kernel, windows), grid_spec=pltpu....  9.57 us
    ppermute x1, waiting for transfers between devices, local(): returned = lax.ppermute(back, 'chan', back_pairs)  5.71 us
    unnamed x10, local copies, waits for them, and re-layouts  5.57 us
    pallas_call x1, Pallas kernels, turn(): pl.pallas_call(turn_kernel, grid=(rows // STEP,), in_specs=[pl.BlockSpec(...  3.15 us
    ppermute x1, starting transfers between devices, local(): near_in = lax.ppermute(block, 'chan', near_pairs)  2.01 us
  transfers between devices with their start and end apart: 10, of which 1 were waited for; matrix products, arithmetic and copies ran while one was open for 3% of the time, Pallas kernels for 32%

profile of v31, /device:TPU:1, one launch (start us, length us, event | category | flops | bytes accessed | tf_op | source)
XLA Modules:
  0.0 68.0 jit_solution(16038708825367575767)
XLA Ops:
  0.6 2.0 %collective-permute-start.1 = (bf16[8192,128]{1,0:T(8,128)(2,1)}, bf16[8192,128]{1,0:T(8,128)(2,1)}, u32[]{:S(2)}, u32[]{:S(2)}) collective-permute-start(bf16[8192,128]{1,0:T(8,128)(2,1)} %bitcast.15), channel_id=1, source_target_pairs={{3,2},{5,4},{6,5},{9,8},{10,9},{11,10},{12,11},{13,12},{14,13},{15... | collective-permute-start | bytes 6291464 | tf_op jit(solution)/shard_map/ppermute | solution.py:314
  2.6 1.3 %collective-permute-start.2 = (bf16[8192,128]{1,0:T(8,128)(2,1)}, bf16[8192,128]{1,0:T(8,128)(2,1)}, u32[]{:S(2)}, u32[]{:S(2)}) collective-permute-start(bf16[8192,128]{1,0:T(8,128)(2,1)} %bitcast.16), channel_id=1, source_target_pairs={{8,0},{5,13},{6,14},{15,7},{0,1},{7,6},{24,16},{21,29},{22,30},{31... | collective-permute-start | bytes 6291464 | tf_op jit(solution)/shard_map/ppermute | solution.py:315
  3.9 0.7 collective-permute-start.3
  4.6 1.3 %collective-permute-start.4 = (s32[1,4]{1,0:T(1,128)}, s32[1,4]{1,0:T(1,128)S(1)}, u32[]{:S(2)}, u32[]{:S(2)}) collective-permute-start(s32[1,4]{1,0:T(1,128)} %param.3), channel_id=1, source_target_pairs={{8,0},{5,13},{6,14},{15,7},{0,1},{7,6},{24,16},{21,29},{22,30},{31... | collective-permute-start | bytes 56 | tf_op jit(solution)/shard_map/ppermute | solution.py:319
  5.9 10.5 %collective-permute-start = (s32[1,4]{1,0:T(1,128)}, s32[1,4]{1,0:T(1,128)S(1)}, u32[]{:S(2)}, u32[]{:S(2)}) collective-permute-start(s32[1,4]{1,0:T(1,128)} %param.3), channel_id=1, source_target_pairs={{1,9},{10,2},{3,11},{12,4},{2,1},{4,3},{17,25},{26,18},{19,27},{28... | collective-permute-start | bytes 56 | tf_op jit(solution)/shard_map/ppermute | solution.py:321
  16.4 1.6 %copy-done.2 = bf16[1024,2,4,128]{3,2,1,0:T(4,128)(2,1)S(1)} copy-done((bf16[1024,2,4,128]{3,2,1,0:T(4,128)(2,1)S(1)}, bf16[1024,2,4,128]{3,2,1,0:T(4,128)(2,1)}, u32[]{:S(2)}) %copy-start.2) | copy-done | bytes 2097176
  18.0 0.3 split.1
  18.3 1.0 %copy-done.3 = bf16[5120,128]{1,0:T(8,128)(2,1)} copy-done((bf16[5120,128]{1,0:T(8,128)(2,1)}, bf16[5120,128]{1,0:T(8,128)(2,1)S(1)}, u32[]{:S(2)}) %copy-start.3) | copy-done | bytes 1310744
  19.4 3.1 %turn.1 = (bf16[128,8192]{1,0:T(8,128)(2,1)S(1)}, bf16[128,8192]{1,0:T(8,128)(2,1)S(1)}) custom-call(bf16[8192,128]{1,0:T(8,128)(2,1)S(1)} %bitcast.18), custom_call_target="tpu_custom_call" | custom-call | bytes 6291456 | tf_op jit(solution)/shard_map/turn/pallas_call | solution.py:83
  22.6 1.3 %copy-done = bf16[128,8192]{1,0:T(8,128)(2,1)} copy-done((bf16[128,8192]{1,0:T(8,128)(2,1)}, bf16[128,8192]{1,0:T(8,128)(2,1)S(1)}, u32[]{:S(2)}) %copy-start) | copy-done | bytes 2097176
  23.9 0.9 %multiply_convert_fusion = (bf16[5,8192]{1,0:T(8,128)(2,1)S(1)}, f32[5,8192]{1,0:T(8,128)S(1)}) fusion(f32[8192]{0:T(1024)S(1)} %fusion.9, f32[5]{0:T(128)S(1)} %iota_multiply_fusion), kind=kLoop, calls=%fused_computation.4 | loop fusion | flops 122880 | bytes 278548 | tf_op jit(solution)/shard_map/convert
  24.9 0.9 %fusion.2 = bf16[4,8192]{1,0:T(4,128)(2,1)S(1)} fusion(f32[5,8192]{1,0:T(8,128)S(1)} %get-tuple-element.51, f32[8192]{0:T(1024)S(1)} %select_multiply_fusion), kind=kLoop, calls=%fused_computation.8 | loop fusion | flops 98304 | bytes 229376 | tf_op jit(solution)/shard_map/convert.1
  25.9 7.5 %collective-permute-start.7 = (bf16[5120,128]{1,0:T(8,128)(2,1)}, bf16[5120,128]{1,0:T(8,128)(2,1)}, u32[]{:S(2)}, u32[]{:S(2)}) collective-permute-start(bf16[5120,128]{1,0:T(8,128)(2,1)} %copy-done.3), channel_id=1, source_target_pairs={{1,9},{10,2},{3,11},{12,4},{2,1},{4,3},{17,25},{26,18},{19,27},{28... | collective-permute-start | bytes 3932168 | tf_op jit(solution)/shard_map/ppermute | solution.py:331
  33.7 1.9 %collective-permute-start.6 = (bf16[2048,128]{1,0:T(8,128)(2,1)S(1)}, bf16[2048,128]{1,0:T(8,128)(2,1)S(1)}, u32[]{:S(2)}, u32[]{:S(2)}) collective-permute-start(bf16[2048,128]{1,0:T(8,128)(2,1)S(1)} %get-tuple-element.40), channel_id=1, source_target_pairs={{1,9},{10,2},{3,11},{12,4},{2,1},{4,3},{17,25},{26,18},{19,27},{28... | collective-permute-start | bytes 1572872 | tf_op jit(solution)/shard_map/ppermute | solution.py:331
  35.7 1.6 %copy-done.1 = bf16[128,8192]{1,0:T(8,128)(2,1)S(1)} copy-done((bf16[128,8192]{1,0:T(8,128)(2,1)S(1)}, bf16[128,8192]{1,0:T(8,128)(2,1)}, u32[]{:S(2)}) %copy-start.1) | copy-done | bytes 2097176
  37.3 9.6 %first_sums.1 = (bf16[9,128,128]{2,1,0:T(8,128)(2,1)S(1)}, bf16[9,128,128]{2,1,0:T(8,128)(2,1)S(1)}, bf16[9,128,128]{2,1,0:T(8,128)(2,1)S(1)}) custom-call(s32[14]{0:T(128)S(1)} %pad_add_fusion.1.switch_ref, bf16[128,8192]{1,0:T(8,128)(2,1)S(1)} %get-tuple-element.32.plain_ref, bf16[128,8192]{1,0:T(8,128)(2,1)S(1)} %copy-done.1, ...), custom_call_target="tpu_custom_call" | custom-call | flops 4831838208 | bytes 8388608 | tf_op jit(solution)/shard_map/first_sums/pallas_call | solution.py:178
  46.8 1.9 %collective-permute-start.5 = (bf16[1024,128]{1,0:T(8,128)(2,1)S(1)}, bf16[1024,128]{1,0:T(8,128)(2,1)S(1)}, u32[]{:S(2)}, u32[]{:S(2)}) collective-permute-start(bf16[1024,128]{1,0:T(8,128)(2,1)S(1)} %get-tuple-element.39), channel_id=1, source_target_pairs={{1,9},{10,2},{3,11},{12,4},{2,1},{4,3},{17,25},{26,18},{19,27},{28... | collective-permute-start | bytes 786440 | tf_op jit(solution)/shard_map/ppermute | solution.py:331
  48.8 6.1 %second_part.2.rest_0_ = f32[1152,128]{1,0:T(8,128)S(1)} custom-call(s32[6]{0:T(128)S(1)} %pad_add_fusion.switch_ref, bf16[128,8192]{1,0:T(8,128)(2,1)S(1)} %get-tuple-element.32.plain_ref, bf16[128,8192]{1,0:T(8,128)(2,1)S(1)} %copy-done.1, bf16[9,8192]{1,0:T(8,128)(2,1)S(1)} %pad_maximum_fusion.coeff_ref, bf16[5120,128]{1,0:T(8,128)(2,1)} %collective-permute-done.7.partner_ref), custom_call_target="tpu_custom_call" | custom-call | flops 1509949440 | bytes 3932160 | tf_op jit(solution)/shard_map/second_part/pallas_call | solution.py:264
  54.9 2.4 %second_part.3.rest_0_ = f32[1152,128]{1,0:T(8,128)S(1)} custom-call(s32[6]{0:T(128)S(1)} %pad_add_fusion.switch_ref, bf16[128,8192]{1,0:T(8,128)(2,1)S(1)} %get-tuple-element.32.plain_ref, bf16[128,8192]{1,0:T(8,128)(2,1)S(1)} %copy-done.1, bf16[9,8192]{1,0:T(8,128)(2,1)S(1)} %pad_maximum_fusion.coeff_ref, ...), custom_call_target="tpu_custom_call" | custom-call | flops 603979776 | bytes 1572864 | tf_op jit(solution)/shard_map/second_part/pallas_call | solution.py:264
  57.3 1.4 %second_last.1 = (bf16[9,128,128]{2,1,0:T(8,128)(2,1)S(1)}, bf16[9,128,128]{2,1,0:T(8,128)(2,1)S(1)}, bf16[9,128,128]{2,1,0:T(8,128)(2,1)S(1)}) custom-call(s32[6]{0:T(128)S(1)} %pad_add_fusion.switch_ref, bf16[128,8192]{1,0:T(8,128)(2,1)S(1)} %get-tuple-element.32.plain_ref, bf16[128,8192]{1,0:T(8,128)(2,1)S(1)} %copy-done.1, ...), custom_call_target="tpu_custom_call" | custom-call | flops 301989888 | bytes 786432 | tf_op jit(solution)/shard_map/second_last/pallas_call | solution.py:264
  58.7 1.9 %collective-permute-start.8 = (bf16[9,128,128]{2,1,0:T(8,128)(2,1)S(1)}, bf16[9,128,128]{2,1,0:T(8,128)(2,1)S(1)}, u32[]{:S(2)}, u32[]{:S(2)}) collective-permute-start(bf16[9,128,128]{2,1,0:T(8,128)(2,1)S(1)} %get-tuple-element.45), channel_id=1, source_target_pairs={{0,8},{13,5},{14,6},{7,15},{9,1},{2,10},{11,3},{4,12},{1,0},{16,24... | collective-permute-start | bytes 884744 | tf_op jit(solution)/shard_map/ppermute | solution.py:342
  60.7 0.7 collective-permute-start.9
  61.4 5.7 %collective-permute-done.8 = bf16[9,128,128]{2,1,0:T(8,128)(2,1)S(1)} collective-permute-done((bf16[9,128,128]{2,1,0:T(8,128)(2,1)S(1)}, bf16[9,128,128]{2,1,0:T(8,128)(2,1)S(1)}, u32[]{:S(2)}, u32[]{:S(2)}) %collective-permute-start.8) | collective-permute-done | bytes 294944 | tf_op jit(solution)/shard_map/ppermute | solution.py:342
  67.1 0.9 %select_bitcast_fusion = (bf16[1,9,128,128]{3,2,1,0:T(8,128)(2,1)}, bf16[1,9,128,128]{3,2,1,0:T(8,128)(2,1)}) fusion(bf16[9,128,128]{2,1,0:T(8,128)(2,1)S(1)} %collective-permute-done.8, bf16[9,128,128]{2,1,0:T(8,128)(2,1)S(1)} %get-tuple-element.47, pred[]{:T(512)S(6)} %or.59, bf16[9,128,128]{2,1,0:T(8,128)(2,1)S(1)} %collective-permute-done.9, ...), kind=kLoop, calls=%fused_computation | loop fusion | flops 442368 | bytes 1769475 | tf_op jit(solution)/shard_map/broadcast_in_dim | solution.py:347
  (25 shorter events, 0.5 us)
Async XLA Ops:
  0.6 25.3 %collective-permute-start.1 = (bf16[8192,128]{1,0:T(8,128)(2,1)}, bf16[8192,128]{1,0:T(8,128)(2,1)}, u32[]{:S(2)}, u32[]{:S(2)}) collective-permute-start(bf16[8192,128]{1,0:T(8,128)(2,1)} %bitcast.15), channel_id=1, source_target_pairs={{3,2},{5,4},{6,5},{9,8},{10,9},{11,10},{12,11},{13,12},{14,13},{15... | collective-permute-start | bytes 6291464 | tf_op jit(solution)/shard_map/ppermute | solution.py:314
  2.6 23.3 %collective-permute-start.2 = (bf16[8192,128]{1,0:T(8,128)(2,1)}, bf16[8192,128]{1,0:T(8,128)(2,1)}, u32[]{:S(2)}, u32[]{:S(2)}) collective-permute-start(bf16[8192,128]{1,0:T(8,128)(2,1)} %bitcast.16), channel_id=1, source_target_pairs={{8,0},{5,13},{6,14},{15,7},{0,1},{7,6},{24,16},{21,29},{22,30},{31... | collective-permute-start | bytes 6291464 | tf_op jit(solution)/shard_map/ppermute | solution.py:315
  3.9 21.9 %collective-permute-start.3 = (s32[1,4]{1,0:T(1,128)}, s32[1,4]{1,0:T(1,128)S(1)}, u32[]{:S(2)}, u32[]{:S(2)}) collective-permute-start(s32[1,4]{1,0:T(1,128)} %param.3), channel_id=1, source_target_pairs={{3,2},{5,4},{6,5},{9,8},{10,9},{11,10},{12,11},{13,12},{14,13},{15... | collective-permute-start | bytes 56 | tf_op jit(solution)/shard_map/ppermute | solution.py:320
  4.6 21.3 %collective-permute-start.4 = (s32[1,4]{1,0:T(1,128)}, s32[1,4]{1,0:T(1,128)S(1)}, u32[]{:S(2)}, u32[]{:S(2)}) collective-permute-start(s32[1,4]{1,0:T(1,128)} %param.3), channel_id=1, source_target_pairs={{8,0},{5,13},{6,14},{15,7},{0,1},{7,6},{24,16},{21,29},{22,30},{31... | collective-permute-start | bytes 56 | tf_op jit(solution)/shard_map/ppermute | solution.py:319
  5.9 27.7 %collective-permute-start = (s32[1,4]{1,0:T(1,128)}, s32[1,4]{1,0:T(1,128)S(1)}, u32[]{:S(2)}, u32[]{:S(2)}) collective-permute-start(s32[1,4]{1,0:T(1,128)} %param.3), channel_id=1, source_target_pairs={{1,9},{10,2},{3,11},{12,4},{2,1},{4,3},{17,25},{26,18},{19,27},{28... | collective-permute-start | bytes 56 | tf_op jit(solution)/shard_map/ppermute | solution.py:321
  16.4 1.6 %copy-start.2 = (bf16[1024,2,4,128]{3,2,1,0:T(4,128)(2,1)S(1)}, bf16[1024,2,4,128]{3,2,1,0:T(4,128)(2,1)}, u32[]{:S(2)}) copy-start(bf16[1024,2,4,128]{3,2,1,0:T(4,128)(2,1)} %param.2) | copy-start | bytes 6291460
  18.3 1.0 %copy-start.3 = (bf16[5120,128]{1,0:T(8,128)(2,1)}, bf16[5120,128]{1,0:T(8,128)(2,1)S(1)}, u32[]{:S(2)}) copy-start(bf16[5120,128]{1,0:T(8,128)(2,1)S(1)} %get-tuple-element.41) | copy-start | bytes 3932164
  19.4 14.2 %copy-start.4 = (s32[1,4]{1,0:T(1,128)S(1)}, s32[1,4]{1,0:T(1,128)}, u32[]{:S(2)}) copy-start(s32[1,4]{1,0:T(1,128)} %param.3) | copy-start | bytes 52
  22.5 1.4 %copy-start = (bf16[128,8192]{1,0:T(8,128)(2,1)}, bf16[128,8192]{1,0:T(8,128)(2,1)S(1)}, u32[]{:S(2)}) copy-start(bf16[128,8192]{1,0:T(8,128)(2,1)S(1)} %get-tuple-element.33.swapped_ref) | copy-start | bytes 6291460
  25.9 22.9 %collective-permute-start.7 = (bf16[5120,128]{1,0:T(8,128)(2,1)}, bf16[5120,128]{1,0:T(8,128)(2,1)}, u32[]{:S(2)}, u32[]{:S(2)}) collective-permute-start(bf16[5120,128]{1,0:T(8,128)(2,1)} %copy-done.3), channel_id=1, source_target_pairs={{1,9},{10,2},{3,11},{12,4},{2,1},{4,3},{17,25},{26,18},{19,27},{28... | collective-permute-start | bytes 3932168 | tf_op jit(solution)/shard_map/ppermute | solution.py:331
  33.7 21.2 %collective-permute-start.6 = (bf16[2048,128]{1,0:T(8,128)(2,1)S(1)}, bf16[2048,128]{1,0:T(8,128)(2,1)S(1)}, u32[]{:S(2)}, u32[]{:S(2)}) collective-permute-start(bf16[2048,128]{1,0:T(8,128)(2,1)S(1)} %get-tuple-element.40), channel_id=1, source_target_pairs={{1,9},{10,2},{3,11},{12,4},{2,1},{4,3},{17,25},{26,18},{19,27},{28... | collective-permute-start | bytes 1572872 | tf_op jit(solution)/shard_map/ppermute | solution.py:331
  35.7 1.6 %copy-start.1 = (bf16[128,8192]{1,0:T(8,128)(2,1)S(1)}, bf16[128,8192]{1,0:T(8,128)(2,1)}, u32[]{:S(2)}) copy-start(bf16[128,8192]{1,0:T(8,128)(2,1)} %copy-done) | copy-start | bytes 6291460
  46.8 10.4 %collective-permute-start.5 = (bf16[1024,128]{1,0:T(8,128)(2,1)S(1)}, bf16[1024,128]{1,0:T(8,128)(2,1)S(1)}, u32[]{:S(2)}, u32[]{:S(2)}) collective-permute-start(bf16[1024,128]{1,0:T(8,128)(2,1)S(1)} %get-tuple-element.39), channel_id=1, source_target_pairs={{1,9},{10,2},{3,11},{12,4},{2,1},{4,3},{17,25},{26,18},{19,27},{28... | collective-permute-start | bytes 786440 | tf_op jit(solution)/shard_map/ppermute | solution.py:331
  58.7 8.4 %collective-permute-start.8 = (bf16[9,128,128]{2,1,0:T(8,128)(2,1)S(1)}, bf16[9,128,128]{2,1,0:T(8,128)(2,1)S(1)}, u32[]{:S(2)}, u32[]{:S(2)}) collective-permute-start(bf16[9,128,128]{2,1,0:T(8,128)(2,1)S(1)} %get-tuple-element.45), channel_id=1, source_target_pairs={{0,8},{13,5},{14,6},{7,15},{9,1},{2,10},{11,3},{4,12},{1,0},{16,24... | collective-permute-start | bytes 884744 | tf_op jit(solution)/shard_map/ppermute | solution.py:342
  60.7 6.4 %collective-permute-start.9 = (bf16[9,128,128]{2,1,0:T(8,128)(2,1)S(1)}, bf16[9,128,128]{2,1,0:T(8,128)(2,1)S(1)}, u32[]{:S(2)}, u32[]{:S(2)}) collective-permute-start(bf16[9,128,128]{2,1,0:T(8,128)(2,1)S(1)} %get-tuple-element.46), channel_id=1, source_target_pairs={{0,7},{7,15},{16,23},{23,31}} | collective-permute-start | bytes 884744 | tf_op jit(solution)/shard_map/ppermute | solution.py:343

commit v32 on v31

--- a/solution.py
+++ b/solution.py
@@ -11,7 +11,7 @@
 HL = 4
 LAGS = 2 * HL + 1
 STEP = 1024
-ENDS = (5, 7, 8)
+ENDS = (4, 7, 8)
 PARAMS = pltpu.CompilerParams(vmem_limit_bytes=16 * 1024 * 1024)
 
 

time: 68.9 us -> 68.3 us (level)
  waiting for transfers between devices: 5.74 us -> 6.84 us
  Pallas kernels: 22.9 us -> 21.8 us
    pallas_call x3, Pallas kernels: 9.87 us -> 8.73 us  [second_sums(): pl.pallas_call(functools.partial(second_kernel, windows, not earlier, las...]
    ppermute x3, waiting for transfers between devices: 0.01 us -> 0.92 us  [local(): second_in = [lax.ppermute(part, 'chan', second_pairs) for part in parts]]
  transfers between devices with their start and end apart: 10 -> 10, of which waited for: 1 -> 2; matrix products, arithmetic and copies ran while one was open for 3% -> 3% of each run, Pallas kernels for 32% -> 30%
where the time goes in v32:
time: 68.3 us; the launch traced here: 67.8 us
  starting transfers between devices  29.6 us (43%)
  Pallas kernels  21.8 us (32%)
  waiting for transfers between devices  6.84 us (10%)
  local copies, waits for them, and re-layouts  5.43 us (8%)
  other arithmetic  3.15 us (5%)
  between operations  0.95 us (1%)
    ppermute x3, starting transfers between devices, local(): second_in = [lax.ppermute(part, 'chan', second_pairs) for part in parts]  11.3 us
    ppermute x1, starting transfers between devices, local(): second_flags = lax.ppermute(quality, 'chan', second_pairs)[0]  10.5 us
    pallas_call x1, Pallas kernels, first_sums(): pl.pallas_call(functools.partial(first_kernel, windows), grid_spec=pltpu....  9.57 us
    pallas_call x3, Pallas kernels, second_sums(): pl.pallas_call(functools.partial(second_kernel, windows, not earlier, las...  8.73 us
    ppermute x1, waiting for transfers between devices, local(): returned = lax.ppermute(back, 'chan', back_pairs)  5.91 us
    unnamed x10, local copies, waits for them, and re-layouts  5.43 us
    pallas_call x1, Pallas kernels, turn(): pl.pallas_call(turn_kernel, grid=(rows // STEP,), in_specs=[pl.BlockSpec(...  3.15 us
    ppermute x1, starting transfers between devices, local(): near_in = lax.ppermute(block, 'chan', near_pairs)  2.01 us
  transfers between devices with their start and end apart: 10, of which 2 were waited for; matrix products, arithmetic and copies ran while one was open for 3% of the time, Pallas kernels for 30%

profile of v32, /device:TPU:1, one launch (start us, length us, event | category | flops | bytes accessed | tf_op | source)
XLA Modules:
  0.0 67.8 jit_solution(5717877155334863651)
XLA Ops:
  0.6 2.0 %collective-permute-start.1 = (bf16[8192,128]{1,0:T(8,128)(2,1)}, bf16[8192,128]{1,0:T(8,128)(2,1)}, u32[]{:S(2)}, u32[]{:S(2)}) collective-permute-start(bf16[8192,128]{1,0:T(8,128)(2,1)} %bitcast.15), channel_id=1, source_target_pairs={{3,2},{5,4},{6,5},{9,8},{10,9},{11,10},{12,11},{13,12},{14,13},{15... | collective-permute-start | bytes 6291464 | tf_op jit(solution)/shard_map/ppermute | solution.py:314
  2.6 1.3 %collective-permute-start.2 = (bf16[8192,128]{1,0:T(8,128)(2,1)}, bf16[8192,128]{1,0:T(8,128)(2,1)}, u32[]{:S(2)}, u32[]{:S(2)}) collective-permute-start(bf16[8192,128]{1,0:T(8,128)(2,1)} %bitcast.16), channel_id=1, source_target_pairs={{8,0},{5,13},{6,14},{15,7},{0,1},{7,6},{24,16},{21,29},{22,30},{31... | collective-permute-start | bytes 6291464 | tf_op jit(solution)/shard_map/ppermute | solution.py:315
  3.9 0.7 collective-permute-start.3
  4.6 1.3 %collective-permute-start.4 = (s32[1,4]{1,0:T(1,128)}, s32[1,4]{1,0:T(1,128)S(1)}, u32[]{:S(2)}, u32[]{:S(2)}) collective-permute-start(s32[1,4]{1,0:T(1,128)} %param.3), channel_id=1, source_target_pairs={{8,0},{5,13},{6,14},{15,7},{0,1},{7,6},{24,16},{21,29},{22,30},{31... | collective-permute-start | bytes 56 | tf_op jit(solution)/shard_map/ppermute | solution.py:319
  5.9 10.5 %collective-permute-start = (s32[1,4]{1,0:T(1,128)}, s32[1,4]{1,0:T(1,128)S(1)}, u32[]{:S(2)}, u32[]{:S(2)}) collective-permute-start(s32[1,4]{1,0:T(1,128)} %param.3), channel_id=1, source_target_pairs={{1,9},{10,2},{3,11},{12,4},{2,1},{4,3},{17,25},{26,18},{19,27},{28... | collective-permute-start | bytes 56 | tf_op jit(solution)/shard_map/ppermute | solution.py:321
  16.4 1.6 %copy-done.2 = bf16[1024,2,4,128]{3,2,1,0:T(4,128)(2,1)S(1)} copy-done((bf16[1024,2,4,128]{3,2,1,0:T(4,128)(2,1)S(1)}, bf16[1024,2,4,128]{3,2,1,0:T(4,128)(2,1)}, u32[]{:S(2)}) %copy-start.2) | copy-done | bytes 2097176
  18.3 0.9 %copy-done.3 = bf16[3072,128]{1,0:T(8,128)(2,1)} copy-done((bf16[3072,128]{1,0:T(8,128)(2,1)}, bf16[3072,128]{1,0:T(8,128)(2,1)S(1)}, u32[]{:S(2)}) %copy-start.3) | copy-done | bytes 786456
  19.2 3.1 %turn.1 = (bf16[128,8192]{1,0:T(8,128)(2,1)S(1)}, bf16[128,8192]{1,0:T(8,128)(2,1)S(1)}) custom-call(bf16[8192,128]{1,0:T(8,128)(2,1)S(1)} %bitcast.18), custom_call_target="tpu_custom_call" | custom-call | bytes 6291456 | tf_op jit(solution)/shard_map/turn/pallas_call | solution.py:83
  22.4 1.3 %copy-done = bf16[128,8192]{1,0:T(8,128)(2,1)} copy-done((bf16[128,8192]{1,0:T(8,128)(2,1)}, bf16[128,8192]{1,0:T(8,128)(2,1)S(1)}, u32[]{:S(2)}) %copy-start) | copy-done | bytes 2097176
  23.9 0.9 %multiply_convert_fusion = (bf16[5,8192]{1,0:T(8,128)(2,1)S(1)}, f32[5,8192]{1,0:T(8,128)S(1)}) fusion(f32[8192]{0:T(1024)S(1)} %fusion.9, f32[5]{0:T(128)S(1)} %iota_multiply_fusion), kind=kLoop, calls=%fused_computation.4 | loop fusion | flops 122880 | bytes 278548 | tf_op jit(solution)/shard_map/convert
  24.9 0.9 %fusion.2 = bf16[4,8192]{1,0:T(4,128)(2,1)S(1)} fusion(f32[5,8192]{1,0:T(8,128)S(1)} %get-tuple-element.51, f32[8192]{0:T(1024)S(1)} %select_multiply_fusion), kind=kLoop, calls=%fused_computation.8 | loop fusion | flops 98304 | bytes 229376 | tf_op jit(solution)/shard_map/convert.1
  25.9 7.5 %collective-permute-start.7 = (bf16[4096,128]{1,0:T(8,128)(2,1)S(1)}, bf16[4096,128]{1,0:T(8,128)(2,1)S(1)}, u32[]{:S(2)}, u32[]{:S(2)}) collective-permute-start(bf16[4096,128]{1,0:T(8,128)(2,1)S(1)} %get-tuple-element.41), channel_id=1, source_target_pairs={{1,9},{10,2},{3,11},{12,4},{2,1},{4,3},{17,25},{26,18},{19,27},{28... | collective-permute-start | bytes 3145736 | tf_op jit(solution)/shard_map/ppermute | solution.py:331
  33.5 1.9 %collective-permute-start.6 = (bf16[3072,128]{1,0:T(8,128)(2,1)}, bf16[3072,128]{1,0:T(8,128)(2,1)S(1)}, u32[]{:S(2)}, u32[]{:S(2)}) collective-permute-start(bf16[3072,128]{1,0:T(8,128)(2,1)} %copy-done.3), channel_id=1, source_target_pairs={{1,9},{10,2},{3,11},{12,4},{2,1},{4,3},{17,25},{26,18},{19,27},{28... | collective-permute-start | bytes 2359304 | tf_op jit(solution)/shard_map/ppermute | solution.py:331
  35.5 1.6 %copy-done.1 = bf16[128,8192]{1,0:T(8,128)(2,1)S(1)} copy-done((bf16[128,8192]{1,0:T(8,128)(2,1)S(1)}, bf16[128,8192]{1,0:T(8,128)(2,1)}, u32[]{:S(2)}) %copy-start.1) | copy-done | bytes 2097176
  37.1 9.6 %first_sums.1 = (bf16[9,128,128]{2,1,0:T(8,128)(2,1)S(1)}, bf16[9,128,128]{2,1,0:T(8,128)(2,1)S(1)}, bf16[9,128,128]{2,1,0:T(8,128)(2,1)S(1)}) custom-call(s32[14]{0:T(128)S(1)} %pad_add_fusion.1.switch_ref, bf16[128,8192]{1,0:T(8,128)(2,1)S(1)} %get-tuple-element.32.plain_ref, bf16[128,8192]{1,0:T(8,128)(2,1)S(1)} %copy-done.1, ...), custom_call_target="tpu_custom_call" | custom-call | flops 4831838208 | bytes 8388608 | tf_op jit(solution)/shard_map/first_sums/pallas_call | solution.py:178
  46.7 1.9 %collective-permute-start.5 = (bf16[1024,128]{1,0:T(8,128)(2,1)S(1)}, bf16[1024,128]{1,0:T(8,128)(2,1)S(1)}, u32[]{:S(2)}, u32[]{:S(2)}) collective-permute-start(bf16[1024,128]{1,0:T(8,128)(2,1)S(1)} %get-tuple-element.39), channel_id=1, source_target_pairs={{1,9},{10,2},{3,11},{12,4},{2,1},{4,3},{17,25},{26,18},{19,27},{28... | collective-permute-start | bytes 786440 | tf_op jit(solution)/shard_map/ppermute | solution.py:331
  48.7 4.1 %second_part.2.rest_0_ = f32[1152,128]{1,0:T(8,128)S(1)} custom-call(s32[6]{0:T(128)S(1)} %pad_add_fusion.switch_ref, bf16[128,8192]{1,0:T(8,128)(2,1)S(1)} %get-tuple-element.32.plain_ref, bf16[128,8192]{1,0:T(8,128)(2,1)S(1)} %copy-done.1, bf16[9,8192]{1,0:T(8,128)(2,1)S(1)} %pad_maximum_fusion.coeff_ref, ...), custom_call_target="tpu_custom_call" | custom-call | flops 1207959552 | bytes 3145728 | tf_op jit(solution)/shard_map/second_part/pallas_call | solution.py:264
  52.8 0.9 %collective-permute-done.6.partner_ref = bf16[3072,128]{1,0:T(8,128)(2,1)S(1)} collective-permute-done((bf16[3072,128]{1,0:T(8,128)(2,1)}, bf16[3072,128]{1,0:T(8,128)(2,1)S(1)}, u32[]{:S(2)}, u32[]{:S(2)}) %collective-permute-start.6) | collective-permute-done | bytes 786464 | tf_op jit(solution)/shard_map/ppermute | solution.py:331
  53.7 3.2 %second_part.3.rest_0_ = f32[1152,128]{1,0:T(8,128)S(1)} custom-call(s32[6]{0:T(128)S(1)} %pad_add_fusion.switch_ref, bf16[128,8192]{1,0:T(8,128)(2,1)S(1)} %get-tuple-element.32.plain_ref, bf16[128,8192]{1,0:T(8,128)(2,1)S(1)} %copy-done.1, bf16[9,8192]{1,0:T(8,128)(2,1)S(1)} %pad_maximum_fusion.coeff_ref, ...), custom_call_target="tpu_custom_call" | custom-call | flops 905969664 | bytes 2359296 | tf_op jit(solution)/shard_map/second_part/pallas_call | solution.py:264
  56.9 1.4 %second_last.1 = (bf16[9,128,128]{2,1,0:T(8,128)(2,1)S(1)}, bf16[9,128,128]{2,1,0:T(8,128)(2,1)S(1)}, bf16[9,128,128]{2,1,0:T(8,128)(2,1)S(1)}) custom-call(s32[6]{0:T(128)S(1)} %pad_add_fusion.switch_ref, bf16[128,8192]{1,0:T(8,128)(2,1)S(1)} %get-tuple-element.32.plain_ref, bf16[128,8192]{1,0:T(8,128)(2,1)S(1)} %copy-done.1, ...), custom_call_target="tpu_custom_call" | custom-call | flops 301989888 | bytes 786432 | tf_op jit(solution)/shard_map/second_last/pallas_call | solution.py:264
  58.4 1.9 %collective-permute-start.8 = (bf16[9,128,128]{2,1,0:T(8,128)(2,1)S(1)}, bf16[9,128,128]{2,1,0:T(8,128)(2,1)S(1)}, u32[]{:S(2)}, u32[]{:S(2)}) collective-permute-start(bf16[9,128,128]{2,1,0:T(8,128)(2,1)S(1)} %get-tuple-element.45), channel_id=1, source_target_pairs={{0,8},{13,5},{14,6},{7,15},{9,1},{2,10},{11,3},{4,12},{1,0},{16,24... | collective-permute-start | bytes 884744 | tf_op jit(solution)/shard_map/ppermute | solution.py:342
  60.3 0.7 %collective-permute-start.9 = (bf16[9,128,128]{2,1,0:T(8,128)(2,1)S(1)}, bf16[9,128,128]{2,1,0:T(8,128)(2,1)S(1)}, u32[]{:S(2)}, u32[]{:S(2)}) collective-permute-start(bf16[9,128,128]{2,1,0:T(8,128)(2,1)S(1)} %get-tuple-element.46), channel_id=1, source_target_pairs={{0,7},{7,15},{16,23},{23,31}} | collective-permute-start | bytes 884744 | tf_op jit(solution)/shard_map/ppermute | solution.py:343
  61.0 5.9 %collective-permute-done.8 = bf16[9,128,128]{2,1,0:T(8,128)(2,1)S(1)} collective-permute-done((bf16[9,128,128]{2,1,0:T(8,128)(2,1)S(1)}, bf16[9,128,128]{2,1,0:T(8,128)(2,1)S(1)}, u32[]{:S(2)}, u32[]{:S(2)}) %collective-permute-start.8) | collective-permute-done | bytes 294944 | tf_op jit(solution)/shard_map/ppermute | solution.py:342
  66.9 0.9 %select_bitcast_fusion = (bf16[1,9,128,128]{3,2,1,0:T(8,128)(2,1)}, bf16[1,9,128,128]{3,2,1,0:T(8,128)(2,1)}) fusion(bf16[9,128,128]{2,1,0:T(8,128)(2,1)S(1)} %collective-permute-done.8, bf16[9,128,128]{2,1,0:T(8,128)(2,1)S(1)} %get-tuple-element.47, pred[]{:T(512)S(6)} %or.59, bf16[9,128,128]{2,1,0:T(8,128)(2,1)S(1)} %collective-permute-done.9, ...), kind=kLoop, calls=%fused_computation | loop fusion | flops 442368 | bytes 1769475 | tf_op jit(solution)/shard_map/broadcast_in_dim | solution.py:347
  (25 shorter events, 0.8 us)
Async XLA Ops:
  0.6 25.3 %collective-permute-start.1 = (bf16[8192,128]{1,0:T(8,128)(2,1)}, bf16[8192,128]{1,0:T(8,128)(2,1)}, u32[]{:S(2)}, u32[]{:S(2)}) collective-permute-start(bf16[8192,128]{1,0:T(8,128)(2,1)} %bitcast.15), channel_id=1, source_target_pairs={{3,2},{5,4},{6,5},{9,8},{10,9},{11,10},{12,11},{13,12},{14,13},{15... | collective-permute-start | bytes 6291464 | tf_op jit(solution)/shard_map/ppermute | solution.py:314
  2.6 23.3 %collective-permute-start.2 = (bf16[8192,128]{1,0:T(8,128)(2,1)}, bf16[8192,128]{1,0:T(8,128)(2,1)}, u32[]{:S(2)}, u32[]{:S(2)}) collective-permute-start(bf16[8192,128]{1,0:T(8,128)(2,1)} %bitcast.16), channel_id=1, source_target_pairs={{8,0},{5,13},{6,14},{15,7},{0,1},{7,6},{24,16},{21,29},{22,30},{31... | collective-permute-start | bytes 6291464 | tf_op jit(solution)/shard_map/ppermute | solution.py:315
  3.9 22.0 %collective-permute-start.3 = (s32[1,4]{1,0:T(1,128)}, s32[1,4]{1,0:T(1,128)S(1)}, u32[]{:S(2)}, u32[]{:S(2)}) collective-permute-start(s32[1,4]{1,0:T(1,128)} %param.3), channel_id=1, source_target_pairs={{3,2},{5,4},{6,5},{9,8},{10,9},{11,10},{12,11},{13,12},{14,13},{15... | collective-permute-start | bytes 56 | tf_op jit(solution)/shard_map/ppermute | solution.py:320
  4.6 21.3 %collective-permute-start.4 = (s32[1,4]{1,0:T(1,128)}, s32[1,4]{1,0:T(1,128)S(1)}, u32[]{:S(2)}, u32[]{:S(2)}) collective-permute-start(s32[1,4]{1,0:T(1,128)} %param.3), channel_id=1, source_target_pairs={{8,0},{5,13},{6,14},{15,7},{0,1},{7,6},{24,16},{21,29},{22,30},{31... | collective-permute-start | bytes 56 | tf_op jit(solution)/shard_map/ppermute | solution.py:319
  5.9 27.5 %collective-permute-start = (s32[1,4]{1,0:T(1,128)}, s32[1,4]{1,0:T(1,128)S(1)}, u32[]{:S(2)}, u32[]{:S(2)}) collective-permute-start(s32[1,4]{1,0:T(1,128)} %param.3), channel_id=1, source_target_pairs={{1,9},{10,2},{3,11},{12,4},{2,1},{4,3},{17,25},{26,18},{19,27},{28... | collective-permute-start | bytes 56 | tf_op jit(solution)/shard_map/ppermute | solution.py:321
  16.4 1.6 %copy-start.2 = (bf16[1024,2,4,128]{3,2,1,0:T(4,128)(2,1)S(1)}, bf16[1024,2,4,128]{3,2,1,0:T(4,128)(2,1)}, u32[]{:S(2)}) copy-start(bf16[1024,2,4,128]{3,2,1,0:T(4,128)(2,1)} %param.2) | copy-start | bytes 6291460
  18.3 0.9 %copy-start.3 = (bf16[3072,128]{1,0:T(8,128)(2,1)}, bf16[3072,128]{1,0:T(8,128)(2,1)S(1)}, u32[]{:S(2)}) copy-start(bf16[3072,128]{1,0:T(8,128)(2,1)S(1)} %get-tuple-element.40) | copy-start | bytes 2359300
  19.2 14.2 %copy-start.4 = (s32[1,4]{1,0:T(1,128)S(1)}, s32[1,4]{1,0:T(1,128)}, u32[]{:S(2)}) copy-start(s32[1,4]{1,0:T(1,128)} %param.3) | copy-start | bytes 52
  22.4 1.4 %copy-start = (bf16[128,8192]{1,0:T(8,128)(2,1)}, bf16[128,8192]{1,0:T(8,128)(2,1)S(1)}, u32[]{:S(2)}) copy-start(bf16[128,8192]{1,0:T(8,128)(2,1)S(1)} %get-tuple-element.33.swapped_ref) | copy-start | bytes 6291460
  25.9 22.7 %collective-permute-start.7 = (bf16[4096,128]{1,0:T(8,128)(2,1)S(1)}, bf16[4096,128]{1,0:T(8,128)(2,1)S(1)}, u32[]{:S(2)}, u32[]{:S(2)}) collective-permute-start(bf16[4096,128]{1,0:T(8,128)(2,1)S(1)} %get-tuple-element.41), channel_id=1, source_target_pairs={{1,9},{10,2},{3,11},{12,4},{2,1},{4,3},{17,25},{26,18},{19,27},{28... | collective-permute-start | bytes 3145736 | tf_op jit(solution)/shard_map/ppermute | solution.py:331
  33.5 20.1 %collective-permute-start.6 = (bf16[3072,128]{1,0:T(8,128)(2,1)}, bf16[3072,128]{1,0:T(8,128)(2,1)S(1)}, u32[]{:S(2)}, u32[]{:S(2)}) collective-permute-start(bf16[3072,128]{1,0:T(8,128)(2,1)} %copy-done.3), channel_id=1, source_target_pairs={{1,9},{10,2},{3,11},{12,4},{2,1},{4,3},{17,25},{26,18},{19,27},{28... | collective-permute-start | bytes 2359304 | tf_op jit(solution)/shard_map/ppermute | solution.py:331
  35.5 1.6 %copy-start.1 = (bf16[128,8192]{1,0:T(8,128)(2,1)S(1)}, bf16[128,8192]{1,0:T(8,128)(2,1)}, u32[]{:S(2)}) copy-start(bf16[128,8192]{1,0:T(8,128)(2,1)} %copy-done) | copy-start | bytes 6291460
  46.7 10.2 %collective-permute-start.5 = (bf16[1024,128]{1,0:T(8,128)(2,1)S(1)}, bf16[1024,128]{1,0:T(8,128)(2,1)S(1)}, u32[]{:S(2)}, u32[]{:S(2)}) collective-permute-start(bf16[1024,128]{1,0:T(8,128)(2,1)S(1)} %get-tuple-element.39), channel_id=1, source_target_pairs={{1,9},{10,2},{3,11},{12,4},{2,1},{4,3},{17,25},{26,18},{19,27},{28... | collective-permute-start | bytes 786440 | tf_op jit(solution)/shard_map/ppermute | solution.py:331
  58.4 8.6 %collective-permute-start.8 = (bf16[9,128,128]{2,1,0:T(8,128)(2,1)S(1)}, bf16[9,128,128]{2,1,0:T(8,128)(2,1)S(1)}, u32[]{:S(2)}, u32[]{:S(2)}) collective-permute-start(bf16[9,128,128]{2,1,0:T(8,128)(2,1)S(1)} %get-tuple-element.45), channel_id=1, source_target_pairs={{0,8},{13,5},{14,6},{7,15},{9,1},{2,10},{11,3},{4,12},{1,0},{16,24... | collective-permute-start | bytes 884744 | tf_op jit(solution)/shard_map/ppermute | solution.py:342
  60.3 6.6 %collective-permute-start.9 = (bf16[9,128,128]{2,1,0:T(8,128)(2,1)S(1)}, bf16[9,128,128]{2,1,0:T(8,128)(2,1)S(1)}, u32[]{:S(2)}, u32[]{:S(2)}) collective-permute-start(bf16[9,128,128]{2,1,0:T(8,128)(2,1)S(1)} %get-tuple-element.46), channel_id=1, source_target_pairs={{0,7},{7,15},{16,23},{23,31}} | collective-permute-start | bytes 884744 | tf_op jit(solution)/shard_map/ppermute | solution.py:343
